TPU v7x, 32 devices: a whole 2x2x4 slice. The times are simulated.
32 devices in a mesh: comp: 2 (over y), gx: 4 (over x, core), gy: 4 (over z).
Axes of the slice: x: 2, y: 2, z: 4, core: 2. Of those that a mesh axis runs over, the one named last changes fastest.
Arguments:
- fields: float32 [2, 32, 128, 1024], P('comp', 'gx', 'gy'), may hold values from -6 to 6
- wet_cells: int32 [32, 1024], P('gx'), may hold values 0 or 1
- flux_weight: float32 [128], replicated, may hold values from -0.5 to 0.5
- variable_sea_response: float32 [128], replicated, may hold values from 0.3 to 1
- diffusivity: float32 [128], replicated, may hold values from 0.05 to 500
- a2o_source: int32 [4, 4, 32, 128], P('gx', 'gy'), may hold values from 0 to 8191, as said below
- a2o_target: int32 [4, 4, 32, 128], P('gx', 'gy'), may hold values from 0 to 8191, as said below
- a2o_count: int32 [4, 4], P('gx', 'gy'), may hold values from 8 to 32, as said below
- a2o_weight: bfloat16 [4, 4, 32, 128, 128], P('gx', 'gy'), may hold values from -0.5 to 1.5
- marine_air_input_index: int32 [4, 4, 32, 128], P('gx', 'gy'), may hold values from 0 to 8191, as said below
- marine_air_output_index: int32 [4, 4, 32, 128], P('gx', 'gy'), may hold values from 0 to 8191, as said below
- marine_air_piece_tally: int32 [4, 4], P('gx', 'gy'), may hold values from 8 to 32, as said below
- marine_air_piece_factor: bfloat16 [4, 4, 32, 128, 128], P('gx', 'gy'), may hold values from -0.5 to 1.5
Outputs:
- new_fields: float32 [2, 32, 128, 1024], P('comp', 'gx', 'gy')
Inputs may be any that keep to these rules, and one draw needn't show every extreme that they name: `a2o_source`: within a block the indices are distinct. `a2o_target`: within a block the indices are distinct. `a2o_count`: some block group uses all 32 blocks. `marine_air_input_index`: within a block the indices are distinct. `marine_air_output_index`: within a block the indices are distinct. `marine_air_piece_tally`: some block group uses all 32 blocks.
All inputs are finite; a program needn't handle non-finite values. No bound on the sum of `wet_cells` on one device may be relied on, other than what follows from the above.
Results may differ from a plain program's by a relative error of at most 0.0024.
Values may be sent and summed in bfloat16 or wider, within the bound.
No kernel may reach another device: no remote copies, remote signals or barrier semaphores. Data moves between devices by JAX's collectives and lax.ppermute only.
A program may use at most 128 MiB of HBM per device.

v0:
```python
import math

import jax
import jax.numpy as jnp
from jax import lax
from jax.sharding import PartitionSpec as P

exact_mode = lax.Precision.HIGHEST
spread_rate = 0.2
mixing_rate = 0.1
heat_gain = 0.5
salt_gain = -0.25


def partner(block, axis, bit):
    count = lax.axis_size(axis)
    route = []
    for low in range(count):
        high = low | 1 << bit
        if high != low and high < count:
            route += [(low, high), (high, low)]
    return lax.ppermute(block, axis, route)


def padded_2(block, sides, width):
    for axis, dim in sides:
        count = lax.axis_size(axis)
        forward = [(i, i + 1) for i in range(count - 1)]
        backward = [(target, source) for source, target in forward]
        low = lax.ppermute(
            lax.slice_in_dim(block, block.shape[dim] - width, None, axis=dim), axis, forward
        )
        high = lax.ppermute(lax.slice_in_dim(block, 0, width, axis=dim), axis, backward)
        block = jnp.concatenate([low, block, high], axis=dim)
    return block


def fourier_tables(columns, groups_x, groups_y):
    per_group = columns // 2 // groups_x
    per_sub = per_group // groups_y
    column_ids = jnp.arange(columns, dtype=jnp.int32)
    block_id = column_ids // (2 * per_group)
    inside = column_ids % (2 * per_group)
    sub_id = inside // (2 * per_sub)
    within = inside % (2 * per_sub)
    part_id = within // per_sub
    wave_ids = block_id * per_group + sub_id * per_sub + within % per_sub
    longitude = jnp.arange(columns, dtype=jnp.int32)
    phase_ids = longitude[:, None] * wave_ids[None, :] % columns
    angles = phase_ids.astype(jnp.float32) * (2.0 * math.pi / columns)
    forward = jnp.where(part_id[None, :] == 0, jnp.cos(angles), jnp.sin(angles))
    col_weight = jnp.where(wave_ids == 0, 1.0, 2.0) / columns
    inverse = forward.T * col_weight[:, None]
    return (forward, inverse, wave_ids)


def sine_table(count):
    ordinal = jnp.arange(1, count + 1, dtype=jnp.int32)
    phase_ids = ordinal[:, None] * ordinal[None, :] % (2 * (count + 1))
    return jnp.sin(phase_ids.astype(jnp.float32) * (math.pi / (count + 1)))


def meridional_rates(count):
    ordinal = jnp.arange(1, count + 1, dtype=jnp.int32).astype(jnp.float32)
    sines_half = jnp.sin(ordinal * (math.pi / (2 * (count + 1))))
    return 4.0 * sines_half * sines_half


def zonal_rates(wave_ids, columns):
    sines_half = jnp.sin(wave_ids.astype(jnp.float32) * (math.pi / columns))
    return 4.0 * sines_half * sines_half


def damp(spectral, sine_matrix, viscous, my_waves, columns):
    mode_count = sine_matrix.shape[0]
    mode_values = jnp.dot(
        sine_matrix, spectral, precision=exact_mode, preferred_element_type=jnp.float32
    )
    decay_rate = (
        meridional_rates(mode_count)[:, None, None] + zonal_rates(my_waves, columns)[None, None, :]
    )
    factor = 1.0 + viscous[None, :, None] * decay_rate
    mode_values = (mode_values.reshape(mode_count, viscous.shape[0], -1) / factor).reshape(
        mode_count, -1
    )
    return jnp.dot(
        sine_matrix, mode_values, precision=exact_mode, preferred_element_type=jnp.float32
    ) * (2.0 / (mode_count + 1))


def block_values(surface, source, weight, count):
    gathered = surface[source]
    block_terms = jnp.einsum("bkl,bl->bk", weight, gathered, preferred_element_type=jnp.float32)
    in_use = jnp.arange(source.shape[0], dtype=jnp.int32)[:, None] < count
    return jnp.where(in_use, block_terms, 0.0)


def local(
    fields,
    wet_cells,
    flux_weight,
    variable_sea_response,
    diffusivity,
    a2o_source,
    a2o_target,
    a2o_count,
    a2o_weight,
    marine_air_input_index,
    marine_air_output_index,
    marine_air_piece_tally,
    marine_air_piece_factor,
):
    band_rows = fields.shape[1]
    channels = fields.shape[2]
    columns = fields.shape[3]
    groups_x = lax.axis_size("gx")
    groups_y = lax.axis_size("gy")
    row_group = lax.axis_index("gx")
    col_group = lax.axis_index("gy")
    is_atmos = lax.axis_index("comp") == 0
    own_slab = fields[0]
    first_channel = col_group * channels
    flux_here = lax.dynamic_slice_in_dim(flux_weight, first_channel, channels)
    gain_here = lax.dynamic_slice_in_dim(variable_sea_response, first_channel, channels)
    atmos_part = jnp.sum(own_slab * flux_here[None, :, None], axis=1)
    ocean_part = jnp.where(col_group == 0, own_slab[:, 0, :], 0.0)
    partial_value = jnp.where(is_atmos, atmos_part, ocean_part)
    surface = lax.psum(partial_value, "gy").astype(jnp.bfloat16).reshape(-1)
    send_source = jnp.where(is_atmos, a2o_source, marine_air_input_index)[0, 0]
    send_weight = jnp.where(is_atmos, a2o_weight, marine_air_piece_factor)[0, 0]
    send_count = jnp.where(is_atmos, a2o_count, marine_air_piece_tally)[0, 0]
    outbound = block_values(surface, send_source, send_weight, send_count)
    landed = partner(outbound, "comp", 0)
    land_target = jnp.where(is_atmos, marine_air_output_index, a2o_target)[0, 0].reshape(-1)
    landing = jnp.zeros((band_rows * columns,), jnp.float32).at[land_target].add(landed.reshape(-1))
    landing = landing.reshape(band_rows, columns)
    forcing = lax.psum(landing, "gy")
    forward, inverse, wave_ids = fourier_tables(columns, groups_x, groups_y)
    latitudes = band_rows * groups_x
    sine_matrix = sine_table(latitudes)
    fourier_cols = forward.reshape(columns, groups_x, -1)
    outgoing = jnp.einsum("rcl,ldj->rdcj", own_slab, fourier_cols, precision=exact_mode)
    incoming = lax.all_to_all(outgoing, "gx", split_axis=1, concat_axis=0, tiled=True)
    wave_cols = incoming.shape[-1]
    my_waves = lax.dynamic_index_in_dim(
        wave_ids.reshape(groups_x, wave_cols), row_group, 0, keepdims=False
    )
    viscous = lax.dynamic_slice_in_dim(diffusivity, first_channel, channels)
    damped = damp(incoming.reshape(latitudes, -1), sine_matrix, viscous, my_waves, columns)
    returning = damped.reshape(latitudes, 1, channels, wave_cols)
    in_bands = lax.all_to_all(returning, "gx", split_axis=0, concat_axis=1, tiled=True)
    harmonic_damping = jnp.einsum(
        "rdcj,djl->rcl",
        in_bands,
        inverse.reshape(groups_x, wave_cols, columns),
        precision=exact_mode,
    )
    atmos_result = harmonic_damping + gain_here[None, :, None] * forcing[:, None, :]
    levels = channels // 2
    wet_here = wet_cells.astype(jnp.float32)
    wet_edge = padded_2(wet_cells.astype(jnp.bfloat16), (("gx", 0),), 1).astype(jnp.float32)
    wet_north = wet_edge[:-2][:, None, None, :]
    wet_south = wet_edge[2:][:, None, None, :]
    wet_west = jnp.roll(wet_here, 1, axis=1)[:, None, None, :]
    wet_east = jnp.roll(wet_here, -1, axis=1)[:, None, None, :]
    wet_full = wet_here[:, None, None, :]
    level_ids = jnp.arange(levels, dtype=jnp.int32)
    top_missing = ((col_group == 0) & (level_ids == 0))[None, None, :, None]
    bottom_missing = ((col_group == groups_y - 1) & (level_ids == levels - 1))[None, None, :, None]
    surface_level = (col_group == 0) & (level_ids == 0)
    tracer_gain = jnp.stack(
        [jnp.where(surface_level, heat_gain, 0.0), jnp.where(surface_level, salt_gain, 0.0)]
    )
    heat_term = tracer_gain[None, :, :, None] * forcing[:, None, None, :]
    tracer = own_slab.reshape(band_rows, 2, levels, columns)
    for ocean_round in range(2):
        padded = padded_2(tracer, (("gx", 0), ("gy", 2)), 1)
        from_north = padded[:-2, :, 1:-1]
        from_south = padded[2:, :, 1:-1]
        upper = jnp.where(top_missing, tracer, padded[1:-1, :, :-2])
        lower = jnp.where(bottom_missing, tracer, padded[1:-1, :, 2:])
        from_west = jnp.roll(tracer, 1, axis=3)
        from_east = jnp.roll(tracer, -1, axis=3)
        inflow = wet_north * (from_north - tracer) + wet_south * (from_south - tracer)
        inflow = inflow + wet_west * (from_west - tracer) + wet_east * (from_east - tracer)
        vertical = upper + lower - 2.0 * tracer
        tracer = wet_full * (
            tracer + spread_rate * (wet_full * inflow) + mixing_rate * vertical + heat_term
        )
    ocean_result = tracer.reshape(band_rows, channels, columns)
    result = jnp.where(is_atmos, atmos_result, ocean_result)
    return result[None]


def solution(mesh):
    in_specs = (
        P("comp", "gx", "gy", None),
        P("gx", None),
        P(),
        P(),
        P(),
        P("gx", "gy", None, None),
        P("gx", "gy", None, None),
        P("gx", "gy"),
        P("gx", "gy", None, None, None),
        P("gx", "gy", None, None),
        P("gx", "gy", None, None),
        P("gx", "gy"),
        P("gx", "gy", None, None, None),
    )
    out_specs = P("comp", "gx", "gy", None)
    return jax.shard_map(local, mesh=mesh, in_specs=in_specs, out_specs=out_specs, check_vma=False)
```

profile of v0, /device:TPU:0, one launch (start us, length us, event | category | flops | bytes accessed | tf_op | source)
XLA Modules:
  0.0 197.6 jit_solution(12578682354553469242)
XLA Ops:
  0.0 0.8 dynamic_slice.16
  0.8 1.4 multiply_reduce_fusion
  2.3 20.8 %psum.14 = bf16[8,1024]{1,0:T(8,128)(2,1)S(1)} all-reduce(f32[8,1024]{1,0:T(8,128)S(1)} %bitcast_select_fusion), channel_id=1, replica_groups=mesh['comp'=2,'gx'=4,'gy'=4] {'gy'}, use_global_device_ids=true, to_apply=%region_1.2 | all-reduce | flops 8192 | bytes 49152 | tf_op jit(solution)/shard_map/psum | solution.py:128
  24.5 0.0 copy-start.14
  24.5 0.0 copy-start.15
  24.5 25.6 %gather_fusion = bf16[4096]{0:T(1024)(128)(2,1)S(1)} fusion(bf16[8192]{0:T(1024)(128)(2,1)S(1)} %bitcast.106, s32[4096]{0:T(1024)S(1)} %fusion.105), kind=kCustom, calls=%fused_computation | custom fusion | bytes 32768 | tf_op jit(solution)/shard_map/gather | solution.py:92
  50.2 0.0 copy-start.6
  50.2 0.6 fusion.96
  50.8 0.1 broadcast_select_fusion.1
  50.9 1.6 collective-permute-start
  52.5 1.3 collective-permute-start.1
  53.8 1.3 collective-permute-start.2
  55.1 4.8 %collective-permute-start.3 = (f32[1,2,16,1024]{3,2,1,0:T(8,128)S(1)}, f32[1,2,16,1024]{3,2,1,0:T(8,128)S(1)}, u32[]{:S(2)}, u32[]{:S(2)}) collective-permute-start(f32[1,2,16,1024]{3,2,1,0:T(8,128)S(1)} %bitcast.116), channel_id=1, source_target_pairs={{0,4},{4,8},{8,12},{1,5},{5,9},{9,13},{2,6},{6,10},{10,14},{3,7},{... | collective-permute-start | bytes 393224 | tf_op jit(solution)/shard_map/ppermute | solution.py:30
  59.9 1.3 collective-permute-start.4
  61.3 21.7 %fusion.40 = f32[8,4,32,256]{3,2,0,1:T(8,128)} fusion(s32[4,256]{1,0:T(4,128)S(1)} %fusion.128, pred[4,256]{1,0:T(4,128)(4,1)S(1)} %fusion.125, f32[1,8,32,1024]{3,2,1,0:T(8,128)S(1)} %copy-done), kind=kOutput, calls=%fused_computation.47 | convolution fusion | flops 3236954112 | bytes 2102272 | tf_op jit(solution)/shard_map/rcl,ldj->rdcj/dot_general | solution.py:142
  83.0 5.2 %all-to-all-start = ((f32[8,4,32,256]{3,2,0,1:T(8,128)}), f32[8,4,32,256]{3,2,0,1:T(8,128)}, u32[]{:S(2)}, u32[]{:S(2)}) async-start(f32[8,4,32,256]{3,2,0,1:T(8,128)} %fusion.40), calls=%async_computation | async-start | bytes 2097152 | tf_op jit(solution)/shard_map/all_to_all | solution.py:143
  88.2 0.1 fusion.170
  88.3 0.1 fusion.169
  88.4 0.0 copy-start.10
  88.4 0.0 copy-start.11
  88.4 0.0 copy-start.16
  88.4 0.0 copy-start.17
  88.4 1.3 fusion.164
  89.8 0.8 fusion.165
  90.7 0.6 iota_add_fusion
  91.4 0.1 multiply_sine_fusion
  91.5 0.7 broadcast_add_fusion
  92.2 0.1 pad_maximum_fusion.22
  92.3 0.5 compare_and_fusion.1
  92.8 0.7 dynamic_slice.13
  93.5 0.6 dynamic_slice.15
  94.1 0.0 collective-permute-done.1
  94.1 0.0 collective-permute-done.2
  94.1 0.0 collective-permute-done.3
  94.2 0.0 collective-permute-done.4
  94.2 0.1 pad_maximum_fusion.21
  94.3 1.3 collective-permute-start.5
  95.6 1.3 collective-permute-start.6
  96.9 0.6 fusion.167
  97.5 0.0 collective-permute-done
  97.5 21.9 %scatter_custom_fusion = f32[8192]{0:T(1024)S(1)} fusion(s32[4096]{0:T(1024)S(1)} %bitcast.119, f32[4096]{0:T(1024)S(1)} %bitcast.123, f32[]{:T(128)} %constant.191.clone.1), kind=kCustom, calls=%fused_computation.143 | custom fusion | flops 4096 | bytes 32772 | tf_op jit(solution)/shard_map/scatter-add | solution.py:135
  119.5 19.0 %psum.15 = f32[8,1024]{1,0:T(8,128)S(1)} all-reduce(f32[8,1024]{1,0:T(8,128)S(1)} %reshape.516), channel_id=1, replica_groups=mesh['comp'=2,'gx'=4,'gy'=4] {'gy'}, use_global_device_ids=true, to_apply=%region_3.4 | all-reduce | flops 8192 | bytes 65536 | tf_op jit(solution)/shard_map/psum | solution.py:137
  138.5 0.0 collective-permute-done.5
  138.5 0.6 copy-done.4
  139.1 0.1 copy-done.5
  139.2 3.5 %fusion.56 = f32[8,2,16,1024]{3,2,1,0:T(8,128)S(1)} fusion(f32[8,2,16,1024]{3,2,1,0:T(8,128)S(1)} %bitcast.111, f32[10,2,1,1024]{3,2,1,0:T(1,128)} %copy-done.5, f32[1,2,16,1024]{3,2,1,0:T(8,128)S(1)} %collective-permute-done.4, f32[1,2,16,1024]{3,2,1,0:T(8,128)S(1)} %collective-permute-done.3, f32[10,2,1,1024]{3,2,1,0:T(1,128)} %copy-done.4, ...), kind=kLoop, calls=%fused_computation.54 | loop fusion | flops 8912896 | bytes 4817056 | tf_op jit(solution)/shard_map/mul | solution.py:187
  142.7 1.3 collective-permute-start.7
  144.0 1.5 collective-permute-start.8
  145.5 1.3 fusion.161
  146.9 0.0 all-to-all-done
  146.9 2.9 %fusion.46 = f32[32,4,8,256]{3,2,1,0:T(8,128)S(1)} fusion(f32[32,256]{1,0:T(8,128)S(1)} %copy-done.7, f32[32]{0:T(128)S(1)} %copy-done.18, s32[32]{0:T(128)S(1)} %copy-done.12, f32[4,8,32,256]{3,2,1,0:T(8,128)} %bitcast.49), kind=kOutput, calls=%fused_computation.50 | convolution fusion | flops 101458944 | bytes 2130176 | tf_op jit(solution)/shard_map/dot_general | solution.py:76
  149.8 0.1 copy.26
  149.9 1.2 convolution_multiply_fusion
  151.1 1.3 copy.28
  152.4 7.2 %all-to-all-start.1 = ((f32[32,1,32,256]{3,2,1,0:T(8,128)}), f32[32,1,32,256]{3,2,1,0:T(8,128)}, u32[]{:S(2)}, u32[]{:S(2)}) async-start(f32[32,1,32,256]{3,2,1,0:T(8,128)} %bitcast.11), calls=%async_computation.1 | async-start | bytes 2097152 | tf_op jit(solution)/shard_map/all_to_all | solution.py:151
  159.6 0.1 pad_maximum_fusion.18
  159.7 1.4 collective-permute-start.10
  161.2 4.6 %collective-permute-start.9 = (f32[10,2,1,1024]{3,2,1,0:T(1,128)S(1)}, f32[10,2,1,1024]{3,2,1,0:T(1,128)S(1)}, u32[]{:S(2)}, u32[]{:S(2)}) collective-permute-start(f32[10,2,1,1024]{3,2,1,0:T(1,128)S(1)} %get-tuple-element.5), channel_id=1, source_target_pairs={{0,1},{1,2},{2,3},{4,5},{5,6},{6,7},{8,9},{9,10},{10,11},{12,13},{... | collective-permute-start | bytes 245768 | tf_op jit(solution)/shard_map/ppermute | solution.py:30
  165.7 0.1 fusion.162
  165.8 0.9 collective-permute-done.10
  166.7 1.7 collective-permute-done.9
  168.4 1.8 fusion.57
  170.2 3.9 %all-to-all-done.1 = f32[32,1,32,256]{3,2,1,0:T(8,128)} async-done(((f32[32,1,32,256]{3,2,1,0:T(8,128)}), f32[32,1,32,256]{3,2,1,0:T(8,128)}, u32[]{:S(2)}, u32[]{:S(2)}) %all-to-all-start.1) | async-done | bytes 1048608 | tf_op jit(solution)/shard_map/all_to_all | solution.py:151
  174.1 23.5 %fusion.53 = f32[1,8,32,1024]{3,2,1,0:T(8,128)} fusion(f32[8,32,1024]{2,1,0:T(8,128)S(1)} %bitcast.114, f32[8,4,32,256]{3,2,0,1:T(8,128)} %bitcast.14, f32[4,256]{1,0:T(4,128)S(1)} %select_multiply_fusion, s32[4,256]{1,0:T(4,128)S(1)} %fusion.128, pred[4,256]{1,0:T(4,128)(4,1)} %copy-done.19, f32[8,1024]{1,0:T(8,128)S(1)} %psum.15, f32[32]{0:T(128)} %dynamic_slice.15, ...), kind=kOutput, calls=%fused_computation.53 | convolution fusion | flops 3238789120 | bytes 3187841 | tf_op jit(solution)/shard_map/rdcj,djl->rcl/dot_general | solution.py:152
  (61 shorter events, 0.5 us)
Async XLA Ops:
  0.0 2.3 %copy-start = (f32[1,8,32,1024]{3,2,1,0:T(8,128)S(1)}, f32[1,8,32,1024]{3,2,1,0:T(8,128)}, u32[]{:S(2)}) copy-start(f32[1,8,32,1024]{3,2,1,0:T(8,128)} %param.13) | copy-start | bytes 3145732
  0.0 24.5 %copy-start.8 = (s32[1,1,32,128]{3,2,1,0:T(8,128)S(1)}, s32[1,1,32,128]{3,2,1,0:T(8,128)}, u32[]{:S(2)}) copy-start(s32[1,1,32,128]{3,2,1,0:T(8,128)} %param.18) | copy-start | bytes 49156
  0.0 24.5 %copy-start.9 = (s32[1,1,32,128]{3,2,1,0:T(8,128)S(1)}, s32[1,1,32,128]{3,2,1,0:T(8,128)}, u32[]{:S(2)}) copy-start(s32[1,1,32,128]{3,2,1,0:T(8,128)} %param.22) | copy-start | bytes 49156
  24.5 25.7 %copy-start.14 = (bf16[1,1,32,128,128]{4,3,2,1,0:T(8,128)(2,1)S(1)}, bf16[1,1,32,128,128]{4,3,2,1,0:T(8,128)(2,1)}, u32[]{:S(2)}) copy-start(bf16[1,1,32,128,128]{4,3,2,1,0:T(8,128)(2,1)} %param.21) | copy-start | bytes 3145732
  24.5 25.7 %copy-start.15 = (bf16[1,1,32,128,128]{4,3,2,1,0:T(8,128)(2,1)S(1)}, bf16[1,1,32,128,128]{4,3,2,1,0:T(8,128)(2,1)}, u32[]{:S(2)}) copy-start(bf16[1,1,32,128,128]{4,3,2,1,0:T(8,128)(2,1)} %param.25) | copy-start | bytes 3145732
  50.2 2.3 %copy-start.6 = (s32[8,1024]{1,0:T(8,128)S(1)}, s32[8,1024]{1,0:T(8,128)}, u32[]{:S(2)}) copy-start(s32[8,1024]{1,0:T(8,128)} %param.14) | copy-start | bytes 98308
  50.9 46.6 %collective-permute-start = (f32[32,128]{1,0:T(8,128)S(1)}, f32[32,128]{1,0:T(8,128)S(1)}, u32[]{:S(2)}, u32[]{:S(2)}) collective-permute-start(f32[32,128]{1,0:T(8,128)S(1)} %broadcast_select_fusion.1), channel_id=1, source_target_pairs={{0,16},{16,0},{1,17},{17,1},{2,18},{18,2},{3,19},{19,3},{4,20},{20... | collective-permute-start | bytes 49160 | tf_op jit(solution)/shard_map/ppermute | solution.py:22
  52.5 41.6 %collective-permute-start.1 = (bf16[1,1024]{1,0:T(2,128)(2,1)S(1)}, bf16[1,1024]{1,0:T(2,128)(2,1)S(1)}, u32[]{:S(2)}, u32[]{:S(2)}) collective-permute-start(bf16[1,1024]{1,0:T(2,128)(2,1)S(1)} %get-tuple-element.29), channel_id=1, source_target_pairs={{0,4},{4,8},{8,12},{1,5},{5,9},{9,13},{2,6},{6,10},{10,14},{3,7},{... | collective-permute-start | bytes 6152 | tf_op jit(solution)/shard_map/ppermute | solution.py:30
  53.8 40.3 %collective-permute-start.2 = (bf16[1,1024]{1,0:T(2,128)(2,1)S(1)}, bf16[1,1024]{1,0:T(2,128)(2,1)S(1)}, u32[]{:S(2)}, u32[]{:S(2)}) collective-permute-start(bf16[1,1024]{1,0:T(2,128)(2,1)S(1)} %get-tuple-element.30), channel_id=1, source_target_pairs={{4,0},{8,4},{12,8},{5,1},{9,5},{13,9},{6,2},{10,6},{14,10},{7,3},{... | collective-permute-start | bytes 6152 | tf_op jit(solution)/shard_map/ppermute | solution.py:33
  55.1 39.0 %collective-permute-start.3 = (f32[1,2,16,1024]{3,2,1,0:T(8,128)S(1)}, f32[1,2,16,1024]{3,2,1,0:T(8,128)S(1)}, u32[]{:S(2)}, u32[]{:S(2)}) collective-permute-start(f32[1,2,16,1024]{3,2,1,0:T(8,128)S(1)} %bitcast.116), channel_id=1, source_target_pairs={{0,4},{4,8},{8,12},{1,5},{5,9},{9,13},{2,6},{6,10},{10,14},{3,7},{... | collective-permute-start | bytes 393224 | tf_op jit(solution)/shard_map/ppermute | solution.py:30
  59.9 34.3 %collective-permute-start.4 = (f32[1,2,16,1024]{3,2,1,0:T(8,128)S(1)}, f32[1,2,16,1024]{3,2,1,0:T(8,128)S(1)}, u32[]{:S(2)}, u32[]{:S(2)}) collective-permute-start(f32[1,2,16,1024]{3,2,1,0:T(8,128)S(1)} %bitcast.115), channel_id=1, source_target_pairs={{4,0},{8,4},{12,8},{5,1},{9,5},{13,9},{6,2},{10,6},{14,10},{7,3},{... | collective-permute-start | bytes 393224 | tf_op jit(solution)/shard_map/ppermute | solution.py:33
  61.2 21.7 %copy-start.19 = (pred[4,256]{1,0:T(4,128)(4,1)}, pred[4,256]{1,0:T(4,128)(4,1)S(1)}, u32[]{:S(2)}) copy-start(pred[4,256]{1,0:T(4,128)(4,1)S(1)} %fusion.125) | copy-start | bytes 3076
  83.0 63.9 %all-to-all-start = ((f32[8,4,32,256]{3,2,0,1:T(8,128)}), f32[8,4,32,256]{3,2,0,1:T(8,128)}, u32[]{:S(2)}, u32[]{:S(2)}) async-start(f32[8,4,32,256]{3,2,0,1:T(8,128)} %fusion.40), calls=%async_computation | async-start | bytes 2097152 | tf_op jit(solution)/shard_map/all_to_all | solution.py:143
  88.4 3.0 %copy-start.10 = (s32[1,1,32,128]{3,2,1,0:T(8,128)S(1)}, s32[1,1,32,128]{3,2,1,0:T(8,128)}, u32[]{:S(2)}) copy-start(s32[1,1,32,128]{3,2,1,0:T(8,128)} %param.23) | copy-start | bytes 49156
  88.4 3.0 %copy-start.11 = (s32[1,1,32,128]{3,2,1,0:T(8,128)S(1)}, s32[1,1,32,128]{3,2,1,0:T(8,128)}, u32[]{:S(2)}) copy-start(s32[1,1,32,128]{3,2,1,0:T(8,128)} %param.19) | copy-start | bytes 49156
  88.4 4.4 %copy-start.16 = (f32[128]{0:T(128)S(1)}, f32[128]{0:T(128)}, u32[]{:S(2)}) copy-start(f32[128]{0:T(128)} %param.17) | copy-start | bytes 1540
  88.4 5.0 %copy-start.17 = (f32[128]{0:T(128)S(1)}, f32[128]{0:T(128)}, u32[]{:S(2)}) copy-start(f32[128]{0:T(128)} %param.16) | copy-start | bytes 1540
  94.3 44.2 %collective-permute-start.5 = (f32[10,2,1,1024]{3,2,1,0:T(1,128)S(1)}, f32[10,2,1,1024]{3,2,1,0:T(1,128)S(1)}, u32[]{:S(2)}, u32[]{:S(2)}) collective-permute-start(f32[10,2,1,1024]{3,2,1,0:T(1,128)S(1)} %get-tuple-element.7), channel_id=1, source_target_pairs={{0,1},{1,2},{2,3},{4,5},{5,6},{6,7},{8,9},{9,10},{10,11},{12,13},{... | collective-permute-start | bytes 245768 | tf_op jit(solution)/shard_map/ppermute | solution.py:30
  95.6 42.9 %collective-permute-start.6 = (f32[10,2,1,1024]{3,2,1,0:T(1,128)S(1)}, f32[10,2,1,1024]{3,2,1,0:T(1,128)S(1)}, u32[]{:S(2)}, u32[]{:S(2)}) collective-permute-start(f32[10,2,1,1024]{3,2,1,0:T(1,128)S(1)} %get-tuple-element.8), channel_id=1, source_target_pairs={{1,0},{2,1},{3,2},{5,4},{6,5},{7,6},{9,8},{10,9},{11,10},{13,12},{... | collective-permute-start | bytes 245768 | tf_op jit(solution)/shard_map/ppermute | solution.py:33
  138.5 0.6 copy-start.4
  138.5 0.7 copy-start.5
  142.7 16.9 %collective-permute-start.7 = (f32[1,2,16,1024]{3,2,1,0:T(8,128)S(1)}, f32[1,2,16,1024]{3,2,1,0:T(8,128)S(1)}, u32[]{:S(2)}, u32[]{:S(2)}) collective-permute-start(f32[1,2,16,1024]{3,2,1,0:T(8,128)S(1)} %get-tuple-element.13), channel_id=1, source_target_pairs={{0,4},{4,8},{8,12},{1,5},{5,9},{9,13},{2,6},{6,10},{10,14},{3,7},{... | collective-permute-start | bytes 393224 | tf_op jit(solution)/shard_map/ppermute | solution.py:30
  144.0 2.8 %copy-start.7 = (f32[32,256]{1,0:T(8,128)S(1)}, f32[32,256]{1,0:T(8,128)}, u32[]{:S(2)}) copy-start(f32[32,256]{1,0:T(8,128)} %broadcast_add_fusion) | copy-start | bytes 98308
  144.0 2.8 %copy-start.12 = (s32[32]{0:T(128)S(1)}, s32[32]{0:T(128)}, u32[]{:S(2)}) copy-start(s32[32]{0:T(128)} %iota_add_fusion) | copy-start | bytes 388
  144.0 2.8 %copy-start.18 = (f32[32]{0:T(128)S(1)}, f32[32]{0:T(128)}, u32[]{:S(2)}) copy-start(f32[32]{0:T(128)} %dynamic_slice.13) | copy-start | bytes 388
  144.0 15.5 %collective-permute-start.8 = (f32[1,2,16,1024]{3,2,1,0:T(8,128)S(1)}, f32[1,2,16,1024]{3,2,1,0:T(8,128)S(1)}, u32[]{:S(2)}, u32[]{:S(2)}) collective-permute-start(f32[1,2,16,1024]{3,2,1,0:T(8,128)S(1)} %get-tuple-element.14), channel_id=1, source_target_pairs={{4,0},{8,4},{12,8},{5,1},{9,5},{13,9},{6,2},{10,6},{14,10},{7,3},{... | collective-permute-start | bytes 393224 | tf_op jit(solution)/shard_map/ppermute | solution.py:33
  152.4 21.7 %all-to-all-start.1 = ((f32[32,1,32,256]{3,2,1,0:T(8,128)}), f32[32,1,32,256]{3,2,1,0:T(8,128)}, u32[]{:S(2)}, u32[]{:S(2)}) async-start(f32[32,1,32,256]{3,2,1,0:T(8,128)} %bitcast.11), calls=%async_computation.1 | async-start | bytes 2097152 | tf_op jit(solution)/shard_map/all_to_all | solution.py:151
  159.6 8.8 %copy-start.1 = (f32[8,2,16,1023]{3,2,1,0:T(8,128)S(1)}, f32[8,2,16,1023]{3,2,1,0:T(8,128)}, u32[]{:S(2)}) copy-start(f32[8,2,16,1023]{3,2,1,0:T(8,128)} %get-tuple-element.10) | copy-start | bytes 3142660
  159.6 8.8 %copy-start.2 = (f32[8,1024]{1,0:T(8,128)S(1)}, f32[8,1024]{1,0:T(8,128)}, u32[]{:S(2)}) copy-start(f32[8,1024]{1,0:T(8,128)} %get-tuple-element.21) | copy-start | bytes 98308
  159.6 8.8 %copy-start.3 = (f32[8,1024]{1,0:T(8,128)S(1)}, f32[8,1024]{1,0:T(8,128)}, u32[]{:S(2)}) copy-start(f32[8,1024]{1,0:T(8,128)} %get-tuple-element.22) | copy-start | bytes 98308
  159.6 8.8 %copy-start.13 = (pred[16]{0:T(512)(128)(4,1)S(1)}, pred[16]{0:T(512)(128)(4,1)}, u32[]{:S(2)}) copy-start(pred[16]{0:T(512)(128)(4,1)} %compare_and_fusion.1) | copy-start | bytes 52
  159.7 7.0 %collective-permute-start.10 = (f32[10,2,1,1024]{3,2,1,0:T(1,128)S(1)}, f32[10,2,1,1024]{3,2,1,0:T(1,128)S(1)}, u32[]{:S(2)}, u32[]{:S(2)}) collective-permute-start(f32[10,2,1,1024]{3,2,1,0:T(1,128)S(1)} %get-tuple-element.6), channel_id=1, source_target_pairs={{1,0},{2,1},{3,2},{5,4},{6,5},{7,6},{9,8},{10,9},{11,10},{13,12},{... | collective-permute-start | bytes 245768 | tf_op jit(solution)/shard_map/ppermute | solution.py:33
  161.2 7.2 %collective-permute-start.9 = (f32[10,2,1,1024]{3,2,1,0:T(1,128)S(1)}, f32[10,2,1,1024]{3,2,1,0:T(1,128)S(1)}, u32[]{:S(2)}, u32[]{:S(2)}) collective-permute-start(f32[10,2,1,1024]{3,2,1,0:T(1,128)S(1)} %get-tuple-element.5), channel_id=1, source_target_pairs={{0,1},{1,2},{2,3},{4,5},{5,6},{6,7},{8,9},{9,10},{10,11},{12,13},{... | collective-permute-start | bytes 245768 | tf_op jit(solution)/shard_map/ppermute | solution.py:30
where the time goes:
time: 198 us
  matrix products  49.9 us (25%)
  blocking collectives  39.8 us (20%)
  local copies, waits for them, and re-layouts  34.3 us (17%)
  starting transfers between devices  33.9 us (17%)
  other arithmetic  31.3 us (16%)
  waiting for transfers between devices  6.52 us (3%)
    gather x1, local copies, waits for them, and re-layouts, block_values(): gathered = surface[source]  25.6 us
    dot_general x1, matrix products, local(): jnp.einsum('rdcj,djl->rcl', in_bands, inverse.reshape(groups_x, wave_cols...  23.5 us
    scatter-add x1, other arithmetic, local(): jnp.zeros((band_rows * columns,), jnp.float32).at[land_target]  21.9 us
    dot_general x1, matrix products, local(): jnp.einsum('rcl,ldj->rdcj', own_slab, fourier_cols, precision=exact_mode)  21.7 us
    psum x1, blocking collectives, local(): surface = lax.psum(partial_value, 'gy').astype(jnp.bfloat16).reshape(-1)  20.8 us
    psum x1, blocking collectives, local(): forcing = lax.psum(landing, 'gy')  19 us
    ppermute x5, starting transfers between devices, padded_2(): lax.ppermute(lax.slice_in_dim(block, block.shape[dim] - width, None, axis...  13.2 us
    all_to_all x1, starting transfers between devices, local(): lax.all_to_all(returning, 'gx', split_axis=0, concat_axis=1, tiled=True)  7.18 us
  transfers between devices with their start and end apart: 13, of which 3 were waited for; matrix products, arithmetic and copies ran while one was open for 32% of the time, Pallas kernels for 0%

commit v1 on v0

v1 whole, which is shorter than its diff:
```python
import functools

import jax
import jax.numpy as jnp
import numpy as np
from jax import lax
from jax.experimental import pallas as pl
from jax.experimental.pallas import tpu as pltpu
from jax.sharding import PartitionSpec as P

spread_rate = 0.2
mixing_rate = 0.1
heat_gain = 0.5
salt_gain = -0.25
LANES = 128
f32 = jnp.float32
bf16 = jnp.bfloat16


def fourier_tables(columns):
    waves = np.arange(columns // 2)
    phase = np.arange(columns)[:, None] * waves[None, :] % columns
    angles = phase * (2.0 * np.pi / columns)
    forward = np.concatenate([np.cos(angles), np.sin(angles)], axis=1)
    weight = np.where(np.arange(columns) % (columns // 2) == 0, 1.0, 2.0) / columns
    inverse = forward.T * weight[:, None]
    half_rates = 2.0 * np.sin(np.pi * waves / columns) ** 2
    return (
        jnp.asarray(forward.astype(np.float32), bf16),
        jnp.asarray(inverse.astype(np.float32), bf16),
        jnp.asarray(half_rates[None, :].astype(np.float32)),
    )


def chain_pairs(count, odd):
    return [(low, low + 1) for low in range(odd, count - 1, 2)]


def both_ways(pairs):
    return [p for a, b in pairs for p in ((a, b), (b, a))]


def channel_column(row, channels, first):
    n = row.shape[1]
    lane = lax.broadcasted_iota(jnp.int32, (channels, n), 1)
    sub = lax.broadcasted_iota(jnp.int32, (channels, n), 0)
    return jnp.sum(jnp.where(lane == sub + first, row, 0.0), axis=1, keepdims=True)


def to_tiles(surface):
    cols = surface.shape[1]
    return jnp.concatenate(
        [surface[:, k : k + LANES] for k in range(0, cols, LANES)], axis=0
    )


def from_tiles(tiles, rows):
    return jnp.concatenate(
        [tiles[k : k + rows] for k in range(0, tiles.shape[0], rows)], axis=1
    )


def surface_kernel(x_ref, flux_ref, s_ref, row_ref):
    _, rows, channels, columns = x_ref.shape
    col_group = lax.axis_index("gy")
    is_atmos = lax.axis_index("comp") == 0

    @pl.when(is_atmos)
    def _():
        weight = channel_column(flux_ref[...], channels, col_group * channels)
        for r in range(rows):
            row_ref[r : r + 1, :] = jnp.sum(x_ref[0, r] * weight, axis=0, keepdims=True)
        s_ref[...] = to_tiles(row_ref[...]).astype(bf16)

    @pl.when(jnp.logical_not(is_atmos))
    def _():
        gain = jnp.where(col_group == 0, 1.0, 0.0)
        for r in range(rows):
            row_ref[r : r + 1, :] = x_ref[0, r, 0:1, :] * gain
        s_ref[...] = to_tiles(row_ref[...]).astype(bf16)


def decay_terms(diff_column, half_rates):
    half = 0.5 / diff_column + half_rates
    sinh = jnp.sqrt(half * (half + 2.0))
    grow = 1.0 + half + sinh
    return 1.0 / grow, jnp.log(grow), sinh


def forward_kernel(
    groups_x, x_ref, wet_ref, diff_ref, rates_ref, table_ref, *refs, xor_masks
):
    msgs = len(xor_masks)
    y_ref, e1_ref, e3_ref, e2_ref, e4_ref = refs[:5]
    pq_ref = refs[5] if not xor_masks else None
    edge_ref = refs[-1]
    _, rows, channels, columns = x_ref.shape
    waves = columns // 2
    row_group = lax.axis_index("gx")
    col_group = lax.axis_index("gy")
    is_atmos = lax.axis_index("comp") == 0

    @pl.when(is_atmos)
    def _():
        step = 256
        flat = x_ref[0].astype(bf16).reshape(rows * channels, columns)
        for n in range(0, columns, step):
            part = jnp.dot(flat, table_ref[:, n : n + step], preferred_element_type=f32)
            y_ref[:, :, n : n + step] = part.reshape(rows, channels, step)
        diff = channel_column(diff_ref[...], channels, col_group * channels)
        total = rows * groups_x
        base = (row_group * rows).astype(f32)
        for n in range(0, waves, LANES):
            lam, alpha, _ = decay_terms(diff, rates_ref[:, n : n + LANES])
            lam2 = lam * lam
            low = jnp.exp(-2.0 * base * alpha)
            high = jnp.exp(-2.0 * (total - rows - base) * alpha)
            for part in (n, n + waves):
                power = low
                p = jnp.zeros((channels, LANES), f32)
                for r in range(rows):
                    power = power * lam2
                    p = lam * p + (1.0 - power) * y_ref[r, :, part : part + LANES]
                power = high
                q = jnp.zeros((channels, LANES), f32)
                for r in reversed(range(rows)):
                    power = power * lam2
                    q = lam * q + (1.0 - power) * y_ref[r, :, part : part + LANES]
                if xor_masks:
                    for mask, out in zip((1, 2, 3), (e1_ref, e2_ref, e3_ref)):
                        if mask in xor_masks:
                            upward = row_group < (row_group ^ mask)
                            out[0:channels, part : part + LANES] = jnp.where(
                                upward, p, q
                            ).astype(bf16)
                else:
                    pq_ref[0, :, part : part + LANES] = p.astype(bf16)
                    pq_ref[1, :, part : part + LANES] = q.astype(bf16)

    @pl.when(jnp.logical_not(is_atmos))
    def _():
        levels = channels // 2
        even_x = row_group % 2 == 0
        even_y = col_group % 2 == 0
        wet = wet_ref[...].astype(f32)
        wet = jnp.concatenate([wet, wet], axis=0).astype(bf16)
        lines = 2 * channels

        def put(out, bottom):
            @pl.when(bottom)
            def _():
                out[0:lines, :] = x_ref[0, rows - 2 :].reshape(lines, columns).astype(bf16)

            @pl.when(jnp.logical_not(bottom))
            def _():
                out[0:lines, :] = x_ref[0, :2].reshape(lines, columns).astype(bf16)

            out[lines : lines + 16, :] = wet

        put(e1_ref, even_x)
        put(e3_ref, jnp.logical_not(even_x))

        def put_edges(out, bottom):
            @pl.when(bottom)
            def _():
                for r in range(rows):
                    for t in range(2):
                        at = (r * 2 + t) * 2
                        c = t * levels + levels - 2
                        edge_ref[at : at + 2, :] = x_ref[0, r, c : c + 2, :]

            @pl.when(jnp.logical_not(bottom))
            def _():
                for r in range(rows):
                    for t in range(2):
                        at = (r * 2 + t) * 2
                        c = t * levels
                        edge_ref[at : at + 2, :] = x_ref[0, r, c : c + 2, :]

            out[0 : rows * 4, :] = edge_ref[...].astype(bf16)

        put_edges(e2_ref, even_y)
        put_edges(e4_ref, jnp.logical_not(even_y))


def regrid_kernel(n_msgs, *refs):
    msgs = refs[:n_msgs]
    (
        a_src, a_dst, a_count, a_weight, m_src, m_dst, m_count, m_weight,
        e1_ref, e3_ref, e2_in, e4_in,
        land_ref, e2_ref, e4_ref,
        weight_ref, hot_ref, gath_ref, val_ref, tail_ref, sem,
    ) = refs[n_msgs:]
    is_atmos = lax.axis_index("comp") == 0
    blocks, points = val_ref.shape
    cells = msgs[0].shape[0]
    rows = 8

    @pl.when(is_atmos)
    def _():
        pltpu.make_async_copy(m_weight.at[0, 0], weight_ref, sem).start()

    @pl.when(jnp.logical_not(is_atmos))
    def _():
        pltpu.make_async_copy(a_weight.at[0, 0], weight_ref, sem).start()

    src = jnp.where(is_atmos, m_src[0, 0], a_src[0, 0])
    dst = jnp.where(is_atmos, m_dst[0, 0], a_dst[0, 0])
    count = jnp.where(is_atmos, m_count[0, 0], a_count[0, 0])
    tiles = cells // rows

    def split(index):
        row = index // (tiles * LANES)
        tile = (index // LANES) % tiles
        return tile * rows + row, index % LANES

    src_row, src_lane = split(src)
    dst_row, dst_lane = split(dst)
    lane_iota = lax.broadcasted_iota(jnp.int32, (LANES, points), 0)
    row_iota = lax.broadcasted_iota(jnp.int32, (cells, points), 0)
    table = msgs[0][...].astype(f32)
    for m in msgs[1:]:
        table = table + m[...].astype(f32)
    table = table.astype(bf16)
    for b in range(blocks):
        hot = jnp.where(lane_iota == src_lane[b : b + 1], 1.0, 0.0).astype(bf16)
        picked = jnp.dot(table, hot, preferred_element_type=f32)
        picked = jnp.where(row_iota == src_row[b : b + 1], picked, 0.0)
        gath_ref[b : b + 1, :] = jnp.sum(picked, axis=0, keepdims=True)
    gathered = gath_ref[...].astype(bf16)

    @pl.when(is_atmos)
    def _():
        pltpu.make_async_copy(m_weight.at[0, 0], weight_ref, sem).wait()

    @pl.when(jnp.logical_not(is_atmos))
    def _():
        pltpu.make_async_copy(a_weight.at[0, 0], weight_ref, sem).wait()

    block_iota = lax.broadcasted_iota(jnp.int32, (blocks, points), 0)
    values = jnp.zeros((blocks, points), f32)
    for b in range(blocks):
        term = lax.dot_general(
            gathered, weight_ref[b], (((1,), (1,)), ((), ())), preferred_element_type=f32
        )
        values = jnp.where(block_iota == b, term, values)
    val_ref[...] = jnp.where(block_iota < count, values, 0.0)
    land = jnp.zeros((2 * cells, LANES), f32)
    for b in range(blocks):
        value = val_ref[b : b + 1, :]
        coarse = value.astype(bf16).astype(f32)
        fine = value - coarse
        mine = row_iota == dst_row[b : b + 1]
        both = jnp.concatenate(
            [jnp.where(mine, coarse, 0.0), jnp.where(mine, fine, 0.0)], axis=0
        ).astype(bf16)
        hot = jnp.where(lane_iota == dst_lane[b : b + 1], 1.0, 0.0).astype(bf16)
        land = land + lax.dot_general(
            both, hot, (((1,), (1,)), ((), ())), preferred_element_type=f32
        )
    land_ref[...] = land[:cells] + land[cells:]

    @pl.when(is_atmos)
    def _():
        e2_ref[...] = e2_in[...]
        e4_ref[...] = e4_in[...]

    @pl.when(jnp.logical_not(is_atmos))
    def _():
        row_group = lax.axis_index("gx")
        col_group = lax.axis_index("gy")
        own = e2_in.shape[0] - 16
        channels = (e1_ref.shape[0] - 16) // 2
        levels = channels // 2
        even_x = row_group % 2 == 0
        lower = jnp.where(
            even_x, e3_ref[channels : 2 * channels, :].astype(f32),
            e1_ref[channels : 2 * channels, :].astype(f32),
        )
        upper = jnp.where(
            even_x, e1_ref[0:channels, :].astype(f32), e3_ref[0:channels, :].astype(f32)
        )
        even_y = col_group % 2 == 0

        def fill(out, inn, bottom):
            for line, values in enumerate((lower, upper)):
                for t in range(2):
                    at = (line * 2 + t) * 2
                    c = t * levels
                    tail_ref[at : at + 2, :] = jnp.where(
                        bottom, values[c + levels - 2 : c + levels], values[c : c + 2]
                    )
            out[0:own, :] = inn[0:own, :]
            tail = tail_ref[...]
            out[own : own + 16, :] = jnp.concatenate([tail, tail], axis=0).astype(bf16)

        fill(e2_ref, e2_in, even_y)
        fill(e4_ref, e4_in, jnp.logical_not(even_y))


def final_kernel(groups_x, groups_y, n_land, xor_masks, *refs):
    (
        x_ref, wet_ref, diff_ref, gain_ref, rates_ref, table_ref, y_ref,
        e1_ref, e3_ref, e2_ref, e4_ref, hsum_ref, ha_ref, hb_ref,
    ) = refs[:14]
    coupling = (e1_ref, e2_ref, e3_ref)
    at = 14
    if not xor_masks:
        pin_ref, qin_ref = refs[14:16]
        at = 16
    out_ref, z_ref, zb_ref, t0_ref, t1_ref, w_ref, c_ref, h_ref = refs[at:]
    _, rows, channels, columns = x_ref.shape
    waves = columns // 2
    row_group = lax.axis_index("gx")
    col_group = lax.axis_index("gy")
    is_atmos = lax.axis_index("comp") == 0

    @pl.when(is_atmos)
    def _():
        diff = channel_column(diff_ref[...], channels, col_group * channels)
        total = rows * groups_x
        base = (row_group * rows).astype(f32)
        for n in range(0, waves, LANES):
            lam, alpha, sinh = decay_terms(diff, rates_ref[:, n : n + LANES])
            lam2 = lam * lam
            low = jnp.exp(-2.0 * base * alpha)
            high = jnp.exp(-2.0 * (total - rows - base) * alpha)
            scale = 1.0 / (
                2.0 * diff * sinh * (1.0 - jnp.exp(-2.0 * (total + 1) * alpha))
            )
            lows, highs = [], []
            power = low
            for r in range(rows):
                power = power * lam2
                lows.append(1.0 - power)
            power = high
            for r in range(rows):
                power = power * lam2
                highs.append((1.0 - power))
            highs = highs[::-1]
            for part in (n, n + waves):
                lanes = slice(part, part + LANES)
                if xor_masks:
                    pin = jnp.zeros((channels, LANES), f32)
                    qin = jnp.zeros((channels, LANES), f32)
                    for mask in xor_masks:
                        other = row_group ^ mask
                        gap = (jnp.abs(row_group - other) - 1) * rows
                        term = jnp.exp(-gap.astype(f32) * alpha)
                        term = term * coupling[mask - 1][0:channels, lanes].astype(f32)
                        pin = pin + jnp.where(other < row_group, term, 0.0)
                        qin = qin + jnp.where(other > row_group, term, 0.0)
                else:
                    pin = pin_ref[:, lanes]
                    qin = qin_ref[:, lanes]
                f = pin
                for r in range(rows):
                    f = lam * f + lows[r] * y_ref[r, :, lanes]
                    z_ref[r, :, 0:LANES] = highs[r] * f
                g = lam * qin
                for r in reversed(range(rows)):
                    z = scale * (z_ref[r, :, 0:LANES] + lows[r] * g)
                    zb_ref[r * channels : (r + 1) * channels, lanes] = z.astype(bf16)
                    g = lam * (g + highs[r] * y_ref[r, :, lanes])
        response = channel_column(gain_ref[...], channels, col_group * channels)
        forcing = from_tiles(hsum_ref[...], rows)
        step = 256
        for n in range(0, columns, step):
            part = jnp.dot(
                zb_ref[...], table_ref[:, n : n + step], preferred_element_type=f32
            ).reshape(rows, channels, step)
            for r in range(rows):
                out_ref[0, r, :, n : n + step] = (
                    part[r] + response * forcing[r : r + 1, n : n + step]
                )

    @pl.when(jnp.logical_not(is_atmos))
    def _():
        levels = channels // 2
        ring = levels + 8
        lines = 2 * channels
        even_x = row_group % 2 == 0
        even_y = col_group % 2 == 0
        first_x = row_group == 0
        last_x = row_group == groups_x - 1
        top = col_group == 0
        bottom = col_group == groups_y - 1

        m1 = e1_ref[lines : lines + 16, :].astype(f32)
        m3 = e3_ref[lines : lines + 16, :].astype(f32)
        below = jnp.where(even_x, m3, m1)[rows - 2 : rows]
        above = jnp.where(even_x, m1, m3)[0:2]
        w_ref[0:2, :] = jnp.where(first_x, 0.0, below)
        w_ref[2 : rows + 2, :] = wet_ref[...].astype(f32)
        w_ref[rows + 2 : rows + 4, :] = jnp.where(last_x, 0.0, above)

        surface = jnp.where(top, 1.0, 0.0)
        own = from_tiles(hsum_ref[...], rows)
        ha = from_tiles(ha_ref[...].astype(f32), rows)
        hb = from_tiles(hb_ref[...].astype(f32), rows)
        h_ref[0:1, :] = jnp.where(even_x, hb, ha)[rows - 1 : rows]
        h_ref[1 : rows + 1, :] = own
        h_ref[rows + 1 : rows + 2, :] = jnp.where(even_x, ha, hb)[0:1]

        span = rows + 2
        north = w_ref[0:span, :]
        here = w_ref[1 : span + 1, :]
        south = w_ref[2 : span + 2, :]
        west = pltpu.roll(here, 1, 1)
        east = pltpu.roll(here, columns - 1, 1)
        c_ref[0, 0:span, :] = here * (
            1.0 - 2.0 * mixing_rate - spread_rate * (north + south + west + east)
        )
        c_ref[1, 0:span, :] = spread_rate * here * north
        c_ref[2, 0:span, :] = spread_rate * here * south
        c_ref[3, 0:span, :] = spread_rate * here * west
        c_ref[4, 0:span, :] = spread_rate * here * east
        c_ref[5, 0:span, :] = mixing_rate * here
        h_ref[0:span, :] = surface * here * h_ref[0:span, :]

        e1 = e1_ref[0:lines, :].astype(f32)
        e3 = e3_ref[0:lines, :].astype(f32)
        below = jnp.where(even_x, e3, e1)
        above = jnp.where(even_x, e1, e3)
        for k in range(2):
            for t in range(2):
                c = k * channels + t * levels
                t0_ref[k, t, 0:levels, :] = below[c : c + levels]
                t0_ref[rows + 2 + k, t, 0:levels, :] = above[c : c + levels]
                t0_ref[k, t, levels:ring, :] = jnp.zeros((8, columns), f32)
                t0_ref[rows + 2 + k, t, levels:ring, :] = jnp.zeros((8, columns), f32)
        for r in range(rows):
            for t in range(2):
                t0_ref[r + 2, t, 0:levels, :] = x_ref[0, r, t * levels : (t + 1) * levels, :]
                t0_ref[r + 2, t, levels:ring, :] = jnp.zeros((8, columns), f32)
        e2 = e2_ref[...].astype(f32)
        e4 = e4_ref[...].astype(f32)
        before = jnp.where(even_y, e4, e2)
        after = jnp.where(even_y, e2, e4)
        for r in range(-1, rows + 1):
            place = {-1: rows, rows: rows + 1}.get(r, r)
            for t in range(2):
                k = (place * 2 + t) * 2
                t0_ref[r + 2, t, levels : levels + 2, :] = after[k : k + 2]
                t0_ref[r + 2, t, ring - 2 : ring, :] = before[k : k + 2]

        def close(ref, r):
            for t in range(2):
                ref[r, t, ring - 1 : ring, :] = jnp.where(
                    top, ref[r, t, 0:1, :], ref[r, t, ring - 1 : ring, :]
                )
                ref[r, t, levels : levels + 1, :] = jnp.where(
                    bottom, ref[r, t, levels - 1 : levels, :], ref[r, t, levels : levels + 1, :]
                )

        gains = (heat_gain, salt_gain)

        def advance(ref, r, t, coefs, size):
            whole = ref[r, t]
            up = pltpu.roll(whole, 1, 0)[:size]
            down = pltpu.roll(whole, ring - 1, 0)[:size]
            mid = whole[:size]
            total = coefs[0] * mid + coefs[5] * (up + down)
            total = total + coefs[1] * ref[r - 1, t, 0:size, :]
            total = total + coefs[2] * ref[r + 1, t, 0:size, :]
            total = total + coefs[3] * pltpu.roll(mid, 1, 1)
            return total + coefs[4] * pltpu.roll(mid, columns - 1, 1)

        def first(r, carry):
            coefs = [c_ref[k, pl.ds(r, 1), :] for k in range(6)]
            close(t0_ref, r + 1)
            heat = h_ref[pl.ds(r, 1), :]
            for t in range(2):
                t1_ref[r, t] = advance(t0_ref, r + 1, t, coefs, ring)
                t1_ref[r, t, 0:1, :] = t1_ref[r, t, 0:1, :] + gains[t] * heat
            close(t1_ref, r)
            return carry

        lax.fori_loop(0, span, first, 0)

        def second(r, carry):
            coefs = [c_ref[k, pl.ds(r, 1), :] for k in range(6)]
            heat = h_ref[pl.ds(r, 1), :]
            for t in range(2):
                c = t * levels
                out_ref[0, r - 1, c : c + levels, :] = advance(t1_ref, r, t, coefs, levels)
                out_ref[0, r - 1, c : c + 1, :] = (
                    out_ref[0, r - 1, c : c + 1, :] + gains[t] * heat
                )
            return carry

        lax.fori_loop(1, span - 1, second, 0)


def local(
    fields,
    wet_cells,
    flux_weight,
    variable_sea_response,
    diffusivity,
    a2o_source,
    a2o_target,
    a2o_count,
    a2o_weight,
    marine_air_input_index,
    marine_air_output_index,
    marine_air_piece_tally,
    marine_air_piece_factor,
):
    _, rows, channels, columns = fields.shape
    groups_x = lax.axis_size("gx")
    groups_y = lax.axis_size("gy")
    blocks, points = a2o_source.shape[2:]
    cells = rows * columns // LANES
    waves = columns // 2
    forward, inverse, half_rates = fourier_tables(columns)
    flux_row = flux_weight[None, :]
    gain_row = variable_sea_response[None, :]
    diff_row = diffusivity[None, :]
    xor_masks = tuple(range(1, groups_x)) if groups_x in (2, 4) else ()
    params = functools.partial(pltpu.CompilerParams, vmem_limit_bytes=40 * 2**20)
    vmem = pl.BlockSpec(memory_space=pltpu.VMEM)
    smem = pl.BlockSpec(memory_space=pltpu.SMEM)
    anywhere = pl.BlockSpec(memory_space=pl.ANY)

    def shape(dims, dtype):
        return jax.ShapeDtypeStruct(dims, dtype)

    partial_surface = pl.pallas_call(
        surface_kernel,
        out_shape=shape((cells, LANES), bf16),
        in_specs=[vmem, vmem],
        out_specs=vmem,
        scratch_shapes=[pltpu.VMEM((rows, columns), f32)],
        compiler_params=params(),
        name="surface_partials",
    )(fields, flux_row)
    surfaces = []
    for mask in range(groups_y):
        route = []
        for j in range(groups_y):
            route += both_ways([(j, groups_y + (j ^ mask))])
        surfaces.append(lax.ppermute(partial_surface, ("comp", "gy"), route))

    lines = 2 * channels + 16
    edges = 4 * rows + 16
    shapes = [
        shape((rows, channels, columns), f32),
        shape((lines, columns), bf16),
        shape((lines, columns), bf16),
        shape((edges, columns), bf16),
        shape((edges, columns), bf16),
    ]
    if not xor_masks:
        shapes.append(shape((2, channels, columns), bf16))
    spectral = pl.pallas_call(
        functools.partial(forward_kernel, groups_x, xor_masks=xor_masks),
        out_shape=shapes,
        in_specs=[vmem] * 5,
        out_specs=[vmem] * len(shapes),
        scratch_shapes=[pltpu.VMEM((4 * rows, columns), f32)],
        compiler_params=params(),
        name="forward_and_halos",
    )(fields, wet_cells, diff_row, half_rates, forward)
    y, e1, e3, e2, e4 = spectral[:5]

    def gx_route(odd):
        pairs = [(groups_x + a, groups_x + b) for a, b in chain_pairs(groups_x, odd)]
        mask = 3 if odd else 1
        if mask in xor_masks:
            pairs += [(a, a ^ mask) for a in range(groups_x) if a < a ^ mask]
        return both_ways(pairs)

    e1 = lax.ppermute(e1, ("comp", "gx"), gx_route(0))
    e3 = lax.ppermute(e3, ("comp", "gx"), gx_route(1))

    landing, e2, e4 = pl.pallas_call(
        functools.partial(regrid_kernel, groups_y),
        out_shape=[
            shape((cells, LANES), f32),
            shape((edges, columns), bf16),
            shape((edges, columns), bf16),
        ],
        in_specs=[vmem] * groups_y
        + [vmem, vmem, smem, anywhere, vmem, vmem, smem, anywhere]
        + [vmem] * 4,
        out_specs=[vmem] * 3,
        scratch_shapes=[
            pltpu.VMEM((blocks, points, points), bf16),
            pltpu.VMEM((LANES, points), bf16),
            pltpu.VMEM((blocks, points), f32),
            pltpu.VMEM((blocks, points), f32),
            pltpu.VMEM((8, columns), f32),
            pltpu.SemaphoreType.DMA,
        ],
        compiler_params=params(),
        name="regrid_blocks",
    )(
        *surfaces,
        a2o_source, a2o_target, a2o_count, a2o_weight,
        marine_air_input_index, marine_air_output_index,
        marine_air_piece_tally, marine_air_piece_factor,
        e1, e3, e2, e4,
    )
    sent = landing.astype(bf16)
    parts = [
        lax.ppermute(sent, "gy", [(j, j ^ mask) for j in range(groups_y)])
        for mask in range(1, groups_y)
    ]
    surface_sum = landing
    for part in parts:
        surface_sum = surface_sum + part.astype(f32)

    axes = ("comp", "gx", "gy")

    def flat(comp, i, j):
        return (comp * groups_x + i) * groups_y + j

    def gy_route(odd):
        pairs = [
            (flat(1, i, a), flat(1, i, b))
            for i in range(groups_x)
            for a, b in chain_pairs(groups_y, odd)
        ]
        if not odd and 2 in xor_masks:
            pairs += [
                (flat(0, i, j), flat(0, i ^ 2, j))
                for i in range(groups_x)
                for j in range(groups_y)
                if i < i ^ 2
            ]
        return both_ways(pairs)

    e2 = lax.ppermute(e2, axes, gy_route(0))
    e4 = lax.ppermute(e4, axes, gy_route(1))

    short = surface_sum.astype(bf16)

    def heat_route(odd):
        return both_ways(
            [(groups_x + a, groups_x + b) for a, b in chain_pairs(groups_x, odd)]
        )

    heat_a = lax.ppermute(short, ("comp", "gx"), heat_route(0))
    heat_b = lax.ppermute(short, ("comp", "gx"), heat_route(1))

    extra = []
    if not xor_masks:
        sums = lax.all_gather(spectral[5], "gx").astype(f32)
        viscous = lax.dynamic_slice_in_dim(
            diffusivity, lax.axis_index("gy") * channels, channels
        )[:, None]
        _, alpha, _ = decay_terms(viscous, half_rates)
        alpha = jnp.concatenate([alpha, alpha], axis=1)
        gap = lax.axis_index("gx") - jnp.arange(groups_x)
        decay = jnp.exp(
            -(rows * jnp.maximum(jnp.abs(gap) - 1, 0))[:, None, None] * alpha[None]
        )
        extra = [
            jnp.sum(jnp.where((gap > 0)[:, None, None], decay * sums[:, 0], 0.0), axis=0),
            jnp.sum(jnp.where((gap < 0)[:, None, None], decay * sums[:, 1], 0.0), axis=0),
        ]

    ring = channels // 2 + 8
    return pl.pallas_call(
        functools.partial(final_kernel, groups_x, groups_y, groups_y, xor_masks),
        out_shape=shape(fields.shape, f32),
        in_specs=[vmem] * (14 + len(extra)),
        out_specs=vmem,
        scratch_shapes=[
            pltpu.VMEM((rows, channels, LANES), f32),
            pltpu.VMEM((rows * channels, columns), bf16),
            pltpu.VMEM((rows + 4, 2, ring, columns), f32),
            pltpu.VMEM((rows + 2, 2, ring, columns), f32),
            pltpu.VMEM((16, columns), f32),
            pltpu.VMEM((6, 16, columns), f32),
            pltpu.VMEM((16, columns), f32),
        ],
        compiler_params=params(),
        name="inverse_or_ocean_steps",
    )(
        fields, wet_cells, diff_row, gain_row, half_rates, inverse, y,
        e1, e3, e2, e4, surface_sum, heat_a, heat_b, *extra,
    )


def solution(mesh):
    in_specs = (
        P("comp", "gx", "gy", None),
        P("gx", None),
        P(),
        P(),
        P(),
        P("gx", "gy", None, None),
        P("gx", "gy", None, None),
        P("gx", "gy"),
        P("gx", "gy", None, None, None),
        P("gx", "gy", None, None),
        P("gx", "gy", None, None),
        P("gx", "gy"),
        P("gx", "gy", None, None, None),
    )
    out_specs = P("comp", "gx", "gy", None)
    return jax.shard_map(local, mesh=mesh, in_specs=in_specs, out_specs=out_specs, check_vma=False)
```

time: 198 us -> 41.9 us (0.21)
  the two profiles are of different devices: /device:TPU:0 before, /device:TPU:13 now
where the time goes in v1:
time: 41.9 us; the launch traced here: 41.6 us
  starting transfers between devices  26.3 us (63%)
  Pallas kernels  7.12 us (17%)
  local copies, waits for them, and re-layouts  4.97 us (12%)
  waiting for transfers between devices  1.61 us (4%)
  between operations  1.56 us (4%)
    ppermute x1, starting transfers between devices, local(): heat_b = lax.ppermute(short, ('comp', 'gx'), heat_route(1))  6 us
    ppermute x4, starting transfers between devices, local(): surfaces.append(lax.ppermute(partial_surface, ('comp', 'gy'), route))  5.66 us
    unnamed x32, local copies, waits for them, and re-layouts  4.97 us
    pallas_call x1, Pallas kernels, local(): pl.pallas_call(functools.partial(final_kernel, groups_x, groups_y, groups...  4.53 us
    ppermute x3, starting transfers between devices, local(): lax.ppermute(sent, 'gy', [(j, j ^ mask) for j in range(groups_y)])  4.17 us
    ppermute x1, starting transfers between devices, local(): e4 = lax.ppermute(e4, axes, gy_route(1))  3.64 us
    ppermute x1, starting transfers between devices, local(): e3 = lax.ppermute(e3, ('comp', 'gx'), gx_route(1))  3.28 us
    pallas_call x1, Pallas kernels, local(): pl.pallas_call(functools.partial(regrid_kernel, groups_y), out_shape=[sha...  2.36 us
  transfers between devices with their start and end apart: 13, of which 2 were waited for; matrix products, arithmetic and copies ran while one was open for 0% of the time, Pallas kernels for 0%

profile of v1, /device:TPU:13, one launch (start us, length us, event | category | flops | bytes accessed | tf_op | source)
XLA Modules:
  0.0 41.6 jit_solution(12597525530104206207)
XLA Ops:
  0.0 0.0 copy-start.14
  0.0 0.0 copy-start
  0.0 1.2 %copy-done = f32[1,8,32,1024]{3,2,1,0:T(8,128)S(1)} copy-done((f32[1,8,32,1024]{3,2,1,0:T(8,128)S(1)}, f32[1,8,32,1024]{3,2,1,0:T(8,128)}, u32[]{:S(2)}) %copy-start) | copy-done | bytes 1048600
  1.2 0.0 copy-start.2
  1.2 1.6 %copy-done.2 = bf16[1024,1024]{1,0:T(8,128)(2,1)S(1)} copy-done((bf16[1024,1024]{1,0:T(8,128)(2,1)S(1)}, bf16[1024,1024]{1,0:T(8,128)(2,1)}, u32[]{:S(2)}) %copy-start.2) | copy-done | bytes 2097176
  2.8 0.0 copy-start.6
  2.8 0.8 %copy-done.6 = s32[8,1024]{1,0:T(8,128)S(1)} copy-done((s32[8,1024]{1,0:T(8,128)S(1)}, s32[8,1024]{1,0:T(8,128)}, u32[]{:S(2)}) %copy-start.6) | copy-done | bytes 32792
  3.6 0.0 copy-start.12
  3.6 0.7 %copy-done.12 = f32[1,512]{1,0:T(1,128)S(1)} copy-done((f32[1,512]{1,0:T(1,128)S(1)}, f32[1,512]{1,0:T(1,128)}, u32[]{:S(2)}) %copy-start.12) | copy-done | bytes 2072
  4.3 0.0 copy-start.13
  4.3 0.7 %copy-done.13 = f32[128]{0:T(128)S(1)} copy-done((f32[128]{0:T(128)S(1)}, f32[128]{0:T(128)}, u32[]{:S(2)}) %copy-start.13) | copy-done | bytes 536
  4.9 0.0 copy-start.4
  4.9 0.0 copy-start.5
  4.9 0.0 copy-start.8
  4.9 0.0 copy-start.9
  4.9 0.0 copy-start.10
  5.0 0.0 copy-start.11
  5.0 0.2 forward_and_halos.1
  5.2 0.0 copy-start.1
  5.2 0.0 copy-start.3
  5.2 0.0 copy-start.7
  5.2 0.0 copy-start.15
  5.2 0.7 %collective-permute-start = (bf16[80,1024]{1,0:T(8,128)(2,1)S(1)}, bf16[80,1024]{1,0:T(8,128)(2,1)S(1)}, u32[]{:S(2)}, u32[]{:S(2)}) collective-permute-start(bf16[80,1024]{1,0:T(8,128)(2,1)S(1)} %get-tuple-element.14), channel_id=1, source_target_pairs={{16,20},{20,16},{24,28},{28,24},{0,4},{4,0},{8,12},{12,8},{17,21},... | collective-permute-start | bytes 491528 | tf_op jit(solution)/shard_map/ppermute | solution.py:574
  6.0 3.3 %collective-permute-start.1 = (bf16[80,1024]{1,0:T(8,128)(2,1)S(1)}, bf16[80,1024]{1,0:T(8,128)(2,1)S(1)}, u32[]{:S(2)}, u32[]{:S(2)}) collective-permute-start(bf16[80,1024]{1,0:T(8,128)(2,1)S(1)} %get-tuple-element.15), channel_id=1, source_target_pairs={{20,24},{24,20},{0,12},{12,0},{4,8},{8,4},{21,25},{25,21},{1,13},{... | collective-permute-start | bytes 491528 | tf_op jit(solution)/shard_map/ppermute | solution.py:575
  9.2 0.0 copy-done.14
  9.3 2.3 %collective-permute-start.5 = (bf16[64,128]{1,0:T(8,128)(2,1)S(1)}, bf16[64,128]{1,0:T(8,128)(2,1)S(1)}, u32[]{:S(2)}, u32[]{:S(2)}) collective-permute-start(bf16[64,128]{1,0:T(8,128)(2,1)S(1)} %surface_partials.1), channel_id=1, source_target_pairs={{0,19},{19,0},{1,18},{18,1},{2,17},{17,2},{3,16},{16,3},{4,23},{23... | collective-permute-start | bytes 49160 | tf_op jit(solution)/shard_map/ppermute | solution.py:543
  11.6 1.1 %collective-permute-start.4 = (bf16[64,128]{1,0:T(8,128)(2,1)S(1)}, bf16[64,128]{1,0:T(8,128)(2,1)S(1)}, u32[]{:S(2)}, u32[]{:S(2)}) collective-permute-start(bf16[64,128]{1,0:T(8,128)(2,1)S(1)} %surface_partials.1), channel_id=1, source_target_pairs={{0,18},{18,0},{1,19},{19,1},{2,16},{16,2},{3,17},{17,3},{4,22},{22... | collective-permute-start | bytes 49160 | tf_op jit(solution)/shard_map/ppermute | solution.py:543
  12.7 1.2 %collective-permute-start.3 = (bf16[64,128]{1,0:T(8,128)(2,1)S(1)}, bf16[64,128]{1,0:T(8,128)(2,1)S(1)}, u32[]{:S(2)}, u32[]{:S(2)}) collective-permute-start(bf16[64,128]{1,0:T(8,128)(2,1)S(1)} %surface_partials.1), channel_id=1, source_target_pairs={{0,17},{17,0},{1,16},{16,1},{2,19},{19,2},{3,18},{18,3},{4,21},{21... | collective-permute-start | bytes 49160 | tf_op jit(solution)/shard_map/ppermute | solution.py:543
  13.8 0.0 collective-permute-done.5.refs_3_
  13.8 1.1 %collective-permute-start.2 = (bf16[64,128]{1,0:T(8,128)(2,1)S(1)}, bf16[64,128]{1,0:T(8,128)(2,1)S(1)}, u32[]{:S(2)}, u32[]{:S(2)}) collective-permute-start(bf16[64,128]{1,0:T(8,128)(2,1)S(1)} %surface_partials.1), channel_id=1, source_target_pairs={{0,16},{16,0},{1,17},{17,1},{2,18},{18,2},{3,19},{19,3},{4,20},{20... | collective-permute-start | bytes 49160 | tf_op jit(solution)/shard_map/ppermute | solution.py:543
  16.3 0.0 collective-permute-done.4.refs_2_
  16.3 0.0 collective-permute-done.3.refs_1_
  16.3 0.4 %collective-permute-done.2.refs_0_ = bf16[64,128]{1,0:T(8,128)(2,1)S(1)} collective-permute-done((bf16[64,128]{1,0:T(8,128)(2,1)S(1)}, bf16[64,128]{1,0:T(8,128)(2,1)S(1)}, u32[]{:S(2)}, u32[]{:S(2)}) %collective-permute-start.2) | collective-permute-done | bytes 16416 | tf_op jit(solution)/shard_map/ppermute | solution.py:543
  16.7 0.0 collective-permute-done.refs_12_.refs_7_
  16.7 0.0 collective-permute-done.1.refs_13_.refs_8_
  16.7 0.0 copy-done.4
  16.7 0.0 copy-done.5
  16.7 0.0 copy-done.8
  16.8 0.0 copy-done.9
  16.8 0.0 copy-done.10
  16.8 0.0 copy-done.11
  16.8 2.4 %regrid_blocks.1 = (f32[64,128]{1,0:T(8,128)S(1)}, bf16[48,1024]{1,0:T(8,128)(2,1)S(1)}, bf16[48,1024]{1,0:T(8,128)(2,1)S(1)}) custom-call(bf16[64,128]{1,0:T(8,128)(2,1)S(1)} %collective-permute-done.2.refs_0_, bf16[64,128]{1,0:T(8,128)(2,1)S(1)} %collective-permute-done.3.refs_1_, bf16[64,128]{1,0:T(8,128)(2,1)S(1)} %collective-permute-done.4.refs_2_, ...), custom_call_target="tpu_custom_call" | custom-call | tf_op jit(solution)/shard_map/regrid_blocks/pallas_call | solution.py:577
  19.2 1.8 %collective-permute-start.10 = (bf16[64,128]{1,0:T(8,128)(2,1)S(1)}, bf16[64,128]{1,0:T(8,128)(2,1)S(1)}, u32[]{:S(2)}, u32[]{:S(2)}) collective-permute-start(bf16[64,128]{1,0:T(8,128)(2,1)S(1)} %convert_element_type.15), channel_id=1, source_target_pairs={{0,3},{1,2},{2,1},{3,0},{4,7},{5,6},{6,5},{7,4},{8,11},{9,10},{10,... | collective-permute-start | bytes 49160 | tf_op jit(solution)/shard_map/ppermute | solution.py:607
  20.9 1.8 %collective-permute-start.9 = (bf16[64,128]{1,0:T(8,128)(2,1)S(1)}, bf16[64,128]{1,0:T(8,128)(2,1)S(1)}, u32[]{:S(2)}, u32[]{:S(2)}) collective-permute-start(bf16[64,128]{1,0:T(8,128)(2,1)S(1)} %convert_element_type.15), channel_id=1, source_target_pairs={{0,2},{1,3},{2,0},{3,1},{4,6},{5,7},{6,4},{7,5},{8,10},{9,11},{10,... | collective-permute-start | bytes 49160 | tf_op jit(solution)/shard_map/ppermute | solution.py:607
  22.8 0.6 %collective-permute-start.8 = (bf16[64,128]{1,0:T(8,128)(2,1)S(1)}, bf16[64,128]{1,0:T(8,128)(2,1)S(1)}, u32[]{:S(2)}, u32[]{:S(2)}) collective-permute-start(bf16[64,128]{1,0:T(8,128)(2,1)S(1)} %convert_element_type.15), channel_id=1, source_target_pairs={{0,1},{1,0},{2,3},{3,2},{4,5},{5,4},{6,7},{7,6},{8,9},{9,8},{10,11... | collective-permute-start | bytes 49160 | tf_op jit(solution)/shard_map/ppermute | solution.py:607
  23.3 0.9 %collective-permute-start.6 = (bf16[48,1024]{1,0:T(8,128)(2,1)S(1)}, bf16[48,1024]{1,0:T(8,128)(2,1)S(1)}, u32[]{:S(2)}, u32[]{:S(2)}) collective-permute-start(bf16[48,1024]{1,0:T(8,128)(2,1)S(1)} %get-tuple-element.18), channel_id=1, source_target_pairs={{16,17},{17,16},{18,19},{19,18},{20,21},{21,20},{22,23},{23,22},{2... | collective-permute-start | bytes 294920 | tf_op jit(solution)/shard_map/ppermute | solution.py:634
  24.2 3.6 %collective-permute-start.7 = (bf16[48,1024]{1,0:T(8,128)(2,1)S(1)}, bf16[48,1024]{1,0:T(8,128)(2,1)S(1)}, u32[]{:S(2)}, u32[]{:S(2)}) collective-permute-start(bf16[48,1024]{1,0:T(8,128)(2,1)S(1)} %get-tuple-element.19), channel_id=1, source_target_pairs={{17,18},{18,17},{21,22},{22,21},{25,26},{26,25},{29,30},{30,29}} | collective-permute-start | bytes 294920 | tf_op jit(solution)/shard_map/ppermute | solution.py:635
  27.9 0.0 collective-permute-done.10
  27.9 0.0 collective-permute-done.9
  27.9 0.0 collective-permute-done.8
  27.9 6.0 %collective-permute-start.12 = (bf16[64,128]{1,0:T(8,128)(2,1)S(1)}, bf16[64,128]{1,0:T(8,128)(2,1)S(1)}, u32[]{:S(2)}, u32[]{:S(2)}) collective-permute-start(bf16[64,128]{1,0:T(8,128)(2,1)S(1)} %get-tuple-element.21), channel_id=1, source_target_pairs={{20,24},{24,20},{21,25},{25,21},{22,26},{26,22},{23,27},{27,23}} | collective-permute-start | bytes 49160 | tf_op jit(solution)/shard_map/ppermute | solution.py:645
  34.0 1.9 %collective-permute-start.11 = (bf16[64,128]{1,0:T(8,128)(2,1)S(1)}, bf16[64,128]{1,0:T(8,128)(2,1)S(1)}, u32[]{:S(2)}, u32[]{:S(2)}) collective-permute-start(bf16[64,128]{1,0:T(8,128)(2,1)S(1)} %get-tuple-element.21), channel_id=1, source_target_pairs={{16,20},{20,16},{24,28},{28,24},{17,21},{21,17},{25,29},{29,25},{1... | collective-permute-start | bytes 49160 | tf_op jit(solution)/shard_map/ppermute | solution.py:644
  35.9 0.0 collective-permute-done.12.refs_13_
  35.9 1.1 %collective-permute-done.11.refs_12_ = bf16[64,128]{1,0:T(8,128)(2,1)S(1)} collective-permute-done((bf16[64,128]{1,0:T(8,128)(2,1)S(1)}, bf16[64,128]{1,0:T(8,128)(2,1)S(1)}, u32[]{:S(2)}, u32[]{:S(2)}) %collective-permute-start.11) | collective-permute-done | bytes 16416 | tf_op jit(solution)/shard_map/ppermute | solution.py:644
  37.0 0.0 collective-permute-done.6.refs_9_
  37.0 0.0 collective-permute-done.7.refs_10_
  37.0 0.0 copy-done.1
  37.0 0.0 copy-done.3
  37.1 0.0 copy-done.7
  37.1 0.0 copy-done.15
  37.1 4.5 %inverse_or_ocean_steps.1 = f32[1,8,32,1024]{3,2,1,0:T(8,128)} custom-call(f32[1,8,32,1024]{3,2,1,0:T(8,128)S(1)} %copy-done.1, s32[8,1024]{1,0:T(8,128)S(1)} %copy-done.7, f32[1,128]{1,0:T(1,128)S(1)} %bitcast.4, f32[1,128]{1,0:T(1,128)S(1)} %bitcast.6, f32[1,512]{1,0:T(1,128)S(1)} %copy-done.12, bf16[1024,1024]{1,0:T(8,128)(2,1)S(1)} %copy-done.3, ...), custom_call_target="tpu_custom_call" | custom-call | tf_op jit(solution)/shard_map/inverse_or_ocean_steps/pallas_call | solution.py:665
  (3 shorter events, 0.1 us)
Async XLA Ops:
  0.0 9.2 %copy-start.14 = (f32[128]{0:T(128)S(1)}, f32[128]{0:T(128)}, u32[]{:S(2)}) copy-start(f32[128]{0:T(128)} %param.18) | copy-start | bytes 1540
  0.0 1.2 %copy-start = (f32[1,8,32,1024]{3,2,1,0:T(8,128)S(1)}, f32[1,8,32,1024]{3,2,1,0:T(8,128)}, u32[]{:S(2)}) copy-start(f32[1,8,32,1024]{3,2,1,0:T(8,128)} %refs_0_.1) | copy-start | bytes 3145732
  1.2 1.6 %copy-start.2 = (bf16[1024,1024]{1,0:T(8,128)(2,1)S(1)}, bf16[1024,1024]{1,0:T(8,128)(2,1)}, u32[]{:S(2)}) copy-start(bf16[1024,1024]{1,0:T(8,128)(2,1)} %constant.6.clone.table_ref) | copy-start | bytes 6291460
  2.8 0.8 %copy-start.6 = (s32[8,1024]{1,0:T(8,128)S(1)}, s32[8,1024]{1,0:T(8,128)}, u32[]{:S(2)}) copy-start(s32[8,1024]{1,0:T(8,128)} %refs_1_.1) | copy-start | bytes 98308
  3.6 0.7 %copy-start.12 = (f32[1,512]{1,0:T(1,128)S(1)}, f32[1,512]{1,0:T(1,128)}, u32[]{:S(2)}) copy-start(f32[1,512]{1,0:T(1,128)} %constant.8.clone.rates_ref.refs_4_) | copy-start | bytes 6148
  4.3 0.7 %copy-start.13 = (f32[128]{0:T(128)S(1)}, f32[128]{0:T(128)}, u32[]{:S(2)}) copy-start(f32[128]{0:T(128)} %param.20) | copy-start | bytes 1540
  4.9 11.8 %copy-start.4 = (bf16[1,1,32,128,128]{4,3,2,1,0:T(8,128)(2,1)S(1)}, bf16[1,1,32,128,128]{4,3,2,1,0:T(8,128)(2,1)}, u32[]{:S(2)}) copy-start(bf16[1,1,32,128,128]{4,3,2,1,0:T(8,128)(2,1)} %refs_7_.1) | copy-start | bytes 3145732
  4.9 11.8 %copy-start.5 = (bf16[1,1,32,128,128]{4,3,2,1,0:T(8,128)(2,1)S(1)}, bf16[1,1,32,128,128]{4,3,2,1,0:T(8,128)(2,1)}, u32[]{:S(2)}) copy-start(bf16[1,1,32,128,128]{4,3,2,1,0:T(8,128)(2,1)} %refs_11_.1) | copy-start | bytes 3145732
  4.9 11.8 %copy-start.8 = (s32[1,1,32,128]{3,2,1,0:T(8,128)S(1)}, s32[1,1,32,128]{3,2,1,0:T(8,128)}, u32[]{:S(2)}) copy-start(s32[1,1,32,128]{3,2,1,0:T(8,128)} %refs_4_.2) | copy-start | bytes 49156
  4.9 11.8 %copy-start.9 = (s32[1,1,32,128]{3,2,1,0:T(8,128)S(1)}, s32[1,1,32,128]{3,2,1,0:T(8,128)}, u32[]{:S(2)}) copy-start(s32[1,1,32,128]{3,2,1,0:T(8,128)} %refs_5_.2) | copy-start | bytes 49156
  4.9 11.8 %copy-start.10 = (s32[1,1,32,128]{3,2,1,0:T(8,128)S(1)}, s32[1,1,32,128]{3,2,1,0:T(8,128)}, u32[]{:S(2)}) copy-start(s32[1,1,32,128]{3,2,1,0:T(8,128)} %refs_8_.1) | copy-start | bytes 49156
  5.0 11.8 %copy-start.11 = (s32[1,1,32,128]{3,2,1,0:T(8,128)S(1)}, s32[1,1,32,128]{3,2,1,0:T(8,128)}, u32[]{:S(2)}) copy-start(s32[1,1,32,128]{3,2,1,0:T(8,128)} %refs_9_.1) | copy-start | bytes 49156
  5.2 31.9 %copy-start.1 = (f32[1,8,32,1024]{3,2,1,0:T(8,128)S(1)}, f32[1,8,32,1024]{3,2,1,0:T(8,128)}, u32[]{:S(2)}) copy-start(f32[1,8,32,1024]{3,2,1,0:T(8,128)} %refs_0_.1) | copy-start | bytes 3145732
  5.2 31.9 %copy-start.3 = (bf16[1024,1024]{1,0:T(8,128)(2,1)S(1)}, bf16[1024,1024]{1,0:T(8,128)(2,1)}, u32[]{:S(2)}) copy-start(bf16[1024,1024]{1,0:T(8,128)(2,1)} %constant.7.clone.refs_5_) | copy-start | bytes 6291460
  5.2 31.9 %copy-start.7 = (s32[8,1024]{1,0:T(8,128)S(1)}, s32[8,1024]{1,0:T(8,128)}, u32[]{:S(2)}) copy-start(s32[8,1024]{1,0:T(8,128)} %refs_1_.1) | copy-start | bytes 98308
  5.2 31.9 %copy-start.15 = (f32[128]{0:T(128)S(1)}, f32[128]{0:T(128)}, u32[]{:S(2)}) copy-start(f32[128]{0:T(128)} %param.19) | copy-start | bytes 1540
  5.2 11.5 %collective-permute-start = (bf16[80,1024]{1,0:T(8,128)(2,1)S(1)}, bf16[80,1024]{1,0:T(8,128)(2,1)S(1)}, u32[]{:S(2)}, u32[]{:S(2)}) collective-permute-start(bf16[80,1024]{1,0:T(8,128)(2,1)S(1)} %get-tuple-element.14), channel_id=1, source_target_pairs={{16,20},{20,16},{24,28},{28,24},{0,4},{4,0},{8,12},{12,8},{17,21},... | collective-permute-start | bytes 491528 | tf_op jit(solution)/shard_map/ppermute | solution.py:574
  6.0 10.8 %collective-permute-start.1 = (bf16[80,1024]{1,0:T(8,128)(2,1)S(1)}, bf16[80,1024]{1,0:T(8,128)(2,1)S(1)}, u32[]{:S(2)}, u32[]{:S(2)}) collective-permute-start(bf16[80,1024]{1,0:T(8,128)(2,1)S(1)} %get-tuple-element.15), channel_id=1, source_target_pairs={{20,24},{24,20},{0,12},{12,0},{4,8},{8,4},{21,25},{25,21},{1,13},{... | collective-permute-start | bytes 491528 | tf_op jit(solution)/shard_map/ppermute | solution.py:575
  9.3 4.5 %collective-permute-start.5 = (bf16[64,128]{1,0:T(8,128)(2,1)S(1)}, bf16[64,128]{1,0:T(8,128)(2,1)S(1)}, u32[]{:S(2)}, u32[]{:S(2)}) collective-permute-start(bf16[64,128]{1,0:T(8,128)(2,1)S(1)} %surface_partials.1), channel_id=1, source_target_pairs={{0,19},{19,0},{1,18},{18,1},{2,17},{17,2},{3,16},{16,3},{4,23},{23... | collective-permute-start | bytes 49160 | tf_op jit(solution)/shard_map/ppermute | solution.py:543
  11.6 4.7 %collective-permute-start.4 = (bf16[64,128]{1,0:T(8,128)(2,1)S(1)}, bf16[64,128]{1,0:T(8,128)(2,1)S(1)}, u32[]{:S(2)}, u32[]{:S(2)}) collective-permute-start(bf16[64,128]{1,0:T(8,128)(2,1)S(1)} %surface_partials.1), channel_id=1, source_target_pairs={{0,18},{18,0},{1,19},{19,1},{2,16},{16,2},{3,17},{17,3},{4,22},{22... | collective-permute-start | bytes 49160 | tf_op jit(solution)/shard_map/ppermute | solution.py:543
  12.7 3.6 %collective-permute-start.3 = (bf16[64,128]{1,0:T(8,128)(2,1)S(1)}, bf16[64,128]{1,0:T(8,128)(2,1)S(1)}, u32[]{:S(2)}, u32[]{:S(2)}) collective-permute-start(bf16[64,128]{1,0:T(8,128)(2,1)S(1)} %surface_partials.1), channel_id=1, source_target_pairs={{0,17},{17,0},{1,16},{16,1},{2,19},{19,2},{3,18},{18,3},{4,21},{21... | collective-permute-start | bytes 49160 | tf_op jit(solution)/shard_map/ppermute | solution.py:543
  13.8 2.9 %collective-permute-start.2 = (bf16[64,128]{1,0:T(8,128)(2,1)S(1)}, bf16[64,128]{1,0:T(8,128)(2,1)S(1)}, u32[]{:S(2)}, u32[]{:S(2)}) collective-permute-start(bf16[64,128]{1,0:T(8,128)(2,1)S(1)} %surface_partials.1), channel_id=1, source_target_pairs={{0,16},{16,0},{1,17},{17,1},{2,18},{18,2},{3,19},{19,3},{4,20},{20... | collective-permute-start | bytes 49160 | tf_op jit(solution)/shard_map/ppermute | solution.py:543
  19.2 8.7 %collective-permute-start.10 = (bf16[64,128]{1,0:T(8,128)(2,1)S(1)}, bf16[64,128]{1,0:T(8,128)(2,1)S(1)}, u32[]{:S(2)}, u32[]{:S(2)}) collective-permute-start(bf16[64,128]{1,0:T(8,128)(2,1)S(1)} %convert_element_type.15), channel_id=1, source_target_pairs={{0,3},{1,2},{2,1},{3,0},{4,7},{5,6},{6,5},{7,4},{8,11},{9,10},{10,... | collective-permute-start | bytes 49160 | tf_op jit(solution)/shard_map/ppermute | solution.py:607
  20.9 7.0 %collective-permute-start.9 = (bf16[64,128]{1,0:T(8,128)(2,1)S(1)}, bf16[64,128]{1,0:T(8,128)(2,1)S(1)}, u32[]{:S(2)}, u32[]{:S(2)}) collective-permute-start(bf16[64,128]{1,0:T(8,128)(2,1)S(1)} %convert_element_type.15), channel_id=1, source_target_pairs={{0,2},{1,3},{2,0},{3,1},{4,6},{5,7},{6,4},{7,5},{8,10},{9,11},{10,... | collective-permute-start | bytes 49160 | tf_op jit(solution)/shard_map/ppermute | solution.py:607
  22.8 5.1 %collective-permute-start.8 = (bf16[64,128]{1,0:T(8,128)(2,1)S(1)}, bf16[64,128]{1,0:T(8,128)(2,1)S(1)}, u32[]{:S(2)}, u32[]{:S(2)}) collective-permute-start(bf16[64,128]{1,0:T(8,128)(2,1)S(1)} %convert_element_type.15), channel_id=1, source_target_pairs={{0,1},{1,0},{2,3},{3,2},{4,5},{5,4},{6,7},{7,6},{8,9},{9,8},{10,11... | collective-permute-start | bytes 49160 | tf_op jit(solution)/shard_map/ppermute | solution.py:607
  23.3 13.7 %collective-permute-start.6 = (bf16[48,1024]{1,0:T(8,128)(2,1)S(1)}, bf16[48,1024]{1,0:T(8,128)(2,1)S(1)}, u32[]{:S(2)}, u32[]{:S(2)}) collective-permute-start(bf16[48,1024]{1,0:T(8,128)(2,1)S(1)} %get-tuple-element.18), channel_id=1, source_target_pairs={{16,17},{17,16},{18,19},{19,18},{20,21},{21,20},{22,23},{23,22},{2... | collective-permute-start | bytes 294920 | tf_op jit(solution)/shard_map/ppermute | solution.py:634
  24.2 12.8 %collective-permute-start.7 = (bf16[48,1024]{1,0:T(8,128)(2,1)S(1)}, bf16[48,1024]{1,0:T(8,128)(2,1)S(1)}, u32[]{:S(2)}, u32[]{:S(2)}) collective-permute-start(bf16[48,1024]{1,0:T(8,128)(2,1)S(1)} %get-tuple-element.19), channel_id=1, source_target_pairs={{17,18},{18,17},{21,22},{22,21},{25,26},{26,25},{29,30},{30,29}} | collective-permute-start | bytes 294920 | tf_op jit(solution)/shard_map/ppermute | solution.py:635
  27.9 7.9 %collective-permute-start.12 = (bf16[64,128]{1,0:T(8,128)(2,1)S(1)}, bf16[64,128]{1,0:T(8,128)(2,1)S(1)}, u32[]{:S(2)}, u32[]{:S(2)}) collective-permute-start(bf16[64,128]{1,0:T(8,128)(2,1)S(1)} %get-tuple-element.21), channel_id=1, source_target_pairs={{20,24},{24,20},{21,25},{25,21},{22,26},{26,22},{23,27},{27,23}} | collective-permute-start | bytes 49160 | tf_op jit(solution)/shard_map/ppermute | solution.py:645
  34.0 3.1 %collective-permute-start.11 = (bf16[64,128]{1,0:T(8,128)(2,1)S(1)}, bf16[64,128]{1,0:T(8,128)(2,1)S(1)}, u32[]{:S(2)}, u32[]{:S(2)}) collective-permute-start(bf16[64,128]{1,0:T(8,128)(2,1)S(1)} %get-tuple-element.21), channel_id=1, source_target_pairs={{16,20},{20,16},{24,28},{28,24},{17,21},{21,17},{25,29},{29,25},{1... | collective-permute-start | bytes 49160 | tf_op jit(solution)/shard_map/ppermute | solution.py:644

commit v2 on v1

--- a/solution.py
+++ b/solution.py
@@ -60,6 +60,11 @@
     )
 
 
+def share(ref, block):
+    for k in range(ref.shape[0]):
+        ref[k] = block
+
+
 def surface_kernel(x_ref, flux_ref, s_ref, row_ref):
     _, rows, channels, columns = x_ref.shape
     col_group = lax.axis_index("gy")
@@ -70,14 +75,14 @@
         weight = channel_column(flux_ref[...], channels, col_group * channels)
         for r in range(rows):
             row_ref[r : r + 1, :] = jnp.sum(x_ref[0, r] * weight, axis=0, keepdims=True)
-        s_ref[...] = to_tiles(row_ref[...]).astype(bf16)
+        share(s_ref, to_tiles(row_ref[...]).astype(bf16))
 
     @pl.when(jnp.logical_not(is_atmos))
     def _():
         gain = jnp.where(col_group == 0, 1.0, 0.0)
         for r in range(rows):
             row_ref[r : r + 1, :] = x_ref[0, r, 0:1, :] * gain
-        s_ref[...] = to_tiles(row_ref[...]).astype(bf16)
+        share(s_ref, to_tiles(row_ref[...]).astype(bf16))
 
 
 def decay_terms(diff_column, half_rates):
@@ -88,12 +93,12 @@
 
 
 def forward_kernel(
-    groups_x, x_ref, wet_ref, diff_ref, rates_ref, table_ref, *refs, xor_masks
+    groups_x, x_ref, wet_ref, diff_ref, rates_ref, table_hbm, after_ref, *refs, xor_masks
 ):
-    msgs = len(xor_masks)
+    del after_ref
     y_ref, e1_ref, e3_ref, e2_ref, e4_ref = refs[:5]
     pq_ref = refs[5] if not xor_masks else None
-    edge_ref = refs[-1]
+    edge_ref, table_ref, sem = refs[-3:]
     _, rows, channels, columns = x_ref.shape
     waves = columns // 2
     row_group = lax.axis_index("gx")
@@ -103,8 +108,18 @@
     @pl.when(is_atmos)
     def _():
         step = 256
+        copies = []
+        for k, n in enumerate(range(0, columns, step)):
+            lanes = pl.ds(n, step)
+            copies.append(
+                pltpu.make_async_copy(
+                    table_hbm.at[:, lanes], table_ref.at[:, lanes], sem.at[k]
+                )
+            )
+            copies[-1].start()
         flat = x_ref[0].astype(bf16).reshape(rows * channels, columns)
-        for n in range(0, columns, step):
+        for k, n in enumerate(range(0, columns, step)):
+            copies[k].wait()
             part = jnp.dot(flat, table_ref[:, n : n + step], preferred_element_type=f32)
             y_ref[:, :, n : n + step] = part.reshape(rows, channels, step)
         diff = channel_column(diff_ref[...], channels, col_group * channels)
@@ -183,17 +198,17 @@
         put_edges(e4_ref, jnp.logical_not(even_y))
 
 
-def regrid_kernel(n_msgs, *refs):
-    msgs = refs[:n_msgs]
+def regrid_kernel(*refs):
     (
-        a_src, a_dst, a_count, a_weight, m_src, m_dst, m_count, m_weight,
+        surfaces_ref, a_src, a_dst, a_count, a_weight, m_src, m_dst, m_count, m_weight,
         e1_ref, e3_ref, e2_in, e4_in,
-        land_ref, e2_ref, e4_ref,
-        weight_ref, hot_ref, gath_ref, val_ref, tail_ref, sem,
-    ) = refs[n_msgs:]
+        land_ref, sent_ref, e2_ref, e4_ref,
+        weight_ref, gath_ref, val_ref, tail_ref, sem,
+    ) = refs
     is_atmos = lax.axis_index("comp") == 0
     blocks, points = val_ref.shape
-    cells = msgs[0].shape[0]
+    groups_y = surfaces_ref.shape[0] // 2
+    cells = surfaces_ref.shape[1]
     rows = 8
 
     @pl.when(is_atmos)
@@ -218,9 +233,10 @@
     dst_row, dst_lane = split(dst)
     lane_iota = lax.broadcasted_iota(jnp.int32, (LANES, points), 0)
     row_iota = lax.broadcasted_iota(jnp.int32, (cells, points), 0)
-    table = msgs[0][...].astype(f32)
-    for m in msgs[1:]:
-        table = table + m[...].astype(f32)
+    other = jnp.where(is_atmos, groups_y, 0)
+    table = surfaces_ref[other].astype(f32)
+    for k in range(1, groups_y):
+        table = table + surfaces_ref[other + k].astype(f32)
     table = table.astype(bf16)
     for b in range(blocks):
         hot = jnp.where(lane_iota == src_lane[b : b + 1], 1.0, 0.0).astype(bf16)
@@ -258,7 +274,9 @@
         land = land + lax.dot_general(
             both, hot, (((1,), (1,)), ((), ())), preferred_element_type=f32
         )
-    land_ref[...] = land[:cells] + land[cells:]
+    land = land[:cells] + land[cells:]
+    land_ref[...] = land
+    share(sent_ref, land.astype(bf16))
 
     @pl.when(is_atmos)
     def _():
@@ -298,16 +316,16 @@
         fill(e4_ref, e4_in, jnp.logical_not(even_y))
 
 
-def final_kernel(groups_x, groups_y, n_land, xor_masks, *refs):
+def final_kernel(groups_x, groups_y, xor_masks, *refs):
     (
         x_ref, wet_ref, diff_ref, gain_ref, rates_ref, table_ref, y_ref,
-        e1_ref, e3_ref, e2_ref, e4_ref, hsum_ref, ha_ref, hb_ref,
-    ) = refs[:14]
+        e1_ref, e3_ref, e2_ref, e4_ref, hsum_ref, heat_ref,
+    ) = refs[:13]
     coupling = (e1_ref, e2_ref, e3_ref)
-    at = 14
+    at = 13
     if not xor_masks:
-        pin_ref, qin_ref = refs[14:16]
-        at = 16
+        pin_ref, qin_ref = refs[13:15]
+        at = 15
     out_ref, z_ref, zb_ref, t0_ref, t1_ref, w_ref, c_ref, h_ref = refs[at:]
     _, rows, channels, columns = x_ref.shape
     waves = columns // 2
@@ -396,11 +414,11 @@
 
         surface = jnp.where(top, 1.0, 0.0)
         own = from_tiles(hsum_ref[...], rows)
-        ha = from_tiles(ha_ref[...].astype(f32), rows)
-        hb = from_tiles(hb_ref[...].astype(f32), rows)
-        h_ref[0:1, :] = jnp.where(even_x, hb, ha)[rows - 1 : rows]
+        below = heat_ref[jnp.maximum(row_group - 1, 0)].astype(f32)
+        above = heat_ref[jnp.minimum(row_group + 1, groups_x - 1)].astype(f32)
+        h_ref[0:1, :] = from_tiles(below, rows)[rows - 1 : rows]
         h_ref[1 : rows + 1, :] = own
-        h_ref[rows + 1 : rows + 2, :] = jnp.where(even_x, ha, hb)[0:1]
+        h_ref[rows + 1 : rows + 2, :] = from_tiles(above, rows)[0:1]
 
         span = rows + 2
         north = w_ref[0:span, :]
@@ -528,19 +546,14 @@
 
     partial_surface = pl.pallas_call(
         surface_kernel,
-        out_shape=shape((cells, LANES), bf16),
+        out_shape=shape((2 * groups_y, cells, LANES), bf16),
         in_specs=[vmem, vmem],
         out_specs=vmem,
         scratch_shapes=[pltpu.VMEM((rows, columns), f32)],
         compiler_params=params(),
         name="surface_partials",
     )(fields, flux_row)
-    surfaces = []
-    for mask in range(groups_y):
-        route = []
-        for j in range(groups_y):
-            route += both_ways([(j, groups_y + (j ^ mask))])
-        surfaces.append(lax.ppermute(partial_surface, ("comp", "gy"), route))
+    surfaces = lax.all_to_all(partial_surface, ("comp", "gy"), 0, 0, tiled=True)
 
     lines = 2 * channels + 16
     edges = 4 * rows + 16
@@ -556,12 +569,16 @@
     spectral = pl.pallas_call(
         functools.partial(forward_kernel, groups_x, xor_masks=xor_masks),
         out_shape=shapes,
-        in_specs=[vmem] * 5,
+        in_specs=[vmem] * 4 + [anywhere] * 2,
         out_specs=[vmem] * len(shapes),
-        scratch_shapes=[pltpu.VMEM((4 * rows, columns), f32)],
+        scratch_shapes=[
+            pltpu.VMEM((4 * rows, columns), f32),
+            pltpu.VMEM((columns, columns), bf16),
+            pltpu.SemaphoreType.DMA((columns // 256,)),
+        ],
         compiler_params=params(),
         name="forward_and_halos",
-    )(fields, wet_cells, diff_row, half_rates, forward)
+    )(fields, wet_cells, diff_row, half_rates, forward, partial_surface)
     y, e1, e3, e2, e4 = spectral[:5]
 
     def gx_route(odd):
@@ -574,20 +591,20 @@
     e1 = lax.ppermute(e1, ("comp", "gx"), gx_route(0))
     e3 = lax.ppermute(e3, ("comp", "gx"), gx_route(1))
 
-    landing, e2, e4 = pl.pallas_call(
-        functools.partial(regrid_kernel, groups_y),
+    landing, sent, e2, e4 = pl.pallas_call(
+        regrid_kernel,
         out_shape=[
             shape((cells, LANES), f32),
+            shape((groups_y, cells, LANES), bf16),
             shape((edges, columns), bf16),
             shape((edges, columns), bf16),
         ],
-        in_specs=[vmem] * groups_y
+        in_specs=[vmem]
         + [vmem, vmem, smem, anywhere, vmem, vmem, smem, anywhere]
         + [vmem] * 4,
-        out_specs=[vmem] * 3,
+        out_specs=[vmem] * 4,
         scratch_shapes=[
             pltpu.VMEM((blocks, points, points), bf16),
-            pltpu.VMEM((LANES, points), bf16),
             pltpu.VMEM((blocks, points), f32),
             pltpu.VMEM((blocks, points), f32),
             pltpu.VMEM((8, columns), f32),
@@ -596,20 +613,17 @@
         compiler_params=params(),
         name="regrid_blocks",
     )(
-        *surfaces,
+        surfaces,
         a2o_source, a2o_target, a2o_count, a2o_weight,
         marine_air_input_index, marine_air_output_index,
         marine_air_piece_tally, marine_air_piece_factor,
         e1, e3, e2, e4,
     )
-    sent = landing.astype(bf16)
-    parts = [
-        lax.ppermute(sent, "gy", [(j, j ^ mask) for j in range(groups_y)])
-        for mask in range(1, groups_y)
-    ]
+    parts = lax.all_to_all(sent, "gy", 0, 0, tiled=True)
+    mine = lax.axis_index("gy")
     surface_sum = landing
-    for part in parts:
-        surface_sum = surface_sum + part.astype(f32)
+    for k in range(groups_y):
+        surface_sum = surface_sum + jnp.where(k == mine, 0.0, parts[k].astype(f32))
 
     axes = ("comp", "gx", "gy")
 
@@ -634,15 +648,8 @@
     e2 = lax.ppermute(e2, axes, gy_route(0))
     e4 = lax.ppermute(e4, axes, gy_route(1))
 
-    short = surface_sum.astype(bf16)
-
-    def heat_route(odd):
-        return both_ways(
-            [(groups_x + a, groups_x + b) for a, b in chain_pairs(groups_x, odd)]
-        )
-
-    heat_a = lax.ppermute(short, ("comp", "gx"), heat_route(0))
-    heat_b = lax.ppermute(short, ("comp", "gx"), heat_route(1))
+    short = jnp.broadcast_to(surface_sum.astype(bf16), (groups_x, cells, LANES))
+    heat = lax.all_to_all(short, "gx", 0, 0, tiled=True)
 
     extra = []
     if not xor_masks:
@@ -663,9 +670,9 @@
 
     ring = channels // 2 + 8
     return pl.pallas_call(
-        functools.partial(final_kernel, groups_x, groups_y, groups_y, xor_masks),
+        functools.partial(final_kernel, groups_x, groups_y, xor_masks),
         out_shape=shape(fields.shape, f32),
-        in_specs=[vmem] * (14 + len(extra)),
+        in_specs=[vmem] * (13 + len(extra)),
         out_specs=vmem,
         scratch_shapes=[
             pltpu.VMEM((rows, channels, LANES), f32),
@@ -680,7 +687,7 @@
         name="inverse_or_ocean_steps",
     )(
         fields, wet_cells, diff_row, gain_row, half_rates, inverse, y,
-        e1, e3, e2, e4, surface_sum, heat_a, heat_b, *extra,
+        e1, e3, e2, e4, surface_sum, heat, *extra,
     )
 
 

time: 41.9 us -> 65.6 us (1.57)
  the two profiles are of different devices: /device:TPU:13 before, /device:TPU:0 now
where the time goes in v2:
time: 65.6 us; the launch traced here: 64.5 us
  starting transfers between devices  21.7 us (33%)
  local copies, waits for them, and re-layouts  19.4 us (30%)
  waiting for transfers between devices  10.4 us (16%)
  Pallas kernels  10.1 us (15%)
  between operations  1.43 us (2%)
  other arithmetic  1.39 us (2%)
    unnamed x54, local copies, waits for them, and re-layouts  18.8 us
    all_to_all x1, starting transfers between devices, local(): surfaces = lax.all_to_all(partial_surface, ('comp', 'gy'), 0, 0, tiled=True)  7.09 us
    all_to_all x1, starting transfers between devices, local(): parts = lax.all_to_all(sent, 'gy', 0, 0, tiled=True)  5.08 us
    all_to_all x1, waiting for transfers between devices, local(): heat = lax.all_to_all(short, 'gx', 0, 0, tiled=True)  4.07 us
    pallas_call x1, Pallas kernels, local(): pl.pallas_call(regrid_kernel, out_shape=[shape((cells, LANES), f32), shap...  3.78 us
    ppermute x1, starting transfers between devices, local(): e3 = lax.ppermute(e3, ('comp', 'gx'), gx_route(1))  3.5 us
    all_to_all x1, starting transfers between devices, local(): heat = lax.all_to_all(short, 'gx', 0, 0, tiled=True)  3.28 us
    ppermute x1, waiting for transfers between devices, local(): e3 = lax.ppermute(e3, ('comp', 'gx'), gx_route(1))  3.24 us
  transfers between devices with their start and end apart: 7, of which 3 were waited for; matrix products, arithmetic and copies ran while one was open for 3% of the time, Pallas kernels for 3%

profile of v2, /device:TPU:0, one launch (start us, length us, event | category | flops | bytes accessed | tf_op | source)
XLA Modules:
  0.0 64.5 jit_solution(9788971568915749795)
XLA Ops:
  0.0 1.2 %copy-done = f32[1,8,32,1024]{3,2,1,0:T(8,128)S(1)} copy-done((f32[1,8,32,1024]{3,2,1,0:T(8,128)S(1)}, f32[1,8,32,1024]{3,2,1,0:T(8,128)}, u32[]{:S(2)}) %copy-start) | copy-done | bytes 1048600
  1.2 0.0 copy-start.23
  1.2 0.7 %copy-done.23 = f32[128]{0:T(128)S(1)} copy-done((f32[128]{0:T(128)S(1)}, f32[128]{0:T(128)}, u32[]{:S(2)}) %copy-start.23) | copy-done | bytes 536
  1.9 0.0 copy-start.1
  1.9 0.0 copy-start.15
  1.9 0.0 copy-start.16
  1.9 0.0 copy-start.17
  1.9 0.9 %surface_partials.1.after_ref = bf16[8,64,128]{2,1,0:T(8,128)(2,1)} custom-call(f32[1,8,32,1024]{3,2,1,0:T(8,128)S(1)} %copy-done, f32[1,128]{1,0:T(1,128)S(1)} %bitcast.23), custom_call_target="tpu_custom_call" | custom-call | tf_op jit(solution)/shard_map/surface_partials/pallas_call | solution.py:547
  2.8 7.1 %all-to-all-start = ((bf16[8,64,128]{2,1,0:T(8,128)(2,1)}), bf16[8,64,128]{2,1,0:T(8,128)(2,1)}, u32[]{:S(2)}, u32[]{:S(2)}) async-start(bf16[8,64,128]{2,1,0:T(8,128)(2,1)} %surface_partials.1.after_ref), calls=%async_computation | async-start | bytes 262144 | tf_op jit(solution)/shard_map/all_to_all | solution.py:556
  9.9 0.0 copy-done.1
  9.9 0.0 copy-start.3
  9.9 1.6 %copy-done.3 = bf16[1024,1024]{1,0:T(8,128)(2,1)S(1)} copy-done((bf16[1024,1024]{1,0:T(8,128)(2,1)S(1)}, bf16[1024,1024]{1,0:T(8,128)(2,1)}, u32[]{:S(2)}) %copy-start.3) | copy-done | bytes 2097176
  11.5 0.0 copy-start.8
  11.5 0.8 %copy-done.8 = s32[8,1024]{1,0:T(8,128)S(1)} copy-done((s32[8,1024]{1,0:T(8,128)S(1)}, s32[8,1024]{1,0:T(8,128)}, u32[]{:S(2)}) %copy-start.8) | copy-done | bytes 32792
  12.2 0.0 copy-start.19
  12.2 0.7 %copy-done.19 = f32[1,512]{1,0:T(1,128)S(1)} copy-done((f32[1,512]{1,0:T(1,128)S(1)}, f32[1,512]{1,0:T(1,128)}, u32[]{:S(2)}) %copy-start.19) | copy-done | bytes 2072
  12.9 0.0 copy-start.21
  12.9 0.7 %copy-done.21 = f32[128]{0:T(128)S(1)} copy-done((f32[128]{0:T(128)S(1)}, f32[128]{0:T(128)}, u32[]{:S(2)}) %copy-start.21) | copy-done | bytes 536
  13.6 2.2 %forward_and_halos.1 = (f32[8,32,1024]{2,1,0:T(8,128)S(1)}, bf16[80,1024]{1,0:T(8,128)(2,1)S(1)}, bf16[80,1024]{1,0:T(8,128)(2,1)S(1)}, bf16[48,1024]{1,0:T(8,128)(2,1)S(1)}, bf16[48,1024]{1,0:T(8,128)(2,1)S(1)}) custom-call(f32[1,8,32,1024]{3,2,1,0:T(8,128)S(1)} %copy-done.1, s32[8,1024]{1,0:T(8,128)S(1)} %copy-done.8, f32[1,128]{1,0:T(1,128)S(1)} %bitcast.21, ...), custom_call_target="tpu_custom_call" | custom-call | tf_op jit(solution)/shard_map/forward_and_halos/pallas_call | solution.py:569
  15.8 0.0 copy-start.6
  15.8 1.0 %copy-done.6 = f32[8,32,1024]{2,1,0:T(8,128)} copy-done((f32[8,32,1024]{2,1,0:T(8,128)}, f32[8,32,1024]{2,1,0:T(8,128)S(1)}, u32[]{:S(2)}) %copy-start.6) | copy-done | bytes 1048600
  16.8 0.0 copy-start.11
  16.8 0.6 copy-done.11
  17.4 0.0 copy-start.13
  17.4 0.6 copy-done.13
  18.1 0.0 copy-start.2
  18.1 0.0 collective-permute-start
  18.1 3.5 %collective-permute-start.1 = (bf16[80,1024]{1,0:T(8,128)(2,1)S(1)}, bf16[80,1024]{1,0:T(8,128)(2,1)S(1)}, u32[]{:S(2)}, u32[]{:S(2)}) collective-permute-start(bf16[80,1024]{1,0:T(8,128)(2,1)S(1)} %get-tuple-element.16), channel_id=1, source_target_pairs={{20,24},{24,20},{0,12},{12,0},{4,8},{8,4},{21,25},{25,21},{1,13},{... | collective-permute-start | bytes 491528 | tf_op jit(solution)/shard_map/ppermute | solution.py:592
  22.9 0.0 collective-permute-done.refs_9_.refs_7_
  22.9 3.2 %collective-permute-done.1.refs_10_.refs_8_ = bf16[80,1024]{1,0:T(8,128)(2,1)S(1)} collective-permute-done((bf16[80,1024]{1,0:T(8,128)(2,1)S(1)}, bf16[80,1024]{1,0:T(8,128)(2,1)S(1)}, u32[]{:S(2)}, u32[]{:S(2)}) %collective-permute-start.1) | collective-permute-done | bytes 163872 | tf_op jit(solution)/shard_map/ppermute | solution.py:592
  26.1 0.0 all-to-all-done.refs_0_
  26.1 0.0 copy-done.15
  26.1 0.0 copy-done.16
  26.1 0.0 copy-done.17
  26.1 0.0 copy-start.4
  26.2 1.2 %copy-done.4 = bf16[1,1,32,128,128]{4,3,2,1,0:T(8,128)(2,1)S(1)} copy-done((bf16[1,1,32,128,128]{4,3,2,1,0:T(8,128)(2,1)S(1)}, bf16[1,1,32,128,128]{4,3,2,1,0:T(8,128)(2,1)}, u32[]{:S(2)}) %copy-start.4) | copy-done | bytes 1048600
  27.4 0.0 copy-start.5
  27.4 1.2 %copy-done.5 = bf16[1,1,32,128,128]{4,3,2,1,0:T(8,128)(2,1)S(1)} copy-done((bf16[1,1,32,128,128]{4,3,2,1,0:T(8,128)(2,1)S(1)}, bf16[1,1,32,128,128]{4,3,2,1,0:T(8,128)(2,1)}, u32[]{:S(2)}) %copy-start.5) | copy-done | bytes 1048600
  28.6 0.0 copy-start.12
  28.6 0.9 %copy-done.12 = bf16[48,1024]{1,0:T(8,128)(2,1)S(1)} copy-done((bf16[48,1024]{1,0:T(8,128)(2,1)S(1)}, bf16[48,1024]{1,0:T(8,128)(2,1)}, u32[]{:S(2)}) %copy-start.12) | copy-done | bytes 98328
  29.5 0.9 %copy-done.14 = bf16[48,1024]{1,0:T(8,128)(2,1)S(1)} copy-done((bf16[48,1024]{1,0:T(8,128)(2,1)S(1)}, bf16[48,1024]{1,0:T(8,128)(2,1)}, u32[]{:S(2)}) %copy-start.14) | copy-done | bytes 98328
  30.4 0.7 %copy-done.18 = s32[1,1,32,128]{3,2,1,0:T(8,128)S(1)} copy-done((s32[1,1,32,128]{3,2,1,0:T(8,128)S(1)}, s32[1,1,32,128]{3,2,1,0:T(8,128)}, u32[]{:S(2)}) %copy-start.18) | copy-done | bytes 16408
  31.1 3.8 %regrid_blocks.1 = (f32[64,128]{1,0:T(8,128)S(1)}, bf16[4,64,128]{2,1,0:T(8,128)(2,1)}, bf16[48,1024]{1,0:T(8,128)(2,1)S(1)}, bf16[48,1024]{1,0:T(8,128)(2,1)S(1)}) custom-call(bf16[8,64,128]{2,1,0:T(8,128)(2,1)} %all-to-all-done.refs_0_, s32[1,1,32,128]{3,2,1,0:T(8,128)S(1)} %copy-done.15, s32[1,1,32,128]{3,2,1,0:T(8,128)S(1)} %copy-done.16, ...), custom_call_target="tpu_custom_call" | custom-call | tf_op jit(solution)/shard_map/regrid_blocks/pallas_call | solution.py:594
  34.9 0.0 copy-start.25
  34.9 0.6 copy-done.25
  35.5 0.6 %copy-done.26 = bf16[48,1024]{1,0:T(8,128)(2,1)} copy-done((bf16[48,1024]{1,0:T(8,128)(2,1)}, bf16[48,1024]{1,0:T(8,128)(2,1)S(1)}, u32[]{:S(2)}) %copy-start.26) | copy-done | bytes 98328
  36.2 5.1 %all-to-all-start.1 = ((bf16[4,64,128]{2,1,0:T(8,128)(2,1)}), bf16[4,64,128]{2,1,0:T(8,128)(2,1)}, u32[]{:S(2)}, u32[]{:S(2)}) async-start(bf16[4,64,128]{2,1,0:T(8,128)(2,1)} %get-tuple-element.22), calls=%async_computation.1 | async-start | bytes 131072 | tf_op jit(solution)/shard_map/all_to_all | solution.py:622
  41.3 1.5 %collective-permute-start.2 = (bf16[48,1024]{1,0:T(8,128)(2,1)}, bf16[48,1024]{1,0:T(8,128)(2,1)}, u32[]{:S(2)}, u32[]{:S(2)}) collective-permute-start(bf16[48,1024]{1,0:T(8,128)(2,1)} %copy-done.26), channel_id=1, source_target_pairs={{16,17},{17,16},{18,19},{19,18},{20,21},{21,20},{22,23},{23,22},{2... | collective-permute-start | bytes 294920 | tf_op jit(solution)/shard_map/ppermute | solution.py:648
  42.8 1.3 %collective-permute-start.3 = (bf16[48,1024]{1,0:T(8,128)(2,1)}, bf16[48,1024]{1,0:T(8,128)(2,1)}, u32[]{:S(2)}, u32[]{:S(2)}) collective-permute-start(bf16[48,1024]{1,0:T(8,128)(2,1)} %copy-done.25), channel_id=1, source_target_pairs={{17,18},{18,17},{21,22},{22,21},{25,26},{26,25},{29,30},{30,29}} | collective-permute-start | bytes 294920 | tf_op jit(solution)/shard_map/ppermute | solution.py:649
  44.0 3.1 %all-to-all-done.1 = bf16[4,64,128]{2,1,0:T(8,128)(2,1)} async-done(((bf16[4,64,128]{2,1,0:T(8,128)(2,1)}), bf16[4,64,128]{2,1,0:T(8,128)(2,1)}, u32[]{:S(2)}, u32[]{:S(2)}) %all-to-all-start.1) | async-done | bytes 65568 | tf_op jit(solution)/shard_map/all_to_all | solution.py:622
  47.1 1.4 %fusion = (bf16[64,128]{1,0:T(8,128)(2,1)S(1)}, f32[64,128]{1,0:T(8,128)}) fusion(bf16[4,64,128]{2,1,0:T(8,128)(2,1)} %all-to-all-done.1, pred[]{:T(512)S(6)} %eq.15, pred[]{:T(512)S(6)} %eq.14, pred[]{:T(512)S(6)} %eq.13, f32[64,128]{1,0:T(8,128)S(1)} %get-tuple-element.21, pred[]{:T(512)S(6)} %eq.12), kind=kLoop, calls=%fused_computation.4 | loop fusion | flops 106496 | bytes 147460 | tf_op jit(solution)/shard_map/convert_element_type | solution.py:651
  48.5 0.6 broadcast_in_dim.23
  49.1 3.3 %all-to-all-start.2 = ((bf16[4,64,128]{2,1,0:T(8,128)(2,1)}), bf16[4,64,128]{2,1,0:T(8,128)(2,1)S(1)}, u32[]{:S(2)}, u32[]{:S(2)}) async-start(bf16[4,64,128]{2,1,0:T(8,128)(2,1)} %broadcast_in_dim.23), calls=%async_computation.2 | async-start | bytes 131072 | tf_op jit(solution)/shard_map/all_to_all | solution.py:652
  52.4 0.0 collective-permute-done.2.refs_9_
  52.4 0.0 collective-permute-done.3.refs_10_
  52.4 4.1 %all-to-all-done.2.refs_12_ = bf16[4,64,128]{2,1,0:T(8,128)(2,1)S(1)} async-done(((bf16[4,64,128]{2,1,0:T(8,128)(2,1)}), bf16[4,64,128]{2,1,0:T(8,128)(2,1)S(1)}, u32[]{:S(2)}, u32[]{:S(2)}) %all-to-all-start.2) | async-done | bytes 65568 | tf_op jit(solution)/shard_map/all_to_all | solution.py:652
  56.5 0.0 copy-done.2
  56.5 1.2 %copy-done.7 = f32[8,32,1024]{2,1,0:T(8,128)S(1)} copy-done((f32[8,32,1024]{2,1,0:T(8,128)S(1)}, f32[8,32,1024]{2,1,0:T(8,128)}, u32[]{:S(2)}) %copy-start.7) | copy-done | bytes 1048600
  57.7 0.8 %copy-done.9 = s32[8,1024]{1,0:T(8,128)S(1)} copy-done((s32[8,1024]{1,0:T(8,128)S(1)}, s32[8,1024]{1,0:T(8,128)}, u32[]{:S(2)}) %copy-start.9) | copy-done | bytes 32792
  58.5 0.8 %copy-done.10 = f32[64,128]{1,0:T(8,128)S(1)} copy-done((f32[64,128]{1,0:T(8,128)S(1)}, f32[64,128]{1,0:T(8,128)}, u32[]{:S(2)}) %copy-start.10) | copy-done | bytes 32792
  59.3 0.7 %copy-done.20 = f32[1,512]{1,0:T(1,128)S(1)} copy-done((f32[1,512]{1,0:T(1,128)S(1)}, f32[1,512]{1,0:T(1,128)}, u32[]{:S(2)}) %copy-start.20) | copy-done | bytes 2072
  59.9 0.7 %copy-done.22 = f32[128]{0:T(128)S(1)} copy-done((f32[128]{0:T(128)S(1)}, f32[128]{0:T(128)}, u32[]{:S(2)}) %copy-start.22) | copy-done | bytes 536
  60.6 0.7 %copy-done.24 = f32[128]{0:T(128)S(1)} copy-done((f32[128]{0:T(128)S(1)}, f32[128]{0:T(128)}, u32[]{:S(2)}) %copy-start.24) | copy-done | bytes 536
  61.3 3.2 %inverse_or_ocean_steps.1 = f32[1,8,32,1024]{3,2,1,0:T(8,128)} custom-call(f32[1,8,32,1024]{3,2,1,0:T(8,128)S(1)} %copy-done.1, s32[8,1024]{1,0:T(8,128)S(1)} %copy-done.9, f32[1,128]{1,0:T(1,128)S(1)} %bitcast.22, f32[1,128]{1,0:T(1,128)S(1)} %bitcast.24, f32[1,512]{1,0:T(1,128)S(1)} %copy-done.20, bf16[1024,1024]{1,0:T(8,128)(2,1)S(1)} %copy-done.2, ...), custom_call_target="tpu_custom_call" | custom-call | tf_op jit(solution)/shard_map/inverse_or_ocean_steps/pallas_call | solution.py:672
  (10 shorter events, 0.0 us)
Async XLA Ops:
  0.0 1.2 %copy-start = (f32[1,8,32,1024]{3,2,1,0:T(8,128)S(1)}, f32[1,8,32,1024]{3,2,1,0:T(8,128)}, u32[]{:S(2)}) copy-start(f32[1,8,32,1024]{3,2,1,0:T(8,128)} %refs_0_.1) | copy-start | bytes 3145732
  1.2 0.7 %copy-start.23 = (f32[128]{0:T(128)S(1)}, f32[128]{0:T(128)}, u32[]{:S(2)}) copy-start(f32[128]{0:T(128)} %param.18) | copy-start | bytes 1540
  1.9 8.0 %copy-start.1 = (f32[1,8,32,1024]{3,2,1,0:T(8,128)S(1)}, f32[1,8,32,1024]{3,2,1,0:T(8,128)}, u32[]{:S(2)}) copy-start(f32[1,8,32,1024]{3,2,1,0:T(8,128)} %refs_0_.1) | copy-start | bytes 3145732
  1.9 24.2 %copy-start.15 = (s32[1,1,32,128]{3,2,1,0:T(8,128)S(1)}, s32[1,1,32,128]{3,2,1,0:T(8,128)}, u32[]{:S(2)}) copy-start(s32[1,1,32,128]{3,2,1,0:T(8,128)} %refs_1_.2) | copy-start | bytes 49156
  1.9 24.2 %copy-start.16 = (s32[1,1,32,128]{3,2,1,0:T(8,128)S(1)}, s32[1,1,32,128]{3,2,1,0:T(8,128)}, u32[]{:S(2)}) copy-start(s32[1,1,32,128]{3,2,1,0:T(8,128)} %refs_2_.1) | copy-start | bytes 49156
  1.9 24.2 %copy-start.17 = (s32[1,1,32,128]{3,2,1,0:T(8,128)S(1)}, s32[1,1,32,128]{3,2,1,0:T(8,128)}, u32[]{:S(2)}) copy-start(s32[1,1,32,128]{3,2,1,0:T(8,128)} %refs_5_.2) | copy-start | bytes 49156
  2.8 23.3 %all-to-all-start = ((bf16[8,64,128]{2,1,0:T(8,128)(2,1)}), bf16[8,64,128]{2,1,0:T(8,128)(2,1)}, u32[]{:S(2)}, u32[]{:S(2)}) async-start(bf16[8,64,128]{2,1,0:T(8,128)(2,1)} %surface_partials.1.after_ref), calls=%async_computation | async-start | bytes 262144 | tf_op jit(solution)/shard_map/all_to_all | solution.py:556
  9.9 1.6 %copy-start.3 = (bf16[1024,1024]{1,0:T(8,128)(2,1)S(1)}, bf16[1024,1024]{1,0:T(8,128)(2,1)}, u32[]{:S(2)}) copy-start(bf16[1024,1024]{1,0:T(8,128)(2,1)} %constant.20.clone.table_hbm) | copy-start | bytes 6291460
  11.5 0.8 %copy-start.8 = (s32[8,1024]{1,0:T(8,128)S(1)}, s32[8,1024]{1,0:T(8,128)}, u32[]{:S(2)}) copy-start(s32[8,1024]{1,0:T(8,128)} %refs_1_.3) | copy-start | bytes 98308
  12.2 0.7 %copy-start.19 = (f32[1,512]{1,0:T(1,128)S(1)}, f32[1,512]{1,0:T(1,128)}, u32[]{:S(2)}) copy-start(f32[1,512]{1,0:T(1,128)} %constant.22.clone.rates_ref.refs_4_) | copy-start | bytes 6148
  12.9 0.7 %copy-start.21 = (f32[128]{0:T(128)S(1)}, f32[128]{0:T(128)}, u32[]{:S(2)}) copy-start(f32[128]{0:T(128)} %param.20) | copy-start | bytes 1540
  15.8 1.0 %copy-start.6 = (f32[8,32,1024]{2,1,0:T(8,128)}, f32[8,32,1024]{2,1,0:T(8,128)S(1)}, u32[]{:S(2)}) copy-start(f32[8,32,1024]{2,1,0:T(8,128)S(1)} %get-tuple-element.14.refs_6_) | copy-start | bytes 3145732
  16.8 0.6 copy-start.11
  17.4 0.6 copy-start.13
  18.1 38.4 %copy-start.2 = (bf16[1024,1024]{1,0:T(8,128)(2,1)S(1)}, bf16[1024,1024]{1,0:T(8,128)(2,1)}, u32[]{:S(2)}) copy-start(bf16[1024,1024]{1,0:T(8,128)(2,1)} %constant.21.clone.refs_5_) | copy-start | bytes 6291460
  18.1 4.8 %collective-permute-start = (bf16[80,1024]{1,0:T(8,128)(2,1)S(1)}, bf16[80,1024]{1,0:T(8,128)(2,1)S(1)}, u32[]{:S(2)}, u32[]{:S(2)}) collective-permute-start(bf16[80,1024]{1,0:T(8,128)(2,1)S(1)} %get-tuple-element.15), channel_id=1, source_target_pairs={{16,20},{20,16},{24,28},{28,24},{0,4},{4,0},{8,12},{12,8},{17,21},... | collective-permute-start | bytes 491528 | tf_op jit(solution)/shard_map/ppermute | solution.py:591
  18.1 8.1 %collective-permute-start.1 = (bf16[80,1024]{1,0:T(8,128)(2,1)S(1)}, bf16[80,1024]{1,0:T(8,128)(2,1)S(1)}, u32[]{:S(2)}, u32[]{:S(2)}) collective-permute-start(bf16[80,1024]{1,0:T(8,128)(2,1)S(1)} %get-tuple-element.16), channel_id=1, source_target_pairs={{20,24},{24,20},{0,12},{12,0},{4,8},{8,4},{21,25},{25,21},{1,13},{... | collective-permute-start | bytes 491528 | tf_op jit(solution)/shard_map/ppermute | solution.py:592
  26.1 1.2 %copy-start.4 = (bf16[1,1,32,128,128]{4,3,2,1,0:T(8,128)(2,1)S(1)}, bf16[1,1,32,128,128]{4,3,2,1,0:T(8,128)(2,1)}, u32[]{:S(2)}) copy-start(bf16[1,1,32,128,128]{4,3,2,1,0:T(8,128)(2,1)} %refs_4_.2) | copy-start | bytes 3145732
  27.4 1.2 %copy-start.5 = (bf16[1,1,32,128,128]{4,3,2,1,0:T(8,128)(2,1)S(1)}, bf16[1,1,32,128,128]{4,3,2,1,0:T(8,128)(2,1)}, u32[]{:S(2)}) copy-start(bf16[1,1,32,128,128]{4,3,2,1,0:T(8,128)(2,1)} %refs_8_.1) | copy-start | bytes 3145732
  28.6 0.9 %copy-start.12 = (bf16[48,1024]{1,0:T(8,128)(2,1)S(1)}, bf16[48,1024]{1,0:T(8,128)(2,1)}, u32[]{:S(2)}) copy-start(bf16[48,1024]{1,0:T(8,128)(2,1)} %copy-done.11) | copy-start | bytes 294916
  29.5 0.9 %copy-start.14 = (bf16[48,1024]{1,0:T(8,128)(2,1)S(1)}, bf16[48,1024]{1,0:T(8,128)(2,1)}, u32[]{:S(2)}) copy-start(bf16[48,1024]{1,0:T(8,128)(2,1)} %copy-done.13) | copy-start | bytes 294916
  30.4 0.7 %copy-start.18 = (s32[1,1,32,128]{3,2,1,0:T(8,128)S(1)}, s32[1,1,32,128]{3,2,1,0:T(8,128)}, u32[]{:S(2)}) copy-start(s32[1,1,32,128]{3,2,1,0:T(8,128)} %refs_6_.1) | copy-start | bytes 49156
  34.9 0.6 copy-start.25
  35.5 0.7 %copy-start.26 = (bf16[48,1024]{1,0:T(8,128)(2,1)}, bf16[48,1024]{1,0:T(8,128)(2,1)S(1)}, u32[]{:S(2)}) copy-start(bf16[48,1024]{1,0:T(8,128)(2,1)S(1)} %get-tuple-element.19) | copy-start | bytes 294916
  36.2 10.9 %all-to-all-start.1 = ((bf16[4,64,128]{2,1,0:T(8,128)(2,1)}), bf16[4,64,128]{2,1,0:T(8,128)(2,1)}, u32[]{:S(2)}, u32[]{:S(2)}) async-start(bf16[4,64,128]{2,1,0:T(8,128)(2,1)} %get-tuple-element.22), calls=%async_computation.1 | async-start | bytes 131072 | tf_op jit(solution)/shard_map/all_to_all | solution.py:622
  41.3 11.2 %collective-permute-start.2 = (bf16[48,1024]{1,0:T(8,128)(2,1)}, bf16[48,1024]{1,0:T(8,128)(2,1)}, u32[]{:S(2)}, u32[]{:S(2)}) collective-permute-start(bf16[48,1024]{1,0:T(8,128)(2,1)} %copy-done.26), channel_id=1, source_target_pairs={{16,17},{17,16},{18,19},{19,18},{20,21},{21,20},{22,23},{23,22},{2... | collective-permute-start | bytes 294920 | tf_op jit(solution)/shard_map/ppermute | solution.py:648
  42.8 9.7 %collective-permute-start.3 = (bf16[48,1024]{1,0:T(8,128)(2,1)}, bf16[48,1024]{1,0:T(8,128)(2,1)}, u32[]{:S(2)}, u32[]{:S(2)}) collective-permute-start(bf16[48,1024]{1,0:T(8,128)(2,1)} %copy-done.25), channel_id=1, source_target_pairs={{17,18},{18,17},{21,22},{22,21},{25,26},{26,25},{29,30},{30,29}} | collective-permute-start | bytes 294920 | tf_op jit(solution)/shard_map/ppermute | solution.py:649
  49.1 7.4 %all-to-all-start.2 = ((bf16[4,64,128]{2,1,0:T(8,128)(2,1)}), bf16[4,64,128]{2,1,0:T(8,128)(2,1)S(1)}, u32[]{:S(2)}, u32[]{:S(2)}) async-start(bf16[4,64,128]{2,1,0:T(8,128)(2,1)} %broadcast_in_dim.23), calls=%async_computation.2 | async-start | bytes 131072 | tf_op jit(solution)/shard_map/all_to_all | solution.py:652
  56.5 1.2 %copy-start.7 = (f32[8,32,1024]{2,1,0:T(8,128)S(1)}, f32[8,32,1024]{2,1,0:T(8,128)}, u32[]{:S(2)}) copy-start(f32[8,32,1024]{2,1,0:T(8,128)} %copy-done.6) | copy-start | bytes 3145732
  57.7 0.8 %copy-start.9 = (s32[8,1024]{1,0:T(8,128)S(1)}, s32[8,1024]{1,0:T(8,128)}, u32[]{:S(2)}) copy-start(s32[8,1024]{1,0:T(8,128)} %refs_1_.3) | copy-start | bytes 98308
  58.5 0.8 %copy-start.10 = (f32[64,128]{1,0:T(8,128)S(1)}, f32[64,128]{1,0:T(8,128)}, u32[]{:S(2)}) copy-start(f32[64,128]{1,0:T(8,128)} %get-tuple-element.24.refs_11_) | copy-start | bytes 98308
  59.3 0.7 %copy-start.20 = (f32[1,512]{1,0:T(1,128)S(1)}, f32[1,512]{1,0:T(1,128)}, u32[]{:S(2)}) copy-start(f32[1,512]{1,0:T(1,128)} %constant.22.clone.rates_ref.refs_4_) | copy-start | bytes 6148
  59.9 0.7 %copy-start.22 = (f32[128]{0:T(128)S(1)}, f32[128]{0:T(128)}, u32[]{:S(2)}) copy-start(f32[128]{0:T(128)} %param.20) | copy-start | bytes 1540
  60.6 0.7 %copy-start.24 = (f32[128]{0:T(128)S(1)}, f32[128]{0:T(128)}, u32[]{:S(2)}) copy-start(f32[128]{0:T(128)} %param.19) | copy-start | bytes 1540

commit v3 on v1

v3 whole, which is shorter than its diff:
```python
import functools

import jax
import jax.numpy as jnp
import numpy as np
from jax import lax
from jax.experimental import pallas as pl
from jax.experimental.pallas import tpu as pltpu
from jax.sharding import PartitionSpec as P

spread_rate = 0.2
mixing_rate = 0.1
heat_gain = 0.5
salt_gain = -0.25
LANES = 128
f32 = jnp.float32
bf16 = jnp.bfloat16


def fourier_tables(columns):
    waves = np.arange(columns // 2)
    phase = np.arange(columns)[:, None] * waves[None, :] % columns
    angles = phase * (2.0 * np.pi / columns)
    forward = np.concatenate([np.cos(angles), np.sin(angles)], axis=1)
    weight = np.where(np.arange(columns) % (columns // 2) == 0, 1.0, 2.0) / columns
    inverse = forward.T * weight[:, None]
    half_rates = 2.0 * np.sin(np.pi * waves / columns) ** 2
    return (
        jnp.asarray(forward.astype(np.float32), bf16),
        jnp.asarray(inverse.astype(np.float32), bf16),
        jnp.asarray(half_rates[None, :].astype(np.float32)),
    )


def both_ways(pairs):
    return [p for a, b in pairs for p in ((a, b), (b, a))]


def channel_column(row, channels, first):
    n = row.shape[1]
    lane = lax.broadcasted_iota(jnp.int32, (channels, n), 1)
    sub = lax.broadcasted_iota(jnp.int32, (channels, n), 0)
    return jnp.sum(jnp.where(lane == sub + first, row, 0.0), axis=1, keepdims=True)


def to_tiles(surface):
    cols = surface.shape[1]
    return jnp.concatenate(
        [surface[:, k : k + LANES] for k in range(0, cols, LANES)], axis=0
    )


def from_tiles(tiles, rows):
    return jnp.concatenate(
        [tiles[k : k + rows] for k in range(0, tiles.shape[0], rows)], axis=1
    )


def surface_kernel(x_ref, flux_ref, s_ref, row_ref):
    _, rows, channels, columns = x_ref.shape
    col_group = lax.axis_index("gy")
    is_atmos = lax.axis_index("comp") == 0

    @pl.when(is_atmos)
    def _():
        weight = channel_column(flux_ref[...], channels, col_group * channels)
        for r in range(rows):
            row_ref[r : r + 1, :] = jnp.sum(x_ref[0, r] * weight, axis=0, keepdims=True)
        s_ref[...] = to_tiles(row_ref[...]).astype(bf16)

    @pl.when(jnp.logical_not(is_atmos))
    def _():
        gain = jnp.where(col_group == 0, 1.0, 0.0)
        for r in range(rows):
            row_ref[r : r + 1, :] = x_ref[0, r, 0:1, :] * gain
        s_ref[...] = to_tiles(row_ref[...]).astype(bf16)


def decay_terms(diff_column, half_rates):
    half = 0.5 / diff_column + half_rates
    sinh = jnp.sqrt(half * (half + 2.0))
    grow = 1.0 + half + sinh
    return 1.0 / grow, jnp.log(grow), sinh


def forward_kernel(
    groups_x, x_ref, wet_ref, diff_ref, rates_ref, table_ref, after_ref,
    y_ref, beside_ref, edges_ref, edge_ref,
):
    del after_ref
    _, rows, channels, columns = x_ref.shape
    waves = columns // 2
    row_group = lax.axis_index("gx")
    col_group = lax.axis_index("gy")
    is_atmos = lax.axis_index("comp") == 0

    @pl.when(is_atmos)
    def _():
        step = 256
        flat = x_ref[0].astype(bf16).reshape(rows * channels, columns)
        for n in range(0, columns, step):
            part = jnp.dot(flat, table_ref[:, n : n + step], preferred_element_type=f32)
            y_ref[:, :, n : n + step] = part.reshape(rows, channels, step)
        diff = channel_column(diff_ref[...], channels, col_group * channels)
        total = rows * groups_x
        base = (row_group * rows).astype(f32)
        for n in range(0, waves, LANES):
            lam, alpha, _ = decay_terms(diff, rates_ref[:, n : n + LANES])
            lam2 = lam * lam
            low = jnp.exp(-2.0 * base * alpha)
            high = jnp.exp(-2.0 * (total - rows - base) * alpha)
            for part in (n, n + waves):
                lanes = slice(part, part + LANES)
                power = low
                p = jnp.zeros((channels, LANES), f32)
                for r in range(rows):
                    power = power * lam2
                    p = lam * p + (1.0 - power) * y_ref[r, :, lanes]
                power = high
                q = jnp.zeros((channels, LANES), f32)
                for r in reversed(range(rows)):
                    power = power * lam2
                    q = lam * q + (1.0 - power) * y_ref[r, :, lanes]
                beside_ref[0:channels, lanes] = p.astype(bf16)
                beside_ref[channels : 2 * channels, lanes] = q.astype(bf16)

    @pl.when(jnp.logical_not(is_atmos))
    def _():
        levels = channels // 2
        lines = 2 * channels
        wet = wet_ref[...].astype(f32)
        beside_ref[0:lines, :] = x_ref[0, :2].reshape(lines, columns).astype(bf16)
        beside_ref[lines : 2 * lines, :] = (
            x_ref[0, rows - 2 :].reshape(lines, columns).astype(bf16)
        )
        beside_ref[2 * lines : 2 * lines + 16, :] = jnp.concatenate([wet, wet], axis=0).astype(
            bf16
        )
        for r in range(rows):
            for t in range(2):
                at = (r * 2 + t) * 4
                c = t * levels
                edge_ref[at : at + 2, :] = x_ref[0, r, c : c + 2, :]
                edge_ref[at + 2 : at + 4, :] = x_ref[0, r, c + levels - 2 : c + levels, :]
        edges_ref[...] = edge_ref[...].astype(bf16)


def regrid_kernel(n_msgs, *refs):
    msgs = refs[:n_msgs]
    (
        a_src, a_dst, a_count, a_weight, m_src, m_dst, m_count, m_weight,
        land_ref, sent_ref, weight_ref, gath_ref, val_ref, sem,
    ) = refs[n_msgs:]
    is_atmos = lax.axis_index("comp") == 0
    blocks, points = val_ref.shape
    cells = msgs[0].shape[0]
    rows = 8

    @pl.when(is_atmos)
    def _():
        pltpu.make_async_copy(m_weight.at[0, 0], weight_ref, sem).start()

    @pl.when(jnp.logical_not(is_atmos))
    def _():
        pltpu.make_async_copy(a_weight.at[0, 0], weight_ref, sem).start()

    src = jnp.where(is_atmos, m_src[0, 0], a_src[0, 0])
    dst = jnp.where(is_atmos, m_dst[0, 0], a_dst[0, 0])
    count = jnp.where(is_atmos, m_count[0, 0], a_count[0, 0])
    tiles = cells // rows

    def split(index):
        row = index // (tiles * LANES)
        tile = (index // LANES) % tiles
        return tile * rows + row, index % LANES

    src_row, src_lane = split(src)
    dst_row, dst_lane = split(dst)
    lane_iota = lax.broadcasted_iota(jnp.int32, (LANES, points), 0)
    row_iota = lax.broadcasted_iota(jnp.int32, (cells, points), 0)
    table = msgs[0][...].astype(f32)
    for m in msgs[1:]:
        table = table + m[...].astype(f32)
    table = table.astype(bf16)
    for b in range(blocks):
        hot = jnp.where(lane_iota == src_lane[b : b + 1], 1.0, 0.0).astype(bf16)
        picked = jnp.dot(table, hot, preferred_element_type=f32)
        picked = jnp.where(row_iota == src_row[b : b + 1], picked, 0.0)
        gath_ref[b : b + 1, :] = jnp.sum(picked, axis=0, keepdims=True)
    gathered = gath_ref[...].astype(bf16)

    @pl.when(is_atmos)
    def _():
        pltpu.make_async_copy(m_weight.at[0, 0], weight_ref, sem).wait()

    @pl.when(jnp.logical_not(is_atmos))
    def _():
        pltpu.make_async_copy(a_weight.at[0, 0], weight_ref, sem).wait()

    block_iota = lax.broadcasted_iota(jnp.int32, (blocks, points), 0)
    values = jnp.zeros((blocks, points), f32)
    for b in range(blocks):
        term = lax.dot_general(
            gathered, weight_ref[b], (((1,), (1,)), ((), ())), preferred_element_type=f32
        )
        values = jnp.where(block_iota == b, term, values)
    val_ref[...] = jnp.where(block_iota < count, values, 0.0)
    land = jnp.zeros((2 * cells, LANES), f32)
    for b in range(blocks):
        value = val_ref[b : b + 1, :]
        coarse = value.astype(bf16).astype(f32)
        fine = value - coarse
        mine = row_iota == dst_row[b : b + 1]
        both = jnp.concatenate(
            [jnp.where(mine, coarse, 0.0), jnp.where(mine, fine, 0.0)], axis=0
        ).astype(bf16)
        hot = jnp.where(lane_iota == dst_lane[b : b + 1], 1.0, 0.0).astype(bf16)
        land = land + lax.dot_general(
            both, hot, (((1,), (1,)), ((), ())), preferred_element_type=f32
        )
    land = land[:cells] + land[cells:]
    land_ref[...] = land
    sent_ref[...] = land.astype(bf16)


def heat_kernel(rows, levels_edges_ref, land_ref, *refs):
    parts = refs[:-3]
    sum_ref, near_ref, far_ref = refs[-3:]
    cells = land_ref.shape[0]
    columns = cells // rows * LANES
    groups_y = levels_edges_ref.shape[0]
    row_group = lax.axis_index("gx")
    col_group = lax.axis_index("gy")
    total = land_ref[...]
    for part in parts:
        total = total + part[...].astype(f32)
    sum_ref[...] = total
    before = jnp.maximum(col_group - 1, 0)
    after = jnp.minimum(col_group + 1, groups_y - 1)

    def corners(row):
        start = row * 8 // 16 * 16
        low = levels_edges_ref[before, start : start + 16, :].astype(f32)
        high = levels_edges_ref[after, start : start + 16, :].astype(f32)
        at = row * 8 - start
        lines = [low[at + 3 : at + 4], low[at + 7 : at + 8], high[at : at + 1], high[at + 4 : at + 5]]
        return to_tiles(jnp.concatenate(lines + [jnp.zeros((4, columns), f32)], axis=0))

    first, last = corners(0), corners(rows - 1)
    even = row_group % 2 == 0
    near_ref[0:cells, :] = total.astype(bf16)
    far_ref[0:cells, :] = total.astype(bf16)
    near_ref[cells:, :] = jnp.where(even, last, first).astype(bf16)
    far_ref[cells:, :] = jnp.where(even, first, last).astype(bf16)


def steps_kernel(
    groups_x, groups_y, summed, x_ref, wet_ref, diff_ref, rates_ref, y_ref, beside_ref,
    edges_ref, *refs,
):
    if summed:
        pin_ref, qin_ref = refs[:2]
    base_ref, zb_ref, c_ref, z_ref, t0_ref, t1_ref, w_ref = refs[-7:]
    _, rows, channels, columns = x_ref.shape
    waves = columns // 2
    row_group = lax.axis_index("gx")
    col_group = lax.axis_index("gy")
    is_atmos = lax.axis_index("comp") == 0

    @pl.when(is_atmos)
    def _():
        diff = channel_column(diff_ref[...], channels, col_group * channels)
        total = rows * groups_x
        base = (row_group * rows).astype(f32)
        for n in range(0, waves, LANES):
            lam, alpha, sinh = decay_terms(diff, rates_ref[:, n : n + LANES])
            lam2 = lam * lam
            low = jnp.exp(-2.0 * base * alpha)
            high = jnp.exp(-2.0 * (total - rows - base) * alpha)
            scale = 1.0 / (
                2.0 * diff * sinh * (1.0 - jnp.exp(-2.0 * (total + 1) * alpha))
            )
            lows, highs = [], []
            power = low
            for r in range(rows):
                power = power * lam2
                lows.append(1.0 - power)
            power = high
            for r in range(rows):
                power = power * lam2
                highs.append(1.0 - power)
            highs = highs[::-1]
            if not summed:
                decays = []
                for band in range(groups_x):
                    gap = (jnp.abs(row_group - band) - 1) * rows
                    decays.append(jnp.exp(-jnp.maximum(gap, 0).astype(f32) * alpha))
            for part in (n, n + waves):
                lanes = slice(part, part + LANES)
                if summed:
                    pin = pin_ref[:, lanes]
                    qin = qin_ref[:, lanes]
                else:
                    pin = jnp.zeros((channels, LANES), f32)
                    qin = jnp.zeros((channels, LANES), f32)
                    for band in range(groups_x):
                        p = beside_ref[band, 0:channels, lanes].astype(f32)
                        q = beside_ref[band, channels : 2 * channels, lanes].astype(f32)
                        pin = pin + jnp.where(band < row_group, decays[band] * p, 0.0)
                        qin = qin + jnp.where(band > row_group, decays[band] * q, 0.0)
                f = pin
                for r in range(rows):
                    f = lam * f + lows[r] * y_ref[r, :, lanes]
                    z_ref[r] = highs[r] * f
                g = lam * qin
                for r in reversed(range(rows)):
                    z = scale * (z_ref[r] + lows[r] * g)
                    zb_ref[r * channels : (r + 1) * channels, lanes] = z.astype(bf16)
                    g = lam * (g + highs[r] * y_ref[r, :, lanes])

    @pl.when(jnp.logical_not(is_atmos))
    def _():
        levels = channels // 2
        ring = levels + 8
        lines = 2 * channels
        first_x = row_group == 0
        last_x = row_group == groups_x - 1
        top = col_group == 0
        bottom = col_group == groups_y - 1
        if summed:
            under, over = 0, 1
        else:
            under = jnp.maximum(row_group - 1, 0)
            over = jnp.minimum(row_group + 1, groups_x - 1)

        below = beside_ref[under, 2 * lines : 2 * lines + 16, :].astype(f32)
        above = beside_ref[over, 2 * lines : 2 * lines + 16, :].astype(f32)
        w_ref[0:2, :] = jnp.where(first_x, 0.0, below[rows - 2 : rows])
        w_ref[2 : rows + 2, :] = wet_ref[...].astype(f32)
        w_ref[rows + 2 : rows + 4, :] = jnp.where(last_x, 0.0, above[0:2])

        span = rows + 2
        north = w_ref[0:span, :]
        here = w_ref[1 : span + 1, :]
        south = w_ref[2 : span + 2, :]
        west = pltpu.roll(here, 1, 1)
        east = pltpu.roll(here, columns - 1, 1)
        c_ref[0, 0:span, :] = here * (
            1.0 - 2.0 * mixing_rate - spread_rate * (north + south + west + east)
        )
        c_ref[1, 0:span, :] = spread_rate * here * north
        c_ref[2, 0:span, :] = spread_rate * here * south
        c_ref[3, 0:span, :] = spread_rate * here * west
        c_ref[4, 0:span, :] = spread_rate * here * east
        c_ref[5, 0:span, :] = mixing_rate * here
        c_ref[6, 0:span, :] = here

        below = beside_ref[under, lines : 2 * lines, :].astype(f32)
        above = beside_ref[over, 0:lines, :].astype(f32)
        blank = jnp.zeros((8, columns), f32)
        for k in range(2):
            for t in range(2):
                c = k * channels + t * levels
                t0_ref[k, t, 0:levels, :] = below[c : c + levels]
                t0_ref[rows + 2 + k, t, 0:levels, :] = above[c : c + levels]
                t0_ref[k, t, levels:ring, :] = blank
                t0_ref[rows + 2 + k, t, levels:ring, :] = blank
        before = edges_ref[jnp.maximum(col_group - 1, 0)].astype(f32)
        after = edges_ref[jnp.minimum(col_group + 1, groups_y - 1)].astype(f32)
        for r in range(rows):
            for t in range(2):
                k = (r * 2 + t) * 4
                t0_ref[r + 2, t, 0:levels, :] = x_ref[0, r, t * levels : (t + 1) * levels, :]
                t0_ref[r + 2, t, levels : levels + 2, :] = after[k : k + 2]
                t0_ref[r + 2, t, ring - 2 : ring, :] = before[k + 2 : k + 4]

        def close(ref, r):
            for t in range(2):
                ref[r, t, ring - 1 : ring, :] = jnp.where(
                    top, ref[r, t, 0:1, :], ref[r, t, ring - 1 : ring, :]
                )
                ref[r, t, levels : levels + 1, :] = jnp.where(
                    bottom, ref[r, t, levels - 1 : levels, :], ref[r, t, levels : levels + 1, :]
                )

        def advance(ref, r, t, coefs, size):
            whole = ref[r, t]
            up = pltpu.roll(whole, 1, 0)[:size]
            down = pltpu.roll(whole, ring - 1, 0)[:size]
            mid = whole[:size]
            total = coefs[0] * mid + coefs[5] * (up + down)
            total = total + coefs[1] * ref[r - 1, t, 0:size, :]
            total = total + coefs[2] * ref[r + 1, t, 0:size, :]
            total = total + coefs[3] * pltpu.roll(mid, 1, 1)
            return total + coefs[4] * pltpu.roll(mid, columns - 1, 1)

        def first(r, carry):
            coefs = [c_ref[k, pl.ds(r, 1), :] for k in range(6)]
            close(t0_ref, r + 1)
            for t in range(2):
                t1_ref[r, t] = advance(t0_ref, r + 1, t, coefs, ring)
            close(t1_ref, r)
            return carry

        lax.fori_loop(0, span, first, 0)

        def second(r, carry):
            coefs = [c_ref[k, pl.ds(r, 1), :] for k in range(6)]
            for t in range(2):
                c = t * levels
                base_ref[r - 1, c : c + levels, :] = advance(t1_ref, r, t, coefs, levels)
            return carry

        lax.fori_loop(1, span - 1, second, 0)


def last_kernel(
    groups_x, groups_y, gain_ref, table_ref, base_ref, zb_ref, c_ref, sum_ref, near_ref,
    far_ref, out_ref, e_ref,
):
    _, rows, channels, columns = out_ref.shape
    row_group = lax.axis_index("gx")
    col_group = lax.axis_index("gy")
    is_atmos = lax.axis_index("comp") == 0

    @pl.when(is_atmos)
    def _():
        response = channel_column(gain_ref[...], channels, col_group * channels)
        forcing = from_tiles(sum_ref[...], rows)
        step = 256
        for n in range(0, columns, step):
            part = jnp.dot(
                zb_ref[...], table_ref[:, n : n + step], preferred_element_type=f32
            ).reshape(rows, channels, step)
            for r in range(rows):
                out_ref[0, r, :, n : n + step] = (
                    part[r] + response * forcing[r : r + 1, n : n + step]
                )

    @pl.when(jnp.logical_not(is_atmos))
    def _():
        out_ref[0] = base_ref[...]
        levels = channels // 2
        cells = sum_ref.shape[0]
        even = row_group % 2 == 0
        below = jnp.where(even, far_ref[...].astype(f32), near_ref[...].astype(f32))
        above = jnp.where(even, near_ref[...].astype(f32), far_ref[...].astype(f32))

        low = from_tiles(below[cells:], 8)
        high = from_tiles(above[cells:], 8)
        by_low = c_ref[1, 1:2, :] * (c_ref[5, 0:1, :] + c_ref[5, 1:2, :])
        by_high = c_ref[2, rows : rows + 1, :] * (
            c_ref[5, rows : rows + 1, :] + c_ref[5, rows + 1 : rows + 2, :]
        )
        has_before = jnp.where(col_group > 0, 1.0, 0.0)
        has_after = jnp.where(col_group < groups_y - 1, 1.0, 0.0)
        for t in range(2):
            for r, factor, lines in ((0, by_low, low), (rows - 1, by_high, high)):
                c = t * levels
                out_ref[0, r, c : c + 1, :] = out_ref[0, r, c : c + 1, :] + (
                    has_before * factor * lines[t : t + 1]
                )
                c = c + levels - 1
                out_ref[0, r, c : c + 1, :] = out_ref[0, r, c : c + 1, :] + (
                    has_after * factor * lines[t + 2 : t + 3]
                )

        @pl.when(col_group == 0)
        def _():
            span = rows + 2
            e_ref[0:1, :] = from_tiles(below[:cells], rows)[rows - 1 : rows]
            e_ref[1 : rows + 1, :] = from_tiles(sum_ref[...], rows)
            e_ref[rows + 1 : span, :] = from_tiles(above[:cells], rows)[0:1]
            e_ref[0:span, :] = c_ref[6, 0:span, :] * e_ref[0:span, :]
            own = slice(1, rows + 1)
            heat = e_ref[own, :]
            second = c_ref[5, own, :] * heat
            first = (c_ref[0, own, :] + 1.0) * heat + second
            first = first + c_ref[1, own, :] * e_ref[0:rows, :]
            first = first + c_ref[2, own, :] * e_ref[2 : rows + 2, :]
            first = first + c_ref[3, own, :] * pltpu.roll(heat, 1, 1)
            first = first + c_ref[4, own, :] * pltpu.roll(heat, columns - 1, 1)
            for t, gain in enumerate((heat_gain, salt_gain)):
                c = t * levels
                for r in range(rows):
                    lines = jnp.concatenate([first[r : r + 1], second[r : r + 1]], axis=0)
                    out_ref[0, r, c : c + 2, :] = out_ref[0, r, c : c + 2, :] + gain * lines


def local(
    fields,
    wet_cells,
    flux_weight,
    variable_sea_response,
    diffusivity,
    a2o_source,
    a2o_target,
    a2o_count,
    a2o_weight,
    marine_air_input_index,
    marine_air_output_index,
    marine_air_piece_tally,
    marine_air_piece_factor,
):
    _, rows, channels, columns = fields.shape
    groups_x = lax.axis_size("gx")
    groups_y = lax.axis_size("gy")
    blocks, points = a2o_source.shape[2:]
    cells = rows * columns // LANES
    forward, inverse, half_rates = fourier_tables(columns)
    flux_row = flux_weight[None, :]
    gain_row = variable_sea_response[None, :]
    diff_row = diffusivity[None, :]
    params = functools.partial(pltpu.CompilerParams, vmem_limit_bytes=40 * 2**20)
    vmem = pl.BlockSpec(memory_space=pltpu.VMEM)
    smem = pl.BlockSpec(memory_space=pltpu.SMEM)
    anywhere = pl.BlockSpec(memory_space=pl.ANY)

    def shape(dims, dtype):
        return jax.ShapeDtypeStruct(dims, dtype)

    partial_surface = pl.pallas_call(
        surface_kernel,
        out_shape=shape((cells, LANES), bf16),
        in_specs=[vmem, vmem],
        out_specs=vmem,
        scratch_shapes=[pltpu.VMEM((rows, columns), f32)],
        compiler_params=params(),
        name="surface_partials",
    )(fields, flux_row)
    surfaces = []
    for mask in range(groups_y):
        route = []
        for j in range(groups_y):
            route += both_ways([(j, groups_y + (j ^ mask))])
        surfaces.append(lax.ppermute(partial_surface, ("comp", "gy"), route))

    lines = 4 * channels + 16
    y, beside, edges = pl.pallas_call(
        functools.partial(forward_kernel, groups_x),
        out_shape=[
            shape((rows, channels, columns), f32),
            shape((lines, columns), bf16),
            shape((8 * rows, columns), bf16),
        ],
        in_specs=[vmem] * 5 + [anywhere],
        out_specs=[vmem] * 3,
        scratch_shapes=[pltpu.VMEM((8 * rows, columns), f32)],
        compiler_params=params(),
        name="forward_and_halos",
    )(fields, wet_cells, diff_row, half_rates, forward, partial_surface)
    beside = lax.all_gather(beside, "gx")
    edges = lax.all_gather(edges, "gy")

    landing, sent = pl.pallas_call(
        functools.partial(regrid_kernel, groups_y),
        out_shape=[shape((cells, LANES), f32), shape((cells, LANES), bf16)],
        in_specs=[vmem] * groups_y
        + [vmem, vmem, smem, anywhere, vmem, vmem, smem, anywhere],
        out_specs=[vmem] * 2,
        scratch_shapes=[
            pltpu.VMEM((blocks, points, points), bf16),
            pltpu.VMEM((blocks, points), f32),
            pltpu.VMEM((blocks, points), f32),
            pltpu.SemaphoreType.DMA,
        ],
        compiler_params=params(),
        name="regrid_blocks",
    )(
        *surfaces,
        a2o_source, a2o_target, a2o_count, a2o_weight,
        marine_air_input_index, marine_air_output_index,
        marine_air_piece_tally, marine_air_piece_factor,
    )
    parts = [
        lax.ppermute(sent, "gy", [(j, j ^ mask) for j in range(groups_y)])
        for mask in range(1, groups_y)
    ]

    extra = []
    if groups_x > 8:
        mine = lax.axis_index("gx")
        viscous = lax.dynamic_slice_in_dim(
            diffusivity, lax.axis_index("gy") * channels, channels
        )[:, None]
        _, alpha, _ = decay_terms(viscous, half_rates)
        alpha = jnp.concatenate([alpha, alpha], axis=1)
        gap = mine - jnp.arange(groups_x)
        decay = jnp.exp(
            -(rows * jnp.maximum(jnp.abs(gap) - 1, 0))[:, None, None] * alpha[None]
        )
        p = beside[:, :channels].astype(f32)
        q = beside[:, channels : 2 * channels].astype(f32)
        extra = [
            jnp.sum(jnp.where((gap > 0)[:, None, None], decay * p, 0.0), axis=0),
            jnp.sum(jnp.where((gap < 0)[:, None, None], decay * q, 0.0), axis=0),
        ]
        near = jnp.stack([jnp.maximum(mine - 1, 0), jnp.minimum(mine + 1, groups_x - 1)])
        beside = jnp.take(beside, near, axis=0)
    ring = channels // 2 + 8
    base, damped, coefs = pl.pallas_call(
        functools.partial(steps_kernel, groups_x, groups_y, groups_x > 8),
        out_shape=[
            shape((rows, channels, columns), f32),
            shape((rows * channels, columns), bf16),
            shape((7, 16, columns), f32),
        ],
        in_specs=[vmem] * (7 + len(extra)),
        out_specs=[vmem] * 3,
        scratch_shapes=[
            pltpu.VMEM((rows, channels, LANES), f32),
            pltpu.VMEM((rows + 4, 2, ring, columns), f32),
            pltpu.VMEM((rows + 2, 2, ring, columns), f32),
            pltpu.VMEM((16, columns), f32),
        ],
        compiler_params=params(),
        name="damping_or_ocean_steps",
    )(fields, wet_cells, diff_row, half_rates, y, beside, edges, *extra)

    surface_sum, near, far = pl.pallas_call(
        functools.partial(heat_kernel, rows),
        out_shape=[
            shape((cells, LANES), f32),
            shape((cells + columns // 16, LANES), bf16),
            shape((cells + columns // 16, LANES), bf16),
        ],
        in_specs=[vmem] * (2 + len(parts)),
        out_specs=[vmem] * 3,
        compiler_params=params(),
        name="surface_sum",
    )(edges, landing, *parts)

    def ring_pairs(odd):
        pairs = [(a, (a + 1) % groups_x) for a in range(odd, groups_x, 2)]
        return both_ways(pairs)

    near = lax.ppermute(near, "gx", ring_pairs(0))
    far = lax.ppermute(far, "gx", ring_pairs(1))
    return pl.pallas_call(
        functools.partial(last_kernel, groups_x, groups_y),
        out_shape=shape(fields.shape, f32),
        in_specs=[vmem] * 8,
        out_specs=vmem,
        scratch_shapes=[pltpu.VMEM((16, columns), f32)],
        compiler_params=params(),
        name="inverse_or_heat",
    )(gain_row, inverse, base, damped, coefs, surface_sum, near, far)


def solution(mesh):
    in_specs = (
        P("comp", "gx", "gy", None),
        P("gx", None),
        P(),
        P(),
        P(),
        P("gx", "gy", None, None),
        P("gx", "gy", None, None),
        P("gx", "gy"),
        P("gx", "gy", None, None, None),
        P("gx", "gy", None, None),
        P("gx", "gy", None, None),
        P("gx", "gy"),
        P("gx", "gy", None, None, None),
    )
    out_specs = P("comp", "gx", "gy", None)
    return jax.shard_map(local, mesh=mesh, in_specs=in_specs, out_specs=out_specs, check_vma=False)
```

time: 41.9 us -> 65.4 us (1.56)
  the two profiles are of different devices: /device:TPU:13 before, /device:TPU:0 now
where the time goes in v3:
time: 65.4 us; the launch traced here: 64.2 us
  between operations  14.9 us (23%)
  blocking collectives  14.8 us (23%)
  starting transfers between devices  13.2 us (20%)
  local copies, waits for them, and re-layouts  9.46 us (14%)
  Pallas kernels  6.72 us (10%)
  waiting for transfers between devices  5.14 us (8%)
    all_gather x1, blocking collectives, local(): edges = lax.all_gather(edges, 'gy')  14.8 us
    unnamed x38, local copies, waits for them, and re-layouts  9.46 us
    ppermute x4, starting transfers between devices, local(): surfaces.append(lax.ppermute(partial_surface, ('comp', 'gy'), route))  7.11 us
    ppermute x4, waiting for transfers between devices, local(): surfaces.append(lax.ppermute(partial_surface, ('comp', 'gy'), route))  5.11 us
    ppermute x3, starting transfers between devices, local(): lax.ppermute(sent, 'gy', [(j, j ^ mask) for j in range(groups_y)])  4.44 us
    pallas_call x1, Pallas kernels, local(): pl.pallas_call(functools.partial(regrid_kernel, groups_y), out_shape=[sha...  2.26 us
    pallas_call x1, Pallas kernels, local(): pl.pallas_call(functools.partial(last_kernel, groups_x, groups_y), out_sh...  1.7 us
    pallas_call x1, Pallas kernels, local(): pl.pallas_call(functools.partial(forward_kernel, groups_x), out_shape=[sh...  1.66 us
  transfers between devices with their start and end apart: 10, of which 2 were waited for; matrix products, arithmetic and copies ran while one was open for 0% of the time, Pallas kernels for 5%

profile of v3, /device:TPU:0, one launch (start us, length us, event | category | flops | bytes accessed | tf_op | source)
XLA Modules:
  0.0 64.2 jit_solution(2823152490557286359)
XLA Ops:
  6.5 0.0 all-gather.4.cloned.1.call-start
  6.5 0.0 copy-start
  6.5 1.2 %copy-done = f32[1,8,32,1024]{3,2,1,0:T(8,128)S(1)} copy-done((f32[1,8,32,1024]{3,2,1,0:T(8,128)S(1)}, f32[1,8,32,1024]{3,2,1,0:T(8,128)}, u32[]{:S(2)}) %copy-start) | copy-done | bytes 1048600
  7.8 0.0 copy-start.17
  7.8 0.7 %copy-done.17 = f32[128]{0:T(128)S(1)} copy-done((f32[128]{0:T(128)S(1)}, f32[128]{0:T(128)}, u32[]{:S(2)}) %copy-start.17) | copy-done | bytes 536
  8.4 0.0 copy-start.9
  8.4 0.0 copy-start.11
  8.4 0.0 copy-start.12
  8.4 0.2 surface_partials.1.after_ref
  8.7 0.0 copy-start.2
  8.7 1.6 %copy-done.2 = bf16[1024,1024]{1,0:T(8,128)(2,1)S(1)} copy-done((bf16[1024,1024]{1,0:T(8,128)(2,1)S(1)}, bf16[1024,1024]{1,0:T(8,128)(2,1)}, u32[]{:S(2)}) %copy-start.2) | copy-done | bytes 2097176
  10.3 0.0 copy-start.7
  10.3 0.8 %copy-done.7 = s32[8,1024]{1,0:T(8,128)S(1)} copy-done((s32[8,1024]{1,0:T(8,128)S(1)}, s32[8,1024]{1,0:T(8,128)}, u32[]{:S(2)}) %copy-start.7) | copy-done | bytes 32792
  11.0 0.0 copy-start.13
  11.0 0.7 %copy-done.13 = f32[1,512]{1,0:T(1,128)S(1)} copy-done((f32[1,512]{1,0:T(1,128)S(1)}, f32[1,512]{1,0:T(1,128)}, u32[]{:S(2)}) %copy-start.13) | copy-done | bytes 2072
  11.7 0.0 copy-start.15
  11.7 0.7 %copy-done.15 = f32[128]{0:T(128)S(1)} copy-done((f32[128]{0:T(128)S(1)}, f32[128]{0:T(128)}, u32[]{:S(2)}) %copy-start.15) | copy-done | bytes 536
  12.4 0.0 copy-start.8
  12.4 0.0 copy-start.14
  12.4 0.0 copy-start.16
  12.4 1.7 %forward_and_halos.1 = (f32[8,32,1024]{2,1,0:T(8,128)S(1)}, bf16[144,1024]{1,0:T(8,128)(2,1)}, bf16[64,1024]{1,0:T(8,128)(2,1)S(1)}) custom-call(f32[1,8,32,1024]{3,2,1,0:T(8,128)S(1)} %copy-done, s32[8,1024]{1,0:T(8,128)S(1)} %copy-done.7, f32[1,128]{1,0:T(1,128)S(1)} %bitcast.8, f32[1,512]{1,0:T(1,128)S(1)} %copy-done.13, ...), custom_call_target="tpu_custom_call" | custom-call | tf_op jit(solution)/shard_map/forward_and_halos/pallas_call | solution.py:539
  14.0 0.0 copy-start.1
  14.0 0.0 all-gather.4.cloned.1.call-update
  14.0 2.0 %collective-permute-start = (bf16[64,128]{1,0:T(8,128)(2,1)S(1)}, bf16[64,128]{1,0:T(8,128)(2,1)S(1)}, u32[]{:S(2)}, u32[]{:S(2)}) collective-permute-start(bf16[64,128]{1,0:T(8,128)(2,1)S(1)} %surface_partials.1.after_ref), channel_id=1, source_target_pairs={{0,16},{16,0},{1,17},{17,1},{2,18},{18,2},{3,19},{19,3},{4,20},{20... | collective-permute-start | bytes 49160 | tf_op jit(solution)/shard_map/ppermute | solution.py:536
  16.1 2.5 %collective-permute-start.1 = (bf16[64,128]{1,0:T(8,128)(2,1)S(1)}, bf16[64,128]{1,0:T(8,128)(2,1)S(1)}, u32[]{:S(2)}, u32[]{:S(2)}) collective-permute-start(bf16[64,128]{1,0:T(8,128)(2,1)S(1)} %surface_partials.1.after_ref), channel_id=1, source_target_pairs={{0,17},{17,0},{1,16},{16,1},{2,19},{19,2},{3,18},{18,3},{4,21},{21... | collective-permute-start | bytes 49160 | tf_op jit(solution)/shard_map/ppermute | solution.py:536
  18.6 2.6 %collective-permute-start.2 = (bf16[64,128]{1,0:T(8,128)(2,1)S(1)}, bf16[64,128]{1,0:T(8,128)(2,1)S(1)}, u32[]{:S(2)}, u32[]{:S(2)}) collective-permute-start(bf16[64,128]{1,0:T(8,128)(2,1)S(1)} %surface_partials.1.after_ref), channel_id=1, source_target_pairs={{0,18},{18,0},{1,19},{19,1},{2,16},{16,2},{3,17},{17,3},{4,22},{22... | collective-permute-start | bytes 49160 | tf_op jit(solution)/shard_map/ppermute | solution.py:536
  21.2 0.0 collective-permute-start.3
  22.5 0.0 collective-permute-done.refs_0_
  22.5 0.0 collective-permute-done.1.refs_1_
  22.5 1.6 %collective-permute-done.2.refs_2_ = bf16[64,128]{1,0:T(8,128)(2,1)S(1)} collective-permute-done((bf16[64,128]{1,0:T(8,128)(2,1)S(1)}, bf16[64,128]{1,0:T(8,128)(2,1)S(1)}, u32[]{:S(2)}, u32[]{:S(2)}) %collective-permute-start.2) | collective-permute-done | bytes 16416 | tf_op jit(solution)/shard_map/ppermute | solution.py:536
  24.1 3.5 %collective-permute-done.3.refs_3_ = bf16[64,128]{1,0:T(8,128)(2,1)S(1)} collective-permute-done((bf16[64,128]{1,0:T(8,128)(2,1)S(1)}, bf16[64,128]{1,0:T(8,128)(2,1)S(1)}, u32[]{:S(2)}, u32[]{:S(2)}) %collective-permute-start.3) | collective-permute-done | bytes 16416 | tf_op jit(solution)/shard_map/ppermute | solution.py:536
  27.6 0.0 copy-done.9
  27.6 0.0 copy-done.10
  27.6 0.0 copy-done.11
  27.6 0.0 copy-done.12
  27.6 0.0 copy-start.5
  27.6 1.2 %copy-done.5 = bf16[1,1,32,128,128]{4,3,2,1,0:T(8,128)(2,1)S(1)} copy-done((bf16[1,1,32,128,128]{4,3,2,1,0:T(8,128)(2,1)S(1)}, bf16[1,1,32,128,128]{4,3,2,1,0:T(8,128)(2,1)}, u32[]{:S(2)}) %copy-start.5) | copy-done | bytes 1048600
  28.9 0.0 copy-start.6
  28.9 1.2 %copy-done.6 = bf16[1,1,32,128,128]{4,3,2,1,0:T(8,128)(2,1)S(1)} copy-done((bf16[1,1,32,128,128]{4,3,2,1,0:T(8,128)(2,1)S(1)}, bf16[1,1,32,128,128]{4,3,2,1,0:T(8,128)(2,1)}, u32[]{:S(2)}) %copy-start.6) | copy-done | bytes 1048600
  30.1 2.3 %regrid_blocks.1 = (f32[64,128]{1,0:T(8,128)S(1)}, bf16[64,128]{1,0:T(8,128)(2,1)S(1)}) custom-call(bf16[64,128]{1,0:T(8,128)(2,1)S(1)} %collective-permute-done.refs_0_, bf16[64,128]{1,0:T(8,128)(2,1)S(1)} %collective-permute-done.1.refs_1_, bf16[64,128]{1,0:T(8,128)(2,1)S(1)} %collective-permute-done.2.refs_2_, ...), custom_call_target="tpu_custom_call" | custom-call | tf_op jit(solution)/shard_map/regrid_blocks/pallas_call | solution.py:555
  32.3 0.1 collective-permute-start.4
  32.4 0.8 %collective-permute-start.5 = (bf16[64,128]{1,0:T(8,128)(2,1)S(1)}, bf16[64,128]{1,0:T(8,128)(2,1)S(1)}, u32[]{:S(2)}, u32[]{:S(2)}) collective-permute-start(bf16[64,128]{1,0:T(8,128)(2,1)S(1)} %get-tuple-element.23), channel_id=1, source_target_pairs={{0,2},{1,3},{2,0},{3,1},{4,6},{5,7},{6,4},{7,5},{8,10},{9,11},{10,... | collective-permute-start | bytes 49160 | tf_op jit(solution)/shard_map/ppermute | solution.py:576
  33.2 3.6 %collective-permute-start.6 = (bf16[64,128]{1,0:T(8,128)(2,1)S(1)}, bf16[64,128]{1,0:T(8,128)(2,1)S(1)}, u32[]{:S(2)}, u32[]{:S(2)}) collective-permute-start(bf16[64,128]{1,0:T(8,128)(2,1)S(1)} %get-tuple-element.23), channel_id=1, source_target_pairs={{0,3},{1,2},{2,1},{3,0},{4,7},{5,6},{6,5},{7,4},{8,11},{9,10},{10,... | collective-permute-start | bytes 49160 | tf_op jit(solution)/shard_map/ppermute | solution.py:576
  36.8 14.8 %all-gather.1 = bf16[256,1024]{1,0:T(8,128)(2,1)S(1)} all-gather(bf16[64,1024]{1,0:T(8,128)(2,1)S(1)} %get-tuple-element.18), channel_id=3, replica_groups=mesh['comp'=2,'gx'=4,'gy'=4] {'gy'}, dimensions={0}, use_global_device_ids=true | all-gather | bytes 655360 | tf_op jit(solution)/shard_map/all_gather | solution.py:553
  51.6 0.0 collective-permute-done.4.refs_0_
  51.6 0.0 collective-permute-done.5.refs_1_
  51.6 0.0 collective-permute-done.6.refs_2_
  51.6 0.0 copy-start.18
  51.6 0.1 collective-permute-start.7
  51.7 1.6 %collective-permute-start.8 = (bf16[128,128]{1,0:T(8,128)(2,1)S(1)}, bf16[128,128]{1,0:T(8,128)(2,1)S(1)}, u32[]{:S(2)}, u32[]{:S(2)}) collective-permute-start(bf16[128,128]{1,0:T(8,128)(2,1)S(1)} %get-tuple-element.26), channel_id=1, source_target_pairs={{4,8},{8,4},{12,0},{0,12},{5,9},{9,5},{13,1},{1,13},{6,10},{10,6},... | collective-permute-start | bytes 98312 | tf_op jit(solution)/shard_map/ppermute | solution.py:638
  53.3 0.0 all-gather.4.cloned.1.call-done
  53.3 0.0 copy-start.3
  53.3 0.0 copy-done.8
  53.3 0.0 copy-done.14
  53.3 0.0 copy-done.16
  53.3 0.0 copy-done.1
  53.3 0.0 copy-start.4
  53.4 1.4 %copy-done.4 = bf16[576,1024]{1,0:T(8,128)(2,1)S(1)} copy-done((bf16[576,1024]{1,0:T(8,128)(2,1)S(1)}, bf16[576,1024]{1,0:T(8,128)(2,1)}, u32[]{:S(2)}) %copy-start.4) | copy-done | bytes 1179672
  54.8 0.8 %damping_or_ocean_steps.1 = (f32[8,32,1024]{2,1,0:T(8,128)S(1)}, bf16[256,1024]{1,0:T(8,128)(2,1)S(1)}, f32[7,16,1024]{2,1,0:T(8,128)S(1)}) custom-call(f32[1,8,32,1024]{3,2,1,0:T(8,128)S(1)} %copy-done.1, s32[8,1024]{1,0:T(8,128)S(1)} %copy-done.8, f32[1,128]{1,0:T(1,128)S(1)} %bitcast.9, f32[1,512]{1,0:T(1,128)S(1)} %copy-done.14, ...), custom_call_target="tpu_custom_call" | custom-call | tf_op jit(solution)/shard_map/damping_or_ocean_steps/pallas_call | solution.py:601
  55.6 0.0 collective-permute-done.7.near_ref
  55.6 0.0 collective-permute-done.8.far_ref
  55.6 0.0 copy-done.18
  55.6 0.0 copy-done.3
  55.6 1.7 %inverse_or_heat.1 = f32[1,8,32,1024]{3,2,1,0:T(8,128)} custom-call(f32[1,128]{1,0:T(1,128)S(1)} %bitcast.11, bf16[1024,1024]{1,0:T(8,128)(2,1)S(1)} %copy-done.3, f32[8,32,1024]{2,1,0:T(8,128)S(1)} %get-tuple-element.19.base_ref, bf16[256,1024]{1,0:T(8,128)(2,1)S(1)} %get-tuple-element.20.zb_ref, f32[7,16,1024]{2,1,0:T(8,128)S(1)} %get-tuple-element.21.c_ref, ...), custom_call_target="tpu_custom_call" | custom-call | tf_op jit(solution)/shard_map/inverse_or_heat/pallas_call | solution.py:639
  (2 shorter events, 0.0 us)
Async XLA Ops:
  6.5 46.8 %all-gather.4.cloned.1.call-start = ((), (), s32[]{:S(2)}) async-start(), calls=%async_computation | async-start | bytes 1474560 | tf_op jit(solution)/shard_map/all_gather | solution.py:552
  6.5 1.2 %copy-start = (f32[1,8,32,1024]{3,2,1,0:T(8,128)S(1)}, f32[1,8,32,1024]{3,2,1,0:T(8,128)}, u32[]{:S(2)}) copy-start(f32[1,8,32,1024]{3,2,1,0:T(8,128)} %x_ref.5) | copy-start | bytes 3145732
  7.8 0.7 %copy-start.17 = (f32[128]{0:T(128)S(1)}, f32[128]{0:T(128)}, u32[]{:S(2)}) copy-start(f32[128]{0:T(128)} %param.18) | copy-start | bytes 1540
  8.4 19.2 %copy-start.9 = (s32[1,1,32,128]{3,2,1,0:T(8,128)S(1)}, s32[1,1,32,128]{3,2,1,0:T(8,128)}, u32[]{:S(2)}) copy-start(s32[1,1,32,128]{3,2,1,0:T(8,128)} %refs_4_.1) | copy-start | bytes 49156
  8.4 19.2 %copy-start.10 = (s32[1,1,32,128]{3,2,1,0:T(8,128)S(1)}, s32[1,1,32,128]{3,2,1,0:T(8,128)}, u32[]{:S(2)}) copy-start(s32[1,1,32,128]{3,2,1,0:T(8,128)} %refs_5_.1) | copy-start | bytes 49156
  8.4 19.2 %copy-start.11 = (s32[1,1,32,128]{3,2,1,0:T(8,128)S(1)}, s32[1,1,32,128]{3,2,1,0:T(8,128)}, u32[]{:S(2)}) copy-start(s32[1,1,32,128]{3,2,1,0:T(8,128)} %refs_8_.1) | copy-start | bytes 49156
  8.4 19.2 %copy-start.12 = (s32[1,1,32,128]{3,2,1,0:T(8,128)S(1)}, s32[1,1,32,128]{3,2,1,0:T(8,128)}, u32[]{:S(2)}) copy-start(s32[1,1,32,128]{3,2,1,0:T(8,128)} %refs_9_.1) | copy-start | bytes 49156
  8.7 1.6 %copy-start.2 = (bf16[1024,1024]{1,0:T(8,128)(2,1)S(1)}, bf16[1024,1024]{1,0:T(8,128)(2,1)}, u32[]{:S(2)}) copy-start(bf16[1024,1024]{1,0:T(8,128)(2,1)} %constant.6.clone.table_ref) | copy-start | bytes 6291460
  10.3 0.8 %copy-start.7 = (s32[8,1024]{1,0:T(8,128)S(1)}, s32[8,1024]{1,0:T(8,128)}, u32[]{:S(2)}) copy-start(s32[8,1024]{1,0:T(8,128)} %wet_ref.3) | copy-start | bytes 98308
  11.0 0.7 %copy-start.13 = (f32[1,512]{1,0:T(1,128)S(1)}, f32[1,512]{1,0:T(1,128)}, u32[]{:S(2)}) copy-start(f32[1,512]{1,0:T(1,128)} %constant.8.clone.rates_ref) | copy-start | bytes 6148
  11.7 0.7 %copy-start.15 = (f32[128]{0:T(128)S(1)}, f32[128]{0:T(128)}, u32[]{:S(2)}) copy-start(f32[128]{0:T(128)} %param.20) | copy-start | bytes 1540
  12.4 41.0 %copy-start.8 = (s32[8,1024]{1,0:T(8,128)S(1)}, s32[8,1024]{1,0:T(8,128)}, u32[]{:S(2)}) copy-start(s32[8,1024]{1,0:T(8,128)} %wet_ref.3) | copy-start | bytes 98308
  12.4 41.0 %copy-start.14 = (f32[1,512]{1,0:T(1,128)S(1)}, f32[1,512]{1,0:T(1,128)}, u32[]{:S(2)}) copy-start(f32[1,512]{1,0:T(1,128)} %constant.8.clone.rates_ref) | copy-start | bytes 6148
  12.4 41.0 %copy-start.16 = (f32[128]{0:T(128)S(1)}, f32[128]{0:T(128)}, u32[]{:S(2)}) copy-start(f32[128]{0:T(128)} %param.20) | copy-start | bytes 1540
  14.0 39.3 %copy-start.1 = (f32[1,8,32,1024]{3,2,1,0:T(8,128)S(1)}, f32[1,8,32,1024]{3,2,1,0:T(8,128)}, u32[]{:S(2)}) copy-start(f32[1,8,32,1024]{3,2,1,0:T(8,128)} %x_ref.5) | copy-start | bytes 3145732
  14.0 8.4 %collective-permute-start = (bf16[64,128]{1,0:T(8,128)(2,1)S(1)}, bf16[64,128]{1,0:T(8,128)(2,1)S(1)}, u32[]{:S(2)}, u32[]{:S(2)}) collective-permute-start(bf16[64,128]{1,0:T(8,128)(2,1)S(1)} %surface_partials.1.after_ref), channel_id=1, source_target_pairs={{0,16},{16,0},{1,17},{17,1},{2,18},{18,2},{3,19},{19,3},{4,20},{20... | collective-permute-start | bytes 49160 | tf_op jit(solution)/shard_map/ppermute | solution.py:536
  16.1 6.4 %collective-permute-start.1 = (bf16[64,128]{1,0:T(8,128)(2,1)S(1)}, bf16[64,128]{1,0:T(8,128)(2,1)S(1)}, u32[]{:S(2)}, u32[]{:S(2)}) collective-permute-start(bf16[64,128]{1,0:T(8,128)(2,1)S(1)} %surface_partials.1.after_ref), channel_id=1, source_target_pairs={{0,17},{17,0},{1,16},{16,1},{2,19},{19,2},{3,18},{18,3},{4,21},{21... | collective-permute-start | bytes 49160 | tf_op jit(solution)/shard_map/ppermute | solution.py:536
  18.6 5.5 %collective-permute-start.2 = (bf16[64,128]{1,0:T(8,128)(2,1)S(1)}, bf16[64,128]{1,0:T(8,128)(2,1)S(1)}, u32[]{:S(2)}, u32[]{:S(2)}) collective-permute-start(bf16[64,128]{1,0:T(8,128)(2,1)S(1)} %surface_partials.1.after_ref), channel_id=1, source_target_pairs={{0,18},{18,0},{1,19},{19,1},{2,16},{16,2},{3,17},{17,3},{4,22},{22... | collective-permute-start | bytes 49160 | tf_op jit(solution)/shard_map/ppermute | solution.py:536
  21.2 6.4 %collective-permute-start.3 = (bf16[64,128]{1,0:T(8,128)(2,1)S(1)}, bf16[64,128]{1,0:T(8,128)(2,1)S(1)}, u32[]{:S(2)}, u32[]{:S(2)}) collective-permute-start(bf16[64,128]{1,0:T(8,128)(2,1)S(1)} %surface_partials.1.after_ref), channel_id=1, source_target_pairs={{0,19},{19,0},{1,18},{18,1},{2,17},{17,2},{3,16},{16,3},{4,23},{23... | collective-permute-start | bytes 49160 | tf_op jit(solution)/shard_map/ppermute | solution.py:536
  27.6 1.2 %copy-start.5 = (bf16[1,1,32,128,128]{4,3,2,1,0:T(8,128)(2,1)S(1)}, bf16[1,1,32,128,128]{4,3,2,1,0:T(8,128)(2,1)}, u32[]{:S(2)}) copy-start(bf16[1,1,32,128,128]{4,3,2,1,0:T(8,128)(2,1)} %refs_7_.1) | copy-start | bytes 3145732
  28.9 1.2 %copy-start.6 = (bf16[1,1,32,128,128]{4,3,2,1,0:T(8,128)(2,1)S(1)}, bf16[1,1,32,128,128]{4,3,2,1,0:T(8,128)(2,1)}, u32[]{:S(2)}) copy-start(bf16[1,1,32,128,128]{4,3,2,1,0:T(8,128)(2,1)} %refs_11_.1) | copy-start | bytes 3145732
  32.3 19.2 %collective-permute-start.4 = (bf16[64,128]{1,0:T(8,128)(2,1)S(1)}, bf16[64,128]{1,0:T(8,128)(2,1)S(1)}, u32[]{:S(2)}, u32[]{:S(2)}) collective-permute-start(bf16[64,128]{1,0:T(8,128)(2,1)S(1)} %get-tuple-element.23), channel_id=1, source_target_pairs={{0,1},{1,0},{2,3},{3,2},{4,5},{5,4},{6,7},{7,6},{8,9},{9,8},{10,11... | collective-permute-start | bytes 49160 | tf_op jit(solution)/shard_map/ppermute | solution.py:576
  32.4 19.1 %collective-permute-start.5 = (bf16[64,128]{1,0:T(8,128)(2,1)S(1)}, bf16[64,128]{1,0:T(8,128)(2,1)S(1)}, u32[]{:S(2)}, u32[]{:S(2)}) collective-permute-start(bf16[64,128]{1,0:T(8,128)(2,1)S(1)} %get-tuple-element.23), channel_id=1, source_target_pairs={{0,2},{1,3},{2,0},{3,1},{4,6},{5,7},{6,4},{7,5},{8,10},{9,11},{10,... | collective-permute-start | bytes 49160 | tf_op jit(solution)/shard_map/ppermute | solution.py:576
  33.2 18.4 %collective-permute-start.6 = (bf16[64,128]{1,0:T(8,128)(2,1)S(1)}, bf16[64,128]{1,0:T(8,128)(2,1)S(1)}, u32[]{:S(2)}, u32[]{:S(2)}) collective-permute-start(bf16[64,128]{1,0:T(8,128)(2,1)S(1)} %get-tuple-element.23), channel_id=1, source_target_pairs={{0,3},{1,2},{2,1},{3,0},{4,7},{5,6},{6,5},{7,4},{8,11},{9,10},{10,... | collective-permute-start | bytes 49160 | tf_op jit(solution)/shard_map/ppermute | solution.py:576
  51.6 4.0 %copy-start.18 = (f32[128]{0:T(128)S(1)}, f32[128]{0:T(128)}, u32[]{:S(2)}) copy-start(f32[128]{0:T(128)} %param.19) | copy-start | bytes 1540
  51.6 4.0 %collective-permute-start.7 = (bf16[128,128]{1,0:T(8,128)(2,1)S(1)}, bf16[128,128]{1,0:T(8,128)(2,1)S(1)}, u32[]{:S(2)}, u32[]{:S(2)}) collective-permute-start(bf16[128,128]{1,0:T(8,128)(2,1)S(1)} %get-tuple-element.25), channel_id=1, source_target_pairs={{0,4},{4,0},{8,12},{12,8},{1,5},{5,1},{9,13},{13,9},{2,6},{6,2},{1... | collective-permute-start | bytes 98312 | tf_op jit(solution)/shard_map/ppermute | solution.py:637
  51.7 3.9 %collective-permute-start.8 = (bf16[128,128]{1,0:T(8,128)(2,1)S(1)}, bf16[128,128]{1,0:T(8,128)(2,1)S(1)}, u32[]{:S(2)}, u32[]{:S(2)}) collective-permute-start(bf16[128,128]{1,0:T(8,128)(2,1)S(1)} %get-tuple-element.26), channel_id=1, source_target_pairs={{4,8},{8,4},{12,0},{0,12},{5,9},{9,5},{13,1},{1,13},{6,10},{10,6},... | collective-permute-start | bytes 98312 | tf_op jit(solution)/shard_map/ppermute | solution.py:638
  53.3 2.3 %copy-start.3 = (bf16[1024,1024]{1,0:T(8,128)(2,1)S(1)}, bf16[1024,1024]{1,0:T(8,128)(2,1)}, u32[]{:S(2)}) copy-start(bf16[1024,1024]{1,0:T(8,128)(2,1)} %constant.7.clone.table_ref) | copy-start | bytes 6291460
  53.3 1.4 %copy-start.4 = (bf16[576,1024]{1,0:T(8,128)(2,1)S(1)}, bf16[576,1024]{1,0:T(8,128)(2,1)}, u32[]{:S(2)}) copy-start(bf16[576,1024]{1,0:T(8,128)(2,1)} %all-gather.4.cloned.1.call-done) | copy-start | bytes 3538948
Sparse Core Ops, SparseCore 0:
  14.2 19.1 all-gather.3

commit v4 on v3

--- a/solution.py
+++ b/solution.py
@@ -56,26 +56,6 @@
     )
 
 
-def surface_kernel(x_ref, flux_ref, s_ref, row_ref):
-    _, rows, channels, columns = x_ref.shape
-    col_group = lax.axis_index("gy")
-    is_atmos = lax.axis_index("comp") == 0
-
-    @pl.when(is_atmos)
-    def _():
-        weight = channel_column(flux_ref[...], channels, col_group * channels)
-        for r in range(rows):
-            row_ref[r : r + 1, :] = jnp.sum(x_ref[0, r] * weight, axis=0, keepdims=True)
-        s_ref[...] = to_tiles(row_ref[...]).astype(bf16)
-
-    @pl.when(jnp.logical_not(is_atmos))
-    def _():
-        gain = jnp.where(col_group == 0, 1.0, 0.0)
-        for r in range(rows):
-            row_ref[r : r + 1, :] = x_ref[0, r, 0:1, :] * gain
-        s_ref[...] = to_tiles(row_ref[...]).astype(bf16)
-
-
 def decay_terms(diff_column, half_rates):
     half = 0.5 / diff_column + half_rates
     sinh = jnp.sqrt(half * (half + 2.0))
@@ -83,25 +63,58 @@
     return 1.0 / grow, jnp.log(grow), sinh
 
 
-def forward_kernel(
-    groups_x, x_ref, wet_ref, diff_ref, rates_ref, table_ref, after_ref,
-    y_ref, beside_ref, edges_ref, edge_ref,
+def start_kernel(
+    groups_x, paired, x_hbm, wet_hbm, flux_hbm, diff_hbm, rates_hbm, table_hbm, *refs
 ):
-    del after_ref
-    _, rows, channels, columns = x_ref.shape
+    s_ref, y_ref, e1_ref, e3_ref, e2_ref, e4_ref = refs[:6]
+    if not paired:
+        pq_ref = refs[6]
+    (
+        x_ref, wet_ref, flux_ref, diff_ref, rates_ref, table_ref, flat_ref, row_ref,
+        edge_ref, x_sem, table_sem, small_sem,
+    ) = refs[-12:]
+    rows, channels, columns = x_ref.shape
     waves = columns // 2
     row_group = lax.axis_index("gx")
     col_group = lax.axis_index("gy")
     is_atmos = lax.axis_index("comp") == 0
+    x_copies = [
+        pltpu.make_async_copy(x_hbm.at[0, r], x_ref.at[r], x_sem.at[r]) for r in range(rows)
+    ]
 
     @pl.when(is_atmos)
     def _():
         step = 256
-        flat = x_ref[0].astype(bf16).reshape(rows * channels, columns)
-        for n in range(0, columns, step):
-            part = jnp.dot(flat, table_ref[:, n : n + step], preferred_element_type=f32)
+        small = [
+            pltpu.make_async_copy(hbm, ref, small_sem.at[k])
+            for k, (hbm, ref) in enumerate(
+                ((flux_hbm, flux_ref), (diff_hbm, diff_ref), (rates_hbm, rates_ref))
+            )
+        ]
+        table = [
+            pltpu.make_async_copy(
+                table_hbm.at[:, pl.ds(n, step)], table_ref.at[:, pl.ds(n, step)], table_sem.at[k]
+            )
+            for k, n in enumerate(range(0, columns, step))
+        ]
+        for copy in small + x_copies + table:
+            copy.start()
+        for copy in small:
+            copy.wait()
+        first = col_group * channels
+        weight = channel_column(flux_ref[...], channels, first)
+        for r in range(rows):
+            x_copies[r].wait()
+            row_ref[r : r + 1, :] = jnp.sum(x_ref[r] * weight, axis=0, keepdims=True)
+            flat_ref[r * channels : (r + 1) * channels, :] = x_ref[r].astype(bf16)
+        s_ref[...] = to_tiles(row_ref[...]).astype(bf16)
+        for k, n in enumerate(range(0, columns, step)):
+            table[k].wait()
+            part = jnp.dot(
+                flat_ref[...], table_ref[:, n : n + step], preferred_element_type=f32
+            )
             y_ref[:, :, n : n + step] = part.reshape(rows, channels, step)
-        diff = channel_column(diff_ref[...], channels, col_group * channels)
+        diff = channel_column(diff_ref[...], channels, first)
         total = rows * groups_x
         base = (row_group * rows).astype(f32)
         for n in range(0, waves, LANES):
@@ -121,28 +134,65 @@
                 for r in reversed(range(rows)):
                     power = power * lam2
                     q = lam * q + (1.0 - power) * y_ref[r, :, lanes]
-                beside_ref[0:channels, lanes] = p.astype(bf16)
-                beside_ref[channels : 2 * channels, lanes] = q.astype(bf16)
+                if paired:
+                    for mask, out in ((1, e1_ref), (2, e2_ref), (3, e3_ref)):
+                        upward = row_group < (row_group ^ mask)
+                        out[0:channels, lanes] = jnp.where(upward, p, q).astype(bf16)
+                else:
+                    pq_ref[0, :, lanes] = p.astype(bf16)
+                    pq_ref[1, :, lanes] = q.astype(bf16)
 
     @pl.when(jnp.logical_not(is_atmos))
     def _():
+        wet_copy = pltpu.make_async_copy(wet_hbm, wet_ref, small_sem.at[0])
+        for copy in x_copies:
+            copy.start()
+        wet_copy.start()
+        for copy in x_copies:
+            copy.wait()
+        gain = jnp.where(col_group == 0, 1.0, 0.0)
+        for r in range(rows):
+            row_ref[r : r + 1, :] = x_ref[r, 0:1, :] * gain
+        s_ref[...] = to_tiles(row_ref[...]).astype(bf16)
         levels = channels // 2
         lines = 2 * channels
+        even_x = row_group % 2 == 0
+        even_y = col_group % 2 == 0
+        wet_copy.wait()
         wet = wet_ref[...].astype(f32)
-        beside_ref[0:lines, :] = x_ref[0, :2].reshape(lines, columns).astype(bf16)
-        beside_ref[lines : 2 * lines, :] = (
-            x_ref[0, rows - 2 :].reshape(lines, columns).astype(bf16)
-        )
-        beside_ref[2 * lines : 2 * lines + 16, :] = jnp.concatenate([wet, wet], axis=0).astype(
-            bf16
-        )
-        for r in range(rows):
-            for t in range(2):
-                at = (r * 2 + t) * 4
-                c = t * levels
-                edge_ref[at : at + 2, :] = x_ref[0, r, c : c + 2, :]
-                edge_ref[at + 2 : at + 4, :] = x_ref[0, r, c + levels - 2 : c + levels, :]
-        edges_ref[...] = edge_ref[...].astype(bf16)
+        wet = jnp.concatenate([wet, wet], axis=0).astype(bf16)
+
+        def put(out, last):
+            @pl.when(last)
+            def _():
+                out[0:lines, :] = x_ref[rows - 2 :].reshape(lines, columns).astype(bf16)
+
+            @pl.when(jnp.logical_not(last))
+            def _():
+                out[0:lines, :] = x_ref[:2].reshape(lines, columns).astype(bf16)
+
+            out[lines : lines + 16, :] = wet
+
+        put(e1_ref, even_x)
+        put(e3_ref, jnp.logical_not(even_x))
+
+        def put_edges(out, level):
+            for r in range(rows):
+                for t in range(2):
+                    at = (r * 2 + t) * 2
+                    c = t * levels + level
+                    edge_ref[at : at + 2, :] = x_ref[r, c : c + 2, :]
+            out[...] = edge_ref[...].astype(bf16)
+
+        @pl.when(even_y)
+        def _():
+            put_edges(e2_ref, levels - 2)
+            put_edges(e4_ref, 0)
+
+        @pl.when(jnp.logical_not(even_y))
+        def _():
+            put_edges(e2_ref, 0)
+            put_edges(e4_ref, levels - 2)
 
 
 def regrid_kernel(n_msgs, *refs):
@@ -223,42 +273,40 @@
     sent_ref[...] = land.astype(bf16)
 
 
-def heat_kernel(rows, levels_edges_ref, land_ref, *refs):
+def heat_kernel(rows, e2_ref, e4_ref, land_ref, *refs):
     parts = refs[:-3]
     sum_ref, near_ref, far_ref = refs[-3:]
     cells = land_ref.shape[0]
     columns = cells // rows * LANES
-    groups_y = levels_edges_ref.shape[0]
-    row_group = lax.axis_index("gx")
-    col_group = lax.axis_index("gy")
+    even_x = lax.axis_index("gx") % 2 == 0
+    even_y = lax.axis_index("gy") % 2 == 0
     total = land_ref[...]
     for part in parts:
         total = total + part[...].astype(f32)
     sum_ref[...] = total
-    before = jnp.maximum(col_group - 1, 0)
-    after = jnp.minimum(col_group + 1, groups_y - 1)
 
     def corners(row):
-        start = row * 8 // 16 * 16
-        low = levels_edges_ref[before, start : start + 16, :].astype(f32)
-        high = levels_edges_ref[after, start : start + 16, :].astype(f32)
-        at = row * 8 - start
-        lines = [low[at + 3 : at + 4], low[at + 7 : at + 8], high[at : at + 1], high[at + 4 : at + 5]]
+        start = row * 4 // 16 * 16
+        one = e2_ref[start : start + 16, :].astype(f32)
+        two = e4_ref[start : start + 16, :].astype(f32)
+        low = jnp.where(even_y, two, one)
+        high = jnp.where(even_y, one, two)
+        at = row * 4 - start
+        lines = [low[at + 1 : at + 2], low[at + 3 : at + 4], high[at : at + 1], high[at + 2 : at + 3]]
         return to_tiles(jnp.concatenate(lines + [jnp.zeros((4, columns), f32)], axis=0))
 
     first, last = corners(0), corners(rows - 1)
-    even = row_group % 2 == 0
     near_ref[0:cells, :] = total.astype(bf16)
     far_ref[0:cells, :] = total.astype(bf16)
-    near_ref[cells:, :] = jnp.where(even, last, first).astype(bf16)
-    far_ref[cells:, :] = jnp.where(even, first, last).astype(bf16)
+    near_ref[cells:, :] = jnp.where(even_x, last, first).astype(bf16)
+    far_ref[cells:, :] = jnp.where(even_x, first, last).astype(bf16)
 
 
 def steps_kernel(
-    groups_x, groups_y, summed, x_ref, wet_ref, diff_ref, rates_ref, y_ref, beside_ref,
-    edges_ref, *refs,
+    groups_x, groups_y, paired, x_ref, wet_ref, diff_ref, rates_ref, y_ref, e1_ref, e3_ref,
+    e2_ref, e4_ref, *refs,
 ):
-    if summed:
+    if not paired:
         pin_ref, qin_ref = refs[:2]
     base_ref, zb_ref, c_ref, z_ref, t0_ref, t1_ref, w_ref = refs[-7:]
     _, rows, channels, columns = x_ref.shape
@@ -290,24 +338,21 @@
                 power = power * lam2
                 highs.append(1.0 - power)
             highs = highs[::-1]
-            if not summed:
-                decays = []
-                for band in range(groups_x):
-                    gap = (jnp.abs(row_group - band) - 1) * rows
-                    decays.append(jnp.exp(-jnp.maximum(gap, 0).astype(f32) * alpha))
             for part in (n, n + waves):
                 lanes = slice(part, part + LANES)
-                if summed:
+                if paired:
+                    pin = jnp.zeros((channels, LANES), f32)
+                    qin = jnp.zeros((channels, LANES), f32)
+                    for mask, msg in ((1, e1_ref), (2, e2_ref), (3, e3_ref)):
+                        band = row_group ^ mask
+                        gap = (jnp.abs(row_group - band) - 1) * rows
+                        term = jnp.exp(-gap.astype(f32) * alpha)
+                        term = term * msg[0:channels, lanes].astype(f32)
+                        pin = pin + jnp.where(band < row_group, term, 0.0)
+                        qin = qin + jnp.where(band > row_group, term, 0.0)
+                else:
                     pin = pin_ref[:, lanes]
                     qin = qin_ref[:, lanes]
-                else:
-                    pin = jnp.zeros((channels, LANES), f32)
-                    qin = jnp.zeros((channels, LANES), f32)
-                    for band in range(groups_x):
-                        p = beside_ref[band, 0:channels, lanes].astype(f32)
-                        q = beside_ref[band, channels : 2 * channels, lanes].astype(f32)
-                        pin = pin + jnp.where(band < row_group, decays[band] * p, 0.0)
-                        qin = qin + jnp.where(band > row_group, decays[band] * q, 0.0)
                 f = pin
                 for r in range(rows):
                     f = lam * f + lows[r] * y_ref[r, :, lanes]
@@ -327,17 +372,16 @@
         last_x = row_group == groups_x - 1
         top = col_group == 0
         bottom = col_group == groups_y - 1
-        if summed:
-            under, over = 0, 1
-        else:
-            under = jnp.maximum(row_group - 1, 0)
-            over = jnp.minimum(row_group + 1, groups_x - 1)
-
-        below = beside_ref[under, 2 * lines : 2 * lines + 16, :].astype(f32)
-        above = beside_ref[over, 2 * lines : 2 * lines + 16, :].astype(f32)
-        w_ref[0:2, :] = jnp.where(first_x, 0.0, below[rows - 2 : rows])
+        even_x = row_group % 2 == 0
+        even_y = col_group % 2 == 0
+
+        one = e1_ref[lines : lines + 16, :].astype(f32)
+        three = e3_ref[lines : lines + 16, :].astype(f32)
+        below = jnp.where(even_x, three, one)[rows - 2 : rows]
+        above = jnp.where(even_x, one, three)[0:2]
+        w_ref[0:2, :] = jnp.where(first_x, 0.0, below)
         w_ref[2 : rows + 2, :] = wet_ref[...].astype(f32)
-        w_ref[rows + 2 : rows + 4, :] = jnp.where(last_x, 0.0, above[0:2])
+        w_ref[rows + 2 : rows + 4, :] = jnp.where(last_x, 0.0, above)
 
         span = rows + 2
         north = w_ref[0:span, :]
@@ -355,8 +399,10 @@
         c_ref[5, 0:span, :] = mixing_rate * here
         c_ref[6, 0:span, :] = here
 
-        below = beside_ref[under, lines : 2 * lines, :].astype(f32)
-        above = beside_ref[over, 0:lines, :].astype(f32)
+        one = e1_ref[0:lines, :].astype(f32)
+        three = e3_ref[0:lines, :].astype(f32)
+        below = jnp.where(even_x, three, one)
+        above = jnp.where(even_x, one, three)
         blank = jnp.zeros((8, columns), f32)
         for k in range(2):
             for t in range(2):
@@ -365,14 +411,16 @@
                 t0_ref[rows + 2 + k, t, 0:levels, :] = above[c : c + levels]
                 t0_ref[k, t, levels:ring, :] = blank
                 t0_ref[rows + 2 + k, t, levels:ring, :] = blank
-        before = edges_ref[jnp.maximum(col_group - 1, 0)].astype(f32)
-        after = edges_ref[jnp.minimum(col_group + 1, groups_y - 1)].astype(f32)
+        one = e2_ref[...].astype(f32)
+        two = e4_ref[...].astype(f32)
+        before = jnp.where(even_y, two, one)
+        after = jnp.where(even_y, one, two)
         for r in range(rows):
             for t in range(2):
-                k = (r * 2 + t) * 4
+                k = (r * 2 + t) * 2
                 t0_ref[r + 2, t, 0:levels, :] = x_ref[0, r, t * levels : (t + 1) * levels, :]
                 t0_ref[r + 2, t, levels : levels + 2, :] = after[k : k + 2]
-                t0_ref[r + 2, t, ring - 2 : ring, :] = before[k + 2 : k + 4]
+                t0_ref[r + 2, t, ring - 2 : ring, :] = before[k : k + 2]
 
         def close(ref, r):
             for t in range(2):
@@ -511,6 +559,7 @@
     flux_row = flux_weight[None, :]
     gain_row = variable_sea_response[None, :]
     diff_row = diffusivity[None, :]
+    paired = groups_x == 4
     params = functools.partial(pltpu.CompilerParams, vmem_limit_bytes=40 * 2**20)
     vmem = pl.BlockSpec(memory_space=pltpu.VMEM)
     smem = pl.BlockSpec(memory_space=pltpu.SMEM)
@@ -519,15 +568,40 @@
     def shape(dims, dtype):
         return jax.ShapeDtypeStruct(dims, dtype)
 
-    partial_surface = pl.pallas_call(
-        surface_kernel,
-        out_shape=shape((cells, LANES), bf16),
-        in_specs=[vmem, vmem],
-        out_specs=vmem,
-        scratch_shapes=[pltpu.VMEM((rows, columns), f32)],
+    lines = 2 * channels + 16
+    shapes = [
+        shape((cells, LANES), bf16),
+        shape((rows, channels, columns), f32),
+        shape((lines, columns), bf16),
+        shape((lines, columns), bf16),
+        shape((4 * rows, columns), bf16),
+        shape((4 * rows, columns), bf16),
+    ]
+    if not paired:
+        shapes.append(shape((2, channels, columns), bf16))
+    partial_surface, y, e1, e3, e2, e4, *sums = pl.pallas_call(
+        functools.partial(start_kernel, groups_x, paired),
+        out_shape=shapes,
+        in_specs=[anywhere] * 6,
+        out_specs=[vmem] * len(shapes),
+        scratch_shapes=[
+            pltpu.VMEM((rows, channels, columns), f32),
+            pltpu.VMEM((rows, columns), jnp.int32),
+            pltpu.VMEM(flux_row.shape, f32),
+            pltpu.VMEM(diff_row.shape, f32),
+            pltpu.VMEM(half_rates.shape, f32),
+            pltpu.VMEM((columns, columns), bf16),
+            pltpu.VMEM((rows * channels, columns), bf16),
+            pltpu.VMEM((rows, columns), f32),
+            pltpu.VMEM((4 * rows, columns), f32),
+            pltpu.SemaphoreType.DMA((rows,)),
+            pltpu.SemaphoreType.DMA((columns // 256,)),
+            pltpu.SemaphoreType.DMA((3,)),
+        ],
         compiler_params=params(),
-        name="surface_partials",
-    )(fields, flux_row)
+        name="surface_and_forward_or_halos",
+    )(fields, wet_cells, flux_row, diff_row, half_rates, forward)
+
     surfaces = []
     for mask in range(groups_y):
         route = []
@@ -535,22 +609,28 @@
             route += both_ways([(j, groups_y + (j ^ mask))])
         surfaces.append(lax.ppermute(partial_surface, ("comp", "gy"), route))
 
-    lines = 4 * channels + 16
-    y, beside, edges = pl.pallas_call(
-        functools.partial(forward_kernel, groups_x),
-        out_shape=[
-            shape((rows, channels, columns), f32),
-            shape((lines, columns), bf16),
-            shape((8 * rows, columns), bf16),
-        ],
-        in_specs=[vmem] * 5 + [anywhere],
-        out_specs=[vmem] * 3,
-        scratch_shapes=[pltpu.VMEM((8 * rows, columns), f32)],
-        compiler_params=params(),
-        name="forward_and_halos",
-    )(fields, wet_cells, diff_row, half_rates, forward, partial_surface)
-    beside = lax.all_gather(beside, "gx")
-    edges = lax.all_gather(edges, "gy")
+    def ring_pairs(count, odd):
+        return [(a, (a + 1) % count) for a in range(odd, count, 2)]
+
+    def flat(comp, i, j):
+        return (comp * groups_x + i) * groups_y + j
+
+    def level_route(odd):
+        pairs = []
+        for i in range(groups_x):
+            for a, b in ring_pairs(groups_y, odd):
+                pairs.append((flat(1, i, a), flat(1, i, b)))
+                if odd or not paired:
+                    pairs.append((flat(0, i, a), flat(0, i, b)))
+            if paired and not odd and i < i ^ 2:
+                pairs += [(flat(0, i, j), flat(0, i ^ 2, j)) for j in range(groups_y)]
+        return both_ways(pairs)
+
+    axes = ("comp", "gx", "gy")
+    e1 = lax.ppermute(e1, "gx", both_ways(ring_pairs(groups_x, 0)))
+    e3 = lax.ppermute(e3, "gx", both_ways(ring_pairs(groups_x, 1)))
+    e2 = lax.ppermute(e2, axes, level_route(0))
+    e4 = lax.ppermute(e4, axes, level_route(1))
 
     landing, sent = pl.pallas_call(
         functools.partial(regrid_kernel, groups_y),
@@ -578,34 +658,30 @@
     ]
 
     extra = []
-    if groups_x > 8:
-        mine = lax.axis_index("gx")
+    if not paired:
+        p, q = jnp.moveaxis(lax.all_gather(sums[0], "gx").astype(f32), 1, 0)
         viscous = lax.dynamic_slice_in_dim(
             diffusivity, lax.axis_index("gy") * channels, channels
         )[:, None]
         _, alpha, _ = decay_terms(viscous, half_rates)
         alpha = jnp.concatenate([alpha, alpha], axis=1)
-        gap = mine - jnp.arange(groups_x)
+        gap = lax.axis_index("gx") - jnp.arange(groups_x)
         decay = jnp.exp(
             -(rows * jnp.maximum(jnp.abs(gap) - 1, 0))[:, None, None] * alpha[None]
         )
-        p = beside[:, :channels].astype(f32)
-        q = beside[:, channels : 2 * channels].astype(f32)
         extra = [
             jnp.sum(jnp.where((gap > 0)[:, None, None], decay * p, 0.0), axis=0),
             jnp.sum(jnp.where((gap < 0)[:, None, None], decay * q, 0.0), axis=0),
         ]
-        near = jnp.stack([jnp.maximum(mine - 1, 0), jnp.minimum(mine + 1, groups_x - 1)])
-        beside = jnp.take(beside, near, axis=0)
     ring = channels // 2 + 8
     base, damped, coefs = pl.pallas_call(
-        functools.partial(steps_kernel, groups_x, groups_y, groups_x > 8),
+        functools.partial(steps_kernel, groups_x, groups_y, paired),
         out_shape=[
             shape((rows, channels, columns), f32),
             shape((rows * channels, columns), bf16),
             shape((7, 16, columns), f32),
         ],
-        in_specs=[vmem] * (7 + len(extra)),
+        in_specs=[vmem] * (9 + len(extra)),
         out_specs=[vmem] * 3,
         scratch_shapes=[
             pltpu.VMEM((rows, channels, LANES), f32),
@@ -615,7 +691,7 @@
         ],
         compiler_params=params(),
         name="damping_or_ocean_steps",
-    )(fields, wet_cells, diff_row, half_rates, y, beside, edges, *extra)
+    )(fields, wet_cells, diff_row, half_rates, y, e1, e3, e2, e4, *extra)
 
     surface_sum, near, far = pl.pallas_call(
         functools.partial(heat_kernel, rows),
@@ -624,18 +700,14 @@
             shape((cells + columns // 16, LANES), bf16),
             shape((cells + columns // 16, LANES), bf16),
         ],
-        in_specs=[vmem] * (2 + len(parts)),
+        in_specs=[vmem] * (3 + len(parts)),
         out_specs=[vmem] * 3,
         compiler_params=params(),
         name="surface_sum",
-    )(edges, landing, *parts)
-
-    def ring_pairs(odd):
-        pairs = [(a, (a + 1) % groups_x) for a in range(odd, groups_x, 2)]
-        return both_ways(pairs)
-
-    near = lax.ppermute(near, "gx", ring_pairs(0))
-    far = lax.ppermute(far, "gx", ring_pairs(1))
+    )(e2, e4, landing, *parts)
+
+    near = lax.ppermute(near, "gx", both_ways(ring_pairs(groups_x, 0)))
+    far = lax.ppermute(far, "gx", both_ways(ring_pairs(groups_x, 1)))
     return pl.pallas_call(
         functools.partial(last_kernel, groups_x, groups_y),
         out_shape=shape(fields.shape, f32),

time: 65.4 us -> 47.8 us (0.73); the launches traced: 64.2 us -> 47.5 us
  blocking collectives: 14.8 us -> 0 us
  between operations: 14.9 us -> 1.47 us
  waiting for transfers between devices: 5.14 us -> 13.1 us
  starting transfers between devices: 13.2 us -> 17.7 us
  local copies, waits for them, and re-layouts: 9.46 us -> 6.48 us
  Pallas kernels: 6.72 us -> 8.8 us
    all_gather x1 -> x0, blocking collectives: 14.8 us -> none  [local(): edges = lax.all_gather(edges, 'gy')]
    ppermute x3, waiting for transfers between devices: 0.01 us -> 10.7 us  [local(): lax.ppermute(sent, 'gy', [(j, j ^ mask) for j in range(groups_y)])]
    ppermute x2 -> x6, starting transfers between devices: 1.67 us -> 7.6 us  [the longest x1 2.62 us: local(): e3 = lax.ppermute(e3, 'gx', both_ways(ring_pairs(groups_x, 1)))]
    ppermute x4, waiting for transfers between devices: 5.11 us -> 1.33 us  [local(): surfaces.append(lax.ppermute(partial_surface, ('comp', 'gy'), route))]
    unnamed x38 -> x34, local copies, waits for them, and re-layouts: 9.46 us -> 6.48 us
    pallas_call x3 -> x2, Pallas kernels: 2.71 us -> 4.8 us  [the longest x1 3.98 us: local(): pl.pallas_call(functools.partial(start_kernel, groups_x, paired), out_sha...]
    ppermute x3, starting transfers between devices: 4.44 us -> 3.3 us  [local(): lax.ppermute(sent, 'gy', [(j, j ^ mask) for j in range(groups_y)])]
    ppermute x2 -> x6, waiting for transfers between devices: 0.01 us -> 1.1 us  [the longest x1 1.08 us: local(): far = lax.ppermute(far, 'gx', both_ways(ring_pairs(groups_x, 1)))]
  transfers between devices with their start and end apart: 10 -> 13, of which waited for: 2 -> 5; matrix products, arithmetic and copies ran while one was open for 0% -> 0% of each run, Pallas kernels for 5% -> 7%
where the time goes in v4:
time: 47.8 us; the launch traced here: 47.5 us
  starting transfers between devices  17.7 us (37%)
  waiting for transfers between devices  13.1 us (27%)
  Pallas kernels  8.8 us (18%)
  local copies, waits for them, and re-layouts  6.48 us (14%)
  between operations  1.47 us (3%)
    ppermute x3, waiting for transfers between devices, local(): lax.ppermute(sent, 'gy', [(j, j ^ mask) for j in range(groups_y)])  10.7 us
    ppermute x4, starting transfers between devices, local(): surfaces.append(lax.ppermute(partial_surface, ('comp', 'gy'), route))  6.78 us
    unnamed x34, local copies, waits for them, and re-layouts  6.48 us
    pallas_call x1, Pallas kernels, local(): pl.pallas_call(functools.partial(start_kernel, groups_x, paired), out_sha...  3.98 us
    ppermute x3, starting transfers between devices, local(): lax.ppermute(sent, 'gy', [(j, j ^ mask) for j in range(groups_y)])  3.3 us
    ppermute x1, starting transfers between devices, local(): e3 = lax.ppermute(e3, 'gx', both_ways(ring_pairs(groups_x, 1)))  2.62 us
    ppermute x1, starting transfers between devices, local(): e4 = lax.ppermute(e4, axes, level_route(1))  2.41 us
    pallas_call x1, Pallas kernels, local(): pl.pallas_call(functools.partial(regrid_kernel, groups_y), out_shape=[sha...  2.26 us
  transfers between devices with their start and end apart: 13, of which 5 were waited for; matrix products, arithmetic and copies ran while one was open for 0% of the time, Pallas kernels for 7%

profile of v4, /device:TPU:0, one launch (start us, length us, event | category | flops | bytes accessed | tf_op | source)
XLA Modules:
  0.0 47.5 jit_solution(14438786506755940766)
XLA Ops:
  0.0 0.0 copy-start.12
  0.0 0.0 copy-start.14
  0.0 0.0 copy-start
  0.0 1.2 %copy-done = f32[1,8,32,1024]{3,2,1,0:T(8,128)S(1)} copy-done((f32[1,8,32,1024]{3,2,1,0:T(8,128)S(1)}, f32[1,8,32,1024]{3,2,1,0:T(8,128)}, u32[]{:S(2)}) %copy-start) | copy-done | bytes 1048600
  1.3 0.0 copy-start.2
  1.3 1.6 %copy-done.2 = bf16[1024,1024]{1,0:T(8,128)(2,1)S(1)} copy-done((bf16[1024,1024]{1,0:T(8,128)(2,1)S(1)}, bf16[1024,1024]{1,0:T(8,128)(2,1)}, u32[]{:S(2)}) %copy-start.2) | copy-done | bytes 2097176
  2.8 0.0 copy-start.6
  2.9 0.8 %copy-done.6 = s32[8,1024]{1,0:T(8,128)S(1)} copy-done((s32[8,1024]{1,0:T(8,128)S(1)}, s32[8,1024]{1,0:T(8,128)}, u32[]{:S(2)}) %copy-start.6) | copy-done | bytes 32792
  3.6 0.0 copy-start.11
  3.6 0.7 %copy-done.11 = f32[1,512]{1,0:T(1,128)S(1)} copy-done((f32[1,512]{1,0:T(1,128)S(1)}, f32[1,512]{1,0:T(1,128)}, u32[]{:S(2)}) %copy-start.11) | copy-done | bytes 2072
  4.3 0.0 copy-start.13
  4.3 0.7 %copy-done.13 = f32[128]{0:T(128)S(1)} copy-done((f32[128]{0:T(128)S(1)}, f32[128]{0:T(128)}, u32[]{:S(2)}) %copy-start.13) | copy-done | bytes 536
  4.9 0.0 copy-start.15
  4.9 0.7 %copy-done.15 = f32[128]{0:T(128)S(1)} copy-done((f32[128]{0:T(128)S(1)}, f32[128]{0:T(128)}, u32[]{:S(2)}) %copy-start.15) | copy-done | bytes 536
  5.6 0.0 copy-start.4
  5.6 0.0 copy-start.5
  5.6 0.0 copy-start.7
  5.6 0.0 copy-start.8
  5.6 0.0 copy-start.9
  5.6 0.0 copy-start.1
  5.6 4.0 %surface_and_forward_or_halos.1 = (bf16[64,128]{1,0:T(8,128)(2,1)S(1)}, f32[8,32,1024]{2,1,0:T(8,128)S(1)}, bf16[80,1024]{1,0:T(8,128)(2,1)S(1)}, bf16[80,1024]{...) custom-call(f32[1,8,32,1024]{3,2,1,0:T(8,128)S(1)} %copy-done, ...), custom_call_target="tpu_custom_call" | custom-call | tf_op jit(solution)/shard_map/surface_and_forward_or_halos/pallas_call | solution.py:582
  9.6 0.5 %collective-permute-start = (bf16[80,1024]{1,0:T(8,128)(2,1)S(1)}, bf16[80,1024]{1,0:T(8,128)(2,1)S(1)}, u32[]{:S(2)}, u32[]{:S(2)}) collective-permute-start(bf16[80,1024]{1,0:T(8,128)(2,1)S(1)} %get-tuple-element.20), channel_id=1, source_target_pairs={{0,4},{4,0},{8,12},{12,8},{1,5},{5,1},{9,13},{13,9},{2,6},{6,2},{1... | collective-permute-start | bytes 491528 | tf_op jit(solution)/shard_map/ppermute | solution.py:630
  10.1 2.6 %collective-permute-start.1 = (bf16[80,1024]{1,0:T(8,128)(2,1)S(1)}, bf16[80,1024]{1,0:T(8,128)(2,1)S(1)}, u32[]{:S(2)}, u32[]{:S(2)}) collective-permute-start(bf16[80,1024]{1,0:T(8,128)(2,1)S(1)} %get-tuple-element.21), channel_id=1, source_target_pairs={{4,8},{8,4},{12,0},{0,12},{5,9},{9,5},{13,1},{1,13},{6,10},{10,6},... | collective-permute-start | bytes 491528 | tf_op jit(solution)/shard_map/ppermute | solution.py:631
  12.8 0.0 collective-permute-start.4
  12.8 3.0 %collective-permute-start.5 = (bf16[64,128]{1,0:T(8,128)(2,1)S(1)}, bf16[64,128]{1,0:T(8,128)(2,1)S(1)}, u32[]{:S(2)}, u32[]{:S(2)}) collective-permute-start(bf16[64,128]{1,0:T(8,128)(2,1)S(1)} %get-tuple-element.27), channel_id=1, source_target_pairs={{0,17},{17,0},{1,16},{16,1},{2,19},{19,2},{3,18},{18,3},{4,21},{21... | collective-permute-start | bytes 49160 | tf_op jit(solution)/shard_map/ppermute | solution.py:610
  15.8 2.0 %collective-permute-start.6 = (bf16[64,128]{1,0:T(8,128)(2,1)S(1)}, bf16[64,128]{1,0:T(8,128)(2,1)S(1)}, u32[]{:S(2)}, u32[]{:S(2)}) collective-permute-start(bf16[64,128]{1,0:T(8,128)(2,1)S(1)} %get-tuple-element.27), channel_id=1, source_target_pairs={{0,18},{18,0},{1,19},{19,1},{2,16},{16,2},{3,17},{17,3},{4,22},{22... | collective-permute-start | bytes 49160 | tf_op jit(solution)/shard_map/ppermute | solution.py:610
  17.8 0.0 collective-permute-done.4.refs_0_
  17.8 1.7 %collective-permute-start.7 = (bf16[64,128]{1,0:T(8,128)(2,1)S(1)}, bf16[64,128]{1,0:T(8,128)(2,1)S(1)}, u32[]{:S(2)}, u32[]{:S(2)}) collective-permute-start(bf16[64,128]{1,0:T(8,128)(2,1)S(1)} %get-tuple-element.27), channel_id=1, source_target_pairs={{0,19},{19,0},{1,18},{18,1},{2,17},{17,2},{3,16},{16,3},{4,23},{23... | collective-permute-start | bytes 49160 | tf_op jit(solution)/shard_map/ppermute | solution.py:610
  19.5 0.0 collective-permute-done.5.refs_1_
  19.5 0.5 %collective-permute-start.2 = (bf16[32,1024]{1,0:T(8,128)(2,1)S(1)}, bf16[32,1024]{1,0:T(8,128)(2,1)S(1)}, u32[]{:S(2)}, u32[]{:S(2)}) collective-permute-start(bf16[32,1024]{1,0:T(8,128)(2,1)S(1)} %get-tuple-element.22), channel_id=1, source_target_pairs={{16,17},{17,16},{18,19},{19,18},{0,8},{8,0},{1,9},{9,1},{2,10},{10... | collective-permute-start | bytes 196616 | tf_op jit(solution)/shard_map/ppermute | solution.py:632
  20.1 1.3 %collective-permute-done.6.refs_2_ = bf16[64,128]{1,0:T(8,128)(2,1)S(1)} collective-permute-done((bf16[64,128]{1,0:T(8,128)(2,1)S(1)}, bf16[64,128]{1,0:T(8,128)(2,1)S(1)}, u32[]{:S(2)}, u32[]{:S(2)}) %collective-permute-start.6) | collective-permute-done | bytes 16416 | tf_op jit(solution)/shard_map/ppermute | solution.py:610
  21.4 2.4 %collective-permute-start.3 = (bf16[32,1024]{1,0:T(8,128)(2,1)S(1)}, bf16[32,1024]{1,0:T(8,128)(2,1)S(1)}, u32[]{:S(2)}, u32[]{:S(2)}) collective-permute-start(bf16[32,1024]{1,0:T(8,128)(2,1)S(1)} %get-tuple-element.23), channel_id=1, source_target_pairs={{17,18},{18,17},{1,2},{2,1},{19,16},{16,19},{3,0},{0,3},{21,22},{2... | collective-permute-start | bytes 196616 | tf_op jit(solution)/shard_map/ppermute | solution.py:633
  25.1 0.0 copy-start.3
  25.1 0.0 collective-permute-done.7.refs_3_
  25.1 0.0 copy-done.4
  25.1 0.0 copy-done.5
  25.1 0.0 copy-done.7
  25.2 0.0 copy-done.8
  25.2 0.0 copy-done.9
  25.2 0.0 copy-start.10
  25.2 0.8 %copy-done.10 = s32[1,1,32,128]{3,2,1,0:T(8,128)S(1)} copy-done((s32[1,1,32,128]{3,2,1,0:T(8,128)S(1)}, s32[1,1,32,128]{3,2,1,0:T(8,128)}, u32[]{:S(2)}) %copy-start.10) | copy-done | bytes 16408
  26.0 0.0 copy-start.16
  26.0 2.3 %regrid_blocks.1 = (f32[64,128]{1,0:T(8,128)S(1)}, bf16[64,128]{1,0:T(8,128)(2,1)S(1)}) custom-call(bf16[64,128]{1,0:T(8,128)(2,1)S(1)} %collective-permute-done.4.refs_0_, bf16[64,128]{1,0:T(8,128)(2,1)S(1)} %collective-permute-done.5.refs_1_, bf16[64,128]{1,0:T(8,128)(2,1)S(1)} %collective-permute-done.6.refs_2_, ...), custom_call_target="tpu_custom_call" | custom-call | tf_op jit(solution)/shard_map/regrid_blocks/pallas_call | solution.py:635
  28.3 0.9 %collective-permute-start.8 = (bf16[64,128]{1,0:T(8,128)(2,1)S(1)}, bf16[64,128]{1,0:T(8,128)(2,1)S(1)}, u32[]{:S(2)}, u32[]{:S(2)}) collective-permute-start(bf16[64,128]{1,0:T(8,128)(2,1)S(1)} %get-tuple-element.29), channel_id=1, source_target_pairs={{0,1},{1,0},{2,3},{3,2},{4,5},{5,4},{6,7},{7,6},{8,9},{9,8},{10,11... | collective-permute-start | bytes 49160 | tf_op jit(solution)/shard_map/ppermute | solution.py:656
  29.2 2.9 %collective-permute-done.8.refs_0_ = bf16[64,128]{1,0:T(8,128)(2,1)S(1)} collective-permute-done((bf16[64,128]{1,0:T(8,128)(2,1)S(1)}, bf16[64,128]{1,0:T(8,128)(2,1)S(1)}, u32[]{:S(2)}, u32[]{:S(2)}) %collective-permute-start.8) | collective-permute-done | bytes 16416 | tf_op jit(solution)/shard_map/ppermute | solution.py:656
  32.1 0.4 collective-permute-start.9
  32.5 4.3 %collective-permute-done.9.refs_1_ = bf16[64,128]{1,0:T(8,128)(2,1)S(1)} collective-permute-done((bf16[64,128]{1,0:T(8,128)(2,1)S(1)}, bf16[64,128]{1,0:T(8,128)(2,1)S(1)}, u32[]{:S(2)}, u32[]{:S(2)}) %collective-permute-start.9) | collective-permute-done | bytes 16416 | tf_op jit(solution)/shard_map/ppermute | solution.py:656
  36.8 2.0 %collective-permute-start.10 = (bf16[64,128]{1,0:T(8,128)(2,1)S(1)}, bf16[64,128]{1,0:T(8,128)(2,1)S(1)}, u32[]{:S(2)}, u32[]{:S(2)}) collective-permute-start(bf16[64,128]{1,0:T(8,128)(2,1)S(1)} %get-tuple-element.29), channel_id=1, source_target_pairs={{0,3},{1,2},{2,1},{3,0},{4,7},{5,6},{6,5},{7,4},{8,11},{9,10},{10,... | collective-permute-start | bytes 49160 | tf_op jit(solution)/shard_map/ppermute | solution.py:656
  38.8 3.5 %collective-permute-done.10.refs_2_ = bf16[64,128]{1,0:T(8,128)(2,1)S(1)} collective-permute-done((bf16[64,128]{1,0:T(8,128)(2,1)S(1)}, bf16[64,128]{1,0:T(8,128)(2,1)S(1)}, u32[]{:S(2)}, u32[]{:S(2)}) %collective-permute-start.10) | collective-permute-done | bytes 16416 | tf_op jit(solution)/shard_map/ppermute | solution.py:656
  42.3 0.0 collective-permute-done.2.e2_ref
  42.3 0.0 collective-permute-done.3.e4_ref
  42.3 0.1 collective-permute-start.11
  42.4 1.5 %collective-permute-start.12 = (bf16[128,128]{1,0:T(8,128)(2,1)S(1)}, bf16[128,128]{1,0:T(8,128)(2,1)S(1)}, u32[]{:S(2)}, u32[]{:S(2)}) collective-permute-start(bf16[128,128]{1,0:T(8,128)(2,1)S(1)} %get-tuple-element.32), channel_id=1, source_target_pairs={{4,8},{8,4},{12,0},{0,12},{5,9},{9,5},{13,1},{1,13},{6,10},{10,6},... | collective-permute-start | bytes 98312 | tf_op jit(solution)/shard_map/ppermute | solution.py:710
  43.9 0.0 collective-permute-done.e1_ref
  43.9 0.0 collective-permute-done.1.e3_ref
  43.9 0.0 copy-done.12
  43.9 0.0 copy-done.14
  43.9 0.0 copy-done.1
  43.9 0.8 %damping_or_ocean_steps.1 = (f32[8,32,1024]{2,1,0:T(8,128)S(1)}, bf16[256,1024]{1,0:T(8,128)(2,1)S(1)}, f32[7,16,1024]{2,1,0:T(8,128)S(1)}) custom-call(f32[1,8,32,1024]{3,2,1,0:T(8,128)S(1)} %copy-done.1, s32[8,1024]{1,0:T(8,128)S(1)} %copy-done.6, f32[1,128]{1,0:T(1,128)S(1)} %bitcast.4, f32[1,512]{1,0:T(1,128)S(1)} %copy-done.12, ...), custom_call_target="tpu_custom_call" | custom-call | tf_op jit(solution)/shard_map/damping_or_ocean_steps/pallas_call | solution.py:677
  44.7 0.0 collective-permute-done.11.near_ref
  44.7 1.1 %collective-permute-done.12.far_ref = bf16[128,128]{1,0:T(8,128)(2,1)S(1)} collective-permute-done((bf16[128,128]{1,0:T(8,128)(2,1)S(1)}, bf16[128,128]{1,0:T(8,128)(2,1)S(1)}, u32[]{:S(2)}, u32[]{:S(2)}) %collective-permute-start.12) | collective-permute-done | bytes 32800 | tf_op jit(solution)/shard_map/ppermute | solution.py:710
  45.8 0.0 copy-done.3
  45.8 0.0 copy-done.16
  45.8 1.7 %inverse_or_heat.1 = f32[1,8,32,1024]{3,2,1,0:T(8,128)} custom-call(f32[1,128]{1,0:T(1,128)S(1)} %bitcast.6, bf16[1024,1024]{1,0:T(8,128)(2,1)S(1)} %copy-done.3, f32[8,32,1024]{2,1,0:T(8,128)S(1)} %get-tuple-element.24.base_ref, bf16[256,1024]{1,0:T(8,128)(2,1)S(1)} %get-tuple-element.25.zb_ref, f32[7,16,1024]{2,1,0:T(8,128)S(1)} %get-tuple-element.26.c_ref, ...), custom_call_target="tpu_custom_call" | custom-call | tf_op jit(solution)/shard_map/inverse_or_heat/pallas_call | solution.py:711
  (1 shorter events, 0.0 us)
Async XLA Ops:
  0.0 43.9 %copy-start.12 = (f32[1,512]{1,0:T(1,128)S(1)}, f32[1,512]{1,0:T(1,128)}, u32[]{:S(2)}) copy-start(f32[1,512]{1,0:T(1,128)} %constant.8.clone.rates_hbm.rates_ref) | copy-start | bytes 6148
  0.0 43.9 %copy-start.14 = (f32[128]{0:T(128)S(1)}, f32[128]{0:T(128)}, u32[]{:S(2)}) copy-start(f32[128]{0:T(128)} %param.20) | copy-start | bytes 1540
  0.0 1.3 %copy-start = (f32[1,8,32,1024]{3,2,1,0:T(8,128)S(1)}, f32[1,8,32,1024]{3,2,1,0:T(8,128)}, u32[]{:S(2)}) copy-start(f32[1,8,32,1024]{3,2,1,0:T(8,128)} %x_ref.1) | copy-start | bytes 3145732
  1.3 1.6 %copy-start.2 = (bf16[1024,1024]{1,0:T(8,128)(2,1)S(1)}, bf16[1024,1024]{1,0:T(8,128)(2,1)}, u32[]{:S(2)}) copy-start(bf16[1024,1024]{1,0:T(8,128)(2,1)} %constant.6.clone.table_hbm) | copy-start | bytes 6291460
  2.8 0.8 %copy-start.6 = (s32[8,1024]{1,0:T(8,128)S(1)}, s32[8,1024]{1,0:T(8,128)}, u32[]{:S(2)}) copy-start(s32[8,1024]{1,0:T(8,128)} %wet_ref.1) | copy-start | bytes 98308
  3.6 0.7 %copy-start.11 = (f32[1,512]{1,0:T(1,128)S(1)}, f32[1,512]{1,0:T(1,128)}, u32[]{:S(2)}) copy-start(f32[1,512]{1,0:T(1,128)} %constant.8.clone.rates_hbm.rates_ref) | copy-start | bytes 6148
  4.3 0.7 %copy-start.13 = (f32[128]{0:T(128)S(1)}, f32[128]{0:T(128)}, u32[]{:S(2)}) copy-start(f32[128]{0:T(128)} %param.20) | copy-start | bytes 1540
  4.9 0.7 %copy-start.15 = (f32[128]{0:T(128)S(1)}, f32[128]{0:T(128)}, u32[]{:S(2)}) copy-start(f32[128]{0:T(128)} %param.18) | copy-start | bytes 1540
  5.6 19.5 %copy-start.4 = (bf16[1,1,32,128,128]{4,3,2,1,0:T(8,128)(2,1)S(1)}, bf16[1,1,32,128,128]{4,3,2,1,0:T(8,128)(2,1)}, u32[]{:S(2)}) copy-start(bf16[1,1,32,128,128]{4,3,2,1,0:T(8,128)(2,1)} %refs_7_.1) | copy-start | bytes 3145732
  5.6 19.5 %copy-start.5 = (bf16[1,1,32,128,128]{4,3,2,1,0:T(8,128)(2,1)S(1)}, bf16[1,1,32,128,128]{4,3,2,1,0:T(8,128)(2,1)}, u32[]{:S(2)}) copy-start(bf16[1,1,32,128,128]{4,3,2,1,0:T(8,128)(2,1)} %refs_11_.1) | copy-start | bytes 3145732
  5.6 19.5 %copy-start.7 = (s32[1,1,32,128]{3,2,1,0:T(8,128)S(1)}, s32[1,1,32,128]{3,2,1,0:T(8,128)}, u32[]{:S(2)}) copy-start(s32[1,1,32,128]{3,2,1,0:T(8,128)} %refs_4_.1) | copy-start | bytes 49156
  5.6 19.6 %copy-start.8 = (s32[1,1,32,128]{3,2,1,0:T(8,128)S(1)}, s32[1,1,32,128]{3,2,1,0:T(8,128)}, u32[]{:S(2)}) copy-start(s32[1,1,32,128]{3,2,1,0:T(8,128)} %refs_5_.1) | copy-start | bytes 49156
  5.6 19.6 %copy-start.9 = (s32[1,1,32,128]{3,2,1,0:T(8,128)S(1)}, s32[1,1,32,128]{3,2,1,0:T(8,128)}, u32[]{:S(2)}) copy-start(s32[1,1,32,128]{3,2,1,0:T(8,128)} %refs_8_.1) | copy-start | bytes 49156
  5.6 38.3 %copy-start.1 = (f32[1,8,32,1024]{3,2,1,0:T(8,128)S(1)}, f32[1,8,32,1024]{3,2,1,0:T(8,128)}, u32[]{:S(2)}) copy-start(f32[1,8,32,1024]{3,2,1,0:T(8,128)} %x_ref.1) | copy-start | bytes 3145732
  9.6 34.3 %collective-permute-start = (bf16[80,1024]{1,0:T(8,128)(2,1)S(1)}, bf16[80,1024]{1,0:T(8,128)(2,1)S(1)}, u32[]{:S(2)}, u32[]{:S(2)}) collective-permute-start(bf16[80,1024]{1,0:T(8,128)(2,1)S(1)} %get-tuple-element.20), channel_id=1, source_target_pairs={{0,4},{4,0},{8,12},{12,8},{1,5},{5,1},{9,13},{13,9},{2,6},{6,2},{1... | collective-permute-start | bytes 491528 | tf_op jit(solution)/shard_map/ppermute | solution.py:630
  10.1 33.7 %collective-permute-start.1 = (bf16[80,1024]{1,0:T(8,128)(2,1)S(1)}, bf16[80,1024]{1,0:T(8,128)(2,1)S(1)}, u32[]{:S(2)}, u32[]{:S(2)}) collective-permute-start(bf16[80,1024]{1,0:T(8,128)(2,1)S(1)} %get-tuple-element.21), channel_id=1, source_target_pairs={{4,8},{8,4},{12,0},{0,12},{5,9},{9,5},{13,1},{1,13},{6,10},{10,6},... | collective-permute-start | bytes 491528 | tf_op jit(solution)/shard_map/ppermute | solution.py:631
  12.8 5.1 %collective-permute-start.4 = (bf16[64,128]{1,0:T(8,128)(2,1)S(1)}, bf16[64,128]{1,0:T(8,128)(2,1)S(1)}, u32[]{:S(2)}, u32[]{:S(2)}) collective-permute-start(bf16[64,128]{1,0:T(8,128)(2,1)S(1)} %get-tuple-element.27), channel_id=1, source_target_pairs={{0,16},{16,0},{1,17},{17,1},{2,18},{18,2},{3,19},{19,3},{4,20},{20... | collective-permute-start | bytes 49160 | tf_op jit(solution)/shard_map/ppermute | solution.py:610
  12.8 6.8 %collective-permute-start.5 = (bf16[64,128]{1,0:T(8,128)(2,1)S(1)}, bf16[64,128]{1,0:T(8,128)(2,1)S(1)}, u32[]{:S(2)}, u32[]{:S(2)}) collective-permute-start(bf16[64,128]{1,0:T(8,128)(2,1)S(1)} %get-tuple-element.27), channel_id=1, source_target_pairs={{0,17},{17,0},{1,16},{16,1},{2,19},{19,2},{3,18},{18,3},{4,21},{21... | collective-permute-start | bytes 49160 | tf_op jit(solution)/shard_map/ppermute | solution.py:610
  15.8 5.6 %collective-permute-start.6 = (bf16[64,128]{1,0:T(8,128)(2,1)S(1)}, bf16[64,128]{1,0:T(8,128)(2,1)S(1)}, u32[]{:S(2)}, u32[]{:S(2)}) collective-permute-start(bf16[64,128]{1,0:T(8,128)(2,1)S(1)} %get-tuple-element.27), channel_id=1, source_target_pairs={{0,18},{18,0},{1,19},{19,1},{2,16},{16,2},{3,17},{17,3},{4,22},{22... | collective-permute-start | bytes 49160 | tf_op jit(solution)/shard_map/ppermute | solution.py:610
  17.8 7.3 %collective-permute-start.7 = (bf16[64,128]{1,0:T(8,128)(2,1)S(1)}, bf16[64,128]{1,0:T(8,128)(2,1)S(1)}, u32[]{:S(2)}, u32[]{:S(2)}) collective-permute-start(bf16[64,128]{1,0:T(8,128)(2,1)S(1)} %get-tuple-element.27), channel_id=1, source_target_pairs={{0,19},{19,0},{1,18},{18,1},{2,17},{17,2},{3,16},{16,3},{4,23},{23... | collective-permute-start | bytes 49160 | tf_op jit(solution)/shard_map/ppermute | solution.py:610
  19.5 22.8 %collective-permute-start.2 = (bf16[32,1024]{1,0:T(8,128)(2,1)S(1)}, bf16[32,1024]{1,0:T(8,128)(2,1)S(1)}, u32[]{:S(2)}, u32[]{:S(2)}) collective-permute-start(bf16[32,1024]{1,0:T(8,128)(2,1)S(1)} %get-tuple-element.22), channel_id=1, source_target_pairs={{16,17},{17,16},{18,19},{19,18},{0,8},{8,0},{1,9},{9,1},{2,10},{10... | collective-permute-start | bytes 196616 | tf_op jit(solution)/shard_map/ppermute | solution.py:632
  21.4 20.9 %collective-permute-start.3 = (bf16[32,1024]{1,0:T(8,128)(2,1)S(1)}, bf16[32,1024]{1,0:T(8,128)(2,1)S(1)}, u32[]{:S(2)}, u32[]{:S(2)}) collective-permute-start(bf16[32,1024]{1,0:T(8,128)(2,1)S(1)} %get-tuple-element.23), channel_id=1, source_target_pairs={{17,18},{18,17},{1,2},{2,1},{19,16},{16,19},{3,0},{0,3},{21,22},{2... | collective-permute-start | bytes 196616 | tf_op jit(solution)/shard_map/ppermute | solution.py:633
  25.1 20.7 %copy-start.3 = (bf16[1024,1024]{1,0:T(8,128)(2,1)S(1)}, bf16[1024,1024]{1,0:T(8,128)(2,1)}, u32[]{:S(2)}) copy-start(bf16[1024,1024]{1,0:T(8,128)(2,1)} %constant.7.clone.table_ref) | copy-start | bytes 6291460
  25.2 0.9 %copy-start.10 = (s32[1,1,32,128]{3,2,1,0:T(8,128)S(1)}, s32[1,1,32,128]{3,2,1,0:T(8,128)}, u32[]{:S(2)}) copy-start(s32[1,1,32,128]{3,2,1,0:T(8,128)} %refs_9_.1) | copy-start | bytes 49156
  26.0 19.8 %copy-start.16 = (f32[128]{0:T(128)S(1)}, f32[128]{0:T(128)}, u32[]{:S(2)}) copy-start(f32[128]{0:T(128)} %param.19) | copy-start | bytes 1540
  28.3 3.8 %collective-permute-start.8 = (bf16[64,128]{1,0:T(8,128)(2,1)S(1)}, bf16[64,128]{1,0:T(8,128)(2,1)S(1)}, u32[]{:S(2)}, u32[]{:S(2)}) collective-permute-start(bf16[64,128]{1,0:T(8,128)(2,1)S(1)} %get-tuple-element.29), channel_id=1, source_target_pairs={{0,1},{1,0},{2,3},{3,2},{4,5},{5,4},{6,7},{7,6},{8,9},{9,8},{10,11... | collective-permute-start | bytes 49160 | tf_op jit(solution)/shard_map/ppermute | solution.py:656
  32.1 4.6 %collective-permute-start.9 = (bf16[64,128]{1,0:T(8,128)(2,1)S(1)}, bf16[64,128]{1,0:T(8,128)(2,1)S(1)}, u32[]{:S(2)}, u32[]{:S(2)}) collective-permute-start(bf16[64,128]{1,0:T(8,128)(2,1)S(1)} %get-tuple-element.29), channel_id=1, source_target_pairs={{0,2},{1,3},{2,0},{3,1},{4,6},{5,7},{6,4},{7,5},{8,10},{9,11},{10,... | collective-permute-start | bytes 49160 | tf_op jit(solution)/shard_map/ppermute | solution.py:656
  36.8 5.5 %collective-permute-start.10 = (bf16[64,128]{1,0:T(8,128)(2,1)S(1)}, bf16[64,128]{1,0:T(8,128)(2,1)S(1)}, u32[]{:S(2)}, u32[]{:S(2)}) collective-permute-start(bf16[64,128]{1,0:T(8,128)(2,1)S(1)} %get-tuple-element.29), channel_id=1, source_target_pairs={{0,3},{1,2},{2,1},{3,0},{4,7},{5,6},{6,5},{7,4},{8,11},{9,10},{10,... | collective-permute-start | bytes 49160 | tf_op jit(solution)/shard_map/ppermute | solution.py:656
  42.3 2.4 %collective-permute-start.11 = (bf16[128,128]{1,0:T(8,128)(2,1)S(1)}, bf16[128,128]{1,0:T(8,128)(2,1)S(1)}, u32[]{:S(2)}, u32[]{:S(2)}) collective-permute-start(bf16[128,128]{1,0:T(8,128)(2,1)S(1)} %get-tuple-element.31), channel_id=1, source_target_pairs={{0,4},{4,0},{8,12},{12,8},{1,5},{5,1},{9,13},{13,9},{2,6},{6,2},{1... | collective-permute-start | bytes 98312 | tf_op jit(solution)/shard_map/ppermute | solution.py:709
  42.4 3.4 %collective-permute-start.12 = (bf16[128,128]{1,0:T(8,128)(2,1)S(1)}, bf16[128,128]{1,0:T(8,128)(2,1)S(1)}, u32[]{:S(2)}, u32[]{:S(2)}) collective-permute-start(bf16[128,128]{1,0:T(8,128)(2,1)S(1)} %get-tuple-element.32), channel_id=1, source_target_pairs={{4,8},{8,4},{12,0},{0,12},{5,9},{9,5},{13,1},{1,13},{6,10},{10,6},... | collective-permute-start | bytes 98312 | tf_op jit(solution)/shard_map/ppermute | solution.py:710

commit v5 on v4

--- a/solution.py
+++ b/solution.py
@@ -18,18 +18,31 @@
 
 
 def fourier_tables(columns):
-    waves = np.arange(columns // 2)
-    phase = np.arange(columns)[:, None] * waves[None, :] % columns
-    angles = phase * (2.0 * np.pi / columns)
-    forward = np.concatenate([np.cos(angles), np.sin(angles)], axis=1)
-    weight = np.where(np.arange(columns) % (columns // 2) == 0, 1.0, 2.0) / columns
-    inverse = forward.T * weight[:, None]
-    half_rates = 2.0 * np.sin(np.pi * waves / columns) ** 2
+    half = columns // 2
+    forward, inverse, rates = [], [], []
+    for first in (0, 1):
+        waves = np.arange(first, half, 2)
+        phase = np.arange(half)[:, None] * waves[None, :] % columns
+        angles = phase * (2.0 * np.pi / columns)
+        table = np.concatenate([np.cos(angles), np.sin(angles)], axis=1)
+        weight = np.where(waves == 0, 1.0, 2.0) / columns
+        forward.append(table)
+        inverse.append(table.T * np.concatenate([weight, weight])[:, None])
+        rates.append(2.0 * np.sin(np.pi * waves / columns) ** 2)
     return (
-        jnp.asarray(forward.astype(np.float32), bf16),
-        jnp.asarray(inverse.astype(np.float32), bf16),
-        jnp.asarray(half_rates[None, :].astype(np.float32)),
+        jnp.asarray(np.stack(forward).astype(np.float32), bf16),
+        jnp.asarray(np.stack(inverse).astype(np.float32), bf16),
+        jnp.asarray(np.concatenate(rates)[None, :].astype(np.float32)),
     )
+
+
+def wave_parts(columns):
+    quarter = columns // 4
+    return [
+        (g * quarter + n, (g * 2 * quarter + n, (g * 2 + 1) * quarter + n))
+        for g in (0, 1)
+        for n in range(0, quarter, LANES)
+    ]
 
 
 def both_ways(pairs):
@@ -74,7 +87,7 @@
         edge_ref, x_sem, table_sem, small_sem,
     ) = refs[-12:]
     rows, channels, columns = x_ref.shape
-    waves = columns // 2
+    half = columns // 2
     row_group = lax.axis_index("gx")
     col_group = lax.axis_index("gy")
     is_atmos = lax.axis_index("comp") == 0
@@ -84,7 +97,6 @@
 
     @pl.when(is_atmos)
     def _():
-        step = 256
         small = [
             pltpu.make_async_copy(hbm, ref, small_sem.at[k])
             for k, (hbm, ref) in enumerate(
@@ -92,10 +104,8 @@
             )
         ]
         table = [
-            pltpu.make_async_copy(
-                table_hbm.at[:, pl.ds(n, step)], table_ref.at[:, pl.ds(n, step)], table_sem.at[k]
-            )
-            for k, n in enumerate(range(0, columns, step))
+            pltpu.make_async_copy(table_hbm.at[k], table_ref.at[k], table_sem.at[k])
+            for k in range(2)
         ]
         for copy in small + x_copies + table:
             copy.start()
@@ -106,23 +116,24 @@
         for r in range(rows):
             x_copies[r].wait()
             row_ref[r : r + 1, :] = jnp.sum(x_ref[r] * weight, axis=0, keepdims=True)
-            flat_ref[r * channels : (r + 1) * channels, :] = x_ref[r].astype(bf16)
+            left, right = x_ref[r, :, :half], x_ref[r, :, half:]
+            flat_ref[r * channels : (r + 1) * channels, :half] = (left + right).astype(bf16)
+            flat_ref[r * channels : (r + 1) * channels, half:] = (left - right).astype(bf16)
         s_ref[...] = to_tiles(row_ref[...]).astype(bf16)
-        for k, n in enumerate(range(0, columns, step)):
+        for k in range(2):
             table[k].wait()
-            part = jnp.dot(
-                flat_ref[...], table_ref[:, n : n + step], preferred_element_type=f32
-            )
-            y_ref[:, :, n : n + step] = part.reshape(rows, channels, step)
+            lanes = slice(k * half, (k + 1) * half)
+            part = jnp.dot(flat_ref[:, lanes], table_ref[k], preferred_element_type=f32)
+            y_ref[:, :, lanes] = part.reshape(rows, channels, half)
         diff = channel_column(diff_ref[...], channels, first)
         total = rows * groups_x
         base = (row_group * rows).astype(f32)
-        for n in range(0, waves, LANES):
+        for n, parts in wave_parts(columns):
             lam, alpha, _ = decay_terms(diff, rates_ref[:, n : n + LANES])
             lam2 = lam * lam
             low = jnp.exp(-2.0 * base * alpha)
             high = jnp.exp(-2.0 * (total - rows - base) * alpha)
-            for part in (n, n + waves):
+            for part in parts:
                 lanes = slice(part, part + LANES)
                 power = low
                 p = jnp.zeros((channels, LANES), f32)
@@ -199,8 +210,11 @@
     msgs = refs[:n_msgs]
     (
         a_src, a_dst, a_count, a_weight, m_src, m_dst, m_count, m_weight,
-        land_ref, sent_ref, weight_ref, gath_ref, val_ref, sem,
+        _, _, e2_in, e4_in,
+        land_ref, sent_ref, e2_ref, e4_ref, weight_ref, gath_ref, val_ref, sem,
     ) = refs[n_msgs:]
+    e2_ref[...] = e2_in[...]
+    e4_ref[...] = e4_in[...]
     is_atmos = lax.axis_index("comp") == 0
     blocks, points = val_ref.shape
     cells = msgs[0].shape[0]
@@ -310,7 +324,6 @@
         pin_ref, qin_ref = refs[:2]
     base_ref, zb_ref, c_ref, z_ref, t0_ref, t1_ref, w_ref = refs[-7:]
     _, rows, channels, columns = x_ref.shape
-    waves = columns // 2
     row_group = lax.axis_index("gx")
     col_group = lax.axis_index("gy")
     is_atmos = lax.axis_index("comp") == 0
@@ -320,7 +333,7 @@
         diff = channel_column(diff_ref[...], channels, col_group * channels)
         total = rows * groups_x
         base = (row_group * rows).astype(f32)
-        for n in range(0, waves, LANES):
+        for n, parts in wave_parts(columns):
             lam, alpha, sinh = decay_terms(diff, rates_ref[:, n : n + LANES])
             lam2 = lam * lam
             low = jnp.exp(-2.0 * base * alpha)
@@ -338,7 +351,7 @@
                 power = power * lam2
                 highs.append(1.0 - power)
             highs = highs[::-1]
-            for part in (n, n + waves):
+            for part in parts:
                 lanes = slice(part, part + LANES)
                 if paired:
                     pin = jnp.zeros((channels, LANES), f32)
@@ -475,15 +488,22 @@
     def _():
         response = channel_column(gain_ref[...], channels, col_group * channels)
         forcing = from_tiles(sum_ref[...], rows)
+        half = columns // 2
         step = 256
-        for n in range(0, columns, step):
-            part = jnp.dot(
-                zb_ref[...], table_ref[:, n : n + step], preferred_element_type=f32
-            ).reshape(rows, channels, step)
+        for n in range(0, half, step):
+            even, odd = [
+                jnp.dot(
+                    zb_ref[:, k * half : (k + 1) * half],
+                    table_ref[k, :, n : n + step],
+                    preferred_element_type=f32,
+                ).reshape(rows, channels, step)
+                for k in range(2)
+            ]
             for r in range(rows):
-                out_ref[0, r, :, n : n + step] = (
-                    part[r] + response * forcing[r : r + 1, n : n + step]
-                )
+                for lane, part in ((n, even[r] + odd[r]), (n + half, even[r] - odd[r])):
+                    out_ref[0, r, :, lane : lane + step] = (
+                        part + response * forcing[r : r + 1, lane : lane + step]
+                    )
 
     @pl.when(jnp.logical_not(is_atmos))
     def _():
@@ -564,6 +584,7 @@
     vmem = pl.BlockSpec(memory_space=pltpu.VMEM)
     smem = pl.BlockSpec(memory_space=pltpu.SMEM)
     anywhere = pl.BlockSpec(memory_space=pl.ANY)
+    hbm = pl.BlockSpec(memory_space=pltpu.HBM)
 
     def shape(dims, dtype):
         return jax.ShapeDtypeStruct(dims, dtype)
@@ -582,7 +603,7 @@
     partial_surface, y, e1, e3, e2, e4, *sums = pl.pallas_call(
         functools.partial(start_kernel, groups_x, paired),
         out_shape=shapes,
-        in_specs=[anywhere] * 6,
+        in_specs=[hbm] * 6,
         out_specs=[vmem] * len(shapes),
         scratch_shapes=[
             pltpu.VMEM((rows, channels, columns), f32),
@@ -590,12 +611,12 @@
             pltpu.VMEM(flux_row.shape, f32),
             pltpu.VMEM(diff_row.shape, f32),
             pltpu.VMEM(half_rates.shape, f32),
-            pltpu.VMEM((columns, columns), bf16),
+            pltpu.VMEM(forward.shape, bf16),
             pltpu.VMEM((rows * channels, columns), bf16),
             pltpu.VMEM((rows, columns), f32),
             pltpu.VMEM((4 * rows, columns), f32),
             pltpu.SemaphoreType.DMA((rows,)),
-            pltpu.SemaphoreType.DMA((columns // 256,)),
+            pltpu.SemaphoreType.DMA((2,)),
             pltpu.SemaphoreType.DMA((3,)),
         ],
         compiler_params=params(),
@@ -626,18 +647,21 @@
                 pairs += [(flat(0, i, j), flat(0, i ^ 2, j)) for j in range(groups_y)]
         return both_ways(pairs)
 
-    axes = ("comp", "gx", "gy")
     e1 = lax.ppermute(e1, "gx", both_ways(ring_pairs(groups_x, 0)))
     e3 = lax.ppermute(e3, "gx", both_ways(ring_pairs(groups_x, 1)))
-    e2 = lax.ppermute(e2, axes, level_route(0))
-    e4 = lax.ppermute(e4, axes, level_route(1))
-
-    landing, sent = pl.pallas_call(
+
+    landing, sent, e2, e4 = pl.pallas_call(
         functools.partial(regrid_kernel, groups_y),
-        out_shape=[shape((cells, LANES), f32), shape((cells, LANES), bf16)],
+        out_shape=[
+            shape((cells, LANES), f32),
+            shape((cells, LANES), bf16),
+            shape(e2.shape, bf16),
+            shape(e4.shape, bf16),
+        ],
         in_specs=[vmem] * groups_y
-        + [vmem, vmem, smem, anywhere, vmem, vmem, smem, anywhere],
-        out_specs=[vmem] * 2,
+        + [vmem, vmem, smem, hbm, vmem, vmem, smem, hbm]
+        + [anywhere, anywhere, vmem, vmem],
+        out_specs=[vmem] * 4,
         scratch_shapes=[
             pltpu.VMEM((blocks, points, points), bf16),
             pltpu.VMEM((blocks, points), f32),
@@ -650,12 +674,16 @@
         *surfaces,
         a2o_source, a2o_target, a2o_count, a2o_weight,
         marine_air_input_index, marine_air_output_index,
-        marine_air_piece_tally, marine_air_piece_factor,
+        marine_air_piece_tally, marine_air_piece_factor, e1, e3, e2, e4,
     )
     parts = [
         lax.ppermute(sent, "gy", [(j, j ^ mask) for j in range(groups_y)])
         for mask in range(1, groups_y)
     ]
+
+    axes = ("comp", "gx", "gy")
+    e2 = lax.ppermute(e2, axes, level_route(0))
+    e4 = lax.ppermute(e4, axes, level_route(1))
 
     extra = []
     if not paired:

time: 47.8 us -> 41.4 us (0.87)
  waiting for transfers between devices: 13.1 us -> 8.2 us
  Pallas kernels: 8.8 us -> 7.26 us
  local copies, waits for them, and re-layouts: 6.48 us -> 5.28 us
  starting transfers between devices: 17.7 us -> 18.8 us
    ppermute x3, waiting for transfers between devices: 10.7 us -> 3.79 us  [local(): lax.ppermute(sent, 'gy', [(j, j ^ mask) for j in range(groups_y)])]
    ppermute x4, waiting for transfers between devices: 1.33 us -> 3.42 us  [local(): surfaces.append(lax.ppermute(partial_surface, ('comp', 'gy'), route))]
    pallas_call x1, Pallas kernels: 3.98 us -> 2.72 us  [local(): pl.pallas_call(functools.partial(start_kernel, groups_x, paired), out_sha...]
    unnamed x34 -> x30, local copies, waits for them, and re-layouts: 6.48 us -> 5.28 us
    ppermute x3, starting transfers between devices: 3.3 us -> 4.39 us  [local(): lax.ppermute(sent, 'gy', [(j, j ^ mask) for j in range(groups_y)])]
    ppermute x1, starting transfers between devices: 2.41 us -> 1.75 us  [local(): e4 = lax.ppermute(e4, axes, level_route(1))]
    ppermute x4, starting transfers between devices: 6.78 us -> 7.3 us  [local(): surfaces.append(lax.ppermute(partial_surface, ('comp', 'gy'), route))]
  transfers between devices with their start and end apart: 13 -> 13, of which waited for: 5 -> 5; matrix products, arithmetic and copies ran while one was open for 0% -> 0% of each run, Pallas kernels for 7% -> 2%
where the time goes in v5:
time: 41.4 us; the launch traced here: 41 us
  starting transfers between devices  18.8 us (45%)
  waiting for transfers between devices  8.2 us (20%)
  Pallas kernels  7.26 us (18%)
  local copies, waits for them, and re-layouts  5.28 us (13%)
  between operations  1.43 us (3%)
    ppermute x4, starting transfers between devices, local(): surfaces.append(lax.ppermute(partial_surface, ('comp', 'gy'), route))  7.3 us
    unnamed x30, local copies, waits for them, and re-layouts  5.28 us
    ppermute x3, starting transfers between devices, local(): lax.ppermute(sent, 'gy', [(j, j ^ mask) for j in range(groups_y)])  4.39 us
    ppermute x3, waiting for transfers between devices, local(): lax.ppermute(sent, 'gy', [(j, j ^ mask) for j in range(groups_y)])  3.79 us
    ppermute x4, waiting for transfers between devices, local(): surfaces.append(lax.ppermute(partial_surface, ('comp', 'gy'), route))  3.42 us
    pallas_call x1, Pallas kernels, local(): pl.pallas_call(functools.partial(start_kernel, groups_x, paired), out_sha...  2.72 us
    ppermute x1, starting transfers between devices, local(): e3 = lax.ppermute(e3, 'gx', both_ways(ring_pairs(groups_x, 1)))  2.61 us
    pallas_call x1, Pallas kernels, local(): pl.pallas_call(functools.partial(regrid_kernel, groups_y), out_shape=[sha...  2.27 us
  transfers between devices with their start and end apart: 13, of which 5 were waited for; matrix products, arithmetic and copies ran while one was open for 0% of the time, Pallas kernels for 2%

profile of v5, /device:TPU:0, one launch (start us, length us, event | category | flops | bytes accessed | tf_op | source)
XLA Modules:
  0.0 41.0 jit_solution(908282540837532852)
XLA Ops:
  0.0 0.0 copy-start.11
  0.0 0.0 copy-start.12
  0.0 0.0 copy-start.13
  0.0 0.7 %copy-done.11 = f32[1,512]{1,0:T(1,128)S(1)} copy-done((f32[1,512]{1,0:T(1,128)S(1)}, f32[1,512]{1,0:T(1,128)}, u32[]{:S(2)}) %copy-start.11) | copy-done | bytes 2072
  0.7 0.0 copy-done.12
  0.7 0.0 copy-done.13
  0.7 0.0 copy-start
  0.7 1.2 %copy-done = f32[1,8,32,1024]{3,2,1,0:T(8,128)S(1)} copy-done((f32[1,8,32,1024]{3,2,1,0:T(8,128)S(1)}, f32[1,8,32,1024]{3,2,1,0:T(8,128)}, u32[]{:S(2)}) %copy-start) | copy-done | bytes 1048600
  1.9 0.0 copy-start.5
  1.9 1.2 %copy-done.5 = bf16[2,512,512]{2,1,0:T(8,128)(2,1)S(1)} copy-done((bf16[2,512,512]{2,1,0:T(8,128)(2,1)S(1)}, bf16[2,512,512]{2,1,0:T(8,128)(2,1)}, u32[]{:S(2)}) %copy-start.5) | copy-done | bytes 1048600
  3.1 0.0 copy-start.6
  3.1 0.8 %copy-done.6 = s32[8,1024]{1,0:T(8,128)S(1)} copy-done((s32[8,1024]{1,0:T(8,128)S(1)}, s32[8,1024]{1,0:T(8,128)}, u32[]{:S(2)}) %copy-start.6) | copy-done | bytes 32792
  3.9 0.0 copy-start.2
  3.9 0.0 copy-start.3
  3.9 0.0 copy-start.7
  3.9 0.0 copy-start.8
  3.9 0.0 copy-start.9
  3.9 2.7 %surface_and_forward_or_halos.1 = (bf16[64,128]{1,0:T(8,128)(2,1)S(1)}, f32[8,32,1024]{2,1,0:T(8,128)S(1)}, bf16[80,1024]{1,0:T(8,128)(2,1)S(1)}, bf16[80,1024]{...) custom-call(f32[1,8,32,1024]{3,2,1,0:T(8,128)S(1)} %copy-done, ...), custom_call_target="tpu_custom_call" | custom-call | tf_op jit(solution)/shard_map/surface_and_forward_or_halos/pallas_call | solution.py:603
  6.6 0.5 %collective-permute-start = (bf16[80,1024]{1,0:T(8,128)(2,1)S(1)}, bf16[80,1024]{1,0:T(8,128)(2,1)S(1)}, u32[]{:S(2)}, u32[]{:S(2)}) collective-permute-start(bf16[80,1024]{1,0:T(8,128)(2,1)S(1)} %get-tuple-element.22), channel_id=1, source_target_pairs={{0,4},{4,0},{8,12},{12,8},{1,5},{5,1},{9,13},{13,9},{2,6},{6,2},{1... | collective-permute-start | bytes 491528 | tf_op jit(solution)/shard_map/ppermute | solution.py:650
  7.2 2.6 %collective-permute-start.1 = (bf16[80,1024]{1,0:T(8,128)(2,1)S(1)}, bf16[80,1024]{1,0:T(8,128)(2,1)S(1)}, u32[]{:S(2)}, u32[]{:S(2)}) collective-permute-start(bf16[80,1024]{1,0:T(8,128)(2,1)S(1)} %get-tuple-element.23), channel_id=1, source_target_pairs={{4,8},{8,4},{12,0},{0,12},{5,9},{9,5},{13,1},{1,13},{6,10},{10,6},... | collective-permute-start | bytes 491528 | tf_op jit(solution)/shard_map/ppermute | solution.py:651
  9.8 0.5 %collective-permute-start.2 = (bf16[64,128]{1,0:T(8,128)(2,1)S(1)}, bf16[64,128]{1,0:T(8,128)(2,1)S(1)}, u32[]{:S(2)}, u32[]{:S(2)}) collective-permute-start(bf16[64,128]{1,0:T(8,128)(2,1)S(1)} %get-tuple-element.24), channel_id=1, source_target_pairs={{0,16},{16,0},{1,17},{17,1},{2,18},{18,2},{3,19},{19,3},{4,20},{20... | collective-permute-start | bytes 49160 | tf_op jit(solution)/shard_map/ppermute | solution.py:631
  10.3 2.5 %collective-permute-start.3 = (bf16[64,128]{1,0:T(8,128)(2,1)S(1)}, bf16[64,128]{1,0:T(8,128)(2,1)S(1)}, u32[]{:S(2)}, u32[]{:S(2)}) collective-permute-start(bf16[64,128]{1,0:T(8,128)(2,1)S(1)} %get-tuple-element.24), channel_id=1, source_target_pairs={{0,17},{17,0},{1,16},{16,1},{2,19},{19,2},{3,18},{18,3},{4,21},{21... | collective-permute-start | bytes 49160 | tf_op jit(solution)/shard_map/ppermute | solution.py:631
  12.8 2.5 %collective-permute-start.4 = (bf16[64,128]{1,0:T(8,128)(2,1)S(1)}, bf16[64,128]{1,0:T(8,128)(2,1)S(1)}, u32[]{:S(2)}, u32[]{:S(2)}) collective-permute-start(bf16[64,128]{1,0:T(8,128)(2,1)S(1)} %get-tuple-element.24), channel_id=1, source_target_pairs={{0,18},{18,0},{1,19},{19,1},{2,16},{16,2},{3,17},{17,3},{4,22},{22... | collective-permute-start | bytes 49160 | tf_op jit(solution)/shard_map/ppermute | solution.py:631
  15.4 0.0 collective-permute-done.2.refs_0_
  15.4 1.7 %collective-permute-start.5 = (bf16[64,128]{1,0:T(8,128)(2,1)S(1)}, bf16[64,128]{1,0:T(8,128)(2,1)S(1)}, u32[]{:S(2)}, u32[]{:S(2)}) collective-permute-start(bf16[64,128]{1,0:T(8,128)(2,1)S(1)} %get-tuple-element.24), channel_id=1, source_target_pairs={{0,19},{19,0},{1,18},{18,1},{2,17},{17,2},{3,16},{16,3},{4,23},{23... | collective-permute-start | bytes 49160 | tf_op jit(solution)/shard_map/ppermute | solution.py:631
  18.4 0.0 collective-permute-done.3.refs_1_
  18.4 0.1 collective-permute-done.4.refs_2_
  18.5 3.3 %collective-permute-done.5.refs_3_ = bf16[64,128]{1,0:T(8,128)(2,1)S(1)} collective-permute-done((bf16[64,128]{1,0:T(8,128)(2,1)S(1)}, bf16[64,128]{1,0:T(8,128)(2,1)S(1)}, u32[]{:S(2)}, u32[]{:S(2)}) %collective-permute-start.5) | collective-permute-done | bytes 16416 | tf_op jit(solution)/shard_map/ppermute | solution.py:631
  21.8 0.0 collective-permute-done.refs_12_.e1_ref
  21.8 0.0 collective-permute-done.1.refs_13_.e3_ref
  21.8 0.0 copy-done.2
  21.8 0.0 copy-done.3
  21.8 0.0 copy-done.7
  21.8 0.0 copy-done.8
  21.9 0.0 copy-done.9
  21.9 0.0 copy-start.10
  21.9 0.7 %copy-done.10 = s32[1,1,32,128]{3,2,1,0:T(8,128)S(1)} copy-done((s32[1,1,32,128]{3,2,1,0:T(8,128)S(1)}, s32[1,1,32,128]{3,2,1,0:T(8,128)}, u32[]{:S(2)}) %copy-start.10) | copy-done | bytes 16408
  22.6 0.0 copy-start.1
  22.6 2.3 %regrid_blocks.1 = (f32[64,128]{1,0:T(8,128)S(1)}, bf16[64,128]{1,0:T(8,128)(2,1)S(1)}, bf16[32,1024]{1,0:T(8,128)(2,1)S(1)}, bf16[32,1024]{1,0:T(8,128)(2,1)S(1)}) custom-call(bf16[64,128]{1,0:T(8,128)(2,1)S(1)} %collective-permute-done.2.refs_0_, bf16[64,128]{1,0:T(8,128)(2,1)S(1)} %collective-permute-done.3.refs_1_, ...), custom_call_target="tpu_custom_call" | custom-call | tf_op jit(solution)/shard_map/regrid_blocks/pallas_call | solution.py:653
  24.9 0.6 %collective-permute-start.6 = (bf16[32,1024]{1,0:T(8,128)(2,1)S(1)}, bf16[32,1024]{1,0:T(8,128)(2,1)S(1)}, u32[]{:S(2)}, u32[]{:S(2)}) collective-permute-start(bf16[32,1024]{1,0:T(8,128)(2,1)S(1)} %get-tuple-element.27), channel_id=1, source_target_pairs={{16,17},{17,16},{18,19},{19,18},{0,8},{8,0},{1,9},{9,1},{2,10},{10... | collective-permute-start | bytes 196616 | tf_op jit(solution)/shard_map/ppermute | solution.py:685
  25.5 1.7 %collective-permute-start.7 = (bf16[32,1024]{1,0:T(8,128)(2,1)S(1)}, bf16[32,1024]{1,0:T(8,128)(2,1)S(1)}, u32[]{:S(2)}, u32[]{:S(2)}) collective-permute-start(bf16[32,1024]{1,0:T(8,128)(2,1)S(1)} %get-tuple-element.28), channel_id=1, source_target_pairs={{17,18},{18,17},{1,2},{2,1},{19,16},{16,19},{3,0},{0,3},{21,22},{2... | collective-permute-start | bytes 196616 | tf_op jit(solution)/shard_map/ppermute | solution.py:686
  27.2 0.0 collective-permute-start.8
  27.2 2.6 %collective-permute-start.9 = (bf16[64,128]{1,0:T(8,128)(2,1)S(1)}, bf16[64,128]{1,0:T(8,128)(2,1)S(1)}, u32[]{:S(2)}, u32[]{:S(2)}) collective-permute-start(bf16[64,128]{1,0:T(8,128)(2,1)S(1)} %get-tuple-element.33), channel_id=1, source_target_pairs={{0,2},{1,3},{2,0},{3,1},{4,6},{5,7},{6,4},{7,5},{8,10},{9,11},{10,... | collective-permute-start | bytes 49160 | tf_op jit(solution)/shard_map/ppermute | solution.py:680
  29.9 1.7 %collective-permute-start.10 = (bf16[64,128]{1,0:T(8,128)(2,1)S(1)}, bf16[64,128]{1,0:T(8,128)(2,1)S(1)}, u32[]{:S(2)}, u32[]{:S(2)}) collective-permute-start(bf16[64,128]{1,0:T(8,128)(2,1)S(1)} %get-tuple-element.33), channel_id=1, source_target_pairs={{0,3},{1,2},{2,1},{3,0},{4,7},{5,6},{6,5},{7,4},{8,11},{9,10},{10,... | collective-permute-start | bytes 49160 | tf_op jit(solution)/shard_map/ppermute | solution.py:680
  31.6 0.4 collective-permute-done.8.refs_0_
  32.0 0.0 collective-permute-done.9.refs_1_
  32.0 3.4 %collective-permute-done.10.refs_2_ = bf16[64,128]{1,0:T(8,128)(2,1)S(1)} collective-permute-done((bf16[64,128]{1,0:T(8,128)(2,1)S(1)}, bf16[64,128]{1,0:T(8,128)(2,1)S(1)}, u32[]{:S(2)}, u32[]{:S(2)}) %collective-permute-start.10) | collective-permute-done | bytes 16416 | tf_op jit(solution)/shard_map/ppermute | solution.py:680
  35.4 0.0 collective-permute-done.6.e2_ref
  35.4 0.0 collective-permute-done.7.e4_ref
  35.5 0.1 collective-permute-start.11
  35.5 1.6 %collective-permute-start.12 = (bf16[128,128]{1,0:T(8,128)(2,1)S(1)}, bf16[128,128]{1,0:T(8,128)(2,1)S(1)}, u32[]{:S(2)}, u32[]{:S(2)}) collective-permute-start(bf16[128,128]{1,0:T(8,128)(2,1)S(1)} %get-tuple-element.36), channel_id=1, source_target_pairs={{4,8},{8,4},{12,0},{0,12},{5,9},{9,5},{13,1},{1,13},{6,10},{10,6},... | collective-permute-start | bytes 98312 | tf_op jit(solution)/shard_map/ppermute | solution.py:738
  37.1 0.0 copy-done.1
  37.1 0.0 copy-start.4
  37.1 0.8 %damping_or_ocean_steps.1 = (f32[8,32,1024]{2,1,0:T(8,128)S(1)}, bf16[256,1024]{1,0:T(8,128)(2,1)S(1)}, f32[7,16,1024]{2,1,0:T(8,128)S(1)}) custom-call(f32[1,8,32,1024]{3,2,1,0:T(8,128)S(1)} %copy-done.1, s32[8,1024]{1,0:T(8,128)S(1)} %copy-done.6, f32[1,128]{1,0:T(1,128)S(1)} %bitcast.4, f32[1,512]{1,0:T(1,128)S(1)} %copy-done.11, ...), custom_call_target="tpu_custom_call" | custom-call | tf_op jit(solution)/shard_map/damping_or_ocean_steps/pallas_call | solution.py:705
  37.9 0.0 collective-permute-done.11.near_ref
  38.0 1.0 %collective-permute-done.12.far_ref = bf16[128,128]{1,0:T(8,128)(2,1)S(1)} collective-permute-done((bf16[128,128]{1,0:T(8,128)(2,1)S(1)}, bf16[128,128]{1,0:T(8,128)(2,1)S(1)}, u32[]{:S(2)}, u32[]{:S(2)}) %collective-permute-start.12) | collective-permute-done | bytes 32800 | tf_op jit(solution)/shard_map/ppermute | solution.py:738
  38.9 0.0 copy-start.14
  38.9 0.0 copy-done.4
  38.9 0.7 %copy-done.14 = f32[128]{0:T(128)S(1)} copy-done((f32[128]{0:T(128)S(1)}, f32[128]{0:T(128)}, u32[]{:S(2)}) %copy-start.14) | copy-done | bytes 536
  39.6 1.4 %inverse_or_heat.1 = f32[1,8,32,1024]{3,2,1,0:T(8,128)} custom-call(f32[1,128]{1,0:T(1,128)S(1)} %bitcast.6, bf16[2,512,512]{2,1,0:T(8,128)(2,1)S(1)} %copy-done.4, f32[8,32,1024]{2,1,0:T(8,128)S(1)} %get-tuple-element.29.base_ref, bf16[256,1024]{1,0:T(8,128)(2,1)S(1)} %get-tuple-element.30.zb_ref, f32[7,16,1024]{2,1,0:T(8,128)S(1)} %get-tuple-element.31.c_ref, ...), custom_call_target="tpu_custom_call" | custom-call | tf_op jit(solution)/shard_map/inverse_or_heat/pallas_call | solution.py:739
  (1 shorter events, 0.0 us)
Async XLA Ops:
  0.0 0.7 %copy-start.11 = (f32[1,512]{1,0:T(1,128)S(1)}, f32[1,512]{1,0:T(1,128)}, u32[]{:S(2)}) copy-start(f32[1,512]{1,0:T(1,128)} %constant.8.clone.rates_hbm.rates_ref) | copy-start | bytes 6148
  0.0 0.7 %copy-start.12 = (f32[128]{0:T(128)S(1)}, f32[128]{0:T(128)}, u32[]{:S(2)}) copy-start(f32[128]{0:T(128)} %param.20) | copy-start | bytes 1540
  0.0 0.7 %copy-start.13 = (f32[128]{0:T(128)S(1)}, f32[128]{0:T(128)}, u32[]{:S(2)}) copy-start(f32[128]{0:T(128)} %param.18) | copy-start | bytes 1540
  0.7 1.2 %copy-start = (f32[1,8,32,1024]{3,2,1,0:T(8,128)S(1)}, f32[1,8,32,1024]{3,2,1,0:T(8,128)}, u32[]{:S(2)}) copy-start(f32[1,8,32,1024]{3,2,1,0:T(8,128)} %x_ref.1) | copy-start | bytes 3145732
  1.9 1.2 %copy-start.5 = (bf16[2,512,512]{2,1,0:T(8,128)(2,1)S(1)}, bf16[2,512,512]{2,1,0:T(8,128)(2,1)}, u32[]{:S(2)}) copy-start(bf16[2,512,512]{2,1,0:T(8,128)(2,1)} %constant.6.clone.table_hbm) | copy-start | bytes 3145732
  3.1 0.8 %copy-start.6 = (s32[8,1024]{1,0:T(8,128)S(1)}, s32[8,1024]{1,0:T(8,128)}, u32[]{:S(2)}) copy-start(s32[8,1024]{1,0:T(8,128)} %wet_ref.1) | copy-start | bytes 98308
  3.9 17.9 %copy-start.2 = (bf16[1,1,32,128,128]{4,3,2,1,0:T(8,128)(2,1)S(1)}, bf16[1,1,32,128,128]{4,3,2,1,0:T(8,128)(2,1)}, u32[]{:S(2)}) copy-start(bf16[1,1,32,128,128]{4,3,2,1,0:T(8,128)(2,1)} %refs_7_.1) | copy-start | bytes 3145732
  3.9 17.9 %copy-start.3 = (bf16[1,1,32,128,128]{4,3,2,1,0:T(8,128)(2,1)S(1)}, bf16[1,1,32,128,128]{4,3,2,1,0:T(8,128)(2,1)}, u32[]{:S(2)}) copy-start(bf16[1,1,32,128,128]{4,3,2,1,0:T(8,128)(2,1)} %refs_11_.1) | copy-start | bytes 3145732
  3.9 17.9 %copy-start.7 = (s32[1,1,32,128]{3,2,1,0:T(8,128)S(1)}, s32[1,1,32,128]{3,2,1,0:T(8,128)}, u32[]{:S(2)}) copy-start(s32[1,1,32,128]{3,2,1,0:T(8,128)} %refs_4_.1) | copy-start | bytes 49156
  3.9 17.9 %copy-start.8 = (s32[1,1,32,128]{3,2,1,0:T(8,128)S(1)}, s32[1,1,32,128]{3,2,1,0:T(8,128)}, u32[]{:S(2)}) copy-start(s32[1,1,32,128]{3,2,1,0:T(8,128)} %refs_5_.1) | copy-start | bytes 49156
  3.9 17.9 %copy-start.9 = (s32[1,1,32,128]{3,2,1,0:T(8,128)S(1)}, s32[1,1,32,128]{3,2,1,0:T(8,128)}, u32[]{:S(2)}) copy-start(s32[1,1,32,128]{3,2,1,0:T(8,128)} %refs_8_.1) | copy-start | bytes 49156
  6.6 15.2 %collective-permute-start = (bf16[80,1024]{1,0:T(8,128)(2,1)S(1)}, bf16[80,1024]{1,0:T(8,128)(2,1)S(1)}, u32[]{:S(2)}, u32[]{:S(2)}) collective-permute-start(bf16[80,1024]{1,0:T(8,128)(2,1)S(1)} %get-tuple-element.22), channel_id=1, source_target_pairs={{0,4},{4,0},{8,12},{12,8},{1,5},{5,1},{9,13},{13,9},{2,6},{6,2},{1... | collective-permute-start | bytes 491528 | tf_op jit(solution)/shard_map/ppermute | solution.py:650
  7.2 14.7 %collective-permute-start.1 = (bf16[80,1024]{1,0:T(8,128)(2,1)S(1)}, bf16[80,1024]{1,0:T(8,128)(2,1)S(1)}, u32[]{:S(2)}, u32[]{:S(2)}) collective-permute-start(bf16[80,1024]{1,0:T(8,128)(2,1)S(1)} %get-tuple-element.23), channel_id=1, source_target_pairs={{4,8},{8,4},{12,0},{0,12},{5,9},{9,5},{13,1},{1,13},{6,10},{10,6},... | collective-permute-start | bytes 491528 | tf_op jit(solution)/shard_map/ppermute | solution.py:651
  9.8 5.6 %collective-permute-start.2 = (bf16[64,128]{1,0:T(8,128)(2,1)S(1)}, bf16[64,128]{1,0:T(8,128)(2,1)S(1)}, u32[]{:S(2)}, u32[]{:S(2)}) collective-permute-start(bf16[64,128]{1,0:T(8,128)(2,1)S(1)} %get-tuple-element.24), channel_id=1, source_target_pairs={{0,16},{16,0},{1,17},{17,1},{2,18},{18,2},{3,19},{19,3},{4,20},{20... | collective-permute-start | bytes 49160 | tf_op jit(solution)/shard_map/ppermute | solution.py:631
  10.3 8.1 %collective-permute-start.3 = (bf16[64,128]{1,0:T(8,128)(2,1)S(1)}, bf16[64,128]{1,0:T(8,128)(2,1)S(1)}, u32[]{:S(2)}, u32[]{:S(2)}) collective-permute-start(bf16[64,128]{1,0:T(8,128)(2,1)S(1)} %get-tuple-element.24), channel_id=1, source_target_pairs={{0,17},{17,0},{1,16},{16,1},{2,19},{19,2},{3,18},{18,3},{4,21},{21... | collective-permute-start | bytes 49160 | tf_op jit(solution)/shard_map/ppermute | solution.py:631
  12.8 5.7 %collective-permute-start.4 = (bf16[64,128]{1,0:T(8,128)(2,1)S(1)}, bf16[64,128]{1,0:T(8,128)(2,1)S(1)}, u32[]{:S(2)}, u32[]{:S(2)}) collective-permute-start(bf16[64,128]{1,0:T(8,128)(2,1)S(1)} %get-tuple-element.24), channel_id=1, source_target_pairs={{0,18},{18,0},{1,19},{19,1},{2,16},{16,2},{3,17},{17,3},{4,22},{22... | collective-permute-start | bytes 49160 | tf_op jit(solution)/shard_map/ppermute | solution.py:631
  15.4 6.4 %collective-permute-start.5 = (bf16[64,128]{1,0:T(8,128)(2,1)S(1)}, bf16[64,128]{1,0:T(8,128)(2,1)S(1)}, u32[]{:S(2)}, u32[]{:S(2)}) collective-permute-start(bf16[64,128]{1,0:T(8,128)(2,1)S(1)} %get-tuple-element.24), channel_id=1, source_target_pairs={{0,19},{19,0},{1,18},{18,1},{2,17},{17,2},{3,16},{16,3},{4,23},{23... | collective-permute-start | bytes 49160 | tf_op jit(solution)/shard_map/ppermute | solution.py:631
  21.9 0.7 %copy-start.10 = (s32[1,1,32,128]{3,2,1,0:T(8,128)S(1)}, s32[1,1,32,128]{3,2,1,0:T(8,128)}, u32[]{:S(2)}) copy-start(s32[1,1,32,128]{3,2,1,0:T(8,128)} %refs_9_.1) | copy-start | bytes 49156
  22.6 14.6 %copy-start.1 = (f32[1,8,32,1024]{3,2,1,0:T(8,128)S(1)}, f32[1,8,32,1024]{3,2,1,0:T(8,128)}, u32[]{:S(2)}) copy-start(f32[1,8,32,1024]{3,2,1,0:T(8,128)} %x_ref.1) | copy-start | bytes 3145732
  24.9 10.5 %collective-permute-start.6 = (bf16[32,1024]{1,0:T(8,128)(2,1)S(1)}, bf16[32,1024]{1,0:T(8,128)(2,1)S(1)}, u32[]{:S(2)}, u32[]{:S(2)}) collective-permute-start(bf16[32,1024]{1,0:T(8,128)(2,1)S(1)} %get-tuple-element.27), channel_id=1, source_target_pairs={{16,17},{17,16},{18,19},{19,18},{0,8},{8,0},{1,9},{9,1},{2,10},{10... | collective-permute-start | bytes 196616 | tf_op jit(solution)/shard_map/ppermute | solution.py:685
  25.5 9.9 %collective-permute-start.7 = (bf16[32,1024]{1,0:T(8,128)(2,1)S(1)}, bf16[32,1024]{1,0:T(8,128)(2,1)S(1)}, u32[]{:S(2)}, u32[]{:S(2)}) collective-permute-start(bf16[32,1024]{1,0:T(8,128)(2,1)S(1)} %get-tuple-element.28), channel_id=1, source_target_pairs={{17,18},{18,17},{1,2},{2,1},{19,16},{16,19},{3,0},{0,3},{21,22},{2... | collective-permute-start | bytes 196616 | tf_op jit(solution)/shard_map/ppermute | solution.py:686
  27.2 4.8 %collective-permute-start.8 = (bf16[64,128]{1,0:T(8,128)(2,1)S(1)}, bf16[64,128]{1,0:T(8,128)(2,1)S(1)}, u32[]{:S(2)}, u32[]{:S(2)}) collective-permute-start(bf16[64,128]{1,0:T(8,128)(2,1)S(1)} %get-tuple-element.33), channel_id=1, source_target_pairs={{0,1},{1,0},{2,3},{3,2},{4,5},{5,4},{6,7},{7,6},{8,9},{9,8},{10,11... | collective-permute-start | bytes 49160 | tf_op jit(solution)/shard_map/ppermute | solution.py:680
  27.2 4.8 %collective-permute-start.9 = (bf16[64,128]{1,0:T(8,128)(2,1)S(1)}, bf16[64,128]{1,0:T(8,128)(2,1)S(1)}, u32[]{:S(2)}, u32[]{:S(2)}) collective-permute-start(bf16[64,128]{1,0:T(8,128)(2,1)S(1)} %get-tuple-element.33), channel_id=1, source_target_pairs={{0,2},{1,3},{2,0},{3,1},{4,6},{5,7},{6,4},{7,5},{8,10},{9,11},{10,... | collective-permute-start | bytes 49160 | tf_op jit(solution)/shard_map/ppermute | solution.py:680
  29.9 5.5 %collective-permute-start.10 = (bf16[64,128]{1,0:T(8,128)(2,1)S(1)}, bf16[64,128]{1,0:T(8,128)(2,1)S(1)}, u32[]{:S(2)}, u32[]{:S(2)}) collective-permute-start(bf16[64,128]{1,0:T(8,128)(2,1)S(1)} %get-tuple-element.33), channel_id=1, source_target_pairs={{0,3},{1,2},{2,1},{3,0},{4,7},{5,6},{6,5},{7,4},{8,11},{9,10},{10,... | collective-permute-start | bytes 49160 | tf_op jit(solution)/shard_map/ppermute | solution.py:680
  35.5 2.5 %collective-permute-start.11 = (bf16[128,128]{1,0:T(8,128)(2,1)S(1)}, bf16[128,128]{1,0:T(8,128)(2,1)S(1)}, u32[]{:S(2)}, u32[]{:S(2)}) collective-permute-start(bf16[128,128]{1,0:T(8,128)(2,1)S(1)} %get-tuple-element.35), channel_id=1, source_target_pairs={{0,4},{4,0},{8,12},{12,8},{1,5},{5,1},{9,13},{13,9},{2,6},{6,2},{1... | collective-permute-start | bytes 98312 | tf_op jit(solution)/shard_map/ppermute | solution.py:737
  35.5 3.4 %collective-permute-start.12 = (bf16[128,128]{1,0:T(8,128)(2,1)S(1)}, bf16[128,128]{1,0:T(8,128)(2,1)S(1)}, u32[]{:S(2)}, u32[]{:S(2)}) collective-permute-start(bf16[128,128]{1,0:T(8,128)(2,1)S(1)} %get-tuple-element.36), channel_id=1, source_target_pairs={{4,8},{8,4},{12,0},{0,12},{5,9},{9,5},{13,1},{1,13},{6,10},{10,6},... | collective-permute-start | bytes 98312 | tf_op jit(solution)/shard_map/ppermute | solution.py:738
  37.1 1.8 %copy-start.4 = (bf16[2,512,512]{2,1,0:T(8,128)(2,1)S(1)}, bf16[2,512,512]{2,1,0:T(8,128)(2,1)}, u32[]{:S(2)}) copy-start(bf16[2,512,512]{2,1,0:T(8,128)(2,1)} %constant.7.clone.table_ref) | copy-start | bytes 3145732
  38.9 0.7 %copy-start.14 = (f32[128]{0:T(128)S(1)}, f32[128]{0:T(128)}, u32[]{:S(2)}) copy-start(f32[128]{0:T(128)} %param.19) | copy-start | bytes 1540

commit v6 on v5

--- a/solution.py
+++ b/solution.py
@@ -19,7 +19,7 @@
 
 def fourier_tables(columns):
     half = columns // 2
-    forward, inverse, rates = [], [], []
+    forward, inverse = [], []
     for first in (0, 1):
         waves = np.arange(first, half, 2)
         phase = np.arange(half)[:, None] * waves[None, :] % columns
@@ -28,21 +28,26 @@
         weight = np.where(waves == 0, 1.0, 2.0) / columns
         forward.append(table)
         inverse.append(table.T * np.concatenate([weight, weight])[:, None])
-        rates.append(2.0 * np.sin(np.pi * waves / columns) ** 2)
     return (
-        jnp.asarray(np.stack(forward).astype(np.float32), bf16),
-        jnp.asarray(np.stack(inverse).astype(np.float32), bf16),
-        jnp.asarray(np.concatenate(rates)[None, :].astype(np.float32)),
+        jnp.asarray(np.concatenate(forward).astype(np.float32), bf16),
+        jnp.asarray(np.concatenate(inverse).astype(np.float32), bf16),
     )
 
 
 def wave_parts(columns):
     quarter = columns // 4
     return [
-        (g * quarter + n, (g * 2 * quarter + n, (g * 2 + 1) * quarter + n))
+        (g, n, (g * 2 * quarter + n, (g * 2 + 1) * quarter + n))
         for g in (0, 1)
         for n in range(0, quarter, LANES)
     ]
+
+
+def half_rates(group, first, count, columns):
+    lane = lax.broadcasted_iota(jnp.int32, (1, count), 1) + first
+    wave = (2 * lane + group).astype(f32)
+    sine = jnp.sin(wave * (np.pi / columns))
+    return 2.0 * sine * sine
 
 
 def both_ways(pairs):
@@ -69,67 +74,84 @@
     )
 
 
-def decay_terms(diff_column, half_rates):
-    half = 0.5 / diff_column + half_rates
+def decay_terms(diff_column, rates):
+    half = 0.5 / diff_column + rates
     sinh = jnp.sqrt(half * (half + 2.0))
     grow = 1.0 + half + sinh
     return 1.0 / grow, jnp.log(grow), sinh
 
 
-def start_kernel(
-    groups_x, paired, x_hbm, wet_hbm, flux_hbm, diff_hbm, rates_hbm, table_hbm, *refs
+def surface_kernel(x_hbm, flux_hbm, s_ref, coarse_ref, x_ref, flux_ref, row_ref, x_sem, sem):
+    rows, channels, columns = x_ref.shape
+    col_group = lax.axis_index("gy")
+    is_atmos = lax.axis_index("comp") == 0
+    flux_copy = pltpu.make_async_copy(flux_hbm, flux_ref, sem)
+    copies = [
+        pltpu.make_async_copy(x_hbm.at[0, r], x_ref.at[r], x_sem.at[r]) for r in range(rows)
+    ]
+
+    @pl.when(is_atmos)
+    def _():
+        for copy in [flux_copy] + copies:
+            copy.start()
+        flux_copy.wait()
+        weight = channel_column(flux_ref[...], channels, col_group * channels)
+        for r in range(rows):
+            copies[r].wait()
+            row_ref[r : r + 1, :] = jnp.sum(x_ref[r] * weight, axis=0, keepdims=True)
+
+    @pl.when(jnp.logical_not(is_atmos))
+    def _():
+        top = [
+            pltpu.make_async_copy(
+                x_hbm.at[0, r, pl.ds(0, 8)], x_ref.at[r, pl.ds(0, 8)], x_sem.at[r]
+            )
+            for r in range(rows)
+        ]
+        for copy in top:
+            copy.start()
+        gain = jnp.where(col_group == 0, 1.0, 0.0)
+        for r in range(rows):
+            top[r].wait()
+            row_ref[r : r + 1, :] = x_ref[r, 0:1, :] * gain
+
+    surface = to_tiles(row_ref[...])
+    s_ref[...] = surface
+    coarse_ref[...] = surface.astype(bf16)
+
+
+def forward_kernel(
+    groups_x, paired, x_ref, wet_ref, diff_ref, table_ref, s_ref, *refs
 ):
-    s_ref, y_ref, e1_ref, e3_ref, e2_ref, e4_ref = refs[:6]
+    kept_ref, y_ref, e1_ref, e3_ref, e2_ref, e4_ref = refs[:6]
     if not paired:
         pq_ref = refs[6]
-    (
-        x_ref, wet_ref, flux_ref, diff_ref, rates_ref, table_ref, flat_ref, row_ref,
-        edge_ref, x_sem, table_sem, small_sem,
-    ) = refs[-12:]
-    rows, channels, columns = x_ref.shape
+    kept_ref[...] = s_ref[...]
+    flat_ref, edge_ref = refs[-2:]
+    _, rows, channels, columns = x_ref.shape
     half = columns // 2
     row_group = lax.axis_index("gx")
     col_group = lax.axis_index("gy")
     is_atmos = lax.axis_index("comp") == 0
-    x_copies = [
-        pltpu.make_async_copy(x_hbm.at[0, r], x_ref.at[r], x_sem.at[r]) for r in range(rows)
-    ]
 
     @pl.when(is_atmos)
     def _():
-        small = [
-            pltpu.make_async_copy(hbm, ref, small_sem.at[k])
-            for k, (hbm, ref) in enumerate(
-                ((flux_hbm, flux_ref), (diff_hbm, diff_ref), (rates_hbm, rates_ref))
-            )
-        ]
-        table = [
-            pltpu.make_async_copy(table_hbm.at[k], table_ref.at[k], table_sem.at[k])
-            for k in range(2)
-        ]
-        for copy in small + x_copies + table:
-            copy.start()
-        for copy in small:
-            copy.wait()
         first = col_group * channels
-        weight = channel_column(flux_ref[...], channels, first)
         for r in range(rows):
-            x_copies[r].wait()
-            row_ref[r : r + 1, :] = jnp.sum(x_ref[r] * weight, axis=0, keepdims=True)
-            left, right = x_ref[r, :, :half], x_ref[r, :, half:]
+            left, right = x_ref[0, r, :, :half], x_ref[0, r, :, half:]
             flat_ref[r * channels : (r + 1) * channels, :half] = (left + right).astype(bf16)
             flat_ref[r * channels : (r + 1) * channels, half:] = (left - right).astype(bf16)
-        s_ref[...] = to_tiles(row_ref[...]).astype(bf16)
         for k in range(2):
-            table[k].wait()
             lanes = slice(k * half, (k + 1) * half)
-            part = jnp.dot(flat_ref[:, lanes], table_ref[k], preferred_element_type=f32)
+            part = jnp.dot(
+                flat_ref[:, lanes], table_ref[lanes, :], preferred_element_type=f32
+            )
             y_ref[:, :, lanes] = part.reshape(rows, channels, half)
         diff = channel_column(diff_ref[...], channels, first)
         total = rows * groups_x
         base = (row_group * rows).astype(f32)
-        for n, parts in wave_parts(columns):
-            lam, alpha, _ = decay_terms(diff, rates_ref[:, n : n + LANES])
+        for group, n, parts in wave_parts(columns):
+            lam, alpha, _ = decay_terms(diff, half_rates(group, n, LANES, columns))
             lam2 = lam * lam
             low = jnp.exp(-2.0 * base * alpha)
             high = jnp.exp(-2.0 * (total - rows - base) * alpha)
@@ -155,32 +177,21 @@
 
     @pl.when(jnp.logical_not(is_atmos))
     def _():
-        wet_copy = pltpu.make_async_copy(wet_hbm, wet_ref, small_sem.at[0])
-        for copy in x_copies:
-            copy.start()
-        wet_copy.start()
-        for copy in x_copies:
-            copy.wait()
-        gain = jnp.where(col_group == 0, 1.0, 0.0)
-        for r in range(rows):
-            row_ref[r : r + 1, :] = x_ref[r, 0:1, :] * gain
-        s_ref[...] = to_tiles(row_ref[...]).astype(bf16)
         levels = channels // 2
         lines = 2 * channels
         even_x = row_group % 2 == 0
         even_y = col_group % 2 == 0
-        wet_copy.wait()
         wet = wet_ref[...].astype(f32)
         wet = jnp.concatenate([wet, wet], axis=0).astype(bf16)
 
         def put(out, last):
             @pl.when(last)
             def _():
-                out[0:lines, :] = x_ref[rows - 2 :].reshape(lines, columns).astype(bf16)
+                out[0:lines, :] = x_ref[0, rows - 2 :].reshape(lines, columns).astype(bf16)
 
             @pl.when(jnp.logical_not(last))
             def _():
-                out[0:lines, :] = x_ref[:2].reshape(lines, columns).astype(bf16)
+                out[0:lines, :] = x_ref[0, :2].reshape(lines, columns).astype(bf16)
 
             out[lines : lines + 16, :] = wet
 
@@ -192,7 +203,7 @@
                 for t in range(2):
                     at = (r * 2 + t) * 2
                     c = t * levels + level
-                    edge_ref[at : at + 2, :] = x_ref[r, c : c + 2, :]
+                    edge_ref[at : at + 2, :] = x_ref[0, r, c : c + 2, :]
             out[...] = edge_ref[...].astype(bf16)
 
         @pl.when(even_y)
@@ -206,18 +217,14 @@
             put_edges(e4_ref, levels - 2)
 
 
-def regrid_kernel(n_msgs, *refs):
-    msgs = refs[:n_msgs]
-    (
-        a_src, a_dst, a_count, a_weight, m_src, m_dst, m_count, m_weight,
-        _, _, e2_in, e4_in,
-        land_ref, sent_ref, e2_ref, e4_ref, weight_ref, gath_ref, val_ref, sem,
-    ) = refs[n_msgs:]
-    e2_ref[...] = e2_in[...]
-    e4_ref[...] = e4_in[...]
+def regrid_kernel(
+    surface_ref, a_src, a_dst, a_count, a_weight, m_src, m_dst, m_count, m_weight,
+    _, __,
+    land_ref, sent_ref, weight_ref, gath_ref, val_ref, sem,
+):
     is_atmos = lax.axis_index("comp") == 0
     blocks, points = val_ref.shape
-    cells = msgs[0].shape[0]
+    cells = surface_ref.shape[0]
     rows = 8
 
     @pl.when(is_atmos)
@@ -242,10 +249,7 @@
     dst_row, dst_lane = split(dst)
     lane_iota = lax.broadcasted_iota(jnp.int32, (LANES, points), 0)
     row_iota = lax.broadcasted_iota(jnp.int32, (cells, points), 0)
-    table = msgs[0][...].astype(f32)
-    for m in msgs[1:]:
-        table = table + m[...].astype(f32)
-    table = table.astype(bf16)
+    table = surface_ref[...]
     for b in range(blocks):
         hot = jnp.where(lane_iota == src_lane[b : b + 1], 1.0, 0.0).astype(bf16)
         picked = jnp.dot(table, hot, preferred_element_type=f32)
@@ -287,16 +291,12 @@
     sent_ref[...] = land.astype(bf16)
 
 
-def heat_kernel(rows, e2_ref, e4_ref, land_ref, *refs):
-    parts = refs[:-3]
-    sum_ref, near_ref, far_ref = refs[-3:]
+def heat_kernel(rows, e2_ref, e4_ref, land_ref, part_ref, sum_ref, near_ref, far_ref):
     cells = land_ref.shape[0]
     columns = cells // rows * LANES
     even_x = lax.axis_index("gx") % 2 == 0
     even_y = lax.axis_index("gy") % 2 == 0
-    total = land_ref[...]
-    for part in parts:
-        total = total + part[...].astype(f32)
+    total = land_ref[...] + part_ref[...].astype(f32)
     sum_ref[...] = total
 
     def corners(row):
@@ -317,7 +317,7 @@
 
 
 def steps_kernel(
-    groups_x, groups_y, paired, x_ref, wet_ref, diff_ref, rates_ref, y_ref, e1_ref, e3_ref,
+    groups_x, groups_y, paired, x_ref, wet_ref, diff_ref, y_ref, e1_ref, e3_ref,
     e2_ref, e4_ref, *refs,
 ):
     if not paired:
@@ -333,8 +333,8 @@
         diff = channel_column(diff_ref[...], channels, col_group * channels)
         total = rows * groups_x
         base = (row_group * rows).astype(f32)
-        for n, parts in wave_parts(columns):
-            lam, alpha, sinh = decay_terms(diff, rates_ref[:, n : n + LANES])
+        for group, n, parts in wave_parts(columns):
+            lam, alpha, sinh = decay_terms(diff, half_rates(group, n, LANES, columns))
             lam2 = lam * lam
             low = jnp.exp(-2.0 * base * alpha)
             high = jnp.exp(-2.0 * (total - rows - base) * alpha)
@@ -494,7 +494,7 @@
             even, odd = [
                 jnp.dot(
                     zb_ref[:, k * half : (k + 1) * half],
-                    table_ref[k, :, n : n + step],
+                    table_ref[k * half : (k + 1) * half, n : n + step],
                     preferred_element_type=f32,
                 ).reshape(rows, channels, step)
                 for k in range(2)
@@ -575,7 +575,7 @@
     groups_y = lax.axis_size("gy")
     blocks, points = a2o_source.shape[2:]
     cells = rows * columns // LANES
-    forward, inverse, half_rates = fourier_tables(columns)
+    forward, inverse = fourier_tables(columns)
     flux_row = flux_weight[None, :]
     gain_row = variable_sea_response[None, :]
     diff_row = diffusivity[None, :]
@@ -583,15 +583,31 @@
     params = functools.partial(pltpu.CompilerParams, vmem_limit_bytes=40 * 2**20)
     vmem = pl.BlockSpec(memory_space=pltpu.VMEM)
     smem = pl.BlockSpec(memory_space=pltpu.SMEM)
+    hbm = pl.BlockSpec(memory_space=pltpu.HBM)
     anywhere = pl.BlockSpec(memory_space=pl.ANY)
-    hbm = pl.BlockSpec(memory_space=pltpu.HBM)
 
     def shape(dims, dtype):
         return jax.ShapeDtypeStruct(dims, dtype)
 
+    partial_surface, coarse = pl.pallas_call(
+        surface_kernel,
+        out_shape=[shape((cells, LANES), f32), shape((cells, LANES), bf16)],
+        in_specs=[hbm, hbm],
+        out_specs=[vmem, vmem],
+        scratch_shapes=[
+            pltpu.VMEM((rows, channels, columns), f32),
+            pltpu.VMEM(flux_row.shape, f32),
+            pltpu.VMEM((rows, columns), f32),
+            pltpu.SemaphoreType.DMA((rows,)),
+            pltpu.SemaphoreType.DMA,
+        ],
+        compiler_params=pltpu.CompilerParams(vmem_limit_bytes=58 * 2**20),
+        name="surface_partials",
+    )(fields, flux_row)
+
     lines = 2 * channels + 16
     shapes = [
-        shape((cells, LANES), bf16),
+        shape((cells, LANES), f32),
         shape((rows, channels, columns), f32),
         shape((lines, columns), bf16),
         shape((lines, columns), bf16),
@@ -601,34 +617,29 @@
     if not paired:
         shapes.append(shape((2, channels, columns), bf16))
     partial_surface, y, e1, e3, e2, e4, *sums = pl.pallas_call(
-        functools.partial(start_kernel, groups_x, paired),
+        functools.partial(forward_kernel, groups_x, paired),
         out_shape=shapes,
-        in_specs=[hbm] * 6,
+        in_specs=[vmem] * 5,
         out_specs=[vmem] * len(shapes),
         scratch_shapes=[
-            pltpu.VMEM((rows, channels, columns), f32),
-            pltpu.VMEM((rows, columns), jnp.int32),
-            pltpu.VMEM(flux_row.shape, f32),
-            pltpu.VMEM(diff_row.shape, f32),
-            pltpu.VMEM(half_rates.shape, f32),
-            pltpu.VMEM(forward.shape, bf16),
             pltpu.VMEM((rows * channels, columns), bf16),
-            pltpu.VMEM((rows, columns), f32),
             pltpu.VMEM((4 * rows, columns), f32),
-            pltpu.SemaphoreType.DMA((rows,)),
-            pltpu.SemaphoreType.DMA((2,)),
-            pltpu.SemaphoreType.DMA((3,)),
         ],
         compiler_params=params(),
-        name="surface_and_forward_or_halos",
-    )(fields, wet_cells, flux_row, diff_row, half_rates, forward)
-
-    surfaces = []
-    for mask in range(groups_y):
-        route = []
-        for j in range(groups_y):
-            route += both_ways([(j, groups_y + (j ^ mask))])
-        surfaces.append(lax.ppermute(partial_surface, ("comp", "gy"), route))
+        name="forward_or_halos",
+    )(fields, wet_cells, diff_row, forward, partial_surface)
+
+    def sum_masks():
+        mask = 1
+        while mask < groups_y:
+            yield [(j, j ^ mask) for j in range(groups_y)]
+            mask *= 2
+
+    surface = partial_surface
+    for route in sum_masks():
+        surface = surface + lax.ppermute(coarse, "gy", route).astype(f32)
+        coarse = surface.astype(bf16)
+    surface = lax.ppermute(coarse, "comp", [(0, 1), (1, 0)])
 
     def ring_pairs(count, odd):
         return [(a, (a + 1) % count) for a in range(odd, count, 2)]
@@ -649,19 +660,15 @@
 
     e1 = lax.ppermute(e1, "gx", both_ways(ring_pairs(groups_x, 0)))
     e3 = lax.ppermute(e3, "gx", both_ways(ring_pairs(groups_x, 1)))
-
-    landing, sent, e2, e4 = pl.pallas_call(
-        functools.partial(regrid_kernel, groups_y),
-        out_shape=[
-            shape((cells, LANES), f32),
-            shape((cells, LANES), bf16),
-            shape(e2.shape, bf16),
-            shape(e4.shape, bf16),
-        ],
-        in_specs=[vmem] * groups_y
-        + [vmem, vmem, smem, hbm, vmem, vmem, smem, hbm]
-        + [anywhere, anywhere, vmem, vmem],
-        out_specs=[vmem] * 4,
+    axes = ("comp", "gx", "gy")
+    e2 = lax.ppermute(e2, axes, level_route(0))
+    e4 = lax.ppermute(e4, axes, level_route(1))
+
+    landing, sent = pl.pallas_call(
+        regrid_kernel,
+        out_shape=[shape((cells, LANES), f32), shape((cells, LANES), bf16)],
+        in_specs=[vmem, vmem, vmem, smem, hbm, vmem, vmem, smem, hbm, anywhere, anywhere],
+        out_specs=[vmem] * 2,
         scratch_shapes=[
             pltpu.VMEM((blocks, points, points), bf16),
             pltpu.VMEM((blocks, points), f32),
@@ -671,19 +678,16 @@
         compiler_params=params(),
         name="regrid_blocks",
     )(
-        *surfaces,
+        surface,
         a2o_source, a2o_target, a2o_count, a2o_weight,
         marine_air_input_index, marine_air_output_index,
-        marine_air_piece_tally, marine_air_piece_factor, e1, e3, e2, e4,
+        marine_air_piece_tally, marine_air_piece_factor, e1, e3,
     )
-    parts = [
-        lax.ppermute(sent, "gy", [(j, j ^ mask) for j in range(groups_y)])
-        for mask in range(1, groups_y)
-    ]
-
-    axes = ("comp", "gx", "gy")
-    e2 = lax.ppermute(e2, axes, level_route(0))
-    e4 = lax.ppermute(e4, axes, level_route(1))
+    *early, final = sum_masks()
+    for route in early:
+        landing = landing + lax.ppermute(sent, "gy", route).astype(f32)
+        sent = landing.astype(bf16)
+    part = lax.ppermute(sent, "gy", final)
 
     extra = []
     if not paired:
@@ -691,8 +695,8 @@
         viscous = lax.dynamic_slice_in_dim(
             diffusivity, lax.axis_index("gy") * channels, channels
         )[:, None]
-        _, alpha, _ = decay_terms(viscous, half_rates)
-        alpha = jnp.concatenate([alpha, alpha], axis=1)
+        rates = [half_rates(g, 0, columns // 4, columns) for g in (0, 0, 1, 1)]
+        _, alpha, _ = decay_terms(viscous, jnp.concatenate(rates, axis=1))
         gap = lax.axis_index("gx") - jnp.arange(groups_x)
         decay = jnp.exp(
             -(rows * jnp.maximum(jnp.abs(gap) - 1, 0))[:, None, None] * alpha[None]
@@ -709,7 +713,7 @@
             shape((rows * channels, columns), bf16),
             shape((7, 16, columns), f32),
         ],
-        in_specs=[vmem] * (9 + len(extra)),
+        in_specs=[vmem] * (8 + len(extra)),
         out_specs=[vmem] * 3,
         scratch_shapes=[
             pltpu.VMEM((rows, channels, LANES), f32),
@@ -719,7 +723,7 @@
         ],
         compiler_params=params(),
         name="damping_or_ocean_steps",
-    )(fields, wet_cells, diff_row, half_rates, y, e1, e3, e2, e4, *extra)
+    )(fields, wet_cells, diff_row, y, e1, e3, e2, e4, *extra)
 
     surface_sum, near, far = pl.pallas_call(
         functools.partial(heat_kernel, rows),
@@ -728,11 +732,11 @@
             shape((cells + columns // 16, LANES), bf16),
             shape((cells + columns // 16, LANES), bf16),
         ],
-        in_specs=[vmem] * (3 + len(parts)),
+        in_specs=[vmem] * 4,
         out_specs=[vmem] * 3,
         compiler_params=params(),
         name="surface_sum",
-    )(e2, e4, landing, *parts)
+    )(e2, e4, landing, part)
 
     near = lax.ppermute(near, "gx", both_ways(ring_pairs(groups_x, 0)))
     far = lax.ppermute(far, "gx", both_ways(ring_pairs(groups_x, 1)))

time: 41.4 us -> 36.4 us (0.88)
  starting transfers between devices: 18.8 us -> 15.2 us
  local copies, waits for them, and re-layouts: 5.28 us -> 4.08 us
    ppermute x7 -> x5, starting transfers between devices: 11.7 us -> 7.85 us  [the longest x2 5.75 us: local(): surface = surface + lax.ppermute(coarse, 'gy', route).astype(f32)]
    ppermute x7 -> x5, waiting for transfers between devices: 7.21 us -> 4.31 us  [the longest x1 2.17 us: local(): part = lax.ppermute(sent, 'gy', final)]
    ppermute x1, starting transfers between devices: 1.75 us -> 3.52 us  [local(): e4 = lax.ppermute(e4, axes, level_route(1))]
    ppermute x1, waiting for transfers between devices: 0.01 us -> 1.68 us  [local(): e4 = lax.ppermute(e4, axes, level_route(1))]
    unnamed x30 -> x28, local copies, waits for them, and re-layouts: 5.28 us -> 4.08 us
    ppermute x1, starting transfers between devices: 2.61 us -> 1.65 us  [local(): e3 = lax.ppermute(e3, 'gx', both_ways(ring_pairs(groups_x, 1)))]
    ppermute x1, starting transfers between devices: 1.6 us -> 0.66 us  [local(): far = lax.ppermute(far, 'gx', both_ways(ring_pairs(groups_x, 1)))]
    ppermute x1, starting transfers between devices: 0.6 us -> 1.49 us  [local(): e2 = lax.ppermute(e2, axes, level_route(0))]
  transfers between devices with their start and end apart: 13 -> 11, of which waited for: 5 -> 6; matrix products, arithmetic and copies ran while one was open for 0% -> 0% of each run, Pallas kernels for 2% -> 4%
where the time goes in v6:
time: 36.4 us; the launch traced here: 36.1 us
  starting transfers between devices  15.2 us (42%)
  waiting for transfers between devices  7.89 us (22%)
  Pallas kernels  7.4 us (20%)
  local copies, waits for them, and re-layouts  4.08 us (11%)
  between operations  1.44 us (4%)
    ppermute x2, starting transfers between devices, local(): surface = surface + lax.ppermute(coarse, 'gy', route).astype(f32)  5.75 us
    unnamed x28, local copies, waits for them, and re-layouts  4.08 us
    ppermute x1, starting transfers between devices, local(): e4 = lax.ppermute(e4, axes, level_route(1))  3.52 us
    pallas_call x1, Pallas kernels, local(): pl.pallas_call(regrid_kernel, out_shape=[shape((cells, LANES), f32), shap...  2.28 us
    ppermute x1, waiting for transfers between devices, local(): part = lax.ppermute(sent, 'gy', final)  2.17 us
    pallas_call x1, Pallas kernels, local(): pl.pallas_call(surface_kernel, out_shape=[shape((cells, LANES), f32), sha...  2.09 us
    ppermute x1, waiting for transfers between devices, local(): far = lax.ppermute(far, 'gx', both_ways(ring_pairs(groups_x, 1)))  1.8 us
    ppermute x1, waiting for transfers between devices, local(): surface = lax.ppermute(coarse, 'comp', [(0, 1), (1, 0)])  1.77 us
  transfers between devices with their start and end apart: 11, of which 6 were waited for; matrix products, arithmetic and copies ran while one was open for 0% of the time, Pallas kernels for 4%

profile of v6, /device:TPU:0, one launch (start us, length us, event | category | flops | bytes accessed | tf_op | source)
XLA Modules:
  0.0 36.1 jit_solution(4324614833806041365)
XLA Ops:
  0.0 0.0 copy-start
  0.0 2.1 %surface_partials.1 = (f32[64,128]{1,0:T(8,128)}, bf16[64,128]{1,0:T(8,128)(2,1)}) custom-call(f32[1,8,32,1024]{3,2,1,0:T(8,128)} %x_ref.3, f32[1,128]{1,0:T(1,128)} %bitcast.6), custom_call_target="tpu_custom_call" | custom-call | tf_op jit(solution)/shard_map/surface_partials/pallas_call | solution.py:592
  2.1 3.1 %collective-permute-start.4 = (bf16[64,128]{1,0:T(8,128)(2,1)}, bf16[64,128]{1,0:T(8,128)(2,1)S(1)}, u32[]{:S(2)}, u32[]{:S(2)}) collective-permute-start(bf16[64,128]{1,0:T(8,128)(2,1)} %get-tuple-element.31), channel_id=1, source_target_pairs={{0,1},{1,0},{2,3},{3,2},{4,5},{5,4},{6,7},{7,6},{8,9},{9,8},{10,11... | collective-permute-start | bytes 49160 | tf_op jit(solution)/shard_map/ppermute | solution.py:640
  5.2 0.0 copy-start.12
  5.2 0.0 copy-done
  5.2 0.7 %copy-done.12 = f32[128]{0:T(128)S(1)} copy-done((f32[128]{0:T(128)S(1)}, f32[128]{0:T(128)}, u32[]{:S(2)}) %copy-start.12) | copy-done | bytes 536
  5.8 0.0 copy-start.2
  5.8 1.2 %copy-done.2 = bf16[1024,512]{1,0:T(8,128)(2,1)S(1)} copy-done((bf16[1024,512]{1,0:T(8,128)(2,1)S(1)}, bf16[1024,512]{1,0:T(8,128)(2,1)}, u32[]{:S(2)}) %copy-start.2) | copy-done | bytes 1048600
  7.1 0.0 copy-start.5
  7.1 0.8 %copy-done.5 = s32[8,1024]{1,0:T(8,128)S(1)} copy-done((s32[8,1024]{1,0:T(8,128)S(1)}, s32[8,1024]{1,0:T(8,128)}, u32[]{:S(2)}) %copy-start.5) | copy-done | bytes 32792
  7.8 0.0 copy-start.7
  7.8 0.8 %copy-done.7 = f32[64,128]{1,0:T(8,128)S(1)} copy-done((f32[64,128]{1,0:T(8,128)S(1)}, f32[64,128]{1,0:T(8,128)}, u32[]{:S(2)}) %copy-start.7) | copy-done | bytes 32792
  8.6 0.0 copy-start.3
  8.6 0.0 copy-start.4
  8.6 0.6 %forward_or_halos.1 = (f32[64,128]{1,0:T(8,128)S(1)}, f32[8,32,1024]{2,1,0:T(8,128)S(1)}, bf16[80,1024]{1,0:T(8,128)(2,1)S(1)}, bf16[80,1024]{1,0:T(8,128)(2,1)S...) custom-call(f32[1,8,32,1024]{3,2,1,0:T(8,128)S(1)} %copy-done, s32[8,1024]{1,0:T(8,128)S(1)} %copy-done.5, ...), custom_call_target="tpu_custom_call" | custom-call | tf_op jit(solution)/shard_map/forward_or_halos/pallas_call | solution.py:619
  9.2 0.0 collective-permute-done.4
  9.3 2.7 %collective-permute-start.5 = (bf16[64,128]{1,0:T(8,128)(2,1)S(1)}, bf16[64,128]{1,0:T(8,128)(2,1)S(1)}, u32[]{:S(2)}, u32[]{:S(2)}) collective-permute-start(bf16[64,128]{1,0:T(8,128)(2,1)S(1)} %fusion), channel_id=1, source_target_pairs={{0,2},{1,3},{2,0},{3,1},{4,6},{5,7},{6,4},{7,5},{8,10},{9,11},{10,... | collective-permute-start | bytes 49160 | tf_op jit(solution)/shard_map/ppermute | solution.py:640
  11.9 0.0 collective-permute-start
  11.9 0.0 copy-start.8
  11.9 0.0 copy-start.9
  11.9 0.0 copy-start.10
  11.9 0.0 copy-start.11
  12.0 1.7 %collective-permute-start.1 = (bf16[80,1024]{1,0:T(8,128)(2,1)S(1)}, bf16[80,1024]{1,0:T(8,128)(2,1)S(1)}, u32[]{:S(2)}, u32[]{:S(2)}) collective-permute-start(bf16[80,1024]{1,0:T(8,128)(2,1)S(1)} %get-tuple-element.24), channel_id=1, source_target_pairs={{4,8},{8,4},{12,0},{0,12},{5,9},{9,5},{13,1},{1,13},{6,10},{10,6},... | collective-permute-start | bytes 491528 | tf_op jit(solution)/shard_map/ppermute | solution.py:662
  13.6 0.4 %collective-permute-done.5 = bf16[64,128]{1,0:T(8,128)(2,1)S(1)} collective-permute-done((bf16[64,128]{1,0:T(8,128)(2,1)S(1)}, bf16[64,128]{1,0:T(8,128)(2,1)S(1)}, u32[]{:S(2)}, u32[]{:S(2)}) %collective-permute-start.5) | collective-permute-done | bytes 16416 | tf_op jit(solution)/shard_map/ppermute | solution.py:640
  14.0 0.7 %collective-permute-start.6 = (bf16[64,128]{1,0:T(8,128)(2,1)S(1)}, bf16[64,128]{1,0:T(8,128)(2,1)S(1)}, u32[]{:S(2)}, u32[]{:S(2)}) collective-permute-start(bf16[64,128]{1,0:T(8,128)(2,1)S(1)} %add_convert_fusion), channel_id=1, source_target_pairs={{0,16},{16,0},{1,17},{17,1},{2,18},{18,2},{3,19},{19,3},{4,20},{20... | collective-permute-start | bytes 49160 | tf_op jit(solution)/shard_map/ppermute | solution.py:642
  16.0 1.8 %collective-permute-done.6.surface_ref = bf16[64,128]{1,0:T(8,128)(2,1)S(1)} collective-permute-done((bf16[64,128]{1,0:T(8,128)(2,1)S(1)}, bf16[64,128]{1,0:T(8,128)(2,1)S(1)}, u32[]{:S(2)}, u32[]{:S(2)}) %collective-permute-start.6) | collective-permute-done | bytes 16416 | tf_op jit(solution)/shard_map/ppermute | solution.py:642
  17.8 0.0 collective-permute-done.e1_ref._
  17.8 0.1 collective-permute-done.1.e3_ref.__
  17.9 0.0 copy-done.3
  17.9 0.0 copy-done.4
  17.9 0.0 copy-done.8
  17.9 0.0 copy-done.9
  17.9 0.0 copy-done.10
  17.9 0.0 copy-done.11
  17.9 2.3 %regrid_blocks.1 = (f32[64,128]{1,0:T(8,128)S(1)}, bf16[64,128]{1,0:T(8,128)(2,1)S(1)}) custom-call(bf16[64,128]{1,0:T(8,128)(2,1)S(1)} %collective-permute-done.6.surface_ref, s32[1,1,32,128]{3,2,1,0:T(8,128)S(1)} %copy-done.8, s32[1,1,32,128]{3,2,1,0:T(8,128)S(1)} %copy-done.9, s32[1,1]{1,0:T(1,128)S(6)} %copy.16.a_count, ...), custom_call_target="tpu_custom_call" | custom-call | tf_op jit(solution)/shard_map/regrid_blocks/pallas_call | solution.py:667
  20.2 0.5 %collective-permute-start.7 = (bf16[64,128]{1,0:T(8,128)(2,1)S(1)}, bf16[64,128]{1,0:T(8,128)(2,1)S(1)}, u32[]{:S(2)}, u32[]{:S(2)}) collective-permute-start(bf16[64,128]{1,0:T(8,128)(2,1)S(1)} %get-tuple-element.33), channel_id=1, source_target_pairs={{0,1},{1,0},{2,3},{3,2},{4,5},{5,4},{6,7},{7,6},{8,9},{9,8},{10,11... | collective-permute-start | bytes 49160 | tf_op jit(solution)/shard_map/ppermute | solution.py:688
  20.7 1.5 %collective-permute-start.2 = (bf16[32,1024]{1,0:T(8,128)(2,1)S(1)}, bf16[32,1024]{1,0:T(8,128)(2,1)S(1)}, u32[]{:S(2)}, u32[]{:S(2)}) collective-permute-start(bf16[32,1024]{1,0:T(8,128)(2,1)S(1)} %get-tuple-element.25), channel_id=1, source_target_pairs={{16,17},{17,16},{18,19},{19,18},{0,8},{8,0},{1,9},{9,1},{2,10},{10... | collective-permute-start | bytes 196616 | tf_op jit(solution)/shard_map/ppermute | solution.py:664
  22.2 3.5 %collective-permute-start.3 = (bf16[32,1024]{1,0:T(8,128)(2,1)S(1)}, bf16[32,1024]{1,0:T(8,128)(2,1)S(1)}, u32[]{:S(2)}, u32[]{:S(2)}) collective-permute-start(bf16[32,1024]{1,0:T(8,128)(2,1)S(1)} %get-tuple-element.26), channel_id=1, source_target_pairs={{17,18},{18,17},{1,2},{2,1},{19,16},{16,19},{3,0},{0,3},{21,22},{2... | collective-permute-start | bytes 196616 | tf_op jit(solution)/shard_map/ppermute | solution.py:665
  25.7 0.0 collective-permute-done.7
  25.8 0.9 %collective-permute-start.8 = (bf16[64,128]{1,0:T(8,128)(2,1)S(1)}, bf16[64,128]{1,0:T(8,128)(2,1)S(1)}, u32[]{:S(2)}, u32[]{:S(2)}) collective-permute-start(bf16[64,128]{1,0:T(8,128)(2,1)S(1)} %get-tuple-element.37), channel_id=1, source_target_pairs={{0,2},{1,3},{2,0},{3,1},{4,6},{5,7},{6,4},{7,5},{8,10},{9,11},{10,... | collective-permute-start | bytes 49160 | tf_op jit(solution)/shard_map/ppermute | solution.py:690
  26.6 0.0 collective-permute-done.2.e2_ref
  26.6 1.7 %collective-permute-done.3.e4_ref = bf16[32,1024]{1,0:T(8,128)(2,1)S(1)} collective-permute-done((bf16[32,1024]{1,0:T(8,128)(2,1)S(1)}, bf16[32,1024]{1,0:T(8,128)(2,1)S(1)}, u32[]{:S(2)}, u32[]{:S(2)}) %collective-permute-start.3) | collective-permute-done | bytes 65568 | tf_op jit(solution)/shard_map/ppermute | solution.py:665
  28.3 2.2 %collective-permute-done.8.part_ref = bf16[64,128]{1,0:T(8,128)(2,1)S(1)} collective-permute-done((bf16[64,128]{1,0:T(8,128)(2,1)S(1)}, bf16[64,128]{1,0:T(8,128)(2,1)S(1)}, u32[]{:S(2)}, u32[]{:S(2)}) %collective-permute-start.8) | collective-permute-done | bytes 16416 | tf_op jit(solution)/shard_map/ppermute | solution.py:690
  30.5 0.0 copy-start.6
  30.5 0.1 collective-permute-start.9
  30.6 0.7 %collective-permute-start.10 = (bf16[128,128]{1,0:T(8,128)(2,1)S(1)}, bf16[128,128]{1,0:T(8,128)(2,1)S(1)}, u32[]{:S(2)}, u32[]{:S(2)}) collective-permute-start(bf16[128,128]{1,0:T(8,128)(2,1)S(1)} %get-tuple-element.36), channel_id=1, source_target_pairs={{4,8},{8,4},{12,0},{0,12},{5,9},{9,5},{13,1},{1,13},{6,10},{10,6},... | collective-permute-start | bytes 98312 | tf_op jit(solution)/shard_map/ppermute | solution.py:742
  31.3 0.0 copy-done.6
  31.3 0.0 copy-start.1
  31.3 0.9 %damping_or_ocean_steps.1 = (f32[8,32,1024]{2,1,0:T(8,128)S(1)}, bf16[256,1024]{1,0:T(8,128)(2,1)S(1)}, f32[7,16,1024]{2,1,0:T(8,128)S(1)}) custom-call(f32[1,8,32,1024]{3,2,1,0:T(8,128)S(1)} %copy-done, s32[8,1024]{1,0:T(8,128)S(1)} %copy-done.6, f32[1,128]{1,0:T(1,128)S(1)} %bitcast.4, f32[8,32,1024]{2,1,0:T(8,128)S(1)} %get-tuple-element.22.y_ref, ...), custom_call_target="tpu_custom_call" | custom-call | tf_op jit(solution)/shard_map/damping_or_ocean_steps/pallas_call | solution.py:709
  32.2 0.0 collective-permute-done.9.near_ref
  32.2 1.8 %collective-permute-done.10.far_ref = bf16[128,128]{1,0:T(8,128)(2,1)S(1)} collective-permute-done((bf16[128,128]{1,0:T(8,128)(2,1)S(1)}, bf16[128,128]{1,0:T(8,128)(2,1)S(1)}, u32[]{:S(2)}, u32[]{:S(2)}) %collective-permute-start.10) | collective-permute-done | bytes 32800 | tf_op jit(solution)/shard_map/ppermute | solution.py:742
  34.0 0.0 copy-start.13
  34.0 0.0 copy-done.1
  34.0 0.7 %copy-done.13 = f32[128]{0:T(128)S(1)} copy-done((f32[128]{0:T(128)S(1)}, f32[128]{0:T(128)}, u32[]{:S(2)}) %copy-start.13) | copy-done | bytes 536
  34.7 1.4 %inverse_or_heat.1 = f32[1,8,32,1024]{3,2,1,0:T(8,128)} custom-call(f32[1,128]{1,0:T(1,128)S(1)} %bitcast.5, bf16[1024,512]{1,0:T(8,128)(2,1)S(1)} %copy-done.1, f32[8,32,1024]{2,1,0:T(8,128)S(1)} %get-tuple-element.27.base_ref, bf16[256,1024]{1,0:T(8,128)(2,1)S(1)} %get-tuple-element.28.zb_ref, f32[7,16,1024]{2,1,0:T(8,128)S(1)} %get-tuple-element.29.c_ref, ...), custom_call_target="tpu_custom_call" | custom-call | tf_op jit(solution)/shard_map/inverse_or_heat/pallas_call | solution.py:743
  (4 shorter events, 0.1 us)
Async XLA Ops:
  0.0 5.2 %copy-start = (f32[1,8,32,1024]{3,2,1,0:T(8,128)S(1)}, f32[1,8,32,1024]{3,2,1,0:T(8,128)}, u32[]{:S(2)}) copy-start(f32[1,8,32,1024]{3,2,1,0:T(8,128)} %x_ref.3) | copy-start | bytes 3145732
  2.1 7.2 %collective-permute-start.4 = (bf16[64,128]{1,0:T(8,128)(2,1)}, bf16[64,128]{1,0:T(8,128)(2,1)S(1)}, u32[]{:S(2)}, u32[]{:S(2)}) collective-permute-start(bf16[64,128]{1,0:T(8,128)(2,1)} %get-tuple-element.31), channel_id=1, source_target_pairs={{0,1},{1,0},{2,3},{3,2},{4,5},{5,4},{6,7},{7,6},{8,9},{9,8},{10,11... | collective-permute-start | bytes 49160 | tf_op jit(solution)/shard_map/ppermute | solution.py:640
  5.2 0.7 %copy-start.12 = (f32[128]{0:T(128)S(1)}, f32[128]{0:T(128)}, u32[]{:S(2)}) copy-start(f32[128]{0:T(128)} %param.19) | copy-start | bytes 1540
  5.8 1.2 %copy-start.2 = (bf16[1024,512]{1,0:T(8,128)(2,1)S(1)}, bf16[1024,512]{1,0:T(8,128)(2,1)}, u32[]{:S(2)}) copy-start(bf16[1024,512]{1,0:T(8,128)(2,1)} %constant.4.clone.table_ref) | copy-start | bytes 3145732
  7.1 0.8 %copy-start.5 = (s32[8,1024]{1,0:T(8,128)S(1)}, s32[8,1024]{1,0:T(8,128)}, u32[]{:S(2)}) copy-start(s32[8,1024]{1,0:T(8,128)} %wet_ref.3) | copy-start | bytes 98308
  7.8 0.8 %copy-start.7 = (f32[64,128]{1,0:T(8,128)S(1)}, f32[64,128]{1,0:T(8,128)}, u32[]{:S(2)}) copy-start(f32[64,128]{1,0:T(8,128)} %get-tuple-element.21.s_ref) | copy-start | bytes 98308
  8.6 9.3 %copy-start.3 = (bf16[1,1,32,128,128]{4,3,2,1,0:T(8,128)(2,1)S(1)}, bf16[1,1,32,128,128]{4,3,2,1,0:T(8,128)(2,1)}, u32[]{:S(2)}) copy-start(bf16[1,1,32,128,128]{4,3,2,1,0:T(8,128)(2,1)} %a_weight.1) | copy-start | bytes 3145732
  8.6 9.3 %copy-start.4 = (bf16[1,1,32,128,128]{4,3,2,1,0:T(8,128)(2,1)S(1)}, bf16[1,1,32,128,128]{4,3,2,1,0:T(8,128)(2,1)}, u32[]{:S(2)}) copy-start(bf16[1,1,32,128,128]{4,3,2,1,0:T(8,128)(2,1)} %m_weight.1) | copy-start | bytes 3145732
  9.3 4.7 %collective-permute-start.5 = (bf16[64,128]{1,0:T(8,128)(2,1)S(1)}, bf16[64,128]{1,0:T(8,128)(2,1)S(1)}, u32[]{:S(2)}, u32[]{:S(2)}) collective-permute-start(bf16[64,128]{1,0:T(8,128)(2,1)S(1)} %fusion), channel_id=1, source_target_pairs={{0,2},{1,3},{2,0},{3,1},{4,6},{5,7},{6,4},{7,5},{8,10},{9,11},{10,... | collective-permute-start | bytes 49160 | tf_op jit(solution)/shard_map/ppermute | solution.py:640
  11.9 5.9 %collective-permute-start = (bf16[80,1024]{1,0:T(8,128)(2,1)S(1)}, bf16[80,1024]{1,0:T(8,128)(2,1)S(1)}, u32[]{:S(2)}, u32[]{:S(2)}) collective-permute-start(bf16[80,1024]{1,0:T(8,128)(2,1)S(1)} %get-tuple-element.23), channel_id=1, source_target_pairs={{0,4},{4,0},{8,12},{12,8},{1,5},{5,1},{9,13},{13,9},{2,6},{6,2},{1... | collective-permute-start | bytes 491528 | tf_op jit(solution)/shard_map/ppermute | solution.py:661
  11.9 6.0 %copy-start.8 = (s32[1,1,32,128]{3,2,1,0:T(8,128)S(1)}, s32[1,1,32,128]{3,2,1,0:T(8,128)}, u32[]{:S(2)}) copy-start(s32[1,1,32,128]{3,2,1,0:T(8,128)} %a_src.1) | copy-start | bytes 49156
  11.9 6.0 %copy-start.9 = (s32[1,1,32,128]{3,2,1,0:T(8,128)S(1)}, s32[1,1,32,128]{3,2,1,0:T(8,128)}, u32[]{:S(2)}) copy-start(s32[1,1,32,128]{3,2,1,0:T(8,128)} %a_dst.1) | copy-start | bytes 49156
  11.9 6.0 %copy-start.10 = (s32[1,1,32,128]{3,2,1,0:T(8,128)S(1)}, s32[1,1,32,128]{3,2,1,0:T(8,128)}, u32[]{:S(2)}) copy-start(s32[1,1,32,128]{3,2,1,0:T(8,128)} %m_src.1) | copy-start | bytes 49156
  11.9 6.0 %copy-start.11 = (s32[1,1,32,128]{3,2,1,0:T(8,128)S(1)}, s32[1,1,32,128]{3,2,1,0:T(8,128)}, u32[]{:S(2)}) copy-start(s32[1,1,32,128]{3,2,1,0:T(8,128)} %m_dst.1) | copy-start | bytes 49156
  12.0 5.9 %collective-permute-start.1 = (bf16[80,1024]{1,0:T(8,128)(2,1)S(1)}, bf16[80,1024]{1,0:T(8,128)(2,1)S(1)}, u32[]{:S(2)}, u32[]{:S(2)}) collective-permute-start(bf16[80,1024]{1,0:T(8,128)(2,1)S(1)} %get-tuple-element.24), channel_id=1, source_target_pairs={{4,8},{8,4},{12,0},{0,12},{5,9},{9,5},{13,1},{1,13},{6,10},{10,6},... | collective-permute-start | bytes 491528 | tf_op jit(solution)/shard_map/ppermute | solution.py:662
  14.0 3.8 %collective-permute-start.6 = (bf16[64,128]{1,0:T(8,128)(2,1)S(1)}, bf16[64,128]{1,0:T(8,128)(2,1)S(1)}, u32[]{:S(2)}, u32[]{:S(2)}) collective-permute-start(bf16[64,128]{1,0:T(8,128)(2,1)S(1)} %add_convert_fusion), channel_id=1, source_target_pairs={{0,16},{16,0},{1,17},{17,1},{2,18},{18,2},{3,19},{19,3},{4,20},{20... | collective-permute-start | bytes 49160 | tf_op jit(solution)/shard_map/ppermute | solution.py:642
  20.2 5.5 %collective-permute-start.7 = (bf16[64,128]{1,0:T(8,128)(2,1)S(1)}, bf16[64,128]{1,0:T(8,128)(2,1)S(1)}, u32[]{:S(2)}, u32[]{:S(2)}) collective-permute-start(bf16[64,128]{1,0:T(8,128)(2,1)S(1)} %get-tuple-element.33), channel_id=1, source_target_pairs={{0,1},{1,0},{2,3},{3,2},{4,5},{5,4},{6,7},{7,6},{8,9},{9,8},{10,11... | collective-permute-start | bytes 49160 | tf_op jit(solution)/shard_map/ppermute | solution.py:688
  20.7 5.9 %collective-permute-start.2 = (bf16[32,1024]{1,0:T(8,128)(2,1)S(1)}, bf16[32,1024]{1,0:T(8,128)(2,1)S(1)}, u32[]{:S(2)}, u32[]{:S(2)}) collective-permute-start(bf16[32,1024]{1,0:T(8,128)(2,1)S(1)} %get-tuple-element.25), channel_id=1, source_target_pairs={{16,17},{17,16},{18,19},{19,18},{0,8},{8,0},{1,9},{9,1},{2,10},{10... | collective-permute-start | bytes 196616 | tf_op jit(solution)/shard_map/ppermute | solution.py:664
  22.2 6.1 %collective-permute-start.3 = (bf16[32,1024]{1,0:T(8,128)(2,1)S(1)}, bf16[32,1024]{1,0:T(8,128)(2,1)S(1)}, u32[]{:S(2)}, u32[]{:S(2)}) collective-permute-start(bf16[32,1024]{1,0:T(8,128)(2,1)S(1)} %get-tuple-element.26), channel_id=1, source_target_pairs={{17,18},{18,17},{1,2},{2,1},{19,16},{16,19},{3,0},{0,3},{21,22},{2... | collective-permute-start | bytes 196616 | tf_op jit(solution)/shard_map/ppermute | solution.py:665
  25.8 4.7 %collective-permute-start.8 = (bf16[64,128]{1,0:T(8,128)(2,1)S(1)}, bf16[64,128]{1,0:T(8,128)(2,1)S(1)}, u32[]{:S(2)}, u32[]{:S(2)}) collective-permute-start(bf16[64,128]{1,0:T(8,128)(2,1)S(1)} %get-tuple-element.37), channel_id=1, source_target_pairs={{0,2},{1,3},{2,0},{3,1},{4,6},{5,7},{6,4},{7,5},{8,10},{9,11},{10,... | collective-permute-start | bytes 49160 | tf_op jit(solution)/shard_map/ppermute | solution.py:690
  30.5 0.8 %copy-start.6 = (s32[8,1024]{1,0:T(8,128)S(1)}, s32[8,1024]{1,0:T(8,128)}, u32[]{:S(2)}) copy-start(s32[8,1024]{1,0:T(8,128)} %wet_ref.3) | copy-start | bytes 98308
  30.5 1.7 %collective-permute-start.9 = (bf16[128,128]{1,0:T(8,128)(2,1)S(1)}, bf16[128,128]{1,0:T(8,128)(2,1)S(1)}, u32[]{:S(2)}, u32[]{:S(2)}) collective-permute-start(bf16[128,128]{1,0:T(8,128)(2,1)S(1)} %get-tuple-element.35), channel_id=1, source_target_pairs={{0,4},{4,0},{8,12},{12,8},{1,5},{5,1},{9,13},{13,9},{2,6},{6,2},{1... | collective-permute-start | bytes 98312 | tf_op jit(solution)/shard_map/ppermute | solution.py:741
  30.6 3.4 %collective-permute-start.10 = (bf16[128,128]{1,0:T(8,128)(2,1)S(1)}, bf16[128,128]{1,0:T(8,128)(2,1)S(1)}, u32[]{:S(2)}, u32[]{:S(2)}) collective-permute-start(bf16[128,128]{1,0:T(8,128)(2,1)S(1)} %get-tuple-element.36), channel_id=1, source_target_pairs={{4,8},{8,4},{12,0},{0,12},{5,9},{9,5},{13,1},{1,13},{6,10},{10,6},... | collective-permute-start | bytes 98312 | tf_op jit(solution)/shard_map/ppermute | solution.py:742
  31.3 2.8 %copy-start.1 = (bf16[1024,512]{1,0:T(8,128)(2,1)S(1)}, bf16[1024,512]{1,0:T(8,128)(2,1)}, u32[]{:S(2)}) copy-start(bf16[1024,512]{1,0:T(8,128)(2,1)} %constant.5.clone.table_ref) | copy-start | bytes 3145732
  34.0 0.7 %copy-start.13 = (f32[128]{0:T(128)S(1)}, f32[128]{0:T(128)}, u32[]{:S(2)}) copy-start(f32[128]{0:T(128)} %param.18) | copy-start | bytes 1540

commit v7 on v6

--- a/solution.py
+++ b/solution.py
@@ -121,32 +121,53 @@
 
 
 def forward_kernel(
-    groups_x, paired, x_ref, wet_ref, diff_ref, table_ref, s_ref, *refs
+    groups_x, paired, x_hbm, wet_hbm, diff_hbm, table_hbm, s_hbm, kept_hbm, *refs
 ):
-    kept_ref, y_ref, e1_ref, e3_ref, e2_ref, e4_ref = refs[:6]
+    del s_hbm, kept_hbm
+    outs = 5 if paired else 6
+    y_hbm, *message_hbm = refs[:outs]
+    y_ref, *message_ref = refs[outs : 2 * outs]
+    e1_ref, e3_ref, e2_ref, e4_ref = message_ref[:4]
     if not paired:
-        pq_ref = refs[6]
-    kept_ref[...] = s_ref[...]
-    flat_ref, edge_ref = refs[-2:]
-    _, rows, channels, columns = x_ref.shape
+        pq_ref = message_ref[4]
+    x_ref, wet_ref, diff_ref, table_ref, flat_ref, edge_ref, sem, out_sem = refs[2 * outs :]
+    rows, channels, columns = x_ref.shape
     half = columns // 2
     row_group = lax.axis_index("gx")
     col_group = lax.axis_index("gy")
     is_atmos = lax.axis_index("comp") == 0
 
+    x_copy = pltpu.make_async_copy(x_hbm.at[0], x_ref, sem.at[0])
+    y_copies = [
+        pltpu.make_async_copy(y_ref.at[r], y_hbm.at[r], out_sem.at[r]) for r in range(rows)
+    ]
+    message_copies = [
+        pltpu.make_async_copy(ref, hbm, out_sem.at[rows + k])
+        for k, (ref, hbm) in enumerate(zip(message_ref, message_hbm))
+    ]
+
     @pl.when(is_atmos)
     def _():
+        table_copy = pltpu.make_async_copy(table_hbm, table_ref, sem.at[1])
+        diff_copy = pltpu.make_async_copy(diff_hbm, diff_ref, sem.at[2])
+        for copy in (x_copy, table_copy, diff_copy):
+            copy.start()
+        x_copy.wait()
         first = col_group * channels
         for r in range(rows):
-            left, right = x_ref[0, r, :, :half], x_ref[0, r, :, half:]
+            left, right = x_ref[r, :, :half], x_ref[r, :, half:]
             flat_ref[r * channels : (r + 1) * channels, :half] = (left + right).astype(bf16)
             flat_ref[r * channels : (r + 1) * channels, half:] = (left - right).astype(bf16)
+        table_copy.wait()
         for k in range(2):
             lanes = slice(k * half, (k + 1) * half)
             part = jnp.dot(
                 flat_ref[:, lanes], table_ref[lanes, :], preferred_element_type=f32
             )
             y_ref[:, :, lanes] = part.reshape(rows, channels, half)
+        for copy in y_copies:
+            copy.start()
+        diff_copy.wait()
         diff = channel_column(diff_ref[...], channels, first)
         total = rows * groups_x
         base = (row_group * rows).astype(f32)
@@ -174,9 +195,18 @@
                 else:
                     pq_ref[0, :, lanes] = p.astype(bf16)
                     pq_ref[1, :, lanes] = q.astype(bf16)
+        for copy in message_copies:
+            copy.start()
+        for copy in y_copies + message_copies:
+            copy.wait()
 
     @pl.when(jnp.logical_not(is_atmos))
     def _():
+        wet_copy = pltpu.make_async_copy(wet_hbm, wet_ref, sem.at[1])
+        for copy in (x_copy, wet_copy):
+            copy.start()
+        x_copy.wait()
+        wet_copy.wait()
         levels = channels // 2
         lines = 2 * channels
         even_x = row_group % 2 == 0
@@ -187,11 +217,11 @@
         def put(out, last):
             @pl.when(last)
             def _():
-                out[0:lines, :] = x_ref[0, rows - 2 :].reshape(lines, columns).astype(bf16)
+                out[0:lines, :] = x_ref[rows - 2 :].reshape(lines, columns).astype(bf16)
 
             @pl.when(jnp.logical_not(last))
             def _():
-                out[0:lines, :] = x_ref[0, :2].reshape(lines, columns).astype(bf16)
+                out[0:lines, :] = x_ref[:2].reshape(lines, columns).astype(bf16)
 
             out[lines : lines + 16, :] = wet
 
@@ -203,7 +233,7 @@
                 for t in range(2):
                     at = (r * 2 + t) * 2
                     c = t * levels + level
-                    edge_ref[at : at + 2, :] = x_ref[0, r, c : c + 2, :]
+                    edge_ref[at : at + 2, :] = x_ref[r, c : c + 2, :]
             out[...] = edge_ref[...].astype(bf16)
 
         @pl.when(even_y)
@@ -216,15 +246,22 @@
             put_edges(e2_ref, 0)
             put_edges(e4_ref, levels - 2)
 
-
-def regrid_kernel(
-    surface_ref, a_src, a_dst, a_count, a_weight, m_src, m_dst, m_count, m_weight,
-    _, __,
-    land_ref, sent_ref, weight_ref, gath_ref, val_ref, sem,
-):
+        for copy in message_copies:
+            copy.start()
+        for copy in message_copies:
+            copy.wait()
+
+
+def regrid_kernel(n_surfaces, *refs):
+    surfaces = refs[:n_surfaces]
+    (
+        a_src, a_dst, a_count, a_weight, m_src, m_dst, m_count, m_weight,
+        _, _,
+        land_ref, sent_ref, weight_ref, gath_ref, val_ref, sem,
+    ) = refs[n_surfaces:]
     is_atmos = lax.axis_index("comp") == 0
     blocks, points = val_ref.shape
-    cells = surface_ref.shape[0]
+    cells = surfaces[0].shape[0]
     rows = 8
 
     @pl.when(is_atmos)
@@ -249,7 +286,7 @@
     dst_row, dst_lane = split(dst)
     lane_iota = lax.broadcasted_iota(jnp.int32, (LANES, points), 0)
     row_iota = lax.broadcasted_iota(jnp.int32, (cells, points), 0)
-    table = surface_ref[...]
+    table = sum(surface[...].astype(f32) for surface in surfaces).astype(bf16)
     for b in range(blocks):
         hot = jnp.where(lane_iota == src_lane[b : b + 1], 1.0, 0.0).astype(bf16)
         picked = jnp.dot(table, hot, preferred_element_type=f32)
@@ -291,7 +328,7 @@
     sent_ref[...] = land.astype(bf16)
 
 
-def heat_kernel(rows, e2_ref, e4_ref, land_ref, part_ref, sum_ref, near_ref, far_ref):
+def heat_kernel(rows, e2_ref, e4_ref, land_ref, part_ref, _, sum_ref, near_ref, far_ref):
     cells = land_ref.shape[0]
     columns = cells // rows * LANES
     even_x = lax.axis_index("gx") % 2 == 0
@@ -316,13 +353,26 @@
     far_ref[cells:, :] = jnp.where(even_x, first, last).astype(bf16)
 
 
-def steps_kernel(
+def advance(ref, r, t, coefs, size):
+    ring, columns = ref.shape[2:]
+    whole = ref[r, t]
+    up = pltpu.roll(whole, 1, 0)[:size]
+    down = pltpu.roll(whole, ring - 1, 0)[:size]
+    mid = whole[:size]
+    total = coefs[0] * mid + coefs[5] * (up + down)
+    total = total + coefs[1] * ref[r - 1, t, 0:size, :]
+    total = total + coefs[2] * ref[r + 1, t, 0:size, :]
+    total = total + coefs[3] * pltpu.roll(mid, 1, 1)
+    return total + coefs[4] * pltpu.roll(mid, columns - 1, 1)
+
+
+def first_step_kernel(
     groups_x, groups_y, paired, x_ref, wet_ref, diff_ref, y_ref, e1_ref, e3_ref,
     e2_ref, e4_ref, *refs,
 ):
     if not paired:
         pin_ref, qin_ref = refs[:2]
-    base_ref, zb_ref, c_ref, z_ref, t0_ref, t1_ref, w_ref = refs[-7:]
+    zb_ref, c_ref, t1_ref, z_ref, t0_ref, w_ref = refs[-6:]
     _, rows, channels, columns = x_ref.shape
     row_group = lax.axis_index("gx")
     col_group = lax.axis_index("gy")
@@ -444,17 +494,6 @@
                     bottom, ref[r, t, levels - 1 : levels, :], ref[r, t, levels : levels + 1, :]
                 )
 
-        def advance(ref, r, t, coefs, size):
-            whole = ref[r, t]
-            up = pltpu.roll(whole, 1, 0)[:size]
-            down = pltpu.roll(whole, ring - 1, 0)[:size]
-            mid = whole[:size]
-            total = coefs[0] * mid + coefs[5] * (up + down)
-            total = total + coefs[1] * ref[r - 1, t, 0:size, :]
-            total = total + coefs[2] * ref[r + 1, t, 0:size, :]
-            total = total + coefs[3] * pltpu.roll(mid, 1, 1)
-            return total + coefs[4] * pltpu.roll(mid, columns - 1, 1)
-
         def first(r, carry):
             coefs = [c_ref[k, pl.ds(r, 1), :] for k in range(6)]
             close(t0_ref, r + 1)
@@ -465,29 +504,15 @@
 
         lax.fori_loop(0, span, first, 0)
 
-        def second(r, carry):
-            coefs = [c_ref[k, pl.ds(r, 1), :] for k in range(6)]
-            for t in range(2):
-                c = t * levels
-                base_ref[r - 1, c : c + levels, :] = advance(t1_ref, r, t, coefs, levels)
-            return carry
-
-        lax.fori_loop(1, span - 1, second, 0)
-
-
-def last_kernel(
-    groups_x, groups_y, gain_ref, table_ref, base_ref, zb_ref, c_ref, sum_ref, near_ref,
-    far_ref, out_ref, e_ref,
-):
-    _, rows, channels, columns = out_ref.shape
-    row_group = lax.axis_index("gx")
-    col_group = lax.axis_index("gy")
+
+def second_step_kernel(gain_ref, table_ref, zb_ref, c_ref, t1_ref, base_ref, column_ref):
+    rows, channels, columns = base_ref.shape
     is_atmos = lax.axis_index("comp") == 0
 
     @pl.when(is_atmos)
     def _():
-        response = channel_column(gain_ref[...], channels, col_group * channels)
-        forcing = from_tiles(sum_ref[...], rows)
+        response = channel_column(gain_ref[...], channels, lax.axis_index("gy") * channels)
+        column_ref[...] = jnp.broadcast_to(response, column_ref.shape)
         half = columns // 2
         step = 256
         for n in range(0, half, step):
@@ -499,11 +524,40 @@
                 ).reshape(rows, channels, step)
                 for k in range(2)
             ]
+            base_ref[:, :, n : n + step] = even + odd
+            base_ref[:, :, n + half : n + half + step] = even - odd
+
+    @pl.when(jnp.logical_not(is_atmos))
+    def _():
+        levels = channels // 2
+
+        def second(r, carry):
+            coefs = [c_ref[k, pl.ds(r, 1), :] for k in range(6)]
+            for t in range(2):
+                c = t * levels
+                base_ref[r - 1, c : c + levels, :] = advance(t1_ref, r, t, coefs, levels)
+            return carry
+
+        lax.fori_loop(1, rows + 1, second, 0)
+
+
+def last_kernel(
+    groups_x, groups_y, column_ref, base_ref, c_ref, sum_ref, near_ref, far_ref, out_ref, e_ref
+):
+    _, rows, channels, columns = out_ref.shape
+    row_group = lax.axis_index("gx")
+    col_group = lax.axis_index("gy")
+    is_atmos = lax.axis_index("comp") == 0
+
+    @pl.when(is_atmos)
+    def _():
+        for k in range(columns // LANES):
+            lanes = slice(k * LANES, (k + 1) * LANES)
             for r in range(rows):
-                for lane, part in ((n, even[r] + odd[r]), (n + half, even[r] - odd[r])):
-                    out_ref[0, r, :, lane : lane + step] = (
-                        part + response * forcing[r : r + 1, lane : lane + step]
-                    )
+                at = k * rows + r
+                out_ref[0, r, :, lanes] = (
+                    base_ref[r, :, lanes] + column_ref[...] * sum_ref[at : at + 1, :]
+                )
 
     @pl.when(jnp.logical_not(is_atmos))
     def _():
@@ -619,27 +673,39 @@
     partial_surface, y, e1, e3, e2, e4, *sums = pl.pallas_call(
         functools.partial(forward_kernel, groups_x, paired),
         out_shape=shapes,
-        in_specs=[vmem] * 5,
-        out_specs=[vmem] * len(shapes),
-        scratch_shapes=[
+        in_specs=[hbm] * 4 + [anywhere],
+        out_specs=[anywhere] + [hbm] * (len(shapes) - 1),
+        scratch_shapes=[pltpu.VMEM(out.shape, out.dtype) for out in shapes[1:]]
+        + [
+            pltpu.VMEM((rows, channels, columns), f32),
+            pltpu.VMEM((rows, columns), jnp.int32),
+            pltpu.VMEM(diff_row.shape, f32),
+            pltpu.VMEM(forward.shape, bf16),
             pltpu.VMEM((rows * channels, columns), bf16),
             pltpu.VMEM((4 * rows, columns), f32),
+            pltpu.SemaphoreType.DMA((3,)),
+            pltpu.SemaphoreType.DMA((rows + len(shapes) - 2,)),
         ],
-        compiler_params=params(),
+        input_output_aliases={4: 0},
+        compiler_params=pltpu.CompilerParams(vmem_limit_bytes=58 * 2**20),
         name="forward_or_halos",
     )(fields, wet_cells, diff_row, forward, partial_surface)
 
-    def sum_masks():
-        mask = 1
-        while mask < groups_y:
-            yield [(j, j ^ mask) for j in range(groups_y)]
-            mask *= 2
+    masks = [1 << bit for bit in range(groups_y.bit_length() - 1)]
+
+    def sum_route(mask):
+        return [(j, j ^ mask) for j in range(groups_y)]
+
+    def partner_route(mask):
+        return both_ways([(j, groups_y + (j ^ mask)) for j in range(groups_y)])
 
     surface = partial_surface
-    for route in sum_masks():
-        surface = surface + lax.ppermute(coarse, "gy", route).astype(f32)
+    for mask in masks[:-1]:
+        surface = surface + lax.ppermute(coarse, "gy", sum_route(mask)).astype(f32)
         coarse = surface.astype(bf16)
-    surface = lax.ppermute(coarse, "comp", [(0, 1), (1, 0)])
+    surfaces = [
+        lax.ppermute(coarse, ("comp", "gy"), partner_route(mask)) for mask in masks[-1:] + [0]
+    ]
 
     def ring_pairs(count, odd):
         return [(a, (a + 1) % count) for a in range(odd, count, 2)]
@@ -665,9 +731,10 @@
     e4 = lax.ppermute(e4, axes, level_route(1))
 
     landing, sent = pl.pallas_call(
-        regrid_kernel,
+        functools.partial(regrid_kernel, len(surfaces)),
         out_shape=[shape((cells, LANES), f32), shape((cells, LANES), bf16)],
-        in_specs=[vmem, vmem, vmem, smem, hbm, vmem, vmem, smem, hbm, anywhere, anywhere],
+        in_specs=[vmem] * len(surfaces)
+        + [vmem, vmem, smem, hbm, vmem, vmem, smem, hbm, anywhere, anywhere],
         out_specs=[vmem] * 2,
         scratch_shapes=[
             pltpu.VMEM((blocks, points, points), bf16),
@@ -678,16 +745,15 @@
         compiler_params=params(),
         name="regrid_blocks",
     )(
-        surface,
+        *surfaces,
         a2o_source, a2o_target, a2o_count, a2o_weight,
         marine_air_input_index, marine_air_output_index,
         marine_air_piece_tally, marine_air_piece_factor, e1, e3,
     )
-    *early, final = sum_masks()
-    for route in early:
-        landing = landing + lax.ppermute(sent, "gy", route).astype(f32)
+    for mask in masks[:-1]:
+        landing = landing + lax.ppermute(sent, "gy", sum_route(mask)).astype(f32)
         sent = landing.astype(bf16)
-    part = lax.ppermute(sent, "gy", final)
+    part = lax.ppermute(sent, "gy", sum_route(masks[-1]))
 
     extra = []
     if not paired:
@@ -706,23 +772,22 @@
             jnp.sum(jnp.where((gap < 0)[:, None, None], decay * q, 0.0), axis=0),
         ]
     ring = channels // 2 + 8
-    base, damped, coefs = pl.pallas_call(
-        functools.partial(steps_kernel, groups_x, groups_y, paired),
+    damped, coefs, stepped = pl.pallas_call(
+        functools.partial(first_step_kernel, groups_x, groups_y, paired),
         out_shape=[
-            shape((rows, channels, columns), f32),
             shape((rows * channels, columns), bf16),
             shape((7, 16, columns), f32),
+            shape((rows + 2, 2, ring, columns), f32),
         ],
         in_specs=[vmem] * (8 + len(extra)),
         out_specs=[vmem] * 3,
         scratch_shapes=[
             pltpu.VMEM((rows, channels, LANES), f32),
             pltpu.VMEM((rows + 4, 2, ring, columns), f32),
-            pltpu.VMEM((rows + 2, 2, ring, columns), f32),
             pltpu.VMEM((16, columns), f32),
         ],
         compiler_params=params(),
-        name="damping_or_ocean_steps",
+        name="damping_or_first_step",
     )(fields, wet_cells, diff_row, y, e1, e3, e2, e4, *extra)
 
     surface_sum, near, far = pl.pallas_call(
@@ -732,23 +797,31 @@
             shape((cells + columns // 16, LANES), bf16),
             shape((cells + columns // 16, LANES), bf16),
         ],
-        in_specs=[vmem] * 4,
+        in_specs=[vmem] * 4 + [anywhere],
         out_specs=[vmem] * 3,
         compiler_params=params(),
         name="surface_sum",
-    )(e2, e4, landing, part)
+    )(e2, e4, landing, part, coefs)
 
     near = lax.ppermute(near, "gx", both_ways(ring_pairs(groups_x, 0)))
     far = lax.ppermute(far, "gx", both_ways(ring_pairs(groups_x, 1)))
+    base, column = pl.pallas_call(
+        second_step_kernel,
+        out_shape=[shape((rows, channels, columns), f32), shape((channels, LANES), f32)],
+        in_specs=[vmem] * 5,
+        out_specs=[vmem] * 2,
+        compiler_params=params(),
+        name="inverse_or_second_step",
+    )(gain_row, inverse, damped, coefs, stepped)
     return pl.pallas_call(
         functools.partial(last_kernel, groups_x, groups_y),
         out_shape=shape(fields.shape, f32),
-        in_specs=[vmem] * 8,
+        in_specs=[vmem] * 6,
         out_specs=vmem,
         scratch_shapes=[pltpu.VMEM((16, columns), f32)],
         compiler_params=params(),
-        name="inverse_or_heat",
-    )(gain_row, inverse, base, damped, coefs, surface_sum, near, far)
+        name="add_surface_terms",
+    )(column, base, coefs, surface_sum, near, far)
 
 
 def solution(mesh):

time: 36.4 us -> 34.4 us (0.945)
  the two profiles are of different devices: /device:TPU:0 before, /device:TPU:5 now
where the time goes in v7:
time: 34.4 us; the launch traced here: 34.2 us
  starting transfers between devices  16.1 us (47%)
  Pallas kernels  11.1 us (32%)
  waiting for transfers between devices  4.7 us (14%)
  between operations  1.51 us (4%)
  other arithmetic  0.77 us (2%)
    ppermute x2, starting transfers between devices, local(): lax.ppermute(coarse, ('comp', 'gy'), partner_route(mask))  3.85 us
    ppermute x1, starting transfers between devices, local(): near = lax.ppermute(near, 'gx', both_ways(ring_pairs(groups_x, 0)))  3.54 us
    pallas_call x1, Pallas kernels, local(): pl.pallas_call(functools.partial(forward_kernel, groups_x, paired), out_s...  2.38 us
    pallas_call x1, Pallas kernels, local(): pl.pallas_call(functools.partial(first_step_kernel, groups_x, groups_y, p...  2.3 us
    pallas_call x1, Pallas kernels, local(): pl.pallas_call(functools.partial(regrid_kernel, len(surfaces)), out_shape...  2.28 us
    ppermute x1, starting transfers between devices, local(): e4 = lax.ppermute(e4, axes, level_route(1))  2.13 us
    ppermute x1, waiting for transfers between devices, local(): far = lax.ppermute(far, 'gx', both_ways(ring_pairs(groups_x, 1)))  2.06 us
    pallas_call x1, Pallas kernels, local(): pl.pallas_call(surface_kernel, out_shape=[shape((cells, LANES), f32), sha...  1.73 us
  transfers between devices with their start and end apart: 11, of which 3 were waited for; matrix products, arithmetic and copies ran while one was open for 2% of the time, Pallas kernels for 17%

profile of v7, /device:TPU:5, one launch (start us, length us, event | category | flops | bytes accessed | tf_op | source)
XLA Modules:
  0.0 34.2 jit_solution(6535457845080730836)
XLA Ops:
  0.0 0.0 copy-start.2
  0.0 0.0 copy-start.9
  0.0 0.0 copy-start.8
  0.0 0.0 copy-start.1
  0.0 0.0 copy-start.7
  0.0 0.0 copy-start.6
  0.0 1.7 %surface_partials.1 = (f32[64,128]{1,0:T(8,128)}, bf16[64,128]{1,0:T(8,128)(2,1)}) custom-call(f32[1,8,32,1024]{3,2,1,0:T(8,128)} %x_ref.1, f32[1,128]{1,0:T(1,128)} %bitcast.6), custom_call_target="tpu_custom_call" | custom-call | tf_op jit(solution)/shard_map/surface_partials/pallas_call | solution.py:646
  1.8 1.4 %collective-permute-start.4 = (bf16[64,128]{1,0:T(8,128)(2,1)}, bf16[64,128]{1,0:T(8,128)(2,1)S(1)}, u32[]{:S(2)}, u32[]{:S(2)}) collective-permute-start(bf16[64,128]{1,0:T(8,128)(2,1)} %get-tuple-element.35), channel_id=1, source_target_pairs={{0,1},{1,0},{2,3},{3,2},{4,5},{5,4},{6,7},{7,6},{8,9},{9,8},{10,11... | collective-permute-start | bytes 49160 | tf_op jit(solution)/shard_map/ppermute | solution.py:704
  3.1 0.0 copy-start
  3.1 0.0 copy-start.5
  3.1 0.0 copy-start.10
  3.1 2.4 %forward_or_halos.1 = (f32[64,128]{1,0:T(8,128)}, f32[8,32,1024]{2,1,0:T(8,128)}, bf16[80,1024]{1,0:T(8,128)(2,1)}, bf16[80,1024]{1,0:T(8,128)(2,1)}, bf16[32,10...) custom-call(f32[1,8,32,1024]{3,2,1,0:T(8,128)} %x_ref.1, s32[8,1024]{1,0:T(8,128)} %wet_ref.1, ...), custom_call_target="tpu_custom_call", output_to_operand_aliasing={{0}: (4, {})} | custom-call | tf_op jit(solution)/shard_map/forward_or_halos/pallas_call | solution.py:673
  5.5 0.0 copy-start.13
  5.5 0.0 copy-start.12
  5.6 0.0 copy-start.3
  5.6 1.0 %collective-permute-start = (bf16[80,1024]{1,0:T(8,128)(2,1)}, bf16[80,1024]{1,0:T(8,128)(2,1)S(1)}, u32[]{:S(2)}, u32[]{:S(2)}) collective-permute-start(bf16[80,1024]{1,0:T(8,128)(2,1)} %get-tuple-element.25), channel_id=1, source_target_pairs={{0,4},{4,0},{8,12},{12,8},{1,5},{5,1},{9,13},{13,9},{2,6},{6,2},{1... | collective-permute-start | bytes 491528 | tf_op jit(solution)/shard_map/ppermute | solution.py:727
  6.6 1.2 %collective-permute-start.1 = (bf16[80,1024]{1,0:T(8,128)(2,1)}, bf16[80,1024]{1,0:T(8,128)(2,1)S(1)}, u32[]{:S(2)}, u32[]{:S(2)}) collective-permute-start(bf16[80,1024]{1,0:T(8,128)(2,1)} %get-tuple-element.26), channel_id=1, source_target_pairs={{4,8},{8,4},{12,0},{0,12},{5,9},{9,5},{13,1},{1,13},{6,10},{10,6},... | collective-permute-start | bytes 491528 | tf_op jit(solution)/shard_map/ppermute | solution.py:728
  7.8 0.0 collective-permute-done.4
  7.8 0.8 %add_convert_fusion = bf16[64,128]{1,0:T(8,128)(2,1)S(1)} fusion(f32[64,128]{1,0:T(8,128)} %get-tuple-element.34, bf16[64,128]{1,0:T(8,128)(2,1)S(1)} %collective-permute-done.4), kind=kLoop, calls=%fused_computation.1 | loop fusion | flops 24576 | bytes 65536 | tf_op jit(solution)/shard_map/convert_element_type | solution.py:705
  8.5 1.8 %collective-permute-start.6 = (bf16[64,128]{1,0:T(8,128)(2,1)S(1)}, bf16[64,128]{1,0:T(8,128)(2,1)S(1)}, u32[]{:S(2)}, u32[]{:S(2)}) collective-permute-start(bf16[64,128]{1,0:T(8,128)(2,1)S(1)} %add_convert_fusion), channel_id=1, source_target_pairs={{0,16},{16,0},{1,17},{17,1},{2,18},{18,2},{3,19},{19,3},{4,20},{20... | collective-permute-start | bytes 49160 | tf_op jit(solution)/shard_map/ppermute | solution.py:707
  10.3 2.1 %collective-permute-start.5 = (bf16[64,128]{1,0:T(8,128)(2,1)S(1)}, bf16[64,128]{1,0:T(8,128)(2,1)S(1)}, u32[]{:S(2)}, u32[]{:S(2)}) collective-permute-start(bf16[64,128]{1,0:T(8,128)(2,1)S(1)} %add_convert_fusion), channel_id=1, source_target_pairs={{0,18},{18,0},{1,19},{19,1},{2,16},{16,2},{3,17},{17,3},{4,22},{22... | collective-permute-start | bytes 49160 | tf_op jit(solution)/shard_map/ppermute | solution.py:707
  13.7 0.0 collective-permute-done.6.refs_1_
  13.7 1.0 %collective-permute-done.5.refs_0_ = bf16[64,128]{1,0:T(8,128)(2,1)S(1)} collective-permute-done((bf16[64,128]{1,0:T(8,128)(2,1)S(1)}, bf16[64,128]{1,0:T(8,128)(2,1)S(1)}, u32[]{:S(2)}, u32[]{:S(2)}) %collective-permute-start.5) | collective-permute-done | bytes 16416 | tf_op jit(solution)/shard_map/ppermute | solution.py:707
  14.7 0.0 collective-permute-done.e1_ref.refs_10_
  14.7 0.0 collective-permute-done.1.e3_ref.refs_11_
  14.7 0.0 copy-done.2
  14.7 0.0 copy-done.9
  14.8 0.0 copy-done.8
  14.8 0.0 copy-done.1
  14.8 0.0 copy-done.7
  14.8 0.0 copy-done.6
  14.8 2.3 %regrid_blocks.1 = (f32[64,128]{1,0:T(8,128)S(1)}, bf16[64,128]{1,0:T(8,128)(2,1)S(1)}) custom-call(bf16[64,128]{1,0:T(8,128)(2,1)S(1)} %collective-permute-done.5.refs_0_, bf16[64,128]{1,0:T(8,128)(2,1)S(1)} %collective-permute-done.6.refs_1_, s32[1,1,32,128]{3,2,1,0:T(8,128)S(1)} %copy-done.6, s32[1,1,32,128]{3,2,1,0:T(8,128)S(1)} %copy-done.7, ...), custom_call_target="tpu_custom_call" | custom-call | tf_op jit(solution)/shard_map/regrid_blocks/pallas_call | solution.py:733
  17.1 0.0 copy-start.4
  17.1 0.0 copy-start.11
  17.1 0.2 collective-permute-start.7
  17.3 0.0 copy-done.13
  17.3 1.4 %collective-permute-start.2 = (bf16[32,1024]{1,0:T(8,128)(2,1)S(1)}, bf16[32,1024]{1,0:T(8,128)(2,1)S(1)}, u32[]{:S(2)}, u32[]{:S(2)}) collective-permute-start(bf16[32,1024]{1,0:T(8,128)(2,1)S(1)} %copy-done.13), channel_id=1, source_target_pairs={{16,17},{17,16},{18,19},{19,18},{0,8},{8,0},{1,9},{9,1},{2,10},{10... | collective-permute-start | bytes 196616 | tf_op jit(solution)/shard_map/ppermute | solution.py:730
  18.6 0.0 copy-done.12
  18.6 2.1 %collective-permute-start.3 = (bf16[32,1024]{1,0:T(8,128)(2,1)S(1)}, bf16[32,1024]{1,0:T(8,128)(2,1)S(1)}, u32[]{:S(2)}, u32[]{:S(2)}) collective-permute-start(bf16[32,1024]{1,0:T(8,128)(2,1)S(1)} %copy-done.12), channel_id=1, source_target_pairs={{17,18},{18,17},{1,2},{2,1},{19,16},{16,19},{3,0},{0,3},{21,22},{2... | collective-permute-start | bytes 196616 | tf_op jit(solution)/shard_map/ppermute | solution.py:731
  20.8 0.0 collective-permute-done.7
  20.8 1.3 %collective-permute-start.8 = (bf16[64,128]{1,0:T(8,128)(2,1)S(1)}, bf16[64,128]{1,0:T(8,128)(2,1)S(1)}, u32[]{:S(2)}, u32[]{:S(2)}) collective-permute-start(bf16[64,128]{1,0:T(8,128)(2,1)S(1)} %get-tuple-element.41), channel_id=1, source_target_pairs={{0,2},{1,3},{2,0},{3,1},{4,6},{5,7},{6,4},{7,5},{8,10},{9,11},{10,... | collective-permute-start | bytes 49160 | tf_op jit(solution)/shard_map/ppermute | solution.py:756
  22.1 0.0 collective-permute-done.2.e2_ref
  22.1 1.6 %collective-permute-done.3.e4_ref = bf16[32,1024]{1,0:T(8,128)(2,1)S(1)} collective-permute-done((bf16[32,1024]{1,0:T(8,128)(2,1)S(1)}, bf16[32,1024]{1,0:T(8,128)(2,1)S(1)}, u32[]{:S(2)}, u32[]{:S(2)}) %collective-permute-start.3) | collective-permute-done | bytes 65568 | tf_op jit(solution)/shard_map/ppermute | solution.py:731
  23.7 0.0 copy-done
  23.7 0.0 copy-done.5
  23.7 0.0 copy-done.10
  23.7 0.0 copy-done.3
  23.7 2.3 %damping_or_first_step.1 = (bf16[256,1024]{1,0:T(8,128)(2,1)S(1)}, f32[7,16,1024]{2,1,0:T(8,128)S(1)}, f32[10,2,24,1024]{3,2,1,0:T(8,128)S(1)}) custom-call(f32[1,8,32,1024]{3,2,1,0:T(8,128)S(1)} %copy-done, s32[8,1024]{1,0:T(8,128)S(1)} %copy-done.5, f32[1,128]{1,0:T(1,128)S(1)} %bitcast.4, f32[8,32,1024]{2,1,0:T(8,128)S(1)} %copy-done.3, ...), custom_call_target="tpu_custom_call" | custom-call | tf_op jit(solution)/shard_map/damping_or_first_step/pallas_call | solution.py:775
  26.0 0.0 collective-permute-done.8.part_ref
  26.1 3.5 %collective-permute-start.9 = (bf16[128,128]{1,0:T(8,128)(2,1)S(1)}, bf16[128,128]{1,0:T(8,128)(2,1)S(1)}, u32[]{:S(2)}, u32[]{:S(2)}) collective-permute-start(bf16[128,128]{1,0:T(8,128)(2,1)S(1)} %get-tuple-element.39), channel_id=1, source_target_pairs={{0,4},{4,0},{8,12},{12,8},{1,5},{5,1},{9,13},{13,9},{2,6},{6,2},{1... | collective-permute-start | bytes 98312 | tf_op jit(solution)/shard_map/ppermute | solution.py:806
  29.6 0.2 collective-permute-start.10
  29.8 0.0 copy-done.4
  29.8 0.0 copy-done.11
  29.8 1.1 %inverse_or_second_step.1 = (f32[8,32,1024]{2,1,0:T(8,128)S(1)}, f32[32,128]{1,0:T(8,128)S(1)}) custom-call(f32[1,128]{1,0:T(1,128)S(1)} %bitcast.5, bf16[1024,512]{1,0:T(8,128)(2,1)S(1)} %copy-done.4, bf16[256,1024]{1,0:T(8,128)(2,1)S(1)} %get-tuple-element.29.zb_ref, f32[7,16,1024]{2,1,0:T(8,128)S(1)} %get-tuple-element.30.c_ref._, ...), custom_call_target="tpu_custom_call" | custom-call | tf_op jit(solution)/shard_map/inverse_or_second_step/pallas_call | solution.py:808
  30.9 0.0 collective-permute-done.9.near_ref
  30.9 2.1 %collective-permute-done.10.far_ref = bf16[128,128]{1,0:T(8,128)(2,1)S(1)} collective-permute-done((bf16[128,128]{1,0:T(8,128)(2,1)S(1)}, bf16[128,128]{1,0:T(8,128)(2,1)S(1)}, u32[]{:S(2)}, u32[]{:S(2)}) %collective-permute-start.10) | collective-permute-done | bytes 32800 | tf_op jit(solution)/shard_map/ppermute | solution.py:807
  33.0 1.3 %add_surface_terms.1 = f32[1,8,32,1024]{3,2,1,0:T(8,128)} custom-call(f32[32,128]{1,0:T(8,128)S(1)} %get-tuple-element.32.column_ref, f32[8,32,1024]{2,1,0:T(8,128)S(1)} %get-tuple-element.33.base_ref, f32[7,16,1024]{2,1,0:T(8,128)S(1)} %get-tuple-element.30.c_ref._, f32[64,128]{1,0:T(8,128)S(1)} %get-tuple-element.38.sum_ref, ...), custom_call_target="tpu_custom_call" | custom-call | tf_op jit(solution)/shard_map/add_surface_terms/pallas_call | solution.py:816
  (2 shorter events, 0.1 us)
Async XLA Ops:
  0.0 14.7 %copy-start.2 = (bf16[1,1,32,128,128]{4,3,2,1,0:T(8,128)(2,1)S(1)}, bf16[1,1,32,128,128]{4,3,2,1,0:T(8,128)(2,1)}, u32[]{:S(2)}) copy-start(bf16[1,1,32,128,128]{4,3,2,1,0:T(8,128)(2,1)} %refs_9_.1) | copy-start | bytes 3145732
  0.0 14.7 %copy-start.9 = (s32[1,1,32,128]{3,2,1,0:T(8,128)S(1)}, s32[1,1,32,128]{3,2,1,0:T(8,128)}, u32[]{:S(2)}) copy-start(s32[1,1,32,128]{3,2,1,0:T(8,128)} %refs_7_.1) | copy-start | bytes 49156
  0.0 14.8 %copy-start.8 = (s32[1,1,32,128]{3,2,1,0:T(8,128)S(1)}, s32[1,1,32,128]{3,2,1,0:T(8,128)}, u32[]{:S(2)}) copy-start(s32[1,1,32,128]{3,2,1,0:T(8,128)} %refs_6_.1) | copy-start | bytes 49156
  0.0 14.8 %copy-start.1 = (bf16[1,1,32,128,128]{4,3,2,1,0:T(8,128)(2,1)S(1)}, bf16[1,1,32,128,128]{4,3,2,1,0:T(8,128)(2,1)}, u32[]{:S(2)}) copy-start(bf16[1,1,32,128,128]{4,3,2,1,0:T(8,128)(2,1)} %refs_5_.1) | copy-start | bytes 3145732
  0.0 14.8 %copy-start.7 = (s32[1,1,32,128]{3,2,1,0:T(8,128)S(1)}, s32[1,1,32,128]{3,2,1,0:T(8,128)}, u32[]{:S(2)}) copy-start(s32[1,1,32,128]{3,2,1,0:T(8,128)} %refs_3_.1) | copy-start | bytes 49156
  0.0 14.8 %copy-start.6 = (s32[1,1,32,128]{3,2,1,0:T(8,128)S(1)}, s32[1,1,32,128]{3,2,1,0:T(8,128)}, u32[]{:S(2)}) copy-start(s32[1,1,32,128]{3,2,1,0:T(8,128)} %refs_2_.1) | copy-start | bytes 49156
  1.8 6.0 %collective-permute-start.4 = (bf16[64,128]{1,0:T(8,128)(2,1)}, bf16[64,128]{1,0:T(8,128)(2,1)S(1)}, u32[]{:S(2)}, u32[]{:S(2)}) collective-permute-start(bf16[64,128]{1,0:T(8,128)(2,1)} %get-tuple-element.35), channel_id=1, source_target_pairs={{0,1},{1,0},{2,3},{3,2},{4,5},{5,4},{6,7},{7,6},{8,9},{9,8},{10,11... | collective-permute-start | bytes 49160 | tf_op jit(solution)/shard_map/ppermute | solution.py:704
  3.1 20.5 %copy-start = (f32[1,8,32,1024]{3,2,1,0:T(8,128)S(1)}, f32[1,8,32,1024]{3,2,1,0:T(8,128)}, u32[]{:S(2)}) copy-start(f32[1,8,32,1024]{3,2,1,0:T(8,128)} %x_ref.1) | copy-start | bytes 3145732
  3.1 20.5 %copy-start.5 = (s32[8,1024]{1,0:T(8,128)S(1)}, s32[8,1024]{1,0:T(8,128)}, u32[]{:S(2)}) copy-start(s32[8,1024]{1,0:T(8,128)} %wet_ref.1) | copy-start | bytes 98308
  3.1 20.5 %copy-start.10 = (f32[128]{0:T(128)S(1)}, f32[128]{0:T(128)}, u32[]{:S(2)}) copy-start(f32[128]{0:T(128)} %param.19) | copy-start | bytes 1540
  5.5 11.8 %copy-start.13 = (bf16[32,1024]{1,0:T(8,128)(2,1)S(1)}, bf16[32,1024]{1,0:T(8,128)(2,1)}, u32[]{:S(2)}) copy-start(bf16[32,1024]{1,0:T(8,128)(2,1)} %get-tuple-element.27) | copy-start | bytes 196612
  5.5 13.1 %copy-start.12 = (bf16[32,1024]{1,0:T(8,128)(2,1)S(1)}, bf16[32,1024]{1,0:T(8,128)(2,1)}, u32[]{:S(2)}) copy-start(bf16[32,1024]{1,0:T(8,128)(2,1)} %get-tuple-element.28) | copy-start | bytes 196612
  5.6 18.1 %copy-start.3 = (f32[8,32,1024]{2,1,0:T(8,128)S(1)}, f32[8,32,1024]{2,1,0:T(8,128)}, u32[]{:S(2)}) copy-start(f32[8,32,1024]{2,1,0:T(8,128)} %get-tuple-element.24.y_ref) | copy-start | bytes 3145732
  5.6 9.2 %collective-permute-start = (bf16[80,1024]{1,0:T(8,128)(2,1)}, bf16[80,1024]{1,0:T(8,128)(2,1)S(1)}, u32[]{:S(2)}, u32[]{:S(2)}) collective-permute-start(bf16[80,1024]{1,0:T(8,128)(2,1)} %get-tuple-element.25), channel_id=1, source_target_pairs={{0,4},{4,0},{8,12},{12,8},{1,5},{5,1},{9,13},{13,9},{2,6},{6,2},{1... | collective-permute-start | bytes 491528 | tf_op jit(solution)/shard_map/ppermute | solution.py:727
  6.6 8.2 %collective-permute-start.1 = (bf16[80,1024]{1,0:T(8,128)(2,1)}, bf16[80,1024]{1,0:T(8,128)(2,1)S(1)}, u32[]{:S(2)}, u32[]{:S(2)}) collective-permute-start(bf16[80,1024]{1,0:T(8,128)(2,1)} %get-tuple-element.26), channel_id=1, source_target_pairs={{4,8},{8,4},{12,0},{0,12},{5,9},{9,5},{13,1},{1,13},{6,10},{10,6},... | collective-permute-start | bytes 491528 | tf_op jit(solution)/shard_map/ppermute | solution.py:728
  8.5 5.1 %collective-permute-start.6 = (bf16[64,128]{1,0:T(8,128)(2,1)S(1)}, bf16[64,128]{1,0:T(8,128)(2,1)S(1)}, u32[]{:S(2)}, u32[]{:S(2)}) collective-permute-start(bf16[64,128]{1,0:T(8,128)(2,1)S(1)} %add_convert_fusion), channel_id=1, source_target_pairs={{0,16},{16,0},{1,17},{17,1},{2,18},{18,2},{3,19},{19,3},{4,20},{20... | collective-permute-start | bytes 49160 | tf_op jit(solution)/shard_map/ppermute | solution.py:707
  10.3 4.4 %collective-permute-start.5 = (bf16[64,128]{1,0:T(8,128)(2,1)S(1)}, bf16[64,128]{1,0:T(8,128)(2,1)S(1)}, u32[]{:S(2)}, u32[]{:S(2)}) collective-permute-start(bf16[64,128]{1,0:T(8,128)(2,1)S(1)} %add_convert_fusion), channel_id=1, source_target_pairs={{0,18},{18,0},{1,19},{19,1},{2,16},{16,2},{3,17},{17,3},{4,22},{22... | collective-permute-start | bytes 49160 | tf_op jit(solution)/shard_map/ppermute | solution.py:707
  17.1 12.7 %copy-start.4 = (bf16[1024,512]{1,0:T(8,128)(2,1)S(1)}, bf16[1024,512]{1,0:T(8,128)(2,1)}, u32[]{:S(2)}) copy-start(bf16[1024,512]{1,0:T(8,128)(2,1)} %constant.5.clone.table_ref) | copy-start | bytes 3145732
  17.1 12.7 %copy-start.11 = (f32[128]{0:T(128)S(1)}, f32[128]{0:T(128)}, u32[]{:S(2)}) copy-start(f32[128]{0:T(128)} %param.18) | copy-start | bytes 1540
  17.1 3.7 %collective-permute-start.7 = (bf16[64,128]{1,0:T(8,128)(2,1)S(1)}, bf16[64,128]{1,0:T(8,128)(2,1)S(1)}, u32[]{:S(2)}, u32[]{:S(2)}) collective-permute-start(bf16[64,128]{1,0:T(8,128)(2,1)S(1)} %get-tuple-element.37), channel_id=1, source_target_pairs={{0,1},{1,0},{2,3},{3,2},{4,5},{5,4},{6,7},{7,6},{8,9},{9,8},{10,11... | collective-permute-start | bytes 49160 | tf_op jit(solution)/shard_map/ppermute | solution.py:754
  17.3 4.8 %collective-permute-start.2 = (bf16[32,1024]{1,0:T(8,128)(2,1)S(1)}, bf16[32,1024]{1,0:T(8,128)(2,1)S(1)}, u32[]{:S(2)}, u32[]{:S(2)}) collective-permute-start(bf16[32,1024]{1,0:T(8,128)(2,1)S(1)} %copy-done.13), channel_id=1, source_target_pairs={{16,17},{17,16},{18,19},{19,18},{0,8},{8,0},{1,9},{9,1},{2,10},{10... | collective-permute-start | bytes 196616 | tf_op jit(solution)/shard_map/ppermute | solution.py:730
  18.6 5.0 %collective-permute-start.3 = (bf16[32,1024]{1,0:T(8,128)(2,1)S(1)}, bf16[32,1024]{1,0:T(8,128)(2,1)S(1)}, u32[]{:S(2)}, u32[]{:S(2)}) collective-permute-start(bf16[32,1024]{1,0:T(8,128)(2,1)S(1)} %copy-done.12), channel_id=1, source_target_pairs={{17,18},{18,17},{1,2},{2,1},{19,16},{16,19},{3,0},{0,3},{21,22},{2... | collective-permute-start | bytes 196616 | tf_op jit(solution)/shard_map/ppermute | solution.py:731
  20.8 5.2 %collective-permute-start.8 = (bf16[64,128]{1,0:T(8,128)(2,1)S(1)}, bf16[64,128]{1,0:T(8,128)(2,1)S(1)}, u32[]{:S(2)}, u32[]{:S(2)}) collective-permute-start(bf16[64,128]{1,0:T(8,128)(2,1)S(1)} %get-tuple-element.41), channel_id=1, source_target_pairs={{0,2},{1,3},{2,0},{3,1},{4,6},{5,7},{6,4},{7,5},{8,10},{9,11},{10,... | collective-permute-start | bytes 49160 | tf_op jit(solution)/shard_map/ppermute | solution.py:756
  26.1 4.8 %collective-permute-start.9 = (bf16[128,128]{1,0:T(8,128)(2,1)S(1)}, bf16[128,128]{1,0:T(8,128)(2,1)S(1)}, u32[]{:S(2)}, u32[]{:S(2)}) collective-permute-start(bf16[128,128]{1,0:T(8,128)(2,1)S(1)} %get-tuple-element.39), channel_id=1, source_target_pairs={{0,4},{4,0},{8,12},{12,8},{1,5},{5,1},{9,13},{13,9},{2,6},{6,2},{1... | collective-permute-start | bytes 98312 | tf_op jit(solution)/shard_map/ppermute | solution.py:806
  29.6 3.4 %collective-permute-start.10 = (bf16[128,128]{1,0:T(8,128)(2,1)S(1)}, bf16[128,128]{1,0:T(8,128)(2,1)S(1)}, u32[]{:S(2)}, u32[]{:S(2)}) collective-permute-start(bf16[128,128]{1,0:T(8,128)(2,1)S(1)} %get-tuple-element.40), channel_id=1, source_target_pairs={{4,8},{8,4},{12,0},{0,12},{5,9},{9,5},{13,1},{1,13},{6,10},{10,6},... | collective-permute-start | bytes 98312 | tf_op jit(solution)/shard_map/ppermute | solution.py:807

commit v8 on v7

--- a/solution.py
+++ b/solution.py
@@ -118,6 +118,12 @@
     surface = to_tiles(row_ref[...])
     s_ref[...] = surface
     coarse_ref[...] = surface.astype(bf16)
+
+
+def pair_kernel(surface_ref, part_ref, _, __, sum_ref, coarse_ref, ___, ____):
+    total = surface_ref[...] + part_ref[...].astype(f32)
+    sum_ref[...] = total
+    coarse_ref[...] = total.astype(bf16)
 
 
 def forward_kernel(
@@ -252,17 +258,37 @@
             copy.wait()
 
 
+def one_hot_kernel(
+    rows, columns, a_src, a_dst, m_src, m_dst, _, src_hot_ref, dst_hot_ref, src_row_ref, dst_row_ref
+):
+    is_atmos = lax.axis_index("comp") == 0
+    blocks, points = src_row_ref.shape
+    lane_iota = lax.broadcasted_iota(jnp.int32, (LANES, points), 0)
+    for a_ref, m_ref, hot_ref, row_ref in (
+        (a_src, m_src, src_hot_ref, src_row_ref),
+        (a_dst, m_dst, dst_hot_ref, dst_row_ref),
+    ):
+        index = jnp.where(is_atmos, m_ref[0, 0], a_ref[0, 0])
+        row = index // columns
+        tile = (index // LANES) % (columns // LANES)
+        row_ref[...] = tile * rows + row
+        lane = index % LANES
+        for b in range(blocks):
+            hot_ref[:, b * points : (b + 1) * points] = jnp.where(
+                lane_iota == lane[b : b + 1], 1.0, 0.0
+            ).astype(bf16)
+
+
 def regrid_kernel(n_surfaces, *refs):
     surfaces = refs[:n_surfaces]
     (
-        a_src, a_dst, a_count, a_weight, m_src, m_dst, m_count, m_weight,
+        src_hot_ref, dst_hot_ref, src_row_ref, dst_row_ref, a_count, m_count, a_weight, m_weight,
         _, _,
         land_ref, sent_ref, weight_ref, gath_ref, val_ref, sem,
     ) = refs[n_surfaces:]
     is_atmos = lax.axis_index("comp") == 0
     blocks, points = val_ref.shape
     cells = surfaces[0].shape[0]
-    rows = 8
 
     @pl.when(is_atmos)
     def _():
@@ -272,26 +298,18 @@
     def _():
         pltpu.make_async_copy(a_weight.at[0, 0], weight_ref, sem).start()
 
-    src = jnp.where(is_atmos, m_src[0, 0], a_src[0, 0])
-    dst = jnp.where(is_atmos, m_dst[0, 0], a_dst[0, 0])
     count = jnp.where(is_atmos, m_count[0, 0], a_count[0, 0])
-    tiles = cells // rows
-
-    def split(index):
-        row = index // (tiles * LANES)
-        tile = (index // LANES) % tiles
-        return tile * rows + row, index % LANES
-
-    src_row, src_lane = split(src)
-    dst_row, dst_lane = split(dst)
-    lane_iota = lax.broadcasted_iota(jnp.int32, (LANES, points), 0)
+    pair = 2 * points
     row_iota = lax.broadcasted_iota(jnp.int32, (cells, points), 0)
     table = sum(surface[...].astype(f32) for surface in surfaces).astype(bf16)
-    for b in range(blocks):
-        hot = jnp.where(lane_iota == src_lane[b : b + 1], 1.0, 0.0).astype(bf16)
-        picked = jnp.dot(table, hot, preferred_element_type=f32)
-        picked = jnp.where(row_iota == src_row[b : b + 1], picked, 0.0)
-        gath_ref[b : b + 1, :] = jnp.sum(picked, axis=0, keepdims=True)
+    for b in range(0, blocks, 2):
+        picked = jnp.dot(
+            table, src_hot_ref[:, b * points : b * points + pair], preferred_element_type=f32
+        )
+        for k in range(2):
+            mine = row_iota == src_row_ref[b + k : b + k + 1, :]
+            part = jnp.where(mine, picked[:, k * points : (k + 1) * points], 0.0)
+            gath_ref[b + k : b + k + 1, :] = jnp.sum(part, axis=0, keepdims=True)
     gathered = gath_ref[...].astype(bf16)
 
     @pl.when(is_atmos)
@@ -304,24 +322,34 @@
 
     block_iota = lax.broadcasted_iota(jnp.int32, (blocks, points), 0)
     values = jnp.zeros((blocks, points), f32)
-    for b in range(blocks):
-        term = lax.dot_general(
-            gathered, weight_ref[b], (((1,), (1,)), ((), ())), preferred_element_type=f32
+    for b in range(0, blocks, 2):
+        terms = lax.dot_general(
+            gathered,
+            weight_ref[b : b + 2].reshape(pair, points),
+            (((1,), (1,)), ((), ())),
+            preferred_element_type=f32,
         )
-        values = jnp.where(block_iota == b, term, values)
+        for k in range(2):
+            values = jnp.where(block_iota == b + k, terms[:, k * points : (k + 1) * points], values)
     val_ref[...] = jnp.where(block_iota < count, values, 0.0)
     land = jnp.zeros((2 * cells, LANES), f32)
-    for b in range(blocks):
-        value = val_ref[b : b + 1, :]
-        coarse = value.astype(bf16).astype(f32)
-        fine = value - coarse
-        mine = row_iota == dst_row[b : b + 1]
-        both = jnp.concatenate(
-            [jnp.where(mine, coarse, 0.0), jnp.where(mine, fine, 0.0)], axis=0
-        ).astype(bf16)
-        hot = jnp.where(lane_iota == dst_lane[b : b + 1], 1.0, 0.0).astype(bf16)
+    for b in range(0, blocks, 2):
+        spread = []
+        for k in range(b, b + 2):
+            value = val_ref[k : k + 1, :]
+            coarse = value.astype(bf16).astype(f32)
+            fine = value - coarse
+            mine = row_iota == dst_row_ref[k : k + 1, :]
+            spread.append(
+                jnp.concatenate(
+                    [jnp.where(mine, coarse, 0.0), jnp.where(mine, fine, 0.0)], axis=0
+                ).astype(bf16)
+            )
         land = land + lax.dot_general(
-            both, hot, (((1,), (1,)), ((), ())), preferred_element_type=f32
+            jnp.concatenate(spread, axis=1),
+            dst_hot_ref[:, b * points : b * points + pair],
+            (((1,), (1,)), ((), ())),
+            preferred_element_type=f32,
         )
     land = land[:cells] + land[cells:]
     land_ref[...] = land
@@ -701,8 +729,21 @@
 
     surface = partial_surface
     for mask in masks[:-1]:
-        surface = surface + lax.ppermute(coarse, "gy", sum_route(mask)).astype(f32)
-        coarse = surface.astype(bf16)
+        part = lax.ppermute(coarse, "gy", sum_route(mask))
+        surface, coarse, e1, e3 = pl.pallas_call(
+            pair_kernel,
+            out_shape=[
+                shape(surface.shape, f32),
+                shape(surface.shape, bf16),
+                shape(e1.shape, bf16),
+                shape(e3.shape, bf16),
+            ],
+            in_specs=[vmem, vmem, anywhere, anywhere],
+            out_specs=[vmem, vmem, anywhere, anywhere],
+            input_output_aliases={2: 2, 3: 3},
+            compiler_params=params(),
+            name="pair_sum",
+        )(surface, part, e1, e3)
     surfaces = [
         lax.ppermute(coarse, ("comp", "gy"), partner_route(mask)) for mask in masks[-1:] + [0]
     ]
@@ -716,10 +757,13 @@
     def level_route(odd):
         pairs = []
         for i in range(groups_x):
-            for a, b in ring_pairs(groups_y, odd):
-                pairs.append((flat(1, i, a), flat(1, i, b)))
+            linked = [(a, a + 1) for a in range(odd, groups_y - 1, 2)]
+            alone = set(range(groups_y)) - {j for pair in linked for j in pair}
+            pairs += [(flat(1, i, a), flat(1, i, b)) for a, b in linked]
+            if i % 2 == 0:
+                pairs += [(flat(1, i, j), flat(1, i + 1, j)) for j in sorted(alone)]
                 if odd or not paired:
-                    pairs.append((flat(0, i, a), flat(0, i, b)))
+                    pairs += [(flat(0, i, j), flat(0, i + 1, j)) for j in range(groups_y)]
             if paired and not odd and i < i ^ 2:
                 pairs += [(flat(0, i, j), flat(0, i ^ 2, j)) for j in range(groups_y)]
         return both_ways(pairs)
@@ -730,11 +774,23 @@
     e2 = lax.ppermute(e2, axes, level_route(0))
     e4 = lax.ppermute(e4, axes, level_route(1))
 
+    one_hots = pl.pallas_call(
+        functools.partial(one_hot_kernel, rows, columns),
+        out_shape=[
+            shape((LANES, blocks * points), bf16),
+            shape((LANES, blocks * points), bf16),
+            shape((blocks, points), jnp.int32),
+            shape((blocks, points), jnp.int32),
+        ],
+        in_specs=[vmem] * 4 + [anywhere],
+        out_specs=[vmem] * 4,
+        compiler_params=params(),
+        name="one_hots",
+    )(a2o_source, a2o_target, marine_air_input_index, marine_air_output_index, coarse)
     landing, sent = pl.pallas_call(
         functools.partial(regrid_kernel, len(surfaces)),
         out_shape=[shape((cells, LANES), f32), shape((cells, LANES), bf16)],
-        in_specs=[vmem] * len(surfaces)
-        + [vmem, vmem, smem, hbm, vmem, vmem, smem, hbm, anywhere, anywhere],
+        in_specs=[vmem] * (len(surfaces) + 4) + [smem, smem, hbm, hbm, anywhere, anywhere],
         out_specs=[vmem] * 2,
         scratch_shapes=[
             pltpu.VMEM((blocks, points, points), bf16),
@@ -745,10 +801,8 @@
         compiler_params=params(),
         name="regrid_blocks",
     )(
-        *surfaces,
-        a2o_source, a2o_target, a2o_count, a2o_weight,
-        marine_air_input_index, marine_air_output_index,
-        marine_air_piece_tally, marine_air_piece_factor, e1, e3,
+        *surfaces, *one_hots, a2o_count, marine_air_piece_tally,
+        a2o_weight, marine_air_piece_factor, e1, e3,
     )
     for mask in masks[:-1]:
         landing = landing + lax.ppermute(sent, "gy", sum_route(mask)).astype(f32)

time: 34.4 us -> 34.3 us (level)
  the two profiles are of different devices: /device:TPU:5 before, /device:TPU:0 now
where the time goes in v8:
time: 34.3 us; the launch traced here: 34 us
  starting transfers between devices  13.6 us (40%)
  Pallas kernels  10.7 us (31%)
  waiting for transfers between devices  5.77 us (17%)
  local copies, waits for them, and re-layouts  2.41 us (7%)
  between operations  1.58 us (5%)
    ppermute x2, starting transfers between devices, local(): lax.ppermute(coarse, ('comp', 'gy'), partner_route(mask))  4.05 us
    pallas_call x1, Pallas kernels, local(): pl.pallas_call(functools.partial(forward_kernel, groups_x, paired), out_s...  3.41 us
    ppermute x1, starting transfers between devices, local(): part = lax.ppermute(coarse, 'gy', sum_route(mask))  3.1 us
    unnamed x34, local copies, waits for them, and re-layouts  2.41 us
    ppermute x1, waiting for transfers between devices, local(): far = lax.ppermute(far, 'gx', both_ways(ring_pairs(groups_x, 1)))  2.21 us
    pallas_call x1, Pallas kernels, local(): pl.pallas_call(surface_kernel, out_shape=[shape((cells, LANES), f32), sha...  2.16 us
    ppermute x1, starting transfers between devices, local(): part = lax.ppermute(sent, 'gy', sum_route(masks[-1]))  2.14 us
    ppermute x1, waiting for transfers between devices, local(): landing = landing + lax.ppermute(sent, 'gy', sum_route(mask)).astype(f32)  1.86 us
  transfers between devices with their start and end apart: 11, of which 4 were waited for; matrix products, arithmetic and copies ran while one was open for 0% of the time, Pallas kernels for 16%

profile of v8, /device:TPU:0, one launch (start us, length us, event | category | flops | bytes accessed | tf_op | source)
XLA Modules:
  0.0 34.0 jit_solution(3539485442838628577)
XLA Ops:
  0.0 0.0 copy-start.9
  0.0 0.0 copy-start.10
  0.0 0.0 copy-start.11
  0.0 0.0 copy-start.12
  0.0 0.0 copy-start.1
  0.0 0.0 copy-start.2
  0.0 2.2 %surface_partials.1 = (f32[64,128]{1,0:T(8,128)}, bf16[64,128]{1,0:T(8,128)(2,1)}) custom-call(f32[1,8,32,1024]{3,2,1,0:T(8,128)} %x_ref.1, f32[1,128]{1,0:T(1,128)} %bitcast.6), custom_call_target="tpu_custom_call" | custom-call | tf_op jit(solution)/shard_map/surface_partials/pallas_call | solution.py:674
  2.2 3.1 %collective-permute-start = (bf16[64,128]{1,0:T(8,128)(2,1)}, bf16[64,128]{1,0:T(8,128)(2,1)S(1)}, u32[]{:S(2)}, u32[]{:S(2)}) collective-permute-start(bf16[64,128]{1,0:T(8,128)(2,1)} %get-tuple-element.33), channel_id=1, source_target_pairs={{0,1},{1,0},{2,3},{3,2},{4,5},{5,4},{6,7},{7,6},{8,9},{9,8},{10,11... | collective-permute-start | bytes 49160 | tf_op jit(solution)/shard_map/ppermute | solution.py:732
  5.3 3.4 %forward_or_halos.1 = (f32[64,128]{1,0:T(8,128)}, f32[8,32,1024]{2,1,0:T(8,128)}, bf16[80,1024]{1,0:T(8,128)(2,1)}, bf16[80,1024]{1,0:T(8,128)(2,1)}, bf16[32,10...) custom-call(f32[1,8,32,1024]{3,2,1,0:T(8,128)} %x_ref.1, s32[8,1024]{1,0:T(8,128)} %wet_ref.1, ...), custom_call_target="tpu_custom_call", output_to_operand_aliasing={{0}: (4, {})} | custom-call | tf_op jit(solution)/shard_map/forward_or_halos/pallas_call | solution.py:701
  8.7 0.0 collective-permute-done.part_ref
  8.7 0.0 copy-start.5
  8.7 0.9 %copy-done.5 = bf16[80,1024]{1,0:T(8,128)(2,1)S(1)} copy-done((bf16[80,1024]{1,0:T(8,128)(2,1)S(1)}, bf16[80,1024]{1,0:T(8,128)(2,1)}, u32[]{:S(2)}) %copy-start.5) | copy-done | bytes 163864
  9.6 0.0 copy-start.8
  9.6 0.8 %copy-done.8 = f32[64,128]{1,0:T(8,128)S(1)} copy-done((f32[64,128]{1,0:T(8,128)S(1)}, f32[64,128]{1,0:T(8,128)}, u32[]{:S(2)}) %copy-start.8) | copy-done | bytes 32792
  10.4 0.6 %pair_sum.1 = (f32[64,128]{1,0:T(8,128)}, bf16[64,128]{1,0:T(8,128)(2,1)S(1)}, bf16[80,1024]{1,0:T(8,128)(2,1)}, bf16[80,1024]{1,0:T(8,128)(2,1)S(1)}) custom-call(f32[64,128]{1,0:T(8,128)S(1)} %copy-done.8, bf16[64,128]{1,0:T(8,128)(2,1)S(1)} %collective-permute-done.part_ref, ...), custom_call_target="tpu_custom_call", output_to_operand_aliasing={{2}: (2, {}), {3}: (3, {})} | custom-call | tf_op jit(solution)/shard_map/pair_sum/pallas_call | solution.py:733
  11.0 0.0 copy-start.6
  11.0 0.7 %copy-done.6 = bf16[80,1024]{1,0:T(8,128)(2,1)} copy-done((bf16[80,1024]{1,0:T(8,128)(2,1)}, bf16[80,1024]{1,0:T(8,128)(2,1)S(1)}, u32[]{:S(2)}) %copy-start.6) | copy-done | bytes 163864
  11.7 0.0 collective-permute-start.1
  11.7 1.6 %collective-permute-start.2 = (bf16[80,1024]{1,0:T(8,128)(2,1)}, bf16[80,1024]{1,0:T(8,128)(2,1)S(1)}, u32[]{:S(2)}, u32[]{:S(2)}) collective-permute-start(bf16[80,1024]{1,0:T(8,128)(2,1)} %copy-done.6), channel_id=1, source_target_pairs={{4,8},{8,4},{12,0},{0,12},{5,9},{9,5},{13,1},{1,13},{6,10},{10,6},... | collective-permute-start | bytes 491528 | tf_op jit(solution)/shard_map/ppermute | solution.py:772
  13.3 2.1 %collective-permute-start.5 = (bf16[64,128]{1,0:T(8,128)(2,1)S(1)}, bf16[64,128]{1,0:T(8,128)(2,1)S(1)}, u32[]{:S(2)}, u32[]{:S(2)}) collective-permute-start(bf16[64,128]{1,0:T(8,128)(2,1)S(1)} %get-tuple-element.45._), channel_id=1, source_target_pairs={{0,18},{18,0},{1,19},{19,1},{2,16},{16,2},{3,17},{17,3},{4,22},{22... | collective-permute-start | bytes 49160 | tf_op jit(solution)/shard_map/ppermute | solution.py:748
  15.4 2.0 %collective-permute-start.6 = (bf16[64,128]{1,0:T(8,128)(2,1)S(1)}, bf16[64,128]{1,0:T(8,128)(2,1)S(1)}, u32[]{:S(2)}, u32[]{:S(2)}) collective-permute-start(bf16[64,128]{1,0:T(8,128)(2,1)S(1)} %get-tuple-element.45._), channel_id=1, source_target_pairs={{0,16},{16,0},{1,17},{17,1},{2,18},{18,2},{3,19},{19,3},{4,20},{20... | collective-permute-start | bytes 49160 | tf_op jit(solution)/shard_map/ppermute | solution.py:748
  18.6 0.0 copy-done.9
  18.7 0.0 copy-done.10
  18.7 0.0 copy-done.11
  18.7 0.0 copy-done.12
  18.7 0.6 %one_hots.1 = (bf16[128,4096]{1,0:T(8,128)(2,1)S(1)}, bf16[128,4096]{1,0:T(8,128)(2,1)S(1)}, s32[32,128]{1,0:T(8,128)S(1)}, s32[32,128]{1,0:T(8,128)S(1)}) custom-call(s32[1,1,32,128]{3,2,1,0:T(8,128)S(1)} %copy-done.9, s32[1,1,32,128]{3,2,1,0:T(8,128)S(1)} %copy-done.10, s32[1,1,32,128]{3,2,1,0:T(8,128)S(1)} %copy-done.11, ...), custom_call_target="tpu_custom_call" | custom-call | tf_op jit(solution)/shard_map/one_hots/pallas_call | solution.py:777
  19.3 0.0 collective-permute-done.5.refs_0_
  19.3 0.0 collective-permute-done.6.refs_1_
  19.3 0.0 collective-permute-done.1.e1_ref.refs_10_
  19.3 0.0 collective-permute-done.2.e3_ref.refs_11_
  19.4 0.0 copy-done.1
  19.4 0.0 copy-done.2
  19.4 0.0 copy-start.16
  19.4 0.0 copy-start.15
  19.4 0.0 copy-start
  19.4 0.0 copy-start.3
  19.4 0.0 copy-start.7
  19.4 0.0 copy-start.13
  19.4 1.4 %regrid_blocks.1 = (f32[64,128]{1,0:T(8,128)S(1)}, bf16[64,128]{1,0:T(8,128)(2,1)S(1)}) custom-call(bf16[64,128]{1,0:T(8,128)(2,1)S(1)} %collective-permute-done.5.refs_0_, bf16[64,128]{1,0:T(8,128)(2,1)S(1)} %collective-permute-done.6.refs_1_, bf16[128,4096]{1,0:T(8,128)(2,1)S(1)} %get-tuple-element.46.refs_2_, ...), custom_call_target="tpu_custom_call" | custom-call | tf_op jit(solution)/shard_map/regrid_blocks/pallas_call | solution.py:790
  20.8 0.0 copy-start.4
  20.8 0.0 copy-start.14
  20.8 1.4 %collective-permute-start.7 = (bf16[64,128]{1,0:T(8,128)(2,1)S(1)}, bf16[64,128]{1,0:T(8,128)(2,1)S(1)}, u32[]{:S(2)}, u32[]{:S(2)}) collective-permute-start(bf16[64,128]{1,0:T(8,128)(2,1)S(1)} %get-tuple-element.51), channel_id=1, source_target_pairs={{0,1},{1,0},{2,3},{3,2},{4,5},{5,4},{6,7},{7,6},{8,9},{9,8},{10,11... | collective-permute-start | bytes 49160 | tf_op jit(solution)/shard_map/ppermute | solution.py:808
  22.2 0.0 copy-done.16
  22.2 0.5 %collective-permute-start.3 = (bf16[32,1024]{1,0:T(8,128)(2,1)S(1)}, bf16[32,1024]{1,0:T(8,128)(2,1)S(1)}, u32[]{:S(2)}, u32[]{:S(2)}) collective-permute-start(bf16[32,1024]{1,0:T(8,128)(2,1)S(1)} %copy-done.16), channel_id=1, source_target_pairs={{16,17},{17,16},{18,19},{19,18},{0,8},{8,0},{1,9},{9,1},{2,10},{10... | collective-permute-start | bytes 196616 | tf_op jit(solution)/shard_map/ppermute | solution.py:774
  22.8 0.0 copy-done.15
  22.8 0.0 collective-permute-start.4
  22.8 1.9 %collective-permute-done.7 = bf16[64,128]{1,0:T(8,128)(2,1)S(1)} collective-permute-done((bf16[64,128]{1,0:T(8,128)(2,1)S(1)}, bf16[64,128]{1,0:T(8,128)(2,1)S(1)}, u32[]{:S(2)}, u32[]{:S(2)}) %collective-permute-start.7) | collective-permute-done | bytes 16416 | tf_op jit(solution)/shard_map/ppermute | solution.py:808
  24.6 2.1 %collective-permute-start.8 = (bf16[64,128]{1,0:T(8,128)(2,1)S(1)}, bf16[64,128]{1,0:T(8,128)(2,1)S(1)}, u32[]{:S(2)}, u32[]{:S(2)}) collective-permute-start(bf16[64,128]{1,0:T(8,128)(2,1)S(1)} %get-tuple-element.55), channel_id=1, source_target_pairs={{0,2},{1,3},{2,0},{3,1},{4,6},{5,7},{6,4},{7,5},{8,10},{9,11},{10,... | collective-permute-start | bytes 49160 | tf_op jit(solution)/shard_map/ppermute | solution.py:810
  26.8 0.0 collective-permute-done.3.e2_ref
  26.8 0.0 collective-permute-done.4.e4_ref
  26.8 0.0 copy-done
  26.8 0.0 copy-done.3
  26.8 0.0 copy-done.7
  26.8 0.0 copy-done.13
  26.8 0.9 %damping_or_first_step.1 = (bf16[256,1024]{1,0:T(8,128)(2,1)S(1)}, f32[7,16,1024]{2,1,0:T(8,128)S(1)}, f32[10,2,24,1024]{3,2,1,0:T(8,128)S(1)}) custom-call(f32[1,8,32,1024]{3,2,1,0:T(8,128)S(1)} %copy-done, s32[8,1024]{1,0:T(8,128)S(1)} %copy-done.7, f32[1,128]{1,0:T(1,128)S(1)} %bitcast.4, f32[8,32,1024]{2,1,0:T(8,128)S(1)} %copy-done.3, ...), custom_call_target="tpu_custom_call" | custom-call | tf_op jit(solution)/shard_map/damping_or_first_step/pallas_call | solution.py:829
  27.8 1.6 %collective-permute-done.8.part_ref = bf16[64,128]{1,0:T(8,128)(2,1)S(1)} collective-permute-done((bf16[64,128]{1,0:T(8,128)(2,1)S(1)}, bf16[64,128]{1,0:T(8,128)(2,1)S(1)}, u32[]{:S(2)}, u32[]{:S(2)}) %collective-permute-start.8) | collective-permute-done | bytes 16416 | tf_op jit(solution)/shard_map/ppermute | solution.py:810
  29.4 0.1 collective-permute-start.9
  29.5 0.6 %collective-permute-start.10 = (bf16[128,128]{1,0:T(8,128)(2,1)S(1)}, bf16[128,128]{1,0:T(8,128)(2,1)S(1)}, u32[]{:S(2)}, u32[]{:S(2)}) collective-permute-start(bf16[128,128]{1,0:T(8,128)(2,1)S(1)} %get-tuple-element.54), channel_id=1, source_target_pairs={{4,8},{8,4},{12,0},{0,12},{5,9},{9,5},{13,1},{1,13},{6,10},{10,6},... | collective-permute-start | bytes 98312 | tf_op jit(solution)/shard_map/ppermute | solution.py:861
  30.1 0.0 copy-done.4
  30.1 0.0 copy-done.14
  30.1 0.4 %inverse_or_second_step.1 = (f32[8,32,1024]{2,1,0:T(8,128)S(1)}, f32[32,128]{1,0:T(8,128)S(1)}) custom-call(f32[1,128]{1,0:T(1,128)S(1)} %bitcast.5, bf16[1024,512]{1,0:T(8,128)(2,1)S(1)} %copy-done.4, bf16[256,1024]{1,0:T(8,128)(2,1)S(1)} %get-tuple-element.40.zb_ref, f32[7,16,1024]{2,1,0:T(8,128)S(1)} %get-tuple-element.41.c_ref._, ...), custom_call_target="tpu_custom_call" | custom-call | tf_op jit(solution)/shard_map/inverse_or_second_step/pallas_call | solution.py:862
  30.6 0.1 collective-permute-done.9.near_ref
  30.7 2.2 %collective-permute-done.10.far_ref = bf16[128,128]{1,0:T(8,128)(2,1)S(1)} collective-permute-done((bf16[128,128]{1,0:T(8,128)(2,1)S(1)}, bf16[128,128]{1,0:T(8,128)(2,1)S(1)}, u32[]{:S(2)}, u32[]{:S(2)}) %collective-permute-start.10) | collective-permute-done | bytes 32800 | tf_op jit(solution)/shard_map/ppermute | solution.py:861
  32.9 1.1 %add_surface_terms.1 = f32[1,8,32,1024]{3,2,1,0:T(8,128)} custom-call(f32[32,128]{1,0:T(8,128)S(1)} %get-tuple-element.43.column_ref, f32[8,32,1024]{2,1,0:T(8,128)S(1)} %get-tuple-element.44.base_ref, f32[7,16,1024]{2,1,0:T(8,128)S(1)} %get-tuple-element.41.c_ref._, f32[64,128]{1,0:T(8,128)S(1)} %get-tuple-element.52.sum_ref, ...), custom_call_target="tpu_custom_call" | custom-call | tf_op jit(solution)/shard_map/add_surface_terms/pallas_call | solution.py:870
  (2 shorter events, 0.0 us)
Async XLA Ops:
  0.0 18.6 %copy-start.9 = (s32[1,1,32,128]{3,2,1,0:T(8,128)S(1)}, s32[1,1,32,128]{3,2,1,0:T(8,128)}, u32[]{:S(2)}) copy-start(s32[1,1,32,128]{3,2,1,0:T(8,128)} %a_src.1) | copy-start | bytes 49156
  0.0 18.7 %copy-start.10 = (s32[1,1,32,128]{3,2,1,0:T(8,128)S(1)}, s32[1,1,32,128]{3,2,1,0:T(8,128)}, u32[]{:S(2)}) copy-start(s32[1,1,32,128]{3,2,1,0:T(8,128)} %a_dst.1) | copy-start | bytes 49156
  0.0 18.7 %copy-start.11 = (s32[1,1,32,128]{3,2,1,0:T(8,128)S(1)}, s32[1,1,32,128]{3,2,1,0:T(8,128)}, u32[]{:S(2)}) copy-start(s32[1,1,32,128]{3,2,1,0:T(8,128)} %m_src.1) | copy-start | bytes 49156
  0.0 18.7 %copy-start.12 = (s32[1,1,32,128]{3,2,1,0:T(8,128)S(1)}, s32[1,1,32,128]{3,2,1,0:T(8,128)}, u32[]{:S(2)}) copy-start(s32[1,1,32,128]{3,2,1,0:T(8,128)} %m_dst.1) | copy-start | bytes 49156
  0.0 19.3 %copy-start.1 = (bf16[1,1,32,128,128]{4,3,2,1,0:T(8,128)(2,1)S(1)}, bf16[1,1,32,128,128]{4,3,2,1,0:T(8,128)(2,1)}, u32[]{:S(2)}) copy-start(bf16[1,1,32,128,128]{4,3,2,1,0:T(8,128)(2,1)} %refs_8_.1) | copy-start | bytes 3145732
  0.0 19.3 %copy-start.2 = (bf16[1,1,32,128,128]{4,3,2,1,0:T(8,128)(2,1)S(1)}, bf16[1,1,32,128,128]{4,3,2,1,0:T(8,128)(2,1)}, u32[]{:S(2)}) copy-start(bf16[1,1,32,128,128]{4,3,2,1,0:T(8,128)(2,1)} %refs_9_.1) | copy-start | bytes 3145732
  2.2 6.5 %collective-permute-start = (bf16[64,128]{1,0:T(8,128)(2,1)}, bf16[64,128]{1,0:T(8,128)(2,1)S(1)}, u32[]{:S(2)}, u32[]{:S(2)}) collective-permute-start(bf16[64,128]{1,0:T(8,128)(2,1)} %get-tuple-element.33), channel_id=1, source_target_pairs={{0,1},{1,0},{2,3},{3,2},{4,5},{5,4},{6,7},{7,6},{8,9},{9,8},{10,11... | collective-permute-start | bytes 49160 | tf_op jit(solution)/shard_map/ppermute | solution.py:732
  8.7 0.9 %copy-start.5 = (bf16[80,1024]{1,0:T(8,128)(2,1)S(1)}, bf16[80,1024]{1,0:T(8,128)(2,1)}, u32[]{:S(2)}) copy-start(bf16[80,1024]{1,0:T(8,128)(2,1)} %get-tuple-element.35.__) | copy-start | bytes 491524
  9.6 0.8 %copy-start.8 = (f32[64,128]{1,0:T(8,128)S(1)}, f32[64,128]{1,0:T(8,128)}, u32[]{:S(2)}) copy-start(f32[64,128]{1,0:T(8,128)} %get-tuple-element.32.surface_ref) | copy-start | bytes 98308
  11.0 0.7 %copy-start.6 = (bf16[80,1024]{1,0:T(8,128)(2,1)}, bf16[80,1024]{1,0:T(8,128)(2,1)S(1)}, u32[]{:S(2)}) copy-start(bf16[80,1024]{1,0:T(8,128)(2,1)S(1)} %get-tuple-element.37) | copy-start | bytes 491524
  11.7 7.6 %collective-permute-start.1 = (bf16[80,1024]{1,0:T(8,128)(2,1)}, bf16[80,1024]{1,0:T(8,128)(2,1)S(1)}, u32[]{:S(2)}, u32[]{:S(2)}) collective-permute-start(bf16[80,1024]{1,0:T(8,128)(2,1)} %get-tuple-element.36), channel_id=1, source_target_pairs={{0,4},{4,0},{8,12},{12,8},{1,5},{5,1},{9,13},{13,9},{2,6},{6,2},{1... | collective-permute-start | bytes 491528 | tf_op jit(solution)/shard_map/ppermute | solution.py:771
  11.7 7.7 %collective-permute-start.2 = (bf16[80,1024]{1,0:T(8,128)(2,1)}, bf16[80,1024]{1,0:T(8,128)(2,1)S(1)}, u32[]{:S(2)}, u32[]{:S(2)}) collective-permute-start(bf16[80,1024]{1,0:T(8,128)(2,1)} %copy-done.6), channel_id=1, source_target_pairs={{4,8},{8,4},{12,0},{0,12},{5,9},{9,5},{13,1},{1,13},{6,10},{10,6},... | collective-permute-start | bytes 491528 | tf_op jit(solution)/shard_map/ppermute | solution.py:772
  13.3 6.0 %collective-permute-start.5 = (bf16[64,128]{1,0:T(8,128)(2,1)S(1)}, bf16[64,128]{1,0:T(8,128)(2,1)S(1)}, u32[]{:S(2)}, u32[]{:S(2)}) collective-permute-start(bf16[64,128]{1,0:T(8,128)(2,1)S(1)} %get-tuple-element.45._), channel_id=1, source_target_pairs={{0,18},{18,0},{1,19},{19,1},{2,16},{16,2},{3,17},{17,3},{4,22},{22... | collective-permute-start | bytes 49160 | tf_op jit(solution)/shard_map/ppermute | solution.py:748
  15.4 4.0 %collective-permute-start.6 = (bf16[64,128]{1,0:T(8,128)(2,1)S(1)}, bf16[64,128]{1,0:T(8,128)(2,1)S(1)}, u32[]{:S(2)}, u32[]{:S(2)}) collective-permute-start(bf16[64,128]{1,0:T(8,128)(2,1)S(1)} %get-tuple-element.45._), channel_id=1, source_target_pairs={{0,16},{16,0},{1,17},{17,1},{2,18},{18,2},{3,19},{19,3},{4,20},{20... | collective-permute-start | bytes 49160 | tf_op jit(solution)/shard_map/ppermute | solution.py:748
  19.4 2.9 %copy-start.16 = (bf16[32,1024]{1,0:T(8,128)(2,1)S(1)}, bf16[32,1024]{1,0:T(8,128)(2,1)}, u32[]{:S(2)}) copy-start(bf16[32,1024]{1,0:T(8,128)(2,1)} %get-tuple-element.38) | copy-start | bytes 196612
  19.4 3.4 %copy-start.15 = (bf16[32,1024]{1,0:T(8,128)(2,1)S(1)}, bf16[32,1024]{1,0:T(8,128)(2,1)}, u32[]{:S(2)}) copy-start(bf16[32,1024]{1,0:T(8,128)(2,1)} %get-tuple-element.39) | copy-start | bytes 196612
  19.4 7.4 %copy-start = (f32[1,8,32,1024]{3,2,1,0:T(8,128)S(1)}, f32[1,8,32,1024]{3,2,1,0:T(8,128)}, u32[]{:S(2)}) copy-start(f32[1,8,32,1024]{3,2,1,0:T(8,128)} %x_ref.1) | copy-start | bytes 3145732
  19.4 7.4 %copy-start.3 = (f32[8,32,1024]{2,1,0:T(8,128)S(1)}, f32[8,32,1024]{2,1,0:T(8,128)}, u32[]{:S(2)}) copy-start(f32[8,32,1024]{2,1,0:T(8,128)} %get-tuple-element.31.y_ref) | copy-start | bytes 3145732
  19.4 7.4 %copy-start.7 = (s32[8,1024]{1,0:T(8,128)S(1)}, s32[8,1024]{1,0:T(8,128)}, u32[]{:S(2)}) copy-start(s32[8,1024]{1,0:T(8,128)} %wet_ref.1) | copy-start | bytes 98308
  19.4 7.4 %copy-start.13 = (f32[128]{0:T(128)S(1)}, f32[128]{0:T(128)}, u32[]{:S(2)}) copy-start(f32[128]{0:T(128)} %param.19) | copy-start | bytes 1540
  20.8 9.3 %copy-start.4 = (bf16[1024,512]{1,0:T(8,128)(2,1)S(1)}, bf16[1024,512]{1,0:T(8,128)(2,1)}, u32[]{:S(2)}) copy-start(bf16[1024,512]{1,0:T(8,128)(2,1)} %constant.5.clone.table_ref) | copy-start | bytes 3145732
  20.8 9.3 %copy-start.14 = (f32[128]{0:T(128)S(1)}, f32[128]{0:T(128)}, u32[]{:S(2)}) copy-start(f32[128]{0:T(128)} %param.18) | copy-start | bytes 1540
  20.8 3.8 %collective-permute-start.7 = (bf16[64,128]{1,0:T(8,128)(2,1)S(1)}, bf16[64,128]{1,0:T(8,128)(2,1)S(1)}, u32[]{:S(2)}, u32[]{:S(2)}) collective-permute-start(bf16[64,128]{1,0:T(8,128)(2,1)S(1)} %get-tuple-element.51), channel_id=1, source_target_pairs={{0,1},{1,0},{2,3},{3,2},{4,5},{5,4},{6,7},{7,6},{8,9},{9,8},{10,11... | collective-permute-start | bytes 49160 | tf_op jit(solution)/shard_map/ppermute | solution.py:808
  22.2 4.6 %collective-permute-start.3 = (bf16[32,1024]{1,0:T(8,128)(2,1)S(1)}, bf16[32,1024]{1,0:T(8,128)(2,1)S(1)}, u32[]{:S(2)}, u32[]{:S(2)}) collective-permute-start(bf16[32,1024]{1,0:T(8,128)(2,1)S(1)} %copy-done.16), channel_id=1, source_target_pairs={{16,17},{17,16},{18,19},{19,18},{0,8},{8,0},{1,9},{9,1},{2,10},{10... | collective-permute-start | bytes 196616 | tf_op jit(solution)/shard_map/ppermute | solution.py:774
  22.8 4.0 %collective-permute-start.4 = (bf16[32,1024]{1,0:T(8,128)(2,1)S(1)}, bf16[32,1024]{1,0:T(8,128)(2,1)S(1)}, u32[]{:S(2)}, u32[]{:S(2)}) collective-permute-start(bf16[32,1024]{1,0:T(8,128)(2,1)S(1)} %copy-done.15), channel_id=1, source_target_pairs={{17,18},{18,17},{16,20},{20,16},{19,23},{23,19},{0,4},{4,0},{1,5},... | collective-permute-start | bytes 196616 | tf_op jit(solution)/shard_map/ppermute | solution.py:775
  24.6 4.7 %collective-permute-start.8 = (bf16[64,128]{1,0:T(8,128)(2,1)S(1)}, bf16[64,128]{1,0:T(8,128)(2,1)S(1)}, u32[]{:S(2)}, u32[]{:S(2)}) collective-permute-start(bf16[64,128]{1,0:T(8,128)(2,1)S(1)} %get-tuple-element.55), channel_id=1, source_target_pairs={{0,2},{1,3},{2,0},{3,1},{4,6},{5,7},{6,4},{7,5},{8,10},{9,11},{10,... | collective-permute-start | bytes 49160 | tf_op jit(solution)/shard_map/ppermute | solution.py:810
  29.4 1.3 %collective-permute-start.9 = (bf16[128,128]{1,0:T(8,128)(2,1)S(1)}, bf16[128,128]{1,0:T(8,128)(2,1)S(1)}, u32[]{:S(2)}, u32[]{:S(2)}) collective-permute-start(bf16[128,128]{1,0:T(8,128)(2,1)S(1)} %get-tuple-element.53), channel_id=1, source_target_pairs={{0,4},{4,0},{8,12},{12,8},{1,5},{5,1},{9,13},{13,9},{2,6},{6,2},{1... | collective-permute-start | bytes 98312 | tf_op jit(solution)/shard_map/ppermute | solution.py:860
  29.5 3.4 %collective-permute-start.10 = (bf16[128,128]{1,0:T(8,128)(2,1)S(1)}, bf16[128,128]{1,0:T(8,128)(2,1)S(1)}, u32[]{:S(2)}, u32[]{:S(2)}) collective-permute-start(bf16[128,128]{1,0:T(8,128)(2,1)S(1)} %get-tuple-element.54), channel_id=1, source_target_pairs={{4,8},{8,4},{12,0},{0,12},{5,9},{9,5},{13,1},{1,13},{6,10},{10,6},... | collective-permute-start | bytes 98312 | tf_op jit(solution)/shard_map/ppermute | solution.py:861

commit v9 on v8

--- a/solution.py
+++ b/solution.py
@@ -81,89 +81,64 @@
     return 1.0 / grow, jnp.log(grow), sinh
 
 
-def surface_kernel(x_hbm, flux_hbm, s_ref, coarse_ref, x_ref, flux_ref, row_ref, x_sem, sem):
-    rows, channels, columns = x_ref.shape
-    col_group = lax.axis_index("gy")
-    is_atmos = lax.axis_index("comp") == 0
-    flux_copy = pltpu.make_async_copy(flux_hbm, flux_ref, sem)
-    copies = [
-        pltpu.make_async_copy(x_hbm.at[0, r], x_ref.at[r], x_sem.at[r]) for r in range(rows)
-    ]
-
-    @pl.when(is_atmos)
-    def _():
-        for copy in [flux_copy] + copies:
-            copy.start()
-        flux_copy.wait()
-        weight = channel_column(flux_ref[...], channels, col_group * channels)
-        for r in range(rows):
-            copies[r].wait()
-            row_ref[r : r + 1, :] = jnp.sum(x_ref[r] * weight, axis=0, keepdims=True)
-
-    @pl.when(jnp.logical_not(is_atmos))
-    def _():
-        top = [
-            pltpu.make_async_copy(
-                x_hbm.at[0, r, pl.ds(0, 8)], x_ref.at[r, pl.ds(0, 8)], x_sem.at[r]
-            )
-            for r in range(rows)
-        ]
-        for copy in top:
-            copy.start()
-        gain = jnp.where(col_group == 0, 1.0, 0.0)
-        for r in range(rows):
-            top[r].wait()
-            row_ref[r : r + 1, :] = x_ref[r, 0:1, :] * gain
-
-    surface = to_tiles(row_ref[...])
-    s_ref[...] = surface
-    coarse_ref[...] = surface.astype(bf16)
-
-
-def pair_kernel(surface_ref, part_ref, _, __, sum_ref, coarse_ref, ___, ____):
-    total = surface_ref[...] + part_ref[...].astype(f32)
-    sum_ref[...] = total
-    coarse_ref[...] = total.astype(bf16)
-
-
-def forward_kernel(
-    groups_x, paired, x_hbm, wet_hbm, diff_hbm, table_hbm, s_hbm, kept_hbm, *refs
+def start_kernel(
+    groups_x, paired, x_hbm, wet_hbm, flux_hbm, diff_hbm, table_hbm, *refs
 ):
-    del s_hbm, kept_hbm
-    outs = 5 if paired else 6
-    y_hbm, *message_hbm = refs[:outs]
-    y_ref, *message_ref = refs[outs : 2 * outs]
+    outs = 7 if paired else 8
+    s_hbm, coarse_hbm, y_hbm, *message_hbm = refs[:outs]
+    s_ref, coarse_ref, y_ref, *message_ref = refs[outs : 2 * outs]
     e1_ref, e3_ref, e2_ref, e4_ref = message_ref[:4]
     if not paired:
         pq_ref = message_ref[4]
-    x_ref, wet_ref, diff_ref, table_ref, flat_ref, edge_ref, sem, out_sem = refs[2 * outs :]
+    (
+        x_ref, wet_ref, flux_ref, diff_ref, table_ref, flat_ref, row_ref, edge_ref,
+        x_sem, sem, out_sem,
+    ) = refs[2 * outs :]
     rows, channels, columns = x_ref.shape
     half = columns // 2
     row_group = lax.axis_index("gx")
     col_group = lax.axis_index("gy")
     is_atmos = lax.axis_index("comp") == 0
 
-    x_copy = pltpu.make_async_copy(x_hbm.at[0], x_ref, sem.at[0])
+    x_copies = [
+        pltpu.make_async_copy(x_hbm.at[0, r], x_ref.at[r], x_sem.at[r]) for r in range(rows)
+    ]
+    surface_copies = [
+        pltpu.make_async_copy(s_ref, s_hbm, out_sem.at[0]),
+        pltpu.make_async_copy(coarse_ref, coarse_hbm, out_sem.at[1]),
+    ]
     y_copies = [
-        pltpu.make_async_copy(y_ref.at[r], y_hbm.at[r], out_sem.at[r]) for r in range(rows)
+        pltpu.make_async_copy(y_ref.at[r], y_hbm.at[r], out_sem.at[2 + r]) for r in range(rows)
     ]
     message_copies = [
-        pltpu.make_async_copy(ref, hbm, out_sem.at[rows + k])
+        pltpu.make_async_copy(ref, hbm, out_sem.at[2 + rows + k])
         for k, (ref, hbm) in enumerate(zip(message_ref, message_hbm))
     ]
 
+    def send_surface():
+        surface = to_tiles(row_ref[...])
+        s_ref[...] = surface
+        coarse_ref[...] = surface.astype(bf16)
+        for copy in surface_copies:
+            copy.start()
+
     @pl.when(is_atmos)
     def _():
-        table_copy = pltpu.make_async_copy(table_hbm, table_ref, sem.at[1])
-        diff_copy = pltpu.make_async_copy(diff_hbm, diff_ref, sem.at[2])
-        for copy in (x_copy, table_copy, diff_copy):
+        flux_copy = pltpu.make_async_copy(flux_hbm, flux_ref, sem.at[0])
+        diff_copy = pltpu.make_async_copy(diff_hbm, diff_ref, sem.at[1])
+        table_copy = pltpu.make_async_copy(table_hbm, table_ref, sem.at[2])
+        for copy in [flux_copy, diff_copy] + x_copies + [table_copy]:
             copy.start()
-        x_copy.wait()
         first = col_group * channels
+        flux_copy.wait()
+        weight = channel_column(flux_ref[...], channels, first)
         for r in range(rows):
+            x_copies[r].wait()
+            row_ref[r : r + 1, :] = jnp.sum(x_ref[r] * weight, axis=0, keepdims=True)
             left, right = x_ref[r, :, :half], x_ref[r, :, half:]
             flat_ref[r * channels : (r + 1) * channels, :half] = (left + right).astype(bf16)
             flat_ref[r * channels : (r + 1) * channels, half:] = (left - right).astype(bf16)
+        send_surface()
         table_copy.wait()
         for k in range(2):
             lanes = slice(k * half, (k + 1) * half)
@@ -203,15 +178,19 @@
                     pq_ref[1, :, lanes] = q.astype(bf16)
         for copy in message_copies:
             copy.start()
-        for copy in y_copies + message_copies:
+        for copy in surface_copies + y_copies + message_copies:
             copy.wait()
 
     @pl.when(jnp.logical_not(is_atmos))
     def _():
-        wet_copy = pltpu.make_async_copy(wet_hbm, wet_ref, sem.at[1])
-        for copy in (x_copy, wet_copy):
+        wet_copy = pltpu.make_async_copy(wet_hbm, wet_ref, sem.at[0])
+        for copy in x_copies + [wet_copy]:
             copy.start()
-        x_copy.wait()
+        gain = jnp.where(col_group == 0, 1.0, 0.0)
+        for r in range(rows):
+            x_copies[r].wait()
+            row_ref[r : r + 1, :] = x_ref[r, 0:1, :] * gain
+        send_surface()
         wet_copy.wait()
         levels = channels // 2
         lines = 2 * channels
@@ -254,7 +233,7 @@
 
         for copy in message_copies:
             copy.start()
-        for copy in message_copies:
+        for copy in surface_copies + message_copies:
             copy.wait()
 
 
@@ -671,25 +650,10 @@
     def shape(dims, dtype):
         return jax.ShapeDtypeStruct(dims, dtype)
 
-    partial_surface, coarse = pl.pallas_call(
-        surface_kernel,
-        out_shape=[shape((cells, LANES), f32), shape((cells, LANES), bf16)],
-        in_specs=[hbm, hbm],
-        out_specs=[vmem, vmem],
-        scratch_shapes=[
-            pltpu.VMEM((rows, channels, columns), f32),
-            pltpu.VMEM(flux_row.shape, f32),
-            pltpu.VMEM((rows, columns), f32),
-            pltpu.SemaphoreType.DMA((rows,)),
-            pltpu.SemaphoreType.DMA,
-        ],
-        compiler_params=pltpu.CompilerParams(vmem_limit_bytes=58 * 2**20),
-        name="surface_partials",
-    )(fields, flux_row)
-
     lines = 2 * channels + 16
     shapes = [
         shape((cells, LANES), f32),
+        shape((cells, LANES), bf16),
         shape((rows, channels, columns), f32),
         shape((lines, columns), bf16),
         shape((lines, columns), bf16),
@@ -698,26 +662,28 @@
     ]
     if not paired:
         shapes.append(shape((2, channels, columns), bf16))
-    partial_surface, y, e1, e3, e2, e4, *sums = pl.pallas_call(
-        functools.partial(forward_kernel, groups_x, paired),
+    partial_surface, coarse, y, e1, e3, e2, e4, *sums = pl.pallas_call(
+        functools.partial(start_kernel, groups_x, paired),
         out_shape=shapes,
-        in_specs=[hbm] * 4 + [anywhere],
-        out_specs=[anywhere] + [hbm] * (len(shapes) - 1),
-        scratch_shapes=[pltpu.VMEM(out.shape, out.dtype) for out in shapes[1:]]
+        in_specs=[hbm] * 5,
+        out_specs=[hbm] * len(shapes),
+        scratch_shapes=[pltpu.VMEM(out.shape, out.dtype) for out in shapes]
         + [
             pltpu.VMEM((rows, channels, columns), f32),
             pltpu.VMEM((rows, columns), jnp.int32),
+            pltpu.VMEM(flux_row.shape, f32),
             pltpu.VMEM(diff_row.shape, f32),
             pltpu.VMEM(forward.shape, bf16),
             pltpu.VMEM((rows * channels, columns), bf16),
+            pltpu.VMEM((rows, columns), f32),
             pltpu.VMEM((4 * rows, columns), f32),
+            pltpu.SemaphoreType.DMA((rows,)),
             pltpu.SemaphoreType.DMA((3,)),
-            pltpu.SemaphoreType.DMA((rows + len(shapes) - 2,)),
+            pltpu.SemaphoreType.DMA((rows + len(shapes) - 1,)),
         ],
-        input_output_aliases={4: 0},
         compiler_params=pltpu.CompilerParams(vmem_limit_bytes=58 * 2**20),
-        name="forward_or_halos",
-    )(fields, wet_cells, diff_row, forward, partial_surface)
+        name="surface_and_forward_or_halos",
+    )(fields, wet_cells, flux_row, diff_row, forward)
 
     masks = [1 << bit for bit in range(groups_y.bit_length() - 1)]
 
@@ -729,21 +695,8 @@
 
     surface = partial_surface
     for mask in masks[:-1]:
-        part = lax.ppermute(coarse, "gy", sum_route(mask))
-        surface, coarse, e1, e3 = pl.pallas_call(
-            pair_kernel,
-            out_shape=[
-                shape(surface.shape, f32),
-                shape(surface.shape, bf16),
-                shape(e1.shape, bf16),
-                shape(e3.shape, bf16),
-            ],
-            in_specs=[vmem, vmem, anywhere, anywhere],
-            out_specs=[vmem, vmem, anywhere, anywhere],
-            input_output_aliases={2: 2, 3: 3},
-            compiler_params=params(),
-            name="pair_sum",
-        )(surface, part, e1, e3)
+        surface = surface + lax.ppermute(coarse, "gy", sum_route(mask)).astype(f32)
+        coarse = surface.astype(bf16)
     surfaces = [
         lax.ppermute(coarse, ("comp", "gy"), partner_route(mask)) for mask in masks[-1:] + [0]
     ]

time: 34.3 us -> 31.2 us (0.910)
  starting transfers between devices: 13.6 us -> 16.1 us
  Pallas kernels: 10.7 us -> 8.24 us
  local copies, waits for them, and re-layouts: 2.41 us -> 0.07 us
  waiting for transfers between devices: 5.77 us -> 4.33 us
  other arithmetic: 0.01 us -> 0.77 us
    pallas_call x3 -> x1, Pallas kernels: 6.18 us -> 3.75 us  [local(): pl.pallas_call(functools.partial(start_kernel, groups_x, paired), out_sha...]
    unnamed x34 -> x28, local copies, waits for them, and re-layouts: 2.41 us -> 0.07 us
    ppermute x1, starting transfers between devices: 0.07 us -> 1.59 us  [local(): near = lax.ppermute(near, 'gx', both_ways(ring_pairs(groups_x, 0)))]
    ppermute x1, waiting for transfers between devices: 1.86 us -> 0.66 us  [local(): landing = landing + lax.ppermute(sent, 'gy', sum_route(mask)).astype(f32)]
    ppermute x1, starting transfers between devices: 0.53 us -> 1.48 us  [local(): e2 = lax.ppermute(e2, axes, level_route(0))]
    convert_element_type x0 -> x1, other arithmetic: none -> 0.76 us  [local(): coarse = surface.astype(bf16)]
    ppermute x1, waiting for transfers between devices: 2.21 us -> 1.58 us  [local(): far = lax.ppermute(far, 'gx', both_ways(ring_pairs(groups_x, 1)))]
    ppermute x1, starting transfers between devices: 0.65 us -> 0.07 us  [local(): far = lax.ppermute(far, 'gx', both_ways(ring_pairs(groups_x, 1)))]
  transfers between devices with their start and end apart: 11 -> 11, of which waited for: 4 -> 5; matrix products, arithmetic and copies ran while one was open for 0% -> 2% of each run, Pallas kernels for 16% -> 6%
where the time goes in v9:
time: 31.2 us; the launch traced here: 31 us
  starting transfers between devices  16.1 us (52%)
  Pallas kernels  8.24 us (26%)
  waiting for transfers between devices  4.33 us (14%)
  between operations  1.52 us (5%)
  other arithmetic  0.77 us (2%)
    ppermute x2, starting transfers between devices, local(): lax.ppermute(coarse, ('comp', 'gy'), partner_route(mask))  4.5 us
    pallas_call x1, Pallas kernels, local(): pl.pallas_call(functools.partial(start_kernel, groups_x, paired), out_sha...  3.75 us
    ppermute x1, starting transfers between devices, local(): surface = surface + lax.ppermute(coarse, 'gy', sum_route(mask)).astype(f32)  3.12 us
    ppermute x1, starting transfers between devices, local(): part = lax.ppermute(sent, 'gy', sum_route(masks[-1]))  2.08 us
    ppermute x1, starting transfers between devices, local(): landing = landing + lax.ppermute(sent, 'gy', sum_route(mask)).astype(f32)  1.65 us
    ppermute x1, waiting for transfers between devices, local(): part = lax.ppermute(sent, 'gy', sum_route(masks[-1]))  1.62 us
    ppermute x1, starting transfers between devices, local(): e3 = lax.ppermute(e3, 'gx', both_ways(ring_pairs(groups_x, 1)))  1.6 us
    ppermute x1, starting transfers between devices, local(): near = lax.ppermute(near, 'gx', both_ways(ring_pairs(groups_x, 0)))  1.59 us
  transfers between devices with their start and end apart: 11, of which 5 were waited for; matrix products, arithmetic and copies ran while one was open for 2% of the time, Pallas kernels for 6%

profile of v9, /device:TPU:0, one launch (start us, length us, event | category | flops | bytes accessed | tf_op | source)
XLA Modules:
  0.0 31.0 jit_solution(6249704594987960866)
XLA Ops:
  0.0 0.0 copy-start.6
  0.0 0.0 copy-start.7
  0.0 0.0 copy-start.8
  0.0 0.0 copy-start.9
  0.0 0.0 copy-start.1
  0.0 0.0 copy-start.2
  0.0 3.7 %surface_and_forward_or_halos.1 = (f32[64,128]{1,0:T(8,128)}, bf16[64,128]{1,0:T(8,128)(2,1)}, f32[8,32,1024]{2,1,0:T(8,128)}, bf16[80,1024]{1,0:T(8,128)(2,1)},...) custom-call(f32[1,8,32,1024]{3,2,1,0:T(8,128)} %x_ref.1, s32[8,1024]{1,0:T(8,128)} %wet_ref.1, ...), custom_call_target="tpu_custom_call" | custom-call | tf_op jit(solution)/shard_map/surface_and_forward_or_halos/pallas_call | solution.py:665
  3.8 3.1 %collective-permute-start.4 = (bf16[64,128]{1,0:T(8,128)(2,1)}, bf16[64,128]{1,0:T(8,128)(2,1)S(1)}, u32[]{:S(2)}, u32[]{:S(2)}) collective-permute-start(bf16[64,128]{1,0:T(8,128)(2,1)} %get-tuple-element.37), channel_id=1, source_target_pairs={{0,1},{1,0},{2,3},{3,2},{4,5},{5,4},{6,7},{7,6},{8,9},{9,8},{10,11... | collective-permute-start | bytes 49160 | tf_op jit(solution)/shard_map/ppermute | solution.py:698
  6.9 0.0 collective-permute-start
  6.9 1.6 %collective-permute-start.1 = (bf16[80,1024]{1,0:T(8,128)(2,1)}, bf16[80,1024]{1,0:T(8,128)(2,1)S(1)}, u32[]{:S(2)}, u32[]{:S(2)}) collective-permute-start(bf16[80,1024]{1,0:T(8,128)(2,1)} %get-tuple-element.28), channel_id=1, source_target_pairs={{4,8},{8,4},{12,0},{0,12},{5,9},{9,5},{13,1},{1,13},{6,10},{10,6},... | collective-permute-start | bytes 491528 | tf_op jit(solution)/shard_map/ppermute | solution.py:725
  8.5 0.3 %collective-permute-done.4 = bf16[64,128]{1,0:T(8,128)(2,1)S(1)} collective-permute-done((bf16[64,128]{1,0:T(8,128)(2,1)}, bf16[64,128]{1,0:T(8,128)(2,1)S(1)}, u32[]{:S(2)}, u32[]{:S(2)}) %collective-permute-start.4) | collective-permute-done | bytes 16416 | tf_op jit(solution)/shard_map/ppermute | solution.py:698
  8.8 0.8 %add_convert_fusion._ = bf16[64,128]{1,0:T(8,128)(2,1)S(1)} fusion(f32[64,128]{1,0:T(8,128)} %get-tuple-element.36, bf16[64,128]{1,0:T(8,128)(2,1)S(1)} %collective-permute-done.4), kind=kLoop, calls=%fused_computation.1 | loop fusion | flops 24576 | bytes 65536 | tf_op jit(solution)/shard_map/convert_element_type | solution.py:699
  9.6 2.8 %collective-permute-start.5 = (bf16[64,128]{1,0:T(8,128)(2,1)S(1)}, bf16[64,128]{1,0:T(8,128)(2,1)S(1)}, u32[]{:S(2)}, u32[]{:S(2)}) collective-permute-start(bf16[64,128]{1,0:T(8,128)(2,1)S(1)} %add_convert_fusion._), channel_id=1, source_target_pairs={{0,18},{18,0},{1,19},{19,1},{2,16},{16,2},{3,17},{17,3},{4,22},{22... | collective-permute-start | bytes 49160 | tf_op jit(solution)/shard_map/ppermute | solution.py:701
  12.4 1.7 %collective-permute-start.6 = (bf16[64,128]{1,0:T(8,128)(2,1)S(1)}, bf16[64,128]{1,0:T(8,128)(2,1)S(1)}, u32[]{:S(2)}, u32[]{:S(2)}) collective-permute-start(bf16[64,128]{1,0:T(8,128)(2,1)S(1)} %add_convert_fusion._), channel_id=1, source_target_pairs={{0,16},{16,0},{1,17},{17,1},{2,18},{18,2},{3,19},{19,3},{4,20},{20... | collective-permute-start | bytes 49160 | tf_op jit(solution)/shard_map/ppermute | solution.py:701
  15.4 0.0 copy-done.6
  15.4 0.0 copy-done.7
  15.4 0.0 copy-done.8
  15.4 0.0 copy-done.9
  15.4 0.6 %one_hots.1 = (bf16[128,4096]{1,0:T(8,128)(2,1)S(1)}, bf16[128,4096]{1,0:T(8,128)(2,1)S(1)}, s32[32,128]{1,0:T(8,128)S(1)}, s32[32,128]{1,0:T(8,128)S(1)}) custom-call(s32[1,1,32,128]{3,2,1,0:T(8,128)S(1)} %copy-done.6, s32[1,1,32,128]{3,2,1,0:T(8,128)S(1)} %copy-done.7, s32[1,1,32,128]{3,2,1,0:T(8,128)S(1)} %copy-done.8, s32[1,1,32,128]{3,2,1,0:T(8,128)S(1)} %copy-done.9, ...), custom_call_target="tpu_custom_call" | custom-call | tf_op jit(solution)/shard_map/one_hots/pallas_call | solution.py:730
  16.1 0.0 collective-permute-done.5.refs_0_
  16.1 0.1 collective-permute-done.6.refs_1_
  16.2 0.0 collective-permute-done.e1_ref.refs_10_
  16.2 0.0 collective-permute-done.1.e3_ref.refs_11_
  16.2 0.0 copy-done.1
  16.2 0.0 copy-done.2
  16.2 0.0 copy-start.13
  16.2 0.0 copy-start.12
  16.2 0.0 copy-start
  16.2 0.0 copy-start.3
  16.2 0.0 copy-start.5
  16.3 0.0 copy-start.10
  16.3 1.4 %regrid_blocks.1 = (f32[64,128]{1,0:T(8,128)S(1)}, bf16[64,128]{1,0:T(8,128)(2,1)S(1)}) custom-call(bf16[64,128]{1,0:T(8,128)(2,1)S(1)} %collective-permute-done.5.refs_0_, bf16[64,128]{1,0:T(8,128)(2,1)S(1)} %collective-permute-done.6.refs_1_, bf16[128,4096]{1,0:T(8,128)(2,1)S(1)} %get-tuple-element.38.refs_2_, ...), custom_call_target="tpu_custom_call" | custom-call | tf_op jit(solution)/shard_map/regrid_blocks/pallas_call | solution.py:743
  17.6 0.0 copy-start.4
  17.6 0.0 copy-start.11
  17.6 1.6 %collective-permute-start.7 = (bf16[64,128]{1,0:T(8,128)(2,1)S(1)}, bf16[64,128]{1,0:T(8,128)(2,1)S(1)}, u32[]{:S(2)}, u32[]{:S(2)}) collective-permute-start(bf16[64,128]{1,0:T(8,128)(2,1)S(1)} %get-tuple-element.43), channel_id=1, source_target_pairs={{0,1},{1,0},{2,3},{3,2},{4,5},{5,4},{6,7},{7,6},{8,9},{9,8},{10,11... | collective-permute-start | bytes 49160 | tf_op jit(solution)/shard_map/ppermute | solution.py:761
  19.3 0.0 copy-done.13
  19.3 1.5 %collective-permute-start.2 = (bf16[32,1024]{1,0:T(8,128)(2,1)S(1)}, bf16[32,1024]{1,0:T(8,128)(2,1)S(1)}, u32[]{:S(2)}, u32[]{:S(2)}) collective-permute-start(bf16[32,1024]{1,0:T(8,128)(2,1)S(1)} %copy-done.13), channel_id=1, source_target_pairs={{16,17},{17,16},{18,19},{19,18},{0,8},{8,0},{1,9},{9,1},{2,10},{10... | collective-permute-start | bytes 196616 | tf_op jit(solution)/shard_map/ppermute | solution.py:727
  20.8 0.0 copy-done.12
  20.8 0.0 collective-permute-start.3
  20.8 0.7 %collective-permute-done.7 = bf16[64,128]{1,0:T(8,128)(2,1)S(1)} collective-permute-done((bf16[64,128]{1,0:T(8,128)(2,1)S(1)}, bf16[64,128]{1,0:T(8,128)(2,1)S(1)}, u32[]{:S(2)}, u32[]{:S(2)}) %collective-permute-start.7) | collective-permute-done | bytes 16416 | tf_op jit(solution)/shard_map/ppermute | solution.py:761
  21.5 2.1 %collective-permute-start.8 = (bf16[64,128]{1,0:T(8,128)(2,1)S(1)}, bf16[64,128]{1,0:T(8,128)(2,1)S(1)}, u32[]{:S(2)}, u32[]{:S(2)}) collective-permute-start(bf16[64,128]{1,0:T(8,128)(2,1)S(1)} %get-tuple-element.47), channel_id=1, source_target_pairs={{0,2},{1,3},{2,0},{3,1},{4,6},{5,7},{6,4},{7,5},{8,10},{9,11},{10,... | collective-permute-start | bytes 49160 | tf_op jit(solution)/shard_map/ppermute | solution.py:763
  23.5 0.0 collective-permute-done.2.e2_ref
  23.6 0.0 collective-permute-done.3.e4_ref
  23.6 0.0 copy-done
  23.6 0.0 copy-done.3
  23.6 0.0 copy-done.5
  23.6 0.0 copy-done.10
  23.6 0.9 %damping_or_first_step.1 = (bf16[256,1024]{1,0:T(8,128)(2,1)S(1)}, f32[7,16,1024]{2,1,0:T(8,128)S(1)}, f32[10,2,24,1024]{3,2,1,0:T(8,128)S(1)}) custom-call(f32[1,8,32,1024]{3,2,1,0:T(8,128)S(1)} %copy-done, s32[8,1024]{1,0:T(8,128)S(1)} %copy-done.5, f32[1,128]{1,0:T(1,128)S(1)} %bitcast.4, f32[8,32,1024]{2,1,0:T(8,128)S(1)} %copy-done.3, ...), custom_call_target="tpu_custom_call" | custom-call | tf_op jit(solution)/shard_map/damping_or_first_step/pallas_call | solution.py:782
  24.5 1.6 %collective-permute-done.8.part_ref = bf16[64,128]{1,0:T(8,128)(2,1)S(1)} collective-permute-done((bf16[64,128]{1,0:T(8,128)(2,1)S(1)}, bf16[64,128]{1,0:T(8,128)(2,1)S(1)}, u32[]{:S(2)}, u32[]{:S(2)}) %collective-permute-start.8) | collective-permute-done | bytes 16416 | tf_op jit(solution)/shard_map/ppermute | solution.py:763
  26.2 0.1 collective-permute-start.10
  26.3 1.6 %collective-permute-start.9 = (bf16[128,128]{1,0:T(8,128)(2,1)S(1)}, bf16[128,128]{1,0:T(8,128)(2,1)S(1)}, u32[]{:S(2)}, u32[]{:S(2)}) collective-permute-start(bf16[128,128]{1,0:T(8,128)(2,1)S(1)} %get-tuple-element.45), channel_id=1, source_target_pairs={{0,4},{4,0},{8,12},{12,8},{1,5},{5,1},{9,13},{13,9},{2,6},{6,2},{1... | collective-permute-start | bytes 98312 | tf_op jit(solution)/shard_map/ppermute | solution.py:813
  27.9 0.0 copy-done.4
  27.9 0.0 copy-done.11
  27.9 0.4 %inverse_or_second_step.1 = (f32[8,32,1024]{2,1,0:T(8,128)S(1)}, f32[32,128]{1,0:T(8,128)S(1)}) custom-call(f32[1,128]{1,0:T(1,128)S(1)} %bitcast.5, bf16[1024,512]{1,0:T(8,128)(2,1)S(1)} %copy-done.4, bf16[256,1024]{1,0:T(8,128)(2,1)S(1)} %get-tuple-element.31.zb_ref, f32[7,16,1024]{2,1,0:T(8,128)S(1)} %get-tuple-element.32.c_ref._, ...), custom_call_target="tpu_custom_call" | custom-call | tf_op jit(solution)/shard_map/inverse_or_second_step/pallas_call | solution.py:815
  28.3 1.6 %collective-permute-done.10.far_ref = bf16[128,128]{1,0:T(8,128)(2,1)S(1)} collective-permute-done((bf16[128,128]{1,0:T(8,128)(2,1)S(1)}, bf16[128,128]{1,0:T(8,128)(2,1)S(1)}, u32[]{:S(2)}, u32[]{:S(2)}) %collective-permute-start.10) | collective-permute-done | bytes 32800 | tf_op jit(solution)/shard_map/ppermute | solution.py:814
  29.9 0.0 collective-permute-done.9.near_ref
  29.9 1.1 %add_surface_terms.1 = f32[1,8,32,1024]{3,2,1,0:T(8,128)} custom-call(f32[32,128]{1,0:T(8,128)S(1)} %get-tuple-element.34.column_ref, f32[8,32,1024]{2,1,0:T(8,128)S(1)} %get-tuple-element.35.base_ref, f32[7,16,1024]{2,1,0:T(8,128)S(1)} %get-tuple-element.32.c_ref._, f32[64,128]{1,0:T(8,128)S(1)} %get-tuple-element.44.sum_ref, ...), custom_call_target="tpu_custom_call" | custom-call | tf_op jit(solution)/shard_map/add_surface_terms/pallas_call | solution.py:823
  (2 shorter events, 0.0 us)
Async XLA Ops:
  0.0 15.4 %copy-start.6 = (s32[1,1,32,128]{3,2,1,0:T(8,128)S(1)}, s32[1,1,32,128]{3,2,1,0:T(8,128)}, u32[]{:S(2)}) copy-start(s32[1,1,32,128]{3,2,1,0:T(8,128)} %a_src.1) | copy-start | bytes 49156
  0.0 15.4 %copy-start.7 = (s32[1,1,32,128]{3,2,1,0:T(8,128)S(1)}, s32[1,1,32,128]{3,2,1,0:T(8,128)}, u32[]{:S(2)}) copy-start(s32[1,1,32,128]{3,2,1,0:T(8,128)} %a_dst.1) | copy-start | bytes 49156
  0.0 15.4 %copy-start.8 = (s32[1,1,32,128]{3,2,1,0:T(8,128)S(1)}, s32[1,1,32,128]{3,2,1,0:T(8,128)}, u32[]{:S(2)}) copy-start(s32[1,1,32,128]{3,2,1,0:T(8,128)} %m_src.1) | copy-start | bytes 49156
  0.0 15.4 %copy-start.9 = (s32[1,1,32,128]{3,2,1,0:T(8,128)S(1)}, s32[1,1,32,128]{3,2,1,0:T(8,128)}, u32[]{:S(2)}) copy-start(s32[1,1,32,128]{3,2,1,0:T(8,128)} %m_dst.1) | copy-start | bytes 49156
  0.0 16.2 %copy-start.1 = (bf16[1,1,32,128,128]{4,3,2,1,0:T(8,128)(2,1)S(1)}, bf16[1,1,32,128,128]{4,3,2,1,0:T(8,128)(2,1)}, u32[]{:S(2)}) copy-start(bf16[1,1,32,128,128]{4,3,2,1,0:T(8,128)(2,1)} %refs_8_.1) | copy-start | bytes 3145732
  0.0 16.2 %copy-start.2 = (bf16[1,1,32,128,128]{4,3,2,1,0:T(8,128)(2,1)S(1)}, bf16[1,1,32,128,128]{4,3,2,1,0:T(8,128)(2,1)}, u32[]{:S(2)}) copy-start(bf16[1,1,32,128,128]{4,3,2,1,0:T(8,128)(2,1)} %refs_9_.1) | copy-start | bytes 3145732
  3.8 5.0 %collective-permute-start.4 = (bf16[64,128]{1,0:T(8,128)(2,1)}, bf16[64,128]{1,0:T(8,128)(2,1)S(1)}, u32[]{:S(2)}, u32[]{:S(2)}) collective-permute-start(bf16[64,128]{1,0:T(8,128)(2,1)} %get-tuple-element.37), channel_id=1, source_target_pairs={{0,1},{1,0},{2,3},{3,2},{4,5},{5,4},{6,7},{7,6},{8,9},{9,8},{10,11... | collective-permute-start | bytes 49160 | tf_op jit(solution)/shard_map/ppermute | solution.py:698
  6.9 9.3 %collective-permute-start = (bf16[80,1024]{1,0:T(8,128)(2,1)}, bf16[80,1024]{1,0:T(8,128)(2,1)S(1)}, u32[]{:S(2)}, u32[]{:S(2)}) collective-permute-start(bf16[80,1024]{1,0:T(8,128)(2,1)} %get-tuple-element.27), channel_id=1, source_target_pairs={{0,4},{4,0},{8,12},{12,8},{1,5},{5,1},{9,13},{13,9},{2,6},{6,2},{1... | collective-permute-start | bytes 491528 | tf_op jit(solution)/shard_map/ppermute | solution.py:724
  6.9 9.3 %collective-permute-start.1 = (bf16[80,1024]{1,0:T(8,128)(2,1)}, bf16[80,1024]{1,0:T(8,128)(2,1)S(1)}, u32[]{:S(2)}, u32[]{:S(2)}) collective-permute-start(bf16[80,1024]{1,0:T(8,128)(2,1)} %get-tuple-element.28), channel_id=1, source_target_pairs={{4,8},{8,4},{12,0},{0,12},{5,9},{9,5},{13,1},{1,13},{6,10},{10,6},... | collective-permute-start | bytes 491528 | tf_op jit(solution)/shard_map/ppermute | solution.py:725
  9.6 6.5 %collective-permute-start.5 = (bf16[64,128]{1,0:T(8,128)(2,1)S(1)}, bf16[64,128]{1,0:T(8,128)(2,1)S(1)}, u32[]{:S(2)}, u32[]{:S(2)}) collective-permute-start(bf16[64,128]{1,0:T(8,128)(2,1)S(1)} %add_convert_fusion._), channel_id=1, source_target_pairs={{0,18},{18,0},{1,19},{19,1},{2,16},{16,2},{3,17},{17,3},{4,22},{22... | collective-permute-start | bytes 49160 | tf_op jit(solution)/shard_map/ppermute | solution.py:701
  12.4 3.7 %collective-permute-start.6 = (bf16[64,128]{1,0:T(8,128)(2,1)S(1)}, bf16[64,128]{1,0:T(8,128)(2,1)S(1)}, u32[]{:S(2)}, u32[]{:S(2)}) collective-permute-start(bf16[64,128]{1,0:T(8,128)(2,1)S(1)} %add_convert_fusion._), channel_id=1, source_target_pairs={{0,16},{16,0},{1,17},{17,1},{2,18},{18,2},{3,19},{19,3},{4,20},{20... | collective-permute-start | bytes 49160 | tf_op jit(solution)/shard_map/ppermute | solution.py:701
  16.2 3.1 %copy-start.13 = (bf16[32,1024]{1,0:T(8,128)(2,1)S(1)}, bf16[32,1024]{1,0:T(8,128)(2,1)}, u32[]{:S(2)}) copy-start(bf16[32,1024]{1,0:T(8,128)(2,1)} %get-tuple-element.29) | copy-start | bytes 196612
  16.2 4.6 %copy-start.12 = (bf16[32,1024]{1,0:T(8,128)(2,1)S(1)}, bf16[32,1024]{1,0:T(8,128)(2,1)}, u32[]{:S(2)}) copy-start(bf16[32,1024]{1,0:T(8,128)(2,1)} %get-tuple-element.30) | copy-start | bytes 196612
  16.2 7.4 %copy-start = (f32[1,8,32,1024]{3,2,1,0:T(8,128)S(1)}, f32[1,8,32,1024]{3,2,1,0:T(8,128)}, u32[]{:S(2)}) copy-start(f32[1,8,32,1024]{3,2,1,0:T(8,128)} %x_ref.1) | copy-start | bytes 3145732
  16.2 7.3 %copy-start.3 = (f32[8,32,1024]{2,1,0:T(8,128)S(1)}, f32[8,32,1024]{2,1,0:T(8,128)}, u32[]{:S(2)}) copy-start(f32[8,32,1024]{2,1,0:T(8,128)} %get-tuple-element.26.y_ref) | copy-start | bytes 3145732
  16.2 7.3 %copy-start.5 = (s32[8,1024]{1,0:T(8,128)S(1)}, s32[8,1024]{1,0:T(8,128)}, u32[]{:S(2)}) copy-start(s32[8,1024]{1,0:T(8,128)} %wet_ref.1) | copy-start | bytes 98308
  16.3 7.3 %copy-start.10 = (f32[128]{0:T(128)S(1)}, f32[128]{0:T(128)}, u32[]{:S(2)}) copy-start(f32[128]{0:T(128)} %param.19) | copy-start | bytes 1540
  17.6 10.3 %copy-start.4 = (bf16[1024,512]{1,0:T(8,128)(2,1)S(1)}, bf16[1024,512]{1,0:T(8,128)(2,1)}, u32[]{:S(2)}) copy-start(bf16[1024,512]{1,0:T(8,128)(2,1)} %constant.5.clone.table_ref) | copy-start | bytes 3145732
  17.6 10.3 %copy-start.11 = (f32[128]{0:T(128)S(1)}, f32[128]{0:T(128)}, u32[]{:S(2)}) copy-start(f32[128]{0:T(128)} %param.18) | copy-start | bytes 1540
  17.6 3.8 %collective-permute-start.7 = (bf16[64,128]{1,0:T(8,128)(2,1)S(1)}, bf16[64,128]{1,0:T(8,128)(2,1)S(1)}, u32[]{:S(2)}, u32[]{:S(2)}) collective-permute-start(bf16[64,128]{1,0:T(8,128)(2,1)S(1)} %get-tuple-element.43), channel_id=1, source_target_pairs={{0,1},{1,0},{2,3},{3,2},{4,5},{5,4},{6,7},{7,6},{8,9},{9,8},{10,11... | collective-permute-start | bytes 49160 | tf_op jit(solution)/shard_map/ppermute | solution.py:761
  19.3 4.3 %collective-permute-start.2 = (bf16[32,1024]{1,0:T(8,128)(2,1)S(1)}, bf16[32,1024]{1,0:T(8,128)(2,1)S(1)}, u32[]{:S(2)}, u32[]{:S(2)}) collective-permute-start(bf16[32,1024]{1,0:T(8,128)(2,1)S(1)} %copy-done.13), channel_id=1, source_target_pairs={{16,17},{17,16},{18,19},{19,18},{0,8},{8,0},{1,9},{9,1},{2,10},{10... | collective-permute-start | bytes 196616 | tf_op jit(solution)/shard_map/ppermute | solution.py:727
  20.8 2.8 %collective-permute-start.3 = (bf16[32,1024]{1,0:T(8,128)(2,1)S(1)}, bf16[32,1024]{1,0:T(8,128)(2,1)S(1)}, u32[]{:S(2)}, u32[]{:S(2)}) collective-permute-start(bf16[32,1024]{1,0:T(8,128)(2,1)S(1)} %copy-done.12), channel_id=1, source_target_pairs={{17,18},{18,17},{16,20},{20,16},{19,23},{23,19},{0,4},{4,0},{1,5},... | collective-permute-start | bytes 196616 | tf_op jit(solution)/shard_map/ppermute | solution.py:728
  21.5 4.7 %collective-permute-start.8 = (bf16[64,128]{1,0:T(8,128)(2,1)S(1)}, bf16[64,128]{1,0:T(8,128)(2,1)S(1)}, u32[]{:S(2)}, u32[]{:S(2)}) collective-permute-start(bf16[64,128]{1,0:T(8,128)(2,1)S(1)} %get-tuple-element.47), channel_id=1, source_target_pairs={{0,2},{1,3},{2,0},{3,1},{4,6},{5,7},{6,4},{7,5},{8,10},{9,11},{10,... | collective-permute-start | bytes 49160 | tf_op jit(solution)/shard_map/ppermute | solution.py:763
  26.2 3.7 %collective-permute-start.10 = (bf16[128,128]{1,0:T(8,128)(2,1)S(1)}, bf16[128,128]{1,0:T(8,128)(2,1)S(1)}, u32[]{:S(2)}, u32[]{:S(2)}) collective-permute-start(bf16[128,128]{1,0:T(8,128)(2,1)S(1)} %get-tuple-element.46), channel_id=1, source_target_pairs={{4,8},{8,4},{12,0},{0,12},{5,9},{9,5},{13,1},{1,13},{6,10},{10,6},... | collective-permute-start | bytes 98312 | tf_op jit(solution)/shard_map/ppermute | solution.py:814
  26.3 3.6 %collective-permute-start.9 = (bf16[128,128]{1,0:T(8,128)(2,1)S(1)}, bf16[128,128]{1,0:T(8,128)(2,1)S(1)}, u32[]{:S(2)}, u32[]{:S(2)}) collective-permute-start(bf16[128,128]{1,0:T(8,128)(2,1)S(1)} %get-tuple-element.45), channel_id=1, source_target_pairs={{0,4},{4,0},{8,12},{12,8},{1,5},{5,1},{9,13},{13,9},{2,6},{6,2},{1... | collective-permute-start | bytes 98312 | tf_op jit(solution)/shard_map/ppermute | solution.py:813

commit v10 on v8

--- a/solution.py
+++ b/solution.py
@@ -81,7 +81,7 @@
     return 1.0 / grow, jnp.log(grow), sinh
 
 
-def surface_kernel(x_hbm, flux_hbm, s_ref, coarse_ref, x_ref, flux_ref, row_ref, x_sem, sem):
+def surface_kernel(x_hbm, flux_hbm, coarse_ref, x_ref, flux_ref, row_ref, x_sem, sem):
     rows, channels, columns = x_ref.shape
     col_group = lax.axis_index("gy")
     is_atmos = lax.axis_index("comp") == 0
@@ -115,65 +115,35 @@
             top[r].wait()
             row_ref[r : r + 1, :] = x_ref[r, 0:1, :] * gain
 
-    surface = to_tiles(row_ref[...])
-    s_ref[...] = surface
-    coarse_ref[...] = surface.astype(bf16)
-
-
-def pair_kernel(surface_ref, part_ref, _, __, sum_ref, coarse_ref, ___, ____):
-    total = surface_ref[...] + part_ref[...].astype(f32)
-    sum_ref[...] = total
-    coarse_ref[...] = total.astype(bf16)
+    coarse_ref[...] = to_tiles(row_ref[...]).astype(bf16)
 
 
 def forward_kernel(
-    groups_x, paired, x_hbm, wet_hbm, diff_hbm, table_hbm, s_hbm, kept_hbm, *refs
+    groups_x, paired, x_ref, wet_ref, diff_ref, table_ref, _, *refs
 ):
-    del s_hbm, kept_hbm
-    outs = 5 if paired else 6
-    y_hbm, *message_hbm = refs[:outs]
-    y_ref, *message_ref = refs[outs : 2 * outs]
-    e1_ref, e3_ref, e2_ref, e4_ref = message_ref[:4]
+    y_ref, e1_ref, e3_ref, e2_ref, e4_ref = refs[:5]
     if not paired:
-        pq_ref = message_ref[4]
-    x_ref, wet_ref, diff_ref, table_ref, flat_ref, edge_ref, sem, out_sem = refs[2 * outs :]
-    rows, channels, columns = x_ref.shape
+        pq_ref = refs[5]
+    flat_ref, edge_ref = refs[-2:]
+    _, rows, channels, columns = x_ref.shape
     half = columns // 2
     row_group = lax.axis_index("gx")
     col_group = lax.axis_index("gy")
     is_atmos = lax.axis_index("comp") == 0
 
-    x_copy = pltpu.make_async_copy(x_hbm.at[0], x_ref, sem.at[0])
-    y_copies = [
-        pltpu.make_async_copy(y_ref.at[r], y_hbm.at[r], out_sem.at[r]) for r in range(rows)
-    ]
-    message_copies = [
-        pltpu.make_async_copy(ref, hbm, out_sem.at[rows + k])
-        for k, (ref, hbm) in enumerate(zip(message_ref, message_hbm))
-    ]
-
     @pl.when(is_atmos)
     def _():
-        table_copy = pltpu.make_async_copy(table_hbm, table_ref, sem.at[1])
-        diff_copy = pltpu.make_async_copy(diff_hbm, diff_ref, sem.at[2])
-        for copy in (x_copy, table_copy, diff_copy):
-            copy.start()
-        x_copy.wait()
         first = col_group * channels
         for r in range(rows):
-            left, right = x_ref[r, :, :half], x_ref[r, :, half:]
+            left, right = x_ref[0, r, :, :half], x_ref[0, r, :, half:]
             flat_ref[r * channels : (r + 1) * channels, :half] = (left + right).astype(bf16)
             flat_ref[r * channels : (r + 1) * channels, half:] = (left - right).astype(bf16)
-        table_copy.wait()
         for k in range(2):
             lanes = slice(k * half, (k + 1) * half)
             part = jnp.dot(
                 flat_ref[:, lanes], table_ref[lanes, :], preferred_element_type=f32
             )
             y_ref[:, :, lanes] = part.reshape(rows, channels, half)
-        for copy in y_copies:
-            copy.start()
-        diff_copy.wait()
         diff = channel_column(diff_ref[...], channels, first)
         total = rows * groups_x
         base = (row_group * rows).astype(f32)
@@ -201,18 +171,9 @@
                 else:
                     pq_ref[0, :, lanes] = p.astype(bf16)
                     pq_ref[1, :, lanes] = q.astype(bf16)
-        for copy in message_copies:
-            copy.start()
-        for copy in y_copies + message_copies:
-            copy.wait()
 
     @pl.when(jnp.logical_not(is_atmos))
     def _():
-        wet_copy = pltpu.make_async_copy(wet_hbm, wet_ref, sem.at[1])
-        for copy in (x_copy, wet_copy):
-            copy.start()
-        x_copy.wait()
-        wet_copy.wait()
         levels = channels // 2
         lines = 2 * channels
         even_x = row_group % 2 == 0
@@ -223,11 +184,11 @@
         def put(out, last):
             @pl.when(last)
             def _():
-                out[0:lines, :] = x_ref[rows - 2 :].reshape(lines, columns).astype(bf16)
+                out[0:lines, :] = x_ref[0, rows - 2 :].reshape(lines, columns).astype(bf16)
 
             @pl.when(jnp.logical_not(last))
             def _():
-                out[0:lines, :] = x_ref[:2].reshape(lines, columns).astype(bf16)
+                out[0:lines, :] = x_ref[0, :2].reshape(lines, columns).astype(bf16)
 
             out[lines : lines + 16, :] = wet
 
@@ -239,7 +200,7 @@
                 for t in range(2):
                     at = (r * 2 + t) * 2
                     c = t * levels + level
-                    edge_ref[at : at + 2, :] = x_ref[r, c : c + 2, :]
+                    edge_ref[at : at + 2, :] = x_ref[0, r, c : c + 2, :]
             out[...] = edge_ref[...].astype(bf16)
 
         @pl.when(even_y)
@@ -251,11 +212,6 @@
         def _():
             put_edges(e2_ref, 0)
             put_edges(e4_ref, levels - 2)
-
-        for copy in message_copies:
-            copy.start()
-        for copy in message_copies:
-            copy.wait()
 
 
 def one_hot_kernel(
@@ -283,22 +239,29 @@
     surfaces = refs[:n_surfaces]
     (
         src_hot_ref, dst_hot_ref, src_row_ref, dst_row_ref, a_count, m_count, a_weight, m_weight,
-        _, _,
-        land_ref, sent_ref, weight_ref, gath_ref, val_ref, sem,
+        _,
+        land_ref, sent_ref, weight_ref, gath_ref, val_ref, count_ref, sem,
     ) = refs[n_surfaces:]
     is_atmos = lax.axis_index("comp") == 0
     blocks, points = val_ref.shape
     cells = surfaces[0].shape[0]
 
+    def operands(weight, count):
+        return [
+            pltpu.make_async_copy(count, count_ref, sem.at[0]),
+            pltpu.make_async_copy(weight.at[0, 0], weight_ref, sem.at[1]),
+        ]
+
     @pl.when(is_atmos)
     def _():
-        pltpu.make_async_copy(m_weight.at[0, 0], weight_ref, sem).start()
+        for copy in operands(m_weight, m_count):
+            copy.start()
 
     @pl.when(jnp.logical_not(is_atmos))
     def _():
-        pltpu.make_async_copy(a_weight.at[0, 0], weight_ref, sem).start()
-
-    count = jnp.where(is_atmos, m_count[0, 0], a_count[0, 0])
+        for copy in operands(a_weight, a_count):
+            copy.start()
+
     pair = 2 * points
     row_iota = lax.broadcasted_iota(jnp.int32, (cells, points), 0)
     table = sum(surface[...].astype(f32) for surface in surfaces).astype(bf16)
@@ -312,14 +275,9 @@
             gath_ref[b + k : b + k + 1, :] = jnp.sum(part, axis=0, keepdims=True)
     gathered = gath_ref[...].astype(bf16)
 
-    @pl.when(is_atmos)
-    def _():
-        pltpu.make_async_copy(m_weight.at[0, 0], weight_ref, sem).wait()
-
-    @pl.when(jnp.logical_not(is_atmos))
-    def _():
-        pltpu.make_async_copy(a_weight.at[0, 0], weight_ref, sem).wait()
-
+    for copy in operands(a_weight, a_count):
+        copy.wait()
+    count = count_ref[0, 0]
     block_iota = lax.broadcasted_iota(jnp.int32, (blocks, points), 0)
     values = jnp.zeros((blocks, points), f32)
     for b in range(0, blocks, 2):
@@ -664,18 +622,17 @@
     paired = groups_x == 4
     params = functools.partial(pltpu.CompilerParams, vmem_limit_bytes=40 * 2**20)
     vmem = pl.BlockSpec(memory_space=pltpu.VMEM)
-    smem = pl.BlockSpec(memory_space=pltpu.SMEM)
     hbm = pl.BlockSpec(memory_space=pltpu.HBM)
     anywhere = pl.BlockSpec(memory_space=pl.ANY)
 
     def shape(dims, dtype):
         return jax.ShapeDtypeStruct(dims, dtype)
 
-    partial_surface, coarse = pl.pallas_call(
+    coarse = pl.pallas_call(
         surface_kernel,
-        out_shape=[shape((cells, LANES), f32), shape((cells, LANES), bf16)],
+        out_shape=shape((cells, LANES), bf16),
         in_specs=[hbm, hbm],
-        out_specs=[vmem, vmem],
+        out_specs=vmem,
         scratch_shapes=[
             pltpu.VMEM((rows, channels, columns), f32),
             pltpu.VMEM(flux_row.shape, f32),
@@ -686,10 +643,13 @@
         compiler_params=pltpu.CompilerParams(vmem_limit_bytes=58 * 2**20),
         name="surface_partials",
     )(fields, flux_row)
+    surfaces = []
+    for mask in reversed(range(groups_y)):
+        route = both_ways([(j, groups_y + (j ^ mask)) for j in range(groups_y)])
+        surfaces.append(lax.ppermute(coarse, ("comp", "gy"), route))
 
     lines = 2 * channels + 16
     shapes = [
-        shape((cells, LANES), f32),
         shape((rows, channels, columns), f32),
         shape((lines, columns), bf16),
         shape((lines, columns), bf16),
@@ -698,55 +658,22 @@
     ]
     if not paired:
         shapes.append(shape((2, channels, columns), bf16))
-    partial_surface, y, e1, e3, e2, e4, *sums = pl.pallas_call(
+    y, e1, e3, e2, e4, *sums = pl.pallas_call(
         functools.partial(forward_kernel, groups_x, paired),
         out_shape=shapes,
-        in_specs=[hbm] * 4 + [anywhere],
-        out_specs=[anywhere] + [hbm] * (len(shapes) - 1),
-        scratch_shapes=[pltpu.VMEM(out.shape, out.dtype) for out in shapes[1:]]
-        + [
-            pltpu.VMEM((rows, channels, columns), f32),
-            pltpu.VMEM((rows, columns), jnp.int32),
-            pltpu.VMEM(diff_row.shape, f32),
-            pltpu.VMEM(forward.shape, bf16),
+        in_specs=[vmem] * 4 + [anywhere],
+        out_specs=[vmem] * len(shapes),
+        scratch_shapes=[
             pltpu.VMEM((rows * channels, columns), bf16),
             pltpu.VMEM((4 * rows, columns), f32),
-            pltpu.SemaphoreType.DMA((3,)),
-            pltpu.SemaphoreType.DMA((rows + len(shapes) - 2,)),
         ],
-        input_output_aliases={4: 0},
-        compiler_params=pltpu.CompilerParams(vmem_limit_bytes=58 * 2**20),
+        compiler_params=params(),
         name="forward_or_halos",
-    )(fields, wet_cells, diff_row, forward, partial_surface)
-
+    )(fields, wet_cells, diff_row, forward, surfaces[0])
     masks = [1 << bit for bit in range(groups_y.bit_length() - 1)]
 
     def sum_route(mask):
         return [(j, j ^ mask) for j in range(groups_y)]
-
-    def partner_route(mask):
-        return both_ways([(j, groups_y + (j ^ mask)) for j in range(groups_y)])
-
-    surface = partial_surface
-    for mask in masks[:-1]:
-        part = lax.ppermute(coarse, "gy", sum_route(mask))
-        surface, coarse, e1, e3 = pl.pallas_call(
-            pair_kernel,
-            out_shape=[
-                shape(surface.shape, f32),
-                shape(surface.shape, bf16),
-                shape(e1.shape, bf16),
-                shape(e3.shape, bf16),
-            ],
-            in_specs=[vmem, vmem, anywhere, anywhere],
-            out_specs=[vmem, vmem, anywhere, anywhere],
-            input_output_aliases={2: 2, 3: 3},
-            compiler_params=params(),
-            name="pair_sum",
-        )(surface, part, e1, e3)
-    surfaces = [
-        lax.ppermute(coarse, ("comp", "gy"), partner_route(mask)) for mask in masks[-1:] + [0]
-    ]
 
     def ring_pairs(count, odd):
         return [(a, (a + 1) % count) for a in range(odd, count, 2)]
@@ -790,19 +717,20 @@
     landing, sent = pl.pallas_call(
         functools.partial(regrid_kernel, len(surfaces)),
         out_shape=[shape((cells, LANES), f32), shape((cells, LANES), bf16)],
-        in_specs=[vmem] * (len(surfaces) + 4) + [smem, smem, hbm, hbm, anywhere, anywhere],
+        in_specs=[vmem] * (len(surfaces) + 4) + [hbm] * 4 + [anywhere],
         out_specs=[vmem] * 2,
         scratch_shapes=[
             pltpu.VMEM((blocks, points, points), bf16),
             pltpu.VMEM((blocks, points), f32),
             pltpu.VMEM((blocks, points), f32),
-            pltpu.SemaphoreType.DMA,
+            pltpu.SMEM((1, 1), jnp.int32),
+            pltpu.SemaphoreType.DMA((2,)),
         ],
         compiler_params=params(),
         name="regrid_blocks",
     )(
         *surfaces, *one_hots, a2o_count, marine_air_piece_tally,
-        a2o_weight, marine_air_piece_factor, e1, e3,
+        a2o_weight, marine_air_piece_factor, y,
     )
     for mask in masks[:-1]:
         landing = landing + lax.ppermute(sent, "gy", sum_route(mask)).astype(f32)

time: 34.3 us -> 38.2 us (1.11); the launches traced: 34 us -> 37.4 us
  local copies, waits for them, and re-layouts: 2.41 us -> 7.98 us
  Pallas kernels: 10.7 us -> 7.37 us
  starting transfers between devices: 13.6 us -> 15.3 us
  waiting for transfers between devices: 5.77 us -> 5.29 us
    unnamed x34 -> x30, local copies, waits for them, and re-layouts: 2.41 us -> 7.98 us
    ppermute x1, waiting for transfers between devices: 0.01 us -> 2.79 us  [local(): e3 = lax.ppermute(e3, 'gx', both_ways(ring_pairs(groups_x, 1)))]
    pallas_call x1, Pallas kernels: 3.41 us -> 0.65 us  [local(): pl.pallas_call(functools.partial(forward_kernel, groups_x, paired), out_s...]
    ppermute x1, waiting for transfers between devices: 1.86 us -> 0.21 us  [local(): landing = landing + lax.ppermute(sent, 'gy', sum_route(mask)).astype(f32)]
    ppermute x1, waiting for transfers between devices: 1.59 us -> 0.01 us  [local(): part = lax.ppermute(sent, 'gy', sum_route(masks[-1]))]
    ppermute x1, starting transfers between devices: 1.6 us -> 0.14 us  [local(): e3 = lax.ppermute(e3, 'gx', both_ways(ring_pairs(groups_x, 1)))]
    ppermute x1, starting transfers between devices: 2.14 us -> 3.15 us  [local(): part = lax.ppermute(sent, 'gy', sum_route(masks[-1]))]
    ppermute x1, starting transfers between devices: 0.53 us -> 1.49 us  [local(): e2 = lax.ppermute(e2, axes, level_route(0))]
  transfers between devices with their start and end apart: 11 -> 12, of which waited for: 4 -> 3; matrix products, arithmetic and copies ran while one was open for 0% -> 0% of each run, Pallas kernels for 16% -> 7%
where the time goes in v10:
time: 38.2 us; the launch traced here: 37.4 us
  starting transfers between devices  15.3 us (40%)
  local copies, waits for them, and re-layouts  7.98 us (21%)
  Pallas kernels  7.37 us (19%)
  waiting for transfers between devices  5.29 us (14%)
  between operations  1.47 us (4%)
    unnamed x30, local copies, waits for them, and re-layouts  7.98 us
    ppermute x4, starting transfers between devices, local(): surfaces.append(lax.ppermute(coarse, ('comp', 'gy'), route))  7.75 us
    ppermute x1, starting transfers between devices, local(): part = lax.ppermute(sent, 'gy', sum_route(masks[-1]))  3.15 us
    ppermute x1, waiting for transfers between devices, local(): e3 = lax.ppermute(e3, 'gx', both_ways(ring_pairs(groups_x, 1)))  2.79 us
    ppermute x1, waiting for transfers between devices, local(): far = lax.ppermute(far, 'gx', both_ways(ring_pairs(groups_x, 1)))  2.27 us
    pallas_call x1, Pallas kernels, local(): pl.pallas_call(surface_kernel, out_shape=shape((cells, LANES), bf16), in_...  2.08 us
    pallas_call x1, Pallas kernels, local(): pl.pallas_call(functools.partial(regrid_kernel, len(surfaces)), out_shape...  1.5 us
    ppermute x1, starting transfers between devices, local(): e2 = lax.ppermute(e2, axes, level_route(0))  1.49 us
  transfers between devices with their start and end apart: 12, of which 3 were waited for; matrix products, arithmetic and copies ran while one was open for 0% of the time, Pallas kernels for 7%

profile of v10, /device:TPU:0, one launch (start us, length us, event | category | flops | bytes accessed | tf_op | source)
XLA Modules:
  0.0 37.4 jit_solution(11012250354328969431)
XLA Ops:
  0.0 0.0 copy-start.3
  0.0 2.1 %surface_partials.1._ = bf16[64,128]{1,0:T(8,128)(2,1)} custom-call(f32[1,8,32,1024]{3,2,1,0:T(8,128)} %x_ref.3, f32[1,128]{1,0:T(1,128)} %bitcast.6), custom_call_target="tpu_custom_call" | custom-call | tf_op jit(solution)/shard_map/surface_partials/pallas_call | solution.py:631
  2.1 5.6 %collective-permute-start = (bf16[64,128]{1,0:T(8,128)(2,1)}, bf16[64,128]{1,0:T(8,128)(2,1)S(1)}, u32[]{:S(2)}, u32[]{:S(2)}) collective-permute-start(bf16[64,128]{1,0:T(8,128)(2,1)} %surface_partials.1._), channel_id=1, source_target_pairs={{0,19},{19,0},{1,18},{18,1},{2,17},{17,2},{3,16},{16,3},{4,23},{23... | collective-permute-start | bytes 49160 | tf_op jit(solution)/shard_map/ppermute | solution.py:649
  7.7 0.9 %collective-permute-start.7 = (bf16[64,128]{1,0:T(8,128)(2,1)}, bf16[64,128]{1,0:T(8,128)(2,1)S(1)}, u32[]{:S(2)}, u32[]{:S(2)}) collective-permute-start(bf16[64,128]{1,0:T(8,128)(2,1)} %surface_partials.1._), channel_id=1, source_target_pairs={{0,16},{16,0},{1,17},{17,1},{2,18},{18,2},{3,19},{19,3},{4,20},{20... | collective-permute-start | bytes 49160 | tf_op jit(solution)/shard_map/ppermute | solution.py:649
  8.7 0.1 collective-permute-start.6
  8.7 1.1 %collective-permute-start.5 = (bf16[64,128]{1,0:T(8,128)(2,1)}, bf16[64,128]{1,0:T(8,128)(2,1)S(1)}, u32[]{:S(2)}, u32[]{:S(2)}) collective-permute-start(bf16[64,128]{1,0:T(8,128)(2,1)} %surface_partials.1._), channel_id=1, source_target_pairs={{0,18},{18,0},{1,19},{19,1},{2,16},{16,2},{3,17},{17,3},{4,22},{22... | collective-permute-start | bytes 49160 | tf_op jit(solution)/shard_map/ppermute | solution.py:649
  11.1 0.0 copy-start.7
  11.1 0.7 %copy-done.7 = bf16[64,128]{1,0:T(8,128)(2,1)S(1)} copy-done((bf16[64,128]{1,0:T(8,128)(2,1)S(1)}, bf16[64,128]{1,0:T(8,128)(2,1)}, u32[]{:S(2)}) %copy-start.7) | copy-done | bytes 16408
  11.9 0.0 copy-start.8
  11.9 0.7 %copy-done.8 = s32[1,1,32,128]{3,2,1,0:T(8,128)S(1)} copy-done((s32[1,1,32,128]{3,2,1,0:T(8,128)S(1)}, s32[1,1,32,128]{3,2,1,0:T(8,128)}, u32[]{:S(2)}) %copy-start.8) | copy-done | bytes 16408
  12.6 0.0 copy-start.9
  12.6 0.7 %copy-done.9 = s32[1,1,32,128]{3,2,1,0:T(8,128)S(1)} copy-done((s32[1,1,32,128]{3,2,1,0:T(8,128)S(1)}, s32[1,1,32,128]{3,2,1,0:T(8,128)}, u32[]{:S(2)}) %copy-start.9) | copy-done | bytes 16408
  13.3 0.0 copy-start.10
  13.3 0.7 %copy-done.10 = s32[1,1,32,128]{3,2,1,0:T(8,128)S(1)} copy-done((s32[1,1,32,128]{3,2,1,0:T(8,128)S(1)}, s32[1,1,32,128]{3,2,1,0:T(8,128)}, u32[]{:S(2)}) %copy-start.10) | copy-done | bytes 16408
  14.0 0.0 copy-start.11
  14.0 0.7 %copy-done.11 = s32[1,1,32,128]{3,2,1,0:T(8,128)S(1)} copy-done((s32[1,1,32,128]{3,2,1,0:T(8,128)S(1)}, s32[1,1,32,128]{3,2,1,0:T(8,128)}, u32[]{:S(2)}) %copy-start.11) | copy-done | bytes 16408
  14.7 0.6 %one_hots.1 = (bf16[128,4096]{1,0:T(8,128)(2,1)S(1)}, bf16[128,4096]{1,0:T(8,128)(2,1)S(1)}, s32[32,128]{1,0:T(8,128)S(1)}, s32[32,128]{1,0:T(8,128)S(1)}) custom-call(s32[1,1,32,128]{3,2,1,0:T(8,128)S(1)} %copy-done.8, s32[1,1,32,128]{3,2,1,0:T(8,128)S(1)} %copy-done.9, s32[1,1,32,128]{3,2,1,0:T(8,128)S(1)} %copy-done.10, s32[1,1,32,128]{3,2,1,0:T(8,128)S(1)} %copy-done.11, ...), custom_call_target="tpu_custom_call" | custom-call | tf_op jit(solution)/shard_map/one_hots/pallas_call | solution.py:704
  15.3 0.0 collective-permute-done._.refs_0_
  15.4 0.0 copy-start
  15.4 1.2 %copy-done = f32[1,8,32,1024]{3,2,1,0:T(8,128)S(1)} copy-done((f32[1,8,32,1024]{3,2,1,0:T(8,128)S(1)}, f32[1,8,32,1024]{3,2,1,0:T(8,128)}, u32[]{:S(2)}) %copy-start) | copy-done | bytes 1048600
  16.6 0.0 copy-start.2
  16.6 1.2 %copy-done.2 = bf16[1024,512]{1,0:T(8,128)(2,1)S(1)} copy-done((bf16[1024,512]{1,0:T(8,128)(2,1)S(1)}, bf16[1024,512]{1,0:T(8,128)(2,1)}, u32[]{:S(2)}) %copy-start.2) | copy-done | bytes 1048600
  17.8 0.0 copy-start.6
  17.8 0.8 %copy-done.6 = s32[8,1024]{1,0:T(8,128)S(1)} copy-done((s32[8,1024]{1,0:T(8,128)S(1)}, s32[8,1024]{1,0:T(8,128)}, u32[]{:S(2)}) %copy-start.6) | copy-done | bytes 32792
  18.6 0.0 copy-start.12
  18.6 0.7 %copy-done.12 = f32[128]{0:T(128)S(1)} copy-done((f32[128]{0:T(128)S(1)}, f32[128]{0:T(128)}, u32[]{:S(2)}) %copy-start.12) | copy-done | bytes 536
  19.2 0.0 copy-start.4
  19.2 0.7 %forward_or_halos.1 = (f32[8,32,1024]{2,1,0:T(8,128)S(1)}, bf16[80,1024]{1,0:T(8,128)(2,1)S(1)}, bf16[80,1024]{1,0:T(8,128)(2,1)S(1)}, bf16[32,1024]{1,0:T(8,128)(2,1)S(1)}, bf16[32,1024]{1,0:T(8,128)(2,1)S(1)}) custom-call(f32[1,8,32,1024]{3,2,1,0:T(8,128)S(1)} %copy-done, s32[8,1024]{1,0:T(8,128)S(1)} %copy-done.6, f32[1,128]{1,0:T(1,128)S(1)} %bitcast.3, ...), custom_call_target="tpu_custom_call" | custom-call | tf_op jit(solution)/shard_map/forward_or_halos/pallas_call | solution.py:661
  19.9 0.0 collective-permute-done.7.refs_3_
  19.9 0.0 collective-permute-done.6.refs_2_
  19.9 0.0 collective-permute-done.5.refs_1_
  19.9 0.0 copy-done.3
  19.9 0.5 %copy-done.4 = bf16[1,1,32,128,128]{4,3,2,1,0:T(8,128)(2,1)S(1)} copy-done((bf16[1,1,32,128,128]{4,3,2,1,0:T(8,128)(2,1)S(1)}, bf16[1,1,32,128,128]{4,3,2,1,0:T(8,128)(2,1)}, u32[]{:S(2)}) %copy-start.4) | copy-done | bytes 1048600
  20.4 0.0 copy-start.1
  20.4 0.0 copy-start.13
  20.5 1.5 %regrid_blocks.1 = (f32[64,128]{1,0:T(8,128)S(1)}, bf16[64,128]{1,0:T(8,128)(2,1)S(1)}) custom-call(bf16[64,128]{1,0:T(8,128)(2,1)S(1)} %collective-permute-done._.refs_0_, bf16[64,128]{1,0:T(8,128)(2,1)S(1)} %collective-permute-done.5.refs_1_, bf16[64,128]{1,0:T(8,128)(2,1)S(1)} %collective-permute-done.6.refs_2_, ...), custom_call_target="tpu_custom_call" | custom-call | tf_op jit(solution)/shard_map/regrid_blocks/pallas_call | solution.py:717
  22.0 0.0 copy-start.5
  22.0 0.0 copy-start.14
  22.0 1.4 %collective-permute-start.8 = (bf16[64,128]{1,0:T(8,128)(2,1)S(1)}, bf16[64,128]{1,0:T(8,128)(2,1)S(1)}, u32[]{:S(2)}, u32[]{:S(2)}) collective-permute-start(bf16[64,128]{1,0:T(8,128)(2,1)S(1)} %get-tuple-element.39), channel_id=1, source_target_pairs={{0,1},{1,0},{2,3},{3,2},{4,5},{5,4},{6,7},{7,6},{8,9},{9,8},{10,11... | collective-permute-start | bytes 49160 | tf_op jit(solution)/shard_map/ppermute | solution.py:736
  23.4 1.5 %collective-permute-start.3 = (bf16[32,1024]{1,0:T(8,128)(2,1)S(1)}, bf16[32,1024]{1,0:T(8,128)(2,1)S(1)}, u32[]{:S(2)}, u32[]{:S(2)}) collective-permute-start(bf16[32,1024]{1,0:T(8,128)(2,1)S(1)} %get-tuple-element.27), channel_id=1, source_target_pairs={{16,17},{17,16},{18,19},{19,18},{0,8},{8,0},{1,9},{9,1},{2,10},{10... | collective-permute-start | bytes 196616 | tf_op jit(solution)/shard_map/ppermute | solution.py:701
  24.9 0.0 collective-permute-start.4
  24.9 0.5 %collective-permute-start.1 = (bf16[80,1024]{1,0:T(8,128)(2,1)S(1)}, bf16[80,1024]{1,0:T(8,128)(2,1)S(1)}, u32[]{:S(2)}, u32[]{:S(2)}) collective-permute-start(bf16[80,1024]{1,0:T(8,128)(2,1)S(1)} %get-tuple-element.25), channel_id=1, source_target_pairs={{0,4},{4,0},{8,12},{12,8},{1,5},{5,1},{9,13},{13,9},{2,6},{6,2},{1... | collective-permute-start | bytes 491528 | tf_op jit(solution)/shard_map/ppermute | solution.py:698
  25.4 0.1 collective-permute-start.2
  25.6 0.2 collective-permute-done.8
  25.8 3.1 %collective-permute-start.9 = (bf16[64,128]{1,0:T(8,128)(2,1)S(1)}, bf16[64,128]{1,0:T(8,128)(2,1)S(1)}, u32[]{:S(2)}, u32[]{:S(2)}) collective-permute-start(bf16[64,128]{1,0:T(8,128)(2,1)S(1)} %get-tuple-element.43), channel_id=1, source_target_pairs={{0,2},{1,3},{2,0},{3,1},{4,6},{5,7},{6,4},{7,5},{8,10},{9,11},{10,... | collective-permute-start | bytes 49160 | tf_op jit(solution)/shard_map/ppermute | solution.py:738
  28.9 0.0 collective-permute-done.3.e2_ref
  28.9 0.0 collective-permute-done.4.e4_ref
  29.0 0.0 collective-permute-done.1.e1_ref
  29.0 2.8 %collective-permute-done.2.e3_ref = bf16[80,1024]{1,0:T(8,128)(2,1)S(1)} collective-permute-done((bf16[80,1024]{1,0:T(8,128)(2,1)S(1)}, bf16[80,1024]{1,0:T(8,128)(2,1)S(1)}, u32[]{:S(2)}, u32[]{:S(2)}) %collective-permute-start.2) | collective-permute-done | bytes 163872 | tf_op jit(solution)/shard_map/ppermute | solution.py:699
  31.7 0.0 copy-done.1
  31.7 0.0 copy-done.13
  31.8 0.9 %damping_or_first_step.1 = (bf16[256,1024]{1,0:T(8,128)(2,1)S(1)}, f32[7,16,1024]{2,1,0:T(8,128)S(1)}, f32[10,2,24,1024]{3,2,1,0:T(8,128)S(1)}) custom-call(f32[1,8,32,1024]{3,2,1,0:T(8,128)S(1)} %copy-done.1, s32[8,1024]{1,0:T(8,128)S(1)} %copy-done.6, f32[1,128]{1,0:T(1,128)S(1)} %bitcast.4, f32[8,32,1024]{2,1,0:T(8,128)S(1)} %get-tuple-element.24.y_ref.refs_12_, ...), custom_call_target="tpu_custom_call" | custom-call | tf_op jit(solution)/shard_map/damping_or_first_step/pallas_call | solution.py:757
  32.7 0.0 collective-permute-done.9.part_ref
  32.7 0.2 collective-permute-start.10
  32.9 0.6 %collective-permute-start.11 = (bf16[128,128]{1,0:T(8,128)(2,1)S(1)}, bf16[128,128]{1,0:T(8,128)(2,1)S(1)}, u32[]{:S(2)}, u32[]{:S(2)}) collective-permute-start(bf16[128,128]{1,0:T(8,128)(2,1)S(1)} %get-tuple-element.42), channel_id=1, source_target_pairs={{4,8},{8,4},{12,0},{0,12},{5,9},{9,5},{13,1},{1,13},{6,10},{10,6},... | collective-permute-start | bytes 98312 | tf_op jit(solution)/shard_map/ppermute | solution.py:789
  33.6 0.0 copy-done.5
  33.6 0.0 copy-done.14
  33.6 0.4 %inverse_or_second_step.1 = (f32[8,32,1024]{2,1,0:T(8,128)S(1)}, f32[32,128]{1,0:T(8,128)S(1)}) custom-call(f32[1,128]{1,0:T(1,128)S(1)} %bitcast.5, bf16[1024,512]{1,0:T(8,128)(2,1)S(1)} %copy-done.5, bf16[256,1024]{1,0:T(8,128)(2,1)S(1)} %get-tuple-element.29.zb_ref, f32[7,16,1024]{2,1,0:T(8,128)S(1)} %get-tuple-element.30.c_ref._, ...), custom_call_target="tpu_custom_call" | custom-call | tf_op jit(solution)/shard_map/inverse_or_second_step/pallas_call | solution.py:790
  34.0 0.0 collective-permute-done.10.near_ref
  34.0 2.3 %collective-permute-done.11.far_ref = bf16[128,128]{1,0:T(8,128)(2,1)S(1)} collective-permute-done((bf16[128,128]{1,0:T(8,128)(2,1)S(1)}, bf16[128,128]{1,0:T(8,128)(2,1)S(1)}, u32[]{:S(2)}, u32[]{:S(2)}) %collective-permute-start.11) | collective-permute-done | bytes 32800 | tf_op jit(solution)/shard_map/ppermute | solution.py:789
  36.3 1.1 %add_surface_terms.1 = f32[1,8,32,1024]{3,2,1,0:T(8,128)} custom-call(f32[32,128]{1,0:T(8,128)S(1)} %get-tuple-element.32.column_ref, f32[8,32,1024]{2,1,0:T(8,128)S(1)} %get-tuple-element.33.base_ref, f32[7,16,1024]{2,1,0:T(8,128)S(1)} %get-tuple-element.30.c_ref._, f32[64,128]{1,0:T(8,128)S(1)} %get-tuple-element.40.sum_ref, ...), custom_call_target="tpu_custom_call" | custom-call | tf_op jit(solution)/shard_map/add_surface_terms/pallas_call | solution.py:798
  (2 shorter events, 0.1 us)
Async XLA Ops:
  0.0 19.9 %copy-start.3 = (bf16[1,1,32,128,128]{4,3,2,1,0:T(8,128)(2,1)S(1)}, bf16[1,1,32,128,128]{4,3,2,1,0:T(8,128)(2,1)}, u32[]{:S(2)}) copy-start(bf16[1,1,32,128,128]{4,3,2,1,0:T(8,128)(2,1)} %refs_10_.1) | copy-start | bytes 3145732
  2.1 13.3 %collective-permute-start = (bf16[64,128]{1,0:T(8,128)(2,1)}, bf16[64,128]{1,0:T(8,128)(2,1)S(1)}, u32[]{:S(2)}, u32[]{:S(2)}) collective-permute-start(bf16[64,128]{1,0:T(8,128)(2,1)} %surface_partials.1._), channel_id=1, source_target_pairs={{0,19},{19,0},{1,18},{18,1},{2,17},{17,2},{3,16},{16,3},{4,23},{23... | collective-permute-start | bytes 49160 | tf_op jit(solution)/shard_map/ppermute | solution.py:649
  7.7 12.2 %collective-permute-start.7 = (bf16[64,128]{1,0:T(8,128)(2,1)}, bf16[64,128]{1,0:T(8,128)(2,1)S(1)}, u32[]{:S(2)}, u32[]{:S(2)}) collective-permute-start(bf16[64,128]{1,0:T(8,128)(2,1)} %surface_partials.1._), channel_id=1, source_target_pairs={{0,16},{16,0},{1,17},{17,1},{2,18},{18,2},{3,19},{19,3},{4,20},{20... | collective-permute-start | bytes 49160 | tf_op jit(solution)/shard_map/ppermute | solution.py:649
  8.7 11.2 %collective-permute-start.6 = (bf16[64,128]{1,0:T(8,128)(2,1)}, bf16[64,128]{1,0:T(8,128)(2,1)S(1)}, u32[]{:S(2)}, u32[]{:S(2)}) collective-permute-start(bf16[64,128]{1,0:T(8,128)(2,1)} %surface_partials.1._), channel_id=1, source_target_pairs={{0,17},{17,0},{1,16},{16,1},{2,19},{19,2},{3,18},{18,3},{4,21},{21... | collective-permute-start | bytes 49160 | tf_op jit(solution)/shard_map/ppermute | solution.py:649
  8.7 11.2 %collective-permute-start.5 = (bf16[64,128]{1,0:T(8,128)(2,1)}, bf16[64,128]{1,0:T(8,128)(2,1)S(1)}, u32[]{:S(2)}, u32[]{:S(2)}) collective-permute-start(bf16[64,128]{1,0:T(8,128)(2,1)} %surface_partials.1._), channel_id=1, source_target_pairs={{0,18},{18,0},{1,19},{19,1},{2,16},{16,2},{3,17},{17,3},{4,22},{22... | collective-permute-start | bytes 49160 | tf_op jit(solution)/shard_map/ppermute | solution.py:649
  11.1 0.7 %copy-start.7 = (bf16[64,128]{1,0:T(8,128)(2,1)S(1)}, bf16[64,128]{1,0:T(8,128)(2,1)}, u32[]{:S(2)}) copy-start(bf16[64,128]{1,0:T(8,128)(2,1)} %surface_partials.1._) | copy-start | bytes 49156
  11.9 0.7 %copy-start.8 = (s32[1,1,32,128]{3,2,1,0:T(8,128)S(1)}, s32[1,1,32,128]{3,2,1,0:T(8,128)}, u32[]{:S(2)}) copy-start(s32[1,1,32,128]{3,2,1,0:T(8,128)} %a_src.1) | copy-start | bytes 49156
  12.6 0.7 %copy-start.9 = (s32[1,1,32,128]{3,2,1,0:T(8,128)S(1)}, s32[1,1,32,128]{3,2,1,0:T(8,128)}, u32[]{:S(2)}) copy-start(s32[1,1,32,128]{3,2,1,0:T(8,128)} %a_dst.1) | copy-start | bytes 49156
  13.3 0.7 %copy-start.10 = (s32[1,1,32,128]{3,2,1,0:T(8,128)S(1)}, s32[1,1,32,128]{3,2,1,0:T(8,128)}, u32[]{:S(2)}) copy-start(s32[1,1,32,128]{3,2,1,0:T(8,128)} %m_src.1) | copy-start | bytes 49156
  14.0 0.7 %copy-start.11 = (s32[1,1,32,128]{3,2,1,0:T(8,128)S(1)}, s32[1,1,32,128]{3,2,1,0:T(8,128)}, u32[]{:S(2)}) copy-start(s32[1,1,32,128]{3,2,1,0:T(8,128)} %m_dst.1) | copy-start | bytes 49156
  15.4 1.2 %copy-start = (f32[1,8,32,1024]{3,2,1,0:T(8,128)S(1)}, f32[1,8,32,1024]{3,2,1,0:T(8,128)}, u32[]{:S(2)}) copy-start(f32[1,8,32,1024]{3,2,1,0:T(8,128)} %x_ref.3) | copy-start | bytes 3145732
  16.6 1.2 %copy-start.2 = (bf16[1024,512]{1,0:T(8,128)(2,1)S(1)}, bf16[1024,512]{1,0:T(8,128)(2,1)}, u32[]{:S(2)}) copy-start(bf16[1024,512]{1,0:T(8,128)(2,1)} %constant.4.clone.table_ref) | copy-start | bytes 3145732
  17.8 0.8 %copy-start.6 = (s32[8,1024]{1,0:T(8,128)S(1)}, s32[8,1024]{1,0:T(8,128)}, u32[]{:S(2)}) copy-start(s32[8,1024]{1,0:T(8,128)} %wet_ref.3) | copy-start | bytes 98308
  18.6 0.7 %copy-start.12 = (f32[128]{0:T(128)S(1)}, f32[128]{0:T(128)}, u32[]{:S(2)}) copy-start(f32[128]{0:T(128)} %param.19) | copy-start | bytes 1540
  19.2 1.2 %copy-start.4 = (bf16[1,1,32,128,128]{4,3,2,1,0:T(8,128)(2,1)S(1)}, bf16[1,1,32,128,128]{4,3,2,1,0:T(8,128)(2,1)}, u32[]{:S(2)}) copy-start(bf16[1,1,32,128,128]{4,3,2,1,0:T(8,128)(2,1)} %refs_11_.1) | copy-start | bytes 3145732
  20.4 11.3 %copy-start.1 = (f32[1,8,32,1024]{3,2,1,0:T(8,128)S(1)}, f32[1,8,32,1024]{3,2,1,0:T(8,128)}, u32[]{:S(2)}) copy-start(f32[1,8,32,1024]{3,2,1,0:T(8,128)} %x_ref.3) | copy-start | bytes 3145732
  20.4 11.3 %copy-start.13 = (f32[128]{0:T(128)S(1)}, f32[128]{0:T(128)}, u32[]{:S(2)}) copy-start(f32[128]{0:T(128)} %param.19) | copy-start | bytes 1540
  22.0 11.6 %copy-start.5 = (bf16[1024,512]{1,0:T(8,128)(2,1)S(1)}, bf16[1024,512]{1,0:T(8,128)(2,1)}, u32[]{:S(2)}) copy-start(bf16[1024,512]{1,0:T(8,128)(2,1)} %constant.5.clone.table_ref) | copy-start | bytes 3145732
  22.0 11.6 %copy-start.14 = (f32[128]{0:T(128)S(1)}, f32[128]{0:T(128)}, u32[]{:S(2)}) copy-start(f32[128]{0:T(128)} %param.18) | copy-start | bytes 1540
  22.0 3.8 %collective-permute-start.8 = (bf16[64,128]{1,0:T(8,128)(2,1)S(1)}, bf16[64,128]{1,0:T(8,128)(2,1)S(1)}, u32[]{:S(2)}, u32[]{:S(2)}) collective-permute-start(bf16[64,128]{1,0:T(8,128)(2,1)S(1)} %get-tuple-element.39), channel_id=1, source_target_pairs={{0,1},{1,0},{2,3},{3,2},{4,5},{5,4},{6,7},{7,6},{8,9},{9,8},{10,11... | collective-permute-start | bytes 49160 | tf_op jit(solution)/shard_map/ppermute | solution.py:736
  23.4 5.5 %collective-permute-start.3 = (bf16[32,1024]{1,0:T(8,128)(2,1)S(1)}, bf16[32,1024]{1,0:T(8,128)(2,1)S(1)}, u32[]{:S(2)}, u32[]{:S(2)}) collective-permute-start(bf16[32,1024]{1,0:T(8,128)(2,1)S(1)} %get-tuple-element.27), channel_id=1, source_target_pairs={{16,17},{17,16},{18,19},{19,18},{0,8},{8,0},{1,9},{9,1},{2,10},{10... | collective-permute-start | bytes 196616 | tf_op jit(solution)/shard_map/ppermute | solution.py:701
  24.9 4.0 %collective-permute-start.4 = (bf16[32,1024]{1,0:T(8,128)(2,1)S(1)}, bf16[32,1024]{1,0:T(8,128)(2,1)S(1)}, u32[]{:S(2)}, u32[]{:S(2)}) collective-permute-start(bf16[32,1024]{1,0:T(8,128)(2,1)S(1)} %get-tuple-element.28), channel_id=1, source_target_pairs={{17,18},{18,17},{16,20},{20,16},{19,23},{23,19},{0,4},{4,0},{1,5},... | collective-permute-start | bytes 196616 | tf_op jit(solution)/shard_map/ppermute | solution.py:702
  24.9 4.0 %collective-permute-start.1 = (bf16[80,1024]{1,0:T(8,128)(2,1)S(1)}, bf16[80,1024]{1,0:T(8,128)(2,1)S(1)}, u32[]{:S(2)}, u32[]{:S(2)}) collective-permute-start(bf16[80,1024]{1,0:T(8,128)(2,1)S(1)} %get-tuple-element.25), channel_id=1, source_target_pairs={{0,4},{4,0},{8,12},{12,8},{1,5},{5,1},{9,13},{13,9},{2,6},{6,2},{1... | collective-permute-start | bytes 491528 | tf_op jit(solution)/shard_map/ppermute | solution.py:698
  25.4 6.3 %collective-permute-start.2 = (bf16[80,1024]{1,0:T(8,128)(2,1)S(1)}, bf16[80,1024]{1,0:T(8,128)(2,1)S(1)}, u32[]{:S(2)}, u32[]{:S(2)}) collective-permute-start(bf16[80,1024]{1,0:T(8,128)(2,1)S(1)} %get-tuple-element.26), channel_id=1, source_target_pairs={{4,8},{8,4},{12,0},{0,12},{5,9},{9,5},{13,1},{1,13},{6,10},{10,6},... | collective-permute-start | bytes 491528 | tf_op jit(solution)/shard_map/ppermute | solution.py:699
  25.8 6.9 %collective-permute-start.9 = (bf16[64,128]{1,0:T(8,128)(2,1)S(1)}, bf16[64,128]{1,0:T(8,128)(2,1)S(1)}, u32[]{:S(2)}, u32[]{:S(2)}) collective-permute-start(bf16[64,128]{1,0:T(8,128)(2,1)S(1)} %get-tuple-element.43), channel_id=1, source_target_pairs={{0,2},{1,3},{2,0},{3,1},{4,6},{5,7},{6,4},{7,5},{8,10},{9,11},{10,... | collective-permute-start | bytes 49160 | tf_op jit(solution)/shard_map/ppermute | solution.py:738
  32.7 1.3 %collective-permute-start.10 = (bf16[128,128]{1,0:T(8,128)(2,1)S(1)}, bf16[128,128]{1,0:T(8,128)(2,1)S(1)}, u32[]{:S(2)}, u32[]{:S(2)}) collective-permute-start(bf16[128,128]{1,0:T(8,128)(2,1)S(1)} %get-tuple-element.41), channel_id=1, source_target_pairs={{0,4},{4,0},{8,12},{12,8},{1,5},{5,1},{9,13},{13,9},{2,6},{6,2},{1... | collective-permute-start | bytes 98312 | tf_op jit(solution)/shard_map/ppermute | solution.py:788
  32.9 3.4 %collective-permute-start.11 = (bf16[128,128]{1,0:T(8,128)(2,1)S(1)}, bf16[128,128]{1,0:T(8,128)(2,1)S(1)}, u32[]{:S(2)}, u32[]{:S(2)}) collective-permute-start(bf16[128,128]{1,0:T(8,128)(2,1)S(1)} %get-tuple-element.42), channel_id=1, source_target_pairs={{4,8},{8,4},{12,0},{0,12},{5,9},{9,5},{13,1},{1,13},{6,10},{10,6},... | collective-permute-start | bytes 98312 | tf_op jit(solution)/shard_map/ppermute | solution.py:789

commit v11 on v9

--- a/solution.py
+++ b/solution.py
@@ -81,12 +81,26 @@
     return 1.0 / grow, jnp.log(grow), sinh
 
 
+def edge_factors(lam, alpha, base, total, rows):
+    lam2 = lam * lam
+    powers = [
+        jnp.exp(-2.0 * base * alpha) * lam2,
+        jnp.exp(-2.0 * (total - rows - base) * alpha) * lam2,
+    ]
+    lows, highs = [], []
+    for _ in range(rows):
+        lows.append(1.0 - powers[0])
+        highs.insert(0, 1.0 - powers[1])
+        powers = [power * lam2 for power in powers]
+    return lows, highs
+
+
 def start_kernel(
     groups_x, paired, x_hbm, wet_hbm, flux_hbm, diff_hbm, table_hbm, *refs
 ):
-    outs = 7 if paired else 8
-    s_hbm, coarse_hbm, y_hbm, *message_hbm = refs[:outs]
-    s_ref, coarse_ref, y_ref, *message_ref = refs[outs : 2 * outs]
+    outs = 6 if paired else 7
+    coarse_hbm, y_hbm, *message_hbm = refs[:outs]
+    coarse_ref, y_ref, *message_ref = refs[outs : 2 * outs]
     e1_ref, e3_ref, e2_ref, e4_ref = message_ref[:4]
     if not paired:
         pq_ref = message_ref[4]
@@ -103,24 +117,18 @@
     x_copies = [
         pltpu.make_async_copy(x_hbm.at[0, r], x_ref.at[r], x_sem.at[r]) for r in range(rows)
     ]
-    surface_copies = [
-        pltpu.make_async_copy(s_ref, s_hbm, out_sem.at[0]),
-        pltpu.make_async_copy(coarse_ref, coarse_hbm, out_sem.at[1]),
-    ]
+    surface_copy = pltpu.make_async_copy(coarse_ref, coarse_hbm, out_sem.at[0])
     y_copies = [
-        pltpu.make_async_copy(y_ref.at[r], y_hbm.at[r], out_sem.at[2 + r]) for r in range(rows)
+        pltpu.make_async_copy(y_ref.at[r], y_hbm.at[r], out_sem.at[1 + r]) for r in range(rows)
     ]
     message_copies = [
-        pltpu.make_async_copy(ref, hbm, out_sem.at[2 + rows + k])
+        pltpu.make_async_copy(ref, hbm, out_sem.at[1 + rows + k])
         for k, (ref, hbm) in enumerate(zip(message_ref, message_hbm))
     ]
 
     def send_surface():
-        surface = to_tiles(row_ref[...])
-        s_ref[...] = surface
-        coarse_ref[...] = surface.astype(bf16)
-        for copy in surface_copies:
-            copy.start()
+        coarse_ref[...] = to_tiles(row_ref[...]).astype(bf16)
+        surface_copy.start()
 
     @pl.when(is_atmos)
     def _():
@@ -154,21 +162,14 @@
         base = (row_group * rows).astype(f32)
         for group, n, parts in wave_parts(columns):
             lam, alpha, _ = decay_terms(diff, half_rates(group, n, LANES, columns))
-            lam2 = lam * lam
-            low = jnp.exp(-2.0 * base * alpha)
-            high = jnp.exp(-2.0 * (total - rows - base) * alpha)
+            lows, highs = edge_factors(lam, alpha, base, total, rows)
             for part in parts:
                 lanes = slice(part, part + LANES)
-                power = low
-                p = jnp.zeros((channels, LANES), f32)
-                for r in range(rows):
-                    power = power * lam2
-                    p = lam * p + (1.0 - power) * y_ref[r, :, lanes]
-                power = high
-                q = jnp.zeros((channels, LANES), f32)
-                for r in reversed(range(rows)):
-                    power = power * lam2
-                    q = lam * q + (1.0 - power) * y_ref[r, :, lanes]
+                p = lows[0] * y_ref[0, :, lanes]
+                q = highs[-1] * y_ref[rows - 1, :, lanes]
+                for r in range(1, rows):
+                    p = lam * p + lows[r] * y_ref[r, :, lanes]
+                    q = lam * q + highs[-1 - r] * y_ref[rows - 1 - r, :, lanes]
                 if paired:
                     for mask, out in ((1, e1_ref), (2, e2_ref), (3, e3_ref)):
                         upward = row_group < (row_group ^ mask)
@@ -178,7 +179,7 @@
                     pq_ref[1, :, lanes] = q.astype(bf16)
         for copy in message_copies:
             copy.start()
-        for copy in surface_copies + y_copies + message_copies:
+        for copy in [surface_copy] + y_copies + message_copies:
             copy.wait()
 
     @pl.when(jnp.logical_not(is_atmos))
@@ -233,7 +234,7 @@
 
         for copy in message_copies:
             copy.start()
-        for copy in surface_copies + message_copies:
+        for copy in [surface_copy] + message_copies:
             copy.wait()
 
 
@@ -392,22 +393,10 @@
         base = (row_group * rows).astype(f32)
         for group, n, parts in wave_parts(columns):
             lam, alpha, sinh = decay_terms(diff, half_rates(group, n, LANES, columns))
-            lam2 = lam * lam
-            low = jnp.exp(-2.0 * base * alpha)
-            high = jnp.exp(-2.0 * (total - rows - base) * alpha)
             scale = 1.0 / (
                 2.0 * diff * sinh * (1.0 - jnp.exp(-2.0 * (total + 1) * alpha))
             )
-            lows, highs = [], []
-            power = low
-            for r in range(rows):
-                power = power * lam2
-                lows.append(1.0 - power)
-            power = high
-            for r in range(rows):
-                power = power * lam2
-                highs.append(1.0 - power)
-            highs = highs[::-1]
+            lows, highs = edge_factors(lam, alpha, base, total, rows)
             for part in parts:
                 lanes = slice(part, part + LANES)
                 if paired:
@@ -549,26 +538,30 @@
 
 
 def last_kernel(
-    groups_x, groups_y, column_ref, base_ref, c_ref, sum_ref, near_ref, far_ref, out_ref, e_ref
+    groups_x, groups_y, column_ref, base_ref, c_ref, sum_ref, near_ref, far_ref, out_hbm,
+    out_ref, e_ref, heat_ref, sem,
 ):
-    _, rows, channels, columns = out_ref.shape
+    rows, channels, columns = out_ref.shape
     row_group = lax.axis_index("gx")
     col_group = lax.axis_index("gy")
     is_atmos = lax.axis_index("comp") == 0
+    copies = [
+        pltpu.make_async_copy(out_ref.at[r], out_hbm.at[0, r], sem.at[r]) for r in range(rows)
+    ]
 
     @pl.when(is_atmos)
     def _():
-        for k in range(columns // LANES):
-            lanes = slice(k * LANES, (k + 1) * LANES)
-            for r in range(rows):
+        for r in range(rows):
+            for k in range(columns // LANES):
+                lanes = slice(k * LANES, (k + 1) * LANES)
                 at = k * rows + r
-                out_ref[0, r, :, lanes] = (
+                out_ref[r, :, lanes] = (
                     base_ref[r, :, lanes] + column_ref[...] * sum_ref[at : at + 1, :]
                 )
+            copies[r].start()
 
     @pl.when(jnp.logical_not(is_atmos))
     def _():
-        out_ref[0] = base_ref[...]
         levels = channels // 2
         cells = sum_ref.shape[0]
         even = row_group % 2 == 0
@@ -583,16 +576,6 @@
         )
         has_before = jnp.where(col_group > 0, 1.0, 0.0)
         has_after = jnp.where(col_group < groups_y - 1, 1.0, 0.0)
-        for t in range(2):
-            for r, factor, lines in ((0, by_low, low), (rows - 1, by_high, high)):
-                c = t * levels
-                out_ref[0, r, c : c + 1, :] = out_ref[0, r, c : c + 1, :] + (
-                    has_before * factor * lines[t : t + 1]
-                )
-                c = c + levels - 1
-                out_ref[0, r, c : c + 1, :] = out_ref[0, r, c : c + 1, :] + (
-                    has_after * factor * lines[t + 2 : t + 3]
-                )
 
         @pl.when(col_group == 0)
         def _():
@@ -609,11 +592,36 @@
             first = first + c_ref[2, own, :] * e_ref[2 : rows + 2, :]
             first = first + c_ref[3, own, :] * pltpu.roll(heat, 1, 1)
             first = first + c_ref[4, own, :] * pltpu.roll(heat, columns - 1, 1)
-            for t, gain in enumerate((heat_gain, salt_gain)):
+            heat_ref[0] = first
+            heat_ref[1] = second
+
+        for r in [1, rows - 2] + list(range(2, rows - 2)) + [0, rows - 1]:
+            out_ref[r] = base_ref[r]
+            for t in range(2):
                 c = t * levels
-                for r in range(rows):
-                    lines = jnp.concatenate([first[r : r + 1], second[r : r + 1]], axis=0)
-                    out_ref[0, r, c : c + 2, :] = out_ref[0, r, c : c + 2, :] + gain * lines
+                for edge, factor, lines in ((0, by_low, low), (rows - 1, by_high, high)):
+                    if r == edge:
+                        out_ref[r, c : c + 1, :] = out_ref[r, c : c + 1, :] + (
+                            has_before * factor * lines[t : t + 1]
+                        )
+                        d = c + levels - 1
+                        out_ref[r, d : d + 1, :] = out_ref[r, d : d + 1, :] + (
+                            has_after * factor * lines[t + 2 : t + 3]
+                        )
+
+            @pl.when(col_group == 0)
+            def _():
+                for t, gain in enumerate((heat_gain, salt_gain)):
+                    c = t * levels
+                    for k in range(2):
+                        out_ref[r, c + k : c + k + 1, :] = (
+                            out_ref[r, c + k : c + k + 1, :] + gain * heat_ref[k, r : r + 1, :]
+                        )
+
+            copies[r].start()
+
+    for copy in copies:
+        copy.wait()
 
 
 def local(
@@ -652,7 +660,6 @@
 
     lines = 2 * channels + 16
     shapes = [
-        shape((cells, LANES), f32),
         shape((cells, LANES), bf16),
         shape((rows, channels, columns), f32),
         shape((lines, columns), bf16),
@@ -662,7 +669,7 @@
     ]
     if not paired:
         shapes.append(shape((2, channels, columns), bf16))
-    partial_surface, coarse, y, e1, e3, e2, e4, *sums = pl.pallas_call(
+    coarse, y, e1, e3, e2, e4, *sums = pl.pallas_call(
         functools.partial(start_kernel, groups_x, paired),
         out_shape=shapes,
         in_specs=[hbm] * 5,
@@ -693,12 +700,16 @@
     def partner_route(mask):
         return both_ways([(j, groups_y + (j ^ mask)) for j in range(groups_y)])
 
-    surface = partial_surface
-    for mask in masks[:-1]:
+    surface = sum(
+        lax.ppermute(coarse, ("comp", "gy"), partner_route(mask)).astype(f32)
+        for mask in masks[:1] + [0]
+    )
+    coarse = surface.astype(bf16)
+    for mask in masks[1:-1]:
         surface = surface + lax.ppermute(coarse, "gy", sum_route(mask)).astype(f32)
         coarse = surface.astype(bf16)
-    surfaces = [
-        lax.ppermute(coarse, ("comp", "gy"), partner_route(mask)) for mask in masks[-1:] + [0]
+    surfaces = [surface] + [
+        lax.ppermute(coarse, "gy", sum_route(mask)) for mask in masks[1:][-1:]
     ]
 
     def ring_pairs(count, odd):
@@ -824,8 +835,13 @@
         functools.partial(last_kernel, groups_x, groups_y),
         out_shape=shape(fields.shape, f32),
         in_specs=[vmem] * 6,
-        out_specs=vmem,
-        scratch_shapes=[pltpu.VMEM((16, columns), f32)],
+        out_specs=hbm,
+        scratch_shapes=[
+            pltpu.VMEM((rows, channels, columns), f32),
+            pltpu.VMEM((16, columns), f32),
+            pltpu.VMEM((2, rows, columns), f32),
+            pltpu.SemaphoreType.DMA((rows,)),
+        ],
         compiler_params=params(),
         name="add_surface_terms",
     )(column, base, coefs, surface_sum, near, far)

time: 31.2 us -> 30 us (0.962)
  other arithmetic: 0.77 us -> 0.02 us
  waiting for transfers between devices: 4.33 us -> 3.65 us
    ppermute x1, starting transfers between devices: 0.07 us -> 1.61 us  [local(): far = lax.ppermute(far, 'gx', both_ways(ring_pairs(groups_x, 1)))]
    ppermute x1, starting transfers between devices: 1.59 us -> 0.07 us  [local(): near = lax.ppermute(near, 'gx', both_ways(ring_pairs(groups_x, 0)))]
    convert_element_type x1, other arithmetic: 0.76 us -> 0.01 us  [local(): coarse = surface.astype(bf16)]
    ppermute x1, waiting for transfers between devices: 1.62 us -> 1.02 us  [local(): part = lax.ppermute(sent, 'gy', sum_route(masks[-1]))]
    ppermute x1, starting transfers between devices: 2.08 us -> 2.66 us  [local(): part = lax.ppermute(sent, 'gy', sum_route(masks[-1]))]
    ppermute x3, starting transfers between devices: 7.62 us -> 7.24 us  [the longest x2 4.58 us: local(): lax.ppermute(coarse, ('comp', 'gy'), partner_route(mask)).astype(f32)]
  transfers between devices with their start and end apart: 11 -> 11, of which waited for: 5 -> 5; matrix products, arithmetic and copies ran while one was open for 2% -> 0% of each run, Pallas kernels for 6% -> 7%
where the time goes in v11:
time: 30 us; the launch traced here: 29.8 us
  starting transfers between devices  16.3 us (54%)
  Pallas kernels  8.23 us (27%)
  waiting for transfers between devices  3.65 us (12%)
  between operations  1.53 us (5%)
    ppermute x2, starting transfers between devices, local(): lax.ppermute(coarse, ('comp', 'gy'), partner_route(mask)).astype(f32)  4.58 us
    pallas_call x1, Pallas kernels, local(): pl.pallas_call(functools.partial(start_kernel, groups_x, paired), out_sha...  3.77 us
    ppermute x1, starting transfers between devices, local(): part = lax.ppermute(sent, 'gy', sum_route(masks[-1]))  2.66 us
    ppermute x1, starting transfers between devices, local(): lax.ppermute(coarse, 'gy', sum_route(mask))  2.65 us
    ppermute x1, starting transfers between devices, local(): landing = landing + lax.ppermute(sent, 'gy', sum_route(mask)).astype(f32)  1.65 us
    ppermute x1, starting transfers between devices, local(): far = lax.ppermute(far, 'gx', both_ways(ring_pairs(groups_x, 1)))  1.61 us
    ppermute x1, starting transfers between devices, local(): e3 = lax.ppermute(e3, 'gx', both_ways(ring_pairs(groups_x, 1)))  1.6 us
    ppermute x1, starting transfers between devices, local(): e2 = lax.ppermute(e2, axes, level_route(0))  1.48 us
  transfers between devices with their start and end apart: 11, of which 5 were waited for; matrix products, arithmetic and copies ran while one was open for 0% of the time, Pallas kernels for 7%

profile of v11, /device:TPU:0, one launch (start us, length us, event | category | flops | bytes accessed | tf_op | source)
XLA Modules:
  0.0 29.8 jit_solution(112231730555629408)
XLA Ops:
  0.0 0.0 copy-start.6
  0.0 0.0 copy-start.7
  0.0 0.0 copy-start.8
  0.0 0.0 copy-start.9
  0.0 0.0 copy-start.1
  0.0 0.0 copy-start.2
  0.0 3.8 %surface_and_forward_or_halos.1 = (bf16[64,128]{1,0:T(8,128)(2,1)}, f32[8,32,1024]{2,1,0:T(8,128)}, bf16[80,1024]{1,0:T(8,128)(2,1)}, bf16[80,1024]{1,0:T(8,128)...) custom-call(f32[1,8,32,1024]{3,2,1,0:T(8,128)} %x_ref.1, s32[8,1024]{1,0:T(8,128)} %wet_ref.1, ...), custom_call_target="tpu_custom_call" | custom-call | tf_op jit(solution)/shard_map/surface_and_forward_or_halos/pallas_call | solution.py:672
  3.8 1.9 %collective-permute-start.5 = (bf16[64,128]{1,0:T(8,128)(2,1)}, bf16[64,128]{1,0:T(8,128)(2,1)S(1)}, u32[]{:S(2)}, u32[]{:S(2)}) collective-permute-start(bf16[64,128]{1,0:T(8,128)(2,1)} %get-tuple-element.35), channel_id=1, source_target_pairs={{0,16},{16,0},{1,17},{17,1},{2,18},{18,2},{3,19},{19,3},{4,20},{20... | collective-permute-start | bytes 49160 | tf_op jit(solution)/shard_map/ppermute | solution.py:704
  5.7 2.7 %collective-permute-start.4 = (bf16[64,128]{1,0:T(8,128)(2,1)}, bf16[64,128]{1,0:T(8,128)(2,1)S(1)}, u32[]{:S(2)}, u32[]{:S(2)}) collective-permute-start(bf16[64,128]{1,0:T(8,128)(2,1)} %get-tuple-element.35), channel_id=1, source_target_pairs={{0,17},{17,0},{1,16},{16,1},{2,19},{19,2},{3,18},{18,3},{4,21},{21... | collective-permute-start | bytes 49160 | tf_op jit(solution)/shard_map/ppermute | solution.py:704
  8.4 0.0 collective-permute-start
  8.4 1.6 %collective-permute-start.1 = (bf16[80,1024]{1,0:T(8,128)(2,1)}, bf16[80,1024]{1,0:T(8,128)(2,1)S(1)}, u32[]{:S(2)}, u32[]{:S(2)}) collective-permute-start(bf16[80,1024]{1,0:T(8,128)(2,1)} %get-tuple-element.27), channel_id=1, source_target_pairs={{4,8},{8,4},{12,0},{0,12},{5,9},{9,5},{13,1},{1,13},{6,10},{10,6},... | collective-permute-start | bytes 491528 | tf_op jit(solution)/shard_map/ppermute | solution.py:736
  10.0 0.0 collective-permute-done.5
  10.0 0.5 %collective-permute-done.4 = bf16[64,128]{1,0:T(8,128)(2,1)S(1)} collective-permute-done((bf16[64,128]{1,0:T(8,128)(2,1)}, bf16[64,128]{1,0:T(8,128)(2,1)S(1)}, u32[]{:S(2)}, u32[]{:S(2)}) %collective-permute-start.4) | collective-permute-done | bytes 16416 | tf_op jit(solution)/shard_map/ppermute | solution.py:704
  10.5 2.7 %collective-permute-start.6 = (bf16[64,128]{1,0:T(8,128)(2,1)S(1)}, bf16[64,128]{1,0:T(8,128)(2,1)S(1)}, u32[]{:S(2)}, u32[]{:S(2)}) collective-permute-start(bf16[64,128]{1,0:T(8,128)(2,1)S(1)} %get-tuple-element.47._), channel_id=1, source_target_pairs={{0,2},{1,3},{2,0},{3,1},{4,6},{5,7},{6,4},{7,5},{8,10},{9,11},{10,... | collective-permute-start | bytes 49160 | tf_op jit(solution)/shard_map/ppermute | solution.py:712
  14.5 0.0 copy-done.6
  14.5 0.0 copy-done.7
  14.5 0.0 copy-done.8
  14.5 0.0 copy-done.9
  14.5 0.6 %one_hots.1 = (bf16[128,4096]{1,0:T(8,128)(2,1)S(1)}, bf16[128,4096]{1,0:T(8,128)(2,1)S(1)}, s32[32,128]{1,0:T(8,128)S(1)}, s32[32,128]{1,0:T(8,128)S(1)}) custom-call(s32[1,1,32,128]{3,2,1,0:T(8,128)S(1)} %copy-done.6, s32[1,1,32,128]{3,2,1,0:T(8,128)S(1)} %copy-done.7, s32[1,1,32,128]{3,2,1,0:T(8,128)S(1)} %copy-done.8, s32[1,1,32,128]{3,2,1,0:T(8,128)S(1)} %copy-done.9, ...), custom_call_target="tpu_custom_call" | custom-call | tf_op jit(solution)/shard_map/one_hots/pallas_call | solution.py:741
  15.2 0.1 collective-permute-done.6.refs_1_
  15.2 0.0 collective-permute-done.e1_ref.refs_10_
  15.2 0.0 collective-permute-done.1.e3_ref.refs_11_
  15.3 0.0 copy-done.1
  15.3 0.0 copy-done.2
  15.3 0.0 copy-start.13
  15.3 0.0 copy-start.12
  15.3 0.0 copy-start
  15.3 0.0 copy-start.3
  15.3 0.0 copy-start.5
  15.3 0.0 copy-start.10
  15.3 1.4 %regrid_blocks.1 = (f32[64,128]{1,0:T(8,128)S(1)}, bf16[64,128]{1,0:T(8,128)(2,1)S(1)}) custom-call(f32[64,128]{1,0:T(8,128)S(1)} %get-tuple-element.48.refs_0_, bf16[64,128]{1,0:T(8,128)(2,1)S(1)} %collective-permute-done.6.refs_1_, bf16[128,4096]{1,0:T(8,128)(2,1)S(1)} %get-tuple-element.36.refs_2_, bf16[128,4096]{1,0:T(8,128)(2,1)S(1)} %get-tuple-element.37.refs_3_, ...), custom_call_target="tpu_custom_call" | custom-call | tf_op jit(solution)/shard_map/regrid_blocks/pallas_call | solution.py:754
  16.7 0.0 copy-start.4
  16.7 0.0 copy-start.11
  16.7 1.6 %collective-permute-start.7 = (bf16[64,128]{1,0:T(8,128)(2,1)S(1)}, bf16[64,128]{1,0:T(8,128)(2,1)S(1)}, u32[]{:S(2)}, u32[]{:S(2)}) collective-permute-start(bf16[64,128]{1,0:T(8,128)(2,1)S(1)} %get-tuple-element.41), channel_id=1, source_target_pairs={{0,1},{1,0},{2,3},{3,2},{4,5},{5,4},{6,7},{7,6},{8,9},{9,8},{10,11... | collective-permute-start | bytes 49160 | tf_op jit(solution)/shard_map/ppermute | solution.py:772
  18.4 0.0 copy-done.13
  18.4 1.5 %collective-permute-start.2 = (bf16[32,1024]{1,0:T(8,128)(2,1)S(1)}, bf16[32,1024]{1,0:T(8,128)(2,1)S(1)}, u32[]{:S(2)}, u32[]{:S(2)}) collective-permute-start(bf16[32,1024]{1,0:T(8,128)(2,1)S(1)} %copy-done.13), channel_id=1, source_target_pairs={{16,17},{17,16},{18,19},{19,18},{0,8},{8,0},{1,9},{9,1},{2,10},{10... | collective-permute-start | bytes 196616 | tf_op jit(solution)/shard_map/ppermute | solution.py:738
  19.9 0.0 copy-done.12
  19.9 0.0 collective-permute-start.3
  19.9 0.7 %collective-permute-done.7 = bf16[64,128]{1,0:T(8,128)(2,1)S(1)} collective-permute-done((bf16[64,128]{1,0:T(8,128)(2,1)S(1)}, bf16[64,128]{1,0:T(8,128)(2,1)S(1)}, u32[]{:S(2)}, u32[]{:S(2)}) %collective-permute-start.7) | collective-permute-done | bytes 16416 | tf_op jit(solution)/shard_map/ppermute | solution.py:772
  20.5 2.7 %collective-permute-start.8 = (bf16[64,128]{1,0:T(8,128)(2,1)S(1)}, bf16[64,128]{1,0:T(8,128)(2,1)S(1)}, u32[]{:S(2)}, u32[]{:S(2)}) collective-permute-start(bf16[64,128]{1,0:T(8,128)(2,1)S(1)} %get-tuple-element.45), channel_id=1, source_target_pairs={{0,2},{1,3},{2,0},{3,1},{4,6},{5,7},{6,4},{7,5},{8,10},{9,11},{10,... | collective-permute-start | bytes 49160 | tf_op jit(solution)/shard_map/ppermute | solution.py:774
  23.2 0.0 collective-permute-done.2.e2_ref
  23.2 0.0 collective-permute-done.3.e4_ref
  23.2 0.0 copy-done
  23.2 0.0 copy-done.3
  23.2 0.0 copy-done.5
  23.2 0.0 copy-done.10
  23.2 1.0 %damping_or_first_step.1 = (bf16[256,1024]{1,0:T(8,128)(2,1)S(1)}, f32[7,16,1024]{2,1,0:T(8,128)S(1)}, f32[10,2,24,1024]{3,2,1,0:T(8,128)S(1)}) custom-call(f32[1,8,32,1024]{3,2,1,0:T(8,128)S(1)} %copy-done, s32[8,1024]{1,0:T(8,128)S(1)} %copy-done.5, f32[1,128]{1,0:T(1,128)S(1)} %bitcast.4, f32[8,32,1024]{2,1,0:T(8,128)S(1)} %copy-done.3, ...), custom_call_target="tpu_custom_call" | custom-call | tf_op jit(solution)/shard_map/damping_or_first_step/pallas_call | solution.py:793
  24.2 1.0 %collective-permute-done.8.part_ref = bf16[64,128]{1,0:T(8,128)(2,1)S(1)} collective-permute-done((bf16[64,128]{1,0:T(8,128)(2,1)S(1)}, bf16[64,128]{1,0:T(8,128)(2,1)S(1)}, u32[]{:S(2)}, u32[]{:S(2)}) %collective-permute-start.8) | collective-permute-done | bytes 16416 | tf_op jit(solution)/shard_map/ppermute | solution.py:774
  25.3 0.1 collective-permute-start.9
  25.4 1.6 %collective-permute-start.10 = (bf16[128,128]{1,0:T(8,128)(2,1)S(1)}, bf16[128,128]{1,0:T(8,128)(2,1)S(1)}, u32[]{:S(2)}, u32[]{:S(2)}) collective-permute-start(bf16[128,128]{1,0:T(8,128)(2,1)S(1)} %get-tuple-element.44), channel_id=1, source_target_pairs={{4,8},{8,4},{12,0},{0,12},{5,9},{9,5},{13,1},{1,13},{6,10},{10,6},... | collective-permute-start | bytes 98312 | tf_op jit(solution)/shard_map/ppermute | solution.py:825
  27.0 0.0 copy-done.4
  27.0 0.0 copy-done.11
  27.0 0.4 %inverse_or_second_step.1 = (f32[8,32,1024]{2,1,0:T(8,128)S(1)}, f32[32,128]{1,0:T(8,128)S(1)}) custom-call(f32[1,128]{1,0:T(1,128)S(1)} %bitcast.5, bf16[1024,512]{1,0:T(8,128)(2,1)S(1)} %copy-done.4, bf16[256,1024]{1,0:T(8,128)(2,1)S(1)} %get-tuple-element.30.zb_ref, f32[7,16,1024]{2,1,0:T(8,128)S(1)} %get-tuple-element.31.c_ref._, ...), custom_call_target="tpu_custom_call" | custom-call | tf_op jit(solution)/shard_map/inverse_or_second_step/pallas_call | solution.py:826
  27.4 0.0 collective-permute-done.9.near_ref
  27.4 1.3 %collective-permute-done.10.far_ref = bf16[128,128]{1,0:T(8,128)(2,1)S(1)} collective-permute-done((bf16[128,128]{1,0:T(8,128)(2,1)S(1)}, bf16[128,128]{1,0:T(8,128)(2,1)S(1)}, u32[]{:S(2)}, u32[]{:S(2)}) %collective-permute-start.10) | collective-permute-done | bytes 32800 | tf_op jit(solution)/shard_map/ppermute | solution.py:825
  28.8 1.0 %add_surface_terms.1 = f32[1,8,32,1024]{3,2,1,0:T(8,128)} custom-call(f32[32,128]{1,0:T(8,128)S(1)} %get-tuple-element.33.column_ref, f32[8,32,1024]{2,1,0:T(8,128)S(1)} %get-tuple-element.34.base_ref, f32[7,16,1024]{2,1,0:T(8,128)S(1)} %get-tuple-element.31.c_ref._, f32[64,128]{1,0:T(8,128)S(1)} %get-tuple-element.42.sum_ref, ...), custom_call_target="tpu_custom_call" | custom-call | tf_op jit(solution)/shard_map/add_surface_terms/pallas_call | solution.py:834
  (3 shorter events, 0.1 us)
Async XLA Ops:
  0.0 14.5 %copy-start.6 = (s32[1,1,32,128]{3,2,1,0:T(8,128)S(1)}, s32[1,1,32,128]{3,2,1,0:T(8,128)}, u32[]{:S(2)}) copy-start(s32[1,1,32,128]{3,2,1,0:T(8,128)} %a_src.1) | copy-start | bytes 49156
  0.0 14.5 %copy-start.7 = (s32[1,1,32,128]{3,2,1,0:T(8,128)S(1)}, s32[1,1,32,128]{3,2,1,0:T(8,128)}, u32[]{:S(2)}) copy-start(s32[1,1,32,128]{3,2,1,0:T(8,128)} %a_dst.1) | copy-start | bytes 49156
  0.0 14.5 %copy-start.8 = (s32[1,1,32,128]{3,2,1,0:T(8,128)S(1)}, s32[1,1,32,128]{3,2,1,0:T(8,128)}, u32[]{:S(2)}) copy-start(s32[1,1,32,128]{3,2,1,0:T(8,128)} %m_src.1) | copy-start | bytes 49156
  0.0 14.5 %copy-start.9 = (s32[1,1,32,128]{3,2,1,0:T(8,128)S(1)}, s32[1,1,32,128]{3,2,1,0:T(8,128)}, u32[]{:S(2)}) copy-start(s32[1,1,32,128]{3,2,1,0:T(8,128)} %m_dst.1) | copy-start | bytes 49156
  0.0 15.2 %copy-start.1 = (bf16[1,1,32,128,128]{4,3,2,1,0:T(8,128)(2,1)S(1)}, bf16[1,1,32,128,128]{4,3,2,1,0:T(8,128)(2,1)}, u32[]{:S(2)}) copy-start(bf16[1,1,32,128,128]{4,3,2,1,0:T(8,128)(2,1)} %refs_8_.1) | copy-start | bytes 3145732
  0.0 15.2 %copy-start.2 = (bf16[1,1,32,128,128]{4,3,2,1,0:T(8,128)(2,1)S(1)}, bf16[1,1,32,128,128]{4,3,2,1,0:T(8,128)(2,1)}, u32[]{:S(2)}) copy-start(bf16[1,1,32,128,128]{4,3,2,1,0:T(8,128)(2,1)} %refs_9_.1) | copy-start | bytes 3145732
  3.8 6.2 %collective-permute-start.5 = (bf16[64,128]{1,0:T(8,128)(2,1)}, bf16[64,128]{1,0:T(8,128)(2,1)S(1)}, u32[]{:S(2)}, u32[]{:S(2)}) collective-permute-start(bf16[64,128]{1,0:T(8,128)(2,1)} %get-tuple-element.35), channel_id=1, source_target_pairs={{0,16},{16,0},{1,17},{17,1},{2,18},{18,2},{3,19},{19,3},{4,20},{20... | collective-permute-start | bytes 49160 | tf_op jit(solution)/shard_map/ppermute | solution.py:704
  5.7 4.8 %collective-permute-start.4 = (bf16[64,128]{1,0:T(8,128)(2,1)}, bf16[64,128]{1,0:T(8,128)(2,1)S(1)}, u32[]{:S(2)}, u32[]{:S(2)}) collective-permute-start(bf16[64,128]{1,0:T(8,128)(2,1)} %get-tuple-element.35), channel_id=1, source_target_pairs={{0,17},{17,0},{1,16},{16,1},{2,19},{19,2},{3,18},{18,3},{4,21},{21... | collective-permute-start | bytes 49160 | tf_op jit(solution)/shard_map/ppermute | solution.py:704
  8.4 6.9 %collective-permute-start = (bf16[80,1024]{1,0:T(8,128)(2,1)}, bf16[80,1024]{1,0:T(8,128)(2,1)S(1)}, u32[]{:S(2)}, u32[]{:S(2)}) collective-permute-start(bf16[80,1024]{1,0:T(8,128)(2,1)} %get-tuple-element.26), channel_id=1, source_target_pairs={{0,4},{4,0},{8,12},{12,8},{1,5},{5,1},{9,13},{13,9},{2,6},{6,2},{1... | collective-permute-start | bytes 491528 | tf_op jit(solution)/shard_map/ppermute | solution.py:735
  8.4 6.9 %collective-permute-start.1 = (bf16[80,1024]{1,0:T(8,128)(2,1)}, bf16[80,1024]{1,0:T(8,128)(2,1)S(1)}, u32[]{:S(2)}, u32[]{:S(2)}) collective-permute-start(bf16[80,1024]{1,0:T(8,128)(2,1)} %get-tuple-element.27), channel_id=1, source_target_pairs={{4,8},{8,4},{12,0},{0,12},{5,9},{9,5},{13,1},{1,13},{6,10},{10,6},... | collective-permute-start | bytes 491528 | tf_op jit(solution)/shard_map/ppermute | solution.py:736
  10.5 4.7 %collective-permute-start.6 = (bf16[64,128]{1,0:T(8,128)(2,1)S(1)}, bf16[64,128]{1,0:T(8,128)(2,1)S(1)}, u32[]{:S(2)}, u32[]{:S(2)}) collective-permute-start(bf16[64,128]{1,0:T(8,128)(2,1)S(1)} %get-tuple-element.47._), channel_id=1, source_target_pairs={{0,2},{1,3},{2,0},{3,1},{4,6},{5,7},{6,4},{7,5},{8,10},{9,11},{10,... | collective-permute-start | bytes 49160 | tf_op jit(solution)/shard_map/ppermute | solution.py:712
  15.3 3.1 %copy-start.13 = (bf16[32,1024]{1,0:T(8,128)(2,1)S(1)}, bf16[32,1024]{1,0:T(8,128)(2,1)}, u32[]{:S(2)}) copy-start(bf16[32,1024]{1,0:T(8,128)(2,1)} %get-tuple-element.28) | copy-start | bytes 196612
  15.3 4.6 %copy-start.12 = (bf16[32,1024]{1,0:T(8,128)(2,1)S(1)}, bf16[32,1024]{1,0:T(8,128)(2,1)}, u32[]{:S(2)}) copy-start(bf16[32,1024]{1,0:T(8,128)(2,1)} %get-tuple-element.29) | copy-start | bytes 196612
  15.3 7.9 %copy-start = (f32[1,8,32,1024]{3,2,1,0:T(8,128)S(1)}, f32[1,8,32,1024]{3,2,1,0:T(8,128)}, u32[]{:S(2)}) copy-start(f32[1,8,32,1024]{3,2,1,0:T(8,128)} %x_ref.1) | copy-start | bytes 3145732
  15.3 7.9 %copy-start.3 = (f32[8,32,1024]{2,1,0:T(8,128)S(1)}, f32[8,32,1024]{2,1,0:T(8,128)}, u32[]{:S(2)}) copy-start(f32[8,32,1024]{2,1,0:T(8,128)} %get-tuple-element.25.y_ref) | copy-start | bytes 3145732
  15.3 7.9 %copy-start.5 = (s32[8,1024]{1,0:T(8,128)S(1)}, s32[8,1024]{1,0:T(8,128)}, u32[]{:S(2)}) copy-start(s32[8,1024]{1,0:T(8,128)} %wet_ref.1) | copy-start | bytes 98308
  15.3 7.9 %copy-start.10 = (f32[128]{0:T(128)S(1)}, f32[128]{0:T(128)}, u32[]{:S(2)}) copy-start(f32[128]{0:T(128)} %param.19) | copy-start | bytes 1540
  16.7 10.3 %copy-start.4 = (bf16[1024,512]{1,0:T(8,128)(2,1)S(1)}, bf16[1024,512]{1,0:T(8,128)(2,1)}, u32[]{:S(2)}) copy-start(bf16[1024,512]{1,0:T(8,128)(2,1)} %constant.5.clone.table_ref) | copy-start | bytes 3145732
  16.7 10.3 %copy-start.11 = (f32[128]{0:T(128)S(1)}, f32[128]{0:T(128)}, u32[]{:S(2)}) copy-start(f32[128]{0:T(128)} %param.18) | copy-start | bytes 1540
  16.7 3.8 %collective-permute-start.7 = (bf16[64,128]{1,0:T(8,128)(2,1)S(1)}, bf16[64,128]{1,0:T(8,128)(2,1)S(1)}, u32[]{:S(2)}, u32[]{:S(2)}) collective-permute-start(bf16[64,128]{1,0:T(8,128)(2,1)S(1)} %get-tuple-element.41), channel_id=1, source_target_pairs={{0,1},{1,0},{2,3},{3,2},{4,5},{5,4},{6,7},{7,6},{8,9},{9,8},{10,11... | collective-permute-start | bytes 49160 | tf_op jit(solution)/shard_map/ppermute | solution.py:772
  18.4 4.8 %collective-permute-start.2 = (bf16[32,1024]{1,0:T(8,128)(2,1)S(1)}, bf16[32,1024]{1,0:T(8,128)(2,1)S(1)}, u32[]{:S(2)}, u32[]{:S(2)}) collective-permute-start(bf16[32,1024]{1,0:T(8,128)(2,1)S(1)} %copy-done.13), channel_id=1, source_target_pairs={{16,17},{17,16},{18,19},{19,18},{0,8},{8,0},{1,9},{9,1},{2,10},{10... | collective-permute-start | bytes 196616 | tf_op jit(solution)/shard_map/ppermute | solution.py:738
  19.9 3.3 %collective-permute-start.3 = (bf16[32,1024]{1,0:T(8,128)(2,1)S(1)}, bf16[32,1024]{1,0:T(8,128)(2,1)S(1)}, u32[]{:S(2)}, u32[]{:S(2)}) collective-permute-start(bf16[32,1024]{1,0:T(8,128)(2,1)S(1)} %copy-done.12), channel_id=1, source_target_pairs={{17,18},{18,17},{16,20},{20,16},{19,23},{23,19},{0,4},{4,0},{1,5},... | collective-permute-start | bytes 196616 | tf_op jit(solution)/shard_map/ppermute | solution.py:739
  20.5 4.7 %collective-permute-start.8 = (bf16[64,128]{1,0:T(8,128)(2,1)S(1)}, bf16[64,128]{1,0:T(8,128)(2,1)S(1)}, u32[]{:S(2)}, u32[]{:S(2)}) collective-permute-start(bf16[64,128]{1,0:T(8,128)(2,1)S(1)} %get-tuple-element.45), channel_id=1, source_target_pairs={{0,2},{1,3},{2,0},{3,1},{4,6},{5,7},{6,4},{7,5},{8,10},{9,11},{10,... | collective-permute-start | bytes 49160 | tf_op jit(solution)/shard_map/ppermute | solution.py:774
  25.3 2.1 %collective-permute-start.9 = (bf16[128,128]{1,0:T(8,128)(2,1)S(1)}, bf16[128,128]{1,0:T(8,128)(2,1)S(1)}, u32[]{:S(2)}, u32[]{:S(2)}) collective-permute-start(bf16[128,128]{1,0:T(8,128)(2,1)S(1)} %get-tuple-element.43), channel_id=1, source_target_pairs={{0,4},{4,0},{8,12},{12,8},{1,5},{5,1},{9,13},{13,9},{2,6},{6,2},{1... | collective-permute-start | bytes 98312 | tf_op jit(solution)/shard_map/ppermute | solution.py:824
  25.4 3.4 %collective-permute-start.10 = (bf16[128,128]{1,0:T(8,128)(2,1)S(1)}, bf16[128,128]{1,0:T(8,128)(2,1)S(1)}, u32[]{:S(2)}, u32[]{:S(2)}) collective-permute-start(bf16[128,128]{1,0:T(8,128)(2,1)S(1)} %get-tuple-element.44), channel_id=1, source_target_pairs={{4,8},{8,4},{12,0},{0,12},{5,9},{9,5},{13,1},{1,13},{6,10},{10,6},... | collective-permute-start | bytes 98312 | tf_op jit(solution)/shard_map/ppermute | solution.py:825

commit v12 on v11

--- a/solution.py
+++ b/solution.py
@@ -74,6 +74,13 @@
     )
 
 
+def lengthen(ref, block):
+    rows = block.shape[0]
+    ref[0:rows, :] = block
+    if ref.shape[0] > rows:
+        ref[rows:, :] = block[: ref.shape[0] - rows]
+
+
 def decay_terms(diff_column, rates):
     half = 0.5 / diff_column + rates
     sinh = jnp.sqrt(half * (half + 2.0))
@@ -98,9 +105,9 @@
 def start_kernel(
     groups_x, paired, x_hbm, wet_hbm, flux_hbm, diff_hbm, table_hbm, *refs
 ):
-    outs = 6 if paired else 7
-    coarse_hbm, y_hbm, *message_hbm = refs[:outs]
-    coarse_ref, y_ref, *message_ref = refs[outs : 2 * outs]
+    outs = 7 if paired else 8
+    coarse_hbm, wide_hbm, y_hbm, *message_hbm = refs[:outs]
+    coarse_ref, wide_ref, y_ref, *message_ref = refs[outs : 2 * outs]
     e1_ref, e3_ref, e2_ref, e4_ref = message_ref[:4]
     if not paired:
         pq_ref = message_ref[4]
@@ -117,18 +124,24 @@
     x_copies = [
         pltpu.make_async_copy(x_hbm.at[0, r], x_ref.at[r], x_sem.at[r]) for r in range(rows)
     ]
-    surface_copy = pltpu.make_async_copy(coarse_ref, coarse_hbm, out_sem.at[0])
+    surface_copies = [
+        pltpu.make_async_copy(coarse_ref, coarse_hbm, out_sem.at[0]),
+        pltpu.make_async_copy(wide_ref, wide_hbm, out_sem.at[1]),
+    ]
     y_copies = [
-        pltpu.make_async_copy(y_ref.at[r], y_hbm.at[r], out_sem.at[1 + r]) for r in range(rows)
+        pltpu.make_async_copy(y_ref.at[r], y_hbm.at[r], out_sem.at[2 + r]) for r in range(rows)
     ]
     message_copies = [
-        pltpu.make_async_copy(ref, hbm, out_sem.at[1 + rows + k])
+        pltpu.make_async_copy(ref, hbm, out_sem.at[2 + rows + k])
         for k, (ref, hbm) in enumerate(zip(message_ref, message_hbm))
     ]
 
     def send_surface():
-        coarse_ref[...] = to_tiles(row_ref[...]).astype(bf16)
-        surface_copy.start()
+        coarse = to_tiles(row_ref[...]).astype(bf16)
+        coarse_ref[...] = coarse
+        lengthen(wide_ref, coarse)
+        for copy in surface_copies:
+            copy.start()
 
     @pl.when(is_atmos)
     def _():
@@ -179,7 +192,7 @@
                     pq_ref[1, :, lanes] = q.astype(bf16)
         for copy in message_copies:
             copy.start()
-        for copy in [surface_copy] + y_copies + message_copies:
+        for copy in surface_copies + y_copies + message_copies:
             copy.wait()
 
     @pl.when(jnp.logical_not(is_atmos))
@@ -234,7 +247,7 @@
 
         for copy in message_copies:
             copy.start()
-        for copy in [surface_copy] + message_copies:
+        for copy in surface_copies + message_copies:
             copy.wait()
 
 
@@ -263,9 +276,11 @@
     surfaces = refs[:n_surfaces]
     (
         src_hot_ref, dst_hot_ref, src_row_ref, dst_row_ref, a_count, m_count, a_weight, m_weight,
-        _, _,
-        land_ref, sent_ref, weight_ref, gath_ref, val_ref, sem,
+        _, _, _, _,
+        *refs,
     ) = refs[n_surfaces:]
+    land_ref, *sent_refs = refs[:-4]
+    weight_ref, gath_ref, val_ref, sem = refs[-4:]
     is_atmos = lax.axis_index("comp") == 0
     blocks, points = val_ref.shape
     cells = surfaces[0].shape[0]
@@ -333,15 +348,20 @@
         )
     land = land[:cells] + land[cells:]
     land_ref[...] = land
-    sent_ref[...] = land.astype(bf16)
-
-
-def heat_kernel(rows, e2_ref, e4_ref, land_ref, part_ref, _, sum_ref, near_ref, far_ref):
+    for sent_ref in sent_refs:
+        lengthen(sent_ref, land.astype(bf16))
+
+
+def heat_kernel(rows, e2_ref, e4_ref, land_ref, _, *refs):
+    parts = refs[:-3]
+    sum_ref, near_ref, far_ref = refs[-3:]
     cells = land_ref.shape[0]
     columns = cells // rows * LANES
     even_x = lax.axis_index("gx") % 2 == 0
     even_y = lax.axis_index("gy") % 2 == 0
-    total = land_ref[...] + part_ref[...].astype(f32)
+    total = land_ref[...]
+    for part in parts:
+        total = total + part[0:cells, :].astype(f32)
     sum_ref[...] = total
 
     def corners(row):
@@ -661,6 +681,7 @@
     lines = 2 * channels + 16
     shapes = [
         shape((cells, LANES), bf16),
+        shape((cells + 16, LANES), bf16),
         shape((rows, channels, columns), f32),
         shape((lines, columns), bf16),
         shape((lines, columns), bf16),
@@ -669,7 +690,7 @@
     ]
     if not paired:
         shapes.append(shape((2, channels, columns), bf16))
-    coarse, y, e1, e3, e2, e4, *sums = pl.pallas_call(
+    coarse, wide, y, e1, e3, e2, e4, *sums = pl.pallas_call(
         functools.partial(start_kernel, groups_x, paired),
         out_shape=shapes,
         in_specs=[hbm] * 5,
@@ -700,10 +721,10 @@
     def partner_route(mask):
         return both_ways([(j, groups_y + (j ^ mask)) for j in range(groups_y)])
 
-    surface = sum(
-        lax.ppermute(coarse, ("comp", "gy"), partner_route(mask)).astype(f32)
-        for mask in masks[:1] + [0]
-    )
+    surface = lax.ppermute(coarse, ("comp", "gy"), partner_route(0)).astype(f32)
+    for mask in masks[:1]:
+        far = lax.ppermute(wide, ("comp", "gy"), partner_route(mask))
+        surface = surface + far[:cells].astype(f32)
     coarse = surface.astype(bf16)
     for mask in masks[1:-1]:
         surface = surface + lax.ppermute(coarse, "gy", sum_route(mask)).astype(f32)
@@ -751,11 +772,12 @@
         compiler_params=params(),
         name="one_hots",
     )(a2o_source, a2o_target, marine_air_input_index, marine_air_output_index, coarse)
-    landing, sent = pl.pallas_call(
+    landing, *sent = pl.pallas_call(
         functools.partial(regrid_kernel, len(surfaces)),
-        out_shape=[shape((cells, LANES), f32), shape((cells, LANES), bf16)],
-        in_specs=[vmem] * (len(surfaces) + 4) + [smem, smem, hbm, hbm, anywhere, anywhere],
-        out_specs=[vmem] * 2,
+        out_shape=[shape((cells, LANES), f32)]
+        + [shape((cells + 16 * (mask - 1), LANES), bf16) for mask in range(1, groups_y)],
+        in_specs=[vmem] * (len(surfaces) + 4) + [smem, smem, hbm, hbm] + [anywhere] * 4,
+        out_specs=[vmem] * groups_y,
         scratch_shapes=[
             pltpu.VMEM((blocks, points, points), bf16),
             pltpu.VMEM((blocks, points), f32),
@@ -766,12 +788,11 @@
         name="regrid_blocks",
     )(
         *surfaces, *one_hots, a2o_count, marine_air_piece_tally,
-        a2o_weight, marine_air_piece_factor, e1, e3,
+        a2o_weight, marine_air_piece_factor, e1, e3, e2, e4,
     )
-    for mask in masks[:-1]:
-        landing = landing + lax.ppermute(sent, "gy", sum_route(mask)).astype(f32)
-        sent = landing.astype(bf16)
-    part = lax.ppermute(sent, "gy", sum_route(masks[-1]))
+    parts = [
+        lax.ppermute(block, "gy", sum_route(mask)) for mask, block in enumerate(sent, 1)
+    ]
 
     extra = []
     if not paired:
@@ -815,11 +836,11 @@
             shape((cells + columns // 16, LANES), bf16),
             shape((cells + columns // 16, LANES), bf16),
         ],
-        in_specs=[vmem] * 4 + [anywhere],
+        in_specs=[vmem] * 3 + [anywhere] + [vmem] * len(parts),
         out_specs=[vmem] * 3,
         compiler_params=params(),
         name="surface_sum",
-    )(e2, e4, landing, part, coefs)
+    )(e2, e4, landing, coefs, *parts)
 
     near = lax.ppermute(near, "gx", both_ways(ring_pairs(groups_x, 0)))
     far = lax.ppermute(far, "gx", both_ways(ring_pairs(groups_x, 1)))

time: 30 us -> 30.2 us (level)
  waiting for transfers between devices: 3.65 us -> 4.67 us
  starting transfers between devices: 16.3 us -> 15.5 us
    ppermute x1, waiting for transfers between devices: 0.01 us -> 1.13 us  [local(): e2 = lax.ppermute(e2, axes, level_route(0))]
    ppermute x1, starting transfers between devices: 1.48 us -> 0.54 us  [local(): e2 = lax.ppermute(e2, axes, level_route(0))]
    ppermute x4 -> x5, starting transfers between devices: 8.89 us -> 9.04 us  [the longest x3 4.45 us: local(): lax.ppermute(block, 'gy', sum_route(mask))]
    ppermute x4 -> x5, waiting for transfers between devices: 2.23 us -> 2.12 us  [the longest x3 1.99 us: local(): lax.ppermute(block, 'gy', sum_route(mask))]
  transfers between devices with their start and end apart: 11 -> 12, of which waited for: 5 -> 6; matrix products, arithmetic and copies ran while one was open for 0% -> 0% of each run, Pallas kernels for 7% -> 7%
where the time goes in v12:
time: 30.2 us; the launch traced here: 30 us
  starting transfers between devices  15.5 us (51%)
  Pallas kernels  8.24 us (27%)
  waiting for transfers between devices  4.67 us (15%)
  between operations  1.5 us (5%)
    ppermute x3, starting transfers between devices, local(): lax.ppermute(block, 'gy', sum_route(mask))  4.45 us
    pallas_call x1, Pallas kernels, local(): pl.pallas_call(functools.partial(start_kernel, groups_x, paired), out_sha...  3.77 us
    ppermute x1, starting transfers between devices, local(): far = lax.ppermute(wide, ('comp', 'gy'), partner_route(mask))  2.9 us
    ppermute x1, starting transfers between devices, local(): lax.ppermute(coarse, 'gy', sum_route(mask))  2.65 us
    ppermute x3, waiting for transfers between devices, local(): lax.ppermute(block, 'gy', sum_route(mask))  1.99 us
    ppermute x1, starting transfers between devices, local(): surface = lax.ppermute(coarse, ('comp', 'gy'), partner_route(0)).astype(f32)  1.68 us
    ppermute x1, starting transfers between devices, local(): far = lax.ppermute(far, 'gx', both_ways(ring_pairs(groups_x, 1)))  1.61 us
    ppermute x1, starting transfers between devices, local(): e3 = lax.ppermute(e3, 'gx', both_ways(ring_pairs(groups_x, 1)))  1.6 us
  transfers between devices with their start and end apart: 12, of which 6 were waited for; matrix products, arithmetic and copies ran while one was open for 0% of the time, Pallas kernels for 7%

profile of v12, /device:TPU:0, one launch (start us, length us, event | category | flops | bytes accessed | tf_op | source)
XLA Modules:
  0.0 30.0 jit_solution(17308769375617768128)
XLA Ops:
  0.0 0.0 copy-start.6
  0.0 0.0 copy-start.7
  0.0 0.0 copy-start.8
  0.0 0.0 copy-start.9
  0.0 0.0 copy-start.2
  0.0 0.0 copy-start.3
  0.0 3.8 %surface_and_forward_or_halos.1 = (bf16[64,128]{1,0:T(8,128)(2,1)}, bf16[80,128]{1,0:T(8,128)(2,1)}, f32[8,32,1024]{2,1,0:T(8,128)}, bf16[80,1024]{1,0:T(8,128)(...) custom-call(f32[1,8,32,1024]{3,2,1,0:T(8,128)} %x_ref.1, s32[8,1024]{1,0:T(8,128)} %wet_ref.1, ...), custom_call_target="tpu_custom_call" | custom-call | tf_op jit(solution)/shard_map/surface_and_forward_or_halos/pallas_call | solution.py:693
  3.8 2.9 %collective-permute-start.5 = (bf16[80,128]{1,0:T(8,128)(2,1)}, bf16[80,128]{1,0:T(8,128)(2,1)S(1)}, u32[]{:S(2)}, u32[]{:S(2)}) collective-permute-start(bf16[80,128]{1,0:T(8,128)(2,1)} %get-tuple-element.39), channel_id=1, source_target_pairs={{0,17},{17,0},{1,16},{16,1},{2,19},{19,2},{3,18},{18,3},{4,21},{21... | collective-permute-start | bytes 61448 | tf_op jit(solution)/shard_map/ppermute | solution.py:726
  6.7 1.7 %collective-permute-start.4 = (bf16[64,128]{1,0:T(8,128)(2,1)}, bf16[64,128]{1,0:T(8,128)(2,1)S(1)}, u32[]{:S(2)}, u32[]{:S(2)}) collective-permute-start(bf16[64,128]{1,0:T(8,128)(2,1)} %get-tuple-element.38), channel_id=1, source_target_pairs={{0,16},{16,0},{1,17},{17,1},{2,18},{18,2},{3,19},{19,3},{4,20},{20... | collective-permute-start | bytes 49160 | tf_op jit(solution)/shard_map/ppermute | solution.py:724
  8.4 0.0 collective-permute-start
  8.4 1.6 %collective-permute-start.1 = (bf16[80,1024]{1,0:T(8,128)(2,1)}, bf16[80,1024]{1,0:T(8,128)(2,1)S(1)}, u32[]{:S(2)}, u32[]{:S(2)}) collective-permute-start(bf16[80,1024]{1,0:T(8,128)(2,1)} %get-tuple-element.30), channel_id=1, source_target_pairs={{4,8},{8,4},{12,0},{0,12},{5,9},{9,5},{13,1},{1,13},{6,10},{10,6},... | collective-permute-start | bytes 491528 | tf_op jit(solution)/shard_map/ppermute | solution.py:757
  10.0 0.5 %collective-permute-start.2 = (bf16[32,1024]{1,0:T(8,128)(2,1)}, bf16[32,1024]{1,0:T(8,128)(2,1)S(1)}, u32[]{:S(2)}, u32[]{:S(2)}) collective-permute-start(bf16[32,1024]{1,0:T(8,128)(2,1)} %get-tuple-element.31), channel_id=1, source_target_pairs={{16,17},{17,16},{18,19},{19,18},{0,8},{8,0},{1,9},{9,1},{2,10},{10... | collective-permute-start | bytes 196616 | tf_op jit(solution)/shard_map/ppermute | solution.py:759
  10.5 0.1 collective-permute-done.4
  10.7 0.0 collective-permute-start.3
  10.7 0.0 collective-permute-done.5
  10.7 2.7 %collective-permute-start.6 = (bf16[64,128]{1,0:T(8,128)(2,1)S(1)}, bf16[64,128]{1,0:T(8,128)(2,1)S(1)}, u32[]{:S(2)}, u32[]{:S(2)}) collective-permute-start(bf16[64,128]{1,0:T(8,128)(2,1)S(1)} %get-tuple-element.51._), channel_id=1, source_target_pairs={{0,2},{1,3},{2,0},{3,1},{4,6},{5,7},{6,4},{7,5},{8,10},{9,11},{10,... | collective-permute-start | bytes 49160 | tf_op jit(solution)/shard_map/ppermute | solution.py:733
  14.6 0.0 copy-done.6
  14.6 0.0 copy-done.7
  14.6 0.0 copy-done.8
  14.7 0.0 copy-done.9
  14.7 0.6 %one_hots.1 = (bf16[128,4096]{1,0:T(8,128)(2,1)S(1)}, bf16[128,4096]{1,0:T(8,128)(2,1)S(1)}, s32[32,128]{1,0:T(8,128)S(1)}, s32[32,128]{1,0:T(8,128)S(1)}) custom-call(s32[1,1,32,128]{3,2,1,0:T(8,128)S(1)} %copy-done.6, s32[1,1,32,128]{3,2,1,0:T(8,128)S(1)} %copy-done.7, s32[1,1,32,128]{3,2,1,0:T(8,128)S(1)} %copy-done.8, s32[1,1,32,128]{3,2,1,0:T(8,128)S(1)} %copy-done.9, ...), custom_call_target="tpu_custom_call" | custom-call | tf_op jit(solution)/shard_map/one_hots/pallas_call | solution.py:762
  15.3 0.1 collective-permute-done.6.refs_1_
  15.4 1.1 %collective-permute-done.2.e2_ref.refs_12_ = bf16[32,1024]{1,0:T(8,128)(2,1)S(1)} collective-permute-done((bf16[32,1024]{1,0:T(8,128)(2,1)}, bf16[32,1024]{1,0:T(8,128)(2,1)S(1)}, u32[]{:S(2)}, u32[]{:S(2)}) %collective-permute-start.2) | collective-permute-done | bytes 65568 | tf_op jit(solution)/shard_map/ppermute | solution.py:759
  16.5 0.0 collective-permute-done.3.e4_ref.refs_13_
  16.5 0.0 collective-permute-done.e1_ref.refs_10_
  16.5 0.0 collective-permute-done.1.e3_ref.refs_11_
  16.5 0.0 copy-done.2
  16.5 0.0 copy-done.3
  16.5 0.0 copy-start
  16.5 0.0 copy-start.1
  16.6 0.0 copy-start.5
  16.6 0.0 copy-start.10
  16.6 1.4 %regrid_blocks.1 = (f32[64,128]{1,0:T(8,128)S(1)}, bf16[64,128]{1,0:T(8,128)(2,1)S(1)}, bf16[80,128]{1,0:T(8,128)(2,1)S(1)}, bf16[96,128]{1,0:T(8,128)(2,1)S(1)}) custom-call(f32[64,128]{1,0:T(8,128)S(1)} %get-tuple-element.52.refs_0_, bf16[64,128]{1,0:T(8,128)(2,1)S(1)} %collective-permute-done.6.refs_1_, bf16[128,4096]{1,0:T(8,128)(2,1)S(1)} %get-tuple-element.40.refs_2_, ...), custom_call_target="tpu_custom_call" | custom-call | tf_op jit(solution)/shard_map/regrid_blocks/pallas_call | solution.py:775
  17.9 0.0 copy-start.4
  18.0 0.0 copy-start.11
  18.0 2.5 %collective-permute-start.9 = (bf16[96,128]{1,0:T(8,128)(2,1)S(1)}, bf16[96,128]{1,0:T(8,128)(2,1)S(1)}, u32[]{:S(2)}, u32[]{:S(2)}) collective-permute-start(bf16[96,128]{1,0:T(8,128)(2,1)S(1)} %get-tuple-element.47), channel_id=1, source_target_pairs={{0,3},{1,2},{2,1},{3,0},{4,7},{5,6},{6,5},{7,4},{8,11},{9,10},{10,... | collective-permute-start | bytes 73736 | tf_op jit(solution)/shard_map/ppermute | solution.py:794
  20.5 0.2 collective-permute-start.8
  20.7 1.7 %collective-permute-start.7 = (bf16[64,128]{1,0:T(8,128)(2,1)S(1)}, bf16[64,128]{1,0:T(8,128)(2,1)S(1)}, u32[]{:S(2)}, u32[]{:S(2)}) collective-permute-start(bf16[64,128]{1,0:T(8,128)(2,1)S(1)} %get-tuple-element.45), channel_id=1, source_target_pairs={{0,1},{1,0},{2,3},{3,2},{4,5},{5,4},{6,7},{7,6},{8,9},{9,8},{10,11... | collective-permute-start | bytes 49160 | tf_op jit(solution)/shard_map/ppermute | solution.py:794
  22.4 0.0 copy-done
  22.4 0.0 copy-done.1
  22.4 0.0 copy-done.5
  22.4 0.0 copy-done.10
  22.4 1.0 %damping_or_first_step.1 = (bf16[256,1024]{1,0:T(8,128)(2,1)S(1)}, f32[7,16,1024]{2,1,0:T(8,128)S(1)}, f32[10,2,24,1024]{3,2,1,0:T(8,128)S(1)}) custom-call(f32[1,8,32,1024]{3,2,1,0:T(8,128)S(1)} %copy-done, s32[8,1024]{1,0:T(8,128)S(1)} %copy-done.5, f32[1,128]{1,0:T(1,128)S(1)} %bitcast.4, f32[8,32,1024]{2,1,0:T(8,128)S(1)} %copy-done.1, ...), custom_call_target="tpu_custom_call" | custom-call | tf_op jit(solution)/shard_map/damping_or_first_step/pallas_call | solution.py:814
  23.4 1.0 %collective-permute-done.7.refs_0_ = bf16[64,128]{1,0:T(8,128)(2,1)S(1)} collective-permute-done((bf16[64,128]{1,0:T(8,128)(2,1)S(1)}, bf16[64,128]{1,0:T(8,128)(2,1)S(1)}, u32[]{:S(2)}, u32[]{:S(2)}) %collective-permute-start.7) | collective-permute-done | bytes 16416 | tf_op jit(solution)/shard_map/ppermute | solution.py:794
  24.4 1.0 %collective-permute-done.8.refs_1_ = bf16[80,128]{1,0:T(8,128)(2,1)S(1)} collective-permute-done((bf16[80,128]{1,0:T(8,128)(2,1)S(1)}, bf16[80,128]{1,0:T(8,128)(2,1)S(1)}, u32[]{:S(2)}, u32[]{:S(2)}) %collective-permute-start.8) | collective-permute-done | bytes 20512 | tf_op jit(solution)/shard_map/ppermute | solution.py:794
  25.4 0.0 collective-permute-done.9.refs_2_
  25.5 0.1 collective-permute-start.10
  25.5 1.6 %collective-permute-start.11 = (bf16[128,128]{1,0:T(8,128)(2,1)S(1)}, bf16[128,128]{1,0:T(8,128)(2,1)S(1)}, u32[]{:S(2)}, u32[]{:S(2)}) collective-permute-start(bf16[128,128]{1,0:T(8,128)(2,1)S(1)} %get-tuple-element.50), channel_id=1, source_target_pairs={{4,8},{8,4},{12,0},{0,12},{5,9},{9,5},{13,1},{1,13},{6,10},{10,6},... | collective-permute-start | bytes 98312 | tf_op jit(solution)/shard_map/ppermute | solution.py:846
  27.2 0.0 copy-done.4
  27.2 0.0 copy-done.11
  27.2 0.4 %inverse_or_second_step.1 = (f32[8,32,1024]{2,1,0:T(8,128)S(1)}, f32[32,128]{1,0:T(8,128)S(1)}) custom-call(f32[1,128]{1,0:T(1,128)S(1)} %bitcast.5, bf16[1024,512]{1,0:T(8,128)(2,1)S(1)} %copy-done.4, bf16[256,1024]{1,0:T(8,128)(2,1)S(1)} %get-tuple-element.33.zb_ref, f32[7,16,1024]{2,1,0:T(8,128)S(1)} %get-tuple-element.34.c_ref._, ...), custom_call_target="tpu_custom_call" | custom-call | tf_op jit(solution)/shard_map/inverse_or_second_step/pallas_call | solution.py:847
  27.6 0.0 collective-permute-done.10.near_ref
  27.6 1.3 %collective-permute-done.11.far_ref = bf16[128,128]{1,0:T(8,128)(2,1)S(1)} collective-permute-done((bf16[128,128]{1,0:T(8,128)(2,1)S(1)}, bf16[128,128]{1,0:T(8,128)(2,1)S(1)}, u32[]{:S(2)}, u32[]{:S(2)}) %collective-permute-start.11) | collective-permute-done | bytes 32800 | tf_op jit(solution)/shard_map/ppermute | solution.py:846
  29.0 1.0 %add_surface_terms.1 = f32[1,8,32,1024]{3,2,1,0:T(8,128)} custom-call(f32[32,128]{1,0:T(8,128)S(1)} %get-tuple-element.36.column_ref, f32[8,32,1024]{2,1,0:T(8,128)S(1)} %get-tuple-element.37.base_ref, f32[7,16,1024]{2,1,0:T(8,128)S(1)} %get-tuple-element.34.c_ref._, f32[64,128]{1,0:T(8,128)S(1)} %get-tuple-element.48.sum_ref, ...), custom_call_target="tpu_custom_call" | custom-call | tf_op jit(solution)/shard_map/add_surface_terms/pallas_call | solution.py:855
  (2 shorter events, 0.1 us)
Async XLA Ops:
  0.0 14.6 %copy-start.6 = (s32[1,1,32,128]{3,2,1,0:T(8,128)S(1)}, s32[1,1,32,128]{3,2,1,0:T(8,128)}, u32[]{:S(2)}) copy-start(s32[1,1,32,128]{3,2,1,0:T(8,128)} %a_src.1) | copy-start | bytes 49156
  0.0 14.6 %copy-start.7 = (s32[1,1,32,128]{3,2,1,0:T(8,128)S(1)}, s32[1,1,32,128]{3,2,1,0:T(8,128)}, u32[]{:S(2)}) copy-start(s32[1,1,32,128]{3,2,1,0:T(8,128)} %a_dst.1) | copy-start | bytes 49156
  0.0 14.6 %copy-start.8 = (s32[1,1,32,128]{3,2,1,0:T(8,128)S(1)}, s32[1,1,32,128]{3,2,1,0:T(8,128)}, u32[]{:S(2)}) copy-start(s32[1,1,32,128]{3,2,1,0:T(8,128)} %m_src.1) | copy-start | bytes 49156
  0.0 14.7 %copy-start.9 = (s32[1,1,32,128]{3,2,1,0:T(8,128)S(1)}, s32[1,1,32,128]{3,2,1,0:T(8,128)}, u32[]{:S(2)}) copy-start(s32[1,1,32,128]{3,2,1,0:T(8,128)} %m_dst.1) | copy-start | bytes 49156
  0.0 16.5 %copy-start.2 = (bf16[1,1,32,128,128]{4,3,2,1,0:T(8,128)(2,1)S(1)}, bf16[1,1,32,128,128]{4,3,2,1,0:T(8,128)(2,1)}, u32[]{:S(2)}) copy-start(bf16[1,1,32,128,128]{4,3,2,1,0:T(8,128)(2,1)} %refs_8_.1) | copy-start | bytes 3145732
  0.0 16.5 %copy-start.3 = (bf16[1,1,32,128,128]{4,3,2,1,0:T(8,128)(2,1)S(1)}, bf16[1,1,32,128,128]{4,3,2,1,0:T(8,128)(2,1)}, u32[]{:S(2)}) copy-start(bf16[1,1,32,128,128]{4,3,2,1,0:T(8,128)(2,1)} %refs_9_.1) | copy-start | bytes 3145732
  3.8 6.9 %collective-permute-start.5 = (bf16[80,128]{1,0:T(8,128)(2,1)}, bf16[80,128]{1,0:T(8,128)(2,1)S(1)}, u32[]{:S(2)}, u32[]{:S(2)}) collective-permute-start(bf16[80,128]{1,0:T(8,128)(2,1)} %get-tuple-element.39), channel_id=1, source_target_pairs={{0,17},{17,0},{1,16},{16,1},{2,19},{19,2},{3,18},{18,3},{4,21},{21... | collective-permute-start | bytes 61448 | tf_op jit(solution)/shard_map/ppermute | solution.py:726
  6.7 3.9 %collective-permute-start.4 = (bf16[64,128]{1,0:T(8,128)(2,1)}, bf16[64,128]{1,0:T(8,128)(2,1)S(1)}, u32[]{:S(2)}, u32[]{:S(2)}) collective-permute-start(bf16[64,128]{1,0:T(8,128)(2,1)} %get-tuple-element.38), channel_id=1, source_target_pairs={{0,16},{16,0},{1,17},{17,1},{2,18},{18,2},{3,19},{19,3},{4,20},{20... | collective-permute-start | bytes 49160 | tf_op jit(solution)/shard_map/ppermute | solution.py:724
  8.4 8.1 %collective-permute-start = (bf16[80,1024]{1,0:T(8,128)(2,1)}, bf16[80,1024]{1,0:T(8,128)(2,1)S(1)}, u32[]{:S(2)}, u32[]{:S(2)}) collective-permute-start(bf16[80,1024]{1,0:T(8,128)(2,1)} %get-tuple-element.29), channel_id=1, source_target_pairs={{0,4},{4,0},{8,12},{12,8},{1,5},{5,1},{9,13},{13,9},{2,6},{6,2},{1... | collective-permute-start | bytes 491528 | tf_op jit(solution)/shard_map/ppermute | solution.py:756
  8.4 8.1 %collective-permute-start.1 = (bf16[80,1024]{1,0:T(8,128)(2,1)}, bf16[80,1024]{1,0:T(8,128)(2,1)S(1)}, u32[]{:S(2)}, u32[]{:S(2)}) collective-permute-start(bf16[80,1024]{1,0:T(8,128)(2,1)} %get-tuple-element.30), channel_id=1, source_target_pairs={{4,8},{8,4},{12,0},{0,12},{5,9},{9,5},{13,1},{1,13},{6,10},{10,6},... | collective-permute-start | bytes 491528 | tf_op jit(solution)/shard_map/ppermute | solution.py:757
  10.0 6.5 %collective-permute-start.2 = (bf16[32,1024]{1,0:T(8,128)(2,1)}, bf16[32,1024]{1,0:T(8,128)(2,1)S(1)}, u32[]{:S(2)}, u32[]{:S(2)}) collective-permute-start(bf16[32,1024]{1,0:T(8,128)(2,1)} %get-tuple-element.31), channel_id=1, source_target_pairs={{16,17},{17,16},{18,19},{19,18},{0,8},{8,0},{1,9},{9,1},{2,10},{10... | collective-permute-start | bytes 196616 | tf_op jit(solution)/shard_map/ppermute | solution.py:759
  10.7 5.9 %collective-permute-start.3 = (bf16[32,1024]{1,0:T(8,128)(2,1)}, bf16[32,1024]{1,0:T(8,128)(2,1)S(1)}, u32[]{:S(2)}, u32[]{:S(2)}) collective-permute-start(bf16[32,1024]{1,0:T(8,128)(2,1)} %get-tuple-element.32), channel_id=1, source_target_pairs={{17,18},{18,17},{16,20},{20,16},{19,23},{23,19},{0,4},{4,0},{1,5},... | collective-permute-start | bytes 196616 | tf_op jit(solution)/shard_map/ppermute | solution.py:760
  10.7 4.7 %collective-permute-start.6 = (bf16[64,128]{1,0:T(8,128)(2,1)S(1)}, bf16[64,128]{1,0:T(8,128)(2,1)S(1)}, u32[]{:S(2)}, u32[]{:S(2)}) collective-permute-start(bf16[64,128]{1,0:T(8,128)(2,1)S(1)} %get-tuple-element.51._), channel_id=1, source_target_pairs={{0,2},{1,3},{2,0},{3,1},{4,6},{5,7},{6,4},{7,5},{8,10},{9,11},{10,... | collective-permute-start | bytes 49160 | tf_op jit(solution)/shard_map/ppermute | solution.py:733
  16.5 5.9 %copy-start = (f32[1,8,32,1024]{3,2,1,0:T(8,128)S(1)}, f32[1,8,32,1024]{3,2,1,0:T(8,128)}, u32[]{:S(2)}) copy-start(f32[1,8,32,1024]{3,2,1,0:T(8,128)} %x_ref.1) | copy-start | bytes 3145732
  16.5 5.9 %copy-start.1 = (f32[8,32,1024]{2,1,0:T(8,128)S(1)}, f32[8,32,1024]{2,1,0:T(8,128)}, u32[]{:S(2)}) copy-start(f32[8,32,1024]{2,1,0:T(8,128)} %get-tuple-element.28.y_ref) | copy-start | bytes 3145732
  16.6 5.9 %copy-start.5 = (s32[8,1024]{1,0:T(8,128)S(1)}, s32[8,1024]{1,0:T(8,128)}, u32[]{:S(2)}) copy-start(s32[8,1024]{1,0:T(8,128)} %wet_ref.1) | copy-start | bytes 98308
  16.6 5.9 %copy-start.10 = (f32[128]{0:T(128)S(1)}, f32[128]{0:T(128)}, u32[]{:S(2)}) copy-start(f32[128]{0:T(128)} %param.19) | copy-start | bytes 1540
  17.9 9.2 %copy-start.4 = (bf16[1024,512]{1,0:T(8,128)(2,1)S(1)}, bf16[1024,512]{1,0:T(8,128)(2,1)}, u32[]{:S(2)}) copy-start(bf16[1024,512]{1,0:T(8,128)(2,1)} %constant.5.clone.table_ref) | copy-start | bytes 3145732
  18.0 9.2 %copy-start.11 = (f32[128]{0:T(128)S(1)}, f32[128]{0:T(128)}, u32[]{:S(2)}) copy-start(f32[128]{0:T(128)} %param.18) | copy-start | bytes 1540
  18.0 7.4 %collective-permute-start.9 = (bf16[96,128]{1,0:T(8,128)(2,1)S(1)}, bf16[96,128]{1,0:T(8,128)(2,1)S(1)}, u32[]{:S(2)}, u32[]{:S(2)}) collective-permute-start(bf16[96,128]{1,0:T(8,128)(2,1)S(1)} %get-tuple-element.47), channel_id=1, source_target_pairs={{0,3},{1,2},{2,1},{3,0},{4,7},{5,6},{6,5},{7,4},{8,11},{9,10},{10,... | collective-permute-start | bytes 73736 | tf_op jit(solution)/shard_map/ppermute | solution.py:794
  20.5 4.9 %collective-permute-start.8 = (bf16[80,128]{1,0:T(8,128)(2,1)S(1)}, bf16[80,128]{1,0:T(8,128)(2,1)S(1)}, u32[]{:S(2)}, u32[]{:S(2)}) collective-permute-start(bf16[80,128]{1,0:T(8,128)(2,1)S(1)} %get-tuple-element.46), channel_id=1, source_target_pairs={{0,2},{1,3},{2,0},{3,1},{4,6},{5,7},{6,4},{7,5},{8,10},{9,11},{10,... | collective-permute-start | bytes 61448 | tf_op jit(solution)/shard_map/ppermute | solution.py:794
  20.7 3.7 %collective-permute-start.7 = (bf16[64,128]{1,0:T(8,128)(2,1)S(1)}, bf16[64,128]{1,0:T(8,128)(2,1)S(1)}, u32[]{:S(2)}, u32[]{:S(2)}) collective-permute-start(bf16[64,128]{1,0:T(8,128)(2,1)S(1)} %get-tuple-element.45), channel_id=1, source_target_pairs={{0,1},{1,0},{2,3},{3,2},{4,5},{5,4},{6,7},{7,6},{8,9},{9,8},{10,11... | collective-permute-start | bytes 49160 | tf_op jit(solution)/shard_map/ppermute | solution.py:794
  25.5 2.1 %collective-permute-start.10 = (bf16[128,128]{1,0:T(8,128)(2,1)S(1)}, bf16[128,128]{1,0:T(8,128)(2,1)S(1)}, u32[]{:S(2)}, u32[]{:S(2)}) collective-permute-start(bf16[128,128]{1,0:T(8,128)(2,1)S(1)} %get-tuple-element.49), channel_id=1, source_target_pairs={{0,4},{4,0},{8,12},{12,8},{1,5},{5,1},{9,13},{13,9},{2,6},{6,2},{1... | collective-permute-start | bytes 98312 | tf_op jit(solution)/shard_map/ppermute | solution.py:845
  25.5 3.4 %collective-permute-start.11 = (bf16[128,128]{1,0:T(8,128)(2,1)S(1)}, bf16[128,128]{1,0:T(8,128)(2,1)S(1)}, u32[]{:S(2)}, u32[]{:S(2)}) collective-permute-start(bf16[128,128]{1,0:T(8,128)(2,1)S(1)} %get-tuple-element.50), channel_id=1, source_target_pairs={{4,8},{8,4},{12,0},{0,12},{5,9},{9,5},{13,1},{1,13},{6,10},{10,6},... | collective-permute-start | bytes 98312 | tf_op jit(solution)/shard_map/ppermute | solution.py:846

commit v13 on v12

--- a/solution.py
+++ b/solution.py
@@ -113,7 +113,7 @@
         pq_ref = message_ref[4]
     (
         x_ref, wet_ref, flux_ref, diff_ref, table_ref, flat_ref, row_ref, edge_ref,
-        x_sem, sem, out_sem,
+        factor_ref, x_sem, sem, out_sem,
     ) = refs[2 * outs :]
     rows, channels, columns = x_ref.shape
     half = columns // 2
@@ -153,6 +153,18 @@
         first = col_group * channels
         flux_copy.wait()
         weight = channel_column(flux_ref[...], channels, first)
+        diff_copy.wait()
+        diff = channel_column(diff_ref[...], channels, first)
+        total = rows * groups_x
+        base = (row_group * rows).astype(f32)
+        tiles = wave_parts(columns)
+        for k, (group, n, _) in enumerate(tiles):
+            lam, alpha, _ = decay_terms(diff, half_rates(group, n, LANES, columns))
+            factor_ref[k, 0] = lam
+            lows, highs = edge_factors(lam, alpha, base, total, rows)
+            for r in range(rows):
+                factor_ref[k, 1 + r] = lows[r]
+                factor_ref[k, 1 + rows + r] = highs[r]
         for r in range(rows):
             x_copies[r].wait()
             row_ref[r : r + 1, :] = jnp.sum(x_ref[r] * weight, axis=0, keepdims=True)
@@ -167,29 +179,29 @@
                 flat_ref[:, lanes], table_ref[lanes, :], preferred_element_type=f32
             )
             y_ref[:, :, lanes] = part.reshape(rows, channels, half)
+            for tile, (group, _, parts) in enumerate(tiles):
+                if group != k:
+                    continue
+                lam = factor_ref[tile, 0]
+                for at in parts:
+                    lanes = slice(at, at + LANES)
+                    here = slice(at - k * half, at - k * half + LANES)
+                    p = factor_ref[tile, 1] * part[0:channels, here]
+                    q = factor_ref[tile, 2 * rows] * part[(rows - 1) * channels :, here]
+                    for r in range(1, rows):
+                        up = part[r * channels : (r + 1) * channels, here]
+                        down = part[(rows - 1 - r) * channels : (rows - r) * channels, here]
+                        p = lam * p + factor_ref[tile, 1 + r] * up
+                        q = lam * q + factor_ref[tile, 2 * rows - r] * down
+                    if paired:
+                        for mask, out in ((1, e1_ref), (2, e2_ref), (3, e3_ref)):
+                            upward = row_group < (row_group ^ mask)
+                            out[0:channels, lanes] = jnp.where(upward, p, q).astype(bf16)
+                    else:
+                        pq_ref[0, :, lanes] = p.astype(bf16)
+                        pq_ref[1, :, lanes] = q.astype(bf16)
         for copy in y_copies:
             copy.start()
-        diff_copy.wait()
-        diff = channel_column(diff_ref[...], channels, first)
-        total = rows * groups_x
-        base = (row_group * rows).astype(f32)
-        for group, n, parts in wave_parts(columns):
-            lam, alpha, _ = decay_terms(diff, half_rates(group, n, LANES, columns))
-            lows, highs = edge_factors(lam, alpha, base, total, rows)
-            for part in parts:
-                lanes = slice(part, part + LANES)
-                p = lows[0] * y_ref[0, :, lanes]
-                q = highs[-1] * y_ref[rows - 1, :, lanes]
-                for r in range(1, rows):
-                    p = lam * p + lows[r] * y_ref[r, :, lanes]
-                    q = lam * q + highs[-1 - r] * y_ref[rows - 1 - r, :, lanes]
-                if paired:
-                    for mask, out in ((1, e1_ref), (2, e2_ref), (3, e3_ref)):
-                        upward = row_group < (row_group ^ mask)
-                        out[0:channels, lanes] = jnp.where(upward, p, q).astype(bf16)
-                else:
-                    pq_ref[0, :, lanes] = p.astype(bf16)
-                    pq_ref[1, :, lanes] = q.astype(bf16)
         for copy in message_copies:
             copy.start()
         for copy in surface_copies + y_copies + message_copies:
@@ -705,6 +717,7 @@
             pltpu.VMEM((rows * channels, columns), bf16),
             pltpu.VMEM((rows, columns), f32),
             pltpu.VMEM((4 * rows, columns), f32),
+            pltpu.VMEM((columns // 2 // LANES, 2 * rows + 1, channels, LANES), f32),
             pltpu.SemaphoreType.DMA((rows,)),
             pltpu.SemaphoreType.DMA((3,)),
             pltpu.SemaphoreType.DMA((rows + len(shapes) - 1,)),

time: 30.2 us -> 30.1 us (level)
  no operation moved by 1% of the time
where the time goes in v13:
time: 30.1 us; the launch traced here: 29.9 us
  starting transfers between devices  15.5 us (51%)
  Pallas kernels  8.13 us (27%)
  waiting for transfers between devices  4.68 us (16%)
  between operations  1.5 us (5%)
    ppermute x3, starting transfers between devices, local(): lax.ppermute(block, 'gy', sum_route(mask))  4.45 us
    pallas_call x1, Pallas kernels, local(): pl.pallas_call(functools.partial(start_kernel, groups_x, paired), out_sha...  3.67 us
    ppermute x1, starting transfers between devices, local(): far = lax.ppermute(wide, ('comp', 'gy'), partner_route(mask))  3 us
    ppermute x1, starting transfers between devices, local(): lax.ppermute(coarse, 'gy', sum_route(mask))  2.65 us
    ppermute x3, waiting for transfers between devices, local(): lax.ppermute(block, 'gy', sum_route(mask))  2 us
    ppermute x1, starting transfers between devices, local(): far = lax.ppermute(far, 'gx', both_ways(ring_pairs(groups_x, 1)))  1.6 us
    ppermute x1, starting transfers between devices, local(): e3 = lax.ppermute(e3, 'gx', both_ways(ring_pairs(groups_x, 1)))  1.6 us
    ppermute x1, starting transfers between devices, local(): surface = lax.ppermute(coarse, ('comp', 'gy'), partner_route(0)).astype(f32)  1.58 us
  transfers between devices with their start and end apart: 12, of which 6 were waited for; matrix products, arithmetic and copies ran while one was open for 0% of the time, Pallas kernels for 7%

profile of v13, /device:TPU:0, one launch (start us, length us, event | category | flops | bytes accessed | tf_op | source)
XLA Modules:
  0.0 29.9 jit_solution(17200137398368436889)
XLA Ops:
  0.0 0.0 copy-start.6
  0.0 0.0 copy-start.7
  0.0 0.0 copy-start.8
  0.0 0.0 copy-start.9
  0.0 0.0 copy-start.2
  0.0 0.0 copy-start.3
  0.0 3.7 %surface_and_forward_or_halos.1 = (bf16[64,128]{1,0:T(8,128)(2,1)}, bf16[80,128]{1,0:T(8,128)(2,1)}, f32[8,32,1024]{2,1,0:T(8,128)}, bf16[80,1024]{1,0:T(8,128)(...) custom-call(f32[1,8,32,1024]{3,2,1,0:T(8,128)} %x_ref.1, s32[8,1024]{1,0:T(8,128)} %wet_ref.1, ...), custom_call_target="tpu_custom_call" | custom-call | tf_op jit(solution)/shard_map/surface_and_forward_or_halos/pallas_call | solution.py:705
  3.7 3.0 %collective-permute-start.5 = (bf16[80,128]{1,0:T(8,128)(2,1)}, bf16[80,128]{1,0:T(8,128)(2,1)S(1)}, u32[]{:S(2)}, u32[]{:S(2)}) collective-permute-start(bf16[80,128]{1,0:T(8,128)(2,1)} %get-tuple-element.39), channel_id=1, source_target_pairs={{0,17},{17,0},{1,16},{16,1},{2,19},{19,2},{3,18},{18,3},{4,21},{21... | collective-permute-start | bytes 61448 | tf_op jit(solution)/shard_map/ppermute | solution.py:739
  6.7 1.6 %collective-permute-start.4 = (bf16[64,128]{1,0:T(8,128)(2,1)}, bf16[64,128]{1,0:T(8,128)(2,1)S(1)}, u32[]{:S(2)}, u32[]{:S(2)}) collective-permute-start(bf16[64,128]{1,0:T(8,128)(2,1)} %get-tuple-element.38), channel_id=1, source_target_pairs={{0,16},{16,0},{1,17},{17,1},{2,18},{18,2},{3,19},{19,3},{4,20},{20... | collective-permute-start | bytes 49160 | tf_op jit(solution)/shard_map/ppermute | solution.py:737
  8.3 0.0 collective-permute-start
  8.3 1.6 %collective-permute-start.1 = (bf16[80,1024]{1,0:T(8,128)(2,1)}, bf16[80,1024]{1,0:T(8,128)(2,1)S(1)}, u32[]{:S(2)}, u32[]{:S(2)}) collective-permute-start(bf16[80,1024]{1,0:T(8,128)(2,1)} %get-tuple-element.30), channel_id=1, source_target_pairs={{4,8},{8,4},{12,0},{0,12},{5,9},{9,5},{13,1},{1,13},{6,10},{10,6},... | collective-permute-start | bytes 491528 | tf_op jit(solution)/shard_map/ppermute | solution.py:770
  9.9 0.5 %collective-permute-start.2 = (bf16[32,1024]{1,0:T(8,128)(2,1)}, bf16[32,1024]{1,0:T(8,128)(2,1)S(1)}, u32[]{:S(2)}, u32[]{:S(2)}) collective-permute-start(bf16[32,1024]{1,0:T(8,128)(2,1)} %get-tuple-element.31), channel_id=1, source_target_pairs={{16,17},{17,16},{18,19},{19,18},{0,8},{8,0},{1,9},{9,1},{2,10},{10... | collective-permute-start | bytes 196616 | tf_op jit(solution)/shard_map/ppermute | solution.py:772
  10.4 0.2 collective-permute-done.4
  10.7 0.0 collective-permute-start.3
  10.7 0.0 collective-permute-done.5
  10.7 2.7 %collective-permute-start.6 = (bf16[64,128]{1,0:T(8,128)(2,1)S(1)}, bf16[64,128]{1,0:T(8,128)(2,1)S(1)}, u32[]{:S(2)}, u32[]{:S(2)}) collective-permute-start(bf16[64,128]{1,0:T(8,128)(2,1)S(1)} %get-tuple-element.51._), channel_id=1, source_target_pairs={{0,2},{1,3},{2,0},{3,1},{4,6},{5,7},{6,4},{7,5},{8,10},{9,11},{10,... | collective-permute-start | bytes 49160 | tf_op jit(solution)/shard_map/ppermute | solution.py:746
  14.6 0.0 copy-done.6
  14.6 0.0 copy-done.7
  14.6 0.0 copy-done.8
  14.7 0.0 copy-done.9
  14.7 0.6 %one_hots.1 = (bf16[128,4096]{1,0:T(8,128)(2,1)S(1)}, bf16[128,4096]{1,0:T(8,128)(2,1)S(1)}, s32[32,128]{1,0:T(8,128)S(1)}, s32[32,128]{1,0:T(8,128)S(1)}) custom-call(s32[1,1,32,128]{3,2,1,0:T(8,128)S(1)} %copy-done.6, s32[1,1,32,128]{3,2,1,0:T(8,128)S(1)} %copy-done.7, s32[1,1,32,128]{3,2,1,0:T(8,128)S(1)} %copy-done.8, s32[1,1,32,128]{3,2,1,0:T(8,128)S(1)} %copy-done.9, ...), custom_call_target="tpu_custom_call" | custom-call | tf_op jit(solution)/shard_map/one_hots/pallas_call | solution.py:775
  15.3 0.1 collective-permute-done.6.refs_1_
  15.4 1.0 %collective-permute-done.2.e2_ref.refs_12_ = bf16[32,1024]{1,0:T(8,128)(2,1)S(1)} collective-permute-done((bf16[32,1024]{1,0:T(8,128)(2,1)}, bf16[32,1024]{1,0:T(8,128)(2,1)S(1)}, u32[]{:S(2)}, u32[]{:S(2)}) %collective-permute-start.2) | collective-permute-done | bytes 65568 | tf_op jit(solution)/shard_map/ppermute | solution.py:772
  16.4 0.0 collective-permute-done.3.e4_ref.refs_13_
  16.4 0.0 collective-permute-done.e1_ref.refs_10_
  16.4 0.0 collective-permute-done.1.e3_ref.refs_11_
  16.4 0.0 copy-done.2
  16.4 0.0 copy-done.3
  16.4 0.0 copy-start
  16.4 0.0 copy-start.1
  16.5 0.0 copy-start.5
  16.5 0.0 copy-start.10
  16.5 1.4 %regrid_blocks.1 = (f32[64,128]{1,0:T(8,128)S(1)}, bf16[64,128]{1,0:T(8,128)(2,1)S(1)}, bf16[80,128]{1,0:T(8,128)(2,1)S(1)}, bf16[96,128]{1,0:T(8,128)(2,1)S(1)}) custom-call(f32[64,128]{1,0:T(8,128)S(1)} %get-tuple-element.52.refs_0_, bf16[64,128]{1,0:T(8,128)(2,1)S(1)} %collective-permute-done.6.refs_1_, bf16[128,4096]{1,0:T(8,128)(2,1)S(1)} %get-tuple-element.40.refs_2_, ...), custom_call_target="tpu_custom_call" | custom-call | tf_op jit(solution)/shard_map/regrid_blocks/pallas_call | solution.py:788
  17.8 0.0 copy-start.4
  17.9 0.0 copy-start.11
  17.9 2.5 %collective-permute-start.9 = (bf16[96,128]{1,0:T(8,128)(2,1)S(1)}, bf16[96,128]{1,0:T(8,128)(2,1)S(1)}, u32[]{:S(2)}, u32[]{:S(2)}) collective-permute-start(bf16[96,128]{1,0:T(8,128)(2,1)S(1)} %get-tuple-element.47), channel_id=1, source_target_pairs={{0,3},{1,2},{2,1},{3,0},{4,7},{5,6},{6,5},{7,4},{8,11},{9,10},{10,... | collective-permute-start | bytes 73736 | tf_op jit(solution)/shard_map/ppermute | solution.py:807
  20.4 0.2 collective-permute-start.8
  20.6 1.7 %collective-permute-start.7 = (bf16[64,128]{1,0:T(8,128)(2,1)S(1)}, bf16[64,128]{1,0:T(8,128)(2,1)S(1)}, u32[]{:S(2)}, u32[]{:S(2)}) collective-permute-start(bf16[64,128]{1,0:T(8,128)(2,1)S(1)} %get-tuple-element.45), channel_id=1, source_target_pairs={{0,1},{1,0},{2,3},{3,2},{4,5},{5,4},{6,7},{7,6},{8,9},{9,8},{10,11... | collective-permute-start | bytes 49160 | tf_op jit(solution)/shard_map/ppermute | solution.py:807
  22.3 0.0 copy-done
  22.3 0.0 copy-done.1
  22.3 0.0 copy-done.5
  22.3 0.0 copy-done.10
  22.3 1.0 %damping_or_first_step.1 = (bf16[256,1024]{1,0:T(8,128)(2,1)S(1)}, f32[7,16,1024]{2,1,0:T(8,128)S(1)}, f32[10,2,24,1024]{3,2,1,0:T(8,128)S(1)}) custom-call(f32[1,8,32,1024]{3,2,1,0:T(8,128)S(1)} %copy-done, s32[8,1024]{1,0:T(8,128)S(1)} %copy-done.5, f32[1,128]{1,0:T(1,128)S(1)} %bitcast.4, f32[8,32,1024]{2,1,0:T(8,128)S(1)} %copy-done.1, ...), custom_call_target="tpu_custom_call" | custom-call | tf_op jit(solution)/shard_map/damping_or_first_step/pallas_call | solution.py:827
  23.3 1.0 %collective-permute-done.7.refs_0_ = bf16[64,128]{1,0:T(8,128)(2,1)S(1)} collective-permute-done((bf16[64,128]{1,0:T(8,128)(2,1)S(1)}, bf16[64,128]{1,0:T(8,128)(2,1)S(1)}, u32[]{:S(2)}, u32[]{:S(2)}) %collective-permute-start.7) | collective-permute-done | bytes 16416 | tf_op jit(solution)/shard_map/ppermute | solution.py:807
  24.3 1.0 %collective-permute-done.8.refs_1_ = bf16[80,128]{1,0:T(8,128)(2,1)S(1)} collective-permute-done((bf16[80,128]{1,0:T(8,128)(2,1)S(1)}, bf16[80,128]{1,0:T(8,128)(2,1)S(1)}, u32[]{:S(2)}, u32[]{:S(2)}) %collective-permute-start.8) | collective-permute-done | bytes 20512 | tf_op jit(solution)/shard_map/ppermute | solution.py:807
  25.3 0.0 collective-permute-done.9.refs_2_
  25.4 0.1 collective-permute-start.10
  25.4 1.6 %collective-permute-start.11 = (bf16[128,128]{1,0:T(8,128)(2,1)S(1)}, bf16[128,128]{1,0:T(8,128)(2,1)S(1)}, u32[]{:S(2)}, u32[]{:S(2)}) collective-permute-start(bf16[128,128]{1,0:T(8,128)(2,1)S(1)} %get-tuple-element.50), channel_id=1, source_target_pairs={{4,8},{8,4},{12,0},{0,12},{5,9},{9,5},{13,1},{1,13},{6,10},{10,6},... | collective-permute-start | bytes 98312 | tf_op jit(solution)/shard_map/ppermute | solution.py:859
  27.0 0.0 copy-done.4
  27.1 0.0 copy-done.11
  27.1 0.4 %inverse_or_second_step.1 = (f32[8,32,1024]{2,1,0:T(8,128)S(1)}, f32[32,128]{1,0:T(8,128)S(1)}) custom-call(f32[1,128]{1,0:T(1,128)S(1)} %bitcast.5, bf16[1024,512]{1,0:T(8,128)(2,1)S(1)} %copy-done.4, bf16[256,1024]{1,0:T(8,128)(2,1)S(1)} %get-tuple-element.33.zb_ref, f32[7,16,1024]{2,1,0:T(8,128)S(1)} %get-tuple-element.34.c_ref._, ...), custom_call_target="tpu_custom_call" | custom-call | tf_op jit(solution)/shard_map/inverse_or_second_step/pallas_call | solution.py:860
  27.5 0.0 collective-permute-done.10.near_ref
  27.5 1.3 %collective-permute-done.11.far_ref = bf16[128,128]{1,0:T(8,128)(2,1)S(1)} collective-permute-done((bf16[128,128]{1,0:T(8,128)(2,1)S(1)}, bf16[128,128]{1,0:T(8,128)(2,1)S(1)}, u32[]{:S(2)}, u32[]{:S(2)}) %collective-permute-start.11) | collective-permute-done | bytes 32800 | tf_op jit(solution)/shard_map/ppermute | solution.py:859
  28.9 1.0 %add_surface_terms.1 = f32[1,8,32,1024]{3,2,1,0:T(8,128)} custom-call(f32[32,128]{1,0:T(8,128)S(1)} %get-tuple-element.36.column_ref, f32[8,32,1024]{2,1,0:T(8,128)S(1)} %get-tuple-element.37.base_ref, f32[7,16,1024]{2,1,0:T(8,128)S(1)} %get-tuple-element.34.c_ref._, f32[64,128]{1,0:T(8,128)S(1)} %get-tuple-element.48.sum_ref, ...), custom_call_target="tpu_custom_call" | custom-call | tf_op jit(solution)/shard_map/add_surface_terms/pallas_call | solution.py:868
  (2 shorter events, 0.1 us)
Async XLA Ops:
  0.0 14.6 %copy-start.6 = (s32[1,1,32,128]{3,2,1,0:T(8,128)S(1)}, s32[1,1,32,128]{3,2,1,0:T(8,128)}, u32[]{:S(2)}) copy-start(s32[1,1,32,128]{3,2,1,0:T(8,128)} %a_src.1) | copy-start | bytes 49156
  0.0 14.6 %copy-start.7 = (s32[1,1,32,128]{3,2,1,0:T(8,128)S(1)}, s32[1,1,32,128]{3,2,1,0:T(8,128)}, u32[]{:S(2)}) copy-start(s32[1,1,32,128]{3,2,1,0:T(8,128)} %a_dst.1) | copy-start | bytes 49156
  0.0 14.6 %copy-start.8 = (s32[1,1,32,128]{3,2,1,0:T(8,128)S(1)}, s32[1,1,32,128]{3,2,1,0:T(8,128)}, u32[]{:S(2)}) copy-start(s32[1,1,32,128]{3,2,1,0:T(8,128)} %m_src.1) | copy-start | bytes 49156
  0.0 14.7 %copy-start.9 = (s32[1,1,32,128]{3,2,1,0:T(8,128)S(1)}, s32[1,1,32,128]{3,2,1,0:T(8,128)}, u32[]{:S(2)}) copy-start(s32[1,1,32,128]{3,2,1,0:T(8,128)} %m_dst.1) | copy-start | bytes 49156
  0.0 16.4 %copy-start.2 = (bf16[1,1,32,128,128]{4,3,2,1,0:T(8,128)(2,1)S(1)}, bf16[1,1,32,128,128]{4,3,2,1,0:T(8,128)(2,1)}, u32[]{:S(2)}) copy-start(bf16[1,1,32,128,128]{4,3,2,1,0:T(8,128)(2,1)} %refs_8_.1) | copy-start | bytes 3145732
  0.0 16.4 %copy-start.3 = (bf16[1,1,32,128,128]{4,3,2,1,0:T(8,128)(2,1)S(1)}, bf16[1,1,32,128,128]{4,3,2,1,0:T(8,128)(2,1)}, u32[]{:S(2)}) copy-start(bf16[1,1,32,128,128]{4,3,2,1,0:T(8,128)(2,1)} %refs_9_.1) | copy-start | bytes 3145732
  3.7 7.0 %collective-permute-start.5 = (bf16[80,128]{1,0:T(8,128)(2,1)}, bf16[80,128]{1,0:T(8,128)(2,1)S(1)}, u32[]{:S(2)}, u32[]{:S(2)}) collective-permute-start(bf16[80,128]{1,0:T(8,128)(2,1)} %get-tuple-element.39), channel_id=1, source_target_pairs={{0,17},{17,0},{1,16},{16,1},{2,19},{19,2},{3,18},{18,3},{4,21},{21... | collective-permute-start | bytes 61448 | tf_op jit(solution)/shard_map/ppermute | solution.py:739
  6.7 3.9 %collective-permute-start.4 = (bf16[64,128]{1,0:T(8,128)(2,1)}, bf16[64,128]{1,0:T(8,128)(2,1)S(1)}, u32[]{:S(2)}, u32[]{:S(2)}) collective-permute-start(bf16[64,128]{1,0:T(8,128)(2,1)} %get-tuple-element.38), channel_id=1, source_target_pairs={{0,16},{16,0},{1,17},{17,1},{2,18},{18,2},{3,19},{19,3},{4,20},{20... | collective-permute-start | bytes 49160 | tf_op jit(solution)/shard_map/ppermute | solution.py:737
  8.3 8.1 %collective-permute-start = (bf16[80,1024]{1,0:T(8,128)(2,1)}, bf16[80,1024]{1,0:T(8,128)(2,1)S(1)}, u32[]{:S(2)}, u32[]{:S(2)}) collective-permute-start(bf16[80,1024]{1,0:T(8,128)(2,1)} %get-tuple-element.29), channel_id=1, source_target_pairs={{0,4},{4,0},{8,12},{12,8},{1,5},{5,1},{9,13},{13,9},{2,6},{6,2},{1... | collective-permute-start | bytes 491528 | tf_op jit(solution)/shard_map/ppermute | solution.py:769
  8.3 8.1 %collective-permute-start.1 = (bf16[80,1024]{1,0:T(8,128)(2,1)}, bf16[80,1024]{1,0:T(8,128)(2,1)S(1)}, u32[]{:S(2)}, u32[]{:S(2)}) collective-permute-start(bf16[80,1024]{1,0:T(8,128)(2,1)} %get-tuple-element.30), channel_id=1, source_target_pairs={{4,8},{8,4},{12,0},{0,12},{5,9},{9,5},{13,1},{1,13},{6,10},{10,6},... | collective-permute-start | bytes 491528 | tf_op jit(solution)/shard_map/ppermute | solution.py:770
  9.9 6.5 %collective-permute-start.2 = (bf16[32,1024]{1,0:T(8,128)(2,1)}, bf16[32,1024]{1,0:T(8,128)(2,1)S(1)}, u32[]{:S(2)}, u32[]{:S(2)}) collective-permute-start(bf16[32,1024]{1,0:T(8,128)(2,1)} %get-tuple-element.31), channel_id=1, source_target_pairs={{16,17},{17,16},{18,19},{19,18},{0,8},{8,0},{1,9},{9,1},{2,10},{10... | collective-permute-start | bytes 196616 | tf_op jit(solution)/shard_map/ppermute | solution.py:772
  10.7 5.8 %collective-permute-start.3 = (bf16[32,1024]{1,0:T(8,128)(2,1)}, bf16[32,1024]{1,0:T(8,128)(2,1)S(1)}, u32[]{:S(2)}, u32[]{:S(2)}) collective-permute-start(bf16[32,1024]{1,0:T(8,128)(2,1)} %get-tuple-element.32), channel_id=1, source_target_pairs={{17,18},{18,17},{16,20},{20,16},{19,23},{23,19},{0,4},{4,0},{1,5},... | collective-permute-start | bytes 196616 | tf_op jit(solution)/shard_map/ppermute | solution.py:773
  10.7 4.7 %collective-permute-start.6 = (bf16[64,128]{1,0:T(8,128)(2,1)S(1)}, bf16[64,128]{1,0:T(8,128)(2,1)S(1)}, u32[]{:S(2)}, u32[]{:S(2)}) collective-permute-start(bf16[64,128]{1,0:T(8,128)(2,1)S(1)} %get-tuple-element.51._), channel_id=1, source_target_pairs={{0,2},{1,3},{2,0},{3,1},{4,6},{5,7},{6,4},{7,5},{8,10},{9,11},{10,... | collective-permute-start | bytes 49160 | tf_op jit(solution)/shard_map/ppermute | solution.py:746
  16.4 5.9 %copy-start = (f32[1,8,32,1024]{3,2,1,0:T(8,128)S(1)}, f32[1,8,32,1024]{3,2,1,0:T(8,128)}, u32[]{:S(2)}) copy-start(f32[1,8,32,1024]{3,2,1,0:T(8,128)} %x_ref.1) | copy-start | bytes 3145732
  16.4 5.9 %copy-start.1 = (f32[8,32,1024]{2,1,0:T(8,128)S(1)}, f32[8,32,1024]{2,1,0:T(8,128)}, u32[]{:S(2)}) copy-start(f32[8,32,1024]{2,1,0:T(8,128)} %get-tuple-element.28.y_ref) | copy-start | bytes 3145732
  16.5 5.9 %copy-start.5 = (s32[8,1024]{1,0:T(8,128)S(1)}, s32[8,1024]{1,0:T(8,128)}, u32[]{:S(2)}) copy-start(s32[8,1024]{1,0:T(8,128)} %wet_ref.1) | copy-start | bytes 98308
  16.5 5.9 %copy-start.10 = (f32[128]{0:T(128)S(1)}, f32[128]{0:T(128)}, u32[]{:S(2)}) copy-start(f32[128]{0:T(128)} %param.19) | copy-start | bytes 1540
  17.8 9.2 %copy-start.4 = (bf16[1024,512]{1,0:T(8,128)(2,1)S(1)}, bf16[1024,512]{1,0:T(8,128)(2,1)}, u32[]{:S(2)}) copy-start(bf16[1024,512]{1,0:T(8,128)(2,1)} %constant.5.clone.table_ref) | copy-start | bytes 3145732
  17.9 9.2 %copy-start.11 = (f32[128]{0:T(128)S(1)}, f32[128]{0:T(128)}, u32[]{:S(2)}) copy-start(f32[128]{0:T(128)} %param.18) | copy-start | bytes 1540
  17.9 7.4 %collective-permute-start.9 = (bf16[96,128]{1,0:T(8,128)(2,1)S(1)}, bf16[96,128]{1,0:T(8,128)(2,1)S(1)}, u32[]{:S(2)}, u32[]{:S(2)}) collective-permute-start(bf16[96,128]{1,0:T(8,128)(2,1)S(1)} %get-tuple-element.47), channel_id=1, source_target_pairs={{0,3},{1,2},{2,1},{3,0},{4,7},{5,6},{6,5},{7,4},{8,11},{9,10},{10,... | collective-permute-start | bytes 73736 | tf_op jit(solution)/shard_map/ppermute | solution.py:807
  20.4 4.9 %collective-permute-start.8 = (bf16[80,128]{1,0:T(8,128)(2,1)S(1)}, bf16[80,128]{1,0:T(8,128)(2,1)S(1)}, u32[]{:S(2)}, u32[]{:S(2)}) collective-permute-start(bf16[80,128]{1,0:T(8,128)(2,1)S(1)} %get-tuple-element.46), channel_id=1, source_target_pairs={{0,2},{1,3},{2,0},{3,1},{4,6},{5,7},{6,4},{7,5},{8,10},{9,11},{10,... | collective-permute-start | bytes 61448 | tf_op jit(solution)/shard_map/ppermute | solution.py:807
  20.6 3.7 %collective-permute-start.7 = (bf16[64,128]{1,0:T(8,128)(2,1)S(1)}, bf16[64,128]{1,0:T(8,128)(2,1)S(1)}, u32[]{:S(2)}, u32[]{:S(2)}) collective-permute-start(bf16[64,128]{1,0:T(8,128)(2,1)S(1)} %get-tuple-element.45), channel_id=1, source_target_pairs={{0,1},{1,0},{2,3},{3,2},{4,5},{5,4},{6,7},{7,6},{8,9},{9,8},{10,11... | collective-permute-start | bytes 49160 | tf_op jit(solution)/shard_map/ppermute | solution.py:807
  25.4 2.1 %collective-permute-start.10 = (bf16[128,128]{1,0:T(8,128)(2,1)S(1)}, bf16[128,128]{1,0:T(8,128)(2,1)S(1)}, u32[]{:S(2)}, u32[]{:S(2)}) collective-permute-start(bf16[128,128]{1,0:T(8,128)(2,1)S(1)} %get-tuple-element.49), channel_id=1, source_target_pairs={{0,4},{4,0},{8,12},{12,8},{1,5},{5,1},{9,13},{13,9},{2,6},{6,2},{1... | collective-permute-start | bytes 98312 | tf_op jit(solution)/shard_map/ppermute | solution.py:858
  25.4 3.4 %collective-permute-start.11 = (bf16[128,128]{1,0:T(8,128)(2,1)S(1)}, bf16[128,128]{1,0:T(8,128)(2,1)S(1)}, u32[]{:S(2)}, u32[]{:S(2)}) collective-permute-start(bf16[128,128]{1,0:T(8,128)(2,1)S(1)} %get-tuple-element.50), channel_id=1, source_target_pairs={{4,8},{8,4},{12,0},{0,12},{5,9},{9,5},{13,1},{1,13},{6,10},{10,6},... | collective-permute-start | bytes 98312 | tf_op jit(solution)/shard_map/ppermute | solution.py:859

commit v14 on v13

--- a/solution.py
+++ b/solution.py
@@ -288,7 +288,7 @@
     surfaces = refs[:n_surfaces]
     (
         src_hot_ref, dst_hot_ref, src_row_ref, dst_row_ref, a_count, m_count, a_weight, m_weight,
-        _, _, _, _,
+        _, _, _,
         *refs,
     ) = refs[n_surfaces:]
     land_ref, *sent_refs = refs[:-4]
@@ -770,9 +770,8 @@
     e3 = lax.ppermute(e3, "gx", both_ways(ring_pairs(groups_x, 1)))
     axes = ("comp", "gx", "gy")
     e2 = lax.ppermute(e2, axes, level_route(0))
-    e4 = lax.ppermute(e4, axes, level_route(1))
-
-    one_hots = pl.pallas_call(
+
+    *one_hots, dst_row = pl.pallas_call(
         functools.partial(one_hot_kernel, rows, columns),
         out_shape=[
             shape((LANES, blocks * points), bf16),
@@ -785,11 +784,13 @@
         compiler_params=params(),
         name="one_hots",
     )(a2o_source, a2o_target, marine_air_input_index, marine_air_output_index, coarse)
+    e4, dst_row = lax.optimization_barrier((e4, dst_row))
+    e4 = lax.ppermute(e4, axes, level_route(1))
     landing, *sent = pl.pallas_call(
         functools.partial(regrid_kernel, len(surfaces)),
         out_shape=[shape((cells, LANES), f32)]
         + [shape((cells + 16 * (mask - 1), LANES), bf16) for mask in range(1, groups_y)],
-        in_specs=[vmem] * (len(surfaces) + 4) + [smem, smem, hbm, hbm] + [anywhere] * 4,
+        in_specs=[vmem] * (len(surfaces) + 4) + [smem, smem, hbm, hbm] + [anywhere] * 3,
         out_specs=[vmem] * groups_y,
         scratch_shapes=[
             pltpu.VMEM((blocks, points, points), bf16),
@@ -800,8 +801,8 @@
         compiler_params=params(),
         name="regrid_blocks",
     )(
-        *surfaces, *one_hots, a2o_count, marine_air_piece_tally,
-        a2o_weight, marine_air_piece_factor, e1, e3, e2, e4,
+        *surfaces, *one_hots, dst_row, a2o_count, marine_air_piece_tally,
+        a2o_weight, marine_air_piece_factor, e1, e3, e2,
     )
     parts = [
         lax.ppermute(block, "gy", sum_route(mask)) for mask, block in enumerate(sent, 1)

time: 30.1 us -> 30.2 us (level)
    ppermute x1, waiting for transfers between devices: 1.03 us -> 0.01 us  [local(): e2 = lax.ppermute(e2, axes, level_route(0))]
    ppermute x1, starting transfers between devices: 0.54 us -> 1.49 us  [local(): e2 = lax.ppermute(e2, axes, level_route(0))]
    ppermute x1, starting transfers between devices: 1.6 us -> 0.65 us  [local(): e3 = lax.ppermute(e3, 'gx', both_ways(ring_pairs(groups_x, 1)))]
    ppermute x1, waiting for transfers between devices: 0.08 us -> 0.89 us  [local(): lax.ppermute(coarse, 'gy', sum_route(mask))]
  transfers between devices with their start and end apart: 12 -> 12, of which waited for: 6 -> 5; matrix products, arithmetic and copies ran while one was open for 0% -> 0% of each run, Pallas kernels for 7% -> 11%
where the time goes in v14:
time: 30.2 us; the launch traced here: 30 us
  starting transfers between devices  15.6 us (52%)
  Pallas kernels  8.13 us (27%)
  waiting for transfers between devices  4.76 us (16%)
  between operations  1.52 us (5%)
    ppermute x3, starting transfers between devices, local(): lax.ppermute(block, 'gy', sum_route(mask))  4.45 us
    pallas_call x1, Pallas kernels, local(): pl.pallas_call(functools.partial(start_kernel, groups_x, paired), out_sha...  3.67 us
    ppermute x1, starting transfers between devices, local(): far = lax.ppermute(wide, ('comp', 'gy'), partner_route(mask))  3 us
    ppermute x1, starting transfers between devices, local(): lax.ppermute(coarse, 'gy', sum_route(mask))  2.65 us
    ppermute x3, waiting for transfers between devices, local(): lax.ppermute(block, 'gy', sum_route(mask))  2.28 us
    ppermute x1, starting transfers between devices, local(): far = lax.ppermute(far, 'gx', both_ways(ring_pairs(groups_x, 1)))  1.6 us
    ppermute x1, starting transfers between devices, local(): surface = lax.ppermute(coarse, ('comp', 'gy'), partner_route(0)).astype(f32)  1.58 us
    ppermute x1, starting transfers between devices, local(): e2 = lax.ppermute(e2, axes, level_route(0))  1.49 us
  transfers between devices with their start and end apart: 12, of which 5 were waited for; matrix products, arithmetic and copies ran while one was open for 0% of the time, Pallas kernels for 11%

profile of v14, /device:TPU:0, one launch (start us, length us, event | category | flops | bytes accessed | tf_op | source)
XLA Modules:
  0.0 30.0 jit_solution(4973434894978603587)
XLA Ops:
  0.0 0.0 copy-start.9
  0.0 0.0 copy-start.8
  0.0 0.0 copy-start.7
  0.0 0.0 copy-start.6
  0.0 0.0 copy-start.2
  0.0 0.0 copy-start.1
  0.0 3.7 %surface_and_forward_or_halos.1 = (bf16[64,128]{1,0:T(8,128)(2,1)}, bf16[80,128]{1,0:T(8,128)(2,1)}, f32[8,32,1024]{2,1,0:T(8,128)}, bf16[80,1024]{1,0:T(8,128)(...) custom-call(f32[1,8,32,1024]{3,2,1,0:T(8,128)} %x_ref.1, s32[8,1024]{1,0:T(8,128)} %wet_ref.1, ...), custom_call_target="tpu_custom_call" | custom-call | tf_op jit(solution)/shard_map/surface_and_forward_or_halos/pallas_call | solution.py:705
  3.7 3.0 %collective-permute-start.4 = (bf16[80,128]{1,0:T(8,128)(2,1)}, bf16[80,128]{1,0:T(8,128)(2,1)S(1)}, u32[]{:S(2)}, u32[]{:S(2)}) collective-permute-start(bf16[80,128]{1,0:T(8,128)(2,1)} %get-tuple-element.36), channel_id=1, source_target_pairs={{0,17},{17,0},{1,16},{16,1},{2,19},{19,2},{3,18},{18,3},{4,21},{21... | collective-permute-start | bytes 61448 | tf_op jit(solution)/shard_map/ppermute | solution.py:739
  6.7 1.6 %collective-permute-start.3 = (bf16[64,128]{1,0:T(8,128)(2,1)}, bf16[64,128]{1,0:T(8,128)(2,1)S(1)}, u32[]{:S(2)}, u32[]{:S(2)}) collective-permute-start(bf16[64,128]{1,0:T(8,128)(2,1)} %get-tuple-element.35), channel_id=1, source_target_pairs={{0,16},{16,0},{1,17},{17,1},{2,18},{18,2},{3,19},{19,3},{4,20},{20... | collective-permute-start | bytes 49160 | tf_op jit(solution)/shard_map/ppermute | solution.py:737
  8.3 1.5 %collective-permute-start.2 = (bf16[32,1024]{1,0:T(8,128)(2,1)}, bf16[32,1024]{1,0:T(8,128)(2,1)S(1)}, u32[]{:S(2)}, u32[]{:S(2)}) collective-permute-start(bf16[32,1024]{1,0:T(8,128)(2,1)} %get-tuple-element.33), channel_id=1, source_target_pairs={{16,17},{17,16},{18,19},{19,18},{0,8},{8,0},{1,9},{9,1},{2,10},{10... | collective-permute-start | bytes 196616 | tf_op jit(solution)/shard_map/ppermute | solution.py:772
  9.8 0.0 collective-permute-start
  9.8 0.6 %collective-permute-start.1 = (bf16[80,1024]{1,0:T(8,128)(2,1)}, bf16[80,1024]{1,0:T(8,128)(2,1)S(1)}, u32[]{:S(2)}, u32[]{:S(2)}) collective-permute-start(bf16[80,1024]{1,0:T(8,128)(2,1)} %get-tuple-element.32), channel_id=1, source_target_pairs={{4,8},{8,4},{12,0},{0,12},{5,9},{9,5},{13,1},{1,13},{6,10},{10,6},... | collective-permute-start | bytes 491528 | tf_op jit(solution)/shard_map/ppermute | solution.py:770
  10.4 0.2 collective-permute-done.3
  10.7 0.0 collective-permute-done.4
  10.7 0.0 copy-done.9
  10.7 0.0 copy-done.8
  10.7 0.0 copy-done.7
  10.7 0.0 copy-done.6
  10.7 0.6 %one_hots.1 = (bf16[128,4096]{1,0:T(8,128)(2,1)S(1)}, bf16[128,4096]{1,0:T(8,128)(2,1)S(1)}, s32[32,128]{1,0:T(8,128)S(1)}, s32[32,128]{1,0:T(8,128)S(1)}) custom-call(s32[1,1,32,128]{3,2,1,0:T(8,128)S(1)} %copy-done.6, s32[1,1,32,128]{3,2,1,0:T(8,128)S(1)} %copy-done.7, s32[1,1,32,128]{3,2,1,0:T(8,128)S(1)} %copy-done.8, s32[1,1,32,128]{3,2,1,0:T(8,128)S(1)} %copy-done.9, ...), custom_call_target="tpu_custom_call" | custom-call | tf_op jit(solution)/shard_map/one_hots/pallas_call | solution.py:774
  11.3 0.1 collective-permute-start.5
  11.4 2.7 %collective-permute-start.6 = (bf16[64,128]{1,0:T(8,128)(2,1)S(1)}, bf16[64,128]{1,0:T(8,128)(2,1)S(1)}, u32[]{:S(2)}, u32[]{:S(2)}) collective-permute-start(bf16[64,128]{1,0:T(8,128)(2,1)S(1)} %get-tuple-element.56._), channel_id=1, source_target_pairs={{0,2},{1,3},{2,0},{3,1},{4,6},{5,7},{6,4},{7,5},{8,10},{9,11},{10,... | collective-permute-start | bytes 49160 | tf_op jit(solution)/shard_map/ppermute | solution.py:746
  15.4 0.9 %collective-permute-done.6.refs_1_ = bf16[64,128]{1,0:T(8,128)(2,1)S(1)} collective-permute-done((bf16[64,128]{1,0:T(8,128)(2,1)S(1)}, bf16[64,128]{1,0:T(8,128)(2,1)S(1)}, u32[]{:S(2)}, u32[]{:S(2)}) %collective-permute-start.6) | collective-permute-done | bytes 16416 | tf_op jit(solution)/shard_map/ppermute | solution.py:746
  16.3 0.0 collective-permute-done.2.e2_ref.refs_12_
  16.3 0.0 collective-permute-done.e1_ref.refs_10_
  16.3 0.0 collective-permute-done.1.e3_ref.refs_11_
  16.3 0.0 copy-done.2
  16.3 0.0 copy-done.1
  16.3 0.0 copy-start
  16.3 0.0 copy-start.3
  16.3 0.0 copy-start.5
  16.3 0.0 copy-start.10
  16.3 1.4 %regrid_blocks.1 = (f32[64,128]{1,0:T(8,128)S(1)}, bf16[64,128]{1,0:T(8,128)(2,1)S(1)}, bf16[80,128]{1,0:T(8,128)(2,1)S(1)}, bf16[96,128]{1,0:T(8,128)(2,1)S(1)}) custom-call(f32[64,128]{1,0:T(8,128)S(1)} %get-tuple-element.55.refs_0_, bf16[64,128]{1,0:T(8,128)(2,1)S(1)} %collective-permute-done.6.refs_1_, bf16[128,4096]{1,0:T(8,128)(2,1)S(1)} %get-tuple-element.44.refs_2_, ...), custom_call_target="tpu_custom_call" | custom-call | tf_op jit(solution)/shard_map/regrid_blocks/pallas_call | solution.py:789
  17.7 0.0 copy-start.4
  17.7 0.0 copy-start.11
  17.7 3.1 %collective-permute-start.9 = (bf16[96,128]{1,0:T(8,128)(2,1)S(1)}, bf16[96,128]{1,0:T(8,128)(2,1)S(1)}, u32[]{:S(2)}, u32[]{:S(2)}) collective-permute-start(bf16[96,128]{1,0:T(8,128)(2,1)S(1)} %get-tuple-element.51), channel_id=1, source_target_pairs={{0,3},{1,2},{2,1},{3,0},{4,7},{5,6},{6,5},{7,4},{8,11},{9,10},{10,... | collective-permute-start | bytes 73736 | tf_op jit(solution)/shard_map/ppermute | solution.py:808
  20.8 0.0 collective-permute-start.8
  20.8 1.4 %collective-permute-start.7 = (bf16[64,128]{1,0:T(8,128)(2,1)S(1)}, bf16[64,128]{1,0:T(8,128)(2,1)S(1)}, u32[]{:S(2)}, u32[]{:S(2)}) collective-permute-start(bf16[64,128]{1,0:T(8,128)(2,1)S(1)} %get-tuple-element.49), channel_id=1, source_target_pairs={{0,1},{1,0},{2,3},{3,2},{4,5},{5,4},{6,7},{7,6},{8,9},{9,8},{10,11... | collective-permute-start | bytes 49160 | tf_op jit(solution)/shard_map/ppermute | solution.py:808
  22.2 0.0 collective-permute-done.5.e4_ref
  22.2 0.0 copy-done
  22.2 0.0 copy-done.3
  22.2 0.0 copy-done.5
  22.2 0.0 copy-done.10
  22.2 1.0 %damping_or_first_step.1 = (bf16[256,1024]{1,0:T(8,128)(2,1)S(1)}, f32[7,16,1024]{2,1,0:T(8,128)S(1)}, f32[10,2,24,1024]{3,2,1,0:T(8,128)S(1)}) custom-call(f32[1,8,32,1024]{3,2,1,0:T(8,128)S(1)} %copy-done, s32[8,1024]{1,0:T(8,128)S(1)} %copy-done.5, f32[1,128]{1,0:T(1,128)S(1)} %bitcast.4, f32[8,32,1024]{2,1,0:T(8,128)S(1)} %copy-done.3, ...), custom_call_target="tpu_custom_call" | custom-call | tf_op jit(solution)/shard_map/damping_or_first_step/pallas_call | solution.py:828
  23.2 1.3 %collective-permute-done.7.refs_0_ = bf16[64,128]{1,0:T(8,128)(2,1)S(1)} collective-permute-done((bf16[64,128]{1,0:T(8,128)(2,1)S(1)}, bf16[64,128]{1,0:T(8,128)(2,1)S(1)}, u32[]{:S(2)}, u32[]{:S(2)}) %collective-permute-start.7) | collective-permute-done | bytes 16416 | tf_op jit(solution)/shard_map/ppermute | solution.py:808
  24.5 0.9 %collective-permute-done.8.refs_1_ = bf16[80,128]{1,0:T(8,128)(2,1)S(1)} collective-permute-done((bf16[80,128]{1,0:T(8,128)(2,1)S(1)}, bf16[80,128]{1,0:T(8,128)(2,1)S(1)}, u32[]{:S(2)}, u32[]{:S(2)}) %collective-permute-start.8) | collective-permute-done | bytes 20512 | tf_op jit(solution)/shard_map/ppermute | solution.py:808
  25.5 0.0 collective-permute-done.9.refs_2_
  25.5 0.1 collective-permute-start.10
  25.6 1.6 %collective-permute-start.11 = (bf16[128,128]{1,0:T(8,128)(2,1)S(1)}, bf16[128,128]{1,0:T(8,128)(2,1)S(1)}, u32[]{:S(2)}, u32[]{:S(2)}) collective-permute-start(bf16[128,128]{1,0:T(8,128)(2,1)S(1)} %get-tuple-element.54), channel_id=1, source_target_pairs={{4,8},{8,4},{12,0},{0,12},{5,9},{9,5},{13,1},{1,13},{6,10},{10,6},... | collective-permute-start | bytes 98312 | tf_op jit(solution)/shard_map/ppermute | solution.py:860
  27.2 0.0 copy-done.4
  27.2 0.0 copy-done.11
  27.2 0.4 %inverse_or_second_step.1 = (f32[8,32,1024]{2,1,0:T(8,128)S(1)}, f32[32,128]{1,0:T(8,128)S(1)}) custom-call(f32[1,128]{1,0:T(1,128)S(1)} %bitcast.5, bf16[1024,512]{1,0:T(8,128)(2,1)S(1)} %copy-done.4, bf16[256,1024]{1,0:T(8,128)(2,1)S(1)} %get-tuple-element.39.zb_ref, f32[7,16,1024]{2,1,0:T(8,128)S(1)} %get-tuple-element.40.c_ref._, ...), custom_call_target="tpu_custom_call" | custom-call | tf_op jit(solution)/shard_map/inverse_or_second_step/pallas_call | solution.py:861
  27.7 0.0 collective-permute-done.10.near_ref
  27.7 1.3 %collective-permute-done.11.far_ref = bf16[128,128]{1,0:T(8,128)(2,1)S(1)} collective-permute-done((bf16[128,128]{1,0:T(8,128)(2,1)S(1)}, bf16[128,128]{1,0:T(8,128)(2,1)S(1)}, u32[]{:S(2)}, u32[]{:S(2)}) %collective-permute-start.11) | collective-permute-done | bytes 32800 | tf_op jit(solution)/shard_map/ppermute | solution.py:860
  29.0 1.0 %add_surface_terms.1 = f32[1,8,32,1024]{3,2,1,0:T(8,128)} custom-call(f32[32,128]{1,0:T(8,128)S(1)} %get-tuple-element.42.column_ref, f32[8,32,1024]{2,1,0:T(8,128)S(1)} %get-tuple-element.43.base_ref, f32[7,16,1024]{2,1,0:T(8,128)S(1)} %get-tuple-element.40.c_ref._, f32[64,128]{1,0:T(8,128)S(1)} %get-tuple-element.52.sum_ref, ...), custom_call_target="tpu_custom_call" | custom-call | tf_op jit(solution)/shard_map/add_surface_terms/pallas_call | solution.py:869
  (2 shorter events, 0.0 us)
Async XLA Ops:
  0.0 10.7 %copy-start.9 = (s32[1,1,32,128]{3,2,1,0:T(8,128)S(1)}, s32[1,1,32,128]{3,2,1,0:T(8,128)}, u32[]{:S(2)}) copy-start(s32[1,1,32,128]{3,2,1,0:T(8,128)} %m_dst.1) | copy-start | bytes 49156
  0.0 10.7 %copy-start.8 = (s32[1,1,32,128]{3,2,1,0:T(8,128)S(1)}, s32[1,1,32,128]{3,2,1,0:T(8,128)}, u32[]{:S(2)}) copy-start(s32[1,1,32,128]{3,2,1,0:T(8,128)} %m_src.1) | copy-start | bytes 49156
  0.0 10.7 %copy-start.7 = (s32[1,1,32,128]{3,2,1,0:T(8,128)S(1)}, s32[1,1,32,128]{3,2,1,0:T(8,128)}, u32[]{:S(2)}) copy-start(s32[1,1,32,128]{3,2,1,0:T(8,128)} %a_dst.1) | copy-start | bytes 49156
  0.0 10.7 %copy-start.6 = (s32[1,1,32,128]{3,2,1,0:T(8,128)S(1)}, s32[1,1,32,128]{3,2,1,0:T(8,128)}, u32[]{:S(2)}) copy-start(s32[1,1,32,128]{3,2,1,0:T(8,128)} %a_src.1) | copy-start | bytes 49156
  0.0 16.3 %copy-start.2 = (bf16[1,1,32,128,128]{4,3,2,1,0:T(8,128)(2,1)S(1)}, bf16[1,1,32,128,128]{4,3,2,1,0:T(8,128)(2,1)}, u32[]{:S(2)}) copy-start(bf16[1,1,32,128,128]{4,3,2,1,0:T(8,128)(2,1)} %refs_9_.1) | copy-start | bytes 3145732
  0.0 16.3 %copy-start.1 = (bf16[1,1,32,128,128]{4,3,2,1,0:T(8,128)(2,1)S(1)}, bf16[1,1,32,128,128]{4,3,2,1,0:T(8,128)(2,1)}, u32[]{:S(2)}) copy-start(bf16[1,1,32,128,128]{4,3,2,1,0:T(8,128)(2,1)} %refs_8_.1) | copy-start | bytes 3145732
  3.7 7.0 %collective-permute-start.4 = (bf16[80,128]{1,0:T(8,128)(2,1)}, bf16[80,128]{1,0:T(8,128)(2,1)S(1)}, u32[]{:S(2)}, u32[]{:S(2)}) collective-permute-start(bf16[80,128]{1,0:T(8,128)(2,1)} %get-tuple-element.36), channel_id=1, source_target_pairs={{0,17},{17,0},{1,16},{16,1},{2,19},{19,2},{3,18},{18,3},{4,21},{21... | collective-permute-start | bytes 61448 | tf_op jit(solution)/shard_map/ppermute | solution.py:739
  6.7 3.9 %collective-permute-start.3 = (bf16[64,128]{1,0:T(8,128)(2,1)}, bf16[64,128]{1,0:T(8,128)(2,1)S(1)}, u32[]{:S(2)}, u32[]{:S(2)}) collective-permute-start(bf16[64,128]{1,0:T(8,128)(2,1)} %get-tuple-element.35), channel_id=1, source_target_pairs={{0,16},{16,0},{1,17},{17,1},{2,18},{18,2},{3,19},{19,3},{4,20},{20... | collective-permute-start | bytes 49160 | tf_op jit(solution)/shard_map/ppermute | solution.py:737
  8.3 8.0 %collective-permute-start.2 = (bf16[32,1024]{1,0:T(8,128)(2,1)}, bf16[32,1024]{1,0:T(8,128)(2,1)S(1)}, u32[]{:S(2)}, u32[]{:S(2)}) collective-permute-start(bf16[32,1024]{1,0:T(8,128)(2,1)} %get-tuple-element.33), channel_id=1, source_target_pairs={{16,17},{17,16},{18,19},{19,18},{0,8},{8,0},{1,9},{9,1},{2,10},{10... | collective-permute-start | bytes 196616 | tf_op jit(solution)/shard_map/ppermute | solution.py:772
  9.8 6.5 %collective-permute-start = (bf16[80,1024]{1,0:T(8,128)(2,1)}, bf16[80,1024]{1,0:T(8,128)(2,1)S(1)}, u32[]{:S(2)}, u32[]{:S(2)}) collective-permute-start(bf16[80,1024]{1,0:T(8,128)(2,1)} %get-tuple-element.31), channel_id=1, source_target_pairs={{0,4},{4,0},{8,12},{12,8},{1,5},{5,1},{9,13},{13,9},{2,6},{6,2},{1... | collective-permute-start | bytes 491528 | tf_op jit(solution)/shard_map/ppermute | solution.py:769
  9.8 6.5 %collective-permute-start.1 = (bf16[80,1024]{1,0:T(8,128)(2,1)}, bf16[80,1024]{1,0:T(8,128)(2,1)S(1)}, u32[]{:S(2)}, u32[]{:S(2)}) collective-permute-start(bf16[80,1024]{1,0:T(8,128)(2,1)} %get-tuple-element.32), channel_id=1, source_target_pairs={{4,8},{8,4},{12,0},{0,12},{5,9},{9,5},{13,1},{1,13},{6,10},{10,6},... | collective-permute-start | bytes 491528 | tf_op jit(solution)/shard_map/ppermute | solution.py:770
  11.3 10.8 %collective-permute-start.5 = (bf16[32,1024]{1,0:T(8,128)(2,1)}, bf16[32,1024]{1,0:T(8,128)(2,1)S(1)}, u32[]{:S(2)}, u32[]{:S(2)}) collective-permute-start(bf16[32,1024]{1,0:T(8,128)(2,1)} %get-tuple-element.38), channel_id=1, source_target_pairs={{17,18},{18,17},{16,20},{20,16},{19,23},{23,19},{0,4},{4,0},{1,5},... | collective-permute-start | bytes 196616 | tf_op jit(solution)/shard_map/ppermute | solution.py:788
  11.4 4.8 %collective-permute-start.6 = (bf16[64,128]{1,0:T(8,128)(2,1)S(1)}, bf16[64,128]{1,0:T(8,128)(2,1)S(1)}, u32[]{:S(2)}, u32[]{:S(2)}) collective-permute-start(bf16[64,128]{1,0:T(8,128)(2,1)S(1)} %get-tuple-element.56._), channel_id=1, source_target_pairs={{0,2},{1,3},{2,0},{3,1},{4,6},{5,7},{6,4},{7,5},{8,10},{9,11},{10,... | collective-permute-start | bytes 49160 | tf_op jit(solution)/shard_map/ppermute | solution.py:746
  16.3 5.9 %copy-start = (f32[1,8,32,1024]{3,2,1,0:T(8,128)S(1)}, f32[1,8,32,1024]{3,2,1,0:T(8,128)}, u32[]{:S(2)}) copy-start(f32[1,8,32,1024]{3,2,1,0:T(8,128)} %x_ref.1) | copy-start | bytes 3145732
  16.3 5.9 %copy-start.3 = (f32[8,32,1024]{2,1,0:T(8,128)S(1)}, f32[8,32,1024]{2,1,0:T(8,128)}, u32[]{:S(2)}) copy-start(f32[8,32,1024]{2,1,0:T(8,128)} %get-tuple-element.30.y_ref) | copy-start | bytes 3145732
  16.3 5.9 %copy-start.5 = (s32[8,1024]{1,0:T(8,128)S(1)}, s32[8,1024]{1,0:T(8,128)}, u32[]{:S(2)}) copy-start(s32[8,1024]{1,0:T(8,128)} %wet_ref.1) | copy-start | bytes 98308
  16.3 5.9 %copy-start.10 = (f32[128]{0:T(128)S(1)}, f32[128]{0:T(128)}, u32[]{:S(2)}) copy-start(f32[128]{0:T(128)} %param.19) | copy-start | bytes 1540
  17.7 9.5 %copy-start.4 = (bf16[1024,512]{1,0:T(8,128)(2,1)S(1)}, bf16[1024,512]{1,0:T(8,128)(2,1)}, u32[]{:S(2)}) copy-start(bf16[1024,512]{1,0:T(8,128)(2,1)} %constant.5.clone.table_ref) | copy-start | bytes 3145732
  17.7 9.5 %copy-start.11 = (f32[128]{0:T(128)S(1)}, f32[128]{0:T(128)}, u32[]{:S(2)}) copy-start(f32[128]{0:T(128)} %param.18) | copy-start | bytes 1540
  17.7 7.8 %collective-permute-start.9 = (bf16[96,128]{1,0:T(8,128)(2,1)S(1)}, bf16[96,128]{1,0:T(8,128)(2,1)S(1)}, u32[]{:S(2)}, u32[]{:S(2)}) collective-permute-start(bf16[96,128]{1,0:T(8,128)(2,1)S(1)} %get-tuple-element.51), channel_id=1, source_target_pairs={{0,3},{1,2},{2,1},{3,0},{4,7},{5,6},{6,5},{7,4},{8,11},{9,10},{10,... | collective-permute-start | bytes 73736 | tf_op jit(solution)/shard_map/ppermute | solution.py:808
  20.8 4.7 %collective-permute-start.8 = (bf16[80,128]{1,0:T(8,128)(2,1)S(1)}, bf16[80,128]{1,0:T(8,128)(2,1)S(1)}, u32[]{:S(2)}, u32[]{:S(2)}) collective-permute-start(bf16[80,128]{1,0:T(8,128)(2,1)S(1)} %get-tuple-element.50), channel_id=1, source_target_pairs={{0,2},{1,3},{2,0},{3,1},{4,6},{5,7},{6,4},{7,5},{8,10},{9,11},{10,... | collective-permute-start | bytes 61448 | tf_op jit(solution)/shard_map/ppermute | solution.py:808
  20.8 3.7 %collective-permute-start.7 = (bf16[64,128]{1,0:T(8,128)(2,1)S(1)}, bf16[64,128]{1,0:T(8,128)(2,1)S(1)}, u32[]{:S(2)}, u32[]{:S(2)}) collective-permute-start(bf16[64,128]{1,0:T(8,128)(2,1)S(1)} %get-tuple-element.49), channel_id=1, source_target_pairs={{0,1},{1,0},{2,3},{3,2},{4,5},{5,4},{6,7},{7,6},{8,9},{9,8},{10,11... | collective-permute-start | bytes 49160 | tf_op jit(solution)/shard_map/ppermute | solution.py:808
  25.5 2.1 %collective-permute-start.10 = (bf16[128,128]{1,0:T(8,128)(2,1)S(1)}, bf16[128,128]{1,0:T(8,128)(2,1)S(1)}, u32[]{:S(2)}, u32[]{:S(2)}) collective-permute-start(bf16[128,128]{1,0:T(8,128)(2,1)S(1)} %get-tuple-element.53), channel_id=1, source_target_pairs={{0,4},{4,0},{8,12},{12,8},{1,5},{5,1},{9,13},{13,9},{2,6},{6,2},{1... | collective-permute-start | bytes 98312 | tf_op jit(solution)/shard_map/ppermute | solution.py:859
  25.6 3.4 %collective-permute-start.11 = (bf16[128,128]{1,0:T(8,128)(2,1)S(1)}, bf16[128,128]{1,0:T(8,128)(2,1)S(1)}, u32[]{:S(2)}, u32[]{:S(2)}) collective-permute-start(bf16[128,128]{1,0:T(8,128)(2,1)S(1)} %get-tuple-element.54), channel_id=1, source_target_pairs={{4,8},{8,4},{12,0},{0,12},{5,9},{9,5},{13,1},{1,13},{6,10},{10,6},... | collective-permute-start | bytes 98312 | tf_op jit(solution)/shard_map/ppermute | solution.py:860

commit v15 on v13

--- a/solution.py
+++ b/solution.py
@@ -245,7 +245,7 @@
                     at = (r * 2 + t) * 2
                     c = t * levels + level
                     edge_ref[at : at + 2, :] = x_ref[r, c : c + 2, :]
-            out[...] = edge_ref[...].astype(bf16)
+            out[0 : rows * 4, :] = edge_ref[...].astype(bf16)
 
         @pl.when(even_y)
         def _():
@@ -384,13 +384,13 @@
         high = jnp.where(even_y, one, two)
         at = row * 4 - start
         lines = [low[at + 1 : at + 2], low[at + 3 : at + 4], high[at : at + 1], high[at + 2 : at + 3]]
-        return to_tiles(jnp.concatenate(lines + [jnp.zeros((4, columns), f32)], axis=0))
+        heat = from_tiles(total, rows)[row : row + 1]
+        blank = jnp.zeros((3, columns), f32)
+        return to_tiles(jnp.concatenate([heat] + lines + [blank], axis=0))
 
     first, last = corners(0), corners(rows - 1)
-    near_ref[0:cells, :] = total.astype(bf16)
-    far_ref[0:cells, :] = total.astype(bf16)
-    near_ref[cells:, :] = jnp.where(even_x, last, first).astype(bf16)
-    far_ref[cells:, :] = jnp.where(even_x, first, last).astype(bf16)
+    near_ref[...] = jnp.where(even_x, last, first).astype(bf16)
+    far_ref[...] = jnp.where(even_x, first, last).astype(bf16)
 
 
 def advance(ref, r, t, coefs, size):
@@ -503,7 +503,7 @@
                 t0_ref[k, t, levels:ring, :] = blank
                 t0_ref[rows + 2 + k, t, levels:ring, :] = blank
         one = e2_ref[...].astype(f32)
-        two = e4_ref[...].astype(f32)
+        two = e4_ref[0 : 4 * rows, :].astype(f32)
         before = jnp.where(even_y, two, one)
         after = jnp.where(even_y, one, two)
         for r in range(rows):
@@ -595,13 +595,12 @@
     @pl.when(jnp.logical_not(is_atmos))
     def _():
         levels = channels // 2
-        cells = sum_ref.shape[0]
         even = row_group % 2 == 0
         below = jnp.where(even, far_ref[...].astype(f32), near_ref[...].astype(f32))
         above = jnp.where(even, near_ref[...].astype(f32), far_ref[...].astype(f32))
 
-        low = from_tiles(below[cells:], 8)
-        high = from_tiles(above[cells:], 8)
+        low = from_tiles(below, 8)
+        high = from_tiles(above, 8)
         by_low = c_ref[1, 1:2, :] * (c_ref[5, 0:1, :] + c_ref[5, 1:2, :])
         by_high = c_ref[2, rows : rows + 1, :] * (
             c_ref[5, rows : rows + 1, :] + c_ref[5, rows + 1 : rows + 2, :]
@@ -612,9 +611,9 @@
         @pl.when(col_group == 0)
         def _():
             span = rows + 2
-            e_ref[0:1, :] = from_tiles(below[:cells], rows)[rows - 1 : rows]
+            e_ref[0:1, :] = low[0:1]
             e_ref[1 : rows + 1, :] = from_tiles(sum_ref[...], rows)
-            e_ref[rows + 1 : span, :] = from_tiles(above[:cells], rows)[0:1]
+            e_ref[rows + 1 : span, :] = high[0:1]
             e_ref[0:span, :] = c_ref[6, 0:span, :] * e_ref[0:span, :]
             own = slice(1, rows + 1)
             heat = e_ref[own, :]
@@ -634,11 +633,11 @@
                 for edge, factor, lines in ((0, by_low, low), (rows - 1, by_high, high)):
                     if r == edge:
                         out_ref[r, c : c + 1, :] = out_ref[r, c : c + 1, :] + (
-                            has_before * factor * lines[t : t + 1]
+                            has_before * factor * lines[t + 1 : t + 2]
                         )
                         d = c + levels - 1
                         out_ref[r, d : d + 1, :] = out_ref[r, d : d + 1, :] + (
-                            has_after * factor * lines[t + 2 : t + 3]
+                            has_after * factor * lines[t + 3 : t + 4]
                         )
 
             @pl.when(col_group == 0)
@@ -698,7 +697,7 @@
         shape((lines, columns), bf16),
         shape((lines, columns), bf16),
         shape((4 * rows, columns), bf16),
-        shape((4 * rows, columns), bf16),
+        shape((4 * rows + 16, columns), bf16),
     ]
     if not paired:
         shapes.append(shape((2, channels, columns), bf16))
@@ -803,8 +802,25 @@
         *surfaces, *one_hots, a2o_count, marine_air_piece_tally,
         a2o_weight, marine_air_piece_factor, e1, e3, e2, e4,
     )
+
+    def landing_route(mask):
+        pairs = [
+            (flat(0, i, j), flat(0, i, j ^ mask))
+            for i in range(groups_x)
+            for j in range(groups_y)
+            if j < j ^ mask
+        ]
+        pairs += [(flat(1, i, 0), flat(1, i, mask)) for i in range(groups_x)]
+        pairs += [
+            (flat(1, i, j), flat(1, i + 1, j))
+            for i in range(0, groups_x, 2)
+            for j in range(groups_y)
+            if j not in (0, mask)
+        ]
+        return both_ways(pairs)
+
     parts = [
-        lax.ppermute(block, "gy", sum_route(mask)) for mask, block in enumerate(sent, 1)
+        lax.ppermute(block, axes, landing_route(mask)) for mask, block in enumerate(sent, 1)
     ]
 
     extra = []
@@ -846,8 +862,8 @@
         functools.partial(heat_kernel, rows),
         out_shape=[
             shape((cells, LANES), f32),
-            shape((cells + columns // 16, LANES), bf16),
-            shape((cells + columns // 16, LANES), bf16),
+            shape((columns // 16, LANES), bf16),
+            shape((columns // 16, LANES), bf16),
         ],
         in_specs=[vmem] * 3 + [anywhere] + [vmem] * len(parts),
         out_specs=[vmem] * 3,

time: 30.1 us -> 29.9 us (level)
  no operation moved by 1% of the time
where the time goes in v15:
time: 29.9 us; the launch traced here: 29.7 us
  starting transfers between devices  15.5 us (52%)
  Pallas kernels  8.16 us (27%)
  waiting for transfers between devices  4.51 us (15%)
  between operations  1.49 us (5%)
    ppermute x3, starting transfers between devices, local(): lax.ppermute(block, axes, landing_route(mask))  4.45 us
    pallas_call x1, Pallas kernels, local(): pl.pallas_call(functools.partial(start_kernel, groups_x, paired), out_sha...  3.69 us
    ppermute x1, starting transfers between devices, local(): far = lax.ppermute(wide, ('comp', 'gy'), partner_route(mask))  3 us
    ppermute x1, starting transfers between devices, local(): lax.ppermute(coarse, 'gy', sum_route(mask))  2.65 us
    ppermute x3, waiting for transfers between devices, local(): lax.ppermute(block, axes, landing_route(mask))  2 us
    ppermute x1, starting transfers between devices, local(): e3 = lax.ppermute(e3, 'gx', both_ways(ring_pairs(groups_x, 1)))  1.6 us
    ppermute x1, starting transfers between devices, local(): far = lax.ppermute(far, 'gx', both_ways(ring_pairs(groups_x, 1)))  1.6 us
    ppermute x1, starting transfers between devices, local(): surface = lax.ppermute(coarse, ('comp', 'gy'), partner_route(0)).astype(f32)  1.59 us
  transfers between devices with their start and end apart: 12, of which 6 were waited for; matrix products, arithmetic and copies ran while one was open for 0% of the time, Pallas kernels for 7%

profile of v15, /device:TPU:0, one launch (start us, length us, event | category | flops | bytes accessed | tf_op | source)
XLA Modules:
  0.0 29.7 jit_solution(3770092091197940819)
XLA Ops:
  0.0 0.0 copy-start.6
  0.0 0.0 copy-start.7
  0.0 0.0 copy-start.8
  0.0 0.0 copy-start.9
  0.0 0.0 copy-start.2
  0.0 0.0 copy-start.3
  0.0 3.7 %surface_and_forward_or_halos.1 = (bf16[64,128]{1,0:T(8,128)(2,1)}, bf16[80,128]{1,0:T(8,128)(2,1)}, f32[8,32,1024]{2,1,0:T(8,128)}, bf16[80,1024]{1,0:T(8,128)(...) custom-call(f32[1,8,32,1024]{3,2,1,0:T(8,128)} %x_ref.1, s32[8,1024]{1,0:T(8,128)} %wet_ref.1, ...), custom_call_target="tpu_custom_call" | custom-call | tf_op jit(solution)/shard_map/surface_and_forward_or_halos/pallas_call | solution.py:704
  3.7 3.0 %collective-permute-start.5 = (bf16[80,128]{1,0:T(8,128)(2,1)}, bf16[80,128]{1,0:T(8,128)(2,1)S(1)}, u32[]{:S(2)}, u32[]{:S(2)}) collective-permute-start(bf16[80,128]{1,0:T(8,128)(2,1)} %get-tuple-element.39), channel_id=1, source_target_pairs={{0,17},{17,0},{1,16},{16,1},{2,19},{19,2},{3,18},{18,3},{4,21},{21... | collective-permute-start | bytes 61448 | tf_op jit(solution)/shard_map/ppermute | solution.py:738
  6.7 1.6 %collective-permute-start.4 = (bf16[64,128]{1,0:T(8,128)(2,1)}, bf16[64,128]{1,0:T(8,128)(2,1)S(1)}, u32[]{:S(2)}, u32[]{:S(2)}) collective-permute-start(bf16[64,128]{1,0:T(8,128)(2,1)} %get-tuple-element.38), channel_id=1, source_target_pairs={{0,16},{16,0},{1,17},{17,1},{2,18},{18,2},{3,19},{19,3},{4,20},{20... | collective-permute-start | bytes 49160 | tf_op jit(solution)/shard_map/ppermute | solution.py:736
  8.3 0.0 collective-permute-start
  8.3 1.6 %collective-permute-start.1 = (bf16[80,1024]{1,0:T(8,128)(2,1)}, bf16[80,1024]{1,0:T(8,128)(2,1)S(1)}, u32[]{:S(2)}, u32[]{:S(2)}) collective-permute-start(bf16[80,1024]{1,0:T(8,128)(2,1)} %get-tuple-element.30), channel_id=1, source_target_pairs={{4,8},{8,4},{12,0},{0,12},{5,9},{9,5},{13,1},{1,13},{6,10},{10,6},... | collective-permute-start | bytes 491528 | tf_op jit(solution)/shard_map/ppermute | solution.py:769
  9.9 0.5 %collective-permute-start.2 = (bf16[32,1024]{1,0:T(8,128)(2,1)}, bf16[32,1024]{1,0:T(8,128)(2,1)S(1)}, u32[]{:S(2)}, u32[]{:S(2)}) collective-permute-start(bf16[32,1024]{1,0:T(8,128)(2,1)} %get-tuple-element.31), channel_id=1, source_target_pairs={{16,17},{17,16},{18,19},{19,18},{0,8},{8,0},{1,9},{9,1},{2,10},{10... | collective-permute-start | bytes 196616 | tf_op jit(solution)/shard_map/ppermute | solution.py:771
  10.5 0.2 collective-permute-done.4
  10.7 0.0 collective-permute-start.3
  10.7 0.0 collective-permute-done.5
  10.7 2.7 %collective-permute-start.6 = (bf16[64,128]{1,0:T(8,128)(2,1)S(1)}, bf16[64,128]{1,0:T(8,128)(2,1)S(1)}, u32[]{:S(2)}, u32[]{:S(2)}) collective-permute-start(bf16[64,128]{1,0:T(8,128)(2,1)S(1)} %get-tuple-element.51._), channel_id=1, source_target_pairs={{0,2},{1,3},{2,0},{3,1},{4,6},{5,7},{6,4},{7,5},{8,10},{9,11},{10,... | collective-permute-start | bytes 49160 | tf_op jit(solution)/shard_map/ppermute | solution.py:745
  14.6 0.0 copy-done.6
  14.7 0.0 copy-done.7
  14.7 0.0 copy-done.8
  14.7 0.0 copy-done.9
  14.7 0.6 %one_hots.1 = (bf16[128,4096]{1,0:T(8,128)(2,1)S(1)}, bf16[128,4096]{1,0:T(8,128)(2,1)S(1)}, s32[32,128]{1,0:T(8,128)S(1)}, s32[32,128]{1,0:T(8,128)S(1)}) custom-call(s32[1,1,32,128]{3,2,1,0:T(8,128)S(1)} %copy-done.6, s32[1,1,32,128]{3,2,1,0:T(8,128)S(1)} %copy-done.7, s32[1,1,32,128]{3,2,1,0:T(8,128)S(1)} %copy-done.8, s32[1,1,32,128]{3,2,1,0:T(8,128)S(1)} %copy-done.9, ...), custom_call_target="tpu_custom_call" | custom-call | tf_op jit(solution)/shard_map/one_hots/pallas_call | solution.py:774
  15.3 0.1 collective-permute-done.6.refs_1_
  15.4 1.0 %collective-permute-done.2.e2_ref.refs_12_ = bf16[32,1024]{1,0:T(8,128)(2,1)S(1)} collective-permute-done((bf16[32,1024]{1,0:T(8,128)(2,1)}, bf16[32,1024]{1,0:T(8,128)(2,1)S(1)}, u32[]{:S(2)}, u32[]{:S(2)}) %collective-permute-start.2) | collective-permute-done | bytes 65568 | tf_op jit(solution)/shard_map/ppermute | solution.py:771
  16.4 0.0 collective-permute-done.3.e4_ref.refs_13_
  16.4 0.0 collective-permute-done.e1_ref.refs_10_
  16.4 0.0 collective-permute-done.1.e3_ref.refs_11_
  16.4 0.0 copy-done.2
  16.4 0.0 copy-done.3
  16.5 0.0 copy-start
  16.5 0.0 copy-start.1
  16.5 0.0 copy-start.5
  16.5 0.0 copy-start.10
  16.5 1.4 %regrid_blocks.1 = (f32[64,128]{1,0:T(8,128)S(1)}, bf16[64,128]{1,0:T(8,128)(2,1)S(1)}, bf16[80,128]{1,0:T(8,128)(2,1)S(1)}, bf16[96,128]{1,0:T(8,128)(2,1)S(1)}) custom-call(f32[64,128]{1,0:T(8,128)S(1)} %get-tuple-element.52.refs_0_, bf16[64,128]{1,0:T(8,128)(2,1)S(1)} %collective-permute-done.6.refs_1_, bf16[128,4096]{1,0:T(8,128)(2,1)S(1)} %get-tuple-element.40.refs_2_, ...), custom_call_target="tpu_custom_call" | custom-call | tf_op jit(solution)/shard_map/regrid_blocks/pallas_call | solution.py:787
  17.9 0.0 copy-start.4
  17.9 0.0 copy-start.11
  17.9 2.5 %collective-permute-start.9 = (bf16[96,128]{1,0:T(8,128)(2,1)S(1)}, bf16[96,128]{1,0:T(8,128)(2,1)S(1)}, u32[]{:S(2)}, u32[]{:S(2)}) collective-permute-start(bf16[96,128]{1,0:T(8,128)(2,1)S(1)} %get-tuple-element.47), channel_id=1, source_target_pairs={{0,3},{3,0},{1,2},{2,1},{4,7},{7,4},{5,6},{6,5},{8,11},{11,8},{9,1... | collective-permute-start | bytes 73736 | tf_op jit(solution)/shard_map/ppermute | solution.py:823
  20.4 0.2 collective-permute-start.8
  20.6 1.7 %collective-permute-start.7 = (bf16[64,128]{1,0:T(8,128)(2,1)S(1)}, bf16[64,128]{1,0:T(8,128)(2,1)S(1)}, u32[]{:S(2)}, u32[]{:S(2)}) collective-permute-start(bf16[64,128]{1,0:T(8,128)(2,1)S(1)} %get-tuple-element.45), channel_id=1, source_target_pairs={{0,1},{1,0},{2,3},{3,2},{4,5},{5,4},{6,7},{7,6},{8,9},{9,8},{10,11... | collective-permute-start | bytes 49160 | tf_op jit(solution)/shard_map/ppermute | solution.py:823
  22.3 0.0 copy-done
  22.4 0.0 copy-done.1
  22.4 0.0 copy-done.5
  22.4 0.0 copy-done.10
  22.4 1.0 %damping_or_first_step.1 = (bf16[256,1024]{1,0:T(8,128)(2,1)S(1)}, f32[7,16,1024]{2,1,0:T(8,128)S(1)}, f32[10,2,24,1024]{3,2,1,0:T(8,128)S(1)}) custom-call(f32[1,8,32,1024]{3,2,1,0:T(8,128)S(1)} %copy-done, s32[8,1024]{1,0:T(8,128)S(1)} %copy-done.5, f32[1,128]{1,0:T(1,128)S(1)} %bitcast.4, f32[8,32,1024]{2,1,0:T(8,128)S(1)} %copy-done.1, ...), custom_call_target="tpu_custom_call" | custom-call | tf_op jit(solution)/shard_map/damping_or_first_step/pallas_call | solution.py:843
  23.3 1.0 %collective-permute-done.7.refs_0_ = bf16[64,128]{1,0:T(8,128)(2,1)S(1)} collective-permute-done((bf16[64,128]{1,0:T(8,128)(2,1)S(1)}, bf16[64,128]{1,0:T(8,128)(2,1)S(1)}, u32[]{:S(2)}, u32[]{:S(2)}) %collective-permute-start.7) | collective-permute-done | bytes 16416 | tf_op jit(solution)/shard_map/ppermute | solution.py:823
  24.4 1.0 %collective-permute-done.8.refs_1_ = bf16[80,128]{1,0:T(8,128)(2,1)S(1)} collective-permute-done((bf16[80,128]{1,0:T(8,128)(2,1)S(1)}, bf16[80,128]{1,0:T(8,128)(2,1)S(1)}, u32[]{:S(2)}, u32[]{:S(2)}) %collective-permute-start.8) | collective-permute-done | bytes 20512 | tf_op jit(solution)/shard_map/ppermute | solution.py:823
  25.3 0.0 collective-permute-done.9.refs_2_
  25.4 0.1 collective-permute-start.10
  25.5 1.6 %collective-permute-start.11 = (bf16[64,128]{1,0:T(8,128)(2,1)S(1)}, bf16[64,128]{1,0:T(8,128)(2,1)S(1)}, u32[]{:S(2)}, u32[]{:S(2)}) collective-permute-start(bf16[64,128]{1,0:T(8,128)(2,1)S(1)} %get-tuple-element.50), channel_id=1, source_target_pairs={{4,8},{8,4},{12,0},{0,12},{5,9},{9,5},{13,1},{1,13},{6,10},{10,6},... | collective-permute-start | bytes 49160 | tf_op jit(solution)/shard_map/ppermute | solution.py:875
  27.1 0.0 copy-done.4
  27.1 0.0 copy-done.11
  27.1 0.4 %inverse_or_second_step.1 = (f32[8,32,1024]{2,1,0:T(8,128)S(1)}, f32[32,128]{1,0:T(8,128)S(1)}) custom-call(f32[1,128]{1,0:T(1,128)S(1)} %bitcast.5, bf16[1024,512]{1,0:T(8,128)(2,1)S(1)} %copy-done.4, bf16[256,1024]{1,0:T(8,128)(2,1)S(1)} %get-tuple-element.33.zb_ref, f32[7,16,1024]{2,1,0:T(8,128)S(1)} %get-tuple-element.34.c_ref._, ...), custom_call_target="tpu_custom_call" | custom-call | tf_op jit(solution)/shard_map/inverse_or_second_step/pallas_call | solution.py:876
  27.5 0.0 collective-permute-done.10.near_ref
  27.5 1.2 %collective-permute-done.11.far_ref = bf16[64,128]{1,0:T(8,128)(2,1)S(1)} collective-permute-done((bf16[64,128]{1,0:T(8,128)(2,1)S(1)}, bf16[64,128]{1,0:T(8,128)(2,1)S(1)}, u32[]{:S(2)}, u32[]{:S(2)}) %collective-permute-start.11) | collective-permute-done | bytes 16416 | tf_op jit(solution)/shard_map/ppermute | solution.py:875
  28.7 1.0 %add_surface_terms.1 = f32[1,8,32,1024]{3,2,1,0:T(8,128)} custom-call(f32[32,128]{1,0:T(8,128)S(1)} %get-tuple-element.36.column_ref, f32[8,32,1024]{2,1,0:T(8,128)S(1)} %get-tuple-element.37.base_ref, f32[7,16,1024]{2,1,0:T(8,128)S(1)} %get-tuple-element.34.c_ref._, f32[64,128]{1,0:T(8,128)S(1)} %get-tuple-element.48.sum_ref, ...), custom_call_target="tpu_custom_call" | custom-call | tf_op jit(solution)/shard_map/add_surface_terms/pallas_call | solution.py:884
  (2 shorter events, 0.1 us)
Async XLA Ops:
  0.0 14.6 %copy-start.6 = (s32[1,1,32,128]{3,2,1,0:T(8,128)S(1)}, s32[1,1,32,128]{3,2,1,0:T(8,128)}, u32[]{:S(2)}) copy-start(s32[1,1,32,128]{3,2,1,0:T(8,128)} %a_src.1) | copy-start | bytes 49156
  0.0 14.7 %copy-start.7 = (s32[1,1,32,128]{3,2,1,0:T(8,128)S(1)}, s32[1,1,32,128]{3,2,1,0:T(8,128)}, u32[]{:S(2)}) copy-start(s32[1,1,32,128]{3,2,1,0:T(8,128)} %a_dst.1) | copy-start | bytes 49156
  0.0 14.7 %copy-start.8 = (s32[1,1,32,128]{3,2,1,0:T(8,128)S(1)}, s32[1,1,32,128]{3,2,1,0:T(8,128)}, u32[]{:S(2)}) copy-start(s32[1,1,32,128]{3,2,1,0:T(8,128)} %m_src.1) | copy-start | bytes 49156
  0.0 14.7 %copy-start.9 = (s32[1,1,32,128]{3,2,1,0:T(8,128)S(1)}, s32[1,1,32,128]{3,2,1,0:T(8,128)}, u32[]{:S(2)}) copy-start(s32[1,1,32,128]{3,2,1,0:T(8,128)} %m_dst.1) | copy-start | bytes 49156
  0.0 16.4 %copy-start.2 = (bf16[1,1,32,128,128]{4,3,2,1,0:T(8,128)(2,1)S(1)}, bf16[1,1,32,128,128]{4,3,2,1,0:T(8,128)(2,1)}, u32[]{:S(2)}) copy-start(bf16[1,1,32,128,128]{4,3,2,1,0:T(8,128)(2,1)} %refs_8_.1) | copy-start | bytes 3145732
  0.0 16.4 %copy-start.3 = (bf16[1,1,32,128,128]{4,3,2,1,0:T(8,128)(2,1)S(1)}, bf16[1,1,32,128,128]{4,3,2,1,0:T(8,128)(2,1)}, u32[]{:S(2)}) copy-start(bf16[1,1,32,128,128]{4,3,2,1,0:T(8,128)(2,1)} %refs_9_.1) | copy-start | bytes 3145732
  3.7 7.0 %collective-permute-start.5 = (bf16[80,128]{1,0:T(8,128)(2,1)}, bf16[80,128]{1,0:T(8,128)(2,1)S(1)}, u32[]{:S(2)}, u32[]{:S(2)}) collective-permute-start(bf16[80,128]{1,0:T(8,128)(2,1)} %get-tuple-element.39), channel_id=1, source_target_pairs={{0,17},{17,0},{1,16},{16,1},{2,19},{19,2},{3,18},{18,3},{4,21},{21... | collective-permute-start | bytes 61448 | tf_op jit(solution)/shard_map/ppermute | solution.py:738
  6.7 3.9 %collective-permute-start.4 = (bf16[64,128]{1,0:T(8,128)(2,1)}, bf16[64,128]{1,0:T(8,128)(2,1)S(1)}, u32[]{:S(2)}, u32[]{:S(2)}) collective-permute-start(bf16[64,128]{1,0:T(8,128)(2,1)} %get-tuple-element.38), channel_id=1, source_target_pairs={{0,16},{16,0},{1,17},{17,1},{2,18},{18,2},{3,19},{19,3},{4,20},{20... | collective-permute-start | bytes 49160 | tf_op jit(solution)/shard_map/ppermute | solution.py:736
  8.3 8.1 %collective-permute-start = (bf16[80,1024]{1,0:T(8,128)(2,1)}, bf16[80,1024]{1,0:T(8,128)(2,1)S(1)}, u32[]{:S(2)}, u32[]{:S(2)}) collective-permute-start(bf16[80,1024]{1,0:T(8,128)(2,1)} %get-tuple-element.29), channel_id=1, source_target_pairs={{0,4},{4,0},{8,12},{12,8},{1,5},{5,1},{9,13},{13,9},{2,6},{6,2},{1... | collective-permute-start | bytes 491528 | tf_op jit(solution)/shard_map/ppermute | solution.py:768
  8.3 8.1 %collective-permute-start.1 = (bf16[80,1024]{1,0:T(8,128)(2,1)}, bf16[80,1024]{1,0:T(8,128)(2,1)S(1)}, u32[]{:S(2)}, u32[]{:S(2)}) collective-permute-start(bf16[80,1024]{1,0:T(8,128)(2,1)} %get-tuple-element.30), channel_id=1, source_target_pairs={{4,8},{8,4},{12,0},{0,12},{5,9},{9,5},{13,1},{1,13},{6,10},{10,6},... | collective-permute-start | bytes 491528 | tf_op jit(solution)/shard_map/ppermute | solution.py:769
  9.9 6.5 %collective-permute-start.2 = (bf16[32,1024]{1,0:T(8,128)(2,1)}, bf16[32,1024]{1,0:T(8,128)(2,1)S(1)}, u32[]{:S(2)}, u32[]{:S(2)}) collective-permute-start(bf16[32,1024]{1,0:T(8,128)(2,1)} %get-tuple-element.31), channel_id=1, source_target_pairs={{16,17},{17,16},{18,19},{19,18},{0,8},{8,0},{1,9},{9,1},{2,10},{10... | collective-permute-start | bytes 196616 | tf_op jit(solution)/shard_map/ppermute | solution.py:771
  10.7 5.8 %collective-permute-start.3 = (bf16[48,1024]{1,0:T(8,128)(2,1)}, bf16[48,1024]{1,0:T(8,128)(2,1)S(1)}, u32[]{:S(2)}, u32[]{:S(2)}) collective-permute-start(bf16[48,1024]{1,0:T(8,128)(2,1)} %get-tuple-element.32), channel_id=1, source_target_pairs={{17,18},{18,17},{16,20},{20,16},{19,23},{23,19},{0,4},{4,0},{1,5},... | collective-permute-start | bytes 294920 | tf_op jit(solution)/shard_map/ppermute | solution.py:772
  10.7 4.7 %collective-permute-start.6 = (bf16[64,128]{1,0:T(8,128)(2,1)S(1)}, bf16[64,128]{1,0:T(8,128)(2,1)S(1)}, u32[]{:S(2)}, u32[]{:S(2)}) collective-permute-start(bf16[64,128]{1,0:T(8,128)(2,1)S(1)} %get-tuple-element.51._), channel_id=1, source_target_pairs={{0,2},{1,3},{2,0},{3,1},{4,6},{5,7},{6,4},{7,5},{8,10},{9,11},{10,... | collective-permute-start | bytes 49160 | tf_op jit(solution)/shard_map/ppermute | solution.py:745
  16.5 5.9 %copy-start = (f32[1,8,32,1024]{3,2,1,0:T(8,128)S(1)}, f32[1,8,32,1024]{3,2,1,0:T(8,128)}, u32[]{:S(2)}) copy-start(f32[1,8,32,1024]{3,2,1,0:T(8,128)} %x_ref.1) | copy-start | bytes 3145732
  16.5 5.9 %copy-start.1 = (f32[8,32,1024]{2,1,0:T(8,128)S(1)}, f32[8,32,1024]{2,1,0:T(8,128)}, u32[]{:S(2)}) copy-start(f32[8,32,1024]{2,1,0:T(8,128)} %get-tuple-element.28.y_ref) | copy-start | bytes 3145732
  16.5 5.9 %copy-start.5 = (s32[8,1024]{1,0:T(8,128)S(1)}, s32[8,1024]{1,0:T(8,128)}, u32[]{:S(2)}) copy-start(s32[8,1024]{1,0:T(8,128)} %wet_ref.1) | copy-start | bytes 98308
  16.5 5.9 %copy-start.10 = (f32[128]{0:T(128)S(1)}, f32[128]{0:T(128)}, u32[]{:S(2)}) copy-start(f32[128]{0:T(128)} %param.19) | copy-start | bytes 1540
  17.9 9.2 %copy-start.4 = (bf16[1024,512]{1,0:T(8,128)(2,1)S(1)}, bf16[1024,512]{1,0:T(8,128)(2,1)}, u32[]{:S(2)}) copy-start(bf16[1024,512]{1,0:T(8,128)(2,1)} %constant.5.clone.table_ref) | copy-start | bytes 3145732
  17.9 9.2 %copy-start.11 = (f32[128]{0:T(128)S(1)}, f32[128]{0:T(128)}, u32[]{:S(2)}) copy-start(f32[128]{0:T(128)} %param.18) | copy-start | bytes 1540
  17.9 7.4 %collective-permute-start.9 = (bf16[96,128]{1,0:T(8,128)(2,1)S(1)}, bf16[96,128]{1,0:T(8,128)(2,1)S(1)}, u32[]{:S(2)}, u32[]{:S(2)}) collective-permute-start(bf16[96,128]{1,0:T(8,128)(2,1)S(1)} %get-tuple-element.47), channel_id=1, source_target_pairs={{0,3},{3,0},{1,2},{2,1},{4,7},{7,4},{5,6},{6,5},{8,11},{11,8},{9,1... | collective-permute-start | bytes 73736 | tf_op jit(solution)/shard_map/ppermute | solution.py:823
  20.4 4.9 %collective-permute-start.8 = (bf16[80,128]{1,0:T(8,128)(2,1)S(1)}, bf16[80,128]{1,0:T(8,128)(2,1)S(1)}, u32[]{:S(2)}, u32[]{:S(2)}) collective-permute-start(bf16[80,128]{1,0:T(8,128)(2,1)S(1)} %get-tuple-element.46), channel_id=1, source_target_pairs={{0,2},{2,0},{1,3},{3,1},{4,6},{6,4},{5,7},{7,5},{8,10},{10,8},{9,1... | collective-permute-start | bytes 61448 | tf_op jit(solution)/shard_map/ppermute | solution.py:823
  20.6 3.7 %collective-permute-start.7 = (bf16[64,128]{1,0:T(8,128)(2,1)S(1)}, bf16[64,128]{1,0:T(8,128)(2,1)S(1)}, u32[]{:S(2)}, u32[]{:S(2)}) collective-permute-start(bf16[64,128]{1,0:T(8,128)(2,1)S(1)} %get-tuple-element.45), channel_id=1, source_target_pairs={{0,1},{1,0},{2,3},{3,2},{4,5},{5,4},{6,7},{7,6},{8,9},{9,8},{10,11... | collective-permute-start | bytes 49160 | tf_op jit(solution)/shard_map/ppermute | solution.py:823
  25.4 2.1 %collective-permute-start.10 = (bf16[64,128]{1,0:T(8,128)(2,1)S(1)}, bf16[64,128]{1,0:T(8,128)(2,1)S(1)}, u32[]{:S(2)}, u32[]{:S(2)}) collective-permute-start(bf16[64,128]{1,0:T(8,128)(2,1)S(1)} %get-tuple-element.49), channel_id=1, source_target_pairs={{0,4},{4,0},{8,12},{12,8},{1,5},{5,1},{9,13},{13,9},{2,6},{6,2},{1... | collective-permute-start | bytes 49160 | tf_op jit(solution)/shard_map/ppermute | solution.py:874
  25.5 3.2 %collective-permute-start.11 = (bf16[64,128]{1,0:T(8,128)(2,1)S(1)}, bf16[64,128]{1,0:T(8,128)(2,1)S(1)}, u32[]{:S(2)}, u32[]{:S(2)}) collective-permute-start(bf16[64,128]{1,0:T(8,128)(2,1)S(1)} %get-tuple-element.50), channel_id=1, source_target_pairs={{4,8},{8,4},{12,0},{0,12},{5,9},{9,5},{13,1},{1,13},{6,10},{10,6},... | collective-permute-start | bytes 49160 | tf_op jit(solution)/shard_map/ppermute | solution.py:875

commit v16 on v15

--- a/solution.py
+++ b/solution.py
@@ -697,7 +697,7 @@
         shape((lines, columns), bf16),
         shape((lines, columns), bf16),
         shape((4 * rows, columns), bf16),
-        shape((4 * rows + 16, columns), bf16),
+        shape((4 * rows, columns), bf16),
     ]
     if not paired:
         shapes.append(shape((2, channels, columns), bf16))
@@ -765,6 +765,7 @@
                 pairs += [(flat(0, i, j), flat(0, i ^ 2, j)) for j in range(groups_y)]
         return both_ways(pairs)
 
+    e1, coarse = lax.optimization_barrier((e1, coarse))
     e1 = lax.ppermute(e1, "gx", both_ways(ring_pairs(groups_x, 0)))
     e3 = lax.ppermute(e3, "gx", both_ways(ring_pairs(groups_x, 1)))
     axes = ("comp", "gx", "gy")

time: 29.9 us -> 31 us (1.037)
  waiting for transfers between devices: 4.51 us -> 6.59 us
  starting transfers between devices: 15.5 us -> 14.5 us
    ppermute x1, waiting for transfers between devices: 0.22 us -> 2 us  [local(): surface = lax.ppermute(coarse, ('comp', 'gy'), partner_route(0)).astype(f32)]
    ppermute x1, starting transfers between devices: 1.6 us -> 0.37 us  [local(): e3 = lax.ppermute(e3, 'gx', both_ways(ring_pairs(groups_x, 1)))]
    ppermute x1, waiting for transfers between devices: 1.03 us -> 0.01 us  [local(): e2 = lax.ppermute(e2, axes, level_route(0))]
    ppermute x1, starting transfers between devices: 0.54 us -> 1.56 us  [local(): e2 = lax.ppermute(e2, axes, level_route(0))]
    ppermute x1, starting transfers between devices: 1.6 us -> 0.65 us  [local(): far = lax.ppermute(far, 'gx', both_ways(ring_pairs(groups_x, 1)))]
    ppermute x1, waiting for transfers between devices: 1.16 us -> 2.06 us  [local(): far = lax.ppermute(far, 'gx', both_ways(ring_pairs(groups_x, 1)))]
    ppermute x3, waiting for transfers between devices: 2 us -> 2.34 us  [local(): lax.ppermute(block, axes, landing_route(mask))]
where the time goes in v16:
time: 31 us; the launch traced here: 30.8 us
  starting transfers between devices  14.5 us (47%)
  Pallas kernels  8.14 us (26%)
  waiting for transfers between devices  6.59 us (21%)
  between operations  1.5 us (5%)
    ppermute x3, starting transfers between devices, local(): lax.ppermute(block, axes, landing_route(mask))  4.45 us
    pallas_call x1, Pallas kernels, local(): pl.pallas_call(functools.partial(start_kernel, groups_x, paired), out_sha...  3.67 us
    ppermute x1, starting transfers between devices, local(): far = lax.ppermute(wide, ('comp', 'gy'), partner_route(mask))  3 us
    ppermute x1, starting transfers between devices, local(): lax.ppermute(coarse, 'gy', sum_route(mask))  2.59 us
    ppermute x3, waiting for transfers between devices, local(): lax.ppermute(block, axes, landing_route(mask))  2.34 us
    ppermute x1, waiting for transfers between devices, local(): far = lax.ppermute(far, 'gx', both_ways(ring_pairs(groups_x, 1)))  2.06 us
    ppermute x1, waiting for transfers between devices, local(): surface = lax.ppermute(coarse, ('comp', 'gy'), partner_route(0)).astype(f32)  2 us
    ppermute x1, starting transfers between devices, local(): surface = lax.ppermute(coarse, ('comp', 'gy'), partner_route(0)).astype(f32)  1.58 us
  transfers between devices with their start and end apart: 12, of which 6 were waited for; matrix products, arithmetic and copies ran while one was open for 0% of the time, Pallas kernels for 7%

profile of v16, /device:TPU:0, one launch (start us, length us, event | category | flops | bytes accessed | tf_op | source)
XLA Modules:
  0.0 30.8 jit_solution(6526223136393350867)
XLA Ops:
  0.0 0.0 copy-start.6
  0.0 0.0 copy-start.7
  0.0 0.0 copy-start.8
  0.0 0.0 copy-start.9
  0.0 0.0 copy-start.2
  0.0 0.0 copy-start.3
  0.0 3.7 %surface_and_forward_or_halos.1 = (bf16[64,128]{1,0:T(8,128)(2,1)}, bf16[80,128]{1,0:T(8,128)(2,1)}, f32[8,32,1024]{2,1,0:T(8,128)}, bf16[80,1024]{1,0:T(8,128)(...) custom-call(f32[1,8,32,1024]{3,2,1,0:T(8,128)} %x_ref.1, s32[8,1024]{1,0:T(8,128)} %wet_ref.1, ...), custom_call_target="tpu_custom_call" | custom-call | tf_op jit(solution)/shard_map/surface_and_forward_or_halos/pallas_call | solution.py:704
  3.7 3.0 %collective-permute-start.1 = (bf16[80,128]{1,0:T(8,128)(2,1)}, bf16[80,128]{1,0:T(8,128)(2,1)S(1)}, u32[]{:S(2)}, u32[]{:S(2)}) collective-permute-start(bf16[80,128]{1,0:T(8,128)(2,1)} %get-tuple-element.33), channel_id=1, source_target_pairs={{0,17},{17,0},{1,16},{16,1},{2,19},{19,2},{3,18},{18,3},{4,21},{21... | collective-permute-start | bytes 61448 | tf_op jit(solution)/shard_map/ppermute | solution.py:738
  6.7 1.6 %collective-permute-start = (bf16[64,128]{1,0:T(8,128)(2,1)}, bf16[64,128]{1,0:T(8,128)(2,1)S(1)}, u32[]{:S(2)}, u32[]{:S(2)}) collective-permute-start(bf16[64,128]{1,0:T(8,128)(2,1)} %get-tuple-element.32), channel_id=1, source_target_pairs={{0,16},{16,0},{1,17},{17,1},{2,18},{18,2},{3,19},{19,3},{4,20},{20... | collective-permute-start | bytes 49160 | tf_op jit(solution)/shard_map/ppermute | solution.py:736
  8.3 0.4 %collective-permute-start.3 = (bf16[80,1024]{1,0:T(8,128)(2,1)}, bf16[80,1024]{1,0:T(8,128)(2,1)S(1)}, u32[]{:S(2)}, u32[]{:S(2)}) collective-permute-start(bf16[80,1024]{1,0:T(8,128)(2,1)} %get-tuple-element.35), channel_id=1, source_target_pairs={{4,8},{8,4},{12,0},{0,12},{5,9},{9,5},{13,1},{1,13},{6,10},{10,6},... | collective-permute-start | bytes 491528 | tf_op jit(solution)/shard_map/ppermute | solution.py:770
  8.7 2.0 %collective-permute-done = bf16[64,128]{1,0:T(8,128)(2,1)S(1)} collective-permute-done((bf16[64,128]{1,0:T(8,128)(2,1)}, bf16[64,128]{1,0:T(8,128)(2,1)S(1)}, u32[]{:S(2)}, u32[]{:S(2)}) %collective-permute-start) | collective-permute-done | bytes 16416 | tf_op jit(solution)/shard_map/ppermute | solution.py:736
  10.7 0.0 collective-permute-done.1
  10.7 0.1 collective-permute-start.2
  10.7 1.6 %collective-permute-start.4 = (bf16[32,1024]{1,0:T(8,128)(2,1)}, bf16[32,1024]{1,0:T(8,128)(2,1)S(1)}, u32[]{:S(2)}, u32[]{:S(2)}) collective-permute-start(bf16[32,1024]{1,0:T(8,128)(2,1)} %get-tuple-element.36), channel_id=1, source_target_pairs={{16,17},{17,16},{18,19},{19,18},{0,8},{8,0},{1,9},{9,1},{2,10},{10... | collective-permute-start | bytes 196616 | tf_op jit(solution)/shard_map/ppermute | solution.py:772
  12.3 0.2 collective-permute-start.5
  12.5 2.6 %collective-permute-start.6 = (bf16[64,128]{1,0:T(8,128)(2,1)S(1)}, bf16[64,128]{1,0:T(8,128)(2,1)S(1)}, u32[]{:S(2)}, u32[]{:S(2)}) collective-permute-start(bf16[64,128]{1,0:T(8,128)(2,1)S(1)} %get-tuple-element.43._), channel_id=1, source_target_pairs={{0,2},{1,3},{2,0},{3,1},{4,6},{5,7},{6,4},{7,5},{8,10},{9,11},{10,... | collective-permute-start | bytes 49160 | tf_op jit(solution)/shard_map/ppermute | solution.py:745
  16.4 0.0 copy-done.6
  16.4 0.0 copy-done.7
  16.4 0.0 copy-done.8
  16.4 0.0 copy-done.9
  16.4 0.6 %one_hots.1 = (bf16[128,4096]{1,0:T(8,128)(2,1)S(1)}, bf16[128,4096]{1,0:T(8,128)(2,1)S(1)}, s32[32,128]{1,0:T(8,128)S(1)}, s32[32,128]{1,0:T(8,128)S(1)}) custom-call(s32[1,1,32,128]{3,2,1,0:T(8,128)S(1)} %copy-done.6, s32[1,1,32,128]{3,2,1,0:T(8,128)S(1)} %copy-done.7, s32[1,1,32,128]{3,2,1,0:T(8,128)S(1)} %copy-done.8, s32[1,1,32,128]{3,2,1,0:T(8,128)S(1)} %copy-done.9, ...), custom_call_target="tpu_custom_call" | custom-call | tf_op jit(solution)/shard_map/one_hots/pallas_call | solution.py:775
  17.0 0.1 collective-permute-done.6.refs_1_
  17.1 0.0 collective-permute-done.4.e2_ref.refs_12_
  17.2 0.0 collective-permute-done.5.e4_ref.refs_13_
  17.2 0.0 collective-permute-done.3.e3_ref.refs_11_
  17.2 0.0 collective-permute-done.2.e1_ref.refs_10_
  17.2 0.0 copy-done.2
  17.2 0.0 copy-done.3
  17.2 0.0 copy-start
  17.2 0.0 copy-start.1
  17.2 0.0 copy-start.5
  17.2 0.0 copy-start.10
  17.2 1.4 %regrid_blocks.1 = (f32[64,128]{1,0:T(8,128)S(1)}, bf16[64,128]{1,0:T(8,128)(2,1)S(1)}, bf16[80,128]{1,0:T(8,128)(2,1)S(1)}, bf16[96,128]{1,0:T(8,128)(2,1)S(1)}) custom-call(f32[64,128]{1,0:T(8,128)S(1)} %get-tuple-element.55.refs_0_, bf16[64,128]{1,0:T(8,128)(2,1)S(1)} %collective-permute-done.6.refs_1_, bf16[128,4096]{1,0:T(8,128)(2,1)S(1)} %get-tuple-element.44.refs_2_, ...), custom_call_target="tpu_custom_call" | custom-call | tf_op jit(solution)/shard_map/regrid_blocks/pallas_call | solution.py:788
  18.6 0.0 copy-start.4
  18.6 0.0 copy-start.11
  18.6 3.1 %collective-permute-start.9 = (bf16[96,128]{1,0:T(8,128)(2,1)S(1)}, bf16[96,128]{1,0:T(8,128)(2,1)S(1)}, u32[]{:S(2)}, u32[]{:S(2)}) collective-permute-start(bf16[96,128]{1,0:T(8,128)(2,1)S(1)} %get-tuple-element.51), channel_id=1, source_target_pairs={{0,3},{3,0},{1,2},{2,1},{4,7},{7,4},{5,6},{6,5},{8,11},{11,8},{9,1... | collective-permute-start | bytes 73736 | tf_op jit(solution)/shard_map/ppermute | solution.py:824
  21.7 0.0 collective-permute-start.8
  21.7 1.3 %collective-permute-start.7 = (bf16[64,128]{1,0:T(8,128)(2,1)S(1)}, bf16[64,128]{1,0:T(8,128)(2,1)S(1)}, u32[]{:S(2)}, u32[]{:S(2)}) collective-permute-start(bf16[64,128]{1,0:T(8,128)(2,1)S(1)} %get-tuple-element.49), channel_id=1, source_target_pairs={{0,1},{1,0},{2,3},{3,2},{4,5},{5,4},{6,7},{7,6},{8,9},{9,8},{10,11... | collective-permute-start | bytes 49160 | tf_op jit(solution)/shard_map/ppermute | solution.py:824
  23.1 0.0 copy-done
  23.1 0.0 copy-done.1
  23.1 0.0 copy-done.5
  23.1 0.0 copy-done.10
  23.1 1.0 %damping_or_first_step.1 = (bf16[256,1024]{1,0:T(8,128)(2,1)S(1)}, f32[7,16,1024]{2,1,0:T(8,128)S(1)}, f32[10,2,24,1024]{3,2,1,0:T(8,128)S(1)}) custom-call(f32[1,8,32,1024]{3,2,1,0:T(8,128)S(1)} %copy-done, s32[8,1024]{1,0:T(8,128)S(1)} %copy-done.5, f32[1,128]{1,0:T(1,128)S(1)} %bitcast.4, f32[8,32,1024]{2,1,0:T(8,128)S(1)} %copy-done.1, ...), custom_call_target="tpu_custom_call" | custom-call | tf_op jit(solution)/shard_map/damping_or_first_step/pallas_call | solution.py:844
  24.1 1.4 %collective-permute-done.7.refs_0_ = bf16[64,128]{1,0:T(8,128)(2,1)S(1)} collective-permute-done((bf16[64,128]{1,0:T(8,128)(2,1)S(1)}, bf16[64,128]{1,0:T(8,128)(2,1)S(1)}, u32[]{:S(2)}, u32[]{:S(2)}) %collective-permute-start.7) | collective-permute-done | bytes 16416 | tf_op jit(solution)/shard_map/ppermute | solution.py:824
  25.5 0.9 %collective-permute-done.8.refs_1_ = bf16[80,128]{1,0:T(8,128)(2,1)S(1)} collective-permute-done((bf16[80,128]{1,0:T(8,128)(2,1)S(1)}, bf16[80,128]{1,0:T(8,128)(2,1)S(1)}, u32[]{:S(2)}, u32[]{:S(2)}) %collective-permute-start.8) | collective-permute-done | bytes 20512 | tf_op jit(solution)/shard_map/ppermute | solution.py:824
  26.4 0.0 collective-permute-done.9.refs_2_
  26.5 0.1 collective-permute-start.10
  26.6 0.7 %collective-permute-start.11 = (bf16[64,128]{1,0:T(8,128)(2,1)S(1)}, bf16[64,128]{1,0:T(8,128)(2,1)S(1)}, u32[]{:S(2)}, u32[]{:S(2)}) collective-permute-start(bf16[64,128]{1,0:T(8,128)(2,1)S(1)} %get-tuple-element.54), channel_id=1, source_target_pairs={{4,8},{8,4},{12,0},{0,12},{5,9},{9,5},{13,1},{1,13},{6,10},{10,6},... | collective-permute-start | bytes 49160 | tf_op jit(solution)/shard_map/ppermute | solution.py:876
  27.2 0.0 copy-done.4
  27.2 0.0 copy-done.11
  27.2 0.4 %inverse_or_second_step.1 = (f32[8,32,1024]{2,1,0:T(8,128)S(1)}, f32[32,128]{1,0:T(8,128)S(1)}) custom-call(f32[1,128]{1,0:T(1,128)S(1)} %bitcast.5, bf16[1024,512]{1,0:T(8,128)(2,1)S(1)} %copy-done.4, bf16[256,1024]{1,0:T(8,128)(2,1)S(1)} %get-tuple-element.38.zb_ref, f32[7,16,1024]{2,1,0:T(8,128)S(1)} %get-tuple-element.39.c_ref._, ...), custom_call_target="tpu_custom_call" | custom-call | tf_op jit(solution)/shard_map/inverse_or_second_step/pallas_call | solution.py:877
  27.7 0.1 collective-permute-done.10.near_ref
  27.7 2.1 %collective-permute-done.11.far_ref = bf16[64,128]{1,0:T(8,128)(2,1)S(1)} collective-permute-done((bf16[64,128]{1,0:T(8,128)(2,1)S(1)}, bf16[64,128]{1,0:T(8,128)(2,1)S(1)}, u32[]{:S(2)}, u32[]{:S(2)}) %collective-permute-start.11) | collective-permute-done | bytes 16416 | tf_op jit(solution)/shard_map/ppermute | solution.py:876
  29.8 1.0 %add_surface_terms.1 = f32[1,8,32,1024]{3,2,1,0:T(8,128)} custom-call(f32[32,128]{1,0:T(8,128)S(1)} %get-tuple-element.41.column_ref, f32[8,32,1024]{2,1,0:T(8,128)S(1)} %get-tuple-element.42.base_ref, f32[7,16,1024]{2,1,0:T(8,128)S(1)} %get-tuple-element.39.c_ref._, f32[64,128]{1,0:T(8,128)S(1)} %get-tuple-element.52.sum_ref, ...), custom_call_target="tpu_custom_call" | custom-call | tf_op jit(solution)/shard_map/add_surface_terms/pallas_call | solution.py:885
  (2 shorter events, 0.1 us)
Async XLA Ops:
  0.0 16.4 %copy-start.6 = (s32[1,1,32,128]{3,2,1,0:T(8,128)S(1)}, s32[1,1,32,128]{3,2,1,0:T(8,128)}, u32[]{:S(2)}) copy-start(s32[1,1,32,128]{3,2,1,0:T(8,128)} %a_src.1) | copy-start | bytes 49156
  0.0 16.4 %copy-start.7 = (s32[1,1,32,128]{3,2,1,0:T(8,128)S(1)}, s32[1,1,32,128]{3,2,1,0:T(8,128)}, u32[]{:S(2)}) copy-start(s32[1,1,32,128]{3,2,1,0:T(8,128)} %a_dst.1) | copy-start | bytes 49156
  0.0 16.4 %copy-start.8 = (s32[1,1,32,128]{3,2,1,0:T(8,128)S(1)}, s32[1,1,32,128]{3,2,1,0:T(8,128)}, u32[]{:S(2)}) copy-start(s32[1,1,32,128]{3,2,1,0:T(8,128)} %m_src.1) | copy-start | bytes 49156
  0.0 16.4 %copy-start.9 = (s32[1,1,32,128]{3,2,1,0:T(8,128)S(1)}, s32[1,1,32,128]{3,2,1,0:T(8,128)}, u32[]{:S(2)}) copy-start(s32[1,1,32,128]{3,2,1,0:T(8,128)} %m_dst.1) | copy-start | bytes 49156
  0.0 17.2 %copy-start.2 = (bf16[1,1,32,128,128]{4,3,2,1,0:T(8,128)(2,1)S(1)}, bf16[1,1,32,128,128]{4,3,2,1,0:T(8,128)(2,1)}, u32[]{:S(2)}) copy-start(bf16[1,1,32,128,128]{4,3,2,1,0:T(8,128)(2,1)} %refs_8_.1) | copy-start | bytes 3145732
  0.0 17.2 %copy-start.3 = (bf16[1,1,32,128,128]{4,3,2,1,0:T(8,128)(2,1)S(1)}, bf16[1,1,32,128,128]{4,3,2,1,0:T(8,128)(2,1)}, u32[]{:S(2)}) copy-start(bf16[1,1,32,128,128]{4,3,2,1,0:T(8,128)(2,1)} %refs_9_.1) | copy-start | bytes 3145732
  3.7 7.0 %collective-permute-start.1 = (bf16[80,128]{1,0:T(8,128)(2,1)}, bf16[80,128]{1,0:T(8,128)(2,1)S(1)}, u32[]{:S(2)}, u32[]{:S(2)}) collective-permute-start(bf16[80,128]{1,0:T(8,128)(2,1)} %get-tuple-element.33), channel_id=1, source_target_pairs={{0,17},{17,0},{1,16},{16,1},{2,19},{19,2},{3,18},{18,3},{4,21},{21... | collective-permute-start | bytes 61448 | tf_op jit(solution)/shard_map/ppermute | solution.py:738
  6.7 3.9 %collective-permute-start = (bf16[64,128]{1,0:T(8,128)(2,1)}, bf16[64,128]{1,0:T(8,128)(2,1)S(1)}, u32[]{:S(2)}, u32[]{:S(2)}) collective-permute-start(bf16[64,128]{1,0:T(8,128)(2,1)} %get-tuple-element.32), channel_id=1, source_target_pairs={{0,16},{16,0},{1,17},{17,1},{2,18},{18,2},{3,19},{19,3},{4,20},{20... | collective-permute-start | bytes 49160 | tf_op jit(solution)/shard_map/ppermute | solution.py:736
  8.3 8.9 %collective-permute-start.3 = (bf16[80,1024]{1,0:T(8,128)(2,1)}, bf16[80,1024]{1,0:T(8,128)(2,1)S(1)}, u32[]{:S(2)}, u32[]{:S(2)}) collective-permute-start(bf16[80,1024]{1,0:T(8,128)(2,1)} %get-tuple-element.35), channel_id=1, source_target_pairs={{4,8},{8,4},{12,0},{0,12},{5,9},{9,5},{13,1},{1,13},{6,10},{10,6},... | collective-permute-start | bytes 491528 | tf_op jit(solution)/shard_map/ppermute | solution.py:770
  10.7 6.5 %collective-permute-start.2 = (bf16[80,1024]{1,0:T(8,128)(2,1)}, bf16[80,1024]{1,0:T(8,128)(2,1)S(1)}, u32[]{:S(2)}, u32[]{:S(2)}) collective-permute-start(bf16[80,1024]{1,0:T(8,128)(2,1)} %get-tuple-element.34), channel_id=1, source_target_pairs={{0,4},{4,0},{8,12},{12,8},{1,5},{5,1},{9,13},{13,9},{2,6},{6,2},{1... | collective-permute-start | bytes 491528 | tf_op jit(solution)/shard_map/ppermute | solution.py:769
  10.7 6.4 %collective-permute-start.4 = (bf16[32,1024]{1,0:T(8,128)(2,1)}, bf16[32,1024]{1,0:T(8,128)(2,1)S(1)}, u32[]{:S(2)}, u32[]{:S(2)}) collective-permute-start(bf16[32,1024]{1,0:T(8,128)(2,1)} %get-tuple-element.36), channel_id=1, source_target_pairs={{16,17},{17,16},{18,19},{19,18},{0,8},{8,0},{1,9},{9,1},{2,10},{10... | collective-permute-start | bytes 196616 | tf_op jit(solution)/shard_map/ppermute | solution.py:772
  12.3 4.9 %collective-permute-start.5 = (bf16[32,1024]{1,0:T(8,128)(2,1)}, bf16[32,1024]{1,0:T(8,128)(2,1)S(1)}, u32[]{:S(2)}, u32[]{:S(2)}) collective-permute-start(bf16[32,1024]{1,0:T(8,128)(2,1)} %get-tuple-element.37), channel_id=1, source_target_pairs={{17,18},{18,17},{16,20},{20,16},{19,23},{23,19},{0,4},{4,0},{1,5},... | collective-permute-start | bytes 196616 | tf_op jit(solution)/shard_map/ppermute | solution.py:773
  12.5 4.7 %collective-permute-start.6 = (bf16[64,128]{1,0:T(8,128)(2,1)S(1)}, bf16[64,128]{1,0:T(8,128)(2,1)S(1)}, u32[]{:S(2)}, u32[]{:S(2)}) collective-permute-start(bf16[64,128]{1,0:T(8,128)(2,1)S(1)} %get-tuple-element.43._), channel_id=1, source_target_pairs={{0,2},{1,3},{2,0},{3,1},{4,6},{5,7},{6,4},{7,5},{8,10},{9,11},{10,... | collective-permute-start | bytes 49160 | tf_op jit(solution)/shard_map/ppermute | solution.py:745
  17.2 5.9 %copy-start = (f32[1,8,32,1024]{3,2,1,0:T(8,128)S(1)}, f32[1,8,32,1024]{3,2,1,0:T(8,128)}, u32[]{:S(2)}) copy-start(f32[1,8,32,1024]{3,2,1,0:T(8,128)} %x_ref.1) | copy-start | bytes 3145732
  17.2 5.9 %copy-start.1 = (f32[8,32,1024]{2,1,0:T(8,128)S(1)}, f32[8,32,1024]{2,1,0:T(8,128)}, u32[]{:S(2)}) copy-start(f32[8,32,1024]{2,1,0:T(8,128)} %get-tuple-element.30.y_ref) | copy-start | bytes 3145732
  17.2 5.9 %copy-start.5 = (s32[8,1024]{1,0:T(8,128)S(1)}, s32[8,1024]{1,0:T(8,128)}, u32[]{:S(2)}) copy-start(s32[8,1024]{1,0:T(8,128)} %wet_ref.1) | copy-start | bytes 98308
  17.2 5.9 %copy-start.10 = (f32[128]{0:T(128)S(1)}, f32[128]{0:T(128)}, u32[]{:S(2)}) copy-start(f32[128]{0:T(128)} %param.19) | copy-start | bytes 1540
  18.6 8.6 %copy-start.4 = (bf16[1024,512]{1,0:T(8,128)(2,1)S(1)}, bf16[1024,512]{1,0:T(8,128)(2,1)}, u32[]{:S(2)}) copy-start(bf16[1024,512]{1,0:T(8,128)(2,1)} %constant.5.clone.table_ref) | copy-start | bytes 3145732
  18.6 8.6 %copy-start.11 = (f32[128]{0:T(128)S(1)}, f32[128]{0:T(128)}, u32[]{:S(2)}) copy-start(f32[128]{0:T(128)} %param.18) | copy-start | bytes 1540
  18.6 7.8 %collective-permute-start.9 = (bf16[96,128]{1,0:T(8,128)(2,1)S(1)}, bf16[96,128]{1,0:T(8,128)(2,1)S(1)}, u32[]{:S(2)}, u32[]{:S(2)}) collective-permute-start(bf16[96,128]{1,0:T(8,128)(2,1)S(1)} %get-tuple-element.51), channel_id=1, source_target_pairs={{0,3},{3,0},{1,2},{2,1},{4,7},{7,4},{5,6},{6,5},{8,11},{11,8},{9,1... | collective-permute-start | bytes 73736 | tf_op jit(solution)/shard_map/ppermute | solution.py:824
  21.7 4.7 %collective-permute-start.8 = (bf16[80,128]{1,0:T(8,128)(2,1)S(1)}, bf16[80,128]{1,0:T(8,128)(2,1)S(1)}, u32[]{:S(2)}, u32[]{:S(2)}) collective-permute-start(bf16[80,128]{1,0:T(8,128)(2,1)S(1)} %get-tuple-element.50), channel_id=1, source_target_pairs={{0,2},{2,0},{1,3},{3,1},{4,6},{6,4},{5,7},{7,5},{8,10},{10,8},{9,1... | collective-permute-start | bytes 61448 | tf_op jit(solution)/shard_map/ppermute | solution.py:824
  21.7 3.7 %collective-permute-start.7 = (bf16[64,128]{1,0:T(8,128)(2,1)S(1)}, bf16[64,128]{1,0:T(8,128)(2,1)S(1)}, u32[]{:S(2)}, u32[]{:S(2)}) collective-permute-start(bf16[64,128]{1,0:T(8,128)(2,1)S(1)} %get-tuple-element.49), channel_id=1, source_target_pairs={{0,1},{1,0},{2,3},{3,2},{4,5},{5,4},{6,7},{7,6},{8,9},{9,8},{10,11... | collective-permute-start | bytes 49160 | tf_op jit(solution)/shard_map/ppermute | solution.py:824
  26.5 1.2 %collective-permute-start.10 = (bf16[64,128]{1,0:T(8,128)(2,1)S(1)}, bf16[64,128]{1,0:T(8,128)(2,1)S(1)}, u32[]{:S(2)}, u32[]{:S(2)}) collective-permute-start(bf16[64,128]{1,0:T(8,128)(2,1)S(1)} %get-tuple-element.53), channel_id=1, source_target_pairs={{0,4},{4,0},{8,12},{12,8},{1,5},{5,1},{9,13},{13,9},{2,6},{6,2},{1... | collective-permute-start | bytes 49160 | tf_op jit(solution)/shard_map/ppermute | solution.py:875
  26.6 3.2 %collective-permute-start.11 = (bf16[64,128]{1,0:T(8,128)(2,1)S(1)}, bf16[64,128]{1,0:T(8,128)(2,1)S(1)}, u32[]{:S(2)}, u32[]{:S(2)}) collective-permute-start(bf16[64,128]{1,0:T(8,128)(2,1)S(1)} %get-tuple-element.54), channel_id=1, source_target_pairs={{4,8},{8,4},{12,0},{0,12},{5,9},{9,5},{13,1},{1,13},{6,10},{10,6},... | collective-permute-start | bytes 49160 | tf_op jit(solution)/shard_map/ppermute | solution.py:876

commit v17 on v16

--- a/solution.py
+++ b/solution.py
@@ -288,7 +288,7 @@
     surfaces = refs[:n_surfaces]
     (
         src_hot_ref, dst_hot_ref, src_row_ref, dst_row_ref, a_count, m_count, a_weight, m_weight,
-        _, _, _, _,
+        _,
         *refs,
     ) = refs[n_surfaces:]
     land_ref, *sent_refs = refs[:-4]
@@ -765,7 +765,6 @@
                 pairs += [(flat(0, i, j), flat(0, i ^ 2, j)) for j in range(groups_y)]
         return both_ways(pairs)
 
-    e1, coarse = lax.optimization_barrier((e1, coarse))
     e1 = lax.ppermute(e1, "gx", both_ways(ring_pairs(groups_x, 0)))
     e3 = lax.ppermute(e3, "gx", both_ways(ring_pairs(groups_x, 1)))
     axes = ("comp", "gx", "gy")
@@ -789,7 +788,7 @@
         functools.partial(regrid_kernel, len(surfaces)),
         out_shape=[shape((cells, LANES), f32)]
         + [shape((cells + 16 * (mask - 1), LANES), bf16) for mask in range(1, groups_y)],
-        in_specs=[vmem] * (len(surfaces) + 4) + [smem, smem, hbm, hbm] + [anywhere] * 4,
+        in_specs=[vmem] * (len(surfaces) + 4) + [smem, smem, hbm, hbm] + [anywhere] * 1,
         out_specs=[vmem] * groups_y,
         scratch_shapes=[
             pltpu.VMEM((blocks, points, points), bf16),
@@ -798,10 +797,11 @@
             pltpu.SemaphoreType.DMA,
         ],
         compiler_params=params(),
+        cost_estimate=pl.CostEstimate(flops=int(2.0 * 1.1e9), bytes_accessed=0, transcendentals=0),
         name="regrid_blocks",
     )(
         *surfaces, *one_hots, a2o_count, marine_air_piece_tally,
-        a2o_weight, marine_air_piece_factor, e1, e3, e2, e4,
+        a2o_weight, marine_air_piece_factor, e3,
     )
 
     def landing_route(mask):

time: 31 us -> 29.5 us (0.952)
  waiting for transfers between devices: 6.59 us -> 4.5 us
  starting transfers between devices: 14.5 us -> 15.1 us
    ppermute x3, waiting for transfers between devices: 2.34 us -> 1.01 us  [local(): lax.ppermute(block, axes, landing_route(mask))]
    ppermute x1, starting transfers between devices: 0.65 us -> 1.28 us  [local(): far = lax.ppermute(far, 'gx', both_ways(ring_pairs(groups_x, 1)))]
    ppermute x1, waiting for transfers between devices: 2.06 us -> 1.48 us  [local(): far = lax.ppermute(far, 'gx', both_ways(ring_pairs(groups_x, 1)))]
  transfers between devices with their start and end apart: 12 -> 12, of which waited for: 6 -> 3; matrix products, arithmetic and copies ran while one was open for 0% -> 0% of each run, Pallas kernels for 7% -> 12%
where the time goes in v17:
time: 29.5 us; the launch traced here: 29.4 us
  starting transfers between devices  15.1 us (51%)
  Pallas kernels  8.15 us (28%)
  waiting for transfers between devices  4.5 us (15%)
  between operations  1.53 us (5%)
    ppermute x3, starting transfers between devices, local(): lax.ppermute(block, axes, landing_route(mask))  4.45 us
    pallas_call x1, Pallas kernels, local(): pl.pallas_call(functools.partial(start_kernel, groups_x, paired), out_sha...  3.67 us
    ppermute x1, starting transfers between devices, local(): far = lax.ppermute(wide, ('comp', 'gy'), partner_route(mask))  3 us
    ppermute x1, starting transfers between devices, local(): lax.ppermute(coarse, 'gy', sum_route(mask))  2.65 us
    ppermute x1, waiting for transfers between devices, local(): surface = lax.ppermute(coarse, ('comp', 'gy'), partner_route(0)).astype(f32)  2 us
    ppermute x1, starting transfers between devices, local(): surface = lax.ppermute(coarse, ('comp', 'gy'), partner_route(0)).astype(f32)  1.58 us
    ppermute x1, starting transfers between devices, local(): e2 = lax.ppermute(e2, axes, level_route(0))  1.49 us
    ppermute x1, waiting for transfers between devices, local(): far = lax.ppermute(far, 'gx', both_ways(ring_pairs(groups_x, 1)))  1.48 us
  transfers between devices with their start and end apart: 12, of which 3 were waited for; matrix products, arithmetic and copies ran while one was open for 0% of the time, Pallas kernels for 12%

profile of v17, /device:TPU:0, one launch (start us, length us, event | category | flops | bytes accessed | tf_op | source)
XLA Modules:
  0.0 29.4 jit_solution(17656719367287397331)
XLA Ops:
  0.0 0.0 copy-start.4
  0.0 0.0 copy-start.5
  0.0 0.0 copy-start.6
  0.0 0.0 copy-start.7
  0.0 0.0 copy-start.10
  0.0 0.0 copy-start.11
  0.0 3.7 %surface_and_forward_or_halos.1 = (bf16[64,128]{1,0:T(8,128)(2,1)}, bf16[80,128]{1,0:T(8,128)(2,1)}, f32[8,32,1024]{2,1,0:T(8,128)}, bf16[80,1024]{1,0:T(8,128)(...) custom-call(f32[1,8,32,1024]{3,2,1,0:T(8,128)} %x_ref.1, s32[8,1024]{1,0:T(8,128)} %wet_ref.1, ...), custom_call_target="tpu_custom_call" | custom-call | tf_op jit(solution)/shard_map/surface_and_forward_or_halos/pallas_call | solution.py:704
  3.7 3.0 %collective-permute-start.5 = (bf16[80,128]{1,0:T(8,128)(2,1)}, bf16[80,128]{1,0:T(8,128)(2,1)S(1)}, u32[]{:S(2)}, u32[]{:S(2)}) collective-permute-start(bf16[80,128]{1,0:T(8,128)(2,1)} %get-tuple-element.39), channel_id=1, source_target_pairs={{0,17},{17,0},{1,16},{16,1},{2,19},{19,2},{3,18},{18,3},{4,21},{21... | collective-permute-start | bytes 61448 | tf_op jit(solution)/shard_map/ppermute | solution.py:738
  6.7 1.6 %collective-permute-start.4 = (bf16[64,128]{1,0:T(8,128)(2,1)}, bf16[64,128]{1,0:T(8,128)(2,1)S(1)}, u32[]{:S(2)}, u32[]{:S(2)}) collective-permute-start(bf16[64,128]{1,0:T(8,128)(2,1)} %get-tuple-element.38), channel_id=1, source_target_pairs={{0,16},{16,0},{1,17},{17,1},{2,18},{18,2},{3,19},{19,3},{4,20},{20... | collective-permute-start | bytes 49160 | tf_op jit(solution)/shard_map/ppermute | solution.py:736
  8.3 0.4 %collective-permute-start.1 = (bf16[80,1024]{1,0:T(8,128)(2,1)}, bf16[80,1024]{1,0:T(8,128)(2,1)S(1)}, u32[]{:S(2)}, u32[]{:S(2)}) collective-permute-start(bf16[80,1024]{1,0:T(8,128)(2,1)} %get-tuple-element.30), channel_id=1, source_target_pairs={{4,8},{8,4},{12,0},{0,12},{5,9},{9,5},{13,1},{1,13},{6,10},{10,6},... | collective-permute-start | bytes 491528 | tf_op jit(solution)/shard_map/ppermute | solution.py:769
  8.7 2.0 %collective-permute-done.4 = bf16[64,128]{1,0:T(8,128)(2,1)S(1)} collective-permute-done((bf16[64,128]{1,0:T(8,128)(2,1)}, bf16[64,128]{1,0:T(8,128)(2,1)S(1)}, u32[]{:S(2)}, u32[]{:S(2)}) %collective-permute-start.4) | collective-permute-done | bytes 16416 | tf_op jit(solution)/shard_map/ppermute | solution.py:736
  10.7 0.0 collective-permute-done.5
  10.7 2.7 %collective-permute-start.6 = (bf16[64,128]{1,0:T(8,128)(2,1)S(1)}, bf16[64,128]{1,0:T(8,128)(2,1)S(1)}, u32[]{:S(2)}, u32[]{:S(2)}) collective-permute-start(bf16[64,128]{1,0:T(8,128)(2,1)S(1)} %get-tuple-element.51._), channel_id=1, source_target_pairs={{0,2},{1,3},{2,0},{3,1},{4,6},{5,7},{6,4},{7,5},{8,10},{9,11},{10,... | collective-permute-start | bytes 49160 | tf_op jit(solution)/shard_map/ppermute | solution.py:745
  13.3 0.0 collective-permute-start
  13.3 1.5 %collective-permute-start.2 = (bf16[32,1024]{1,0:T(8,128)(2,1)}, bf16[32,1024]{1,0:T(8,128)(2,1)S(1)}, u32[]{:S(2)}, u32[]{:S(2)}) collective-permute-start(bf16[32,1024]{1,0:T(8,128)(2,1)} %get-tuple-element.31), channel_id=1, source_target_pairs={{16,17},{17,16},{18,19},{19,18},{0,8},{8,0},{1,9},{9,1},{2,10},{10... | collective-permute-start | bytes 196616 | tf_op jit(solution)/shard_map/ppermute | solution.py:771
  14.8 0.2 collective-permute-start.3
  16.3 0.0 copy-done.4
  16.4 0.0 copy-done.5
  16.4 0.0 copy-done.6
  16.4 0.0 copy-done.7
  16.4 0.6 %one_hots.1 = (bf16[128,4096]{1,0:T(8,128)(2,1)S(1)}, bf16[128,4096]{1,0:T(8,128)(2,1)S(1)}, s32[32,128]{1,0:T(8,128)S(1)}, s32[32,128]{1,0:T(8,128)S(1)}) custom-call(s32[1,1,32,128]{3,2,1,0:T(8,128)S(1)} %copy-done.4, s32[1,1,32,128]{3,2,1,0:T(8,128)S(1)} %copy-done.5, s32[1,1,32,128]{3,2,1,0:T(8,128)S(1)} %copy-done.6, s32[1,1,32,128]{3,2,1,0:T(8,128)S(1)} %copy-done.7, ...), custom_call_target="tpu_custom_call" | custom-call | tf_op jit(solution)/shard_map/one_hots/pallas_call | solution.py:774
  17.0 0.0 collective-permute-done.6.refs_1_
  17.0 0.0 collective-permute-done.1.e3_ref.refs_10_
  17.0 0.0 copy-done.10
  17.0 0.0 copy-done.11
  17.1 0.0 copy-start
  17.1 0.0 copy-start.1
  17.1 0.0 copy-start.3
  17.1 0.0 copy-start.8
  17.1 1.4 %regrid_blocks.1 = (f32[64,128]{1,0:T(8,128)S(1)}, bf16[64,128]{1,0:T(8,128)(2,1)S(1)}, bf16[80,128]{1,0:T(8,128)(2,1)S(1)}, bf16[96,128]{1,0:T(8,128)(2,1)S(1)}) custom-call(f32[64,128]{1,0:T(8,128)S(1)} %get-tuple-element.52.refs_0_, bf16[64,128]{1,0:T(8,128)(2,1)S(1)} %collective-permute-done.6.refs_1_, bf16[128,4096]{1,0:T(8,128)(2,1)S(1)} %get-tuple-element.40.refs_2_, ...), custom_call_target="tpu_custom_call" | custom-call | flops 2200000000 | tf_op jit(solution)/shard_map/regrid_blocks/pallas_call | solution.py:787
  18.5 0.0 copy-start.2
  18.5 0.0 copy-start.9
  18.5 1.5 %collective-permute-start.9 = (bf16[96,128]{1,0:T(8,128)(2,1)S(1)}, bf16[96,128]{1,0:T(8,128)(2,1)S(1)}, u32[]{:S(2)}, u32[]{:S(2)}) collective-permute-start(bf16[96,128]{1,0:T(8,128)(2,1)S(1)} %get-tuple-element.47), channel_id=1, source_target_pairs={{0,3},{3,0},{1,2},{2,1},{4,7},{7,4},{5,6},{6,5},{8,11},{11,8},{9,1... | collective-permute-start | bytes 73736 | tf_op jit(solution)/shard_map/ppermute | solution.py:824
  20.0 1.1 %collective-permute-start.8 = (bf16[80,128]{1,0:T(8,128)(2,1)S(1)}, bf16[80,128]{1,0:T(8,128)(2,1)S(1)}, u32[]{:S(2)}, u32[]{:S(2)}) collective-permute-start(bf16[80,128]{1,0:T(8,128)(2,1)S(1)} %get-tuple-element.46), channel_id=1, source_target_pairs={{0,2},{2,0},{1,3},{3,1},{4,6},{6,4},{5,7},{7,5},{8,10},{10,8},{9,1... | collective-permute-start | bytes 61448 | tf_op jit(solution)/shard_map/ppermute | solution.py:824
  21.1 0.0 collective-permute-done.2.e2_ref
  21.1 1.9 %collective-permute-start.7 = (bf16[64,128]{1,0:T(8,128)(2,1)S(1)}, bf16[64,128]{1,0:T(8,128)(2,1)S(1)}, u32[]{:S(2)}, u32[]{:S(2)}) collective-permute-start(bf16[64,128]{1,0:T(8,128)(2,1)S(1)} %get-tuple-element.45), channel_id=1, source_target_pairs={{0,1},{1,0},{2,3},{3,2},{4,5},{5,4},{6,7},{7,6},{8,9},{9,8},{10,11... | collective-permute-start | bytes 49160 | tf_op jit(solution)/shard_map/ppermute | solution.py:824
  23.0 0.0 collective-permute-done.3.e4_ref
  23.0 0.0 collective-permute-done.e1_ref
  23.0 0.0 copy-done
  23.0 0.0 copy-done.1
  23.0 0.0 copy-done.3
  23.0 0.0 copy-done.8
  23.0 1.0 %damping_or_first_step.1 = (bf16[256,1024]{1,0:T(8,128)(2,1)S(1)}, f32[7,16,1024]{2,1,0:T(8,128)S(1)}, f32[10,2,24,1024]{3,2,1,0:T(8,128)S(1)}) custom-call(f32[1,8,32,1024]{3,2,1,0:T(8,128)S(1)} %copy-done, s32[8,1024]{1,0:T(8,128)S(1)} %copy-done.3, f32[1,128]{1,0:T(1,128)S(1)} %bitcast.4, f32[8,32,1024]{2,1,0:T(8,128)S(1)} %copy-done.1, ...), custom_call_target="tpu_custom_call" | custom-call | tf_op jit(solution)/shard_map/damping_or_first_step/pallas_call | solution.py:844
  24.0 1.0 %collective-permute-done.7.refs_0_ = bf16[64,128]{1,0:T(8,128)(2,1)S(1)} collective-permute-done((bf16[64,128]{1,0:T(8,128)(2,1)S(1)}, bf16[64,128]{1,0:T(8,128)(2,1)S(1)}, u32[]{:S(2)}, u32[]{:S(2)}) %collective-permute-start.7) | collective-permute-done | bytes 16416 | tf_op jit(solution)/shard_map/ppermute | solution.py:824
  25.0 0.0 collective-permute-done.8.refs_1_
  25.0 0.0 collective-permute-done.9.refs_2_
  25.0 0.1 collective-permute-start.10
  25.1 1.3 %collective-permute-start.11 = (bf16[64,128]{1,0:T(8,128)(2,1)S(1)}, bf16[64,128]{1,0:T(8,128)(2,1)S(1)}, u32[]{:S(2)}, u32[]{:S(2)}) collective-permute-start(bf16[64,128]{1,0:T(8,128)(2,1)S(1)} %get-tuple-element.50), channel_id=1, source_target_pairs={{4,8},{8,4},{12,0},{0,12},{5,9},{9,5},{13,1},{1,13},{6,10},{10,6},... | collective-permute-start | bytes 49160 | tf_op jit(solution)/shard_map/ppermute | solution.py:876
  26.4 0.0 copy-done.2
  26.4 0.0 copy-done.9
  26.4 0.4 %inverse_or_second_step.1 = (f32[8,32,1024]{2,1,0:T(8,128)S(1)}, f32[32,128]{1,0:T(8,128)S(1)}) custom-call(f32[1,128]{1,0:T(1,128)S(1)} %bitcast.5, bf16[1024,512]{1,0:T(8,128)(2,1)S(1)} %copy-done.2, bf16[256,1024]{1,0:T(8,128)(2,1)S(1)} %get-tuple-element.33.zb_ref, f32[7,16,1024]{2,1,0:T(8,128)S(1)} %get-tuple-element.34.c_ref._, ...), custom_call_target="tpu_custom_call" | custom-call | tf_op jit(solution)/shard_map/inverse_or_second_step/pallas_call | solution.py:877
  26.9 0.0 collective-permute-done.10.near_ref
  26.9 1.5 %collective-permute-done.11.far_ref = bf16[64,128]{1,0:T(8,128)(2,1)S(1)} collective-permute-done((bf16[64,128]{1,0:T(8,128)(2,1)S(1)}, bf16[64,128]{1,0:T(8,128)(2,1)S(1)}, u32[]{:S(2)}, u32[]{:S(2)}) %collective-permute-start.11) | collective-permute-done | bytes 16416 | tf_op jit(solution)/shard_map/ppermute | solution.py:876
  28.3 1.0 %add_surface_terms.1 = f32[1,8,32,1024]{3,2,1,0:T(8,128)} custom-call(f32[32,128]{1,0:T(8,128)S(1)} %get-tuple-element.36.column_ref, f32[8,32,1024]{2,1,0:T(8,128)S(1)} %get-tuple-element.37.base_ref, f32[7,16,1024]{2,1,0:T(8,128)S(1)} %get-tuple-element.34.c_ref._, f32[64,128]{1,0:T(8,128)S(1)} %get-tuple-element.48.sum_ref, ...), custom_call_target="tpu_custom_call" | custom-call | tf_op jit(solution)/shard_map/add_surface_terms/pallas_call | solution.py:885
  (2 shorter events, 0.1 us)
Async XLA Ops:
  0.0 16.3 %copy-start.4 = (s32[1,1,32,128]{3,2,1,0:T(8,128)S(1)}, s32[1,1,32,128]{3,2,1,0:T(8,128)}, u32[]{:S(2)}) copy-start(s32[1,1,32,128]{3,2,1,0:T(8,128)} %a_src.1) | copy-start | bytes 49156
  0.0 16.4 %copy-start.5 = (s32[1,1,32,128]{3,2,1,0:T(8,128)S(1)}, s32[1,1,32,128]{3,2,1,0:T(8,128)}, u32[]{:S(2)}) copy-start(s32[1,1,32,128]{3,2,1,0:T(8,128)} %a_dst.1) | copy-start | bytes 49156
  0.0 16.4 %copy-start.6 = (s32[1,1,32,128]{3,2,1,0:T(8,128)S(1)}, s32[1,1,32,128]{3,2,1,0:T(8,128)}, u32[]{:S(2)}) copy-start(s32[1,1,32,128]{3,2,1,0:T(8,128)} %m_src.1) | copy-start | bytes 49156
  0.0 16.4 %copy-start.7 = (s32[1,1,32,128]{3,2,1,0:T(8,128)S(1)}, s32[1,1,32,128]{3,2,1,0:T(8,128)}, u32[]{:S(2)}) copy-start(s32[1,1,32,128]{3,2,1,0:T(8,128)} %m_dst.1) | copy-start | bytes 49156
  0.0 17.0 %copy-start.10 = (bf16[1,1,32,128,128]{4,3,2,1,0:T(8,128)(2,1)S(1)}, bf16[1,1,32,128,128]{4,3,2,1,0:T(8,128)(2,1)}, u32[]{:S(2)}) copy-start(bf16[1,1,32,128,128]{4,3,2,1,0:T(8,128)(2,1)} %refs_8_.1) | copy-start | bytes 3145732
  0.0 17.0 %copy-start.11 = (bf16[1,1,32,128,128]{4,3,2,1,0:T(8,128)(2,1)S(1)}, bf16[1,1,32,128,128]{4,3,2,1,0:T(8,128)(2,1)}, u32[]{:S(2)}) copy-start(bf16[1,1,32,128,128]{4,3,2,1,0:T(8,128)(2,1)} %refs_9_.1) | copy-start | bytes 3145732
  3.7 7.0 %collective-permute-start.5 = (bf16[80,128]{1,0:T(8,128)(2,1)}, bf16[80,128]{1,0:T(8,128)(2,1)S(1)}, u32[]{:S(2)}, u32[]{:S(2)}) collective-permute-start(bf16[80,128]{1,0:T(8,128)(2,1)} %get-tuple-element.39), channel_id=1, source_target_pairs={{0,17},{17,0},{1,16},{16,1},{2,19},{19,2},{3,18},{18,3},{4,21},{21... | collective-permute-start | bytes 61448 | tf_op jit(solution)/shard_map/ppermute | solution.py:738
  6.7 3.9 %collective-permute-start.4 = (bf16[64,128]{1,0:T(8,128)(2,1)}, bf16[64,128]{1,0:T(8,128)(2,1)S(1)}, u32[]{:S(2)}, u32[]{:S(2)}) collective-permute-start(bf16[64,128]{1,0:T(8,128)(2,1)} %get-tuple-element.38), channel_id=1, source_target_pairs={{0,16},{16,0},{1,17},{17,1},{2,18},{18,2},{3,19},{19,3},{4,20},{20... | collective-permute-start | bytes 49160 | tf_op jit(solution)/shard_map/ppermute | solution.py:736
  8.3 8.7 %collective-permute-start.1 = (bf16[80,1024]{1,0:T(8,128)(2,1)}, bf16[80,1024]{1,0:T(8,128)(2,1)S(1)}, u32[]{:S(2)}, u32[]{:S(2)}) collective-permute-start(bf16[80,1024]{1,0:T(8,128)(2,1)} %get-tuple-element.30), channel_id=1, source_target_pairs={{4,8},{8,4},{12,0},{0,12},{5,9},{9,5},{13,1},{1,13},{6,10},{10,6},... | collective-permute-start | bytes 491528 | tf_op jit(solution)/shard_map/ppermute | solution.py:769
  10.7 6.3 %collective-permute-start.6 = (bf16[64,128]{1,0:T(8,128)(2,1)S(1)}, bf16[64,128]{1,0:T(8,128)(2,1)S(1)}, u32[]{:S(2)}, u32[]{:S(2)}) collective-permute-start(bf16[64,128]{1,0:T(8,128)(2,1)S(1)} %get-tuple-element.51._), channel_id=1, source_target_pairs={{0,2},{1,3},{2,0},{3,1},{4,6},{5,7},{6,4},{7,5},{8,10},{9,11},{10,... | collective-permute-start | bytes 49160 | tf_op jit(solution)/shard_map/ppermute | solution.py:745
  13.3 9.6 %collective-permute-start = (bf16[80,1024]{1,0:T(8,128)(2,1)}, bf16[80,1024]{1,0:T(8,128)(2,1)S(1)}, u32[]{:S(2)}, u32[]{:S(2)}) collective-permute-start(bf16[80,1024]{1,0:T(8,128)(2,1)} %get-tuple-element.29), channel_id=1, source_target_pairs={{0,4},{4,0},{8,12},{12,8},{1,5},{5,1},{9,13},{13,9},{2,6},{6,2},{1... | collective-permute-start | bytes 491528 | tf_op jit(solution)/shard_map/ppermute | solution.py:768
  13.3 7.8 %collective-permute-start.2 = (bf16[32,1024]{1,0:T(8,128)(2,1)}, bf16[32,1024]{1,0:T(8,128)(2,1)S(1)}, u32[]{:S(2)}, u32[]{:S(2)}) collective-permute-start(bf16[32,1024]{1,0:T(8,128)(2,1)} %get-tuple-element.31), channel_id=1, source_target_pairs={{16,17},{17,16},{18,19},{19,18},{0,8},{8,0},{1,9},{9,1},{2,10},{10... | collective-permute-start | bytes 196616 | tf_op jit(solution)/shard_map/ppermute | solution.py:771
  14.8 8.1 %collective-permute-start.3 = (bf16[32,1024]{1,0:T(8,128)(2,1)}, bf16[32,1024]{1,0:T(8,128)(2,1)S(1)}, u32[]{:S(2)}, u32[]{:S(2)}) collective-permute-start(bf16[32,1024]{1,0:T(8,128)(2,1)} %get-tuple-element.32), channel_id=1, source_target_pairs={{17,18},{18,17},{16,20},{20,16},{19,23},{23,19},{0,4},{4,0},{1,5},... | collective-permute-start | bytes 196616 | tf_op jit(solution)/shard_map/ppermute | solution.py:772
  17.1 5.9 %copy-start = (f32[1,8,32,1024]{3,2,1,0:T(8,128)S(1)}, f32[1,8,32,1024]{3,2,1,0:T(8,128)}, u32[]{:S(2)}) copy-start(f32[1,8,32,1024]{3,2,1,0:T(8,128)} %x_ref.1) | copy-start | bytes 3145732
  17.1 5.9 %copy-start.1 = (f32[8,32,1024]{2,1,0:T(8,128)S(1)}, f32[8,32,1024]{2,1,0:T(8,128)}, u32[]{:S(2)}) copy-start(f32[8,32,1024]{2,1,0:T(8,128)} %get-tuple-element.28.y_ref) | copy-start | bytes 3145732
  17.1 5.9 %copy-start.3 = (s32[8,1024]{1,0:T(8,128)S(1)}, s32[8,1024]{1,0:T(8,128)}, u32[]{:S(2)}) copy-start(s32[8,1024]{1,0:T(8,128)} %wet_ref.1) | copy-start | bytes 98308
  17.1 5.9 %copy-start.8 = (f32[128]{0:T(128)S(1)}, f32[128]{0:T(128)}, u32[]{:S(2)}) copy-start(f32[128]{0:T(128)} %param.19) | copy-start | bytes 1540
  18.5 7.9 %copy-start.2 = (bf16[1024,512]{1,0:T(8,128)(2,1)S(1)}, bf16[1024,512]{1,0:T(8,128)(2,1)}, u32[]{:S(2)}) copy-start(bf16[1024,512]{1,0:T(8,128)(2,1)} %constant.5.clone.table_ref) | copy-start | bytes 3145732
  18.5 7.9 %copy-start.9 = (f32[128]{0:T(128)S(1)}, f32[128]{0:T(128)}, u32[]{:S(2)}) copy-start(f32[128]{0:T(128)} %param.18) | copy-start | bytes 1540
  18.5 6.5 %collective-permute-start.9 = (bf16[96,128]{1,0:T(8,128)(2,1)S(1)}, bf16[96,128]{1,0:T(8,128)(2,1)S(1)}, u32[]{:S(2)}, u32[]{:S(2)}) collective-permute-start(bf16[96,128]{1,0:T(8,128)(2,1)S(1)} %get-tuple-element.47), channel_id=1, source_target_pairs={{0,3},{3,0},{1,2},{2,1},{4,7},{7,4},{5,6},{6,5},{8,11},{11,8},{9,1... | collective-permute-start | bytes 73736 | tf_op jit(solution)/shard_map/ppermute | solution.py:824
  20.0 5.0 %collective-permute-start.8 = (bf16[80,128]{1,0:T(8,128)(2,1)S(1)}, bf16[80,128]{1,0:T(8,128)(2,1)S(1)}, u32[]{:S(2)}, u32[]{:S(2)}) collective-permute-start(bf16[80,128]{1,0:T(8,128)(2,1)S(1)} %get-tuple-element.46), channel_id=1, source_target_pairs={{0,2},{2,0},{1,3},{3,1},{4,6},{6,4},{5,7},{7,5},{8,10},{10,8},{9,1... | collective-permute-start | bytes 61448 | tf_op jit(solution)/shard_map/ppermute | solution.py:824
  21.1 3.9 %collective-permute-start.7 = (bf16[64,128]{1,0:T(8,128)(2,1)S(1)}, bf16[64,128]{1,0:T(8,128)(2,1)S(1)}, u32[]{:S(2)}, u32[]{:S(2)}) collective-permute-start(bf16[64,128]{1,0:T(8,128)(2,1)S(1)} %get-tuple-element.45), channel_id=1, source_target_pairs={{0,1},{1,0},{2,3},{3,2},{4,5},{5,4},{6,7},{7,6},{8,9},{9,8},{10,11... | collective-permute-start | bytes 49160 | tf_op jit(solution)/shard_map/ppermute | solution.py:824
  25.0 1.8 %collective-permute-start.10 = (bf16[64,128]{1,0:T(8,128)(2,1)S(1)}, bf16[64,128]{1,0:T(8,128)(2,1)S(1)}, u32[]{:S(2)}, u32[]{:S(2)}) collective-permute-start(bf16[64,128]{1,0:T(8,128)(2,1)S(1)} %get-tuple-element.49), channel_id=1, source_target_pairs={{0,4},{4,0},{8,12},{12,8},{1,5},{5,1},{9,13},{13,9},{2,6},{6,2},{1... | collective-permute-start | bytes 49160 | tf_op jit(solution)/shard_map/ppermute | solution.py:875
  25.1 3.2 %collective-permute-start.11 = (bf16[64,128]{1,0:T(8,128)(2,1)S(1)}, bf16[64,128]{1,0:T(8,128)(2,1)S(1)}, u32[]{:S(2)}, u32[]{:S(2)}) collective-permute-start(bf16[64,128]{1,0:T(8,128)(2,1)S(1)} %get-tuple-element.50), channel_id=1, source_target_pairs={{4,8},{8,4},{12,0},{0,12},{5,9},{9,5},{13,1},{1,13},{6,10},{10,6},... | collective-permute-start | bytes 49160 | tf_op jit(solution)/shard_map/ppermute | solution.py:876

commit v18 on v17

--- a/solution.py
+++ b/solution.py
@@ -264,10 +264,14 @@
 
 
 def one_hot_kernel(
-    rows, columns, a_src, a_dst, m_src, m_dst, _, src_hot_ref, dst_hot_ref, src_row_ref, dst_row_ref
+    rows, columns, a_src, a_dst, a_count, m_src, m_dst, m_count, src_hot_ref, dst_hot_ref,
+    src_row_ref, dst_row_ref, used_ref,
 ):
     is_atmos = lax.axis_index("comp") == 0
     blocks, points = src_row_ref.shape
+    count = jnp.where(is_atmos, m_count[0, 0], a_count[0, 0])
+    block_iota = lax.broadcasted_iota(jnp.int32, (blocks, points), 0)
+    used_ref[...] = jnp.where(block_iota < count, 1, 0)
     lane_iota = lax.broadcasted_iota(jnp.int32, (LANES, points), 0)
     for a_ref, m_ref, hot_ref, row_ref in (
         (a_src, m_src, src_hot_ref, src_row_ref),
@@ -287,7 +291,7 @@
 def regrid_kernel(n_surfaces, *refs):
     surfaces = refs[:n_surfaces]
     (
-        src_hot_ref, dst_hot_ref, src_row_ref, dst_row_ref, a_count, m_count, a_weight, m_weight,
+        src_hot_ref, dst_hot_ref, src_row_ref, dst_row_ref, used_ref, a_weight, m_weight,
         _,
         *refs,
     ) = refs[n_surfaces:]
@@ -305,7 +309,6 @@
     def _():
         pltpu.make_async_copy(a_weight.at[0, 0], weight_ref, sem).start()
 
-    count = jnp.where(is_atmos, m_count[0, 0], a_count[0, 0])
     pair = 2 * points
     row_iota = lax.broadcasted_iota(jnp.int32, (cells, points), 0)
     table = sum(surface[...].astype(f32) for surface in surfaces).astype(bf16)
@@ -338,7 +341,7 @@
         )
         for k in range(2):
             values = jnp.where(block_iota == b + k, terms[:, k * points : (k + 1) * points], values)
-    val_ref[...] = jnp.where(block_iota < count, values, 0.0)
+    val_ref[...] = jnp.where(used_ref[...] > 0, values, 0.0)
     land = jnp.zeros((2 * cells, LANES), f32)
     for b in range(0, blocks, 2):
         spread = []
@@ -725,6 +728,24 @@
         name="surface_and_forward_or_halos",
     )(fields, wet_cells, flux_row, diff_row, forward)
 
+    one_hots = pl.pallas_call(
+        functools.partial(one_hot_kernel, rows, columns),
+        out_shape=[
+            shape((LANES, blocks * points), bf16),
+            shape((LANES, blocks * points), bf16),
+            shape((blocks, points), jnp.int32),
+            shape((blocks, points), jnp.int32),
+            shape((blocks, points), jnp.int32),
+        ],
+        in_specs=[vmem, vmem, smem] * 2,
+        out_specs=[vmem] * 5,
+        compiler_params=params(),
+        name="one_hots",
+    )(
+        a2o_source, a2o_target, a2o_count,
+        marine_air_input_index, marine_air_output_index, marine_air_piece_tally,
+    )
+
     masks = [1 << bit for bit in range(groups_y.bit_length() - 1)]
 
     def sum_route(mask):
@@ -738,6 +759,8 @@
         far = lax.ppermute(wide, ("comp", "gy"), partner_route(mask))
         surface = surface + far[:cells].astype(f32)
     coarse = surface.astype(bf16)
+    *one_hots, used = one_hots
+    coarse, used = lax.optimization_barrier((coarse, used))
     for mask in masks[1:-1]:
         surface = surface + lax.ppermute(coarse, "gy", sum_route(mask)).astype(f32)
         coarse = surface.astype(bf16)
@@ -771,24 +794,11 @@
     e2 = lax.ppermute(e2, axes, level_route(0))
     e4 = lax.ppermute(e4, axes, level_route(1))
 
-    one_hots = pl.pallas_call(
-        functools.partial(one_hot_kernel, rows, columns),
-        out_shape=[
-            shape((LANES, blocks * points), bf16),
-            shape((LANES, blocks * points), bf16),
-            shape((blocks, points), jnp.int32),
-            shape((blocks, points), jnp.int32),
-        ],
-        in_specs=[vmem] * 4 + [anywhere],
-        out_specs=[vmem] * 4,
-        compiler_params=params(),
-        name="one_hots",
-    )(a2o_source, a2o_target, marine_air_input_index, marine_air_output_index, coarse)
     landing, *sent = pl.pallas_call(
         functools.partial(regrid_kernel, len(surfaces)),
         out_shape=[shape((cells, LANES), f32)]
         + [shape((cells + 16 * (mask - 1), LANES), bf16) for mask in range(1, groups_y)],
-        in_specs=[vmem] * (len(surfaces) + 4) + [smem, smem, hbm, hbm] + [anywhere] * 1,
+        in_specs=[vmem] * (len(surfaces) + 5) + [hbm, hbm] + [anywhere] * 1,
         out_specs=[vmem] * groups_y,
         scratch_shapes=[
             pltpu.VMEM((blocks, points, points), bf16),
@@ -797,11 +807,10 @@
             pltpu.SemaphoreType.DMA,
         ],
         compiler_params=params(),
-        cost_estimate=pl.CostEstimate(flops=int(2.0 * 1.1e9), bytes_accessed=0, transcendentals=0),
+        cost_estimate=pl.CostEstimate(flops=2_200_000_000, bytes_accessed=0, transcendentals=0),
         name="regrid_blocks",
     )(
-        *surfaces, *one_hots, a2o_count, marine_air_piece_tally,
-        a2o_weight, marine_air_piece_factor, e3,
+        *surfaces, *one_hots, used, a2o_weight, marine_air_piece_factor, e3,
     )
 
     def landing_route(mask):

time: 29.5 us -> 29.2 us (0.990)
  waiting for transfers between devices: 4.5 us -> 3.89 us
  starting transfers between devices: 15.1 us -> 15.5 us
    ppermute x1, waiting for transfers between devices: 2 us -> 0.05 us  [local(): surface = lax.ppermute(coarse, ('comp', 'gy'), partner_route(0)).astype(f32)]
    ppermute x3, waiting for transfers between devices: 1.01 us -> 2.34 us  [local(): lax.ppermute(block, axes, landing_route(mask))]
    ppermute x1, starting transfers between devices: 0.01 us -> 0.93 us  [local(): e1 = lax.ppermute(e1, 'gx', both_ways(ring_pairs(groups_x, 0)))]
    ppermute x1, starting transfers between devices: 1.49 us -> 0.56 us  [local(): e2 = lax.ppermute(e2, axes, level_route(0))]
    ppermute x1, waiting for transfers between devices: 0.01 us -> 0.34 us  [local(): lax.ppermute(coarse, 'gy', sum_route(mask))]
    ppermute x1, starting transfers between devices: 1.28 us -> 1.61 us  [local(): far = lax.ppermute(far, 'gx', both_ways(ring_pairs(groups_x, 1)))]
    ppermute x1, waiting for transfers between devices: 1.48 us -> 1.16 us  [local(): far = lax.ppermute(far, 'gx', both_ways(ring_pairs(groups_x, 1)))]
  transfers between devices with their start and end apart: 12 -> 12, of which waited for: 3 -> 4; matrix products, arithmetic and copies ran while one was open for 0% -> 0% of each run, Pallas kernels for 12% -> 12%
where the time goes in v18:
time: 29.2 us; the launch traced here: 29.1 us
  starting transfers between devices  15.5 us (53%)
  Pallas kernels  8.13 us (28%)
  waiting for transfers between devices  3.89 us (13%)
  between operations  1.5 us (5%)
    ppermute x3, starting transfers between devices, local(): lax.ppermute(block, axes, landing_route(mask))  4.45 us
    pallas_call x1, Pallas kernels, local(): pl.pallas_call(functools.partial(start_kernel, groups_x, paired), out_sha...  3.67 us
    ppermute x1, starting transfers between devices, local(): far = lax.ppermute(wide, ('comp', 'gy'), partner_route(mask))  3 us
    ppermute x1, starting transfers between devices, local(): lax.ppermute(coarse, 'gy', sum_route(mask))  2.65 us
    ppermute x3, waiting for transfers between devices, local(): lax.ppermute(block, axes, landing_route(mask))  2.34 us
    ppermute x1, starting transfers between devices, local(): far = lax.ppermute(far, 'gx', both_ways(ring_pairs(groups_x, 1)))  1.61 us
    ppermute x1, starting transfers between devices, local(): surface = lax.ppermute(coarse, ('comp', 'gy'), partner_route(0)).astype(f32)  1.58 us
    pallas_call x1, Pallas kernels, local(): pl.pallas_call(functools.partial(regrid_kernel, len(surfaces)), out_shape...  1.36 us
  transfers between devices with their start and end apart: 12, of which 4 were waited for; matrix products, arithmetic and copies ran while one was open for 0% of the time, Pallas kernels for 12%

profile of v18, /device:TPU:0, one launch (start us, length us, event | category | flops | bytes accessed | tf_op | source)
XLA Modules:
  0.0 29.1 jit_solution(13536407513149947684)
XLA Ops:
  0.0 0.0 copy-start.4
  0.0 0.0 copy-start.5
  0.0 0.0 copy-start.6
  0.0 0.0 copy-start.7
  0.0 0.0 copy-start.10
  0.0 0.0 copy-start.11
  0.0 3.7 %surface_and_forward_or_halos.1 = (bf16[64,128]{1,0:T(8,128)(2,1)}, bf16[80,128]{1,0:T(8,128)(2,1)}, f32[8,32,1024]{2,1,0:T(8,128)}, bf16[80,1024]{1,0:T(8,128)(...) custom-call(f32[1,8,32,1024]{3,2,1,0:T(8,128)} %x_ref.1, s32[8,1024]{1,0:T(8,128)} %wet_ref.1, ...), custom_call_target="tpu_custom_call" | custom-call | tf_op jit(solution)/shard_map/surface_and_forward_or_halos/pallas_call | solution.py:707
  3.7 3.0 %collective-permute-start.5 = (bf16[80,128]{1,0:T(8,128)(2,1)}, bf16[80,128]{1,0:T(8,128)(2,1)S(1)}, u32[]{:S(2)}, u32[]{:S(2)}) collective-permute-start(bf16[80,128]{1,0:T(8,128)(2,1)} %get-tuple-element.42), channel_id=1, source_target_pairs={{0,17},{17,0},{1,16},{16,1},{2,19},{19,2},{3,18},{18,3},{4,21},{21... | collective-permute-start | bytes 61448 | tf_op jit(solution)/shard_map/ppermute | solution.py:759
  6.7 1.6 %collective-permute-start.4 = (bf16[64,128]{1,0:T(8,128)(2,1)}, bf16[64,128]{1,0:T(8,128)(2,1)S(1)}, u32[]{:S(2)}, u32[]{:S(2)}) collective-permute-start(bf16[64,128]{1,0:T(8,128)(2,1)} %get-tuple-element.41), channel_id=1, source_target_pairs={{0,16},{16,0},{1,17},{17,1},{2,18},{18,2},{3,19},{19,3},{4,20},{20... | collective-permute-start | bytes 49160 | tf_op jit(solution)/shard_map/ppermute | solution.py:757
  8.3 0.4 %collective-permute-start.1 = (bf16[80,1024]{1,0:T(8,128)(2,1)}, bf16[80,1024]{1,0:T(8,128)(2,1)S(1)}, u32[]{:S(2)}, u32[]{:S(2)}) collective-permute-start(bf16[80,1024]{1,0:T(8,128)(2,1)} %get-tuple-element.33), channel_id=1, source_target_pairs={{4,8},{8,4},{12,0},{0,12},{5,9},{9,5},{13,1},{1,13},{6,10},{10,6},... | collective-permute-start | bytes 491528 | tf_op jit(solution)/shard_map/ppermute | solution.py:792
  10.0 0.0 copy-done.4
  10.0 0.0 copy-done.5
  10.0 0.0 copy-done.6
  10.0 0.0 copy-done.7
  10.0 0.6 %one_hots.1 = (bf16[128,4096]{1,0:T(8,128)(2,1)S(1)}, bf16[128,4096]{1,0:T(8,128)(2,1)S(1)}, s32[32,128]{1,0:T(8,128)S(1)}, s32[32,128]{1,0:T(8,128)S(1)}, s32[32,128]{1,0:T(8,128)S(1)}) custom-call(s32[1,1,32,128]{3,2,1,0:T(8,128)S(1)} %copy-done.4, s32[1,1,32,128]{3,2,1,0:T(8,128)S(1)} %copy-done.5, s32[1,1]{1,0:T(1,128)S(6)} %copy.16.a_count, ...), custom_call_target="tpu_custom_call" | custom-call | tf_op jit(solution)/shard_map/one_hots/pallas_call | solution.py:731
  10.6 0.0 collective-permute-done.4
  10.7 0.0 collective-permute-done.5
  10.7 2.7 %collective-permute-start.6 = (bf16[64,128]{1,0:T(8,128)(2,1)S(1)}, bf16[64,128]{1,0:T(8,128)(2,1)S(1)}, u32[]{:S(2)}, u32[]{:S(2)}) collective-permute-start(bf16[64,128]{1,0:T(8,128)(2,1)S(1)} %get-tuple-element.44), channel_id=1, source_target_pairs={{0,2},{1,3},{2,0},{3,1},{4,6},{5,7},{6,4},{7,5},{8,10},{9,11},{10,... | collective-permute-start | bytes 49160 | tf_op jit(solution)/shard_map/ppermute | solution.py:768
  13.3 0.9 %collective-permute-start = (bf16[80,1024]{1,0:T(8,128)(2,1)}, bf16[80,1024]{1,0:T(8,128)(2,1)S(1)}, u32[]{:S(2)}, u32[]{:S(2)}) collective-permute-start(bf16[80,1024]{1,0:T(8,128)(2,1)} %get-tuple-element.32), channel_id=1, source_target_pairs={{0,4},{4,0},{8,12},{12,8},{1,5},{5,1},{9,13},{13,9},{2,6},{6,2},{1... | collective-permute-start | bytes 491528 | tf_op jit(solution)/shard_map/ppermute | solution.py:791
  14.3 0.6 %collective-permute-start.2 = (bf16[32,1024]{1,0:T(8,128)(2,1)}, bf16[32,1024]{1,0:T(8,128)(2,1)S(1)}, u32[]{:S(2)}, u32[]{:S(2)}) collective-permute-start(bf16[32,1024]{1,0:T(8,128)(2,1)} %get-tuple-element.34), channel_id=1, source_target_pairs={{16,17},{17,16},{18,19},{19,18},{0,8},{8,0},{1,9},{9,1},{2,10},{10... | collective-permute-start | bytes 196616 | tf_op jit(solution)/shard_map/ppermute | solution.py:794
  14.8 0.2 collective-permute-start.3
  15.0 0.3 %collective-permute-done.6.refs_1_ = bf16[64,128]{1,0:T(8,128)(2,1)S(1)} collective-permute-done((bf16[64,128]{1,0:T(8,128)(2,1)S(1)}, bf16[64,128]{1,0:T(8,128)(2,1)S(1)}, u32[]{:S(2)}, u32[]{:S(2)}) %collective-permute-start.6) | collective-permute-done | bytes 16416 | tf_op jit(solution)/shard_map/ppermute | solution.py:768
  15.4 0.0 collective-permute-done.1.e3_ref.refs_9_
  15.4 0.0 copy-done.10
  15.4 0.0 copy-done.11
  15.4 0.0 copy-start
  15.4 0.0 copy-start.1
  15.4 0.0 copy-start.3
  15.4 0.0 copy-start.8
  15.4 1.4 %regrid_blocks.1 = (f32[64,128]{1,0:T(8,128)S(1)}, bf16[64,128]{1,0:T(8,128)(2,1)S(1)}, bf16[80,128]{1,0:T(8,128)(2,1)S(1)}, bf16[96,128]{1,0:T(8,128)(2,1)S(1)}) custom-call(f32[64,128]{1,0:T(8,128)S(1)} %get-tuple-element.58.refs_0_, bf16[64,128]{1,0:T(8,128)(2,1)S(1)} %collective-permute-done.6.refs_1_, bf16[128,4096]{1,0:T(8,128)(2,1)S(1)} %get-tuple-element.45.refs_2_, ...), custom_call_target="tpu_custom_call" | custom-call | flops 2200000000 | tf_op jit(solution)/shard_map/regrid_blocks/pallas_call | solution.py:797
  16.8 0.0 copy-start.2
  16.8 0.0 copy-start.9
  16.8 3.1 %collective-permute-start.9 = (bf16[96,128]{1,0:T(8,128)(2,1)S(1)}, bf16[96,128]{1,0:T(8,128)(2,1)S(1)}, u32[]{:S(2)}, u32[]{:S(2)}) collective-permute-start(bf16[96,128]{1,0:T(8,128)(2,1)S(1)} %get-tuple-element.53), channel_id=1, source_target_pairs={{0,3},{3,0},{1,2},{2,1},{4,7},{7,4},{5,6},{6,5},{8,11},{11,8},{9,1... | collective-permute-start | bytes 73736 | tf_op jit(solution)/shard_map/ppermute | solution.py:833
  20.0 0.0 collective-permute-start.8
  20.0 0.0 collective-permute-done.2.e2_ref
  20.0 1.3 %collective-permute-start.7 = (bf16[64,128]{1,0:T(8,128)(2,1)S(1)}, bf16[64,128]{1,0:T(8,128)(2,1)S(1)}, u32[]{:S(2)}, u32[]{:S(2)}) collective-permute-start(bf16[64,128]{1,0:T(8,128)(2,1)S(1)} %get-tuple-element.51), channel_id=1, source_target_pairs={{0,1},{1,0},{2,3},{3,2},{4,5},{5,4},{6,7},{7,6},{8,9},{9,8},{10,11... | collective-permute-start | bytes 49160 | tf_op jit(solution)/shard_map/ppermute | solution.py:833
  21.3 0.0 collective-permute-done.3.e4_ref
  21.3 0.0 collective-permute-done.e1_ref
  21.3 0.0 copy-done
  21.3 0.0 copy-done.1
  21.3 0.0 copy-done.3
  21.3 0.0 copy-done.8
  21.3 1.0 %damping_or_first_step.1 = (bf16[256,1024]{1,0:T(8,128)(2,1)S(1)}, f32[7,16,1024]{2,1,0:T(8,128)S(1)}, f32[10,2,24,1024]{3,2,1,0:T(8,128)S(1)}) custom-call(f32[1,8,32,1024]{3,2,1,0:T(8,128)S(1)} %copy-done, s32[8,1024]{1,0:T(8,128)S(1)} %copy-done.3, f32[1,128]{1,0:T(1,128)S(1)} %bitcast.4, f32[8,32,1024]{2,1,0:T(8,128)S(1)} %copy-done.1, ...), custom_call_target="tpu_custom_call" | custom-call | tf_op jit(solution)/shard_map/damping_or_first_step/pallas_call | solution.py:853
  22.3 1.4 %collective-permute-done.7.refs_0_ = bf16[64,128]{1,0:T(8,128)(2,1)S(1)} collective-permute-done((bf16[64,128]{1,0:T(8,128)(2,1)S(1)}, bf16[64,128]{1,0:T(8,128)(2,1)S(1)}, u32[]{:S(2)}, u32[]{:S(2)}) %collective-permute-start.7) | collective-permute-done | bytes 16416 | tf_op jit(solution)/shard_map/ppermute | solution.py:833
  23.7 0.9 %collective-permute-done.8.refs_1_ = bf16[80,128]{1,0:T(8,128)(2,1)S(1)} collective-permute-done((bf16[80,128]{1,0:T(8,128)(2,1)S(1)}, bf16[80,128]{1,0:T(8,128)(2,1)S(1)}, u32[]{:S(2)}, u32[]{:S(2)}) %collective-permute-start.8) | collective-permute-done | bytes 20512 | tf_op jit(solution)/shard_map/ppermute | solution.py:833
  24.6 0.0 collective-permute-done.9.refs_2_
  24.7 0.1 collective-permute-start.10
  24.8 1.6 %collective-permute-start.11 = (bf16[64,128]{1,0:T(8,128)(2,1)S(1)}, bf16[64,128]{1,0:T(8,128)(2,1)S(1)}, u32[]{:S(2)}, u32[]{:S(2)}) collective-permute-start(bf16[64,128]{1,0:T(8,128)(2,1)S(1)} %get-tuple-element.56), channel_id=1, source_target_pairs={{4,8},{8,4},{12,0},{0,12},{5,9},{9,5},{13,1},{1,13},{6,10},{10,6},... | collective-permute-start | bytes 49160 | tf_op jit(solution)/shard_map/ppermute | solution.py:885
  26.4 0.0 copy-done.2
  26.4 0.0 copy-done.9
  26.4 0.4 %inverse_or_second_step.1 = (f32[8,32,1024]{2,1,0:T(8,128)S(1)}, f32[32,128]{1,0:T(8,128)S(1)}) custom-call(f32[1,128]{1,0:T(1,128)S(1)} %bitcast.5, bf16[1024,512]{1,0:T(8,128)(2,1)S(1)} %copy-done.2, bf16[256,1024]{1,0:T(8,128)(2,1)S(1)} %get-tuple-element.36.zb_ref, f32[7,16,1024]{2,1,0:T(8,128)S(1)} %get-tuple-element.37.c_ref._, ...), custom_call_target="tpu_custom_call" | custom-call | tf_op jit(solution)/shard_map/inverse_or_second_step/pallas_call | solution.py:886
  26.8 0.0 collective-permute-done.10.near_ref
  26.9 1.2 %collective-permute-done.11.far_ref = bf16[64,128]{1,0:T(8,128)(2,1)S(1)} collective-permute-done((bf16[64,128]{1,0:T(8,128)(2,1)S(1)}, bf16[64,128]{1,0:T(8,128)(2,1)S(1)}, u32[]{:S(2)}, u32[]{:S(2)}) %collective-permute-start.11) | collective-permute-done | bytes 16416 | tf_op jit(solution)/shard_map/ppermute | solution.py:885
  28.0 1.0 %add_surface_terms.1 = f32[1,8,32,1024]{3,2,1,0:T(8,128)} custom-call(f32[32,128]{1,0:T(8,128)S(1)} %get-tuple-element.39.column_ref, f32[8,32,1024]{2,1,0:T(8,128)S(1)} %get-tuple-element.40.base_ref, f32[7,16,1024]{2,1,0:T(8,128)S(1)} %get-tuple-element.37.c_ref._, f32[64,128]{1,0:T(8,128)S(1)} %get-tuple-element.54.sum_ref, ...), custom_call_target="tpu_custom_call" | custom-call | tf_op jit(solution)/shard_map/add_surface_terms/pallas_call | solution.py:894
  (2 shorter events, 0.1 us)
Async XLA Ops:
  0.0 10.0 %copy-start.4 = (s32[1,1,32,128]{3,2,1,0:T(8,128)S(1)}, s32[1,1,32,128]{3,2,1,0:T(8,128)}, u32[]{:S(2)}) copy-start(s32[1,1,32,128]{3,2,1,0:T(8,128)} %a_src.1) | copy-start | bytes 49156
  0.0 10.0 %copy-start.5 = (s32[1,1,32,128]{3,2,1,0:T(8,128)S(1)}, s32[1,1,32,128]{3,2,1,0:T(8,128)}, u32[]{:S(2)}) copy-start(s32[1,1,32,128]{3,2,1,0:T(8,128)} %a_dst.1) | copy-start | bytes 49156
  0.0 10.0 %copy-start.6 = (s32[1,1,32,128]{3,2,1,0:T(8,128)S(1)}, s32[1,1,32,128]{3,2,1,0:T(8,128)}, u32[]{:S(2)}) copy-start(s32[1,1,32,128]{3,2,1,0:T(8,128)} %m_src.1) | copy-start | bytes 49156
  0.0 10.0 %copy-start.7 = (s32[1,1,32,128]{3,2,1,0:T(8,128)S(1)}, s32[1,1,32,128]{3,2,1,0:T(8,128)}, u32[]{:S(2)}) copy-start(s32[1,1,32,128]{3,2,1,0:T(8,128)} %m_dst.1) | copy-start | bytes 49156
  0.0 15.4 %copy-start.10 = (bf16[1,1,32,128,128]{4,3,2,1,0:T(8,128)(2,1)S(1)}, bf16[1,1,32,128,128]{4,3,2,1,0:T(8,128)(2,1)}, u32[]{:S(2)}) copy-start(bf16[1,1,32,128,128]{4,3,2,1,0:T(8,128)(2,1)} %refs_7_.1) | copy-start | bytes 3145732
  0.0 15.4 %copy-start.11 = (bf16[1,1,32,128,128]{4,3,2,1,0:T(8,128)(2,1)S(1)}, bf16[1,1,32,128,128]{4,3,2,1,0:T(8,128)(2,1)}, u32[]{:S(2)}) copy-start(bf16[1,1,32,128,128]{4,3,2,1,0:T(8,128)(2,1)} %refs_8_.1) | copy-start | bytes 3145732
  3.7 7.0 %collective-permute-start.5 = (bf16[80,128]{1,0:T(8,128)(2,1)}, bf16[80,128]{1,0:T(8,128)(2,1)S(1)}, u32[]{:S(2)}, u32[]{:S(2)}) collective-permute-start(bf16[80,128]{1,0:T(8,128)(2,1)} %get-tuple-element.42), channel_id=1, source_target_pairs={{0,17},{17,0},{1,16},{16,1},{2,19},{19,2},{3,18},{18,3},{4,21},{21... | collective-permute-start | bytes 61448 | tf_op jit(solution)/shard_map/ppermute | solution.py:759
  6.7 3.9 %collective-permute-start.4 = (bf16[64,128]{1,0:T(8,128)(2,1)}, bf16[64,128]{1,0:T(8,128)(2,1)S(1)}, u32[]{:S(2)}, u32[]{:S(2)}) collective-permute-start(bf16[64,128]{1,0:T(8,128)(2,1)} %get-tuple-element.41), channel_id=1, source_target_pairs={{0,16},{16,0},{1,17},{17,1},{2,18},{18,2},{3,19},{19,3},{4,20},{20... | collective-permute-start | bytes 49160 | tf_op jit(solution)/shard_map/ppermute | solution.py:757
  8.3 7.1 %collective-permute-start.1 = (bf16[80,1024]{1,0:T(8,128)(2,1)}, bf16[80,1024]{1,0:T(8,128)(2,1)S(1)}, u32[]{:S(2)}, u32[]{:S(2)}) collective-permute-start(bf16[80,1024]{1,0:T(8,128)(2,1)} %get-tuple-element.33), channel_id=1, source_target_pairs={{4,8},{8,4},{12,0},{0,12},{5,9},{9,5},{13,1},{1,13},{6,10},{10,6},... | collective-permute-start | bytes 491528 | tf_op jit(solution)/shard_map/ppermute | solution.py:792
  10.7 4.7 %collective-permute-start.6 = (bf16[64,128]{1,0:T(8,128)(2,1)S(1)}, bf16[64,128]{1,0:T(8,128)(2,1)S(1)}, u32[]{:S(2)}, u32[]{:S(2)}) collective-permute-start(bf16[64,128]{1,0:T(8,128)(2,1)S(1)} %get-tuple-element.44), channel_id=1, source_target_pairs={{0,2},{1,3},{2,0},{3,1},{4,6},{5,7},{6,4},{7,5},{8,10},{9,11},{10,... | collective-permute-start | bytes 49160 | tf_op jit(solution)/shard_map/ppermute | solution.py:768
  13.3 8.0 %collective-permute-start = (bf16[80,1024]{1,0:T(8,128)(2,1)}, bf16[80,1024]{1,0:T(8,128)(2,1)S(1)}, u32[]{:S(2)}, u32[]{:S(2)}) collective-permute-start(bf16[80,1024]{1,0:T(8,128)(2,1)} %get-tuple-element.32), channel_id=1, source_target_pairs={{0,4},{4,0},{8,12},{12,8},{1,5},{5,1},{9,13},{13,9},{2,6},{6,2},{1... | collective-permute-start | bytes 491528 | tf_op jit(solution)/shard_map/ppermute | solution.py:791
  14.3 5.7 %collective-permute-start.2 = (bf16[32,1024]{1,0:T(8,128)(2,1)}, bf16[32,1024]{1,0:T(8,128)(2,1)S(1)}, u32[]{:S(2)}, u32[]{:S(2)}) collective-permute-start(bf16[32,1024]{1,0:T(8,128)(2,1)} %get-tuple-element.34), channel_id=1, source_target_pairs={{16,17},{17,16},{18,19},{19,18},{0,8},{8,0},{1,9},{9,1},{2,10},{10... | collective-permute-start | bytes 196616 | tf_op jit(solution)/shard_map/ppermute | solution.py:794
  14.8 6.5 %collective-permute-start.3 = (bf16[32,1024]{1,0:T(8,128)(2,1)}, bf16[32,1024]{1,0:T(8,128)(2,1)S(1)}, u32[]{:S(2)}, u32[]{:S(2)}) collective-permute-start(bf16[32,1024]{1,0:T(8,128)(2,1)} %get-tuple-element.35), channel_id=1, source_target_pairs={{17,18},{18,17},{16,20},{20,16},{19,23},{23,19},{0,4},{4,0},{1,5},... | collective-permute-start | bytes 196616 | tf_op jit(solution)/shard_map/ppermute | solution.py:795
  15.4 5.9 %copy-start = (f32[1,8,32,1024]{3,2,1,0:T(8,128)S(1)}, f32[1,8,32,1024]{3,2,1,0:T(8,128)}, u32[]{:S(2)}) copy-start(f32[1,8,32,1024]{3,2,1,0:T(8,128)} %x_ref.1) | copy-start | bytes 3145732
  15.4 5.9 %copy-start.1 = (f32[8,32,1024]{2,1,0:T(8,128)S(1)}, f32[8,32,1024]{2,1,0:T(8,128)}, u32[]{:S(2)}) copy-start(f32[8,32,1024]{2,1,0:T(8,128)} %get-tuple-element.31.y_ref) | copy-start | bytes 3145732
  15.4 5.9 %copy-start.3 = (s32[8,1024]{1,0:T(8,128)S(1)}, s32[8,1024]{1,0:T(8,128)}, u32[]{:S(2)}) copy-start(s32[8,1024]{1,0:T(8,128)} %wet_ref.1) | copy-start | bytes 98308
  15.4 5.9 %copy-start.8 = (f32[128]{0:T(128)S(1)}, f32[128]{0:T(128)}, u32[]{:S(2)}) copy-start(f32[128]{0:T(128)} %param.19) | copy-start | bytes 1540
  16.8 9.6 %copy-start.2 = (bf16[1024,512]{1,0:T(8,128)(2,1)S(1)}, bf16[1024,512]{1,0:T(8,128)(2,1)}, u32[]{:S(2)}) copy-start(bf16[1024,512]{1,0:T(8,128)(2,1)} %constant.5.clone.table_ref) | copy-start | bytes 3145732
  16.8 9.6 %copy-start.9 = (f32[128]{0:T(128)S(1)}, f32[128]{0:T(128)}, u32[]{:S(2)}) copy-start(f32[128]{0:T(128)} %param.18) | copy-start | bytes 1540
  16.8 7.8 %collective-permute-start.9 = (bf16[96,128]{1,0:T(8,128)(2,1)S(1)}, bf16[96,128]{1,0:T(8,128)(2,1)S(1)}, u32[]{:S(2)}, u32[]{:S(2)}) collective-permute-start(bf16[96,128]{1,0:T(8,128)(2,1)S(1)} %get-tuple-element.53), channel_id=1, source_target_pairs={{0,3},{3,0},{1,2},{2,1},{4,7},{7,4},{5,6},{6,5},{8,11},{11,8},{9,1... | collective-permute-start | bytes 73736 | tf_op jit(solution)/shard_map/ppermute | solution.py:833
  20.0 4.7 %collective-permute-start.8 = (bf16[80,128]{1,0:T(8,128)(2,1)S(1)}, bf16[80,128]{1,0:T(8,128)(2,1)S(1)}, u32[]{:S(2)}, u32[]{:S(2)}) collective-permute-start(bf16[80,128]{1,0:T(8,128)(2,1)S(1)} %get-tuple-element.52), channel_id=1, source_target_pairs={{0,2},{2,0},{1,3},{3,1},{4,6},{6,4},{5,7},{7,5},{8,10},{10,8},{9,1... | collective-permute-start | bytes 61448 | tf_op jit(solution)/shard_map/ppermute | solution.py:833
  20.0 3.7 %collective-permute-start.7 = (bf16[64,128]{1,0:T(8,128)(2,1)S(1)}, bf16[64,128]{1,0:T(8,128)(2,1)S(1)}, u32[]{:S(2)}, u32[]{:S(2)}) collective-permute-start(bf16[64,128]{1,0:T(8,128)(2,1)S(1)} %get-tuple-element.51), channel_id=1, source_target_pairs={{0,1},{1,0},{2,3},{3,2},{4,5},{5,4},{6,7},{7,6},{8,9},{9,8},{10,11... | collective-permute-start | bytes 49160 | tf_op jit(solution)/shard_map/ppermute | solution.py:833
  24.7 2.1 %collective-permute-start.10 = (bf16[64,128]{1,0:T(8,128)(2,1)S(1)}, bf16[64,128]{1,0:T(8,128)(2,1)S(1)}, u32[]{:S(2)}, u32[]{:S(2)}) collective-permute-start(bf16[64,128]{1,0:T(8,128)(2,1)S(1)} %get-tuple-element.55), channel_id=1, source_target_pairs={{0,4},{4,0},{8,12},{12,8},{1,5},{5,1},{9,13},{13,9},{2,6},{6,2},{1... | collective-permute-start | bytes 49160 | tf_op jit(solution)/shard_map/ppermute | solution.py:884
  24.8 3.2 %collective-permute-start.11 = (bf16[64,128]{1,0:T(8,128)(2,1)S(1)}, bf16[64,128]{1,0:T(8,128)(2,1)S(1)}, u32[]{:S(2)}, u32[]{:S(2)}) collective-permute-start(bf16[64,128]{1,0:T(8,128)(2,1)S(1)} %get-tuple-element.56), channel_id=1, source_target_pairs={{4,8},{8,4},{12,0},{0,12},{5,9},{9,5},{13,1},{1,13},{6,10},{10,6},... | collective-permute-start | bytes 49160 | tf_op jit(solution)/shard_map/ppermute | solution.py:885

commit v19 on v18

--- a/solution.py
+++ b/solution.py
@@ -102,12 +102,20 @@
     return lows, highs
 
 
+def fold(values, flat_ref, r):
+    channels, columns = values.shape
+    half = columns // 2
+    left, right = values[:, :half], values[:, half:]
+    flat_ref[r * channels : (r + 1) * channels, :half] = (left + right).astype(bf16)
+    flat_ref[r * channels : (r + 1) * channels, half:] = (left - right).astype(bf16)
+
+
 def start_kernel(
     groups_x, paired, x_hbm, wet_hbm, flux_hbm, diff_hbm, table_hbm, *refs
 ):
-    outs = 7 if paired else 8
-    coarse_hbm, wide_hbm, y_hbm, *message_hbm = refs[:outs]
-    coarse_ref, wide_ref, y_ref, *message_ref = refs[outs : 2 * outs]
+    outs = 6 if paired else 7
+    coarse_hbm, wide_hbm, *message_hbm = refs[:outs]
+    coarse_ref, wide_ref, *message_ref = refs[outs : 2 * outs]
     e1_ref, e3_ref, e2_ref, e4_ref = message_ref[:4]
     if not paired:
         pq_ref = message_ref[4]
@@ -128,11 +136,8 @@
         pltpu.make_async_copy(coarse_ref, coarse_hbm, out_sem.at[0]),
         pltpu.make_async_copy(wide_ref, wide_hbm, out_sem.at[1]),
     ]
-    y_copies = [
-        pltpu.make_async_copy(y_ref.at[r], y_hbm.at[r], out_sem.at[2 + r]) for r in range(rows)
-    ]
     message_copies = [
-        pltpu.make_async_copy(ref, hbm, out_sem.at[2 + rows + k])
+        pltpu.make_async_copy(ref, hbm, out_sem.at[2 + k])
         for k, (ref, hbm) in enumerate(zip(message_ref, message_hbm))
     ]
 
@@ -168,9 +173,7 @@
         for r in range(rows):
             x_copies[r].wait()
             row_ref[r : r + 1, :] = jnp.sum(x_ref[r] * weight, axis=0, keepdims=True)
-            left, right = x_ref[r, :, :half], x_ref[r, :, half:]
-            flat_ref[r * channels : (r + 1) * channels, :half] = (left + right).astype(bf16)
-            flat_ref[r * channels : (r + 1) * channels, half:] = (left - right).astype(bf16)
+            fold(x_ref[r], flat_ref, r)
         send_surface()
         table_copy.wait()
         for k in range(2):
@@ -178,7 +181,6 @@
             part = jnp.dot(
                 flat_ref[:, lanes], table_ref[lanes, :], preferred_element_type=f32
             )
-            y_ref[:, :, lanes] = part.reshape(rows, channels, half)
             for tile, (group, _, parts) in enumerate(tiles):
                 if group != k:
                     continue
@@ -200,11 +202,19 @@
                     else:
                         pq_ref[0, :, lanes] = p.astype(bf16)
                         pq_ref[1, :, lanes] = q.astype(bf16)
-        for copy in y_copies:
+        sums_copies = [
+            pltpu.make_async_copy(
+                message_ref[k].at[pl.ds(0, channels)],
+                message_hbm[k].at[pl.ds(0, channels)],
+                out_sem.at[2 + k],
+            )
+            for k in range(3)
+        ]
+        if not paired:
+            sums_copies = message_copies[4:]
+        for copy in sums_copies:
             copy.start()
-        for copy in message_copies:
-            copy.start()
-        for copy in surface_copies + y_copies + message_copies:
+        for copy in surface_copies + sums_copies:
             copy.wait()
 
     @pl.when(jnp.logical_not(is_atmos))
@@ -410,12 +420,12 @@
 
 
 def first_step_kernel(
-    groups_x, groups_y, paired, x_ref, wet_ref, diff_ref, y_ref, e1_ref, e3_ref,
+    groups_x, groups_y, paired, x_ref, wet_ref, diff_ref, table_ref, e1_ref, e3_ref,
     e2_ref, e4_ref, *refs,
 ):
     if not paired:
         pin_ref, qin_ref = refs[:2]
-    zb_ref, c_ref, t1_ref, z_ref, t0_ref, w_ref = refs[-6:]
+    zb_ref, c_ref, t1_ref, y_ref, flat_ref, z_ref, t0_ref, w_ref = refs[-8:]
     _, rows, channels, columns = x_ref.shape
     row_group = lax.axis_index("gx")
     col_group = lax.axis_index("gy")
@@ -423,6 +433,15 @@
 
     @pl.when(is_atmos)
     def _():
+        half = columns // 2
+        for r in range(rows):
+            fold(x_ref[0, r], flat_ref, r)
+        for k in range(2):
+            lanes = slice(k * half, (k + 1) * half)
+            part = jnp.dot(
+                flat_ref[:, lanes], table_ref[lanes, :], preferred_element_type=f32
+            )
+            y_ref[:, :, lanes] = part.reshape(rows, channels, half)
         diff = channel_column(diff_ref[...], channels, col_group * channels)
         total = rows * groups_x
         base = (row_group * rows).astype(f32)
@@ -696,7 +715,6 @@
     shapes = [
         shape((cells, LANES), bf16),
         shape((cells + 16, LANES), bf16),
-        shape((rows, channels, columns), f32),
         shape((lines, columns), bf16),
         shape((lines, columns), bf16),
         shape((4 * rows, columns), bf16),
@@ -704,7 +722,7 @@
     ]
     if not paired:
         shapes.append(shape((2, channels, columns), bf16))
-    coarse, wide, y, e1, e3, e2, e4, *sums = pl.pallas_call(
+    coarse, wide, e1, e3, e2, e4, *sums = pl.pallas_call(
         functools.partial(start_kernel, groups_x, paired),
         out_shape=shapes,
         in_specs=[hbm] * 5,
@@ -722,7 +740,7 @@
             pltpu.VMEM((columns // 2 // LANES, 2 * rows + 1, channels, LANES), f32),
             pltpu.SemaphoreType.DMA((rows,)),
             pltpu.SemaphoreType.DMA((3,)),
-            pltpu.SemaphoreType.DMA((rows + len(shapes) - 1,)),
+            pltpu.SemaphoreType.DMA((len(shapes),)),
         ],
         compiler_params=pltpu.CompilerParams(vmem_limit_bytes=58 * 2**20),
         name="surface_and_forward_or_halos",
@@ -860,13 +878,15 @@
         in_specs=[vmem] * (8 + len(extra)),
         out_specs=[vmem] * 3,
         scratch_shapes=[
+            pltpu.VMEM((rows, channels, columns), f32),
+            pltpu.VMEM((rows * channels, columns), bf16),
             pltpu.VMEM((rows, channels, LANES), f32),
             pltpu.VMEM((rows + 4, 2, ring, columns), f32),
             pltpu.VMEM((16, columns), f32),
         ],
         compiler_params=params(),
         name="damping_or_first_step",
-    )(fields, wet_cells, diff_row, y, e1, e3, e2, e4, *extra)
+    )(fields, wet_cells, diff_row, forward, e1, e3, e2, e4, *extra)
 
     surface_sum, near, far = pl.pallas_call(
         functools.partial(heat_kernel, rows),

time: 29.2 us -> 28.9 us (0.990)
  Pallas kernels: 8.13 us -> 7.62 us
    ppermute x1, starting transfers between devices: 0.56 us -> 1.49 us  [local(): e2 = lax.ppermute(e2, axes, level_route(0))]
    pallas_call x1, Pallas kernels: 3.67 us -> 3.21 us  [local(): pl.pallas_call(functools.partial(start_kernel, groups_x, paired), out_sha...]
    ppermute x3, waiting for transfers between devices: 2.34 us -> 1.89 us  [local(): lax.ppermute(block, axes, landing_route(mask))]
    ppermute x1, starting transfers between devices: 0.93 us -> 0.51 us  [local(): e1 = lax.ppermute(e1, 'gx', both_ways(ring_pairs(groups_x, 0)))]
    ppermute x1, starting transfers between devices: 1.58 us -> 1.21 us  [local(): surface = lax.ppermute(coarse, ('comp', 'gy'), partner_route(0)).astype(f32)]
    ppermute x1, waiting for transfers between devices: 0.05 us -> 0.42 us  [local(): surface = lax.ppermute(coarse, ('comp', 'gy'), partner_route(0)).astype(f32)]
    ppermute x1, starting transfers between devices: 3 us -> 3.37 us  [local(): far = lax.ppermute(wide, ('comp', 'gy'), partner_route(mask))]
  transfers between devices with their start and end apart: 12 -> 12, of which waited for: 4 -> 5; matrix products, arithmetic and copies ran while one was open for 0% -> 0% of each run, Pallas kernels for 12% -> 12%
where the time goes in v19:
time: 28.9 us; the launch traced here: 28.7 us
  starting transfers between devices  15.7 us (54%)
  Pallas kernels  7.62 us (26%)
  waiting for transfers between devices  3.85 us (13%)
  between operations  1.5 us (5%)
    ppermute x3, starting transfers between devices, local(): lax.ppermute(block, axes, landing_route(mask))  4.45 us
    ppermute x1, starting transfers between devices, local(): far = lax.ppermute(wide, ('comp', 'gy'), partner_route(mask))  3.37 us
    pallas_call x1, Pallas kernels, local(): pl.pallas_call(functools.partial(start_kernel, groups_x, paired), out_sha...  3.21 us
    ppermute x1, starting transfers between devices, local(): lax.ppermute(coarse, 'gy', sum_route(mask))  2.65 us
    ppermute x3, waiting for transfers between devices, local(): lax.ppermute(block, axes, landing_route(mask))  1.89 us
    ppermute x1, starting transfers between devices, local(): far = lax.ppermute(far, 'gx', both_ways(ring_pairs(groups_x, 1)))  1.56 us
    ppermute x1, starting transfers between devices, local(): e2 = lax.ppermute(e2, axes, level_route(0))  1.49 us
    pallas_call x1, Pallas kernels, local(): pl.pallas_call(functools.partial(regrid_kernel, len(surfaces)), out_shape...  1.36 us
  transfers between devices with their start and end apart: 12, of which 5 were waited for; matrix products, arithmetic and copies ran while one was open for 0% of the time, Pallas kernels for 12%

profile of v19, /device:TPU:0, one launch (start us, length us, event | category | flops | bytes accessed | tf_op | source)
XLA Modules:
  0.0 28.7 jit_solution(10805124604080405926)
XLA Ops:
  0.0 0.0 copy-start.7
  0.0 0.0 copy-start.6
  0.0 0.0 copy-start.5
  0.0 0.0 copy-start.4
  0.0 0.0 copy-start.11
  0.0 0.0 copy-start.10
  0.0 3.2 %surface_and_forward_or_halos.1 = (bf16[64,128]{1,0:T(8,128)(2,1)}, bf16[80,128]{1,0:T(8,128)(2,1)}, bf16[80,1024]{1,0:T(8,128)(2,1)}, bf16[80,1024]{1,0:T(8,128...) custom-call(f32[1,8,32,1024]{3,2,1,0:T(8,128)} %x_ref.1, s32[8,1024]{1,0:T(8,128)} %wet_ref.1, ...), custom_call_target="tpu_custom_call" | custom-call | tf_op jit(solution)/shard_map/surface_and_forward_or_halos/pallas_call | solution.py:725
  3.2 3.4 %collective-permute-start.5 = (bf16[80,128]{1,0:T(8,128)(2,1)}, bf16[80,128]{1,0:T(8,128)(2,1)S(1)}, u32[]{:S(2)}, u32[]{:S(2)}) collective-permute-start(bf16[80,128]{1,0:T(8,128)(2,1)} %get-tuple-element.40), channel_id=1, source_target_pairs={{0,17},{17,0},{1,16},{16,1},{2,19},{19,2},{3,18},{18,3},{4,21},{21... | collective-permute-start | bytes 61448 | tf_op jit(solution)/shard_map/ppermute | solution.py:777
  6.6 1.2 %collective-permute-start.4 = (bf16[64,128]{1,0:T(8,128)(2,1)}, bf16[64,128]{1,0:T(8,128)(2,1)S(1)}, u32[]{:S(2)}, u32[]{:S(2)}) collective-permute-start(bf16[64,128]{1,0:T(8,128)(2,1)} %get-tuple-element.39), channel_id=1, source_target_pairs={{0,16},{16,0},{1,17},{17,1},{2,18},{18,2},{3,19},{19,3},{4,20},{20... | collective-permute-start | bytes 49160 | tf_op jit(solution)/shard_map/ppermute | solution.py:775
  7.8 0.4 %collective-permute-start.1 = (bf16[80,1024]{1,0:T(8,128)(2,1)}, bf16[80,1024]{1,0:T(8,128)(2,1)S(1)}, u32[]{:S(2)}, u32[]{:S(2)}) collective-permute-start(bf16[80,1024]{1,0:T(8,128)(2,1)} %get-tuple-element.31), channel_id=1, source_target_pairs={{4,8},{8,4},{12,0},{0,12},{5,9},{9,5},{13,1},{1,13},{6,10},{10,6},... | collective-permute-start | bytes 491528 | tf_op jit(solution)/shard_map/ppermute | solution.py:810
  9.5 0.0 copy-done.7
  9.5 0.0 copy-done.6
  9.5 0.0 copy-done.5
  9.5 0.0 copy-done.4
  9.5 0.6 %one_hots.1 = (bf16[128,4096]{1,0:T(8,128)(2,1)S(1)}, bf16[128,4096]{1,0:T(8,128)(2,1)S(1)}, s32[32,128]{1,0:T(8,128)S(1)}, s32[32,128]{1,0:T(8,128)S(1)}, s32[32,128]{1,0:T(8,128)S(1)}) custom-call(s32[1,1,32,128]{3,2,1,0:T(8,128)S(1)} %copy-done.4, s32[1,1,32,128]{3,2,1,0:T(8,128)S(1)} %copy-done.5, s32[1,1]{1,0:T(1,128)S(6)} %copy.16.a_count, ...), custom_call_target="tpu_custom_call" | custom-call | tf_op jit(solution)/shard_map/one_hots/pallas_call | solution.py:749
  10.1 0.4 %collective-permute-done.4 = bf16[64,128]{1,0:T(8,128)(2,1)S(1)} collective-permute-done((bf16[64,128]{1,0:T(8,128)(2,1)}, bf16[64,128]{1,0:T(8,128)(2,1)S(1)}, u32[]{:S(2)}, u32[]{:S(2)}) %collective-permute-start.4) | collective-permute-done | bytes 16416 | tf_op jit(solution)/shard_map/ppermute | solution.py:775
  10.6 0.0 collective-permute-done.5
  10.6 2.7 %collective-permute-start.6 = (bf16[64,128]{1,0:T(8,128)(2,1)S(1)}, bf16[64,128]{1,0:T(8,128)(2,1)S(1)}, u32[]{:S(2)}, u32[]{:S(2)}) collective-permute-start(bf16[64,128]{1,0:T(8,128)(2,1)S(1)} %get-tuple-element.42), channel_id=1, source_target_pairs={{0,2},{1,3},{2,0},{3,1},{4,6},{5,7},{6,4},{7,5},{8,10},{9,11},{10,... | collective-permute-start | bytes 49160 | tf_op jit(solution)/shard_map/ppermute | solution.py:786
  13.2 1.5 %collective-permute-start.2 = (bf16[32,1024]{1,0:T(8,128)(2,1)}, bf16[32,1024]{1,0:T(8,128)(2,1)S(1)}, u32[]{:S(2)}, u32[]{:S(2)}) collective-permute-start(bf16[32,1024]{1,0:T(8,128)(2,1)} %get-tuple-element.32), channel_id=1, source_target_pairs={{16,17},{17,16},{18,19},{19,18},{0,8},{8,0},{1,9},{9,1},{2,10},{10... | collective-permute-start | bytes 196616 | tf_op jit(solution)/shard_map/ppermute | solution.py:812
  14.7 0.0 collective-permute-start.3
  14.7 0.5 %collective-permute-start = (bf16[80,1024]{1,0:T(8,128)(2,1)}, bf16[80,1024]{1,0:T(8,128)(2,1)S(1)}, u32[]{:S(2)}, u32[]{:S(2)}) collective-permute-start(bf16[80,1024]{1,0:T(8,128)(2,1)} %get-tuple-element.30), channel_id=1, source_target_pairs={{0,4},{4,0},{8,12},{12,8},{1,5},{5,1},{9,13},{13,9},{2,6},{6,2},{1... | collective-permute-start | bytes 491528 | tf_op jit(solution)/shard_map/ppermute | solution.py:809
  15.2 0.3 %collective-permute-done.6.refs_1_ = bf16[64,128]{1,0:T(8,128)(2,1)S(1)} collective-permute-done((bf16[64,128]{1,0:T(8,128)(2,1)S(1)}, bf16[64,128]{1,0:T(8,128)(2,1)S(1)}, u32[]{:S(2)}, u32[]{:S(2)}) %collective-permute-start.6) | collective-permute-done | bytes 16416 | tf_op jit(solution)/shard_map/ppermute | solution.py:786
  15.6 0.0 collective-permute-done.1.e3_ref.refs_9_
  15.6 0.0 copy-done.11
  15.6 0.0 copy-done.10
  15.6 0.0 copy-start
  15.6 0.0 copy-start.1
  15.6 0.0 copy-start.3
  15.6 0.0 copy-start.8
  15.6 1.4 %regrid_blocks.1 = (f32[64,128]{1,0:T(8,128)S(1)}, bf16[64,128]{1,0:T(8,128)(2,1)S(1)}, bf16[80,128]{1,0:T(8,128)(2,1)S(1)}, bf16[96,128]{1,0:T(8,128)(2,1)S(1)}) custom-call(f32[64,128]{1,0:T(8,128)S(1)} %get-tuple-element.56.refs_0_, bf16[64,128]{1,0:T(8,128)(2,1)S(1)} %collective-permute-done.6.refs_1_, bf16[128,4096]{1,0:T(8,128)(2,1)S(1)} %get-tuple-element.43.refs_2_, ...), custom_call_target="tpu_custom_call" | custom-call | flops 2200000000 | tf_op jit(solution)/shard_map/regrid_blocks/pallas_call | solution.py:815
  17.0 0.0 copy-start.2
  17.0 0.0 copy-start.9
  17.0 2.5 %collective-permute-start.9 = (bf16[96,128]{1,0:T(8,128)(2,1)S(1)}, bf16[96,128]{1,0:T(8,128)(2,1)S(1)}, u32[]{:S(2)}, u32[]{:S(2)}) collective-permute-start(bf16[96,128]{1,0:T(8,128)(2,1)S(1)} %get-tuple-element.51), channel_id=1, source_target_pairs={{0,3},{3,0},{1,2},{2,1},{4,7},{7,4},{5,6},{6,5},{8,11},{11,8},{9,1... | collective-permute-start | bytes 73736 | tf_op jit(solution)/shard_map/ppermute | solution.py:851
  19.5 0.0 collective-permute-start.8
  19.5 0.0 collective-permute-done.2.e2_ref
  19.5 2.0 %collective-permute-start.7 = (bf16[64,128]{1,0:T(8,128)(2,1)S(1)}, bf16[64,128]{1,0:T(8,128)(2,1)S(1)}, u32[]{:S(2)}, u32[]{:S(2)}) collective-permute-start(bf16[64,128]{1,0:T(8,128)(2,1)S(1)} %get-tuple-element.49), channel_id=1, source_target_pairs={{0,1},{1,0},{2,3},{3,2},{4,5},{5,4},{6,7},{7,6},{8,9},{9,8},{10,11... | collective-permute-start | bytes 49160 | tf_op jit(solution)/shard_map/ppermute | solution.py:851
  21.5 0.0 collective-permute-done.3.e4_ref
  21.5 0.0 collective-permute-done.e1_ref
  21.5 0.0 copy-done
  21.5 0.0 copy-done.1
  21.5 0.0 copy-done.3
  21.5 0.0 copy-done.8
  21.5 0.9 %damping_or_first_step.1 = (bf16[256,1024]{1,0:T(8,128)(2,1)S(1)}, f32[7,16,1024]{2,1,0:T(8,128)S(1)}, f32[10,2,24,1024]{3,2,1,0:T(8,128)S(1)}) custom-call(f32[1,8,32,1024]{3,2,1,0:T(8,128)S(1)} %copy-done, s32[8,1024]{1,0:T(8,128)S(1)} %copy-done.3, f32[1,128]{1,0:T(1,128)S(1)} %bitcast.4, bf16[1024,512]{1,0:T(8,128)(2,1)S(1)} %copy-done.1, ...), custom_call_target="tpu_custom_call" | custom-call | tf_op jit(solution)/shard_map/damping_or_first_step/pallas_call | solution.py:871
  22.4 0.8 %collective-permute-done.7.refs_0_ = bf16[64,128]{1,0:T(8,128)(2,1)S(1)} collective-permute-done((bf16[64,128]{1,0:T(8,128)(2,1)S(1)}, bf16[64,128]{1,0:T(8,128)(2,1)S(1)}, u32[]{:S(2)}, u32[]{:S(2)}) %collective-permute-start.7) | collective-permute-done | bytes 16416 | tf_op jit(solution)/shard_map/ppermute | solution.py:851
  23.3 1.1 %collective-permute-done.8.refs_1_ = bf16[80,128]{1,0:T(8,128)(2,1)S(1)} collective-permute-done((bf16[80,128]{1,0:T(8,128)(2,1)S(1)}, bf16[80,128]{1,0:T(8,128)(2,1)S(1)}, u32[]{:S(2)}, u32[]{:S(2)}) %collective-permute-start.8) | collective-permute-done | bytes 20512 | tf_op jit(solution)/shard_map/ppermute | solution.py:851
  24.3 0.0 collective-permute-done.9.refs_2_
  24.4 0.1 collective-permute-start.10
  24.5 1.6 %collective-permute-start.11 = (bf16[64,128]{1,0:T(8,128)(2,1)S(1)}, bf16[64,128]{1,0:T(8,128)(2,1)S(1)}, u32[]{:S(2)}, u32[]{:S(2)}) collective-permute-start(bf16[64,128]{1,0:T(8,128)(2,1)S(1)} %get-tuple-element.54), channel_id=1, source_target_pairs={{4,8},{8,4},{12,0},{0,12},{5,9},{9,5},{13,1},{1,13},{6,10},{10,6},... | collective-permute-start | bytes 49160 | tf_op jit(solution)/shard_map/ppermute | solution.py:905
  26.0 0.0 copy-done.2
  26.0 0.0 copy-done.9
  26.0 0.4 %inverse_or_second_step.1 = (f32[8,32,1024]{2,1,0:T(8,128)S(1)}, f32[32,128]{1,0:T(8,128)S(1)}) custom-call(f32[1,128]{1,0:T(1,128)S(1)} %bitcast.5, bf16[1024,512]{1,0:T(8,128)(2,1)S(1)} %copy-done.2, bf16[256,1024]{1,0:T(8,128)(2,1)S(1)} %get-tuple-element.34.zb_ref, f32[7,16,1024]{2,1,0:T(8,128)S(1)} %get-tuple-element.35.c_ref._, ...), custom_call_target="tpu_custom_call" | custom-call | tf_op jit(solution)/shard_map/inverse_or_second_step/pallas_call | solution.py:906
  26.5 0.0 collective-permute-done.10.near_ref
  26.5 1.2 %collective-permute-done.11.far_ref = bf16[64,128]{1,0:T(8,128)(2,1)S(1)} collective-permute-done((bf16[64,128]{1,0:T(8,128)(2,1)S(1)}, bf16[64,128]{1,0:T(8,128)(2,1)S(1)}, u32[]{:S(2)}, u32[]{:S(2)}) %collective-permute-start.11) | collective-permute-done | bytes 16416 | tf_op jit(solution)/shard_map/ppermute | solution.py:905
  27.7 1.0 %add_surface_terms.1 = f32[1,8,32,1024]{3,2,1,0:T(8,128)} custom-call(f32[32,128]{1,0:T(8,128)S(1)} %get-tuple-element.37.column_ref, f32[8,32,1024]{2,1,0:T(8,128)S(1)} %get-tuple-element.38.base_ref, f32[7,16,1024]{2,1,0:T(8,128)S(1)} %get-tuple-element.35.c_ref._, f32[64,128]{1,0:T(8,128)S(1)} %get-tuple-element.52.sum_ref, ...), custom_call_target="tpu_custom_call" | custom-call | tf_op jit(solution)/shard_map/add_surface_terms/pallas_call | solution.py:914
  (2 shorter events, 0.1 us)
Async XLA Ops:
  0.0 9.5 %copy-start.7 = (s32[1,1,32,128]{3,2,1,0:T(8,128)S(1)}, s32[1,1,32,128]{3,2,1,0:T(8,128)}, u32[]{:S(2)}) copy-start(s32[1,1,32,128]{3,2,1,0:T(8,128)} %m_dst.1) | copy-start | bytes 49156
  0.0 9.5 %copy-start.6 = (s32[1,1,32,128]{3,2,1,0:T(8,128)S(1)}, s32[1,1,32,128]{3,2,1,0:T(8,128)}, u32[]{:S(2)}) copy-start(s32[1,1,32,128]{3,2,1,0:T(8,128)} %m_src.1) | copy-start | bytes 49156
  0.0 9.5 %copy-start.5 = (s32[1,1,32,128]{3,2,1,0:T(8,128)S(1)}, s32[1,1,32,128]{3,2,1,0:T(8,128)}, u32[]{:S(2)}) copy-start(s32[1,1,32,128]{3,2,1,0:T(8,128)} %a_dst.1) | copy-start | bytes 49156
  0.0 9.5 %copy-start.4 = (s32[1,1,32,128]{3,2,1,0:T(8,128)S(1)}, s32[1,1,32,128]{3,2,1,0:T(8,128)}, u32[]{:S(2)}) copy-start(s32[1,1,32,128]{3,2,1,0:T(8,128)} %a_src.1) | copy-start | bytes 49156
  0.0 15.6 %copy-start.11 = (bf16[1,1,32,128,128]{4,3,2,1,0:T(8,128)(2,1)S(1)}, bf16[1,1,32,128,128]{4,3,2,1,0:T(8,128)(2,1)}, u32[]{:S(2)}) copy-start(bf16[1,1,32,128,128]{4,3,2,1,0:T(8,128)(2,1)} %refs_8_.1) | copy-start | bytes 3145732
  0.0 15.6 %copy-start.10 = (bf16[1,1,32,128,128]{4,3,2,1,0:T(8,128)(2,1)S(1)}, bf16[1,1,32,128,128]{4,3,2,1,0:T(8,128)(2,1)}, u32[]{:S(2)}) copy-start(bf16[1,1,32,128,128]{4,3,2,1,0:T(8,128)(2,1)} %refs_7_.1) | copy-start | bytes 3145732
  3.2 7.3 %collective-permute-start.5 = (bf16[80,128]{1,0:T(8,128)(2,1)}, bf16[80,128]{1,0:T(8,128)(2,1)S(1)}, u32[]{:S(2)}, u32[]{:S(2)}) collective-permute-start(bf16[80,128]{1,0:T(8,128)(2,1)} %get-tuple-element.40), channel_id=1, source_target_pairs={{0,17},{17,0},{1,16},{16,1},{2,19},{19,2},{3,18},{18,3},{4,21},{21... | collective-permute-start | bytes 61448 | tf_op jit(solution)/shard_map/ppermute | solution.py:777
  6.6 3.9 %collective-permute-start.4 = (bf16[64,128]{1,0:T(8,128)(2,1)}, bf16[64,128]{1,0:T(8,128)(2,1)S(1)}, u32[]{:S(2)}, u32[]{:S(2)}) collective-permute-start(bf16[64,128]{1,0:T(8,128)(2,1)} %get-tuple-element.39), channel_id=1, source_target_pairs={{0,16},{16,0},{1,17},{17,1},{2,18},{18,2},{3,19},{19,3},{4,20},{20... | collective-permute-start | bytes 49160 | tf_op jit(solution)/shard_map/ppermute | solution.py:775
  7.8 7.7 %collective-permute-start.1 = (bf16[80,1024]{1,0:T(8,128)(2,1)}, bf16[80,1024]{1,0:T(8,128)(2,1)S(1)}, u32[]{:S(2)}, u32[]{:S(2)}) collective-permute-start(bf16[80,1024]{1,0:T(8,128)(2,1)} %get-tuple-element.31), channel_id=1, source_target_pairs={{4,8},{8,4},{12,0},{0,12},{5,9},{9,5},{13,1},{1,13},{6,10},{10,6},... | collective-permute-start | bytes 491528 | tf_op jit(solution)/shard_map/ppermute | solution.py:810
  10.6 5.0 %collective-permute-start.6 = (bf16[64,128]{1,0:T(8,128)(2,1)S(1)}, bf16[64,128]{1,0:T(8,128)(2,1)S(1)}, u32[]{:S(2)}, u32[]{:S(2)}) collective-permute-start(bf16[64,128]{1,0:T(8,128)(2,1)S(1)} %get-tuple-element.42), channel_id=1, source_target_pairs={{0,2},{1,3},{2,0},{3,1},{4,6},{5,7},{6,4},{7,5},{8,10},{9,11},{10,... | collective-permute-start | bytes 49160 | tf_op jit(solution)/shard_map/ppermute | solution.py:786
  13.2 6.3 %collective-permute-start.2 = (bf16[32,1024]{1,0:T(8,128)(2,1)}, bf16[32,1024]{1,0:T(8,128)(2,1)S(1)}, u32[]{:S(2)}, u32[]{:S(2)}) collective-permute-start(bf16[32,1024]{1,0:T(8,128)(2,1)} %get-tuple-element.32), channel_id=1, source_target_pairs={{16,17},{17,16},{18,19},{19,18},{0,8},{8,0},{1,9},{9,1},{2,10},{10... | collective-permute-start | bytes 196616 | tf_op jit(solution)/shard_map/ppermute | solution.py:812
  14.7 6.8 %collective-permute-start.3 = (bf16[32,1024]{1,0:T(8,128)(2,1)}, bf16[32,1024]{1,0:T(8,128)(2,1)S(1)}, u32[]{:S(2)}, u32[]{:S(2)}) collective-permute-start(bf16[32,1024]{1,0:T(8,128)(2,1)} %get-tuple-element.33), channel_id=1, source_target_pairs={{17,18},{18,17},{16,20},{20,16},{19,23},{23,19},{0,4},{4,0},{1,5},... | collective-permute-start | bytes 196616 | tf_op jit(solution)/shard_map/ppermute | solution.py:813
  14.7 6.8 %collective-permute-start = (bf16[80,1024]{1,0:T(8,128)(2,1)}, bf16[80,1024]{1,0:T(8,128)(2,1)S(1)}, u32[]{:S(2)}, u32[]{:S(2)}) collective-permute-start(bf16[80,1024]{1,0:T(8,128)(2,1)} %get-tuple-element.30), channel_id=1, source_target_pairs={{0,4},{4,0},{8,12},{12,8},{1,5},{5,1},{9,13},{13,9},{2,6},{6,2},{1... | collective-permute-start | bytes 491528 | tf_op jit(solution)/shard_map/ppermute | solution.py:809
  15.6 5.9 %copy-start = (f32[1,8,32,1024]{3,2,1,0:T(8,128)S(1)}, f32[1,8,32,1024]{3,2,1,0:T(8,128)}, u32[]{:S(2)}) copy-start(f32[1,8,32,1024]{3,2,1,0:T(8,128)} %x_ref.1) | copy-start | bytes 3145732
  15.6 5.9 %copy-start.1 = (bf16[1024,512]{1,0:T(8,128)(2,1)S(1)}, bf16[1024,512]{1,0:T(8,128)(2,1)}, u32[]{:S(2)}) copy-start(bf16[1024,512]{1,0:T(8,128)(2,1)} %constant.4.clone.table_hbm.table_ref) | copy-start | bytes 3145732
  15.6 5.9 %copy-start.3 = (s32[8,1024]{1,0:T(8,128)S(1)}, s32[8,1024]{1,0:T(8,128)}, u32[]{:S(2)}) copy-start(s32[8,1024]{1,0:T(8,128)} %wet_ref.1) | copy-start | bytes 98308
  15.6 5.9 %copy-start.8 = (f32[128]{0:T(128)S(1)}, f32[128]{0:T(128)}, u32[]{:S(2)}) copy-start(f32[128]{0:T(128)} %param.19) | copy-start | bytes 1540
  17.0 9.0 %copy-start.2 = (bf16[1024,512]{1,0:T(8,128)(2,1)S(1)}, bf16[1024,512]{1,0:T(8,128)(2,1)}, u32[]{:S(2)}) copy-start(bf16[1024,512]{1,0:T(8,128)(2,1)} %constant.5.clone.table_ref) | copy-start | bytes 3145732
  17.0 9.0 %copy-start.9 = (f32[128]{0:T(128)S(1)}, f32[128]{0:T(128)}, u32[]{:S(2)}) copy-start(f32[128]{0:T(128)} %param.18) | copy-start | bytes 1540
  17.0 7.3 %collective-permute-start.9 = (bf16[96,128]{1,0:T(8,128)(2,1)S(1)}, bf16[96,128]{1,0:T(8,128)(2,1)S(1)}, u32[]{:S(2)}, u32[]{:S(2)}) collective-permute-start(bf16[96,128]{1,0:T(8,128)(2,1)S(1)} %get-tuple-element.51), channel_id=1, source_target_pairs={{0,3},{3,0},{1,2},{2,1},{4,7},{7,4},{5,6},{6,5},{8,11},{11,8},{9,1... | collective-permute-start | bytes 73736 | tf_op jit(solution)/shard_map/ppermute | solution.py:851
  19.5 4.8 %collective-permute-start.8 = (bf16[80,128]{1,0:T(8,128)(2,1)S(1)}, bf16[80,128]{1,0:T(8,128)(2,1)S(1)}, u32[]{:S(2)}, u32[]{:S(2)}) collective-permute-start(bf16[80,128]{1,0:T(8,128)(2,1)S(1)} %get-tuple-element.50), channel_id=1, source_target_pairs={{0,2},{2,0},{1,3},{3,1},{4,6},{6,4},{5,7},{7,5},{8,10},{10,8},{9,1... | collective-permute-start | bytes 61448 | tf_op jit(solution)/shard_map/ppermute | solution.py:851
  19.5 3.7 %collective-permute-start.7 = (bf16[64,128]{1,0:T(8,128)(2,1)S(1)}, bf16[64,128]{1,0:T(8,128)(2,1)S(1)}, u32[]{:S(2)}, u32[]{:S(2)}) collective-permute-start(bf16[64,128]{1,0:T(8,128)(2,1)S(1)} %get-tuple-element.49), channel_id=1, source_target_pairs={{0,1},{1,0},{2,3},{3,2},{4,5},{5,4},{6,7},{7,6},{8,9},{9,8},{10,11... | collective-permute-start | bytes 49160 | tf_op jit(solution)/shard_map/ppermute | solution.py:851
  24.4 2.1 %collective-permute-start.10 = (bf16[64,128]{1,0:T(8,128)(2,1)S(1)}, bf16[64,128]{1,0:T(8,128)(2,1)S(1)}, u32[]{:S(2)}, u32[]{:S(2)}) collective-permute-start(bf16[64,128]{1,0:T(8,128)(2,1)S(1)} %get-tuple-element.53), channel_id=1, source_target_pairs={{0,4},{4,0},{8,12},{12,8},{1,5},{5,1},{9,13},{13,9},{2,6},{6,2},{1... | collective-permute-start | bytes 49160 | tf_op jit(solution)/shard_map/ppermute | solution.py:904
  24.5 3.2 %collective-permute-start.11 = (bf16[64,128]{1,0:T(8,128)(2,1)S(1)}, bf16[64,128]{1,0:T(8,128)(2,1)S(1)}, u32[]{:S(2)}, u32[]{:S(2)}) collective-permute-start(bf16[64,128]{1,0:T(8,128)(2,1)S(1)} %get-tuple-element.54), channel_id=1, source_target_pairs={{4,8},{8,4},{12,0},{0,12},{5,9},{9,5},{13,1},{1,13},{6,10},{10,6},... | collective-permute-start | bytes 49160 | tf_op jit(solution)/shard_map/ppermute | solution.py:905

commit v20 on v19

--- a/solution.py
+++ b/solution.py
@@ -152,8 +152,13 @@
     def _():
         flux_copy = pltpu.make_async_copy(flux_hbm, flux_ref, sem.at[0])
         diff_copy = pltpu.make_async_copy(diff_hbm, diff_ref, sem.at[1])
-        table_copy = pltpu.make_async_copy(table_hbm, table_ref, sem.at[2])
-        for copy in [flux_copy, diff_copy] + x_copies + [table_copy]:
+        table_copies = [
+            pltpu.make_async_copy(
+                table_hbm.at[pl.ds(k * half, half)], table_ref.at[pl.ds(k * half, half)], sem.at[2 + k]
+            )
+            for k in range(2)
+        ]
+        for copy in [flux_copy, diff_copy] + x_copies + table_copies:
             copy.start()
         first = col_group * channels
         flux_copy.wait()
@@ -175,8 +180,8 @@
             row_ref[r : r + 1, :] = jnp.sum(x_ref[r] * weight, axis=0, keepdims=True)
             fold(x_ref[r], flat_ref, r)
         send_surface()
-        table_copy.wait()
         for k in range(2):
+            table_copies[k].wait()
             lanes = slice(k * half, (k + 1) * half)
             part = jnp.dot(
                 flat_ref[:, lanes], table_ref[lanes, :], preferred_element_type=f32
@@ -739,7 +744,7 @@
             pltpu.VMEM((4 * rows, columns), f32),
             pltpu.VMEM((columns // 2 // LANES, 2 * rows + 1, channels, LANES), f32),
             pltpu.SemaphoreType.DMA((rows,)),
-            pltpu.SemaphoreType.DMA((3,)),
+            pltpu.SemaphoreType.DMA((4,)),
             pltpu.SemaphoreType.DMA((len(shapes),)),
         ],
         compiler_params=pltpu.CompilerParams(vmem_limit_bytes=58 * 2**20),
@@ -764,7 +769,7 @@
         marine_air_input_index, marine_air_output_index, marine_air_piece_tally,
     )
 
-    masks = [1 << bit for bit in range(groups_y.bit_length() - 1)]
+    masks = [1 << bit for bit in reversed(range(groups_y.bit_length() - 1))]
 
     def sum_route(mask):
         return [(j, j ^ mask) for j in range(groups_y)]

time: 28.9 us -> 28.9 us (level)
    ppermute x1, starting transfers between devices: 2.65 us -> 1.64 us  [local(): lax.ppermute(coarse, 'gy', sum_route(mask))]
    ppermute x1, starting transfers between devices: 3.37 us -> 4.36 us  [local(): far = lax.ppermute(wide, ('comp', 'gy'), partner_route(mask))]
  transfers between devices with their start and end apart: 12 -> 12, of which waited for: 5 -> 6; matrix products, arithmetic and copies ran while one was open for 0% -> 0% of each run, Pallas kernels for 12% -> 12%
where the time goes in v20:
time: 28.9 us; the launch traced here: 28.7 us
  starting transfers between devices  15.7 us (54%)
  Pallas kernels  7.64 us (26%)
  waiting for transfers between devices  3.8 us (13%)
  between operations  1.49 us (5%)
    ppermute x3, starting transfers between devices, local(): lax.ppermute(block, axes, landing_route(mask))  4.45 us
    ppermute x1, starting transfers between devices, local(): far = lax.ppermute(wide, ('comp', 'gy'), partner_route(mask))  4.36 us
    pallas_call x1, Pallas kernels, local(): pl.pallas_call(functools.partial(start_kernel, groups_x, paired), out_sha...  3.24 us
    ppermute x3, waiting for transfers between devices, local(): lax.ppermute(block, axes, landing_route(mask))  1.95 us
    ppermute x1, starting transfers between devices, local(): lax.ppermute(coarse, 'gy', sum_route(mask))  1.64 us
    ppermute x1, starting transfers between devices, local(): far = lax.ppermute(far, 'gx', both_ways(ring_pairs(groups_x, 1)))  1.6 us
    ppermute x1, starting transfers between devices, local(): e2 = lax.ppermute(e2, axes, level_route(0))  1.49 us
    pallas_call x1, Pallas kernels, local(): pl.pallas_call(functools.partial(regrid_kernel, len(surfaces)), out_shape...  1.35 us
  transfers between devices with their start and end apart: 12, of which 6 were waited for; matrix products, arithmetic and copies ran while one was open for 0% of the time, Pallas kernels for 12%

profile of v20, /device:TPU:0, one launch (start us, length us, event | category | flops | bytes accessed | tf_op | source)
XLA Modules:
  0.0 28.7 jit_solution(3193011833503397856)
XLA Ops:
  0.0 0.0 copy-start.7
  0.0 0.0 copy-start.6
  0.0 0.0 copy-start.5
  0.0 0.0 copy-start.4
  0.0 0.0 copy-start.11
  0.0 0.0 copy-start.10
  0.0 3.2 %surface_and_forward_or_halos.1 = (bf16[64,128]{1,0:T(8,128)(2,1)}, bf16[80,128]{1,0:T(8,128)(2,1)}, bf16[80,1024]{1,0:T(8,128)(2,1)}, bf16[80,1024]{1,0:T(8,128...) custom-call(f32[1,8,32,1024]{3,2,1,0:T(8,128)} %x_ref.1, s32[8,1024]{1,0:T(8,128)} %wet_ref.1, ...), custom_call_target="tpu_custom_call" | custom-call | tf_op jit(solution)/shard_map/surface_and_forward_or_halos/pallas_call | solution.py:730
  3.3 4.4 %collective-permute-start.5 = (bf16[80,128]{1,0:T(8,128)(2,1)}, bf16[80,128]{1,0:T(8,128)(2,1)S(1)}, u32[]{:S(2)}, u32[]{:S(2)}) collective-permute-start(bf16[80,128]{1,0:T(8,128)(2,1)} %get-tuple-element.40), channel_id=1, source_target_pairs={{0,18},{18,0},{1,19},{19,1},{2,16},{16,2},{3,17},{17,3},{4,22},{22... | collective-permute-start | bytes 61448 | tf_op jit(solution)/shard_map/ppermute | solution.py:782
  7.6 1.2 %collective-permute-start.4 = (bf16[64,128]{1,0:T(8,128)(2,1)}, bf16[64,128]{1,0:T(8,128)(2,1)S(1)}, u32[]{:S(2)}, u32[]{:S(2)}) collective-permute-start(bf16[64,128]{1,0:T(8,128)(2,1)} %get-tuple-element.39), channel_id=1, source_target_pairs={{0,16},{16,0},{1,17},{17,1},{2,18},{18,2},{3,19},{19,3},{4,20},{20... | collective-permute-start | bytes 49160 | tf_op jit(solution)/shard_map/ppermute | solution.py:780
  8.8 0.4 %collective-permute-start.1 = (bf16[80,1024]{1,0:T(8,128)(2,1)}, bf16[80,1024]{1,0:T(8,128)(2,1)S(1)}, u32[]{:S(2)}, u32[]{:S(2)}) collective-permute-start(bf16[80,1024]{1,0:T(8,128)(2,1)} %get-tuple-element.31), channel_id=1, source_target_pairs={{4,8},{8,4},{12,0},{0,12},{5,9},{9,5},{13,1},{1,13},{6,10},{10,6},... | collective-permute-start | bytes 491528 | tf_op jit(solution)/shard_map/ppermute | solution.py:815
  10.5 0.0 copy-done.7
  10.5 0.0 copy-done.6
  10.5 0.0 copy-done.5
  10.5 0.0 copy-done.4
  10.6 0.6 %one_hots.1 = (bf16[128,4096]{1,0:T(8,128)(2,1)S(1)}, bf16[128,4096]{1,0:T(8,128)(2,1)S(1)}, s32[32,128]{1,0:T(8,128)S(1)}, s32[32,128]{1,0:T(8,128)S(1)}, s32[32,128]{1,0:T(8,128)S(1)}) custom-call(s32[1,1,32,128]{3,2,1,0:T(8,128)S(1)} %copy-done.4, s32[1,1,32,128]{3,2,1,0:T(8,128)S(1)} %copy-done.5, s32[1,1]{1,0:T(1,128)S(6)} %copy.16.a_count, ...), custom_call_target="tpu_custom_call" | custom-call | tf_op jit(solution)/shard_map/one_hots/pallas_call | solution.py:754
  11.2 0.4 %collective-permute-done.4 = bf16[64,128]{1,0:T(8,128)(2,1)S(1)} collective-permute-done((bf16[64,128]{1,0:T(8,128)(2,1)}, bf16[64,128]{1,0:T(8,128)(2,1)S(1)}, u32[]{:S(2)}, u32[]{:S(2)}) %collective-permute-start.4) | collective-permute-done | bytes 16416 | tf_op jit(solution)/shard_map/ppermute | solution.py:780
  11.6 0.0 collective-permute-done.5
  11.6 1.6 %collective-permute-start.6 = (bf16[64,128]{1,0:T(8,128)(2,1)S(1)}, bf16[64,128]{1,0:T(8,128)(2,1)S(1)}, u32[]{:S(2)}, u32[]{:S(2)}) collective-permute-start(bf16[64,128]{1,0:T(8,128)(2,1)S(1)} %get-tuple-element.42), channel_id=1, source_target_pairs={{0,1},{1,0},{2,3},{3,2},{4,5},{5,4},{6,7},{7,6},{8,9},{9,8},{10,11... | collective-permute-start | bytes 49160 | tf_op jit(solution)/shard_map/ppermute | solution.py:791
  13.2 1.5 %collective-permute-start.2 = (bf16[32,1024]{1,0:T(8,128)(2,1)}, bf16[32,1024]{1,0:T(8,128)(2,1)S(1)}, u32[]{:S(2)}, u32[]{:S(2)}) collective-permute-start(bf16[32,1024]{1,0:T(8,128)(2,1)} %get-tuple-element.32), channel_id=1, source_target_pairs={{16,17},{17,16},{18,19},{19,18},{0,8},{8,0},{1,9},{9,1},{2,10},{10... | collective-permute-start | bytes 196616 | tf_op jit(solution)/shard_map/ppermute | solution.py:817
  14.7 0.0 collective-permute-start.3
  14.7 0.5 %collective-permute-start = (bf16[80,1024]{1,0:T(8,128)(2,1)}, bf16[80,1024]{1,0:T(8,128)(2,1)S(1)}, u32[]{:S(2)}, u32[]{:S(2)}) collective-permute-start(bf16[80,1024]{1,0:T(8,128)(2,1)} %get-tuple-element.30), channel_id=1, source_target_pairs={{0,4},{4,0},{8,12},{12,8},{1,5},{5,1},{9,13},{13,9},{2,6},{6,2},{1... | collective-permute-start | bytes 491528 | tf_op jit(solution)/shard_map/ppermute | solution.py:814
  15.2 0.2 collective-permute-done.6.refs_1_
  15.5 0.1 collective-permute-done.1.e3_ref.refs_9_
  15.5 0.0 copy-done.11
  15.5 0.0 copy-done.10
  15.5 0.0 copy-start
  15.5 0.0 copy-start.1
  15.5 0.0 copy-start.3
  15.5 0.0 copy-start.8
  15.6 1.4 %regrid_blocks.1 = (f32[64,128]{1,0:T(8,128)S(1)}, bf16[64,128]{1,0:T(8,128)(2,1)S(1)}, bf16[80,128]{1,0:T(8,128)(2,1)S(1)}, bf16[96,128]{1,0:T(8,128)(2,1)S(1)}) custom-call(f32[64,128]{1,0:T(8,128)S(1)} %get-tuple-element.56.refs_0_, bf16[64,128]{1,0:T(8,128)(2,1)S(1)} %collective-permute-done.6.refs_1_, bf16[128,4096]{1,0:T(8,128)(2,1)S(1)} %get-tuple-element.43.refs_2_, ...), custom_call_target="tpu_custom_call" | custom-call | flops 2200000000 | tf_op jit(solution)/shard_map/regrid_blocks/pallas_call | solution.py:820
  16.9 0.0 copy-start.2
  16.9 0.0 copy-start.9
  16.9 2.7 %collective-permute-start.9 = (bf16[96,128]{1,0:T(8,128)(2,1)S(1)}, bf16[96,128]{1,0:T(8,128)(2,1)S(1)}, u32[]{:S(2)}, u32[]{:S(2)}) collective-permute-start(bf16[96,128]{1,0:T(8,128)(2,1)S(1)} %get-tuple-element.51), channel_id=1, source_target_pairs={{0,3},{3,0},{1,2},{2,1},{4,7},{7,4},{5,6},{6,5},{8,11},{11,8},{9,1... | collective-permute-start | bytes 73736 | tf_op jit(solution)/shard_map/ppermute | solution.py:856
  19.6 0.4 %collective-permute-start.8 = (bf16[80,128]{1,0:T(8,128)(2,1)S(1)}, bf16[80,128]{1,0:T(8,128)(2,1)S(1)}, u32[]{:S(2)}, u32[]{:S(2)}) collective-permute-start(bf16[80,128]{1,0:T(8,128)(2,1)S(1)} %get-tuple-element.50), channel_id=1, source_target_pairs={{0,2},{2,0},{1,3},{3,1},{4,6},{6,4},{5,7},{7,5},{8,10},{10,8},{9,1... | collective-permute-start | bytes 61448 | tf_op jit(solution)/shard_map/ppermute | solution.py:856
  20.0 0.0 collective-permute-done.2.e2_ref
  20.0 1.4 %collective-permute-start.7 = (bf16[64,128]{1,0:T(8,128)(2,1)S(1)}, bf16[64,128]{1,0:T(8,128)(2,1)S(1)}, u32[]{:S(2)}, u32[]{:S(2)}) collective-permute-start(bf16[64,128]{1,0:T(8,128)(2,1)S(1)} %get-tuple-element.49), channel_id=1, source_target_pairs={{0,1},{1,0},{2,3},{3,2},{4,5},{5,4},{6,7},{7,6},{8,9},{9,8},{10,11... | collective-permute-start | bytes 49160 | tf_op jit(solution)/shard_map/ppermute | solution.py:856
  21.4 0.0 collective-permute-done.3.e4_ref
  21.4 0.0 collective-permute-done.e1_ref
  21.4 0.0 copy-done
  21.4 0.0 copy-done.1
  21.4 0.0 copy-done.3
  21.4 0.0 copy-done.8
  21.4 0.9 %damping_or_first_step.1 = (bf16[256,1024]{1,0:T(8,128)(2,1)S(1)}, f32[7,16,1024]{2,1,0:T(8,128)S(1)}, f32[10,2,24,1024]{3,2,1,0:T(8,128)S(1)}) custom-call(f32[1,8,32,1024]{3,2,1,0:T(8,128)S(1)} %copy-done, s32[8,1024]{1,0:T(8,128)S(1)} %copy-done.3, f32[1,128]{1,0:T(1,128)S(1)} %bitcast.4, bf16[1024,512]{1,0:T(8,128)(2,1)S(1)} %copy-done.1, ...), custom_call_target="tpu_custom_call" | custom-call | tf_op jit(solution)/shard_map/damping_or_first_step/pallas_call | solution.py:876
  22.4 1.4 %collective-permute-done.7.refs_0_ = bf16[64,128]{1,0:T(8,128)(2,1)S(1)} collective-permute-done((bf16[64,128]{1,0:T(8,128)(2,1)S(1)}, bf16[64,128]{1,0:T(8,128)(2,1)S(1)}, u32[]{:S(2)}, u32[]{:S(2)}) %collective-permute-start.7) | collective-permute-done | bytes 16416 | tf_op jit(solution)/shard_map/ppermute | solution.py:856
  23.8 0.5 %collective-permute-done.8.refs_1_ = bf16[80,128]{1,0:T(8,128)(2,1)S(1)} collective-permute-done((bf16[80,128]{1,0:T(8,128)(2,1)S(1)}, bf16[80,128]{1,0:T(8,128)(2,1)S(1)}, u32[]{:S(2)}, u32[]{:S(2)}) %collective-permute-start.8) | collective-permute-done | bytes 20512 | tf_op jit(solution)/shard_map/ppermute | solution.py:856
  24.3 0.0 collective-permute-done.9.refs_2_
  24.4 0.1 collective-permute-start.10
  24.4 1.6 %collective-permute-start.11 = (bf16[64,128]{1,0:T(8,128)(2,1)S(1)}, bf16[64,128]{1,0:T(8,128)(2,1)S(1)}, u32[]{:S(2)}, u32[]{:S(2)}) collective-permute-start(bf16[64,128]{1,0:T(8,128)(2,1)S(1)} %get-tuple-element.54), channel_id=1, source_target_pairs={{4,8},{8,4},{12,0},{0,12},{5,9},{9,5},{13,1},{1,13},{6,10},{10,6},... | collective-permute-start | bytes 49160 | tf_op jit(solution)/shard_map/ppermute | solution.py:910
  26.1 0.0 copy-done.2
  26.1 0.0 copy-done.9
  26.1 0.4 %inverse_or_second_step.1 = (f32[8,32,1024]{2,1,0:T(8,128)S(1)}, f32[32,128]{1,0:T(8,128)S(1)}) custom-call(f32[1,128]{1,0:T(1,128)S(1)} %bitcast.5, bf16[1024,512]{1,0:T(8,128)(2,1)S(1)} %copy-done.2, bf16[256,1024]{1,0:T(8,128)(2,1)S(1)} %get-tuple-element.34.zb_ref, f32[7,16,1024]{2,1,0:T(8,128)S(1)} %get-tuple-element.35.c_ref._, ...), custom_call_target="tpu_custom_call" | custom-call | tf_op jit(solution)/shard_map/inverse_or_second_step/pallas_call | solution.py:911
  26.5 0.0 collective-permute-done.10.near_ref
  26.5 1.2 %collective-permute-done.11.far_ref = bf16[64,128]{1,0:T(8,128)(2,1)S(1)} collective-permute-done((bf16[64,128]{1,0:T(8,128)(2,1)S(1)}, bf16[64,128]{1,0:T(8,128)(2,1)S(1)}, u32[]{:S(2)}, u32[]{:S(2)}) %collective-permute-start.11) | collective-permute-done | bytes 16416 | tf_op jit(solution)/shard_map/ppermute | solution.py:910
  27.7 1.0 %add_surface_terms.1 = f32[1,8,32,1024]{3,2,1,0:T(8,128)} custom-call(f32[32,128]{1,0:T(8,128)S(1)} %get-tuple-element.37.column_ref, f32[8,32,1024]{2,1,0:T(8,128)S(1)} %get-tuple-element.38.base_ref, f32[7,16,1024]{2,1,0:T(8,128)S(1)} %get-tuple-element.35.c_ref._, f32[64,128]{1,0:T(8,128)S(1)} %get-tuple-element.52.sum_ref, ...), custom_call_target="tpu_custom_call" | custom-call | tf_op jit(solution)/shard_map/add_surface_terms/pallas_call | solution.py:919
  (2 shorter events, 0.1 us)
Async XLA Ops:
  0.0 10.5 %copy-start.7 = (s32[1,1,32,128]{3,2,1,0:T(8,128)S(1)}, s32[1,1,32,128]{3,2,1,0:T(8,128)}, u32[]{:S(2)}) copy-start(s32[1,1,32,128]{3,2,1,0:T(8,128)} %m_dst.1) | copy-start | bytes 49156
  0.0 10.5 %copy-start.6 = (s32[1,1,32,128]{3,2,1,0:T(8,128)S(1)}, s32[1,1,32,128]{3,2,1,0:T(8,128)}, u32[]{:S(2)}) copy-start(s32[1,1,32,128]{3,2,1,0:T(8,128)} %m_src.1) | copy-start | bytes 49156
  0.0 10.5 %copy-start.5 = (s32[1,1,32,128]{3,2,1,0:T(8,128)S(1)}, s32[1,1,32,128]{3,2,1,0:T(8,128)}, u32[]{:S(2)}) copy-start(s32[1,1,32,128]{3,2,1,0:T(8,128)} %a_dst.1) | copy-start | bytes 49156
  0.0 10.5 %copy-start.4 = (s32[1,1,32,128]{3,2,1,0:T(8,128)S(1)}, s32[1,1,32,128]{3,2,1,0:T(8,128)}, u32[]{:S(2)}) copy-start(s32[1,1,32,128]{3,2,1,0:T(8,128)} %a_src.1) | copy-start | bytes 49156
  0.0 15.5 %copy-start.11 = (bf16[1,1,32,128,128]{4,3,2,1,0:T(8,128)(2,1)S(1)}, bf16[1,1,32,128,128]{4,3,2,1,0:T(8,128)(2,1)}, u32[]{:S(2)}) copy-start(bf16[1,1,32,128,128]{4,3,2,1,0:T(8,128)(2,1)} %refs_8_.1) | copy-start | bytes 3145732
  0.0 15.5 %copy-start.10 = (bf16[1,1,32,128,128]{4,3,2,1,0:T(8,128)(2,1)S(1)}, bf16[1,1,32,128,128]{4,3,2,1,0:T(8,128)(2,1)}, u32[]{:S(2)}) copy-start(bf16[1,1,32,128,128]{4,3,2,1,0:T(8,128)(2,1)} %refs_7_.1) | copy-start | bytes 3145732
  3.3 8.3 %collective-permute-start.5 = (bf16[80,128]{1,0:T(8,128)(2,1)}, bf16[80,128]{1,0:T(8,128)(2,1)S(1)}, u32[]{:S(2)}, u32[]{:S(2)}) collective-permute-start(bf16[80,128]{1,0:T(8,128)(2,1)} %get-tuple-element.40), channel_id=1, source_target_pairs={{0,18},{18,0},{1,19},{19,1},{2,16},{16,2},{3,17},{17,3},{4,22},{22... | collective-permute-start | bytes 61448 | tf_op jit(solution)/shard_map/ppermute | solution.py:782
  7.6 3.9 %collective-permute-start.4 = (bf16[64,128]{1,0:T(8,128)(2,1)}, bf16[64,128]{1,0:T(8,128)(2,1)S(1)}, u32[]{:S(2)}, u32[]{:S(2)}) collective-permute-start(bf16[64,128]{1,0:T(8,128)(2,1)} %get-tuple-element.39), channel_id=1, source_target_pairs={{0,16},{16,0},{1,17},{17,1},{2,18},{18,2},{3,19},{19,3},{4,20},{20... | collective-permute-start | bytes 49160 | tf_op jit(solution)/shard_map/ppermute | solution.py:780
  8.8 6.7 %collective-permute-start.1 = (bf16[80,1024]{1,0:T(8,128)(2,1)}, bf16[80,1024]{1,0:T(8,128)(2,1)S(1)}, u32[]{:S(2)}, u32[]{:S(2)}) collective-permute-start(bf16[80,1024]{1,0:T(8,128)(2,1)} %get-tuple-element.31), channel_id=1, source_target_pairs={{4,8},{8,4},{12,0},{0,12},{5,9},{9,5},{13,1},{1,13},{6,10},{10,6},... | collective-permute-start | bytes 491528 | tf_op jit(solution)/shard_map/ppermute | solution.py:815
  11.6 3.9 %collective-permute-start.6 = (bf16[64,128]{1,0:T(8,128)(2,1)S(1)}, bf16[64,128]{1,0:T(8,128)(2,1)S(1)}, u32[]{:S(2)}, u32[]{:S(2)}) collective-permute-start(bf16[64,128]{1,0:T(8,128)(2,1)S(1)} %get-tuple-element.42), channel_id=1, source_target_pairs={{0,1},{1,0},{2,3},{3,2},{4,5},{5,4},{6,7},{7,6},{8,9},{9,8},{10,11... | collective-permute-start | bytes 49160 | tf_op jit(solution)/shard_map/ppermute | solution.py:791
  13.2 6.8 %collective-permute-start.2 = (bf16[32,1024]{1,0:T(8,128)(2,1)}, bf16[32,1024]{1,0:T(8,128)(2,1)S(1)}, u32[]{:S(2)}, u32[]{:S(2)}) collective-permute-start(bf16[32,1024]{1,0:T(8,128)(2,1)} %get-tuple-element.32), channel_id=1, source_target_pairs={{16,17},{17,16},{18,19},{19,18},{0,8},{8,0},{1,9},{9,1},{2,10},{10... | collective-permute-start | bytes 196616 | tf_op jit(solution)/shard_map/ppermute | solution.py:817
  14.7 6.7 %collective-permute-start.3 = (bf16[32,1024]{1,0:T(8,128)(2,1)}, bf16[32,1024]{1,0:T(8,128)(2,1)S(1)}, u32[]{:S(2)}, u32[]{:S(2)}) collective-permute-start(bf16[32,1024]{1,0:T(8,128)(2,1)} %get-tuple-element.33), channel_id=1, source_target_pairs={{17,18},{18,17},{16,20},{20,16},{19,23},{23,19},{0,4},{4,0},{1,5},... | collective-permute-start | bytes 196616 | tf_op jit(solution)/shard_map/ppermute | solution.py:818
  14.7 6.7 %collective-permute-start = (bf16[80,1024]{1,0:T(8,128)(2,1)}, bf16[80,1024]{1,0:T(8,128)(2,1)S(1)}, u32[]{:S(2)}, u32[]{:S(2)}) collective-permute-start(bf16[80,1024]{1,0:T(8,128)(2,1)} %get-tuple-element.30), channel_id=1, source_target_pairs={{0,4},{4,0},{8,12},{12,8},{1,5},{5,1},{9,13},{13,9},{2,6},{6,2},{1... | collective-permute-start | bytes 491528 | tf_op jit(solution)/shard_map/ppermute | solution.py:814
  15.5 5.9 %copy-start = (f32[1,8,32,1024]{3,2,1,0:T(8,128)S(1)}, f32[1,8,32,1024]{3,2,1,0:T(8,128)}, u32[]{:S(2)}) copy-start(f32[1,8,32,1024]{3,2,1,0:T(8,128)} %x_ref.1) | copy-start | bytes 3145732
  15.5 5.9 %copy-start.1 = (bf16[1024,512]{1,0:T(8,128)(2,1)S(1)}, bf16[1024,512]{1,0:T(8,128)(2,1)}, u32[]{:S(2)}) copy-start(bf16[1024,512]{1,0:T(8,128)(2,1)} %constant.4.clone.table_hbm.table_ref) | copy-start | bytes 3145732
  15.5 5.9 %copy-start.3 = (s32[8,1024]{1,0:T(8,128)S(1)}, s32[8,1024]{1,0:T(8,128)}, u32[]{:S(2)}) copy-start(s32[8,1024]{1,0:T(8,128)} %wet_ref.1) | copy-start | bytes 98308
  15.5 5.9 %copy-start.8 = (f32[128]{0:T(128)S(1)}, f32[128]{0:T(128)}, u32[]{:S(2)}) copy-start(f32[128]{0:T(128)} %param.19) | copy-start | bytes 1540
  16.9 9.1 %copy-start.2 = (bf16[1024,512]{1,0:T(8,128)(2,1)S(1)}, bf16[1024,512]{1,0:T(8,128)(2,1)}, u32[]{:S(2)}) copy-start(bf16[1024,512]{1,0:T(8,128)(2,1)} %constant.5.clone.table_ref) | copy-start | bytes 3145732
  16.9 9.1 %copy-start.9 = (f32[128]{0:T(128)S(1)}, f32[128]{0:T(128)}, u32[]{:S(2)}) copy-start(f32[128]{0:T(128)} %param.18) | copy-start | bytes 1540
  16.9 7.4 %collective-permute-start.9 = (bf16[96,128]{1,0:T(8,128)(2,1)S(1)}, bf16[96,128]{1,0:T(8,128)(2,1)S(1)}, u32[]{:S(2)}, u32[]{:S(2)}) collective-permute-start(bf16[96,128]{1,0:T(8,128)(2,1)S(1)} %get-tuple-element.51), channel_id=1, source_target_pairs={{0,3},{3,0},{1,2},{2,1},{4,7},{7,4},{5,6},{6,5},{8,11},{11,8},{9,1... | collective-permute-start | bytes 73736 | tf_op jit(solution)/shard_map/ppermute | solution.py:856
  19.6 4.7 %collective-permute-start.8 = (bf16[80,128]{1,0:T(8,128)(2,1)S(1)}, bf16[80,128]{1,0:T(8,128)(2,1)S(1)}, u32[]{:S(2)}, u32[]{:S(2)}) collective-permute-start(bf16[80,128]{1,0:T(8,128)(2,1)S(1)} %get-tuple-element.50), channel_id=1, source_target_pairs={{0,2},{2,0},{1,3},{3,1},{4,6},{6,4},{5,7},{7,5},{8,10},{10,8},{9,1... | collective-permute-start | bytes 61448 | tf_op jit(solution)/shard_map/ppermute | solution.py:856
  20.0 3.7 %collective-permute-start.7 = (bf16[64,128]{1,0:T(8,128)(2,1)S(1)}, bf16[64,128]{1,0:T(8,128)(2,1)S(1)}, u32[]{:S(2)}, u32[]{:S(2)}) collective-permute-start(bf16[64,128]{1,0:T(8,128)(2,1)S(1)} %get-tuple-element.49), channel_id=1, source_target_pairs={{0,1},{1,0},{2,3},{3,2},{4,5},{5,4},{6,7},{7,6},{8,9},{9,8},{10,11... | collective-permute-start | bytes 49160 | tf_op jit(solution)/shard_map/ppermute | solution.py:856
  24.4 2.1 %collective-permute-start.10 = (bf16[64,128]{1,0:T(8,128)(2,1)S(1)}, bf16[64,128]{1,0:T(8,128)(2,1)S(1)}, u32[]{:S(2)}, u32[]{:S(2)}) collective-permute-start(bf16[64,128]{1,0:T(8,128)(2,1)S(1)} %get-tuple-element.53), channel_id=1, source_target_pairs={{0,4},{4,0},{8,12},{12,8},{1,5},{5,1},{9,13},{13,9},{2,6},{6,2},{1... | collective-permute-start | bytes 49160 | tf_op jit(solution)/shard_map/ppermute | solution.py:909
  24.4 3.2 %collective-permute-start.11 = (bf16[64,128]{1,0:T(8,128)(2,1)S(1)}, bf16[64,128]{1,0:T(8,128)(2,1)S(1)}, u32[]{:S(2)}, u32[]{:S(2)}) collective-permute-start(bf16[64,128]{1,0:T(8,128)(2,1)S(1)} %get-tuple-element.54), channel_id=1, source_target_pairs={{4,8},{8,4},{12,0},{0,12},{5,9},{9,5},{13,1},{1,13},{6,10},{10,6},... | collective-permute-start | bytes 49160 | tf_op jit(solution)/shard_map/ppermute | solution.py:910

commit v21 on v20

--- a/solution.py
+++ b/solution.py
@@ -817,10 +817,14 @@
     e2 = lax.ppermute(e2, axes, level_route(0))
     e4 = lax.ppermute(e4, axes, level_route(1))
 
+    landing_order = sorted(range(1, groups_y), key=lambda mask: (mask % 2, -mask))
     landing, *sent = pl.pallas_call(
         functools.partial(regrid_kernel, len(surfaces)),
         out_shape=[shape((cells, LANES), f32)]
-        + [shape((cells + 16 * (mask - 1), LANES), bf16) for mask in range(1, groups_y)],
+        + [
+            shape((cells + 16 * (groups_y - 2 - landing_order.index(mask)), LANES), bf16)
+            for mask in range(1, groups_y)
+        ],
         in_specs=[vmem] * (len(surfaces) + 5) + [hbm, hbm] + [anywhere] * 1,
         out_specs=[vmem] * groups_y,
         scratch_shapes=[

time: 28.9 us -> 29.3 us (1.014)
  waiting for transfers between devices: 3.8 us -> 4.69 us
  starting transfers between devices: 15.7 us -> 15.2 us
    ppermute x3, waiting for transfers between devices: 1.95 us -> 2.76 us  [local(): lax.ppermute(block, axes, landing_route(mask))]
    ppermute x3, starting transfers between devices: 4.45 us -> 4 us  [local(): lax.ppermute(block, axes, landing_route(mask))]
  transfers between devices with their start and end apart: 12 -> 12, of which waited for: 6 -> 5; matrix products, arithmetic and copies ran while one was open for 0% -> 0% of each run, Pallas kernels for 12% -> 11%
where the time goes in v21:
time: 29.3 us; the launch traced here: 29.1 us
  starting transfers between devices  15.2 us (52%)
  Pallas kernels  7.64 us (26%)
  waiting for transfers between devices  4.69 us (16%)
  between operations  1.5 us (5%)
    ppermute x1, starting transfers between devices, local(): far = lax.ppermute(wide, ('comp', 'gy'), partner_route(mask))  4.36 us
    ppermute x3, starting transfers between devices, local(): lax.ppermute(block, axes, landing_route(mask))  4 us
    pallas_call x1, Pallas kernels, local(): pl.pallas_call(functools.partial(start_kernel, groups_x, paired), out_sha...  3.24 us
    ppermute x3, waiting for transfers between devices, local(): lax.ppermute(block, axes, landing_route(mask))  2.76 us
    ppermute x1, starting transfers between devices, local(): lax.ppermute(coarse, 'gy', sum_route(mask))  1.64 us
    ppermute x1, starting transfers between devices, local(): far = lax.ppermute(far, 'gx', both_ways(ring_pairs(groups_x, 1)))  1.52 us
    ppermute x1, starting transfers between devices, local(): e2 = lax.ppermute(e2, axes, level_route(0))  1.49 us
    pallas_call x1, Pallas kernels, local(): pl.pallas_call(functools.partial(regrid_kernel, len(surfaces)), out_shape...  1.35 us
  transfers between devices with their start and end apart: 12, of which 5 were waited for; matrix products, arithmetic and copies ran while one was open for 0% of the time, Pallas kernels for 11%

profile of v21, /device:TPU:0, one launch (start us, length us, event | category | flops | bytes accessed | tf_op | source)
XLA Modules:
  0.0 29.1 jit_solution(13300553387246836965)
XLA Ops:
  0.0 0.0 copy-start.7
  0.0 0.0 copy-start.6
  0.0 0.0 copy-start.5
  0.0 0.0 copy-start.4
  0.0 0.0 copy-start.11
  0.0 0.0 copy-start.10
  0.0 3.2 %surface_and_forward_or_halos.1 = (bf16[64,128]{1,0:T(8,128)(2,1)}, bf16[80,128]{1,0:T(8,128)(2,1)}, bf16[80,1024]{1,0:T(8,128)(2,1)}, bf16[80,1024]{1,0:T(8,128...) custom-call(f32[1,8,32,1024]{3,2,1,0:T(8,128)} %x_ref.1, s32[8,1024]{1,0:T(8,128)} %wet_ref.1, ...), custom_call_target="tpu_custom_call" | custom-call | tf_op jit(solution)/shard_map/surface_and_forward_or_halos/pallas_call | solution.py:730
  3.3 4.4 %collective-permute-start.5 = (bf16[80,128]{1,0:T(8,128)(2,1)}, bf16[80,128]{1,0:T(8,128)(2,1)S(1)}, u32[]{:S(2)}, u32[]{:S(2)}) collective-permute-start(bf16[80,128]{1,0:T(8,128)(2,1)} %get-tuple-element.40), channel_id=1, source_target_pairs={{0,18},{18,0},{1,19},{19,1},{2,16},{16,2},{3,17},{17,3},{4,22},{22... | collective-permute-start | bytes 61448 | tf_op jit(solution)/shard_map/ppermute | solution.py:782
  7.6 1.2 %collective-permute-start.4 = (bf16[64,128]{1,0:T(8,128)(2,1)}, bf16[64,128]{1,0:T(8,128)(2,1)S(1)}, u32[]{:S(2)}, u32[]{:S(2)}) collective-permute-start(bf16[64,128]{1,0:T(8,128)(2,1)} %get-tuple-element.39), channel_id=1, source_target_pairs={{0,16},{16,0},{1,17},{17,1},{2,18},{18,2},{3,19},{19,3},{4,20},{20... | collective-permute-start | bytes 49160 | tf_op jit(solution)/shard_map/ppermute | solution.py:780
  8.8 0.4 %collective-permute-start.1 = (bf16[80,1024]{1,0:T(8,128)(2,1)}, bf16[80,1024]{1,0:T(8,128)(2,1)S(1)}, u32[]{:S(2)}, u32[]{:S(2)}) collective-permute-start(bf16[80,1024]{1,0:T(8,128)(2,1)} %get-tuple-element.31), channel_id=1, source_target_pairs={{4,8},{8,4},{12,0},{0,12},{5,9},{9,5},{13,1},{1,13},{6,10},{10,6},... | collective-permute-start | bytes 491528 | tf_op jit(solution)/shard_map/ppermute | solution.py:815
  10.5 0.0 copy-done.7
  10.5 0.0 copy-done.6
  10.5 0.0 copy-done.5
  10.5 0.0 copy-done.4
  10.6 0.6 %one_hots.1 = (bf16[128,4096]{1,0:T(8,128)(2,1)S(1)}, bf16[128,4096]{1,0:T(8,128)(2,1)S(1)}, s32[32,128]{1,0:T(8,128)S(1)}, s32[32,128]{1,0:T(8,128)S(1)}, s32[32,128]{1,0:T(8,128)S(1)}) custom-call(s32[1,1,32,128]{3,2,1,0:T(8,128)S(1)} %copy-done.4, s32[1,1,32,128]{3,2,1,0:T(8,128)S(1)} %copy-done.5, s32[1,1]{1,0:T(1,128)S(6)} %copy.16.a_count, ...), custom_call_target="tpu_custom_call" | custom-call | tf_op jit(solution)/shard_map/one_hots/pallas_call | solution.py:754
  11.2 0.4 %collective-permute-done.4 = bf16[64,128]{1,0:T(8,128)(2,1)S(1)} collective-permute-done((bf16[64,128]{1,0:T(8,128)(2,1)}, bf16[64,128]{1,0:T(8,128)(2,1)S(1)}, u32[]{:S(2)}, u32[]{:S(2)}) %collective-permute-start.4) | collective-permute-done | bytes 16416 | tf_op jit(solution)/shard_map/ppermute | solution.py:780
  11.6 0.0 collective-permute-done.5
  11.6 1.6 %collective-permute-start.6 = (bf16[64,128]{1,0:T(8,128)(2,1)S(1)}, bf16[64,128]{1,0:T(8,128)(2,1)S(1)}, u32[]{:S(2)}, u32[]{:S(2)}) collective-permute-start(bf16[64,128]{1,0:T(8,128)(2,1)S(1)} %get-tuple-element.42), channel_id=1, source_target_pairs={{0,1},{1,0},{2,3},{3,2},{4,5},{5,4},{6,7},{7,6},{8,9},{9,8},{10,11... | collective-permute-start | bytes 49160 | tf_op jit(solution)/shard_map/ppermute | solution.py:791
  13.2 1.5 %collective-permute-start.2 = (bf16[32,1024]{1,0:T(8,128)(2,1)}, bf16[32,1024]{1,0:T(8,128)(2,1)S(1)}, u32[]{:S(2)}, u32[]{:S(2)}) collective-permute-start(bf16[32,1024]{1,0:T(8,128)(2,1)} %get-tuple-element.32), channel_id=1, source_target_pairs={{16,17},{17,16},{18,19},{19,18},{0,8},{8,0},{1,9},{9,1},{2,10},{10... | collective-permute-start | bytes 196616 | tf_op jit(solution)/shard_map/ppermute | solution.py:817
  14.7 0.0 collective-permute-start.3
  14.7 0.5 %collective-permute-start = (bf16[80,1024]{1,0:T(8,128)(2,1)}, bf16[80,1024]{1,0:T(8,128)(2,1)S(1)}, u32[]{:S(2)}, u32[]{:S(2)}) collective-permute-start(bf16[80,1024]{1,0:T(8,128)(2,1)} %get-tuple-element.30), channel_id=1, source_target_pairs={{0,4},{4,0},{8,12},{12,8},{1,5},{5,1},{9,13},{13,9},{2,6},{6,2},{1... | collective-permute-start | bytes 491528 | tf_op jit(solution)/shard_map/ppermute | solution.py:814
  15.2 0.2 collective-permute-done.6.refs_1_
  15.5 0.1 collective-permute-done.1.e3_ref.refs_9_
  15.5 0.0 copy-done.11
  15.5 0.0 copy-done.10
  15.5 0.0 copy-start
  15.5 0.0 copy-start.1
  15.5 0.0 copy-start.3
  15.5 0.0 copy-start.8
  15.6 1.4 %regrid_blocks.1 = (f32[64,128]{1,0:T(8,128)S(1)}, bf16[64,128]{1,0:T(8,128)(2,1)S(1)}, bf16[96,128]{1,0:T(8,128)(2,1)S(1)}, bf16[80,128]{1,0:T(8,128)(2,1)S(1)}) custom-call(f32[64,128]{1,0:T(8,128)S(1)} %get-tuple-element.56.refs_0_, bf16[64,128]{1,0:T(8,128)(2,1)S(1)} %collective-permute-done.6.refs_1_, bf16[128,4096]{1,0:T(8,128)(2,1)S(1)} %get-tuple-element.43.refs_2_, ...), custom_call_target="tpu_custom_call" | custom-call | flops 2200000000 | tf_op jit(solution)/shard_map/regrid_blocks/pallas_call | solution.py:821
  16.9 0.0 copy-start.2
  16.9 0.0 copy-start.9
  16.9 1.6 %collective-permute-start.8 = (bf16[96,128]{1,0:T(8,128)(2,1)S(1)}, bf16[96,128]{1,0:T(8,128)(2,1)S(1)}, u32[]{:S(2)}, u32[]{:S(2)}) collective-permute-start(bf16[96,128]{1,0:T(8,128)(2,1)S(1)} %get-tuple-element.50), channel_id=1, source_target_pairs={{0,2},{2,0},{1,3},{3,1},{4,6},{6,4},{5,7},{7,5},{8,10},{10,8},{9,1... | collective-permute-start | bytes 73736 | tf_op jit(solution)/shard_map/ppermute | solution.py:860
  18.5 2.4 %collective-permute-start.9 = (bf16[80,128]{1,0:T(8,128)(2,1)S(1)}, bf16[80,128]{1,0:T(8,128)(2,1)S(1)}, u32[]{:S(2)}, u32[]{:S(2)}) collective-permute-start(bf16[80,128]{1,0:T(8,128)(2,1)S(1)} %get-tuple-element.51), channel_id=1, source_target_pairs={{0,3},{3,0},{1,2},{2,1},{4,7},{7,4},{5,6},{6,5},{8,11},{11,8},{9,1... | collective-permute-start | bytes 61448 | tf_op jit(solution)/shard_map/ppermute | solution.py:860
  20.9 0.0 collective-permute-done.2.e2_ref
  20.9 0.0 collective-permute-start.7
  20.9 0.0 collective-permute-done.3.e4_ref
  21.0 0.0 collective-permute-done.e1_ref
  21.0 0.0 copy-done
  21.0 0.0 copy-done.1
  21.0 0.0 copy-done.3
  21.0 0.0 copy-done.8
  21.0 0.9 %damping_or_first_step.1 = (bf16[256,1024]{1,0:T(8,128)(2,1)S(1)}, f32[7,16,1024]{2,1,0:T(8,128)S(1)}, f32[10,2,24,1024]{3,2,1,0:T(8,128)S(1)}) custom-call(f32[1,8,32,1024]{3,2,1,0:T(8,128)S(1)} %copy-done, s32[8,1024]{1,0:T(8,128)S(1)} %copy-done.3, f32[1,128]{1,0:T(1,128)S(1)} %bitcast.4, bf16[1024,512]{1,0:T(8,128)(2,1)S(1)} %copy-done.1, ...), custom_call_target="tpu_custom_call" | custom-call | tf_op jit(solution)/shard_map/damping_or_first_step/pallas_call | solution.py:880
  21.9 2.8 %collective-permute-done.7.refs_0_ = bf16[64,128]{1,0:T(8,128)(2,1)S(1)} collective-permute-done((bf16[64,128]{1,0:T(8,128)(2,1)S(1)}, bf16[64,128]{1,0:T(8,128)(2,1)S(1)}, u32[]{:S(2)}, u32[]{:S(2)}) %collective-permute-start.7) | collective-permute-done | bytes 16416 | tf_op jit(solution)/shard_map/ppermute | solution.py:860
  24.7 0.0 collective-permute-done.9.refs_2_
  24.7 0.0 collective-permute-done.8.refs_1_
  24.7 0.1 collective-permute-start.10
  24.8 1.5 %collective-permute-start.11 = (bf16[64,128]{1,0:T(8,128)(2,1)S(1)}, bf16[64,128]{1,0:T(8,128)(2,1)S(1)}, u32[]{:S(2)}, u32[]{:S(2)}) collective-permute-start(bf16[64,128]{1,0:T(8,128)(2,1)S(1)} %get-tuple-element.54), channel_id=1, source_target_pairs={{4,8},{8,4},{12,0},{0,12},{5,9},{9,5},{13,1},{1,13},{6,10},{10,6},... | collective-permute-start | bytes 49160 | tf_op jit(solution)/shard_map/ppermute | solution.py:914
  26.3 0.0 copy-done.2
  26.3 0.0 copy-done.9
  26.4 0.4 %inverse_or_second_step.1 = (f32[8,32,1024]{2,1,0:T(8,128)S(1)}, f32[32,128]{1,0:T(8,128)S(1)}) custom-call(f32[1,128]{1,0:T(1,128)S(1)} %bitcast.5, bf16[1024,512]{1,0:T(8,128)(2,1)S(1)} %copy-done.2, bf16[256,1024]{1,0:T(8,128)(2,1)S(1)} %get-tuple-element.34.zb_ref, f32[7,16,1024]{2,1,0:T(8,128)S(1)} %get-tuple-element.35.c_ref._, ...), custom_call_target="tpu_custom_call" | custom-call | tf_op jit(solution)/shard_map/inverse_or_second_step/pallas_call | solution.py:915
  26.8 0.0 collective-permute-done.10.near_ref
  26.8 1.2 %collective-permute-done.11.far_ref = bf16[64,128]{1,0:T(8,128)(2,1)S(1)} collective-permute-done((bf16[64,128]{1,0:T(8,128)(2,1)S(1)}, bf16[64,128]{1,0:T(8,128)(2,1)S(1)}, u32[]{:S(2)}, u32[]{:S(2)}) %collective-permute-start.11) | collective-permute-done | bytes 16416 | tf_op jit(solution)/shard_map/ppermute | solution.py:914
  28.1 1.0 %add_surface_terms.1 = f32[1,8,32,1024]{3,2,1,0:T(8,128)} custom-call(f32[32,128]{1,0:T(8,128)S(1)} %get-tuple-element.37.column_ref, f32[8,32,1024]{2,1,0:T(8,128)S(1)} %get-tuple-element.38.base_ref, f32[7,16,1024]{2,1,0:T(8,128)S(1)} %get-tuple-element.35.c_ref._, f32[64,128]{1,0:T(8,128)S(1)} %get-tuple-element.52.sum_ref, ...), custom_call_target="tpu_custom_call" | custom-call | tf_op jit(solution)/shard_map/add_surface_terms/pallas_call | solution.py:923
  (2 shorter events, 0.1 us)
Async XLA Ops:
  0.0 10.5 %copy-start.7 = (s32[1,1,32,128]{3,2,1,0:T(8,128)S(1)}, s32[1,1,32,128]{3,2,1,0:T(8,128)}, u32[]{:S(2)}) copy-start(s32[1,1,32,128]{3,2,1,0:T(8,128)} %m_dst.1) | copy-start | bytes 49156
  0.0 10.5 %copy-start.6 = (s32[1,1,32,128]{3,2,1,0:T(8,128)S(1)}, s32[1,1,32,128]{3,2,1,0:T(8,128)}, u32[]{:S(2)}) copy-start(s32[1,1,32,128]{3,2,1,0:T(8,128)} %m_src.1) | copy-start | bytes 49156
  0.0 10.5 %copy-start.5 = (s32[1,1,32,128]{3,2,1,0:T(8,128)S(1)}, s32[1,1,32,128]{3,2,1,0:T(8,128)}, u32[]{:S(2)}) copy-start(s32[1,1,32,128]{3,2,1,0:T(8,128)} %a_dst.1) | copy-start | bytes 49156
  0.0 10.5 %copy-start.4 = (s32[1,1,32,128]{3,2,1,0:T(8,128)S(1)}, s32[1,1,32,128]{3,2,1,0:T(8,128)}, u32[]{:S(2)}) copy-start(s32[1,1,32,128]{3,2,1,0:T(8,128)} %a_src.1) | copy-start | bytes 49156
  0.0 15.5 %copy-start.11 = (bf16[1,1,32,128,128]{4,3,2,1,0:T(8,128)(2,1)S(1)}, bf16[1,1,32,128,128]{4,3,2,1,0:T(8,128)(2,1)}, u32[]{:S(2)}) copy-start(bf16[1,1,32,128,128]{4,3,2,1,0:T(8,128)(2,1)} %refs_8_.1) | copy-start | bytes 3145732
  0.0 15.5 %copy-start.10 = (bf16[1,1,32,128,128]{4,3,2,1,0:T(8,128)(2,1)S(1)}, bf16[1,1,32,128,128]{4,3,2,1,0:T(8,128)(2,1)}, u32[]{:S(2)}) copy-start(bf16[1,1,32,128,128]{4,3,2,1,0:T(8,128)(2,1)} %refs_7_.1) | copy-start | bytes 3145732
  3.3 8.3 %collective-permute-start.5 = (bf16[80,128]{1,0:T(8,128)(2,1)}, bf16[80,128]{1,0:T(8,128)(2,1)S(1)}, u32[]{:S(2)}, u32[]{:S(2)}) collective-permute-start(bf16[80,128]{1,0:T(8,128)(2,1)} %get-tuple-element.40), channel_id=1, source_target_pairs={{0,18},{18,0},{1,19},{19,1},{2,16},{16,2},{3,17},{17,3},{4,22},{22... | collective-permute-start | bytes 61448 | tf_op jit(solution)/shard_map/ppermute | solution.py:782
  7.6 3.9 %collective-permute-start.4 = (bf16[64,128]{1,0:T(8,128)(2,1)}, bf16[64,128]{1,0:T(8,128)(2,1)S(1)}, u32[]{:S(2)}, u32[]{:S(2)}) collective-permute-start(bf16[64,128]{1,0:T(8,128)(2,1)} %get-tuple-element.39), channel_id=1, source_target_pairs={{0,16},{16,0},{1,17},{17,1},{2,18},{18,2},{3,19},{19,3},{4,20},{20... | collective-permute-start | bytes 49160 | tf_op jit(solution)/shard_map/ppermute | solution.py:780
  8.8 6.7 %collective-permute-start.1 = (bf16[80,1024]{1,0:T(8,128)(2,1)}, bf16[80,1024]{1,0:T(8,128)(2,1)S(1)}, u32[]{:S(2)}, u32[]{:S(2)}) collective-permute-start(bf16[80,1024]{1,0:T(8,128)(2,1)} %get-tuple-element.31), channel_id=1, source_target_pairs={{4,8},{8,4},{12,0},{0,12},{5,9},{9,5},{13,1},{1,13},{6,10},{10,6},... | collective-permute-start | bytes 491528 | tf_op jit(solution)/shard_map/ppermute | solution.py:815
  11.6 3.9 %collective-permute-start.6 = (bf16[64,128]{1,0:T(8,128)(2,1)S(1)}, bf16[64,128]{1,0:T(8,128)(2,1)S(1)}, u32[]{:S(2)}, u32[]{:S(2)}) collective-permute-start(bf16[64,128]{1,0:T(8,128)(2,1)S(1)} %get-tuple-element.42), channel_id=1, source_target_pairs={{0,1},{1,0},{2,3},{3,2},{4,5},{5,4},{6,7},{7,6},{8,9},{9,8},{10,11... | collective-permute-start | bytes 49160 | tf_op jit(solution)/shard_map/ppermute | solution.py:791
  13.2 7.7 %collective-permute-start.2 = (bf16[32,1024]{1,0:T(8,128)(2,1)}, bf16[32,1024]{1,0:T(8,128)(2,1)S(1)}, u32[]{:S(2)}, u32[]{:S(2)}) collective-permute-start(bf16[32,1024]{1,0:T(8,128)(2,1)} %get-tuple-element.32), channel_id=1, source_target_pairs={{16,17},{17,16},{18,19},{19,18},{0,8},{8,0},{1,9},{9,1},{2,10},{10... | collective-permute-start | bytes 196616 | tf_op jit(solution)/shard_map/ppermute | solution.py:817
  14.7 6.2 %collective-permute-start.3 = (bf16[32,1024]{1,0:T(8,128)(2,1)}, bf16[32,1024]{1,0:T(8,128)(2,1)S(1)}, u32[]{:S(2)}, u32[]{:S(2)}) collective-permute-start(bf16[32,1024]{1,0:T(8,128)(2,1)} %get-tuple-element.33), channel_id=1, source_target_pairs={{17,18},{18,17},{16,20},{20,16},{19,23},{23,19},{0,4},{4,0},{1,5},... | collective-permute-start | bytes 196616 | tf_op jit(solution)/shard_map/ppermute | solution.py:818
  14.7 6.2 %collective-permute-start = (bf16[80,1024]{1,0:T(8,128)(2,1)}, bf16[80,1024]{1,0:T(8,128)(2,1)S(1)}, u32[]{:S(2)}, u32[]{:S(2)}) collective-permute-start(bf16[80,1024]{1,0:T(8,128)(2,1)} %get-tuple-element.30), channel_id=1, source_target_pairs={{0,4},{4,0},{8,12},{12,8},{1,5},{5,1},{9,13},{13,9},{2,6},{6,2},{1... | collective-permute-start | bytes 491528 | tf_op jit(solution)/shard_map/ppermute | solution.py:814
  15.5 5.4 %copy-start = (f32[1,8,32,1024]{3,2,1,0:T(8,128)S(1)}, f32[1,8,32,1024]{3,2,1,0:T(8,128)}, u32[]{:S(2)}) copy-start(f32[1,8,32,1024]{3,2,1,0:T(8,128)} %x_ref.1) | copy-start | bytes 3145732
  15.5 5.5 %copy-start.1 = (bf16[1024,512]{1,0:T(8,128)(2,1)S(1)}, bf16[1024,512]{1,0:T(8,128)(2,1)}, u32[]{:S(2)}) copy-start(bf16[1024,512]{1,0:T(8,128)(2,1)} %constant.4.clone.table_hbm.table_ref) | copy-start | bytes 3145732
  15.5 5.5 %copy-start.3 = (s32[8,1024]{1,0:T(8,128)S(1)}, s32[8,1024]{1,0:T(8,128)}, u32[]{:S(2)}) copy-start(s32[8,1024]{1,0:T(8,128)} %wet_ref.1) | copy-start | bytes 98308
  15.5 5.5 %copy-start.8 = (f32[128]{0:T(128)S(1)}, f32[128]{0:T(128)}, u32[]{:S(2)}) copy-start(f32[128]{0:T(128)} %param.19) | copy-start | bytes 1540
  16.9 9.4 %copy-start.2 = (bf16[1024,512]{1,0:T(8,128)(2,1)S(1)}, bf16[1024,512]{1,0:T(8,128)(2,1)}, u32[]{:S(2)}) copy-start(bf16[1024,512]{1,0:T(8,128)(2,1)} %constant.5.clone.table_ref) | copy-start | bytes 3145732
  16.9 9.4 %copy-start.9 = (f32[128]{0:T(128)S(1)}, f32[128]{0:T(128)}, u32[]{:S(2)}) copy-start(f32[128]{0:T(128)} %param.18) | copy-start | bytes 1540
  16.9 7.7 %collective-permute-start.8 = (bf16[96,128]{1,0:T(8,128)(2,1)S(1)}, bf16[96,128]{1,0:T(8,128)(2,1)S(1)}, u32[]{:S(2)}, u32[]{:S(2)}) collective-permute-start(bf16[96,128]{1,0:T(8,128)(2,1)S(1)} %get-tuple-element.50), channel_id=1, source_target_pairs={{0,2},{2,0},{1,3},{3,1},{4,6},{6,4},{5,7},{7,5},{8,10},{10,8},{9,1... | collective-permute-start | bytes 73736 | tf_op jit(solution)/shard_map/ppermute | solution.py:860
  18.5 6.2 %collective-permute-start.9 = (bf16[80,128]{1,0:T(8,128)(2,1)S(1)}, bf16[80,128]{1,0:T(8,128)(2,1)S(1)}, u32[]{:S(2)}, u32[]{:S(2)}) collective-permute-start(bf16[80,128]{1,0:T(8,128)(2,1)S(1)} %get-tuple-element.51), channel_id=1, source_target_pairs={{0,3},{3,0},{1,2},{2,1},{4,7},{7,4},{5,6},{6,5},{8,11},{11,8},{9,1... | collective-permute-start | bytes 61448 | tf_op jit(solution)/shard_map/ppermute | solution.py:860
  20.9 3.7 %collective-permute-start.7 = (bf16[64,128]{1,0:T(8,128)(2,1)S(1)}, bf16[64,128]{1,0:T(8,128)(2,1)S(1)}, u32[]{:S(2)}, u32[]{:S(2)}) collective-permute-start(bf16[64,128]{1,0:T(8,128)(2,1)S(1)} %get-tuple-element.49), channel_id=1, source_target_pairs={{0,1},{1,0},{2,3},{3,2},{4,5},{5,4},{6,7},{7,6},{8,9},{9,8},{10,11... | collective-permute-start | bytes 49160 | tf_op jit(solution)/shard_map/ppermute | solution.py:860
  24.7 2.1 %collective-permute-start.10 = (bf16[64,128]{1,0:T(8,128)(2,1)S(1)}, bf16[64,128]{1,0:T(8,128)(2,1)S(1)}, u32[]{:S(2)}, u32[]{:S(2)}) collective-permute-start(bf16[64,128]{1,0:T(8,128)(2,1)S(1)} %get-tuple-element.53), channel_id=1, source_target_pairs={{0,4},{4,0},{8,12},{12,8},{1,5},{5,1},{9,13},{13,9},{2,6},{6,2},{1... | collective-permute-start | bytes 49160 | tf_op jit(solution)/shard_map/ppermute | solution.py:913
  24.8 3.2 %collective-permute-start.11 = (bf16[64,128]{1,0:T(8,128)(2,1)S(1)}, bf16[64,128]{1,0:T(8,128)(2,1)S(1)}, u32[]{:S(2)}, u32[]{:S(2)}) collective-permute-start(bf16[64,128]{1,0:T(8,128)(2,1)S(1)} %get-tuple-element.54), channel_id=1, source_target_pairs={{4,8},{8,4},{12,0},{0,12},{5,9},{9,5},{13,1},{1,13},{6,10},{10,6},... | collective-permute-start | bytes 49160 | tf_op jit(solution)/shard_map/ppermute | solution.py:914

commit v22 on v21

--- a/solution.py
+++ b/solution.py
@@ -560,14 +560,14 @@
         lax.fori_loop(0, span, first, 0)
 
 
-def second_step_kernel(gain_ref, table_ref, zb_ref, c_ref, t1_ref, base_ref, column_ref):
+def second_step_kernel(gain_ref, table_ref, zb_ref, c_ref, t1_ref, sum_ref, base_ref):
     rows, channels, columns = base_ref.shape
     is_atmos = lax.axis_index("comp") == 0
 
     @pl.when(is_atmos)
     def _():
         response = channel_column(gain_ref[...], channels, lax.axis_index("gy") * channels)
-        column_ref[...] = jnp.broadcast_to(response, column_ref.shape)
+        forcing = from_tiles(sum_ref[...], rows)
         half = columns // 2
         step = 256
         for n in range(0, half, step):
@@ -579,8 +579,10 @@
                 ).reshape(rows, channels, step)
                 for k in range(2)
             ]
-            base_ref[:, :, n : n + step] = even + odd
-            base_ref[:, :, n + half : n + half + step] = even - odd
+            for r in range(rows):
+                for lane, part in ((n, even[r] + odd[r]), (n + half, even[r] - odd[r])):
+                    lanes = slice(lane, lane + step)
+                    base_ref[r, :, lanes] = part + response * forcing[r : r + 1, lanes]
 
     @pl.when(jnp.logical_not(is_atmos))
     def _():
@@ -597,7 +599,7 @@
 
 
 def last_kernel(
-    groups_x, groups_y, column_ref, base_ref, c_ref, sum_ref, near_ref, far_ref, out_hbm,
+    groups_x, groups_y, base_ref, c_ref, sum_ref, near_ref, far_ref, out_hbm,
     out_ref, e_ref, heat_ref, sem,
 ):
     rows, channels, columns = out_ref.shape
@@ -607,17 +609,19 @@
     copies = [
         pltpu.make_async_copy(out_ref.at[r], out_hbm.at[0, r], sem.at[r]) for r in range(rows)
     ]
+    as_they_are = [
+        pltpu.make_async_copy(base_ref.at[r], out_hbm.at[0, r], sem.at[r]) for r in range(rows)
+    ]
 
     @pl.when(is_atmos)
     def _():
-        for r in range(rows):
-            for k in range(columns // LANES):
-                lanes = slice(k * LANES, (k + 1) * LANES)
-                at = k * rows + r
-                out_ref[r, :, lanes] = (
-                    base_ref[r, :, lanes] + column_ref[...] * sum_ref[at : at + 1, :]
-                )
-            copies[r].start()
+        for copy in as_they_are:
+            copy.start()
+
+    @pl.when(jnp.logical_and(jnp.logical_not(is_atmos), col_group > 0))
+    def _():
+        for copy in as_they_are[1:-1]:
+            copy.start()
 
     @pl.when(jnp.logical_not(is_atmos))
     def _():
@@ -653,30 +657,36 @@
             heat_ref[0] = first
             heat_ref[1] = second
 
-        for r in [1, rows - 2] + list(range(2, rows - 2)) + [0, rows - 1]:
+        for r in (0, rows - 1):
             out_ref[r] = base_ref[r]
-            for t in range(2):
-                c = t * levels
-                for edge, factor, lines in ((0, by_low, low), (rows - 1, by_high, high)):
-                    if r == edge:
-                        out_ref[r, c : c + 1, :] = out_ref[r, c : c + 1, :] + (
-                            has_before * factor * lines[t + 1 : t + 2]
-                        )
-                        d = c + levels - 1
-                        out_ref[r, d : d + 1, :] = out_ref[r, d : d + 1, :] + (
-                            has_after * factor * lines[t + 3 : t + 4]
-                        )
-
-            @pl.when(col_group == 0)
-            def _():
+        for t in range(2):
+            c = t * levels
+            d = c + levels - 1
+            for r, factor, lines in ((0, by_low, low), (rows - 1, by_high, high)):
+                out_ref[r, c : c + 1, :] = out_ref[r, c : c + 1, :] + (
+                    has_before * factor * lines[t + 1 : t + 2]
+                )
+                out_ref[r, d : d + 1, :] = out_ref[r, d : d + 1, :] + (
+                    has_after * factor * lines[t + 3 : t + 4]
+                )
+
+        @pl.when(col_group == 0)
+        def _():
+            for r in range(rows):
+                if r not in (0, rows - 1):
+                    out_ref[r] = base_ref[r]
                 for t, gain in enumerate((heat_gain, salt_gain)):
                     c = t * levels
                     for k in range(2):
                         out_ref[r, c + k : c + k + 1, :] = (
                             out_ref[r, c + k : c + k + 1, :] + gain * heat_ref[k, r : r + 1, :]
                         )
-
-            copies[r].start()
+                copies[r].start()
+
+        @pl.when(col_group > 0)
+        def _():
+            copies[0].start()
+            copies[-1].start()
 
     for copy in copies:
         copy.wait()
@@ -912,18 +922,18 @@
 
     near = lax.ppermute(near, "gx", both_ways(ring_pairs(groups_x, 0)))
     far = lax.ppermute(far, "gx", both_ways(ring_pairs(groups_x, 1)))
-    base, column = pl.pallas_call(
+    base = pl.pallas_call(
         second_step_kernel,
-        out_shape=[shape((rows, channels, columns), f32), shape((channels, LANES), f32)],
-        in_specs=[vmem] * 5,
-        out_specs=[vmem] * 2,
+        out_shape=shape((rows, channels, columns), f32),
+        in_specs=[vmem] * 6,
+        out_specs=vmem,
         compiler_params=params(),
         name="inverse_or_second_step",
-    )(gain_row, inverse, damped, coefs, stepped)
+    )(gain_row, inverse, damped, coefs, stepped, surface_sum)
     return pl.pallas_call(
         functools.partial(last_kernel, groups_x, groups_y),
         out_shape=shape(fields.shape, f32),
-        in_specs=[vmem] * 6,
+        in_specs=[vmem] * 5,
         out_specs=hbm,
         scratch_shapes=[
             pltpu.VMEM((rows, channels, columns), f32),
@@ -933,7 +943,7 @@
         ],
         compiler_params=params(),
         name="add_surface_terms",
-    )(column, base, coefs, surface_sum, near, far)
+    )(base, coefs, surface_sum, near, far)
 
 
 def solution(mesh):

time: 29.3 us -> 29.2 us (level)
  no operation moved by 1% of the time
where the time goes in v22:
time: 29.2 us; the launch traced here: 29.1 us
  starting transfers between devices  15.2 us (52%)
  Pallas kernels  7.63 us (26%)
  waiting for transfers between devices  4.7 us (16%)
  between operations  1.5 us (5%)
    ppermute x1, starting transfers between devices, local(): far = lax.ppermute(wide, ('comp', 'gy'), partner_route(mask))  4.35 us
    ppermute x3, starting transfers between devices, local(): lax.ppermute(block, axes, landing_route(mask))  4.01 us
    pallas_call x1, Pallas kernels, local(): pl.pallas_call(functools.partial(start_kernel, groups_x, paired), out_sha...  3.24 us
    ppermute x3, waiting for transfers between devices, local(): lax.ppermute(block, axes, landing_route(mask))  2.76 us
    ppermute x1, starting transfers between devices, local(): lax.ppermute(coarse, 'gy', sum_route(mask))  1.64 us
    ppermute x1, starting transfers between devices, local(): far = lax.ppermute(far, 'gx', both_ways(ring_pairs(groups_x, 1)))  1.51 us
    ppermute x1, starting transfers between devices, local(): e2 = lax.ppermute(e2, axes, level_route(0))  1.49 us
    pallas_call x1, Pallas kernels, local(): pl.pallas_call(functools.partial(regrid_kernel, len(surfaces)), out_shape...  1.35 us
  transfers between devices with their start and end apart: 12, of which 5 were waited for; matrix products, arithmetic and copies ran while one was open for 0% of the time, Pallas kernels for 11%

profile of v22, /device:TPU:0, one launch (start us, length us, event | category | flops | bytes accessed | tf_op | source)
XLA Modules:
  0.0 29.1 jit_solution(14844530154333028991)
XLA Ops:
  0.0 0.0 copy-start.7
  0.0 0.0 copy-start.6
  0.0 0.0 copy-start.5
  0.0 0.0 copy-start.4
  0.0 0.0 copy-start.11
  0.0 0.0 copy-start.10
  0.0 3.2 %surface_and_forward_or_halos.1 = (bf16[64,128]{1,0:T(8,128)(2,1)}, bf16[80,128]{1,0:T(8,128)(2,1)}, bf16[80,1024]{1,0:T(8,128)(2,1)}, bf16[80,1024]{1,0:T(8,128...) custom-call(f32[1,8,32,1024]{3,2,1,0:T(8,128)} %x_ref.1, s32[8,1024]{1,0:T(8,128)} %wet_ref.1, ...), custom_call_target="tpu_custom_call" | custom-call | tf_op jit(solution)/shard_map/surface_and_forward_or_halos/pallas_call | solution.py:740
  3.3 4.4 %collective-permute-start.5 = (bf16[80,128]{1,0:T(8,128)(2,1)}, bf16[80,128]{1,0:T(8,128)(2,1)S(1)}, u32[]{:S(2)}, u32[]{:S(2)}) collective-permute-start(bf16[80,128]{1,0:T(8,128)(2,1)} %get-tuple-element.36), channel_id=1, source_target_pairs={{0,18},{18,0},{1,19},{19,1},{2,16},{16,2},{3,17},{17,3},{4,22},{22... | collective-permute-start | bytes 61448 | tf_op jit(solution)/shard_map/ppermute | solution.py:792
  7.6 1.2 %collective-permute-start.4 = (bf16[64,128]{1,0:T(8,128)(2,1)}, bf16[64,128]{1,0:T(8,128)(2,1)S(1)}, u32[]{:S(2)}, u32[]{:S(2)}) collective-permute-start(bf16[64,128]{1,0:T(8,128)(2,1)} %get-tuple-element.35), channel_id=1, source_target_pairs={{0,16},{16,0},{1,17},{17,1},{2,18},{18,2},{3,19},{19,3},{4,20},{20... | collective-permute-start | bytes 49160 | tf_op jit(solution)/shard_map/ppermute | solution.py:790
  8.9 0.4 %collective-permute-start.1 = (bf16[80,1024]{1,0:T(8,128)(2,1)}, bf16[80,1024]{1,0:T(8,128)(2,1)S(1)}, u32[]{:S(2)}, u32[]{:S(2)}) collective-permute-start(bf16[80,1024]{1,0:T(8,128)(2,1)} %get-tuple-element.29), channel_id=1, source_target_pairs={{4,8},{8,4},{12,0},{0,12},{5,9},{9,5},{13,1},{1,13},{6,10},{10,6},... | collective-permute-start | bytes 491528 | tf_op jit(solution)/shard_map/ppermute | solution.py:825
  10.5 0.0 copy-done.7
  10.5 0.0 copy-done.6
  10.5 0.0 copy-done.5
  10.6 0.0 copy-done.4
  10.6 0.6 %one_hots.1 = (bf16[128,4096]{1,0:T(8,128)(2,1)S(1)}, bf16[128,4096]{1,0:T(8,128)(2,1)S(1)}, s32[32,128]{1,0:T(8,128)S(1)}, s32[32,128]{1,0:T(8,128)S(1)}, s32[32,128]{1,0:T(8,128)S(1)}) custom-call(s32[1,1,32,128]{3,2,1,0:T(8,128)S(1)} %copy-done.4, s32[1,1,32,128]{3,2,1,0:T(8,128)S(1)} %copy-done.5, s32[1,1]{1,0:T(1,128)S(6)} %copy.16.a_count, ...), custom_call_target="tpu_custom_call" | custom-call | tf_op jit(solution)/shard_map/one_hots/pallas_call | solution.py:764
  11.2 0.4 %collective-permute-done.4 = bf16[64,128]{1,0:T(8,128)(2,1)S(1)} collective-permute-done((bf16[64,128]{1,0:T(8,128)(2,1)}, bf16[64,128]{1,0:T(8,128)(2,1)S(1)}, u32[]{:S(2)}, u32[]{:S(2)}) %collective-permute-start.4) | collective-permute-done | bytes 16416 | tf_op jit(solution)/shard_map/ppermute | solution.py:790
  11.6 0.0 collective-permute-done.5
  11.6 1.6 %collective-permute-start.6 = (bf16[64,128]{1,0:T(8,128)(2,1)S(1)}, bf16[64,128]{1,0:T(8,128)(2,1)S(1)}, u32[]{:S(2)}, u32[]{:S(2)}) collective-permute-start(bf16[64,128]{1,0:T(8,128)(2,1)S(1)} %get-tuple-element.38), channel_id=1, source_target_pairs={{0,1},{1,0},{2,3},{3,2},{4,5},{5,4},{6,7},{7,6},{8,9},{9,8},{10,11... | collective-permute-start | bytes 49160 | tf_op jit(solution)/shard_map/ppermute | solution.py:801
  13.2 1.5 %collective-permute-start.2 = (bf16[32,1024]{1,0:T(8,128)(2,1)}, bf16[32,1024]{1,0:T(8,128)(2,1)S(1)}, u32[]{:S(2)}, u32[]{:S(2)}) collective-permute-start(bf16[32,1024]{1,0:T(8,128)(2,1)} %get-tuple-element.30), channel_id=1, source_target_pairs={{16,17},{17,16},{18,19},{19,18},{0,8},{8,0},{1,9},{9,1},{2,10},{10... | collective-permute-start | bytes 196616 | tf_op jit(solution)/shard_map/ppermute | solution.py:827
  14.7 0.0 collective-permute-start.3
  14.7 0.5 %collective-permute-start = (bf16[80,1024]{1,0:T(8,128)(2,1)}, bf16[80,1024]{1,0:T(8,128)(2,1)S(1)}, u32[]{:S(2)}, u32[]{:S(2)}) collective-permute-start(bf16[80,1024]{1,0:T(8,128)(2,1)} %get-tuple-element.28), channel_id=1, source_target_pairs={{0,4},{4,0},{8,12},{12,8},{1,5},{5,1},{9,13},{13,9},{2,6},{6,2},{1... | collective-permute-start | bytes 491528 | tf_op jit(solution)/shard_map/ppermute | solution.py:824
  15.2 0.2 collective-permute-done.6.refs_1_
  15.5 0.1 collective-permute-done.1.e3_ref.refs_9_
  15.5 0.0 copy-done.11
  15.5 0.0 copy-done.10
  15.5 0.0 copy-start
  15.5 0.0 copy-start.1
  15.5 0.0 copy-start.3
  15.5 0.0 copy-start.8
  15.6 1.4 %regrid_blocks.1 = (f32[64,128]{1,0:T(8,128)S(1)}, bf16[64,128]{1,0:T(8,128)(2,1)S(1)}, bf16[96,128]{1,0:T(8,128)(2,1)S(1)}, bf16[80,128]{1,0:T(8,128)(2,1)S(1)}) custom-call(f32[64,128]{1,0:T(8,128)S(1)} %get-tuple-element.52.refs_0_, bf16[64,128]{1,0:T(8,128)(2,1)S(1)} %collective-permute-done.6.refs_1_, bf16[128,4096]{1,0:T(8,128)(2,1)S(1)} %get-tuple-element.39.refs_2_, ...), custom_call_target="tpu_custom_call" | custom-call | flops 2200000000 | tf_op jit(solution)/shard_map/regrid_blocks/pallas_call | solution.py:831
  16.9 0.0 copy-start.2
  16.9 0.0 copy-start.9
  16.9 1.6 %collective-permute-start.8 = (bf16[96,128]{1,0:T(8,128)(2,1)S(1)}, bf16[96,128]{1,0:T(8,128)(2,1)S(1)}, u32[]{:S(2)}, u32[]{:S(2)}) collective-permute-start(bf16[96,128]{1,0:T(8,128)(2,1)S(1)} %get-tuple-element.46), channel_id=1, source_target_pairs={{0,2},{2,0},{1,3},{3,1},{4,6},{6,4},{5,7},{7,5},{8,10},{10,8},{9,1... | collective-permute-start | bytes 73736 | tf_op jit(solution)/shard_map/ppermute | solution.py:870
  18.5 2.4 %collective-permute-start.9 = (bf16[80,128]{1,0:T(8,128)(2,1)S(1)}, bf16[80,128]{1,0:T(8,128)(2,1)S(1)}, u32[]{:S(2)}, u32[]{:S(2)}) collective-permute-start(bf16[80,128]{1,0:T(8,128)(2,1)S(1)} %get-tuple-element.47), channel_id=1, source_target_pairs={{0,3},{3,0},{1,2},{2,1},{4,7},{7,4},{5,6},{6,5},{8,11},{11,8},{9,1... | collective-permute-start | bytes 61448 | tf_op jit(solution)/shard_map/ppermute | solution.py:870
  20.9 0.0 collective-permute-done.2.e2_ref
  21.0 0.0 collective-permute-start.7
  21.0 0.0 collective-permute-done.3.e4_ref
  21.0 0.0 collective-permute-done.e1_ref
  21.0 0.0 copy-done
  21.0 0.0 copy-done.1
  21.0 0.0 copy-done.3
  21.0 0.0 copy-done.8
  21.0 0.9 %damping_or_first_step.1 = (bf16[256,1024]{1,0:T(8,128)(2,1)S(1)}, f32[7,16,1024]{2,1,0:T(8,128)S(1)}, f32[10,2,24,1024]{3,2,1,0:T(8,128)S(1)}) custom-call(f32[1,8,32,1024]{3,2,1,0:T(8,128)S(1)} %copy-done, s32[8,1024]{1,0:T(8,128)S(1)} %copy-done.3, f32[1,128]{1,0:T(1,128)S(1)} %bitcast.4, bf16[1024,512]{1,0:T(8,128)(2,1)S(1)} %copy-done.1, ...), custom_call_target="tpu_custom_call" | custom-call | tf_op jit(solution)/shard_map/damping_or_first_step/pallas_call | solution.py:890
  21.9 2.8 %collective-permute-done.7.refs_0_ = bf16[64,128]{1,0:T(8,128)(2,1)S(1)} collective-permute-done((bf16[64,128]{1,0:T(8,128)(2,1)S(1)}, bf16[64,128]{1,0:T(8,128)(2,1)S(1)}, u32[]{:S(2)}, u32[]{:S(2)}) %collective-permute-start.7) | collective-permute-done | bytes 16416 | tf_op jit(solution)/shard_map/ppermute | solution.py:870
  24.7 0.0 collective-permute-done.9.refs_2_
  24.7 0.0 collective-permute-done.8.refs_1_
  24.7 0.1 collective-permute-start.10
  24.8 1.5 %collective-permute-start.11 = (bf16[64,128]{1,0:T(8,128)(2,1)S(1)}, bf16[64,128]{1,0:T(8,128)(2,1)S(1)}, u32[]{:S(2)}, u32[]{:S(2)}) collective-permute-start(bf16[64,128]{1,0:T(8,128)(2,1)S(1)} %get-tuple-element.50), channel_id=1, source_target_pairs={{4,8},{8,4},{12,0},{0,12},{5,9},{9,5},{13,1},{1,13},{6,10},{10,6},... | collective-permute-start | bytes 49160 | tf_op jit(solution)/shard_map/ppermute | solution.py:924
  26.3 0.0 copy-done.2
  26.3 0.0 copy-done.9
  26.3 0.5 %inverse_or_second_step.1.base_ref = f32[8,32,1024]{2,1,0:T(8,128)S(1)} custom-call(f32[1,128]{1,0:T(1,128)S(1)} %bitcast.5, bf16[1024,512]{1,0:T(8,128)(2,1)S(1)} %copy-done.2, bf16[256,1024]{1,0:T(8,128)(2,1)S(1)} %get-tuple-element.32.zb_ref, f32[7,16,1024]{2,1,0:T(8,128)S(1)} %get-tuple-element.33._.c_ref, ...), custom_call_target="tpu_custom_call" | custom-call | tf_op jit(solution)/shard_map/inverse_or_second_step/pallas_call | solution.py:925
  26.8 0.0 collective-permute-done.10.near_ref
  26.8 1.2 %collective-permute-done.11.far_ref = bf16[64,128]{1,0:T(8,128)(2,1)S(1)} collective-permute-done((bf16[64,128]{1,0:T(8,128)(2,1)S(1)}, bf16[64,128]{1,0:T(8,128)(2,1)S(1)}, u32[]{:S(2)}, u32[]{:S(2)}) %collective-permute-start.11) | collective-permute-done | bytes 16416 | tf_op jit(solution)/shard_map/ppermute | solution.py:924
  28.1 1.0 %add_surface_terms.1 = f32[1,8,32,1024]{3,2,1,0:T(8,128)} custom-call(f32[8,32,1024]{2,1,0:T(8,128)S(1)} %inverse_or_second_step.1.base_ref, f32[7,16,1024]{2,1,0:T(8,128)S(1)} %get-tuple-element.33._.c_ref, f32[64,128]{1,0:T(8,128)S(1)} %get-tuple-element.48.sum_ref, bf16[64,128]{1,0:T(8,128)(2,1)S(1)} %collective-permute-done.10.near_ref, ...), custom_call_target="tpu_custom_call" | custom-call | tf_op jit(solution)/shard_map/add_surface_terms/pallas_call | solution.py:933
  (2 shorter events, 0.1 us)
Async XLA Ops:
  0.0 10.5 %copy-start.7 = (s32[1,1,32,128]{3,2,1,0:T(8,128)S(1)}, s32[1,1,32,128]{3,2,1,0:T(8,128)}, u32[]{:S(2)}) copy-start(s32[1,1,32,128]{3,2,1,0:T(8,128)} %m_dst.1) | copy-start | bytes 49156
  0.0 10.5 %copy-start.6 = (s32[1,1,32,128]{3,2,1,0:T(8,128)S(1)}, s32[1,1,32,128]{3,2,1,0:T(8,128)}, u32[]{:S(2)}) copy-start(s32[1,1,32,128]{3,2,1,0:T(8,128)} %m_src.1) | copy-start | bytes 49156
  0.0 10.5 %copy-start.5 = (s32[1,1,32,128]{3,2,1,0:T(8,128)S(1)}, s32[1,1,32,128]{3,2,1,0:T(8,128)}, u32[]{:S(2)}) copy-start(s32[1,1,32,128]{3,2,1,0:T(8,128)} %a_dst.1) | copy-start | bytes 49156
  0.0 10.5 %copy-start.4 = (s32[1,1,32,128]{3,2,1,0:T(8,128)S(1)}, s32[1,1,32,128]{3,2,1,0:T(8,128)}, u32[]{:S(2)}) copy-start(s32[1,1,32,128]{3,2,1,0:T(8,128)} %a_src.1) | copy-start | bytes 49156
  0.0 15.5 %copy-start.11 = (bf16[1,1,32,128,128]{4,3,2,1,0:T(8,128)(2,1)S(1)}, bf16[1,1,32,128,128]{4,3,2,1,0:T(8,128)(2,1)}, u32[]{:S(2)}) copy-start(bf16[1,1,32,128,128]{4,3,2,1,0:T(8,128)(2,1)} %refs_8_.1) | copy-start | bytes 3145732
  0.0 15.5 %copy-start.10 = (bf16[1,1,32,128,128]{4,3,2,1,0:T(8,128)(2,1)S(1)}, bf16[1,1,32,128,128]{4,3,2,1,0:T(8,128)(2,1)}, u32[]{:S(2)}) copy-start(bf16[1,1,32,128,128]{4,3,2,1,0:T(8,128)(2,1)} %refs_7_.1) | copy-start | bytes 3145732
  3.3 8.3 %collective-permute-start.5 = (bf16[80,128]{1,0:T(8,128)(2,1)}, bf16[80,128]{1,0:T(8,128)(2,1)S(1)}, u32[]{:S(2)}, u32[]{:S(2)}) collective-permute-start(bf16[80,128]{1,0:T(8,128)(2,1)} %get-tuple-element.36), channel_id=1, source_target_pairs={{0,18},{18,0},{1,19},{19,1},{2,16},{16,2},{3,17},{17,3},{4,22},{22... | collective-permute-start | bytes 61448 | tf_op jit(solution)/shard_map/ppermute | solution.py:792
  7.6 3.9 %collective-permute-start.4 = (bf16[64,128]{1,0:T(8,128)(2,1)}, bf16[64,128]{1,0:T(8,128)(2,1)S(1)}, u32[]{:S(2)}, u32[]{:S(2)}) collective-permute-start(bf16[64,128]{1,0:T(8,128)(2,1)} %get-tuple-element.35), channel_id=1, source_target_pairs={{0,16},{16,0},{1,17},{17,1},{2,18},{18,2},{3,19},{19,3},{4,20},{20... | collective-permute-start | bytes 49160 | tf_op jit(solution)/shard_map/ppermute | solution.py:790
  8.9 6.7 %collective-permute-start.1 = (bf16[80,1024]{1,0:T(8,128)(2,1)}, bf16[80,1024]{1,0:T(8,128)(2,1)S(1)}, u32[]{:S(2)}, u32[]{:S(2)}) collective-permute-start(bf16[80,1024]{1,0:T(8,128)(2,1)} %get-tuple-element.29), channel_id=1, source_target_pairs={{4,8},{8,4},{12,0},{0,12},{5,9},{9,5},{13,1},{1,13},{6,10},{10,6},... | collective-permute-start | bytes 491528 | tf_op jit(solution)/shard_map/ppermute | solution.py:825
  11.6 3.9 %collective-permute-start.6 = (bf16[64,128]{1,0:T(8,128)(2,1)S(1)}, bf16[64,128]{1,0:T(8,128)(2,1)S(1)}, u32[]{:S(2)}, u32[]{:S(2)}) collective-permute-start(bf16[64,128]{1,0:T(8,128)(2,1)S(1)} %get-tuple-element.38), channel_id=1, source_target_pairs={{0,1},{1,0},{2,3},{3,2},{4,5},{5,4},{6,7},{7,6},{8,9},{9,8},{10,11... | collective-permute-start | bytes 49160 | tf_op jit(solution)/shard_map/ppermute | solution.py:801
  13.2 7.7 %collective-permute-start.2 = (bf16[32,1024]{1,0:T(8,128)(2,1)}, bf16[32,1024]{1,0:T(8,128)(2,1)S(1)}, u32[]{:S(2)}, u32[]{:S(2)}) collective-permute-start(bf16[32,1024]{1,0:T(8,128)(2,1)} %get-tuple-element.30), channel_id=1, source_target_pairs={{16,17},{17,16},{18,19},{19,18},{0,8},{8,0},{1,9},{9,1},{2,10},{10... | collective-permute-start | bytes 196616 | tf_op jit(solution)/shard_map/ppermute | solution.py:827
  14.7 6.2 %collective-permute-start.3 = (bf16[32,1024]{1,0:T(8,128)(2,1)}, bf16[32,1024]{1,0:T(8,128)(2,1)S(1)}, u32[]{:S(2)}, u32[]{:S(2)}) collective-permute-start(bf16[32,1024]{1,0:T(8,128)(2,1)} %get-tuple-element.31), channel_id=1, source_target_pairs={{17,18},{18,17},{16,20},{20,16},{19,23},{23,19},{0,4},{4,0},{1,5},... | collective-permute-start | bytes 196616 | tf_op jit(solution)/shard_map/ppermute | solution.py:828
  14.7 6.2 %collective-permute-start = (bf16[80,1024]{1,0:T(8,128)(2,1)}, bf16[80,1024]{1,0:T(8,128)(2,1)S(1)}, u32[]{:S(2)}, u32[]{:S(2)}) collective-permute-start(bf16[80,1024]{1,0:T(8,128)(2,1)} %get-tuple-element.28), channel_id=1, source_target_pairs={{0,4},{4,0},{8,12},{12,8},{1,5},{5,1},{9,13},{13,9},{2,6},{6,2},{1... | collective-permute-start | bytes 491528 | tf_op jit(solution)/shard_map/ppermute | solution.py:824
  15.5 5.4 %copy-start = (f32[1,8,32,1024]{3,2,1,0:T(8,128)S(1)}, f32[1,8,32,1024]{3,2,1,0:T(8,128)}, u32[]{:S(2)}) copy-start(f32[1,8,32,1024]{3,2,1,0:T(8,128)} %x_ref.1) | copy-start | bytes 3145732
  15.5 5.5 %copy-start.1 = (bf16[1024,512]{1,0:T(8,128)(2,1)S(1)}, bf16[1024,512]{1,0:T(8,128)(2,1)}, u32[]{:S(2)}) copy-start(bf16[1024,512]{1,0:T(8,128)(2,1)} %constant.4.clone.table_hbm.table_ref) | copy-start | bytes 3145732
  15.5 5.5 %copy-start.3 = (s32[8,1024]{1,0:T(8,128)S(1)}, s32[8,1024]{1,0:T(8,128)}, u32[]{:S(2)}) copy-start(s32[8,1024]{1,0:T(8,128)} %wet_ref.1) | copy-start | bytes 98308
  15.5 5.5 %copy-start.8 = (f32[128]{0:T(128)S(1)}, f32[128]{0:T(128)}, u32[]{:S(2)}) copy-start(f32[128]{0:T(128)} %param.19) | copy-start | bytes 1540
  16.9 9.4 %copy-start.2 = (bf16[1024,512]{1,0:T(8,128)(2,1)S(1)}, bf16[1024,512]{1,0:T(8,128)(2,1)}, u32[]{:S(2)}) copy-start(bf16[1024,512]{1,0:T(8,128)(2,1)} %constant.5.clone.table_ref) | copy-start | bytes 3145732
  16.9 9.4 %copy-start.9 = (f32[128]{0:T(128)S(1)}, f32[128]{0:T(128)}, u32[]{:S(2)}) copy-start(f32[128]{0:T(128)} %param.18) | copy-start | bytes 1540
  16.9 7.8 %collective-permute-start.8 = (bf16[96,128]{1,0:T(8,128)(2,1)S(1)}, bf16[96,128]{1,0:T(8,128)(2,1)S(1)}, u32[]{:S(2)}, u32[]{:S(2)}) collective-permute-start(bf16[96,128]{1,0:T(8,128)(2,1)S(1)} %get-tuple-element.46), channel_id=1, source_target_pairs={{0,2},{2,0},{1,3},{3,1},{4,6},{6,4},{5,7},{7,5},{8,10},{10,8},{9,1... | collective-permute-start | bytes 73736 | tf_op jit(solution)/shard_map/ppermute | solution.py:870
  18.5 6.2 %collective-permute-start.9 = (bf16[80,128]{1,0:T(8,128)(2,1)S(1)}, bf16[80,128]{1,0:T(8,128)(2,1)S(1)}, u32[]{:S(2)}, u32[]{:S(2)}) collective-permute-start(bf16[80,128]{1,0:T(8,128)(2,1)S(1)} %get-tuple-element.47), channel_id=1, source_target_pairs={{0,3},{3,0},{1,2},{2,1},{4,7},{7,4},{5,6},{6,5},{8,11},{11,8},{9,1... | collective-permute-start | bytes 61448 | tf_op jit(solution)/shard_map/ppermute | solution.py:870
  21.0 3.7 %collective-permute-start.7 = (bf16[64,128]{1,0:T(8,128)(2,1)S(1)}, bf16[64,128]{1,0:T(8,128)(2,1)S(1)}, u32[]{:S(2)}, u32[]{:S(2)}) collective-permute-start(bf16[64,128]{1,0:T(8,128)(2,1)S(1)} %get-tuple-element.45), channel_id=1, source_target_pairs={{0,1},{1,0},{2,3},{3,2},{4,5},{5,4},{6,7},{7,6},{8,9},{9,8},{10,11... | collective-permute-start | bytes 49160 | tf_op jit(solution)/shard_map/ppermute | solution.py:870
  24.7 2.1 %collective-permute-start.10 = (bf16[64,128]{1,0:T(8,128)(2,1)S(1)}, bf16[64,128]{1,0:T(8,128)(2,1)S(1)}, u32[]{:S(2)}, u32[]{:S(2)}) collective-permute-start(bf16[64,128]{1,0:T(8,128)(2,1)S(1)} %get-tuple-element.49), channel_id=1, source_target_pairs={{0,4},{4,0},{8,12},{12,8},{1,5},{5,1},{9,13},{13,9},{2,6},{6,2},{1... | collective-permute-start | bytes 49160 | tf_op jit(solution)/shard_map/ppermute | solution.py:923
  24.8 3.2 %collective-permute-start.11 = (bf16[64,128]{1,0:T(8,128)(2,1)S(1)}, bf16[64,128]{1,0:T(8,128)(2,1)S(1)}, u32[]{:S(2)}, u32[]{:S(2)}) collective-permute-start(bf16[64,128]{1,0:T(8,128)(2,1)S(1)} %get-tuple-element.50), channel_id=1, source_target_pairs={{4,8},{8,4},{12,0},{0,12},{5,9},{9,5},{13,1},{1,13},{6,10},{10,6},... | collective-permute-start | bytes 49160 | tf_op jit(solution)/shard_map/ppermute | solution.py:924

commit v23 on v22

--- a/solution.py
+++ b/solution.py
@@ -779,7 +779,7 @@
         marine_air_input_index, marine_air_output_index, marine_air_piece_tally,
     )
 
-    masks = [1 << bit for bit in reversed(range(groups_y.bit_length() - 1))]
+    masks = [1 << bit for bit in range(groups_y.bit_length() - 1)]
 
     def sum_route(mask):
         return [(j, j ^ mask) for j in range(groups_y)]
@@ -827,14 +827,10 @@
     e2 = lax.ppermute(e2, axes, level_route(0))
     e4 = lax.ppermute(e4, axes, level_route(1))
 
-    landing_order = sorted(range(1, groups_y), key=lambda mask: (mask % 2, -mask))
     landing, *sent = pl.pallas_call(
         functools.partial(regrid_kernel, len(surfaces)),
         out_shape=[shape((cells, LANES), f32)]
-        + [
-            shape((cells + 16 * (groups_y - 2 - landing_order.index(mask)), LANES), bf16)
-            for mask in range(1, groups_y)
-        ],
+        + [shape((cells + 16 * (mask - 1), LANES), bf16) for mask in range(1, groups_y)],
         in_specs=[vmem] * (len(surfaces) + 5) + [hbm, hbm] + [anywhere] * 1,
         out_specs=[vmem] * groups_y,
         scratch_shapes=[

time: 29.2 us -> 28.9 us (0.990)
  waiting for transfers between devices: 4.7 us -> 3.86 us
  starting transfers between devices: 15.2 us -> 15.7 us
    ppermute x1, starting transfers between devices: 1.64 us -> 2.65 us  [local(): lax.ppermute(coarse, 'gy', sum_route(mask))]
    ppermute x1, starting transfers between devices: 4.35 us -> 3.34 us  [local(): far = lax.ppermute(wide, ('comp', 'gy'), partner_route(mask))]
    ppermute x3, waiting for transfers between devices: 2.76 us -> 1.89 us  [local(): lax.ppermute(block, axes, landing_route(mask))]
    ppermute x3, starting transfers between devices: 4.01 us -> 4.45 us  [local(): lax.ppermute(block, axes, landing_route(mask))]
  transfers between devices with their start and end apart: 12 -> 12, of which waited for: 5 -> 5; matrix products, arithmetic and copies ran while one was open for 0% -> 0% of each run, Pallas kernels for 11% -> 12%
where the time goes in v23:
time: 28.9 us; the launch traced here: 28.7 us
  starting transfers between devices  15.7 us (54%)
  Pallas kernels  7.65 us (26%)
  waiting for transfers between devices  3.86 us (13%)
  between operations  1.5 us (5%)
    ppermute x3, starting transfers between devices, local(): lax.ppermute(block, axes, landing_route(mask))  4.45 us
    ppermute x1, starting transfers between devices, local(): far = lax.ppermute(wide, ('comp', 'gy'), partner_route(mask))  3.34 us
    pallas_call x1, Pallas kernels, local(): pl.pallas_call(functools.partial(start_kernel, groups_x, paired), out_sha...  3.24 us
    ppermute x1, starting transfers between devices, local(): lax.ppermute(coarse, 'gy', sum_route(mask))  2.65 us
    ppermute x3, waiting for transfers between devices, local(): lax.ppermute(block, axes, landing_route(mask))  1.89 us
    ppermute x1, starting transfers between devices, local(): far = lax.ppermute(far, 'gx', both_ways(ring_pairs(groups_x, 1)))  1.55 us
    ppermute x1, starting transfers between devices, local(): e2 = lax.ppermute(e2, axes, level_route(0))  1.49 us
    pallas_call x1, Pallas kernels, local(): pl.pallas_call(functools.partial(regrid_kernel, len(surfaces)), out_shape...  1.36 us
  transfers between devices with their start and end apart: 12, of which 5 were waited for; matrix products, arithmetic and copies ran while one was open for 0% of the time, Pallas kernels for 12%

profile of v23, /device:TPU:0, one launch (start us, length us, event | category | flops | bytes accessed | tf_op | source)
XLA Modules:
  0.0 28.7 jit_solution(13807765843300077640)
XLA Ops:
  0.0 0.0 copy-start.7
  0.0 0.0 copy-start.6
  0.0 0.0 copy-start.5
  0.0 0.0 copy-start.4
  0.0 0.0 copy-start.11
  0.0 0.0 copy-start.10
  0.0 3.2 %surface_and_forward_or_halos.1 = (bf16[64,128]{1,0:T(8,128)(2,1)}, bf16[80,128]{1,0:T(8,128)(2,1)}, bf16[80,1024]{1,0:T(8,128)(2,1)}, bf16[80,1024]{1,0:T(8,128...) custom-call(f32[1,8,32,1024]{3,2,1,0:T(8,128)} %x_ref.1, s32[8,1024]{1,0:T(8,128)} %wet_ref.1, ...), custom_call_target="tpu_custom_call" | custom-call | tf_op jit(solution)/shard_map/surface_and_forward_or_halos/pallas_call | solution.py:740
  3.3 3.3 %collective-permute-start.5 = (bf16[80,128]{1,0:T(8,128)(2,1)}, bf16[80,128]{1,0:T(8,128)(2,1)S(1)}, u32[]{:S(2)}, u32[]{:S(2)}) collective-permute-start(bf16[80,128]{1,0:T(8,128)(2,1)} %get-tuple-element.36), channel_id=1, source_target_pairs={{0,17},{17,0},{1,16},{16,1},{2,19},{19,2},{3,18},{18,3},{4,21},{21... | collective-permute-start | bytes 61448 | tf_op jit(solution)/shard_map/ppermute | solution.py:792
  6.6 1.2 %collective-permute-start.4 = (bf16[64,128]{1,0:T(8,128)(2,1)}, bf16[64,128]{1,0:T(8,128)(2,1)S(1)}, u32[]{:S(2)}, u32[]{:S(2)}) collective-permute-start(bf16[64,128]{1,0:T(8,128)(2,1)} %get-tuple-element.35), channel_id=1, source_target_pairs={{0,16},{16,0},{1,17},{17,1},{2,18},{18,2},{3,19},{19,3},{4,20},{20... | collective-permute-start | bytes 49160 | tf_op jit(solution)/shard_map/ppermute | solution.py:790
  7.8 0.4 %collective-permute-start.1 = (bf16[80,1024]{1,0:T(8,128)(2,1)}, bf16[80,1024]{1,0:T(8,128)(2,1)S(1)}, u32[]{:S(2)}, u32[]{:S(2)}) collective-permute-start(bf16[80,1024]{1,0:T(8,128)(2,1)} %get-tuple-element.29), channel_id=1, source_target_pairs={{4,8},{8,4},{12,0},{0,12},{5,9},{9,5},{13,1},{1,13},{6,10},{10,6},... | collective-permute-start | bytes 491528 | tf_op jit(solution)/shard_map/ppermute | solution.py:825
  9.5 0.0 copy-done.7
  9.5 0.0 copy-done.6
  9.5 0.0 copy-done.5
  9.5 0.0 copy-done.4
  9.5 0.6 %one_hots.1 = (bf16[128,4096]{1,0:T(8,128)(2,1)S(1)}, bf16[128,4096]{1,0:T(8,128)(2,1)S(1)}, s32[32,128]{1,0:T(8,128)S(1)}, s32[32,128]{1,0:T(8,128)S(1)}, s32[32,128]{1,0:T(8,128)S(1)}) custom-call(s32[1,1,32,128]{3,2,1,0:T(8,128)S(1)} %copy-done.4, s32[1,1,32,128]{3,2,1,0:T(8,128)S(1)} %copy-done.5, s32[1,1]{1,0:T(1,128)S(6)} %copy.16.a_count, ...), custom_call_target="tpu_custom_call" | custom-call | tf_op jit(solution)/shard_map/one_hots/pallas_call | solution.py:764
  10.2 0.4 %collective-permute-done.4 = bf16[64,128]{1,0:T(8,128)(2,1)S(1)} collective-permute-done((bf16[64,128]{1,0:T(8,128)(2,1)}, bf16[64,128]{1,0:T(8,128)(2,1)S(1)}, u32[]{:S(2)}, u32[]{:S(2)}) %collective-permute-start.4) | collective-permute-done | bytes 16416 | tf_op jit(solution)/shard_map/ppermute | solution.py:790
  10.6 0.0 collective-permute-done.5
  10.6 2.7 %collective-permute-start.6 = (bf16[64,128]{1,0:T(8,128)(2,1)S(1)}, bf16[64,128]{1,0:T(8,128)(2,1)S(1)}, u32[]{:S(2)}, u32[]{:S(2)}) collective-permute-start(bf16[64,128]{1,0:T(8,128)(2,1)S(1)} %get-tuple-element.38), channel_id=1, source_target_pairs={{0,2},{1,3},{2,0},{3,1},{4,6},{5,7},{6,4},{7,5},{8,10},{9,11},{10,... | collective-permute-start | bytes 49160 | tf_op jit(solution)/shard_map/ppermute | solution.py:801
  13.2 1.5 %collective-permute-start.2 = (bf16[32,1024]{1,0:T(8,128)(2,1)}, bf16[32,1024]{1,0:T(8,128)(2,1)S(1)}, u32[]{:S(2)}, u32[]{:S(2)}) collective-permute-start(bf16[32,1024]{1,0:T(8,128)(2,1)} %get-tuple-element.30), channel_id=1, source_target_pairs={{16,17},{17,16},{18,19},{19,18},{0,8},{8,0},{1,9},{9,1},{2,10},{10... | collective-permute-start | bytes 196616 | tf_op jit(solution)/shard_map/ppermute | solution.py:827
  14.7 0.0 collective-permute-start.3
  14.7 0.5 %collective-permute-start = (bf16[80,1024]{1,0:T(8,128)(2,1)}, bf16[80,1024]{1,0:T(8,128)(2,1)S(1)}, u32[]{:S(2)}, u32[]{:S(2)}) collective-permute-start(bf16[80,1024]{1,0:T(8,128)(2,1)} %get-tuple-element.28), channel_id=1, source_target_pairs={{0,4},{4,0},{8,12},{12,8},{1,5},{5,1},{9,13},{13,9},{2,6},{6,2},{1... | collective-permute-start | bytes 491528 | tf_op jit(solution)/shard_map/ppermute | solution.py:824
  15.2 0.3 %collective-permute-done.6.refs_1_ = bf16[64,128]{1,0:T(8,128)(2,1)S(1)} collective-permute-done((bf16[64,128]{1,0:T(8,128)(2,1)S(1)}, bf16[64,128]{1,0:T(8,128)(2,1)S(1)}, u32[]{:S(2)}, u32[]{:S(2)}) %collective-permute-start.6) | collective-permute-done | bytes 16416 | tf_op jit(solution)/shard_map/ppermute | solution.py:801
  15.6 0.0 collective-permute-done.1.e3_ref.refs_9_
  15.6 0.0 copy-done.11
  15.6 0.0 copy-done.10
  15.6 0.0 copy-start
  15.6 0.0 copy-start.1
  15.6 0.0 copy-start.3
  15.6 0.0 copy-start.8
  15.6 1.4 %regrid_blocks.1 = (f32[64,128]{1,0:T(8,128)S(1)}, bf16[64,128]{1,0:T(8,128)(2,1)S(1)}, bf16[80,128]{1,0:T(8,128)(2,1)S(1)}, bf16[96,128]{1,0:T(8,128)(2,1)S(1)}) custom-call(f32[64,128]{1,0:T(8,128)S(1)} %get-tuple-element.52.refs_0_, bf16[64,128]{1,0:T(8,128)(2,1)S(1)} %collective-permute-done.6.refs_1_, bf16[128,4096]{1,0:T(8,128)(2,1)S(1)} %get-tuple-element.39.refs_2_, ...), custom_call_target="tpu_custom_call" | custom-call | flops 2200000000 | tf_op jit(solution)/shard_map/regrid_blocks/pallas_call | solution.py:830
  17.0 0.0 copy-start.2
  17.0 0.0 copy-start.9
  17.0 2.5 %collective-permute-start.9 = (bf16[96,128]{1,0:T(8,128)(2,1)S(1)}, bf16[96,128]{1,0:T(8,128)(2,1)S(1)}, u32[]{:S(2)}, u32[]{:S(2)}) collective-permute-start(bf16[96,128]{1,0:T(8,128)(2,1)S(1)} %get-tuple-element.47), channel_id=1, source_target_pairs={{0,3},{3,0},{1,2},{2,1},{4,7},{7,4},{5,6},{6,5},{8,11},{11,8},{9,1... | collective-permute-start | bytes 73736 | tf_op jit(solution)/shard_map/ppermute | solution.py:866
  19.5 0.0 collective-permute-start.8
  19.5 0.0 collective-permute-done.2.e2_ref
  19.5 2.0 %collective-permute-start.7 = (bf16[64,128]{1,0:T(8,128)(2,1)S(1)}, bf16[64,128]{1,0:T(8,128)(2,1)S(1)}, u32[]{:S(2)}, u32[]{:S(2)}) collective-permute-start(bf16[64,128]{1,0:T(8,128)(2,1)S(1)} %get-tuple-element.45), channel_id=1, source_target_pairs={{0,1},{1,0},{2,3},{3,2},{4,5},{5,4},{6,7},{7,6},{8,9},{9,8},{10,11... | collective-permute-start | bytes 49160 | tf_op jit(solution)/shard_map/ppermute | solution.py:866
  21.5 0.0 collective-permute-done.3.e4_ref
  21.5 0.0 collective-permute-done.e1_ref
  21.5 0.0 copy-done
  21.5 0.0 copy-done.1
  21.5 0.0 copy-done.3
  21.5 0.0 copy-done.8
  21.5 0.9 %damping_or_first_step.1 = (bf16[256,1024]{1,0:T(8,128)(2,1)S(1)}, f32[7,16,1024]{2,1,0:T(8,128)S(1)}, f32[10,2,24,1024]{3,2,1,0:T(8,128)S(1)}) custom-call(f32[1,8,32,1024]{3,2,1,0:T(8,128)S(1)} %copy-done, s32[8,1024]{1,0:T(8,128)S(1)} %copy-done.3, f32[1,128]{1,0:T(1,128)S(1)} %bitcast.4, bf16[1024,512]{1,0:T(8,128)(2,1)S(1)} %copy-done.1, ...), custom_call_target="tpu_custom_call" | custom-call | tf_op jit(solution)/shard_map/damping_or_first_step/pallas_call | solution.py:886
  22.5 0.8 %collective-permute-done.7.refs_0_ = bf16[64,128]{1,0:T(8,128)(2,1)S(1)} collective-permute-done((bf16[64,128]{1,0:T(8,128)(2,1)S(1)}, bf16[64,128]{1,0:T(8,128)(2,1)S(1)}, u32[]{:S(2)}, u32[]{:S(2)}) %collective-permute-start.7) | collective-permute-done | bytes 16416 | tf_op jit(solution)/shard_map/ppermute | solution.py:866
  23.3 1.1 %collective-permute-done.8.refs_1_ = bf16[80,128]{1,0:T(8,128)(2,1)S(1)} collective-permute-done((bf16[80,128]{1,0:T(8,128)(2,1)S(1)}, bf16[80,128]{1,0:T(8,128)(2,1)S(1)}, u32[]{:S(2)}, u32[]{:S(2)}) %collective-permute-start.8) | collective-permute-done | bytes 20512 | tf_op jit(solution)/shard_map/ppermute | solution.py:866
  24.4 0.0 collective-permute-done.9.refs_2_
  24.4 0.1 collective-permute-start.10
  24.5 1.5 %collective-permute-start.11 = (bf16[64,128]{1,0:T(8,128)(2,1)S(1)}, bf16[64,128]{1,0:T(8,128)(2,1)S(1)}, u32[]{:S(2)}, u32[]{:S(2)}) collective-permute-start(bf16[64,128]{1,0:T(8,128)(2,1)S(1)} %get-tuple-element.50), channel_id=1, source_target_pairs={{4,8},{8,4},{12,0},{0,12},{5,9},{9,5},{13,1},{1,13},{6,10},{10,6},... | collective-permute-start | bytes 49160 | tf_op jit(solution)/shard_map/ppermute | solution.py:920
  26.0 0.0 copy-done.2
  26.0 0.0 copy-done.9
  26.0 0.5 %inverse_or_second_step.1.base_ref = f32[8,32,1024]{2,1,0:T(8,128)S(1)} custom-call(f32[1,128]{1,0:T(1,128)S(1)} %bitcast.5, bf16[1024,512]{1,0:T(8,128)(2,1)S(1)} %copy-done.2, bf16[256,1024]{1,0:T(8,128)(2,1)S(1)} %get-tuple-element.32.zb_ref, f32[7,16,1024]{2,1,0:T(8,128)S(1)} %get-tuple-element.33._.c_ref, ...), custom_call_target="tpu_custom_call" | custom-call | tf_op jit(solution)/shard_map/inverse_or_second_step/pallas_call | solution.py:921
  26.5 0.0 collective-permute-done.10.near_ref
  26.5 1.2 %collective-permute-done.11.far_ref = bf16[64,128]{1,0:T(8,128)(2,1)S(1)} collective-permute-done((bf16[64,128]{1,0:T(8,128)(2,1)S(1)}, bf16[64,128]{1,0:T(8,128)(2,1)S(1)}, u32[]{:S(2)}, u32[]{:S(2)}) %collective-permute-start.11) | collective-permute-done | bytes 16416 | tf_op jit(solution)/shard_map/ppermute | solution.py:920
  27.7 1.0 %add_surface_terms.1 = f32[1,8,32,1024]{3,2,1,0:T(8,128)} custom-call(f32[8,32,1024]{2,1,0:T(8,128)S(1)} %inverse_or_second_step.1.base_ref, f32[7,16,1024]{2,1,0:T(8,128)S(1)} %get-tuple-element.33._.c_ref, f32[64,128]{1,0:T(8,128)S(1)} %get-tuple-element.48.sum_ref, bf16[64,128]{1,0:T(8,128)(2,1)S(1)} %collective-permute-done.10.near_ref, ...), custom_call_target="tpu_custom_call" | custom-call | tf_op jit(solution)/shard_map/add_surface_terms/pallas_call | solution.py:929
  (2 shorter events, 0.1 us)
Async XLA Ops:
  0.0 9.5 %copy-start.7 = (s32[1,1,32,128]{3,2,1,0:T(8,128)S(1)}, s32[1,1,32,128]{3,2,1,0:T(8,128)}, u32[]{:S(2)}) copy-start(s32[1,1,32,128]{3,2,1,0:T(8,128)} %m_dst.1) | copy-start | bytes 49156
  0.0 9.5 %copy-start.6 = (s32[1,1,32,128]{3,2,1,0:T(8,128)S(1)}, s32[1,1,32,128]{3,2,1,0:T(8,128)}, u32[]{:S(2)}) copy-start(s32[1,1,32,128]{3,2,1,0:T(8,128)} %m_src.1) | copy-start | bytes 49156
  0.0 9.5 %copy-start.5 = (s32[1,1,32,128]{3,2,1,0:T(8,128)S(1)}, s32[1,1,32,128]{3,2,1,0:T(8,128)}, u32[]{:S(2)}) copy-start(s32[1,1,32,128]{3,2,1,0:T(8,128)} %a_dst.1) | copy-start | bytes 49156
  0.0 9.5 %copy-start.4 = (s32[1,1,32,128]{3,2,1,0:T(8,128)S(1)}, s32[1,1,32,128]{3,2,1,0:T(8,128)}, u32[]{:S(2)}) copy-start(s32[1,1,32,128]{3,2,1,0:T(8,128)} %a_src.1) | copy-start | bytes 49156
  0.0 15.6 %copy-start.11 = (bf16[1,1,32,128,128]{4,3,2,1,0:T(8,128)(2,1)S(1)}, bf16[1,1,32,128,128]{4,3,2,1,0:T(8,128)(2,1)}, u32[]{:S(2)}) copy-start(bf16[1,1,32,128,128]{4,3,2,1,0:T(8,128)(2,1)} %refs_8_.1) | copy-start | bytes 3145732
  0.0 15.6 %copy-start.10 = (bf16[1,1,32,128,128]{4,3,2,1,0:T(8,128)(2,1)S(1)}, bf16[1,1,32,128,128]{4,3,2,1,0:T(8,128)(2,1)}, u32[]{:S(2)}) copy-start(bf16[1,1,32,128,128]{4,3,2,1,0:T(8,128)(2,1)} %refs_7_.1) | copy-start | bytes 3145732
  3.3 7.3 %collective-permute-start.5 = (bf16[80,128]{1,0:T(8,128)(2,1)}, bf16[80,128]{1,0:T(8,128)(2,1)S(1)}, u32[]{:S(2)}, u32[]{:S(2)}) collective-permute-start(bf16[80,128]{1,0:T(8,128)(2,1)} %get-tuple-element.36), channel_id=1, source_target_pairs={{0,17},{17,0},{1,16},{16,1},{2,19},{19,2},{3,18},{18,3},{4,21},{21... | collective-permute-start | bytes 61448 | tf_op jit(solution)/shard_map/ppermute | solution.py:792
  6.6 3.9 %collective-permute-start.4 = (bf16[64,128]{1,0:T(8,128)(2,1)}, bf16[64,128]{1,0:T(8,128)(2,1)S(1)}, u32[]{:S(2)}, u32[]{:S(2)}) collective-permute-start(bf16[64,128]{1,0:T(8,128)(2,1)} %get-tuple-element.35), channel_id=1, source_target_pairs={{0,16},{16,0},{1,17},{17,1},{2,18},{18,2},{3,19},{19,3},{4,20},{20... | collective-permute-start | bytes 49160 | tf_op jit(solution)/shard_map/ppermute | solution.py:790
  7.8 7.7 %collective-permute-start.1 = (bf16[80,1024]{1,0:T(8,128)(2,1)}, bf16[80,1024]{1,0:T(8,128)(2,1)S(1)}, u32[]{:S(2)}, u32[]{:S(2)}) collective-permute-start(bf16[80,1024]{1,0:T(8,128)(2,1)} %get-tuple-element.29), channel_id=1, source_target_pairs={{4,8},{8,4},{12,0},{0,12},{5,9},{9,5},{13,1},{1,13},{6,10},{10,6},... | collective-permute-start | bytes 491528 | tf_op jit(solution)/shard_map/ppermute | solution.py:825
  10.6 5.0 %collective-permute-start.6 = (bf16[64,128]{1,0:T(8,128)(2,1)S(1)}, bf16[64,128]{1,0:T(8,128)(2,1)S(1)}, u32[]{:S(2)}, u32[]{:S(2)}) collective-permute-start(bf16[64,128]{1,0:T(8,128)(2,1)S(1)} %get-tuple-element.38), channel_id=1, source_target_pairs={{0,2},{1,3},{2,0},{3,1},{4,6},{5,7},{6,4},{7,5},{8,10},{9,11},{10,... | collective-permute-start | bytes 49160 | tf_op jit(solution)/shard_map/ppermute | solution.py:801
  13.2 6.3 %collective-permute-start.2 = (bf16[32,1024]{1,0:T(8,128)(2,1)}, bf16[32,1024]{1,0:T(8,128)(2,1)S(1)}, u32[]{:S(2)}, u32[]{:S(2)}) collective-permute-start(bf16[32,1024]{1,0:T(8,128)(2,1)} %get-tuple-element.30), channel_id=1, source_target_pairs={{16,17},{17,16},{18,19},{19,18},{0,8},{8,0},{1,9},{9,1},{2,10},{10... | collective-permute-start | bytes 196616 | tf_op jit(solution)/shard_map/ppermute | solution.py:827
  14.7 6.8 %collective-permute-start.3 = (bf16[32,1024]{1,0:T(8,128)(2,1)}, bf16[32,1024]{1,0:T(8,128)(2,1)S(1)}, u32[]{:S(2)}, u32[]{:S(2)}) collective-permute-start(bf16[32,1024]{1,0:T(8,128)(2,1)} %get-tuple-element.31), channel_id=1, source_target_pairs={{17,18},{18,17},{16,20},{20,16},{19,23},{23,19},{0,4},{4,0},{1,5},... | collective-permute-start | bytes 196616 | tf_op jit(solution)/shard_map/ppermute | solution.py:828
  14.7 6.8 %collective-permute-start = (bf16[80,1024]{1,0:T(8,128)(2,1)}, bf16[80,1024]{1,0:T(8,128)(2,1)S(1)}, u32[]{:S(2)}, u32[]{:S(2)}) collective-permute-start(bf16[80,1024]{1,0:T(8,128)(2,1)} %get-tuple-element.28), channel_id=1, source_target_pairs={{0,4},{4,0},{8,12},{12,8},{1,5},{5,1},{9,13},{13,9},{2,6},{6,2},{1... | collective-permute-start | bytes 491528 | tf_op jit(solution)/shard_map/ppermute | solution.py:824
  15.6 5.9 %copy-start = (f32[1,8,32,1024]{3,2,1,0:T(8,128)S(1)}, f32[1,8,32,1024]{3,2,1,0:T(8,128)}, u32[]{:S(2)}) copy-start(f32[1,8,32,1024]{3,2,1,0:T(8,128)} %x_ref.1) | copy-start | bytes 3145732
  15.6 5.9 %copy-start.1 = (bf16[1024,512]{1,0:T(8,128)(2,1)S(1)}, bf16[1024,512]{1,0:T(8,128)(2,1)}, u32[]{:S(2)}) copy-start(bf16[1024,512]{1,0:T(8,128)(2,1)} %constant.4.clone.table_hbm.table_ref) | copy-start | bytes 3145732
  15.6 5.9 %copy-start.3 = (s32[8,1024]{1,0:T(8,128)S(1)}, s32[8,1024]{1,0:T(8,128)}, u32[]{:S(2)}) copy-start(s32[8,1024]{1,0:T(8,128)} %wet_ref.1) | copy-start | bytes 98308
  15.6 5.9 %copy-start.8 = (f32[128]{0:T(128)S(1)}, f32[128]{0:T(128)}, u32[]{:S(2)}) copy-start(f32[128]{0:T(128)} %param.19) | copy-start | bytes 1540
  17.0 9.0 %copy-start.2 = (bf16[1024,512]{1,0:T(8,128)(2,1)S(1)}, bf16[1024,512]{1,0:T(8,128)(2,1)}, u32[]{:S(2)}) copy-start(bf16[1024,512]{1,0:T(8,128)(2,1)} %constant.5.clone.table_ref) | copy-start | bytes 3145732
  17.0 9.0 %copy-start.9 = (f32[128]{0:T(128)S(1)}, f32[128]{0:T(128)}, u32[]{:S(2)}) copy-start(f32[128]{0:T(128)} %param.18) | copy-start | bytes 1540
  17.0 7.3 %collective-permute-start.9 = (bf16[96,128]{1,0:T(8,128)(2,1)S(1)}, bf16[96,128]{1,0:T(8,128)(2,1)S(1)}, u32[]{:S(2)}, u32[]{:S(2)}) collective-permute-start(bf16[96,128]{1,0:T(8,128)(2,1)S(1)} %get-tuple-element.47), channel_id=1, source_target_pairs={{0,3},{3,0},{1,2},{2,1},{4,7},{7,4},{5,6},{6,5},{8,11},{11,8},{9,1... | collective-permute-start | bytes 73736 | tf_op jit(solution)/shard_map/ppermute | solution.py:866
  19.5 4.8 %collective-permute-start.8 = (bf16[80,128]{1,0:T(8,128)(2,1)S(1)}, bf16[80,128]{1,0:T(8,128)(2,1)S(1)}, u32[]{:S(2)}, u32[]{:S(2)}) collective-permute-start(bf16[80,128]{1,0:T(8,128)(2,1)S(1)} %get-tuple-element.46), channel_id=1, source_target_pairs={{0,2},{2,0},{1,3},{3,1},{4,6},{6,4},{5,7},{7,5},{8,10},{10,8},{9,1... | collective-permute-start | bytes 61448 | tf_op jit(solution)/shard_map/ppermute | solution.py:866
  19.5 3.7 %collective-permute-start.7 = (bf16[64,128]{1,0:T(8,128)(2,1)S(1)}, bf16[64,128]{1,0:T(8,128)(2,1)S(1)}, u32[]{:S(2)}, u32[]{:S(2)}) collective-permute-start(bf16[64,128]{1,0:T(8,128)(2,1)S(1)} %get-tuple-element.45), channel_id=1, source_target_pairs={{0,1},{1,0},{2,3},{3,2},{4,5},{5,4},{6,7},{7,6},{8,9},{9,8},{10,11... | collective-permute-start | bytes 49160 | tf_op jit(solution)/shard_map/ppermute | solution.py:866
  24.4 2.1 %collective-permute-start.10 = (bf16[64,128]{1,0:T(8,128)(2,1)S(1)}, bf16[64,128]{1,0:T(8,128)(2,1)S(1)}, u32[]{:S(2)}, u32[]{:S(2)}) collective-permute-start(bf16[64,128]{1,0:T(8,128)(2,1)S(1)} %get-tuple-element.49), channel_id=1, source_target_pairs={{0,4},{4,0},{8,12},{12,8},{1,5},{5,1},{9,13},{13,9},{2,6},{6,2},{1... | collective-permute-start | bytes 49160 | tf_op jit(solution)/shard_map/ppermute | solution.py:919
  24.5 3.2 %collective-permute-start.11 = (bf16[64,128]{1,0:T(8,128)(2,1)S(1)}, bf16[64,128]{1,0:T(8,128)(2,1)S(1)}, u32[]{:S(2)}, u32[]{:S(2)}) collective-permute-start(bf16[64,128]{1,0:T(8,128)(2,1)S(1)} %get-tuple-element.50), channel_id=1, source_target_pairs={{4,8},{8,4},{12,0},{0,12},{5,9},{9,5},{13,1},{1,13},{6,10},{10,6},... | collective-permute-start | bytes 49160 | tf_op jit(solution)/shard_map/ppermute | solution.py:920

commit v24 on v23

--- a/solution.py
+++ b/solution.py
@@ -280,7 +280,7 @@
 
 def one_hot_kernel(
     rows, columns, a_src, a_dst, a_count, m_src, m_dst, m_count, src_hot_ref, dst_hot_ref,
-    src_row_ref, dst_row_ref, used_ref,
+    src_row_ref, dst_mask_ref, used_ref,
 ):
     is_atmos = lax.axis_index("comp") == 0
     blocks, points = src_row_ref.shape
@@ -288,25 +288,26 @@
     block_iota = lax.broadcasted_iota(jnp.int32, (blocks, points), 0)
     used_ref[...] = jnp.where(block_iota < count, 1, 0)
     lane_iota = lax.broadcasted_iota(jnp.int32, (LANES, points), 0)
-    for a_ref, m_ref, hot_ref, row_ref in (
-        (a_src, m_src, src_hot_ref, src_row_ref),
-        (a_dst, m_dst, dst_hot_ref, dst_row_ref),
-    ):
+    cells = dst_mask_ref.shape[0]
+    row_iota = lax.broadcasted_iota(jnp.int32, (cells, points), 0)
+    for a_ref, m_ref, hot_ref in ((a_src, m_src, src_hot_ref), (a_dst, m_dst, dst_hot_ref)):
         index = jnp.where(is_atmos, m_ref[0, 0], a_ref[0, 0])
-        row = index // columns
         tile = (index // LANES) % (columns // LANES)
-        row_ref[...] = tile * rows + row
+        row = tile * rows + index // columns
+        if hot_ref is src_hot_ref:
+            src_row_ref[...] = row
         lane = index % LANES
         for b in range(blocks):
-            hot_ref[:, b * points : (b + 1) * points] = jnp.where(
-                lane_iota == lane[b : b + 1], 1.0, 0.0
-            ).astype(bf16)
+            at = slice(b * points, (b + 1) * points)
+            hot_ref[:, at] = jnp.where(lane_iota == lane[b : b + 1], 1.0, 0.0).astype(bf16)
+            if hot_ref is dst_hot_ref:
+                dst_mask_ref[:, at] = jnp.where(row_iota == row[b : b + 1], 1.0, 0.0).astype(bf16)
 
 
 def regrid_kernel(n_surfaces, *refs):
     surfaces = refs[:n_surfaces]
     (
-        src_hot_ref, dst_hot_ref, src_row_ref, dst_row_ref, used_ref, a_weight, m_weight,
+        src_hot_ref, dst_hot_ref, src_row_ref, dst_mask_ref, used_ref, a_weight, m_weight,
         _,
         *refs,
     ) = refs[n_surfaces:]
@@ -362,14 +363,10 @@
         spread = []
         for k in range(b, b + 2):
             value = val_ref[k : k + 1, :]
-            coarse = value.astype(bf16).astype(f32)
-            fine = value - coarse
-            mine = row_iota == dst_row_ref[k : k + 1, :]
-            spread.append(
-                jnp.concatenate(
-                    [jnp.where(mine, coarse, 0.0), jnp.where(mine, fine, 0.0)], axis=0
-                ).astype(bf16)
-            )
+            coarse = value.astype(bf16)
+            fine = (value - coarse.astype(f32)).astype(bf16)
+            mine = dst_mask_ref[:, k * points : (k + 1) * points]
+            spread.append(jnp.concatenate([mine * coarse, mine * fine], axis=0))
         land = land + lax.dot_general(
             jnp.concatenate(spread, axis=1),
             dst_hot_ref[:, b * points : b * points + pair],
@@ -767,7 +764,7 @@
             shape((LANES, blocks * points), bf16),
             shape((LANES, blocks * points), bf16),
             shape((blocks, points), jnp.int32),
-            shape((blocks, points), jnp.int32),
+            shape((cells, blocks * points), bf16),
             shape((blocks, points), jnp.int32),
         ],
         in_specs=[vmem, vmem, smem] * 2,

time: 28.9 us -> 28.9 us (level)
  no operation moved by 1% of the time
where the time goes in v24:
time: 28.9 us; the launch traced here: 28.8 us
  starting transfers between devices  15.6 us (54%)
  Pallas kernels  7.82 us (27%)
  waiting for transfers between devices  3.75 us (13%)
  between operations  1.5 us (5%)
    ppermute x3, starting transfers between devices, local(): lax.ppermute(block, axes, landing_route(mask))  4.45 us
    ppermute x1, starting transfers between devices, local(): far = lax.ppermute(wide, ('comp', 'gy'), partner_route(mask))  3.34 us
    pallas_call x1, Pallas kernels, local(): pl.pallas_call(functools.partial(start_kernel, groups_x, paired), out_sha...  3.24 us
    ppermute x1, starting transfers between devices, local(): lax.ppermute(coarse, 'gy', sum_route(mask))  2.65 us
    ppermute x3, waiting for transfers between devices, local(): lax.ppermute(block, axes, landing_route(mask))  1.75 us
    ppermute x1, starting transfers between devices, local(): far = lax.ppermute(far, 'gx', both_ways(ring_pairs(groups_x, 1)))  1.51 us
    ppermute x1, starting transfers between devices, local(): e2 = lax.ppermute(e2, axes, level_route(0))  1.49 us
    pallas_call x1, Pallas kernels, local(): pl.pallas_call(functools.partial(regrid_kernel, len(surfaces)), out_shape...  1.35 us
  transfers between devices with their start and end apart: 12, of which 5 were waited for; matrix products, arithmetic and copies ran while one was open for 0% of the time, Pallas kernels for 12%

profile of v24, /device:TPU:0, one launch (start us, length us, event | category | flops | bytes accessed | tf_op | source)
XLA Modules:
  0.0 28.8 jit_solution(2900641541647540811)
XLA Ops:
  0.0 0.0 copy-start.7
  0.0 0.0 copy-start.6
  0.0 0.0 copy-start.5
  0.0 0.0 copy-start.4
  0.0 0.0 copy-start.11
  0.0 0.0 copy-start.10
  0.0 3.2 %surface_and_forward_or_halos.1 = (bf16[64,128]{1,0:T(8,128)(2,1)}, bf16[80,128]{1,0:T(8,128)(2,1)}, bf16[80,1024]{1,0:T(8,128)(2,1)}, bf16[80,1024]{1,0:T(8,128...) custom-call(f32[1,8,32,1024]{3,2,1,0:T(8,128)} %x_ref.1, s32[8,1024]{1,0:T(8,128)} %wet_ref.1, ...), custom_call_target="tpu_custom_call" | custom-call | tf_op jit(solution)/shard_map/surface_and_forward_or_halos/pallas_call | solution.py:737
  3.3 3.3 %collective-permute-start.5 = (bf16[80,128]{1,0:T(8,128)(2,1)}, bf16[80,128]{1,0:T(8,128)(2,1)S(1)}, u32[]{:S(2)}, u32[]{:S(2)}) collective-permute-start(bf16[80,128]{1,0:T(8,128)(2,1)} %get-tuple-element.36), channel_id=1, source_target_pairs={{0,17},{17,0},{1,16},{16,1},{2,19},{19,2},{3,18},{18,3},{4,21},{21... | collective-permute-start | bytes 61448 | tf_op jit(solution)/shard_map/ppermute | solution.py:789
  6.6 1.2 %collective-permute-start.4 = (bf16[64,128]{1,0:T(8,128)(2,1)}, bf16[64,128]{1,0:T(8,128)(2,1)S(1)}, u32[]{:S(2)}, u32[]{:S(2)}) collective-permute-start(bf16[64,128]{1,0:T(8,128)(2,1)} %get-tuple-element.35), channel_id=1, source_target_pairs={{0,16},{16,0},{1,17},{17,1},{2,18},{18,2},{3,19},{19,3},{4,20},{20... | collective-permute-start | bytes 49160 | tf_op jit(solution)/shard_map/ppermute | solution.py:787
  7.8 0.4 %collective-permute-start.1 = (bf16[80,1024]{1,0:T(8,128)(2,1)}, bf16[80,1024]{1,0:T(8,128)(2,1)S(1)}, u32[]{:S(2)}, u32[]{:S(2)}) collective-permute-start(bf16[80,1024]{1,0:T(8,128)(2,1)} %get-tuple-element.29), channel_id=1, source_target_pairs={{4,8},{8,4},{12,0},{0,12},{5,9},{9,5},{13,1},{1,13},{6,10},{10,6},... | collective-permute-start | bytes 491528 | tf_op jit(solution)/shard_map/ppermute | solution.py:822
  9.5 0.0 copy-done.7
  9.5 0.0 copy-done.6
  9.5 0.0 copy-done.5
  9.5 0.0 copy-done.4
  9.5 0.8 %one_hots.1 = (bf16[128,4096]{1,0:T(8,128)(2,1)S(1)}, bf16[128,4096]{1,0:T(8,128)(2,1)S(1)}, s32[32,128]{1,0:T(8,128)S(1)}, bf16[64,4096]{1,0:T(8,128)(2,1)S(1)}, s32[32,128]{1,0:T(8,128)S(1)}) custom-call(s32[1,1,32,128]{3,2,1,0:T(8,128)S(1)} %copy-done.4, s32[1,1,32,128]{3,2,1,0:T(8,128)S(1)} %copy-done.5, s32[1,1]{1,0:T(1,128)S(6)} %copy.16.a_count, ...), custom_call_target="tpu_custom_call" | custom-call | tf_op jit(solution)/shard_map/one_hots/pallas_call | solution.py:761
  10.4 0.2 collective-permute-done.4
  10.6 0.0 collective-permute-done.5
  10.6 2.7 %collective-permute-start.6 = (bf16[64,128]{1,0:T(8,128)(2,1)S(1)}, bf16[64,128]{1,0:T(8,128)(2,1)S(1)}, u32[]{:S(2)}, u32[]{:S(2)}) collective-permute-start(bf16[64,128]{1,0:T(8,128)(2,1)S(1)} %get-tuple-element.38), channel_id=1, source_target_pairs={{0,2},{1,3},{2,0},{3,1},{4,6},{5,7},{6,4},{7,5},{8,10},{9,11},{10,... | collective-permute-start | bytes 49160 | tf_op jit(solution)/shard_map/ppermute | solution.py:798
  13.2 1.5 %collective-permute-start.2 = (bf16[32,1024]{1,0:T(8,128)(2,1)}, bf16[32,1024]{1,0:T(8,128)(2,1)S(1)}, u32[]{:S(2)}, u32[]{:S(2)}) collective-permute-start(bf16[32,1024]{1,0:T(8,128)(2,1)} %get-tuple-element.30), channel_id=1, source_target_pairs={{16,17},{17,16},{18,19},{19,18},{0,8},{8,0},{1,9},{9,1},{2,10},{10... | collective-permute-start | bytes 196616 | tf_op jit(solution)/shard_map/ppermute | solution.py:824
  14.7 0.0 collective-permute-start.3
  14.7 0.5 %collective-permute-start = (bf16[80,1024]{1,0:T(8,128)(2,1)}, bf16[80,1024]{1,0:T(8,128)(2,1)S(1)}, u32[]{:S(2)}, u32[]{:S(2)}) collective-permute-start(bf16[80,1024]{1,0:T(8,128)(2,1)} %get-tuple-element.28), channel_id=1, source_target_pairs={{0,4},{4,0},{8,12},{12,8},{1,5},{5,1},{9,13},{13,9},{2,6},{6,2},{1... | collective-permute-start | bytes 491528 | tf_op jit(solution)/shard_map/ppermute | solution.py:821
  15.2 0.5 %collective-permute-done.6.refs_1_ = bf16[64,128]{1,0:T(8,128)(2,1)S(1)} collective-permute-done((bf16[64,128]{1,0:T(8,128)(2,1)S(1)}, bf16[64,128]{1,0:T(8,128)(2,1)S(1)}, u32[]{:S(2)}, u32[]{:S(2)}) %collective-permute-start.6) | collective-permute-done | bytes 16416 | tf_op jit(solution)/shard_map/ppermute | solution.py:798
  15.8 0.0 collective-permute-done.1.e3_ref.refs_9_
  15.8 0.0 copy-done.11
  15.8 0.0 copy-done.10
  15.8 0.0 copy-start
  15.8 0.0 copy-start.1
  15.8 0.0 copy-start.3
  15.8 0.0 copy-start.8
  15.8 1.4 %regrid_blocks.1 = (f32[64,128]{1,0:T(8,128)S(1)}, bf16[64,128]{1,0:T(8,128)(2,1)S(1)}, bf16[80,128]{1,0:T(8,128)(2,1)S(1)}, bf16[96,128]{1,0:T(8,128)(2,1)S(1)}) custom-call(f32[64,128]{1,0:T(8,128)S(1)} %get-tuple-element.52.refs_0_, bf16[64,128]{1,0:T(8,128)(2,1)S(1)} %collective-permute-done.6.refs_1_, bf16[128,4096]{1,0:T(8,128)(2,1)S(1)} %get-tuple-element.39.refs_2_, ...), custom_call_target="tpu_custom_call" | custom-call | flops 2200000000 | tf_op jit(solution)/shard_map/regrid_blocks/pallas_call | solution.py:827
  17.2 0.0 copy-start.2
  17.2 0.0 copy-start.9
  17.2 2.3 %collective-permute-start.9 = (bf16[96,128]{1,0:T(8,128)(2,1)S(1)}, bf16[96,128]{1,0:T(8,128)(2,1)S(1)}, u32[]{:S(2)}, u32[]{:S(2)}) collective-permute-start(bf16[96,128]{1,0:T(8,128)(2,1)S(1)} %get-tuple-element.47), channel_id=1, source_target_pairs={{0,3},{3,0},{1,2},{2,1},{4,7},{7,4},{5,6},{6,5},{8,11},{11,8},{9,1... | collective-permute-start | bytes 73736 | tf_op jit(solution)/shard_map/ppermute | solution.py:863
  19.5 0.0 collective-permute-start.8
  19.6 0.0 collective-permute-done.2.e2_ref
  19.6 2.1 %collective-permute-start.7 = (bf16[64,128]{1,0:T(8,128)(2,1)S(1)}, bf16[64,128]{1,0:T(8,128)(2,1)S(1)}, u32[]{:S(2)}, u32[]{:S(2)}) collective-permute-start(bf16[64,128]{1,0:T(8,128)(2,1)S(1)} %get-tuple-element.45), channel_id=1, source_target_pairs={{0,1},{1,0},{2,3},{3,2},{4,5},{5,4},{6,7},{7,6},{8,9},{9,8},{10,11... | collective-permute-start | bytes 49160 | tf_op jit(solution)/shard_map/ppermute | solution.py:863
  21.7 0.0 collective-permute-done.3.e4_ref
  21.7 0.0 collective-permute-done.e1_ref
  21.7 0.0 copy-done
  21.7 0.0 copy-done.1
  21.7 0.0 copy-done.3
  21.7 0.0 copy-done.8
  21.7 0.9 %damping_or_first_step.1 = (bf16[256,1024]{1,0:T(8,128)(2,1)S(1)}, f32[7,16,1024]{2,1,0:T(8,128)S(1)}, f32[10,2,24,1024]{3,2,1,0:T(8,128)S(1)}) custom-call(f32[1,8,32,1024]{3,2,1,0:T(8,128)S(1)} %copy-done, s32[8,1024]{1,0:T(8,128)S(1)} %copy-done.3, f32[1,128]{1,0:T(1,128)S(1)} %bitcast.4, bf16[1024,512]{1,0:T(8,128)(2,1)S(1)} %copy-done.1, ...), custom_call_target="tpu_custom_call" | custom-call | tf_op jit(solution)/shard_map/damping_or_first_step/pallas_call | solution.py:883
  22.6 0.8 %collective-permute-done.7.refs_0_ = bf16[64,128]{1,0:T(8,128)(2,1)S(1)} collective-permute-done((bf16[64,128]{1,0:T(8,128)(2,1)S(1)}, bf16[64,128]{1,0:T(8,128)(2,1)S(1)}, u32[]{:S(2)}, u32[]{:S(2)}) %collective-permute-start.7) | collective-permute-done | bytes 16416 | tf_op jit(solution)/shard_map/ppermute | solution.py:863
  23.4 1.0 %collective-permute-done.8.refs_1_ = bf16[80,128]{1,0:T(8,128)(2,1)S(1)} collective-permute-done((bf16[80,128]{1,0:T(8,128)(2,1)S(1)}, bf16[80,128]{1,0:T(8,128)(2,1)S(1)}, u32[]{:S(2)}, u32[]{:S(2)}) %collective-permute-start.8) | collective-permute-done | bytes 20512 | tf_op jit(solution)/shard_map/ppermute | solution.py:863
  24.4 0.0 collective-permute-done.9.refs_2_
  24.4 0.1 collective-permute-start.10
  24.5 1.5 %collective-permute-start.11 = (bf16[64,128]{1,0:T(8,128)(2,1)S(1)}, bf16[64,128]{1,0:T(8,128)(2,1)S(1)}, u32[]{:S(2)}, u32[]{:S(2)}) collective-permute-start(bf16[64,128]{1,0:T(8,128)(2,1)S(1)} %get-tuple-element.50), channel_id=1, source_target_pairs={{4,8},{8,4},{12,0},{0,12},{5,9},{9,5},{13,1},{1,13},{6,10},{10,6},... | collective-permute-start | bytes 49160 | tf_op jit(solution)/shard_map/ppermute | solution.py:917
  26.0 0.0 copy-done.2
  26.0 0.0 copy-done.9
  26.0 0.5 %inverse_or_second_step.1.base_ref = f32[8,32,1024]{2,1,0:T(8,128)S(1)} custom-call(f32[1,128]{1,0:T(1,128)S(1)} %bitcast.5, bf16[1024,512]{1,0:T(8,128)(2,1)S(1)} %copy-done.2, bf16[256,1024]{1,0:T(8,128)(2,1)S(1)} %get-tuple-element.32.zb_ref, f32[7,16,1024]{2,1,0:T(8,128)S(1)} %get-tuple-element.33._.c_ref, ...), custom_call_target="tpu_custom_call" | custom-call | tf_op jit(solution)/shard_map/inverse_or_second_step/pallas_call | solution.py:918
  26.5 0.0 collective-permute-done.10.near_ref
  26.5 1.2 %collective-permute-done.11.far_ref = bf16[64,128]{1,0:T(8,128)(2,1)S(1)} collective-permute-done((bf16[64,128]{1,0:T(8,128)(2,1)S(1)}, bf16[64,128]{1,0:T(8,128)(2,1)S(1)}, u32[]{:S(2)}, u32[]{:S(2)}) %collective-permute-start.11) | collective-permute-done | bytes 16416 | tf_op jit(solution)/shard_map/ppermute | solution.py:917
  27.8 1.0 %add_surface_terms.1 = f32[1,8,32,1024]{3,2,1,0:T(8,128)} custom-call(f32[8,32,1024]{2,1,0:T(8,128)S(1)} %inverse_or_second_step.1.base_ref, f32[7,16,1024]{2,1,0:T(8,128)S(1)} %get-tuple-element.33._.c_ref, f32[64,128]{1,0:T(8,128)S(1)} %get-tuple-element.48.sum_ref, bf16[64,128]{1,0:T(8,128)(2,1)S(1)} %collective-permute-done.10.near_ref, ...), custom_call_target="tpu_custom_call" | custom-call | tf_op jit(solution)/shard_map/add_surface_terms/pallas_call | solution.py:926
  (2 shorter events, 0.1 us)
Async XLA Ops:
  0.0 9.5 %copy-start.7 = (s32[1,1,32,128]{3,2,1,0:T(8,128)S(1)}, s32[1,1,32,128]{3,2,1,0:T(8,128)}, u32[]{:S(2)}) copy-start(s32[1,1,32,128]{3,2,1,0:T(8,128)} %m_dst.1) | copy-start | bytes 49156
  0.0 9.5 %copy-start.6 = (s32[1,1,32,128]{3,2,1,0:T(8,128)S(1)}, s32[1,1,32,128]{3,2,1,0:T(8,128)}, u32[]{:S(2)}) copy-start(s32[1,1,32,128]{3,2,1,0:T(8,128)} %m_src.1) | copy-start | bytes 49156
  0.0 9.5 %copy-start.5 = (s32[1,1,32,128]{3,2,1,0:T(8,128)S(1)}, s32[1,1,32,128]{3,2,1,0:T(8,128)}, u32[]{:S(2)}) copy-start(s32[1,1,32,128]{3,2,1,0:T(8,128)} %a_dst.1) | copy-start | bytes 49156
  0.0 9.5 %copy-start.4 = (s32[1,1,32,128]{3,2,1,0:T(8,128)S(1)}, s32[1,1,32,128]{3,2,1,0:T(8,128)}, u32[]{:S(2)}) copy-start(s32[1,1,32,128]{3,2,1,0:T(8,128)} %a_src.1) | copy-start | bytes 49156
  0.0 15.8 %copy-start.11 = (bf16[1,1,32,128,128]{4,3,2,1,0:T(8,128)(2,1)S(1)}, bf16[1,1,32,128,128]{4,3,2,1,0:T(8,128)(2,1)}, u32[]{:S(2)}) copy-start(bf16[1,1,32,128,128]{4,3,2,1,0:T(8,128)(2,1)} %refs_8_.1) | copy-start | bytes 3145732
  0.0 15.8 %copy-start.10 = (bf16[1,1,32,128,128]{4,3,2,1,0:T(8,128)(2,1)S(1)}, bf16[1,1,32,128,128]{4,3,2,1,0:T(8,128)(2,1)}, u32[]{:S(2)}) copy-start(bf16[1,1,32,128,128]{4,3,2,1,0:T(8,128)(2,1)} %refs_7_.1) | copy-start | bytes 3145732
  3.3 7.3 %collective-permute-start.5 = (bf16[80,128]{1,0:T(8,128)(2,1)}, bf16[80,128]{1,0:T(8,128)(2,1)S(1)}, u32[]{:S(2)}, u32[]{:S(2)}) collective-permute-start(bf16[80,128]{1,0:T(8,128)(2,1)} %get-tuple-element.36), channel_id=1, source_target_pairs={{0,17},{17,0},{1,16},{16,1},{2,19},{19,2},{3,18},{18,3},{4,21},{21... | collective-permute-start | bytes 61448 | tf_op jit(solution)/shard_map/ppermute | solution.py:789
  6.6 3.9 %collective-permute-start.4 = (bf16[64,128]{1,0:T(8,128)(2,1)}, bf16[64,128]{1,0:T(8,128)(2,1)S(1)}, u32[]{:S(2)}, u32[]{:S(2)}) collective-permute-start(bf16[64,128]{1,0:T(8,128)(2,1)} %get-tuple-element.35), channel_id=1, source_target_pairs={{0,16},{16,0},{1,17},{17,1},{2,18},{18,2},{3,19},{19,3},{4,20},{20... | collective-permute-start | bytes 49160 | tf_op jit(solution)/shard_map/ppermute | solution.py:787
  7.8 7.9 %collective-permute-start.1 = (bf16[80,1024]{1,0:T(8,128)(2,1)}, bf16[80,1024]{1,0:T(8,128)(2,1)S(1)}, u32[]{:S(2)}, u32[]{:S(2)}) collective-permute-start(bf16[80,1024]{1,0:T(8,128)(2,1)} %get-tuple-element.29), channel_id=1, source_target_pairs={{4,8},{8,4},{12,0},{0,12},{5,9},{9,5},{13,1},{1,13},{6,10},{10,6},... | collective-permute-start | bytes 491528 | tf_op jit(solution)/shard_map/ppermute | solution.py:822
  10.6 5.2 %collective-permute-start.6 = (bf16[64,128]{1,0:T(8,128)(2,1)S(1)}, bf16[64,128]{1,0:T(8,128)(2,1)S(1)}, u32[]{:S(2)}, u32[]{:S(2)}) collective-permute-start(bf16[64,128]{1,0:T(8,128)(2,1)S(1)} %get-tuple-element.38), channel_id=1, source_target_pairs={{0,2},{1,3},{2,0},{3,1},{4,6},{5,7},{6,4},{7,5},{8,10},{9,11},{10,... | collective-permute-start | bytes 49160 | tf_op jit(solution)/shard_map/ppermute | solution.py:798
  13.2 6.3 %collective-permute-start.2 = (bf16[32,1024]{1,0:T(8,128)(2,1)}, bf16[32,1024]{1,0:T(8,128)(2,1)S(1)}, u32[]{:S(2)}, u32[]{:S(2)}) collective-permute-start(bf16[32,1024]{1,0:T(8,128)(2,1)} %get-tuple-element.30), channel_id=1, source_target_pairs={{16,17},{17,16},{18,19},{19,18},{0,8},{8,0},{1,9},{9,1},{2,10},{10... | collective-permute-start | bytes 196616 | tf_op jit(solution)/shard_map/ppermute | solution.py:824
  14.7 7.0 %collective-permute-start.3 = (bf16[32,1024]{1,0:T(8,128)(2,1)}, bf16[32,1024]{1,0:T(8,128)(2,1)S(1)}, u32[]{:S(2)}, u32[]{:S(2)}) collective-permute-start(bf16[32,1024]{1,0:T(8,128)(2,1)} %get-tuple-element.31), channel_id=1, source_target_pairs={{17,18},{18,17},{16,20},{20,16},{19,23},{23,19},{0,4},{4,0},{1,5},... | collective-permute-start | bytes 196616 | tf_op jit(solution)/shard_map/ppermute | solution.py:825
  14.7 7.0 %collective-permute-start = (bf16[80,1024]{1,0:T(8,128)(2,1)}, bf16[80,1024]{1,0:T(8,128)(2,1)S(1)}, u32[]{:S(2)}, u32[]{:S(2)}) collective-permute-start(bf16[80,1024]{1,0:T(8,128)(2,1)} %get-tuple-element.28), channel_id=1, source_target_pairs={{0,4},{4,0},{8,12},{12,8},{1,5},{5,1},{9,13},{13,9},{2,6},{6,2},{1... | collective-permute-start | bytes 491528 | tf_op jit(solution)/shard_map/ppermute | solution.py:821
  15.8 5.9 %copy-start = (f32[1,8,32,1024]{3,2,1,0:T(8,128)S(1)}, f32[1,8,32,1024]{3,2,1,0:T(8,128)}, u32[]{:S(2)}) copy-start(f32[1,8,32,1024]{3,2,1,0:T(8,128)} %x_ref.1) | copy-start | bytes 3145732
  15.8 5.9 %copy-start.1 = (bf16[1024,512]{1,0:T(8,128)(2,1)S(1)}, bf16[1024,512]{1,0:T(8,128)(2,1)}, u32[]{:S(2)}) copy-start(bf16[1024,512]{1,0:T(8,128)(2,1)} %constant.4.clone.table_hbm.table_ref) | copy-start | bytes 3145732
  15.8 5.9 %copy-start.3 = (s32[8,1024]{1,0:T(8,128)S(1)}, s32[8,1024]{1,0:T(8,128)}, u32[]{:S(2)}) copy-start(s32[8,1024]{1,0:T(8,128)} %wet_ref.1) | copy-start | bytes 98308
  15.8 5.9 %copy-start.8 = (f32[128]{0:T(128)S(1)}, f32[128]{0:T(128)}, u32[]{:S(2)}) copy-start(f32[128]{0:T(128)} %param.19) | copy-start | bytes 1540
  17.2 8.8 %copy-start.2 = (bf16[1024,512]{1,0:T(8,128)(2,1)S(1)}, bf16[1024,512]{1,0:T(8,128)(2,1)}, u32[]{:S(2)}) copy-start(bf16[1024,512]{1,0:T(8,128)(2,1)} %constant.5.clone.table_ref) | copy-start | bytes 3145732
  17.2 8.8 %copy-start.9 = (f32[128]{0:T(128)S(1)}, f32[128]{0:T(128)}, u32[]{:S(2)}) copy-start(f32[128]{0:T(128)} %param.18) | copy-start | bytes 1540
  17.2 7.2 %collective-permute-start.9 = (bf16[96,128]{1,0:T(8,128)(2,1)S(1)}, bf16[96,128]{1,0:T(8,128)(2,1)S(1)}, u32[]{:S(2)}, u32[]{:S(2)}) collective-permute-start(bf16[96,128]{1,0:T(8,128)(2,1)S(1)} %get-tuple-element.47), channel_id=1, source_target_pairs={{0,3},{3,0},{1,2},{2,1},{4,7},{7,4},{5,6},{6,5},{8,11},{11,8},{9,1... | collective-permute-start | bytes 73736 | tf_op jit(solution)/shard_map/ppermute | solution.py:863
  19.5 4.9 %collective-permute-start.8 = (bf16[80,128]{1,0:T(8,128)(2,1)S(1)}, bf16[80,128]{1,0:T(8,128)(2,1)S(1)}, u32[]{:S(2)}, u32[]{:S(2)}) collective-permute-start(bf16[80,128]{1,0:T(8,128)(2,1)S(1)} %get-tuple-element.46), channel_id=1, source_target_pairs={{0,2},{2,0},{1,3},{3,1},{4,6},{6,4},{5,7},{7,5},{8,10},{10,8},{9,1... | collective-permute-start | bytes 61448 | tf_op jit(solution)/shard_map/ppermute | solution.py:863
  19.6 3.8 %collective-permute-start.7 = (bf16[64,128]{1,0:T(8,128)(2,1)S(1)}, bf16[64,128]{1,0:T(8,128)(2,1)S(1)}, u32[]{:S(2)}, u32[]{:S(2)}) collective-permute-start(bf16[64,128]{1,0:T(8,128)(2,1)S(1)} %get-tuple-element.45), channel_id=1, source_target_pairs={{0,1},{1,0},{2,3},{3,2},{4,5},{5,4},{6,7},{7,6},{8,9},{9,8},{10,11... | collective-permute-start | bytes 49160 | tf_op jit(solution)/shard_map/ppermute | solution.py:863
  24.4 2.1 %collective-permute-start.10 = (bf16[64,128]{1,0:T(8,128)(2,1)S(1)}, bf16[64,128]{1,0:T(8,128)(2,1)S(1)}, u32[]{:S(2)}, u32[]{:S(2)}) collective-permute-start(bf16[64,128]{1,0:T(8,128)(2,1)S(1)} %get-tuple-element.49), channel_id=1, source_target_pairs={{0,4},{4,0},{8,12},{12,8},{1,5},{5,1},{9,13},{13,9},{2,6},{6,2},{1... | collective-permute-start | bytes 49160 | tf_op jit(solution)/shard_map/ppermute | solution.py:916
  24.5 3.2 %collective-permute-start.11 = (bf16[64,128]{1,0:T(8,128)(2,1)S(1)}, bf16[64,128]{1,0:T(8,128)(2,1)S(1)}, u32[]{:S(2)}, u32[]{:S(2)}) collective-permute-start(bf16[64,128]{1,0:T(8,128)(2,1)S(1)} %get-tuple-element.50), channel_id=1, source_target_pairs={{4,8},{8,4},{12,0},{0,12},{5,9},{9,5},{13,1},{1,13},{6,10},{10,6},... | collective-permute-start | bytes 49160 | tf_op jit(solution)/shard_map/ppermute | solution.py:917

commit v25 on v23

--- a/solution.py
+++ b/solution.py
@@ -310,19 +310,11 @@
         _,
         *refs,
     ) = refs[n_surfaces:]
-    land_ref, *sent_refs = refs[:-4]
-    weight_ref, gath_ref, val_ref, sem = refs[-4:]
+    land_ref, *sent_refs = refs[:-2]
+    gath_ref, val_ref = refs[-2:]
     is_atmos = lax.axis_index("comp") == 0
     blocks, points = val_ref.shape
     cells = surfaces[0].shape[0]
-
-    @pl.when(is_atmos)
-    def _():
-        pltpu.make_async_copy(m_weight.at[0, 0], weight_ref, sem).start()
-
-    @pl.when(jnp.logical_not(is_atmos))
-    def _():
-        pltpu.make_async_copy(a_weight.at[0, 0], weight_ref, sem).start()
 
     pair = 2 * points
     row_iota = lax.broadcasted_iota(jnp.int32, (cells, points), 0)
@@ -337,26 +329,30 @@
             gath_ref[b + k : b + k + 1, :] = jnp.sum(part, axis=0, keepdims=True)
     gathered = gath_ref[...].astype(bf16)
 
+    def block_products(weight_ref):
+        block_iota = lax.broadcasted_iota(jnp.int32, (blocks, points), 0)
+        values = jnp.zeros((blocks, points), f32)
+        for b in range(0, blocks, 2):
+            terms = lax.dot_general(
+                gathered,
+                weight_ref[0, 0, b : b + 2].reshape(pair, points),
+                (((1,), (1,)), ((), ())),
+                preferred_element_type=f32,
+            )
+            for k in range(2):
+                values = jnp.where(
+                    block_iota == b + k, terms[:, k * points : (k + 1) * points], values
+                )
+        val_ref[...] = jnp.where(used_ref[...] > 0, values, 0.0)
+
     @pl.when(is_atmos)
     def _():
-        pltpu.make_async_copy(m_weight.at[0, 0], weight_ref, sem).wait()
+        block_products(m_weight)
 
     @pl.when(jnp.logical_not(is_atmos))
     def _():
-        pltpu.make_async_copy(a_weight.at[0, 0], weight_ref, sem).wait()
-
-    block_iota = lax.broadcasted_iota(jnp.int32, (blocks, points), 0)
-    values = jnp.zeros((blocks, points), f32)
-    for b in range(0, blocks, 2):
-        terms = lax.dot_general(
-            gathered,
-            weight_ref[b : b + 2].reshape(pair, points),
-            (((1,), (1,)), ((), ())),
-            preferred_element_type=f32,
-        )
-        for k in range(2):
-            values = jnp.where(block_iota == b + k, terms[:, k * points : (k + 1) * points], values)
-    val_ref[...] = jnp.where(used_ref[...] > 0, values, 0.0)
+        block_products(a_weight)
+
     land = jnp.zeros((2 * cells, LANES), f32)
     for b in range(0, blocks, 2):
         spread = []
@@ -831,13 +827,11 @@
         functools.partial(regrid_kernel, len(surfaces)),
         out_shape=[shape((cells, LANES), f32)]
         + [shape((cells + 16 * (mask - 1), LANES), bf16) for mask in range(1, groups_y)],
-        in_specs=[vmem] * (len(surfaces) + 5) + [hbm, hbm] + [anywhere] * 1,
+        in_specs=[vmem] * (len(surfaces) + 7) + [anywhere] * 1,
         out_specs=[vmem] * groups_y,
         scratch_shapes=[
-            pltpu.VMEM((blocks, points, points), bf16),
             pltpu.VMEM((blocks, points), f32),
             pltpu.VMEM((blocks, points), f32),
-            pltpu.SemaphoreType.DMA,
         ],
         compiler_params=params(),
         cost_estimate=pl.CostEstimate(flops=2_200_000_000, bytes_accessed=0, transcendentals=0),

time: 28.9 us -> 28.8 us (level)
  transfers between devices with their start and end apart: 12 -> 12, of which waited for: 5 -> 5; matrix products, arithmetic and copies ran while one was open for 0% -> 0% of each run, Pallas kernels for 12% -> 11%
where the time goes in v25:
time: 28.8 us; the launch traced here: 28.6 us
  starting transfers between devices  15.7 us (55%)
  Pallas kernels  7.48 us (26%)
  waiting for transfers between devices  3.88 us (13%)
  between operations  1.5 us (5%)
    ppermute x3, starting transfers between devices, local(): lax.ppermute(block, axes, landing_route(mask))  4.45 us
    ppermute x1, starting transfers between devices, local(): far = lax.ppermute(wide, ('comp', 'gy'), partner_route(mask))  3.34 us
    pallas_call x1, Pallas kernels, local(): pl.pallas_call(functools.partial(start_kernel, groups_x, paired), out_sha...  3.24 us
    ppermute x1, starting transfers between devices, local(): lax.ppermute(coarse, 'gy', sum_route(mask))  2.65 us
    ppermute x3, waiting for transfers between devices, local(): lax.ppermute(block, axes, landing_route(mask))  1.91 us
    ppermute x1, starting transfers between devices, local(): far = lax.ppermute(far, 'gx', both_ways(ring_pairs(groups_x, 1)))  1.54 us
    ppermute x1, starting transfers between devices, local(): e2 = lax.ppermute(e2, axes, level_route(0))  1.49 us
    ppermute x1, starting transfers between devices, local(): surface = lax.ppermute(coarse, ('comp', 'gy'), partner_route(0)).astype(f32)  1.23 us
  transfers between devices with their start and end apart: 12, of which 5 were waited for; matrix products, arithmetic and copies ran while one was open for 0% of the time, Pallas kernels for 11%

profile of v25, /device:TPU:0, one launch (start us, length us, event | category | flops | bytes accessed | tf_op | source)
XLA Modules:
  0.0 28.6 jit_solution(3470354046665100743)
XLA Ops:
  0.0 0.0 copy-start.7
  0.0 0.0 copy-start.6
  0.0 0.0 copy-start.5
  0.0 0.0 copy-start.4
  0.0 0.0 copy-start.11
  0.0 0.0 copy-start.10
  0.0 3.2 %surface_and_forward_or_halos.1 = (bf16[64,128]{1,0:T(8,128)(2,1)}, bf16[80,128]{1,0:T(8,128)(2,1)}, bf16[80,1024]{1,0:T(8,128)(2,1)}, bf16[80,1024]{1,0:T(8,128...) custom-call(f32[1,8,32,1024]{3,2,1,0:T(8,128)} %x_ref.1, s32[8,1024]{1,0:T(8,128)} %wet_ref.1, ...), custom_call_target="tpu_custom_call" | custom-call | tf_op jit(solution)/shard_map/surface_and_forward_or_halos/pallas_call | solution.py:736
  3.3 3.3 %collective-permute-start.5 = (bf16[80,128]{1,0:T(8,128)(2,1)}, bf16[80,128]{1,0:T(8,128)(2,1)S(1)}, u32[]{:S(2)}, u32[]{:S(2)}) collective-permute-start(bf16[80,128]{1,0:T(8,128)(2,1)} %get-tuple-element.36), channel_id=1, source_target_pairs={{0,17},{17,0},{1,16},{16,1},{2,19},{19,2},{3,18},{18,3},{4,21},{21... | collective-permute-start | bytes 61448 | tf_op jit(solution)/shard_map/ppermute | solution.py:788
  6.6 1.2 %collective-permute-start.4 = (bf16[64,128]{1,0:T(8,128)(2,1)}, bf16[64,128]{1,0:T(8,128)(2,1)S(1)}, u32[]{:S(2)}, u32[]{:S(2)}) collective-permute-start(bf16[64,128]{1,0:T(8,128)(2,1)} %get-tuple-element.35), channel_id=1, source_target_pairs={{0,16},{16,0},{1,17},{17,1},{2,18},{18,2},{3,19},{19,3},{4,20},{20... | collective-permute-start | bytes 49160 | tf_op jit(solution)/shard_map/ppermute | solution.py:786
  7.8 0.4 %collective-permute-start.1 = (bf16[80,1024]{1,0:T(8,128)(2,1)}, bf16[80,1024]{1,0:T(8,128)(2,1)S(1)}, u32[]{:S(2)}, u32[]{:S(2)}) collective-permute-start(bf16[80,1024]{1,0:T(8,128)(2,1)} %get-tuple-element.29), channel_id=1, source_target_pairs={{4,8},{8,4},{12,0},{0,12},{5,9},{9,5},{13,1},{1,13},{6,10},{10,6},... | collective-permute-start | bytes 491528 | tf_op jit(solution)/shard_map/ppermute | solution.py:821
  9.5 0.0 copy-done.7
  9.5 0.0 copy-done.6
  9.5 0.0 copy-done.5
  9.5 0.0 copy-done.4
  9.5 0.6 %one_hots.1 = (bf16[128,4096]{1,0:T(8,128)(2,1)S(1)}, bf16[128,4096]{1,0:T(8,128)(2,1)S(1)}, s32[32,128]{1,0:T(8,128)S(1)}, s32[32,128]{1,0:T(8,128)S(1)}, s32[32,128]{1,0:T(8,128)S(1)}) custom-call(s32[1,1,32,128]{3,2,1,0:T(8,128)S(1)} %copy-done.4, s32[1,1,32,128]{3,2,1,0:T(8,128)S(1)} %copy-done.5, s32[1,1]{1,0:T(1,128)S(6)} %copy.16.a_count, ...), custom_call_target="tpu_custom_call" | custom-call | tf_op jit(solution)/shard_map/one_hots/pallas_call | solution.py:760
  10.2 0.4 %collective-permute-done.4 = bf16[64,128]{1,0:T(8,128)(2,1)S(1)} collective-permute-done((bf16[64,128]{1,0:T(8,128)(2,1)}, bf16[64,128]{1,0:T(8,128)(2,1)S(1)}, u32[]{:S(2)}, u32[]{:S(2)}) %collective-permute-start.4) | collective-permute-done | bytes 16416 | tf_op jit(solution)/shard_map/ppermute | solution.py:786
  10.6 0.0 collective-permute-done.5
  10.6 2.7 %collective-permute-start.6 = (bf16[64,128]{1,0:T(8,128)(2,1)S(1)}, bf16[64,128]{1,0:T(8,128)(2,1)S(1)}, u32[]{:S(2)}, u32[]{:S(2)}) collective-permute-start(bf16[64,128]{1,0:T(8,128)(2,1)S(1)} %get-tuple-element.38), channel_id=1, source_target_pairs={{0,2},{1,3},{2,0},{3,1},{4,6},{5,7},{6,4},{7,5},{8,10},{9,11},{10,... | collective-permute-start | bytes 49160 | tf_op jit(solution)/shard_map/ppermute | solution.py:797
  13.2 1.5 %collective-permute-start.2 = (bf16[32,1024]{1,0:T(8,128)(2,1)}, bf16[32,1024]{1,0:T(8,128)(2,1)S(1)}, u32[]{:S(2)}, u32[]{:S(2)}) collective-permute-start(bf16[32,1024]{1,0:T(8,128)(2,1)} %get-tuple-element.30), channel_id=1, source_target_pairs={{16,17},{17,16},{18,19},{19,18},{0,8},{8,0},{1,9},{9,1},{2,10},{10... | collective-permute-start | bytes 196616 | tf_op jit(solution)/shard_map/ppermute | solution.py:823
  14.7 0.0 collective-permute-start.3
  14.7 0.5 %collective-permute-start = (bf16[80,1024]{1,0:T(8,128)(2,1)}, bf16[80,1024]{1,0:T(8,128)(2,1)S(1)}, u32[]{:S(2)}, u32[]{:S(2)}) collective-permute-start(bf16[80,1024]{1,0:T(8,128)(2,1)} %get-tuple-element.28), channel_id=1, source_target_pairs={{0,4},{4,0},{8,12},{12,8},{1,5},{5,1},{9,13},{13,9},{2,6},{6,2},{1... | collective-permute-start | bytes 491528 | tf_op jit(solution)/shard_map/ppermute | solution.py:820
  15.2 0.3 %collective-permute-done.6.refs_1_ = bf16[64,128]{1,0:T(8,128)(2,1)S(1)} collective-permute-done((bf16[64,128]{1,0:T(8,128)(2,1)S(1)}, bf16[64,128]{1,0:T(8,128)(2,1)S(1)}, u32[]{:S(2)}, u32[]{:S(2)}) %collective-permute-start.6) | collective-permute-done | bytes 16416 | tf_op jit(solution)/shard_map/ppermute | solution.py:797
  15.6 0.0 collective-permute-done.1.e3_ref.refs_9_
  15.6 0.0 copy-done.11
  15.6 0.0 copy-done.10
  15.6 0.0 copy-start
  15.6 0.0 copy-start.1
  15.6 0.0 copy-start.3
  15.6 0.0 copy-start.8
  15.6 1.2 %regrid_blocks.1 = (f32[64,128]{1,0:T(8,128)S(1)}, bf16[64,128]{1,0:T(8,128)(2,1)S(1)}, bf16[80,128]{1,0:T(8,128)(2,1)S(1)}, bf16[96,128]{1,0:T(8,128)(2,1)S(1)}) custom-call(f32[64,128]{1,0:T(8,128)S(1)} %get-tuple-element.52.refs_0_, bf16[64,128]{1,0:T(8,128)(2,1)S(1)} %collective-permute-done.6.refs_1_, bf16[128,4096]{1,0:T(8,128)(2,1)S(1)} %get-tuple-element.39.refs_2_, ...), custom_call_target="tpu_custom_call" | custom-call | flops 2200000000 | tf_op jit(solution)/shard_map/regrid_blocks/pallas_call | solution.py:826
  16.9 0.0 copy-start.2
  16.9 0.0 copy-start.9
  16.9 2.5 %collective-permute-start.9 = (bf16[96,128]{1,0:T(8,128)(2,1)S(1)}, bf16[96,128]{1,0:T(8,128)(2,1)S(1)}, u32[]{:S(2)}, u32[]{:S(2)}) collective-permute-start(bf16[96,128]{1,0:T(8,128)(2,1)S(1)} %get-tuple-element.47), channel_id=1, source_target_pairs={{0,3},{3,0},{1,2},{2,1},{4,7},{7,4},{5,6},{6,5},{8,11},{11,8},{9,1... | collective-permute-start | bytes 73736 | tf_op jit(solution)/shard_map/ppermute | solution.py:860
  19.4 0.0 collective-permute-start.8
  19.4 0.0 collective-permute-done.2.e2_ref
  19.4 2.0 %collective-permute-start.7 = (bf16[64,128]{1,0:T(8,128)(2,1)S(1)}, bf16[64,128]{1,0:T(8,128)(2,1)S(1)}, u32[]{:S(2)}, u32[]{:S(2)}) collective-permute-start(bf16[64,128]{1,0:T(8,128)(2,1)S(1)} %get-tuple-element.45), channel_id=1, source_target_pairs={{0,1},{1,0},{2,3},{3,2},{4,5},{5,4},{6,7},{7,6},{8,9},{9,8},{10,11... | collective-permute-start | bytes 49160 | tf_op jit(solution)/shard_map/ppermute | solution.py:860
  21.3 0.0 collective-permute-done.3.e4_ref
  21.3 0.0 collective-permute-done.e1_ref
  21.3 0.0 copy-done
  21.3 0.0 copy-done.1
  21.4 0.0 copy-done.3
  21.4 0.0 copy-done.8
  21.4 0.9 %damping_or_first_step.1 = (bf16[256,1024]{1,0:T(8,128)(2,1)S(1)}, f32[7,16,1024]{2,1,0:T(8,128)S(1)}, f32[10,2,24,1024]{3,2,1,0:T(8,128)S(1)}) custom-call(f32[1,8,32,1024]{3,2,1,0:T(8,128)S(1)} %copy-done, s32[8,1024]{1,0:T(8,128)S(1)} %copy-done.3, f32[1,128]{1,0:T(1,128)S(1)} %bitcast.4, bf16[1024,512]{1,0:T(8,128)(2,1)S(1)} %copy-done.1, ...), custom_call_target="tpu_custom_call" | custom-call | tf_op jit(solution)/shard_map/damping_or_first_step/pallas_call | solution.py:880
  22.3 0.8 %collective-permute-done.7.refs_0_ = bf16[64,128]{1,0:T(8,128)(2,1)S(1)} collective-permute-done((bf16[64,128]{1,0:T(8,128)(2,1)S(1)}, bf16[64,128]{1,0:T(8,128)(2,1)S(1)}, u32[]{:S(2)}, u32[]{:S(2)}) %collective-permute-start.7) | collective-permute-done | bytes 16416 | tf_op jit(solution)/shard_map/ppermute | solution.py:860
  23.1 1.1 %collective-permute-done.8.refs_1_ = bf16[80,128]{1,0:T(8,128)(2,1)S(1)} collective-permute-done((bf16[80,128]{1,0:T(8,128)(2,1)S(1)}, bf16[80,128]{1,0:T(8,128)(2,1)S(1)}, u32[]{:S(2)}, u32[]{:S(2)}) %collective-permute-start.8) | collective-permute-done | bytes 20512 | tf_op jit(solution)/shard_map/ppermute | solution.py:860
  24.2 0.0 collective-permute-done.9.refs_2_
  24.3 0.1 collective-permute-start.10
  24.3 1.5 %collective-permute-start.11 = (bf16[64,128]{1,0:T(8,128)(2,1)S(1)}, bf16[64,128]{1,0:T(8,128)(2,1)S(1)}, u32[]{:S(2)}, u32[]{:S(2)}) collective-permute-start(bf16[64,128]{1,0:T(8,128)(2,1)S(1)} %get-tuple-element.50), channel_id=1, source_target_pairs={{4,8},{8,4},{12,0},{0,12},{5,9},{9,5},{13,1},{1,13},{6,10},{10,6},... | collective-permute-start | bytes 49160 | tf_op jit(solution)/shard_map/ppermute | solution.py:914
  25.9 0.0 copy-done.2
  25.9 0.0 copy-done.9
  25.9 0.4 %inverse_or_second_step.1.base_ref = f32[8,32,1024]{2,1,0:T(8,128)S(1)} custom-call(f32[1,128]{1,0:T(1,128)S(1)} %bitcast.5, bf16[1024,512]{1,0:T(8,128)(2,1)S(1)} %copy-done.2, bf16[256,1024]{1,0:T(8,128)(2,1)S(1)} %get-tuple-element.32.zb_ref, f32[7,16,1024]{2,1,0:T(8,128)S(1)} %get-tuple-element.33._.c_ref, ...), custom_call_target="tpu_custom_call" | custom-call | tf_op jit(solution)/shard_map/inverse_or_second_step/pallas_call | solution.py:915
  26.3 0.0 collective-permute-done.10.near_ref
  26.4 1.2 %collective-permute-done.11.far_ref = bf16[64,128]{1,0:T(8,128)(2,1)S(1)} collective-permute-done((bf16[64,128]{1,0:T(8,128)(2,1)S(1)}, bf16[64,128]{1,0:T(8,128)(2,1)S(1)}, u32[]{:S(2)}, u32[]{:S(2)}) %collective-permute-start.11) | collective-permute-done | bytes 16416 | tf_op jit(solution)/shard_map/ppermute | solution.py:914
  27.6 1.0 %add_surface_terms.1 = f32[1,8,32,1024]{3,2,1,0:T(8,128)} custom-call(f32[8,32,1024]{2,1,0:T(8,128)S(1)} %inverse_or_second_step.1.base_ref, f32[7,16,1024]{2,1,0:T(8,128)S(1)} %get-tuple-element.33._.c_ref, f32[64,128]{1,0:T(8,128)S(1)} %get-tuple-element.48.sum_ref, bf16[64,128]{1,0:T(8,128)(2,1)S(1)} %collective-permute-done.10.near_ref, ...), custom_call_target="tpu_custom_call" | custom-call | tf_op jit(solution)/shard_map/add_surface_terms/pallas_call | solution.py:923
  (2 shorter events, 0.1 us)
Async XLA Ops:
  0.0 9.5 %copy-start.7 = (s32[1,1,32,128]{3,2,1,0:T(8,128)S(1)}, s32[1,1,32,128]{3,2,1,0:T(8,128)}, u32[]{:S(2)}) copy-start(s32[1,1,32,128]{3,2,1,0:T(8,128)} %m_dst.1) | copy-start | bytes 49156
  0.0 9.5 %copy-start.6 = (s32[1,1,32,128]{3,2,1,0:T(8,128)S(1)}, s32[1,1,32,128]{3,2,1,0:T(8,128)}, u32[]{:S(2)}) copy-start(s32[1,1,32,128]{3,2,1,0:T(8,128)} %m_src.1) | copy-start | bytes 49156
  0.0 9.5 %copy-start.5 = (s32[1,1,32,128]{3,2,1,0:T(8,128)S(1)}, s32[1,1,32,128]{3,2,1,0:T(8,128)}, u32[]{:S(2)}) copy-start(s32[1,1,32,128]{3,2,1,0:T(8,128)} %a_dst.1) | copy-start | bytes 49156
  0.0 9.5 %copy-start.4 = (s32[1,1,32,128]{3,2,1,0:T(8,128)S(1)}, s32[1,1,32,128]{3,2,1,0:T(8,128)}, u32[]{:S(2)}) copy-start(s32[1,1,32,128]{3,2,1,0:T(8,128)} %a_src.1) | copy-start | bytes 49156
  0.0 15.6 %copy-start.11 = (bf16[1,1,32,128,128]{4,3,2,1,0:T(8,128)(2,1)S(1)}, bf16[1,1,32,128,128]{4,3,2,1,0:T(8,128)(2,1)}, u32[]{:S(2)}) copy-start(bf16[1,1,32,128,128]{4,3,2,1,0:T(8,128)(2,1)} %refs_8_.1) | copy-start | bytes 3145732
  0.0 15.6 %copy-start.10 = (bf16[1,1,32,128,128]{4,3,2,1,0:T(8,128)(2,1)S(1)}, bf16[1,1,32,128,128]{4,3,2,1,0:T(8,128)(2,1)}, u32[]{:S(2)}) copy-start(bf16[1,1,32,128,128]{4,3,2,1,0:T(8,128)(2,1)} %refs_7_.1) | copy-start | bytes 3145732
  3.3 7.3 %collective-permute-start.5 = (bf16[80,128]{1,0:T(8,128)(2,1)}, bf16[80,128]{1,0:T(8,128)(2,1)S(1)}, u32[]{:S(2)}, u32[]{:S(2)}) collective-permute-start(bf16[80,128]{1,0:T(8,128)(2,1)} %get-tuple-element.36), channel_id=1, source_target_pairs={{0,17},{17,0},{1,16},{16,1},{2,19},{19,2},{3,18},{18,3},{4,21},{21... | collective-permute-start | bytes 61448 | tf_op jit(solution)/shard_map/ppermute | solution.py:788
  6.6 3.9 %collective-permute-start.4 = (bf16[64,128]{1,0:T(8,128)(2,1)}, bf16[64,128]{1,0:T(8,128)(2,1)S(1)}, u32[]{:S(2)}, u32[]{:S(2)}) collective-permute-start(bf16[64,128]{1,0:T(8,128)(2,1)} %get-tuple-element.35), channel_id=1, source_target_pairs={{0,16},{16,0},{1,17},{17,1},{2,18},{18,2},{3,19},{19,3},{4,20},{20... | collective-permute-start | bytes 49160 | tf_op jit(solution)/shard_map/ppermute | solution.py:786
  7.8 7.7 %collective-permute-start.1 = (bf16[80,1024]{1,0:T(8,128)(2,1)}, bf16[80,1024]{1,0:T(8,128)(2,1)S(1)}, u32[]{:S(2)}, u32[]{:S(2)}) collective-permute-start(bf16[80,1024]{1,0:T(8,128)(2,1)} %get-tuple-element.29), channel_id=1, source_target_pairs={{4,8},{8,4},{12,0},{0,12},{5,9},{9,5},{13,1},{1,13},{6,10},{10,6},... | collective-permute-start | bytes 491528 | tf_op jit(solution)/shard_map/ppermute | solution.py:821
  10.6 5.0 %collective-permute-start.6 = (bf16[64,128]{1,0:T(8,128)(2,1)S(1)}, bf16[64,128]{1,0:T(8,128)(2,1)S(1)}, u32[]{:S(2)}, u32[]{:S(2)}) collective-permute-start(bf16[64,128]{1,0:T(8,128)(2,1)S(1)} %get-tuple-element.38), channel_id=1, source_target_pairs={{0,2},{1,3},{2,0},{3,1},{4,6},{5,7},{6,4},{7,5},{8,10},{9,11},{10,... | collective-permute-start | bytes 49160 | tf_op jit(solution)/shard_map/ppermute | solution.py:797
  13.2 6.1 %collective-permute-start.2 = (bf16[32,1024]{1,0:T(8,128)(2,1)}, bf16[32,1024]{1,0:T(8,128)(2,1)S(1)}, u32[]{:S(2)}, u32[]{:S(2)}) collective-permute-start(bf16[32,1024]{1,0:T(8,128)(2,1)} %get-tuple-element.30), channel_id=1, source_target_pairs={{16,17},{17,16},{18,19},{19,18},{0,8},{8,0},{1,9},{9,1},{2,10},{10... | collective-permute-start | bytes 196616 | tf_op jit(solution)/shard_map/ppermute | solution.py:823
  14.7 6.6 %collective-permute-start.3 = (bf16[32,1024]{1,0:T(8,128)(2,1)}, bf16[32,1024]{1,0:T(8,128)(2,1)S(1)}, u32[]{:S(2)}, u32[]{:S(2)}) collective-permute-start(bf16[32,1024]{1,0:T(8,128)(2,1)} %get-tuple-element.31), channel_id=1, source_target_pairs={{17,18},{18,17},{16,20},{20,16},{19,23},{23,19},{0,4},{4,0},{1,5},... | collective-permute-start | bytes 196616 | tf_op jit(solution)/shard_map/ppermute | solution.py:824
  14.7 6.6 %collective-permute-start = (bf16[80,1024]{1,0:T(8,128)(2,1)}, bf16[80,1024]{1,0:T(8,128)(2,1)S(1)}, u32[]{:S(2)}, u32[]{:S(2)}) collective-permute-start(bf16[80,1024]{1,0:T(8,128)(2,1)} %get-tuple-element.28), channel_id=1, source_target_pairs={{0,4},{4,0},{8,12},{12,8},{1,5},{5,1},{9,13},{13,9},{2,6},{6,2},{1... | collective-permute-start | bytes 491528 | tf_op jit(solution)/shard_map/ppermute | solution.py:820
  15.6 5.8 %copy-start = (f32[1,8,32,1024]{3,2,1,0:T(8,128)S(1)}, f32[1,8,32,1024]{3,2,1,0:T(8,128)}, u32[]{:S(2)}) copy-start(f32[1,8,32,1024]{3,2,1,0:T(8,128)} %x_ref.1) | copy-start | bytes 3145732
  15.6 5.7 %copy-start.1 = (bf16[1024,512]{1,0:T(8,128)(2,1)S(1)}, bf16[1024,512]{1,0:T(8,128)(2,1)}, u32[]{:S(2)}) copy-start(bf16[1024,512]{1,0:T(8,128)(2,1)} %constant.4.clone.table_hbm.table_ref) | copy-start | bytes 3145732
  15.6 5.7 %copy-start.3 = (s32[8,1024]{1,0:T(8,128)S(1)}, s32[8,1024]{1,0:T(8,128)}, u32[]{:S(2)}) copy-start(s32[8,1024]{1,0:T(8,128)} %wet_ref.1) | copy-start | bytes 98308
  15.6 5.7 %copy-start.8 = (f32[128]{0:T(128)S(1)}, f32[128]{0:T(128)}, u32[]{:S(2)}) copy-start(f32[128]{0:T(128)} %param.19) | copy-start | bytes 1540
  16.9 9.0 %copy-start.2 = (bf16[1024,512]{1,0:T(8,128)(2,1)S(1)}, bf16[1024,512]{1,0:T(8,128)(2,1)}, u32[]{:S(2)}) copy-start(bf16[1024,512]{1,0:T(8,128)(2,1)} %constant.5.clone.table_ref) | copy-start | bytes 3145732
  16.9 9.0 %copy-start.9 = (f32[128]{0:T(128)S(1)}, f32[128]{0:T(128)}, u32[]{:S(2)}) copy-start(f32[128]{0:T(128)} %param.18) | copy-start | bytes 1540
  16.9 7.3 %collective-permute-start.9 = (bf16[96,128]{1,0:T(8,128)(2,1)S(1)}, bf16[96,128]{1,0:T(8,128)(2,1)S(1)}, u32[]{:S(2)}, u32[]{:S(2)}) collective-permute-start(bf16[96,128]{1,0:T(8,128)(2,1)S(1)} %get-tuple-element.47), channel_id=1, source_target_pairs={{0,3},{3,0},{1,2},{2,1},{4,7},{7,4},{5,6},{6,5},{8,11},{11,8},{9,1... | collective-permute-start | bytes 73736 | tf_op jit(solution)/shard_map/ppermute | solution.py:860
  19.4 4.8 %collective-permute-start.8 = (bf16[80,128]{1,0:T(8,128)(2,1)S(1)}, bf16[80,128]{1,0:T(8,128)(2,1)S(1)}, u32[]{:S(2)}, u32[]{:S(2)}) collective-permute-start(bf16[80,128]{1,0:T(8,128)(2,1)S(1)} %get-tuple-element.46), channel_id=1, source_target_pairs={{0,2},{2,0},{1,3},{3,1},{4,6},{6,4},{5,7},{7,5},{8,10},{10,8},{9,1... | collective-permute-start | bytes 61448 | tf_op jit(solution)/shard_map/ppermute | solution.py:860
  19.4 3.7 %collective-permute-start.7 = (bf16[64,128]{1,0:T(8,128)(2,1)S(1)}, bf16[64,128]{1,0:T(8,128)(2,1)S(1)}, u32[]{:S(2)}, u32[]{:S(2)}) collective-permute-start(bf16[64,128]{1,0:T(8,128)(2,1)S(1)} %get-tuple-element.45), channel_id=1, source_target_pairs={{0,1},{1,0},{2,3},{3,2},{4,5},{5,4},{6,7},{7,6},{8,9},{9,8},{10,11... | collective-permute-start | bytes 49160 | tf_op jit(solution)/shard_map/ppermute | solution.py:860
  24.3 2.1 %collective-permute-start.10 = (bf16[64,128]{1,0:T(8,128)(2,1)S(1)}, bf16[64,128]{1,0:T(8,128)(2,1)S(1)}, u32[]{:S(2)}, u32[]{:S(2)}) collective-permute-start(bf16[64,128]{1,0:T(8,128)(2,1)S(1)} %get-tuple-element.49), channel_id=1, source_target_pairs={{0,4},{4,0},{8,12},{12,8},{1,5},{5,1},{9,13},{13,9},{2,6},{6,2},{1... | collective-permute-start | bytes 49160 | tf_op jit(solution)/shard_map/ppermute | solution.py:913
  24.3 3.2 %collective-permute-start.11 = (bf16[64,128]{1,0:T(8,128)(2,1)S(1)}, bf16[64,128]{1,0:T(8,128)(2,1)S(1)}, u32[]{:S(2)}, u32[]{:S(2)}) collective-permute-start(bf16[64,128]{1,0:T(8,128)(2,1)S(1)} %get-tuple-element.50), channel_id=1, source_target_pairs={{4,8},{8,4},{12,0},{0,12},{5,9},{9,5},{13,1},{1,13},{6,10},{10,6},... | collective-permute-start | bytes 49160 | tf_op jit(solution)/shard_map/ppermute | solution.py:914
